TPU v7x, 32 devices: a whole 2x2x4 slice. The times are simulated.
32 devices in a mesh: groups: 2 (over x), feat: 8 (over z, y), rep: 2 (over core).
Axes of the slice: x: 2, y: 2, z: 4, core: 2. Of those that a mesh axis runs over, the one named last changes fastest.
Arguments:
- src_feats: bfloat16 [768, 24576], P('feat', 'groups'), parts along dimension 1, may hold values from -6 to 6
- nbr_one: int32 [16, 2, 10, 192], P('groups', 'rep'), parts along dimension 0, may hold values from 0 to 12287
- counts: int32 [16, 2], P(('groups', 'feat'), 'rep'), parts along dimension 0, may hold values from 1 to 192, as said below
- seed_rows: int32 [2048], P(('groups', 'feat', 'rep')), parts along dimension 0, may hold values from 0 to 3071, as said below
- nbr_two: int32 [2048, 15], P(('groups', 'feat', 'rep')), parts along dimension 0, may hold values from 0 to 3071, as said below
- w1_self: bfloat16 [768, 512], P('feat'), may hold values from -0.15625 to 0.15625
- w1_nbr: bfloat16 [768, 512], P('feat'), may hold values from -0.15625 to 0.15625
- bias_one: float32 [512], replicated, may hold values from -3 to 3
- w2_self: bfloat16 [512, 512], replicated, may hold values from -0.25 to 0.25
- w2_nbr: bfloat16 [512, 512], replicated, may hold values from -0.25 to 0.25
- bias_two: float32 [512], replicated, may hold values from -3 to 3
Outputs:
- hidden_one: bfloat16 [16, 2, 192, 512], P(('groups', 'feat'), 'rep'), parts along dimension 0
- seed_out: bfloat16 [2048, 512], P(('groups', 'feat', 'rep')), parts along dimension 0
There are 2 independent parts, one for each index of `groups`. A program takes and returns all parts, laid end to end along the dimension named above; an argument that names none is the same for every part. Nothing has to cross between parts.
Inputs may be any that keep to these rules, and one draw needn't show every extreme that they name: `counts`: in every draw one partition has exactly 192 live rows. `seed_rows`: every entry is a live layer-one row p * 192 + j with j < the live rows of partition p. `nbr_two`: every entry is a live layer-one row p * 192 + j with j < the live rows of partition p.
All inputs are finite; a program needn't handle non-finite values.
Results may differ from a plain program's by a relative error of at most 0.013.
Values may be sent and summed in bfloat16 or wider, within the bound.
No kernel may reach another device: no remote copies, remote signals or barrier semaphores. Data moves between devices by JAX's collectives and lax.ppermute only.
A program may use at most 128 MiB of HBM per device.

v0:
```python
import jax
import jax.numpy as jnp
from jax import lax
from jax.sharding import PartitionSpec as P


def body(
    src_feats,
    nbr_one,
    counts,
    seed_rows,
    nbr_two,
    w1_self,
    w1_nbr,
    bias_one,
    w2_self,
    w2_nbr,
    bias_two,
):
    n_feat = lax.axis_size("feat")
    n_rep = lax.axis_size("rep")
    rep_pos = lax.axis_index("rep")
    fslice = src_feats.shape[0]
    fanout_one = nbr_one.shape[2]
    pcap = nbr_one.shape[3]
    width = w1_self.shape[1]
    rows_one = n_feat * n_rep * pcap
    owned = src_feats[:, :rows_one].reshape(fslice, n_feat, n_rep, pcap)
    self_part = lax.dynamic_index_in_dim(owned, rep_pos, 2, keepdims=False)
    node_major = jnp.transpose(src_feats)
    picked = jnp.take(node_major, nbr_one[:, 0].reshape(-1), axis=0).reshape(
        n_feat, fanout_one, pcap, fslice
    )
    mean_rows = (jnp.sum(picked.astype(jnp.float32), axis=1) / fanout_one).astype(jnp.bfloat16)
    mean_part = jnp.transpose(mean_rows, (2, 0, 1))
    stacked = jnp.stack([self_part, mean_part])
    weights = jnp.stack([w1_self, w1_nbr])
    partial_value = jnp.einsum(
        "sfor,sfh->orh", stacked, weights, preferred_element_type=jnp.float32
    )
    pre_one = lax.psum_scatter(
        partial_value.astype(jnp.bfloat16), "feat", scatter_dimension=0, tiled=True
    ).astype(jnp.float32)[0]
    live = jnp.arange(pcap) < counts[0, 0]
    hidden = jnp.where(live[:, None], jnp.maximum(pre_one + bias_one, 0.0), 0.0).astype(
        jnp.bfloat16
    )
    seed_count = seed_rows.shape[0]
    fanout_two = nbr_two.shape[1]
    table = lax.all_gather(hidden, ("feat", "rep"), axis=0, tiled=True)
    wanted = jnp.concatenate([seed_rows[:, None], nbr_two], axis=1).reshape(-1)
    fetched = jnp.take(table, wanted, axis=0).reshape(seed_count, fanout_two + 1, width)
    self_two = fetched[:, 0]
    agg_two = (jnp.sum(fetched[:, 1:].astype(jnp.float32), axis=1) / fanout_two).astype(
        jnp.bfloat16
    )
    pre_two = (
        jnp.dot(self_two, w2_self, preferred_element_type=jnp.float32)
        + jnp.dot(agg_two, w2_nbr, preferred_element_type=jnp.float32)
        + bias_two
    )
    seed_out = jnp.maximum(pre_two, 0.0).astype(jnp.bfloat16)
    return (hidden[None, None], seed_out)


def solution(mesh):
    placed = (
        P("feat", "groups"),
        P("groups", "rep", None, None),
        P(("groups", "feat"), "rep"),
        P(("groups", "feat", "rep")),
        P(("groups", "feat", "rep"), None),
        P("feat", None),
        P("feat", None),
        P(),
        P(),
        P(),
        P(),
    )
    return jax.shard_map(
        body,
        mesh=mesh,
        in_specs=placed,
        out_specs=(P(("groups", "feat"), "rep", None, None), P(("groups", "feat", "rep"), None)),
        check_vma=False,
    )
```

profile of v0, /device:TPU:0, one launch (start us, length us, event | category | flops | bytes accessed | tf_op | source)
XLA Modules:
  0.0 208.6 jit_solution(4552656024327140025)
XLA Ops:
  7.2 0.0 copy-start
  7.2 0.0 copy-start.2
  7.2 0.0 reduce-scatter.2.cloned.1.call-start
  7.2 4.6 %copy.19 = bf16[96,12288]{0,1:T(8,128)(2,1)} copy(bf16[96,12288]{1,0:T(8,128)(2,1)} %param.11) | data formatting | bytes 4718592 | tf_op args[0]
  11.8 0.0 copy-done.2
  11.8 0.2 reduce
  12.0 0.1 reshape_squeeze.6
  12.2 0.1 compare_select_fusion
  12.3 54.3 %gather_fusion = bf16[15360,96]{1,0:T(8,128)(2,1)} fusion(bf16[12288,96]{1,0:T(8,128)(2,1)} %bitcast.50, s32[15360]{0:T(1024)S(1)} %broadcast_clamp_fusion), kind=kCustom, calls=%fused_computation | custom fusion | bytes 5959680 | tf_op jit(solution)/shard_map/jit(_take)/gather | solution.py:31
  66.6 0.0 slice-start
  66.6 6.9 %convert_reduce_fusion = f32[8,192,96]{2,1,0:T(8,128)S(1)} fusion(bf16[8,10,192,96]{3,2,1,0:T(8,128)(2,1)} %bitcast.51, pred[8,10,192]{2,1,0:T(8,128)(4,1)S(1)} %copy.18), kind=kLoop, calls=%fused_computation.2 | loop fusion | flops 4276224 | bytes 3554304 | tf_op jit(solution)/shard_map/reduce_sum | solution.py:34
  73.6 0.0 copy-start.7
  73.6 0.0 copy-start.8
  73.6 0.1 fusion.14
  73.7 0.0 slice-done
  73.7 0.9 reshape.157
  74.7 0.0 copy-start.3
  74.7 0.8 constant_dynamic-slice_fusion
  75.5 0.0 copy-start.4
  75.5 0.0 copy-start.6
  75.5 1.3 copy.23
  76.8 0.0 copy-done.7
  76.8 0.0 copy-done.8
  76.8 1.8 bitcast_convert_fusion
  78.6 0.0 reduce-scatter.2.cloned.1.call-update
  78.6 0.0 all-gather.2.cloned.1.call-start
  79.3 67.0 %reduce-scatter.2.cloned.1.call-done = bf16[1,192,512]{2,1,0:T(8,128)(2,1)} async-done(((bf16[8,192,512]{2,1,0:T(8,128)(2,1)}), bf16[1,192,512]{2,1,0:T(8,128)(2,1)}) %reduce-scatter.2.cloned.1.call-update) | async-done | bytes 196624 | tf_op jit(solution)/shard_map/reduce_scatter | solution.py:41
  146.3 0.0 copy-done.3
  146.3 1.7 fusion.13
  148.0 0.0 all-gather.2.cloned.1.call-update
  148.0 0.0 copy-done.4
  148.1 0.0 copy-done.6
  148.1 0.1 copy.20
  148.2 0.1 reshape.158
  148.3 1.7 fusion.9
  150.0 43.0 %all-gather.2.cloned.1.call-done = bf16[3072,512]{1,0:T(8,128)(2,1)} async-done(((bf16[192,512]{1,0:T(8,128)(2,1)}), bf16[3072,512]{1,0:T(8,128)(2,1)}) %all-gather.2.cloned.1.call-update) | async-done | bytes 3145744 | tf_op jit(solution)/shard_map/all_gather | solution.py:50
  193.0 6.3 %gather_fusion.1 = bf16[1024,512]{1,0:T(8,128)(2,1)S(1)} fusion(bf16[3072,512]{1,0:T(8,128)(2,1)} %all-gather.2.cloned.1.call-done, s32[1024]{0:T(1024)S(1)} %broadcast_clamp_fusion.1), kind=kCustom, calls=%fused_computation.1 | custom fusion | bytes 2101248 | tf_op jit(solution)/shard_map/jit(_take)/gather | solution.py:52
  199.3 0.0 copy-start.1
  199.3 0.0 copy-start.5
  199.3 1.2 copy_select_fusion
  200.5 0.1 convert_reduce_fusion.1
  200.7 0.0 copy-done
  200.7 0.2 fusion.17
  200.9 0.0 copy-done.1
  200.9 0.0 copy-done.5
  200.9 0.8 fusion.2
  (7 shorter events, 0.1 us)
Async XLA Ops:
  7.2 193.5 %copy-start = (bf16[512,512]{1,0:T(8,128)(2,1)S(1)}, bf16[512,512]{1,0:T(8,128)(2,1)}, u32[]{:S(2)}) copy-start(bf16[512,512]{1,0:T(8,128)(2,1)} %param.19) | copy-start | bytes 1572868
  7.2 4.6 %copy-start.2 = (s32[8,1,10,192]{3,1,2,0:T(1,128)S(1)}, s32[8,1,10,192]{3,1,2,0:T(1,128)}, u32[]{:S(2)}) copy-start(s32[8,1,10,192]{3,1,2,0:T(1,128)} %param.12) | copy-start | bytes 184324
  7.2 139.1 %reduce-scatter.2.cloned.1.call-start = ((), (), s32[]{:S(2)}) async-start(), calls=%async_computation.1 | async-start | bytes 1769472 | tf_op jit(solution)/shard_map/reduce_scatter | solution.py:41
  66.6 7.1 %slice-start = ((bf16[96,12288]{1,0:T(8,128)(2,1)}), bf16[96,3072]{1,0:T(8,128)(2,1)S(1)}, s32[]{:S(2)}) async-start(bf16[96,12288]{1,0:T(8,128)(2,1)} %param.11), calls=%async_computation.3 | async-start | bytes 1179648 | tf_op jit(solution)/shard_map/slice | solution.py:28
  73.6 3.2 %copy-start.7 = (bf16[96,512]{1,0:T(8,128)(2,1)S(1)}, bf16[96,512]{1,0:T(8,128)(2,1)}, u32[]{:S(2)}) copy-start(bf16[96,512]{1,0:T(8,128)(2,1)} %param.17) | copy-start | bytes 294916
  73.6 3.2 %copy-start.8 = (bf16[96,512]{1,0:T(8,128)(2,1)S(1)}, bf16[96,512]{1,0:T(8,128)(2,1)}, u32[]{:S(2)}) copy-start(bf16[96,512]{1,0:T(8,128)(2,1)} %param.16) | copy-start | bytes 294916
  74.7 71.6 %copy-start.3 = (f32[512]{0:T(512)S(1)}, f32[512]{0:T(512)}, u32[]{:S(2)}) copy-start(f32[512]{0:T(512)} %param.18) | copy-start | bytes 6148
  75.5 72.5 %copy-start.4 = (s32[64,15]{0,1:T(8,128)S(1)}, s32[64,15]{0,1:T(8,128)}, u32[]{:S(2)}) copy-start(s32[64,15]{0,1:T(8,128)} %param.15) | copy-start | bytes 11524
  75.5 72.5 %copy-start.6 = (s32[64]{0:T(128)S(1)}, s32[64]{0:T(128)}, u32[]{:S(2)}) copy-start(s32[64]{0:T(128)} %param.14) | copy-start | bytes 772
  78.6 114.3 %all-gather.2.cloned.1.call-start = ((), (), s32[]{:S(2)}) async-start(), calls=%async_computation.2 | async-start | bytes 3342336 | tf_op jit(solution)/shard_map/all_gather | solution.py:50
  199.3 1.6 copy-start.1
  199.3 1.6 copy-start.5
Sparse Core Ops, SparseCore 0:
  78.8 67.5 reduce-scatter.1
  148.8 44.0 all-gather.1
where the time goes:
time: 209 us
  waiting for transfers between devices  110 us (53%)
  local copies, waits for them, and re-layouts  68.6 us (33%)
  between operations  15 us (7%)
  other arithmetic  12.1 us (6%)
  matrix products  2.83 us (1%)
    reduce_scatter x1, waiting for transfers between devices, body(): lax.psum_scatter(partial_value.astype(jnp.bfloat16), 'feat', scatter_dime...  67 us
    gather x1, local copies, waits for them, and re-layouts, body(): jnp.take(node_major, nbr_one[:, 0].reshape(-1), axis=0)  54.3 us
    all_gather x1, waiting for transfers between devices, body(): table = lax.all_gather(hidden, ('feat', 'rep'), axis=0, tiled=True)  43 us
    reduce_sum x1, other arithmetic, body(): jnp.sum(picked.astype(jnp.float32), axis=1) / fanout_one  6.94 us
    gather x1, local copies, waits for them, and re-layouts, body(): jnp.take(table, wanted, axis=0).reshape(seed_count, fanout_two + 1, width)  6.28 us
    unnamed x20, local copies, waits for them, and re-layouts  5.9 us
  transfers between devices with their start and end apart: 2, of which 2 were waited for; matrix products, arithmetic and copies ran while one was open for 1% of the time, Pallas kernels for 0%

commit v1 on v0

v1 whole, which is shorter than its diff:
```python
import functools

import jax
import jax.numpy as jnp
from jax import lax
from jax.experimental import pallas as pl
from jax.experimental.pallas import tpu as pltpu
from jax.sharding import PartitionSpec as P

LANES = 128
VMEM_LIMIT = 50 * 1024 * 1024


def folds(fslice, pcap):
    return 4 * fslice == 3 * LANES and pcap % 64 == 0


def lookup_kernel(n_feat, n_rep, fanout, pcap, nbr_ref, src_ref, out_ref, table, total):
    fslice, nodes = src_ref.shape
    rep_pos = lax.axis_index("rep")
    width = 512

    def turn(step, carry):
        at = pl.multiple_of(step * width, width)
        block = src_ref[:, pl.ds(at, width)].astype(jnp.float32)
        table[pl.ds(at, width), :fslice] = block.T
        return carry

    lax.fori_loop(0, nodes // width, turn, 0)

    def partition(p, carry):
        first = p * (fanout * pcap)

        def group(g, inner):
            at = pl.multiple_of(g * 8, 8)
            for u in range(8):
                rows = [
                    table[pl.ds(nbr_ref[first + k * pcap + at + u], 1), :] for k in range(fanout)
                ]
                while len(rows) > 1:
                    rows = [a + b for a, b in zip(rows[::2], rows[1::2])] + (
                        [rows[-1]] if len(rows) % 2 else []
                    )
                total[pl.ds(at + u, 1), :] = rows[0]
            return inner

        lax.fori_loop(0, pcap // 8, group, 0)
        own_at = pl.multiple_of((p * n_rep + rep_pos) * pcap, 64)
        own = table[pl.ds(own_at, pcap), :]
        mean = total[...] / fanout
        if folds(fslice, pcap):
            lane = lax.broadcasted_iota(jnp.int32, (pcap, LANES), 1)
            turned = pltpu.roll(mean, fslice, 1)
            left = jnp.where(lane < fslice, own, turned)
            cut = pcap // 4 * 3
            part = pcap // 4
            tail_left = left[cut:]
            tail_right = turned[cut:]
            extra = jnp.concatenate(
                [pltpu.roll(tail_left, 64, 1), tail_left, pltpu.roll(tail_right, 64, 1)], axis=0
            )
            right = jnp.where(lane[:cut] < 64, turned[:cut], extra)
            out_ref[p, :, :LANES] = left[:cut].astype(jnp.bfloat16)
            out_ref[p, :, LANES:] = right.astype(jnp.bfloat16)
        else:
            out_ref[p, :, :fslice] = own[:, :fslice].astype(jnp.bfloat16)
            out_ref[p, :, fslice:] = mean[:, :fslice].astype(jnp.bfloat16)
        return carry

    lax.fori_loop(0, n_feat, partition, 0)


def count_kernel(pcap, idx_ref, out_ref):
    base = (lax.axis_index("feat") * lax.axis_size("rep") + lax.axis_index("rep")) * pcap
    seeds, columns = idx_ref.shape
    block = 256

    def rows(step, carry):
        at = pl.multiple_of(step * block, block)
        idx = idx_ref[pl.ds(at, block), :] - base
        slot = lax.broadcasted_iota(jnp.int32, (block, pcap), 1)
        own = jnp.where(slot == idx[:, :1], 1.0, 0.0)
        near = jnp.zeros((block, pcap), jnp.float32)
        for k in range(1, columns):
            near = near + jnp.where(slot == idx[:, k : k + 1], 1.0, 0.0)
        out_ref[0, pl.ds(at, block), :] = own.astype(jnp.bfloat16)
        out_ref[1, pl.ds(at, block), :] = near.astype(jnp.bfloat16)
        return carry

    lax.fori_loop(0, seeds // block, rows, 0)


def layer_kernel(
    pcap, fanout_two, count_ref, got_ref, w_ref, bias_ref, ws_ref, wn_ref, times_ref, hidden_ref, part_ref
):
    n_feat, _, _ = got_ref.shape
    width = w_ref.shape[2]
    pre = jnp.zeros((pcap, width), jnp.float32)
    for f in range(n_feat):
        block = got_ref[f]
        weight = w_ref[f]
        if block.shape[0] != pcap:
            cut = block.shape[0]
            part = cut // 3
            tail = block[:, LANES:].astype(jnp.float32)
            lane = lax.broadcasted_iota(jnp.int32, (part, LANES), 1)
            turned = pltpu.roll(tail, 64, 1)
            low_left = jnp.where(lane < 64, turned[:part], tail[part : 2 * part])
            left = jnp.concatenate([block[:, :LANES], low_left.astype(jnp.bfloat16)], axis=0)
            right = jnp.concatenate([tail, turned[2 * part :]], axis=0).astype(jnp.bfloat16)
            pre = pre + jnp.dot(left, weight[:LANES], preferred_element_type=jnp.float32)
            pre = pre + jnp.dot(right[:, :64], weight[LANES:], preferred_element_type=jnp.float32)
        else:
            pre = pre + jnp.dot(block, weight, preferred_element_type=jnp.float32)
    live = lax.broadcasted_iota(jnp.int32, (pcap, width), 0) < count_ref[0, 0]
    hidden = jnp.where(live, jnp.maximum(pre + bias_ref[...], 0.0), 0.0).astype(jnp.bfloat16)
    hidden_ref[...] = hidden
    own = jnp.dot(hidden, ws_ref[...], preferred_element_type=jnp.float32).astype(jnp.bfloat16)
    near = (
        jnp.dot(hidden, wn_ref[...], preferred_element_type=jnp.float32) / fanout_two
    ).astype(jnp.bfloat16)
    block = 256

    def rows(step, carry):
        at = pl.multiple_of(step * block, block)
        value = jnp.dot(
            times_ref[0, pl.ds(at, block), :], own, preferred_element_type=jnp.float32
        ) + jnp.dot(times_ref[1, pl.ds(at, block), :], near, preferred_element_type=jnp.float32)
        part_ref[pl.ds(at, block), :] = value.astype(jnp.bfloat16)
        return carry

    lax.fori_loop(0, part_ref.shape[0] // block, rows, 0)


def body(
    src_feats,
    nbr_one,
    counts,
    seed_rows,
    nbr_two,
    w1_self,
    w1_nbr,
    bias_one,
    w2_self,
    w2_nbr,
    bias_two,
):
    n_feat = lax.axis_size("feat")
    n_rep = lax.axis_size("rep")
    fslice, nodes = src_feats.shape
    fanout_one, pcap = nbr_one.shape[2:]
    width = w1_self.shape[1]
    seed_count, fanout_two = nbr_two.shape
    seeds = seed_count * n_feat * n_rep
    params = pltpu.CompilerParams(vmem_limit_bytes=VMEM_LIMIT)
    vmem = pl.BlockSpec(memory_space=pltpu.VMEM)
    smem = pl.BlockSpec(memory_space=pltpu.SMEM)

    weights = lax.all_gather(jnp.concatenate([w1_self, w1_nbr], axis=0), "feat", axis=0)
    wanted = jnp.concatenate([seed_rows[:, None], nbr_two], axis=1)
    wanted = lax.all_gather(wanted, ("feat", "rep"), axis=0, tiled=True)

    sent_shape = (pcap // 4 * 3, 2 * LANES) if folds(fslice, pcap) else (pcap, 2 * fslice)
    sent = pl.pallas_call(
        functools.partial(lookup_kernel, n_feat, n_rep, fanout_one, pcap),
        out_shape=jax.ShapeDtypeStruct((n_feat, *sent_shape), jnp.bfloat16),
        in_specs=[smem, vmem],
        out_specs=vmem,
        scratch_shapes=[
            pltpu.VMEM((nodes, LANES), jnp.float32),
            pltpu.VMEM((pcap, LANES), jnp.float32),
        ],
        compiler_params=params,
        name="lookup",
    )(nbr_one.reshape(-1), src_feats)
    got = lax.all_to_all(sent, "feat", 0, 0, tiled=True)

    times = pl.pallas_call(
        functools.partial(count_kernel, pcap),
        out_shape=jax.ShapeDtypeStruct((2, seeds, pcap), jnp.bfloat16),
        in_specs=[vmem],
        out_specs=vmem,
        compiler_params=params,
        name="times",
    )(wanted)

    hidden, partial_seed = pl.pallas_call(
        functools.partial(layer_kernel, pcap, fanout_two),
        out_shape=(
            jax.ShapeDtypeStruct((pcap, width), jnp.bfloat16),
            jax.ShapeDtypeStruct((seeds, width), jnp.bfloat16),
        ),
        in_specs=[smem] + [vmem] * 6,
        out_specs=(vmem, vmem),
        compiler_params=params,
        name="layers",
    )(counts, got, weights, bias_one[None], w2_self, w2_nbr, times)

    parts = lax.all_to_all(
        partial_seed.reshape(n_feat * n_rep, seed_count, width), ("feat", "rep"), 0, 0, tiled=True
    )
    pre_two = jnp.sum(parts.astype(jnp.float32), axis=0) + bias_two
    seed_out = jnp.maximum(pre_two, 0.0).astype(jnp.bfloat16)
    return (hidden[None, None], seed_out)


def solution(mesh):
    placed = (
        P("feat", "groups"),
        P("groups", "rep", None, None),
        P(("groups", "feat"), "rep"),
        P(("groups", "feat", "rep")),
        P(("groups", "feat", "rep"), None),
        P("feat", None),
        P("feat", None),
        P(),
        P(),
        P(),
        P(),
    )
    return jax.shard_map(
        body,
        mesh=mesh,
        in_specs=placed,
        out_specs=(P(("groups", "feat"), "rep", None, None), P(("groups", "feat", "rep"), None)),
        check_vma=False,
    )
```

time: 209 us -> 121 us (0.58)
  waiting for transfers between devices: 110 us -> 0.04 us
  local copies, waits for them, and re-layouts: 68.6 us -> 1.98 us
  blocking collectives: 0 us -> 65.2 us
  Pallas kernels: 0 us -> 27.7 us
  other arithmetic: 12.1 us -> 3.53 us
  starting transfers between devices: 0.08 us -> 7.45 us
  matrix products: 2.83 us -> 0 us
    reduce_scatter x1 -> x0, waiting for transfers between devices: 67 us -> none  [body(): lax.psum_scatter(partial_value.astype(jnp.bfloat16), 'feat', scatter_dime...]
    gather x2 -> x0, local copies, waits for them, and re-layouts: 60.6 us -> none  [the longest x1 54.3 us: body(): jnp.take(node_major, nbr_one[:, 0].reshape(-1), axis=0)]
    all_gather x1, waiting for transfers between devices: 43 us -> 0.02 us  [body(): lax.all_gather(jnp.concatenate([w1_self, w1_nbr], axis=0), 'feat', axis=0)]
    all_gather x0 -> x1, blocking collectives: none -> 34.9 us  [body(): wanted = lax.all_gather(wanted, ('feat', 'rep'), axis=0, tiled=True)]
    all_to_all x0 -> x1, blocking collectives: none -> 30.2 us  [body(): lax.all_to_all(partial_seed.reshape(n_feat * n_rep, seed_count, width), (...]
    pallas_call x0 -> x3, Pallas kernels: none -> 27.7 us  [the longest x1 20.7 us: body(): pl.pallas_call(functools.partial(lookup_kernel, n_feat, n_rep, fanout_one...]
    all_to_all x0 -> x1, starting transfers between devices: none -> 7.41 us  [body(): got = lax.all_to_all(sent, 'feat', 0, 0, tiled=True)]
    reduce_sum x2 -> x1, other arithmetic: 7.08 us -> 0.15 us  [body(): pre_two = jnp.sum(parts.astype(jnp.float32), axis=0) + bias_two]
  transfers between devices with their start and end apart: 2 -> 2, of which waited for: 2 -> 0; matrix products, arithmetic and copies ran while one was open for 1% -> 1% of each run, Pallas kernels for 0% -> 19%
where the time goes in v1:
time: 121 us
  blocking collectives  65.2 us (54%)
  Pallas kernels  27.7 us (23%)
  between operations  14.8 us (12%)
  starting transfers between devices  7.45 us (6%)
  other arithmetic  3.53 us (3%)
  local copies, waits for them, and re-layouts  1.98 us (2%)
    all_gather x1, blocking collectives, body(): wanted = lax.all_gather(wanted, ('feat', 'rep'), axis=0, tiled=True)  34.9 us
    all_to_all x1, blocking collectives, body(): lax.all_to_all(partial_seed.reshape(n_feat * n_rep, seed_count, width), (...  30.2 us
    pallas_call x1, Pallas kernels, body(): pl.pallas_call(functools.partial(lookup_kernel, n_feat, n_rep, fanout_one...  20.7 us
    all_to_all x1, starting transfers between devices, body(): got = lax.all_to_all(sent, 'feat', 0, 0, tiled=True)  7.41 us
    pallas_call x1, Pallas kernels, body(): pl.pallas_call(functools.partial(layer_kernel, pcap, fanout_two), out_sha...  4.22 us
    pallas_call x1, Pallas kernels, body(): pl.pallas_call(functools.partial(count_kernel, pcap), out_shape=jax.Shape...  2.77 us
  transfers between devices with their start and end apart: 2, of which 0 were waited for; matrix products, arithmetic and copies ran while one was open for 1% of the time, Pallas kernels for 19%

profile of v1, /device:TPU:0, one launch (start us, length us, event | category | flops | bytes accessed | tf_op | source)
XLA Modules:
  0.0 120.7 jit_solution(3498969804312928429)
XLA Ops:
  7.2 0.0 all-gather.4.cloned.1.call-start
  7.2 1.6 %pad_maximum_fusion = bf16[192,512]{1,0:T(8,128)(2,1)} fusion(bf16[96,512]{1,0:T(8,128)(2,1)} %param.17, bf16[96,512]{1,0:T(8,128)(2,1)} %param.16), kind=kLoop, calls=%fused_computation.1 | loop fusion | flops 393216 | bytes 393216 | tf_op jit(solution)/shard_map/concatenate | solution.py:159
  8.8 0.0 all-gather.4.cloned.1.call-update
  8.9 1.1 reduce
  10.0 0.1 reshape.11.nbr_ref
  10.1 0.0 copy-start
  10.1 1.7 %copy-done = bf16[96,12288]{1,0:T(8,128)(2,1)S(1)} copy-done((bf16[96,12288]{1,0:T(8,128)(2,1)S(1)}, bf16[96,12288]{1,0:T(8,128)(2,1)}, u32[]{:S(2)}) %copy-start) | copy-done | bytes 2359320
  11.7 0.0 copy-start.4
  11.7 0.0 copy-start.6
  11.7 20.7 %lookup.1 = bf16[8,144,256]{2,1,0:T(8,128)(2,1)} custom-call(s32[15360]{0:T(1024)S(1)} %reshape.11.nbr_ref, bf16[96,12288]{1,0:T(8,128)(2,1)S(1)} %copy-done), custom_call_target="tpu_custom_call" | custom-call | tf_op jit(solution)/shard_map/lookup/pallas_call | solution.py:164
  32.5 0.0 copy-start.1
  32.5 0.0 copy-start.2
  32.5 0.0 copy-start.3
  32.5 7.4 %all-to-all-start = ((bf16[8,144,256]{2,1,0:T(8,128)(2,1)}), bf16[8,144,256]{2,1,0:T(8,128)(2,1)S(1)}, u32[]{:S(2)}, u32[]{:S(2)}) async-start(bf16[8,144,256]{2,1,0:T(8,128)(2,1)} %lookup.1), calls=%async_computation | async-start | bytes 1179648 | tf_op jit(solution)/shard_map/all_to_all | solution.py:176
  40.5 0.0 copy-done.4
  40.5 0.0 copy-done.6
  40.6 34.9 %all-gather.1 = s32[16,64,16]{1,2,0:T(8,128)S(1)} all-gather(s32[1,64,16]{1,2,0:T(8,128)S(1)} %add_bitcast_fusion), channel_id=1, replica_groups=mesh['groups'=2,'feat'=8,'rep'=2] {'feat','rep'}, dimensions={0}, use_global_device_ids=true | all-gather | bytes 69632 | tf_op jit(solution)/shard_map/all_gather | solution.py:161
  75.5 0.2 copy.14
  75.7 2.8 %times.1.times_ref = bf16[2,1024,192]{2,1,0:T(8,128)(2,1)S(1)} custom-call(s32[1024,16]{1,0:T(8,128)S(1)} %bitcast.8), custom_call_target="tpu_custom_call" | custom-call | tf_op jit(solution)/shard_map/times/pallas_call | solution.py:178
  78.5 0.0 all-to-all-done.got_ref
  78.5 0.0 all-gather.4.cloned.1.call-done
  78.5 0.0 copy-done.1
  78.5 0.0 copy-done.2
  78.6 0.0 copy-done.3
  78.6 4.2 %layers.1 = (bf16[192,512]{1,0:T(8,128)(2,1)}, bf16[1024,512]{1,0:T(8,128)(2,1)S(1)}) custom-call(s32[1,1]{1,0:T(1,128)S(6)} %copy.15.count_ref, bf16[8,144,256]{2,1,0:T(8,128)(2,1)S(1)} %all-to-all-done.got_ref, bf16[8,192,512]{2,1,0:T(8,128)(2,1)} %bitcast.11, f32[1,512]{1,0:T(1,128)S(1)} %bitcast.10, bf16[512,512]{1,0:T(8,128)(2,1)S(1)} %copy-done.1, ...), custom_call_target="tpu_custom_call" | custom-call | tf_op jit(solution)/shard_map/layers/pallas_call | solution.py:187
  82.8 0.0 copy-start.5
  82.8 30.2 %all_to_all.10 = bf16[16,64,512]{2,1,0:T(8,128)(2,1)S(1)} all-to-all(bf16[16,64,512]{2,1,0:T(8,128)(2,1)S(1)} %bitcast.9), channel_id=1, replica_groups=mesh['groups'=2,'feat'=8,'rep'=2] {'feat','rep'}, dimensions={0} | all-to-all | bytes 2097152 | tf_op jit(solution)/shard_map/all_to_all | solution.py:199
  113.0 0.1 convert_reduce_fusion
  113.2 0.0 copy-done.5
  113.2 0.6 maximum_convert_fusion
  (1 shorter events, 0.0 us)
Async XLA Ops:
  7.2 71.4 %all-gather.4.cloned.1.call-start = ((), (), s32[]{:S(2)}) async-start(), calls=%async_computation.2 | async-start | bytes 1769472 | tf_op jit(solution)/shard_map/all_gather | solution.py:159
  10.1 1.7 %copy-start = (bf16[96,12288]{1,0:T(8,128)(2,1)S(1)}, bf16[96,12288]{1,0:T(8,128)(2,1)}, u32[]{:S(2)}) copy-start(bf16[96,12288]{1,0:T(8,128)(2,1)} %src_ref.1) | copy-start | bytes 7077892
  11.7 28.8 %copy-start.4 = (s32[64,15]{0,1:T(8,128)S(1)}, s32[64,15]{0,1:T(8,128)}, u32[]{:S(2)}) copy-start(s32[64,15]{0,1:T(8,128)} %param.15) | copy-start | bytes 11524
  11.7 28.8 %copy-start.6 = (s32[64]{0:T(128)S(1)}, s32[64]{0:T(128)}, u32[]{:S(2)}) copy-start(s32[64]{0:T(128)} %param.14) | copy-start | bytes 772
  32.5 46.1 %copy-start.1 = (bf16[512,512]{1,0:T(8,128)(2,1)S(1)}, bf16[512,512]{1,0:T(8,128)(2,1)}, u32[]{:S(2)}) copy-start(bf16[512,512]{1,0:T(8,128)(2,1)} %ws_ref.1) | copy-start | bytes 1572868
  32.5 46.1 %copy-start.2 = (bf16[512,512]{1,0:T(8,128)(2,1)S(1)}, bf16[512,512]{1,0:T(8,128)(2,1)}, u32[]{:S(2)}) copy-start(bf16[512,512]{1,0:T(8,128)(2,1)} %wn_ref.1) | copy-start | bytes 1572868
  32.5 46.1 %copy-start.3 = (f32[512]{0:T(512)S(1)}, f32[512]{0:T(512)}, u32[]{:S(2)}) copy-start(f32[512]{0:T(512)} %param.18) | copy-start | bytes 6148
  32.5 46.0 %all-to-all-start = ((bf16[8,144,256]{2,1,0:T(8,128)(2,1)}), bf16[8,144,256]{2,1,0:T(8,128)(2,1)S(1)}, u32[]{:S(2)}, u32[]{:S(2)}) async-start(bf16[8,144,256]{2,1,0:T(8,128)(2,1)} %lookup.1), calls=%async_computation | async-start | bytes 1179648 | tf_op jit(solution)/shard_map/all_to_all | solution.py:176
  82.8 30.4 %copy-start.5 = (f32[512]{0:T(512)S(1)}, f32[512]{0:T(512)}, u32[]{:S(2)}) copy-start(f32[512]{0:T(512)} %param.21) | copy-start | bytes 6148
Sparse Core Ops, SparseCore 0:
  10.8 57.3 all-gather.3

commit v2 on v1

v2 whole, which is shorter than its diff:
```python
import functools

import jax
import jax.numpy as jnp
from jax import lax
from jax.experimental import pallas as pl
from jax.experimental.pallas import tpu as pltpu
from jax.sharding import PartitionSpec as P

LANES = 128
MIB = 1024 * 1024


def folds(fslice, pcap):
    return 4 * fslice == 3 * LANES and pcap % 64 == 0


def turn_kernel(src_ref, table_ref):
    fslice, nodes = src_ref.shape
    width = 512

    def turn(step, carry):
        at = pl.multiple_of(step * width, width)
        table_ref[pl.ds(at, width), :fslice] = src_ref[:, pl.ds(at, width)].astype(jnp.float32).T
        return carry

    lax.fori_loop(0, nodes // width, turn, 0)


def mean_kernel(steps, n_rep, fanout, pcap, fslice, nbr_ref, table_ref, *refs):
    out_refs, total = refs[:-1], refs[-1]
    feat_pos = lax.axis_index("feat")
    rep_pos = lax.axis_index("rep")
    for step, out_ref in zip(steps, out_refs):
        p = jnp.bitwise_xor(feat_pos, step)
        first = p * (fanout * pcap)

        def group(g, carry):
            at = pl.multiple_of(g * 8, 8)
            for u in range(8):
                rows = [
                    table_ref[pl.ds(nbr_ref[first + k * pcap + at + u], 1), :]
                    for k in range(fanout)
                ]
                while len(rows) > 1:
                    rows = [a + b for a, b in zip(rows[::2], rows[1::2])] + (
                        [rows[-1]] if len(rows) % 2 else []
                    )
                total[pl.ds(at + u, 1), :] = rows[0]
            return carry

        lax.fori_loop(0, pcap // 8, group, 0)
        own_at = pl.multiple_of((p * n_rep + rep_pos) * pcap, 64)
        own = table_ref[pl.ds(own_at, pcap), :]
        mean = total[...] / fanout
        if folds(fslice, pcap):
            lane = lax.broadcasted_iota(jnp.int32, (pcap, LANES), 1)
            turned = pltpu.roll(mean, fslice, 1)
            left = jnp.where(lane < fslice, own, turned)
            cut = pcap // 4 * 3
            tail_left = left[cut:]
            tail_right = turned[cut:]
            extra = jnp.concatenate(
                [pltpu.roll(tail_left, 64, 1), tail_left, pltpu.roll(tail_right, 64, 1)], axis=0
            )
            right = jnp.where(lane[:cut] < 64, turned[:cut], extra)
            out_ref[:, :LANES] = left[:cut].astype(jnp.bfloat16)
            out_ref[:, LANES:] = right.astype(jnp.bfloat16)
        else:
            out_ref[:, :fslice] = own[:, :fslice].astype(jnp.bfloat16)
            out_ref[:, fslice:] = mean[:, :fslice].astype(jnp.bfloat16)


def prepare_kernel(fslice, pcap, seed_count, n_idx, mine_ref, other_ref, w_ref, own_ref, near_ref):
    n_feat = mine_ref.shape[0]
    rep_pos = lax.axis_index("rep")
    base = (lax.axis_index("feat") * lax.axis_size("rep") + rep_pos) * pcap
    base = base.astype(jnp.float32)
    pair = 2 * seed_count
    slot = lax.broadcasted_iota(jnp.int32, (pcap, pair), 0).astype(jnp.float32)
    low = lax.broadcasted_iota(jnp.int32, (n_idx, pair), 1) < seed_count
    for half, ref in enumerate((mine_ref, other_ref)):
        for s in range(n_feat):
            w_ref[s, rep_pos if half == 0 else 1 - rep_pos] = ref[s, :fslice]
        for s in range(0, n_feat, 2):
            first = ref[s, fslice : fslice + n_idx, :pair].astype(jnp.float32)
            second = ref[s + 1, fslice : fslice + n_idx, :pair].astype(jnp.float32)
            high_part = jnp.where(low, first, pltpu.roll(second, seed_count, 1))
            low_part = jnp.where(low, pltpu.roll(first, seed_count, 1), second)
            row = high_part * 128.0 + low_part - base
            own = jnp.where(slot == row[:1], 1.0, 0.0)
            near = jnp.zeros((pcap, pair), jnp.float32)
            for k in range(1, n_idx):
                near = near + jnp.where(slot == row[k : k + 1], 1.0, 0.0)
            place = pl.ds(s * seed_count, pair)
            own_ref[half, place, :] = own.T.astype(jnp.bfloat16)
            near_ref[half, place, :] = near.T.astype(jnp.bfloat16)


def layer_kernel(fanout_two, n_feat, *refs):
    count_ref = refs[0]
    got_refs = refs[1 : 1 + n_feat]
    w_ref, bias_ref, ws_ref, wn_ref, own_ref, near_ref = refs[1 + n_feat : 7 + n_feat]
    hidden_ref, value_ref, part_ref = refs[7 + n_feat :]
    pcap, width = hidden_ref.shape
    fslice = w_ref.shape[2]
    pre = jnp.zeros((pcap, width), jnp.float32)
    for f, got_ref in enumerate(got_refs):
        block = got_ref[...]
        weight = w_ref[f].reshape(2 * fslice, width)
        if block.shape[0] != pcap:
            part = block.shape[0] // 3
            tail = block[:, LANES:].astype(jnp.float32)
            lane = lax.broadcasted_iota(jnp.int32, (part, LANES), 1)
            turned = pltpu.roll(tail, 64, 1)
            low_left = jnp.where(lane < 64, turned[:part], tail[part : 2 * part])
            left = jnp.concatenate([block[:, :LANES], low_left.astype(jnp.bfloat16)], axis=0)
            right = jnp.concatenate([tail, turned[2 * part :]], axis=0).astype(jnp.bfloat16)
            pre = pre + jnp.dot(left, weight[:LANES], preferred_element_type=jnp.float32)
            pre = pre + jnp.dot(right[:, :64], weight[LANES:], preferred_element_type=jnp.float32)
        else:
            pre = pre + jnp.dot(block, weight, preferred_element_type=jnp.float32)
    live = lax.broadcasted_iota(jnp.int32, (pcap, width), 0) < count_ref[0, 0]
    hidden = jnp.where(live, jnp.maximum(pre + bias_ref[...], 0.0), 0.0).astype(jnp.bfloat16)
    hidden_ref[...] = hidden
    value_ref[0] = jnp.dot(hidden, ws_ref[...], preferred_element_type=jnp.float32).astype(
        jnp.bfloat16
    )
    value_ref[1] = (
        jnp.dot(hidden, wn_ref[...], preferred_element_type=jnp.float32) / fanout_two
    ).astype(jnp.bfloat16)
    part_ref[...] = (
        jnp.dot(own_ref[1], value_ref[0], preferred_element_type=jnp.float32)
        + jnp.dot(near_ref[1], value_ref[1], preferred_element_type=jnp.float32)
    ).astype(jnp.bfloat16)


def share_kernel(own_ref, near_ref, value_ref, got_ref, *out_refs):
    rows = out_refs[0].shape[0]
    for s, out_ref in enumerate(out_refs):
        place = pl.ds(s * rows, rows)
        out_ref[...] = (
            jnp.dot(own_ref[0, place, :], value_ref[0], preferred_element_type=jnp.float32)
            + jnp.dot(near_ref[0, place, :], value_ref[1], preferred_element_type=jnp.float32)
            + got_ref[place, :].astype(jnp.float32)
        ).astype(jnp.bfloat16)


def swap(value, axis, step):
    size = lax.axis_size(axis)
    return lax.ppermute(value, axis, [(i, i ^ step) for i in range(size)])


def body(
    src_feats,
    nbr_one,
    counts,
    seed_rows,
    nbr_two,
    w1_self,
    w1_nbr,
    bias_one,
    w2_self,
    w2_nbr,
    bias_two,
):
    n_feat = lax.axis_size("feat")
    n_rep = lax.axis_size("rep")
    fslice, nodes = src_feats.shape
    fanout_one, pcap = nbr_one.shape[2:]
    width = w1_self.shape[1]
    seed_count, fanout_two = nbr_two.shape
    n_idx = fanout_two + 1
    bf16 = jnp.bfloat16
    vmem = pl.BlockSpec(memory_space=pltpu.VMEM)
    smem = pl.BlockSpec(memory_space=pltpu.SMEM)
    table_bytes = nodes * LANES * 4

    def call(kernel, name, shapes, ins, args, scratch=(), limit=16 * MIB):
        return pl.pallas_call(
            kernel,
            out_shape=tuple(jax.ShapeDtypeStruct(shape, dtype) for shape, dtype in shapes),
            in_specs=ins,
            out_specs=(vmem,) * len(shapes),
            scratch_shapes=scratch,
            compiler_params=pltpu.CompilerParams(vmem_limit_bytes=limit),
            name=name,
        )(*args)

    rows = jnp.concatenate([seed_rows[None], nbr_two.T], axis=0)
    digits = jnp.concatenate([rows // 128, rows % 128], axis=1).astype(bf16)
    digits = jnp.pad(digits, ((0, 0), (0, width - 2 * seed_count)))
    half = jnp.where(lax.axis_index("rep") == 0, w1_self, w1_nbr)
    parcel = jnp.concatenate([half, digits], axis=0)
    parcels = [parcel] + [swap(parcel, "feat", s) for s in range(1, n_feat)]

    (table,) = call(
        turn_kernel,
        "turn",
        [((nodes, LANES), jnp.float32)],
        [vmem],
        (src_feats,),
        limit=table_bytes + 12 * MIB,
    )
    neighbors = nbr_one.reshape(-1)
    sent_shape = (pcap // 4 * 3, 2 * LANES) if folds(fslice, pcap) else (pcap, 2 * fslice)
    far = list(range(n_feat // 2, n_feat))
    close = list(range(1, n_feat // 2)) + [0]
    got = [None] * n_feat
    for steps in (far, close):
        sent = call(
            functools.partial(mean_kernel, steps, n_rep, fanout_one, pcap, fslice),
            "mean",
            [(sent_shape, bf16)] * len(steps),
            [smem, vmem],
            (neighbors, table),
            scratch=[pltpu.VMEM((pcap, LANES), jnp.float32)],
            limit=table_bytes + 8 * MIB,
        )
        for step, chunk in zip(steps, sent):
            got[step] = swap(chunk, "feat", step) if step else chunk

    mine = jnp.stack(parcels)
    other = swap(mine, "rep", 1)
    weights, own_times, near_times = call(
        functools.partial(prepare_kernel, fslice, pcap, seed_count, n_idx),
        "prepare",
        [
            ((n_feat, n_rep, fslice, width), bf16),
            ((2, n_feat * seed_count, pcap), bf16),
            ((2, n_feat * seed_count, pcap), bf16),
        ],
        [vmem] * 2,
        (mine, other),
    )
    hidden, value, for_other = call(
        functools.partial(layer_kernel, fanout_two, n_feat),
        "layers",
        [
            ((pcap, width), bf16),
            ((2, pcap, width), bf16),
            ((n_feat * seed_count, width), bf16),
        ],
        [smem] + [vmem] * (n_feat + 6),
        (counts, *got, weights, bias_one[None], w2_self, w2_nbr, own_times, near_times),
    )
    from_other = swap(for_other, "rep", 1)
    shares = call(
        share_kernel,
        "share",
        [((seed_count, width), bf16)] * n_feat,
        [vmem] * 4,
        (own_times, near_times, value, from_other),
    )
    pre_two = bias_two
    for s, share in enumerate(shares):
        pre_two = pre_two + (swap(share, "feat", s) if s else share).astype(jnp.float32)
    seed_out = jnp.maximum(pre_two, 0.0).astype(bf16)
    return (hidden[None, None], seed_out)


def solution(mesh):
    placed = (
        P("feat", "groups"),
        P("groups", "rep", None, None),
        P(("groups", "feat"), "rep"),
        P(("groups", "feat", "rep")),
        P(("groups", "feat", "rep"), None),
        P("feat", None),
        P("feat", None),
        P(),
        P(),
        P(),
        P(),
    )
    return jax.shard_map(
        body,
        mesh=mesh,
        in_specs=placed,
        out_specs=(P(("groups", "feat"), "rep", None, None), P(("groups", "feat", "rep"), None)),
        check_vma=False,
    )
```

time: 121 us -> 93 us (0.77)
  blocking collectives: 65.2 us -> 0 us
  starting transfers between devices: 7.45 us -> 41.4 us
  waiting for transfers between devices: 0.04 us -> 19.6 us
  between operations: 14.8 us -> 1.53 us
  local copies, waits for them, and re-layouts: 1.98 us -> 0.18 us
    ppermute x0 -> x23, starting transfers between devices: none -> 41.4 us  [swap(): return lax.ppermute(value, axis, [(i, i ^ step) for i in range(size)])]
    all_gather x1 -> x0, blocking collectives: 34.9 us -> none  [body(): wanted = lax.all_gather(wanted, ('feat', 'rep'), axis=0, tiled=True)]
    all_to_all x1 -> x0, blocking collectives: 30.2 us -> none  [body(): lax.all_to_all(partial_seed.reshape(n_feat * n_rep, seed_count, width), (...]
    ppermute x0 -> x23, waiting for transfers between devices: none -> 19.6 us  [swap(): return lax.ppermute(value, axis, [(i, i ^ step) for i in range(size)])]
    all_to_all x1 -> x0, starting transfers between devices: 7.41 us -> none  [body(): got = lax.all_to_all(sent, 'feat', 0, 0, tiled=True)]
    unnamed x14 -> x18, local copies, waits for them, and re-layouts: 1.68 us -> 0.08 us
    concatenate x1 -> x2, other arithmetic: 1.63 us -> 0.09 us  [the longest x1 0.08 us: body(): digits = jnp.concatenate([rows // 128, rows % 128], axis=1).astype(bf16)]
    pallas_call x3 -> x6, Pallas kernels: 27.7 us -> 27.3 us  [call(): pl.pallas_call(kernel, out_shape=tuple((jax.ShapeDtypeStruct(shape, dtype...]
  transfers between devices with their start and end apart: 2 -> 23, of which waited for: 0 -> 7; matrix products, arithmetic and copies ran while one was open for 1% -> 0% of each run, Pallas kernels for 19% -> 27%
where the time goes in v2:
time: 93 us; the launch traced here: 92.8 us
  starting transfers between devices  41.4 us (45%)
  Pallas kernels  27.3 us (29%)
  waiting for transfers between devices  19.6 us (21%)
  other arithmetic  2.79 us (3%)
  between operations  1.53 us (2%)
    ppermute x23, starting transfers between devices, swap(): return lax.ppermute(value, axis, [(i, i ^ step) for i in range(size)])  41.4 us
    pallas_call x6, Pallas kernels, call(): pl.pallas_call(kernel, out_shape=tuple((jax.ShapeDtypeStruct(shape, dtype...  27.3 us
    ppermute x23, waiting for transfers between devices, swap(): return lax.ppermute(value, axis, [(i, i ^ step) for i in range(size)])  19.6 us
  transfers between devices with their start and end apart: 23, of which 7 were waited for; matrix products, arithmetic and copies ran while one was open for 0% of the time, Pallas kernels for 27%

profile of v2, /device:TPU:0, one launch (start us, length us, event | category | flops | bytes accessed | tf_op | source)
XLA Modules:
  0.0 92.8 jit_solution(6484711444193996832)
XLA Ops:
  0.6 0.0 copy-start.4
  0.6 0.0 copy-start
  0.7 0.9 fusion.3
  1.5 0.1 fusion.2
  1.6 0.9 broadcast_select_fusion
  2.5 3.0 %collective-permute-start.7 = (bf16[112,512]{1,0:T(8,128)(2,1)S(1)}, bf16[112,512]{1,0:T(8,128)(2,1)S(1)}, u32[]{:S(2)}, u32[]{:S(2)}) collective-permute-start(bf16[112,512]{1,0:T(8,128)(2,1)S(1)} %pad_maximum_fusion), channel_id=1, source_target_pairs={{0,2},{2,0},{4,6},{6,4},{8,10},{10,8},{12,14},{14,12},{1,3},{3,1},... | collective-permute-start | bytes 344072 | tf_op jit(solution)/shard_map/ppermute | solution.py:151
  5.6 1.6 %collective-permute-start.8 = (bf16[112,512]{1,0:T(8,128)(2,1)S(1)}, bf16[112,512]{1,0:T(8,128)(2,1)S(1)}, u32[]{:S(2)}, u32[]{:S(2)}) collective-permute-start(bf16[112,512]{1,0:T(8,128)(2,1)S(1)} %pad_maximum_fusion), channel_id=1, source_target_pairs={{0,4},{2,6},{4,0},{6,2},{8,12},{10,14},{12,8},{14,10},{1,5},{3,7},... | collective-permute-start | bytes 344072 | tf_op jit(solution)/shard_map/ppermute | solution.py:151
  7.1 0.0 collective-permute-start.9
  7.1 3.0 %collective-permute-start.10 = (bf16[112,512]{1,0:T(8,128)(2,1)S(1)}, bf16[112,512]{1,0:T(8,128)(2,1)S(1)}, u32[]{:S(2)}, u32[]{:S(2)}) collective-permute-start(bf16[112,512]{1,0:T(8,128)(2,1)S(1)} %pad_maximum_fusion), channel_id=1, source_target_pairs={{0,8},{2,10},{4,12},{6,14},{8,0},{10,2},{12,4},{14,6},{1,9},{3,11}... | collective-permute-start | bytes 344072 | tf_op jit(solution)/shard_map/ppermute | solution.py:151
  10.1 1.3 %collective-permute-start.11 = (bf16[112,512]{1,0:T(8,128)(2,1)S(1)}, bf16[112,512]{1,0:T(8,128)(2,1)S(1)}, u32[]{:S(2)}, u32[]{:S(2)}) collective-permute-start(bf16[112,512]{1,0:T(8,128)(2,1)S(1)} %pad_maximum_fusion), channel_id=1, source_target_pairs={{0,10},{2,8},{4,14},{6,12},{8,2},{10,0},{12,6},{14,4},{1,11},{3,9}... | collective-permute-start | bytes 344072 | tf_op jit(solution)/shard_map/ppermute | solution.py:151
  11.4 0.0 collective-permute-done.7
  11.4 3.7 %collective-permute-start.12 = (bf16[112,512]{1,0:T(8,128)(2,1)S(1)}, bf16[112,512]{1,0:T(8,128)(2,1)S(1)}, u32[]{:S(2)}, u32[]{:S(2)}) collective-permute-start(bf16[112,512]{1,0:T(8,128)(2,1)S(1)} %pad_maximum_fusion), channel_id=1, source_target_pairs={{0,12},{2,14},{4,8},{6,10},{8,4},{10,6},{12,0},{14,2},{1,13},{3,15... | collective-permute-start | bytes 344072 | tf_op jit(solution)/shard_map/ppermute | solution.py:151
  15.1 0.0 collective-permute-done.8
  15.1 0.2 collective-permute-start.13
  15.3 0.0 collective-permute-done.9
  15.3 0.3 collective-permute-done.10
  15.7 11.7 %collective-permute-done.11 = bf16[112,512]{1,0:T(8,128)(2,1)S(1)} collective-permute-done((bf16[112,512]{1,0:T(8,128)(2,1)S(1)}, bf16[112,512]{1,0:T(8,128)(2,1)S(1)}, u32[]{:S(2)}, u32[]{:S(2)}) %collective-permute-start.11) | collective-permute-done | bytes 114720 | tf_op jit(solution)/shard_map/ppermute | solution.py:151
  27.4 0.0 collective-permute-done.12
  27.5 0.0 collective-permute-done.13
  27.5 0.1 collective-permute-start.14
  27.6 0.0 copy-done.4
  27.6 0.2 reduce
  27.8 0.1 reshape.8.nbr_ref
  27.9 0.0 copy-done
  27.9 2.5 %turn.1.table_ref = f32[12288,128]{1,0:T(8,128)S(1)} custom-call(bf16[96,12288]{1,0:T(8,128)(2,1)S(1)} %copy-done), custom_call_target="tpu_custom_call" | custom-call | tf_op jit(solution)/shard_map/turn/pallas_call | solution.py:180
  30.4 9.9 %mean.2 = (bf16[144,256]{1,0:T(8,128)(2,1)S(1)}, bf16[144,256]{1,0:T(8,128)(2,1)S(1)}, bf16[144,256]{1,0:T(8,128)(2,1)S(1)}, bf16[144,256]{1,0:T(8,128)(2,1)S(1)}) custom-call(s32[15360]{0:T(1024)S(1)} %reshape.8.nbr_ref, f32[12288,128]{1,0:T(8,128)S(1)} %turn.1.table_ref), custom_call_target="tpu_custom_call" | custom-call | tf_op jit(solution)/shard_map/mean/pallas_call | solution.py:180
  40.3 0.9 collective-permute-start
  41.1 4.2 %collective-permute-start.1 = (bf16[144,256]{1,0:T(8,128)(2,1)S(1)}, bf16[144,256]{1,0:T(8,128)(2,1)S(1)}, u32[]{:S(2)}, u32[]{:S(2)}) collective-permute-start(bf16[144,256]{1,0:T(8,128)(2,1)S(1)} %get-tuple-element.26), channel_id=1, source_target_pairs={{0,4},{2,6},{4,0},{6,2},{8,12},{10,14},{12,8},{14,10},{1,5},{3,7},... | collective-permute-start | bytes 221192 | tf_op jit(solution)/shard_map/ppermute | solution.py:151
  45.4 1.0 %collective-permute-start.2 = (bf16[144,256]{1,0:T(8,128)(2,1)S(1)}, bf16[144,256]{1,0:T(8,128)(2,1)S(1)}, u32[]{:S(2)}, u32[]{:S(2)}) collective-permute-start(bf16[144,256]{1,0:T(8,128)(2,1)S(1)} %get-tuple-element.27), channel_id=1, source_target_pairs={{0,6},{2,4},{4,2},{6,0},{8,14},{10,12},{12,10},{14,8},{1,7},{3,5},... | collective-permute-start | bytes 221192 | tf_op jit(solution)/shard_map/ppermute | solution.py:151
  46.3 9.9 %mean.3 = (bf16[144,256]{1,0:T(8,128)(2,1)S(1)}, bf16[144,256]{1,0:T(8,128)(2,1)S(1)}, bf16[144,256]{1,0:T(8,128)(2,1)S(1)}, bf16[144,256]{1,0:T(8,128)(2,1)S(1)}) custom-call(s32[15360]{0:T(1024)S(1)} %reshape.8.nbr_ref, f32[12288,128]{1,0:T(8,128)S(1)} %turn.1.table_ref), custom_call_target="tpu_custom_call" | custom-call | tf_op jit(solution)/shard_map/mean/pallas_call | solution.py:180
  56.2 3.4 %collective-permute-start.3 = (bf16[144,256]{1,0:T(8,128)(2,1)S(1)}, bf16[144,256]{1,0:T(8,128)(2,1)S(1)}, u32[]{:S(2)}, u32[]{:S(2)}) collective-permute-start(bf16[144,256]{1,0:T(8,128)(2,1)S(1)} %get-tuple-element.28), channel_id=1, source_target_pairs={{0,8},{2,10},{4,12},{6,14},{8,0},{10,2},{12,4},{14,6},{1,9},{3,11}... | collective-permute-start | bytes 221192 | tf_op jit(solution)/shard_map/ppermute | solution.py:151
  59.6 0.0 collective-permute-done.refs_2_
  59.6 0.1 collective-permute-start.4
  59.6 0.0 collective-permute-done.1.refs_3_
  59.6 2.3 %collective-permute-start.5 = (bf16[144,256]{1,0:T(8,128)(2,1)S(1)}, bf16[144,256]{1,0:T(8,128)(2,1)S(1)}, u32[]{:S(2)}, u32[]{:S(2)}) collective-permute-start(bf16[144,256]{1,0:T(8,128)(2,1)S(1)} %get-tuple-element.30), channel_id=1, source_target_pairs={{0,12},{2,14},{4,8},{6,10},{8,4},{10,6},{12,0},{14,2},{1,13},{3,15... | collective-permute-start | bytes 221192 | tf_op jit(solution)/shard_map/ppermute | solution.py:151
  62.0 0.0 collective-permute-done.14.other_ref
  62.0 2.4 %collective-permute-start.6 = (bf16[144,256]{1,0:T(8,128)(2,1)S(1)}, bf16[144,256]{1,0:T(8,128)(2,1)S(1)}, u32[]{:S(2)}, u32[]{:S(2)}) collective-permute-start(bf16[144,256]{1,0:T(8,128)(2,1)S(1)} %get-tuple-element.31), channel_id=1, source_target_pairs={{0,14},{2,12},{4,10},{6,8},{8,6},{10,4},{12,2},{14,0},{1,15},{3,13... | collective-permute-start | bytes 221192 | tf_op jit(solution)/shard_map/ppermute | solution.py:151
  65.0 2.7 %prepare.1 = (bf16[8,2,96,512]{3,2,1,0:T(8,128)(2,1)S(1)}, bf16[2,512,192]{2,1,0:T(8,128)(2,1)S(1)}, bf16[2,512,192]{2,1,0:T(8,128)(2,1)S(1)}) custom-call(bf16[8,112,512]{2,1,0:T(8,128)(2,1)S(1)} %bitcast_dynamic-update-slice_fusion.mine_ref, bf16[8,112,512]{2,1,0:T(8,128)(2,1)} %collective-permute-done.14.other_ref), custom_call_target="tpu_custom_call" | custom-call | tf_op jit(solution)/shard_map/prepare/pallas_call | solution.py:180
  67.7 0.0 collective-permute-done.2.refs_4_
  67.7 0.0 collective-permute-done.3.refs_5_
  67.8 2.1 %collective-permute-done.4.refs_6_ = bf16[144,256]{1,0:T(8,128)(2,1)S(1)} collective-permute-done((bf16[144,256]{1,0:T(8,128)(2,1)S(1)}, bf16[144,256]{1,0:T(8,128)(2,1)S(1)}, u32[]{:S(2)}, u32[]{:S(2)}) %collective-permute-start.4) | collective-permute-done | bytes 73760 | tf_op jit(solution)/shard_map/ppermute | solution.py:151
  69.8 0.0 collective-permute-done.5.refs_7_
  69.8 0.0 collective-permute-done.6.refs_8_
  69.8 0.0 copy-done.1
  69.9 0.0 copy-start.5
  69.9 1.7 %layers.1 = (bf16[192,512]{1,0:T(8,128)(2,1)}, bf16[2,192,512]{2,1,0:T(8,128)(2,1)S(1)}, bf16[512,512]{1,0:T(8,128)(2,1)S(1)}) custom-call(s32[1,1]{1,0:T(1,128)S(6)} %copy.20.refs_0_, bf16[144,256]{1,0:T(8,128)(2,1)S(1)} %get-tuple-element.24.refs_1_, bf16[144,256]{1,0:T(8,128)(2,1)S(1)} %collective-permute-done.refs_2_, ...), custom_call_target="tpu_custom_call" | custom-call | tf_op jit(solution)/shard_map/layers/pallas_call | solution.py:180
  71.6 0.1 collective-permute-start.15
  71.7 1.9 %collective-permute-done.15.got_ref = bf16[512,512]{1,0:T(8,128)(2,1)S(1)} collective-permute-done((bf16[512,512]{1,0:T(8,128)(2,1)S(1)}, bf16[512,512]{1,0:T(8,128)(2,1)S(1)}, u32[]{:S(2)}, u32[]{:S(2)}) %collective-permute-start.15) | collective-permute-done | bytes 524320 | tf_op jit(solution)/shard_map/ppermute | solution.py:151
  73.6 0.7 share.1
  74.3 4.1 %collective-permute-start.22 = (bf16[64,512]{1,0:T(8,128)(2,1)S(1)}, bf16[64,512]{1,0:T(8,128)(2,1)S(1)}, u32[]{:S(2)}, u32[]{:S(2)}) collective-permute-start(bf16[64,512]{1,0:T(8,128)(2,1)S(1)} %get-tuple-element.45), channel_id=1, source_target_pairs={{0,14},{2,12},{4,10},{6,8},{8,6},{10,4},{12,2},{14,0},{1,15},{3,13... | collective-permute-start | bytes 196616 | tf_op jit(solution)/shard_map/ppermute | solution.py:151
  78.4 0.6 collective-permute-start.21
  79.0 2.8 %collective-permute-start.20 = (bf16[64,512]{1,0:T(8,128)(2,1)S(1)}, bf16[64,512]{1,0:T(8,128)(2,1)S(1)}, u32[]{:S(2)}, u32[]{:S(2)}) collective-permute-start(bf16[64,512]{1,0:T(8,128)(2,1)S(1)} %get-tuple-element.43), channel_id=1, source_target_pairs={{0,10},{2,8},{4,14},{6,12},{8,2},{10,0},{12,6},{14,4},{1,11},{3,9}... | collective-permute-start | bytes 196616 | tf_op jit(solution)/shard_map/ppermute | solution.py:151
  81.9 0.1 collective-permute-start.19
  82.0 2.5 %collective-permute-start.18 = (bf16[64,512]{1,0:T(8,128)(2,1)S(1)}, bf16[64,512]{1,0:T(8,128)(2,1)S(1)}, u32[]{:S(2)}, u32[]{:S(2)}) collective-permute-start(bf16[64,512]{1,0:T(8,128)(2,1)S(1)} %get-tuple-element.41), channel_id=1, source_target_pairs={{0,6},{2,4},{4,2},{6,0},{8,14},{10,12},{12,10},{14,8},{1,7},{3,5},... | collective-permute-start | bytes 196616 | tf_op jit(solution)/shard_map/ppermute | solution.py:151
  84.5 0.0 collective-permute-done.22
  84.5 2.7 %collective-permute-start.17 = (bf16[64,512]{1,0:T(8,128)(2,1)S(1)}, bf16[64,512]{1,0:T(8,128)(2,1)S(1)}, u32[]{:S(2)}, u32[]{:S(2)}) collective-permute-start(bf16[64,512]{1,0:T(8,128)(2,1)S(1)} %get-tuple-element.40), channel_id=1, source_target_pairs={{0,4},{2,6},{4,0},{6,2},{8,12},{10,14},{12,8},{14,10},{1,5},{3,7},... | collective-permute-start | bytes 196616 | tf_op jit(solution)/shard_map/ppermute | solution.py:151
  87.2 0.0 collective-permute-done.21
  87.2 1.4 %collective-permute-start.16 = (bf16[64,512]{1,0:T(8,128)(2,1)S(1)}, bf16[64,512]{1,0:T(8,128)(2,1)S(1)}, u32[]{:S(2)}, u32[]{:S(2)}) collective-permute-start(bf16[64,512]{1,0:T(8,128)(2,1)S(1)} %get-tuple-element.39), channel_id=1, source_target_pairs={{0,2},{2,0},{4,6},{6,4},{8,10},{10,8},{12,14},{14,12},{1,3},{3,1},... | collective-permute-start | bytes 196616 | tf_op jit(solution)/shard_map/ppermute | solution.py:151
  88.6 1.5 %collective-permute-done.20 = bf16[64,512]{1,0:T(8,128)(2,1)S(1)} collective-permute-done((bf16[64,512]{1,0:T(8,128)(2,1)S(1)}, bf16[64,512]{1,0:T(8,128)(2,1)S(1)}, u32[]{:S(2)}, u32[]{:S(2)}) %collective-permute-start.20) | collective-permute-done | bytes 65568 | tf_op jit(solution)/shard_map/ppermute | solution.py:151
  90.1 1.1 %collective-permute-done.19 = bf16[64,512]{1,0:T(8,128)(2,1)S(1)} collective-permute-done((bf16[64,512]{1,0:T(8,128)(2,1)S(1)}, bf16[64,512]{1,0:T(8,128)(2,1)S(1)}, u32[]{:S(2)}, u32[]{:S(2)}) %collective-permute-start.19) | collective-permute-done | bytes 65568 | tf_op jit(solution)/shard_map/ppermute | solution.py:151
  91.2 0.0 collective-permute-done.18
  91.2 0.9 collective-permute-done.17
  92.1 0.0 collective-permute-done.16
  92.1 0.7 maximum_convert_fusion
  (15 shorter events, 0.1 us)
Async XLA Ops:
  0.6 26.9 %copy-start.4 = (s32[8,1,10,192]{3,1,2,0:T(1,128)S(1)}, s32[8,1,10,192]{3,1,2,0:T(1,128)}, u32[]{:S(2)}) copy-start(s32[8,1,10,192]{3,1,2,0:T(1,128)} %param.12) | copy-start | bytes 184324
  0.6 27.2 %copy-start = (bf16[96,12288]{1,0:T(8,128)(2,1)S(1)}, bf16[96,12288]{1,0:T(8,128)(2,1)}, u32[]{:S(2)}) copy-start(bf16[96,12288]{1,0:T(8,128)(2,1)} %src_ref.1) | copy-start | bytes 7077892
  2.5 8.9 %collective-permute-start.7 = (bf16[112,512]{1,0:T(8,128)(2,1)S(1)}, bf16[112,512]{1,0:T(8,128)(2,1)S(1)}, u32[]{:S(2)}, u32[]{:S(2)}) collective-permute-start(bf16[112,512]{1,0:T(8,128)(2,1)S(1)} %pad_maximum_fusion), channel_id=1, source_target_pairs={{0,2},{2,0},{4,6},{6,4},{8,10},{10,8},{12,14},{14,12},{1,3},{3,1},... | collective-permute-start | bytes 344072 | tf_op jit(solution)/shard_map/ppermute | solution.py:151
  5.6 9.6 %collective-permute-start.8 = (bf16[112,512]{1,0:T(8,128)(2,1)S(1)}, bf16[112,512]{1,0:T(8,128)(2,1)S(1)}, u32[]{:S(2)}, u32[]{:S(2)}) collective-permute-start(bf16[112,512]{1,0:T(8,128)(2,1)S(1)} %pad_maximum_fusion), channel_id=1, source_target_pairs={{0,4},{2,6},{4,0},{6,2},{8,12},{10,14},{12,8},{14,10},{1,5},{3,7},... | collective-permute-start | bytes 344072 | tf_op jit(solution)/shard_map/ppermute | solution.py:151
  7.1 8.2 %collective-permute-start.9 = (bf16[112,512]{1,0:T(8,128)(2,1)S(1)}, bf16[112,512]{1,0:T(8,128)(2,1)S(1)}, u32[]{:S(2)}, u32[]{:S(2)}) collective-permute-start(bf16[112,512]{1,0:T(8,128)(2,1)S(1)} %pad_maximum_fusion), channel_id=1, source_target_pairs={{0,6},{2,4},{4,2},{6,0},{8,14},{10,12},{12,10},{14,8},{1,7},{3,5},... | collective-permute-start | bytes 344072 | tf_op jit(solution)/shard_map/ppermute | solution.py:151
  7.1 8.6 %collective-permute-start.10 = (bf16[112,512]{1,0:T(8,128)(2,1)S(1)}, bf16[112,512]{1,0:T(8,128)(2,1)S(1)}, u32[]{:S(2)}, u32[]{:S(2)}) collective-permute-start(bf16[112,512]{1,0:T(8,128)(2,1)S(1)} %pad_maximum_fusion), channel_id=1, source_target_pairs={{0,8},{2,10},{4,12},{6,14},{8,0},{10,2},{12,4},{14,6},{1,9},{3,11}... | collective-permute-start | bytes 344072 | tf_op jit(solution)/shard_map/ppermute | solution.py:151
  10.1 17.3 %collective-permute-start.11 = (bf16[112,512]{1,0:T(8,128)(2,1)S(1)}, bf16[112,512]{1,0:T(8,128)(2,1)S(1)}, u32[]{:S(2)}, u32[]{:S(2)}) collective-permute-start(bf16[112,512]{1,0:T(8,128)(2,1)S(1)} %pad_maximum_fusion), channel_id=1, source_target_pairs={{0,10},{2,8},{4,14},{6,12},{8,2},{10,0},{12,6},{14,4},{1,11},{3,9}... | collective-permute-start | bytes 344072 | tf_op jit(solution)/shard_map/ppermute | solution.py:151
  11.4 16.0 %collective-permute-start.12 = (bf16[112,512]{1,0:T(8,128)(2,1)S(1)}, bf16[112,512]{1,0:T(8,128)(2,1)S(1)}, u32[]{:S(2)}, u32[]{:S(2)}) collective-permute-start(bf16[112,512]{1,0:T(8,128)(2,1)S(1)} %pad_maximum_fusion), channel_id=1, source_target_pairs={{0,12},{2,14},{4,8},{6,10},{8,4},{10,6},{12,0},{14,2},{1,13},{3,15... | collective-permute-start | bytes 344072 | tf_op jit(solution)/shard_map/ppermute | solution.py:151
  15.1 12.3 %collective-permute-start.13 = (bf16[112,512]{1,0:T(8,128)(2,1)S(1)}, bf16[112,512]{1,0:T(8,128)(2,1)S(1)}, u32[]{:S(2)}, u32[]{:S(2)}) collective-permute-start(bf16[112,512]{1,0:T(8,128)(2,1)S(1)} %pad_maximum_fusion), channel_id=1, source_target_pairs={{0,14},{2,12},{4,10},{6,8},{8,6},{10,4},{12,2},{14,0},{1,15},{3,13... | collective-permute-start | bytes 344072 | tf_op jit(solution)/shard_map/ppermute | solution.py:151
  27.5 34.5 %collective-permute-start.14 = (bf16[8,112,512]{2,1,0:T(8,128)(2,1)S(1)}, bf16[8,112,512]{2,1,0:T(8,128)(2,1)}, u32[]{:S(2)}, u32[]{:S(2)}) collective-permute-start(bf16[8,112,512]{2,1,0:T(8,128)(2,1)S(1)} %bitcast_dynamic-update-slice_fusion.mine_ref), channel_id=1, source_target_pairs={{0,1},{1,0},{2,3},{3,2},{4,5},{5,4},{6,7},{7,6},{8,9},{9,8},{10,11... | collective-permute-start | bytes 2752520 | tf_op jit(solution)/shard_map/ppermute | solution.py:151
  40.3 19.3 %collective-permute-start = (bf16[144,256]{1,0:T(8,128)(2,1)S(1)}, bf16[144,256]{1,0:T(8,128)(2,1)S(1)}, u32[]{:S(2)}, u32[]{:S(2)}) collective-permute-start(bf16[144,256]{1,0:T(8,128)(2,1)S(1)} %get-tuple-element.25), channel_id=1, source_target_pairs={{0,2},{2,0},{4,6},{6,4},{8,10},{10,8},{12,14},{14,12},{1,3},{3,1},... | collective-permute-start | bytes 221192 | tf_op jit(solution)/shard_map/ppermute | solution.py:151
  41.1 18.5 %collective-permute-start.1 = (bf16[144,256]{1,0:T(8,128)(2,1)S(1)}, bf16[144,256]{1,0:T(8,128)(2,1)S(1)}, u32[]{:S(2)}, u32[]{:S(2)}) collective-permute-start(bf16[144,256]{1,0:T(8,128)(2,1)S(1)} %get-tuple-element.26), channel_id=1, source_target_pairs={{0,4},{2,6},{4,0},{6,2},{8,12},{10,14},{12,8},{14,10},{1,5},{3,7},... | collective-permute-start | bytes 221192 | tf_op jit(solution)/shard_map/ppermute | solution.py:151
  45.4 24.5 %copy-start.1 = (bf16[512,512]{1,0:T(8,128)(2,1)S(1)}, bf16[512,512]{1,0:T(8,128)(2,1)}, u32[]{:S(2)}) copy-start(bf16[512,512]{1,0:T(8,128)(2,1)} %refs_11_.1) | copy-start | bytes 1572868
  45.4 24.5 %copy-start.2 = (bf16[512,512]{1,0:T(8,128)(2,1)S(1)}, bf16[512,512]{1,0:T(8,128)(2,1)}, u32[]{:S(2)}) copy-start(bf16[512,512]{1,0:T(8,128)(2,1)} %refs_12_.1) | copy-start | bytes 1572868
  45.4 24.5 %copy-start.3 = (f32[512]{0:T(512)S(1)}, f32[512]{0:T(512)}, u32[]{:S(2)}) copy-start(f32[512]{0:T(512)} %param.18) | copy-start | bytes 6148
  45.4 22.4 %collective-permute-start.2 = (bf16[144,256]{1,0:T(8,128)(2,1)S(1)}, bf16[144,256]{1,0:T(8,128)(2,1)S(1)}, u32[]{:S(2)}, u32[]{:S(2)}) collective-permute-start(bf16[144,256]{1,0:T(8,128)(2,1)S(1)} %get-tuple-element.27), channel_id=1, source_target_pairs={{0,6},{2,4},{4,2},{6,0},{8,14},{10,12},{12,10},{14,8},{1,7},{3,5},... | collective-permute-start | bytes 221192 | tf_op jit(solution)/shard_map/ppermute | solution.py:151
  56.2 11.5 %collective-permute-start.3 = (bf16[144,256]{1,0:T(8,128)(2,1)S(1)}, bf16[144,256]{1,0:T(8,128)(2,1)S(1)}, u32[]{:S(2)}, u32[]{:S(2)}) collective-permute-start(bf16[144,256]{1,0:T(8,128)(2,1)S(1)} %get-tuple-element.28), channel_id=1, source_target_pairs={{0,8},{2,10},{4,12},{6,14},{8,0},{10,2},{12,4},{14,6},{1,9},{3,11}... | collective-permute-start | bytes 221192 | tf_op jit(solution)/shard_map/ppermute | solution.py:151
  59.6 10.3 %collective-permute-start.4 = (bf16[144,256]{1,0:T(8,128)(2,1)S(1)}, bf16[144,256]{1,0:T(8,128)(2,1)S(1)}, u32[]{:S(2)}, u32[]{:S(2)}) collective-permute-start(bf16[144,256]{1,0:T(8,128)(2,1)S(1)} %get-tuple-element.29), channel_id=1, source_target_pairs={{0,10},{2,8},{4,14},{6,12},{8,2},{10,0},{12,6},{14,4},{1,11},{3,9}... | collective-permute-start | bytes 221192 | tf_op jit(solution)/shard_map/ppermute | solution.py:151
  59.6 10.2 %collective-permute-start.5 = (bf16[144,256]{1,0:T(8,128)(2,1)S(1)}, bf16[144,256]{1,0:T(8,128)(2,1)S(1)}, u32[]{:S(2)}, u32[]{:S(2)}) collective-permute-start(bf16[144,256]{1,0:T(8,128)(2,1)S(1)} %get-tuple-element.30), channel_id=1, source_target_pairs={{0,12},{2,14},{4,8},{6,10},{8,4},{10,6},{12,0},{14,2},{1,13},{3,15... | collective-permute-start | bytes 221192 | tf_op jit(solution)/shard_map/ppermute | solution.py:151
  62.0 7.8 %collective-permute-start.6 = (bf16[144,256]{1,0:T(8,128)(2,1)S(1)}, bf16[144,256]{1,0:T(8,128)(2,1)S(1)}, u32[]{:S(2)}, u32[]{:S(2)}) collective-permute-start(bf16[144,256]{1,0:T(8,128)(2,1)S(1)} %get-tuple-element.31), channel_id=1, source_target_pairs={{0,14},{2,12},{4,10},{6,8},{8,6},{10,4},{12,2},{14,0},{1,15},{3,13... | collective-permute-start | bytes 221192 | tf_op jit(solution)/shard_map/ppermute | solution.py:151
  69.9 22.2 %copy-start.5 = (f32[512]{0:T(512)S(1)}, f32[512]{0:T(512)}, u32[]{:S(2)}) copy-start(f32[512]{0:T(512)} %param.21) | copy-start | bytes 6148
  71.6 2.0 %collective-permute-start.15 = (bf16[512,512]{1,0:T(8,128)(2,1)S(1)}, bf16[512,512]{1,0:T(8,128)(2,1)S(1)}, u32[]{:S(2)}, u32[]{:S(2)}) collective-permute-start(bf16[512,512]{1,0:T(8,128)(2,1)S(1)} %get-tuple-element.37), channel_id=1, source_target_pairs={{0,1},{1,0},{2,3},{3,2},{4,5},{5,4},{6,7},{7,6},{8,9},{9,8},{10,11... | collective-permute-start | bytes 1572872 | tf_op jit(solution)/shard_map/ppermute | solution.py:151
  74.3 10.2 %collective-permute-start.22 = (bf16[64,512]{1,0:T(8,128)(2,1)S(1)}, bf16[64,512]{1,0:T(8,128)(2,1)S(1)}, u32[]{:S(2)}, u32[]{:S(2)}) collective-permute-start(bf16[64,512]{1,0:T(8,128)(2,1)S(1)} %get-tuple-element.45), channel_id=1, source_target_pairs={{0,14},{2,12},{4,10},{6,8},{8,6},{10,4},{12,2},{14,0},{1,15},{3,13... | collective-permute-start | bytes 196616 | tf_op jit(solution)/shard_map/ppermute | solution.py:151
  78.4 8.8 %collective-permute-start.21 = (bf16[64,512]{1,0:T(8,128)(2,1)S(1)}, bf16[64,512]{1,0:T(8,128)(2,1)S(1)}, u32[]{:S(2)}, u32[]{:S(2)}) collective-permute-start(bf16[64,512]{1,0:T(8,128)(2,1)S(1)} %get-tuple-element.44), channel_id=1, source_target_pairs={{0,12},{2,14},{4,8},{6,10},{8,4},{10,6},{12,0},{14,2},{1,13},{3,15... | collective-permute-start | bytes 196616 | tf_op jit(solution)/shard_map/ppermute | solution.py:151
  79.0 11.1 %collective-permute-start.20 = (bf16[64,512]{1,0:T(8,128)(2,1)S(1)}, bf16[64,512]{1,0:T(8,128)(2,1)S(1)}, u32[]{:S(2)}, u32[]{:S(2)}) collective-permute-start(bf16[64,512]{1,0:T(8,128)(2,1)S(1)} %get-tuple-element.43), channel_id=1, source_target_pairs={{0,10},{2,8},{4,14},{6,12},{8,2},{10,0},{12,6},{14,4},{1,11},{3,9}... | collective-permute-start | bytes 196616 | tf_op jit(solution)/shard_map/ppermute | solution.py:151
  81.9 9.3 %collective-permute-start.19 = (bf16[64,512]{1,0:T(8,128)(2,1)S(1)}, bf16[64,512]{1,0:T(8,128)(2,1)S(1)}, u32[]{:S(2)}, u32[]{:S(2)}) collective-permute-start(bf16[64,512]{1,0:T(8,128)(2,1)S(1)} %get-tuple-element.42), channel_id=1, source_target_pairs={{0,8},{2,10},{4,12},{6,14},{8,0},{10,2},{12,4},{14,6},{1,9},{3,11}... | collective-permute-start | bytes 196616 | tf_op jit(solution)/shard_map/ppermute | solution.py:151
  82.0 9.2 %collective-permute-start.18 = (bf16[64,512]{1,0:T(8,128)(2,1)S(1)}, bf16[64,512]{1,0:T(8,128)(2,1)S(1)}, u32[]{:S(2)}, u32[]{:S(2)}) collective-permute-start(bf16[64,512]{1,0:T(8,128)(2,1)S(1)} %get-tuple-element.41), channel_id=1, source_target_pairs={{0,6},{2,4},{4,2},{6,0},{8,14},{10,12},{12,10},{14,8},{1,7},{3,5},... | collective-permute-start | bytes 196616 | tf_op jit(solution)/shard_map/ppermute | solution.py:151
  84.5 7.6 %collective-permute-start.17 = (bf16[64,512]{1,0:T(8,128)(2,1)S(1)}, bf16[64,512]{1,0:T(8,128)(2,1)S(1)}, u32[]{:S(2)}, u32[]{:S(2)}) collective-permute-start(bf16[64,512]{1,0:T(8,128)(2,1)S(1)} %get-tuple-element.40), channel_id=1, source_target_pairs={{0,4},{2,6},{4,0},{6,2},{8,12},{10,14},{12,8},{14,10},{1,5},{3,7},... | collective-permute-start | bytes 196616 | tf_op jit(solution)/shard_map/ppermute | solution.py:151
  87.2 4.9 %collective-permute-start.16 = (bf16[64,512]{1,0:T(8,128)(2,1)S(1)}, bf16[64,512]{1,0:T(8,128)(2,1)S(1)}, u32[]{:S(2)}, u32[]{:S(2)}) collective-permute-start(bf16[64,512]{1,0:T(8,128)(2,1)S(1)} %get-tuple-element.39), channel_id=1, source_target_pairs={{0,2},{2,0},{4,6},{6,4},{8,10},{10,8},{12,14},{14,12},{1,3},{3,1},... | collective-permute-start | bytes 196616 | tf_op jit(solution)/shard_map/ppermute | solution.py:151

commit v3 on v2

v3 whole, which is shorter than its diff:
```python
import functools

import jax
import jax.numpy as jnp
from jax import lax
from jax.experimental import pallas as pl
from jax.experimental.pallas import tpu as pltpu
from jax.sharding import PartitionSpec as P

LANES = 128
MIB = 1024 * 1024


def folds(fslice, pcap):
    return 4 * fslice == 3 * LANES and pcap % 64 == 0


def split_rows(fslice):
    return -(-fslice // 32) * 16


def turn_kernel(pcap, src_ref, seed_ref, nbr_ref, w_self_ref, w_nbr_ref, table_ref, parcel_ref):
    fslice, nodes = src_ref.shape
    n_feat = parcel_ref.shape[0]
    first_core = lax.axis_index("rep") == 0
    width = 512

    def turn(step, carry):
        at = pl.multiple_of(step * width, width)
        table_ref[pl.ds(at, width), :fslice] = src_ref[:, pl.ds(at, width)].astype(jnp.float32).T
        return carry

    lax.fori_loop(0, nodes // width, turn, 0)

    part = split_rows(fslice)
    idx = jnp.concatenate([seed_ref[...], nbr_ref[...]], axis=0)
    high = lax.shift_right_logical(idx, 7)
    digits = jnp.concatenate([high, idx - high * 128], axis=1).astype(jnp.float32)
    digits = digits.astype(jnp.bfloat16)
    half = jnp.where(first_core, w_self_ref[...], w_nbr_ref[...])
    for p in range(n_feat):
        block = src_ref[:, 2 * p * pcap : 2 * (p + 1) * pcap].astype(jnp.float32)
        own = jnp.where(first_core, block[:, :pcap], block[:, pcap:])
        rest = own[part:]
        if rest.shape[0] < part:
            rest = jnp.concatenate([rest, own[: part - rest.shape[0]]], axis=0)
        parcel_ref[p, :fslice, :] = half
        parcel_ref[p, fslice:, : 2 * pcap] = jnp.concatenate([own[:part], rest], axis=1).astype(
            jnp.bfloat16
        )
        parcel_ref[p, fslice : fslice + idx.shape[0], 2 * pcap :] = digits


def mean_kernel(fanout, pcap, fslice, nbr_ref, table_ref, out_ref, total):
    def partition(p, carry):
        first = p * (fanout * pcap)

        def group(g, inner):
            at = pl.multiple_of(g * 8, 8)
            for u in range(8):
                rows = [
                    table_ref[pl.ds(nbr_ref[first + k * pcap + at + u], 1), :]
                    for k in range(fanout)
                ]
                while len(rows) > 1:
                    rows = [a + b for a, b in zip(rows[::2], rows[1::2])] + (
                        [rows[-1]] if len(rows) % 2 else []
                    )
                total[pl.ds(at + u, 1), :] = rows[0]
            return inner

        lax.fori_loop(0, pcap // 8, group, 0)
        mean = total[...] / fanout
        if folds(fslice, pcap):
            lane = lax.broadcasted_iota(jnp.int32, (pcap // 4, LANES), 1)
            cut = pcap // 4 * 3
            part = pcap // 4
            tail = mean[cut:]
            for b in range(3):
                shift = (fslice - 32 * b) % LANES
                moved = pltpu.roll(tail, shift, 1) if shift else tail
                rows = pl.ds(b * part, part)
                out_ref[p, rows, :] = jnp.where(
                    lane < fslice, mean[b * part : (b + 1) * part], moved
                ).astype(jnp.bfloat16)
        else:
            out_ref[p] = mean[:, :fslice].astype(jnp.bfloat16)
        return carry

    lax.fori_loop(0, out_ref.shape[0], partition, 0)


def unfold(block, fslice, pcap):
    if block.shape[0] == pcap:
        return block
    part = block.shape[0] // 3
    wide = block.astype(jnp.float32)
    lane = lax.broadcasted_iota(jnp.int32, (part, LANES), 1)
    tail = pltpu.roll(wide[:part], LANES - fslice, 1)
    for b in (1, 2):
        shift = (32 * b - fslice) % LANES
        moved = wide[b * part : (b + 1) * part]
        moved = pltpu.roll(moved, shift, 1) if shift else moved
        tail = jnp.where(lane // 32 == b, moved, tail)
    return jnp.concatenate([wide, tail], axis=0)[:, :fslice].astype(jnp.bfloat16)


def prepare_kernel(
    fslice, seed_count, n_idx, mine_ref, other_ref, bias_ref, pre_ref, w_ref, own_ref, near_ref
):
    n_feat = mine_ref.shape[0]
    pcap = pre_ref.shape[0]
    part = split_rows(fslice)
    rep_pos = lax.axis_index("rep")
    first_core = rep_pos == 0
    base = (lax.axis_index("feat") * lax.axis_size("rep") + rep_pos) * pcap
    base = base.astype(jnp.float32)
    pair = 2 * seed_count
    slot = lax.broadcasted_iota(jnp.int32, (pcap, pair), 0).astype(jnp.float32)
    low = lax.broadcasted_iota(jnp.int32, (n_idx, pair), 1) < seed_count
    pre = jnp.zeros(pre_ref.shape, jnp.float32)
    for f in range(n_feat):
        mine, other = mine_ref[f, :fslice], other_ref[f, :fslice]
        w_ref[f] = jnp.where(first_core, other, mine)
        both = mine_ref[f, fslice:, : 2 * pcap].astype(jnp.float32)
        own = jnp.concatenate([both[:, :pcap], both[: fslice - part, pcap:]], axis=0)
        pre = pre + jnp.dot(
            own.T.astype(jnp.bfloat16),
            jnp.where(first_core, mine, other),
            preferred_element_type=jnp.float32,
        )
    pre_ref[...] = pre + bias_ref[...]
    for half, ref in enumerate((mine_ref, other_ref)):
        for s in range(0, n_feat, 2):
            first = ref[s, fslice : fslice + n_idx, 2 * pcap :].astype(jnp.float32)
            second = ref[s + 1, fslice : fslice + n_idx, 2 * pcap :].astype(jnp.float32)
            high_part = jnp.where(low, first, pltpu.roll(second, seed_count, 1))
            low_part = jnp.where(low, pltpu.roll(first, seed_count, 1), second)
            row = high_part * 128.0 + low_part - base
            own = jnp.where(slot == row[:1], 1.0, 0.0)
            near = jnp.zeros((pcap, pair), jnp.float32)
            for k in range(1, n_idx):
                near = near + jnp.where(slot == row[k : k + 1], 1.0, 0.0)
            place = pl.ds(s * seed_count, pair)
            own_ref[half, place, :] = own.T.astype(jnp.bfloat16)
            near_ref[half, place, :] = near.T.astype(jnp.bfloat16)


def layer_kernel(
    fanout_two,
    count_ref,
    got_ref,
    pre_ref,
    w_ref,
    ws_ref,
    wn_ref,
    own_ref,
    near_ref,
    hidden_ref,
    value_ref,
    part_ref,
):
    pcap, width = hidden_ref.shape
    fslice = w_ref.shape[1]
    pre = pre_ref[...]
    for f in range(got_ref.shape[0]):
        pre = pre + jnp.dot(
            unfold(got_ref[f], fslice, pcap), w_ref[f], preferred_element_type=jnp.float32
        )
    live = lax.broadcasted_iota(jnp.int32, (pcap, width), 0) < count_ref[0, 0]
    hidden = jnp.where(live, jnp.maximum(pre, 0.0), 0.0).astype(jnp.bfloat16)
    hidden_ref[...] = hidden
    value_ref[0] = jnp.dot(hidden, ws_ref[...], preferred_element_type=jnp.float32).astype(
        jnp.bfloat16
    )
    value_ref[1] = (
        jnp.dot(hidden, wn_ref[...], preferred_element_type=jnp.float32) / fanout_two
    ).astype(jnp.bfloat16)
    part_ref[...] = (
        jnp.dot(own_ref[1], value_ref[0], preferred_element_type=jnp.float32)
        + jnp.dot(near_ref[1], value_ref[1], preferred_element_type=jnp.float32)
    ).astype(jnp.bfloat16)


def share_kernel(own_ref, near_ref, value_ref, got_ref, out_ref):
    out_ref[...] = (
        jnp.dot(own_ref[0], value_ref[0], preferred_element_type=jnp.float32)
        + jnp.dot(near_ref[0], value_ref[1], preferred_element_type=jnp.float32)
        + got_ref[...].astype(jnp.float32)
    ).astype(jnp.bfloat16)


def swap(value, axis, step):
    size = lax.axis_size(axis)
    return lax.ppermute(value, axis, [(i, i ^ step) for i in range(size)])


def body(
    src_feats,
    nbr_one,
    counts,
    seed_rows,
    nbr_two,
    w1_self,
    w1_nbr,
    bias_one,
    w2_self,
    w2_nbr,
    bias_two,
):
    n_feat = lax.axis_size("feat")
    fslice, nodes = src_feats.shape
    fanout_one, pcap = nbr_one.shape[2:]
    width = w1_self.shape[1]
    seed_count, fanout_two = nbr_two.shape
    n_idx = fanout_two + 1
    bf16 = jnp.bfloat16
    vmem = pl.BlockSpec(memory_space=pltpu.VMEM)
    smem = pl.BlockSpec(memory_space=pltpu.SMEM)
    table_bytes = nodes * LANES * 4

    def call(kernel, name, shapes, ins, args, scratch=(), limit=16 * MIB, cost_us=1):
        return pl.pallas_call(
            kernel,
            out_shape=tuple(jax.ShapeDtypeStruct(shape, dtype) for shape, dtype in shapes),
            in_specs=ins,
            out_specs=(vmem,) * len(shapes),
            scratch_shapes=scratch,
            compiler_params=pltpu.CompilerParams(vmem_limit_bytes=limit),
            cost_estimate=pl.CostEstimate(
                flops=0, bytes_accessed=int(cost_us * 3_600_000), transcendentals=0
            ),
            name=name,
        )(*args)

    table, parcel = call(
        functools.partial(turn_kernel, pcap),
        "turn",
        [
            ((nodes, LANES), jnp.float32),
            ((n_feat, fslice + split_rows(fslice), width), bf16),
        ],
        [vmem] * 5,
        (src_feats, seed_rows[None], nbr_two.T, w1_self, w1_nbr),
        limit=table_bytes + 12 * MIB,
        cost_us=3,
    )
    mine = lax.all_to_all(parcel, "feat", 0, 0, tiled=True)

    sent_shape = (pcap // 4 * 3, LANES) if folds(fslice, pcap) else (pcap, fslice)
    (sent,) = call(
        functools.partial(mean_kernel, fanout_one, pcap, fslice),
        "mean",
        [((n_feat, *sent_shape), bf16)],
        [smem, vmem],
        (nbr_one.reshape(-1), table),
        scratch=[pltpu.VMEM((pcap, LANES), jnp.float32)],
        limit=table_bytes + 8 * MIB,
        cost_us=20,
    )
    got = lax.all_to_all(sent, "feat", 0, 0, tiled=True)

    other = swap(mine, "rep", 1)
    pre, w_nbr, own_times, near_times = call(
        functools.partial(prepare_kernel, fslice, seed_count, n_idx),
        "prepare",
        [
            ((pcap, width), jnp.float32),
            ((n_feat, fslice, width), bf16),
            ((2, n_feat * seed_count, pcap), bf16),
            ((2, n_feat * seed_count, pcap), bf16),
        ],
        [vmem] * 3,
        (mine, other, bias_one[None]),
        cost_us=3,
    )
    hidden, value, for_other = call(
        functools.partial(layer_kernel, fanout_two),
        "layers",
        [
            ((pcap, width), bf16),
            ((2, pcap, width), bf16),
            ((n_feat * seed_count, width), bf16),
        ],
        [smem] + [vmem] * 7,
        (counts, got, pre, w_nbr, w2_self, w2_nbr, own_times, near_times),
    )
    from_other = swap(for_other, "rep", 1)
    (shares,) = call(
        share_kernel,
        "share",
        [((n_feat * seed_count, width), bf16)],
        [vmem] * 4,
        (own_times, near_times, value, from_other),
    )
    parts = lax.all_to_all(shares.reshape(n_feat, seed_count, width), "feat", 0, 0, tiled=True)
    pre_two = jnp.sum(parts.astype(jnp.float32), axis=0) + bias_two
    seed_out = jnp.maximum(pre_two, 0.0).astype(bf16)
    return (hidden[None, None], seed_out)


def solution(mesh):
    placed = (
        P("feat", "groups"),
        P("groups", "rep", None, None),
        P(("groups", "feat"), "rep"),
        P(("groups", "feat", "rep")),
        P(("groups", "feat", "rep"), None),
        P("feat", None),
        P("feat", None),
        P(),
        P(),
        P(),
        P(),
    )
    return jax.shard_map(
        body,
        mesh=mesh,
        in_specs=placed,
        out_specs=(P(("groups", "feat"), "rep", None, None), P(("groups", "feat", "rep"), None)),
        check_vma=False,
    )
```

time: 93 us -> 112 us (1.20)
  blocking collectives: 0 us -> 54.3 us
  starting transfers between devices: 41.4 us -> 4.13 us
  local copies, waits for them, and re-layouts: 0.18 us -> 16.2 us
  waiting for transfers between devices: 19.6 us -> 8.24 us
  other arithmetic: 2.79 us -> 0.91 us
  Pallas kernels: 27.3 us -> 25.8 us
    all_to_all x0 -> x2, blocking collectives: none -> 54.3 us  [the longest x1 36.1 us: body(): mine = lax.all_to_all(parcel, 'feat', 0, 0, tiled=True)]
    ppermute x23 -> x2, starting transfers between devices: 41.4 us -> 0.07 us  [swap(): return lax.ppermute(value, axis, [(i, i ^ step) for i in range(size)])]
    ppermute x23 -> x2, waiting for transfers between devices: 19.6 us -> 1.9 us  [swap(): return lax.ppermute(value, axis, [(i, i ^ step) for i in range(size)])]
    unnamed x18 -> x32, local copies, waits for them, and re-layouts: 0.08 us -> 16.1 us
    all_to_all x0 -> x1, waiting for transfers between devices: none -> 6.34 us  [body(): got = lax.all_to_all(sent, 'feat', 0, 0, tiled=True)]
    all_to_all x0 -> x1, starting transfers between devices: none -> 4.06 us  [body(): got = lax.all_to_all(sent, 'feat', 0, 0, tiled=True)]
    pallas_call x6 -> x5, Pallas kernels: 27.3 us -> 25.8 us  [call(): pl.pallas_call(kernel, out_shape=tuple((jax.ShapeDtypeStruct(shape, dtype...]
  transfers between devices with their start and end apart: 23 -> 3, of which waited for: 7 -> 2; matrix products, arithmetic and copies ran while one was open for 0% -> 0% of each run, Pallas kernels for 27% -> 18%
where the time goes in v3:
time: 112 us; the launch traced here: 111 us
  blocking collectives  54.3 us (48%)
  Pallas kernels  25.8 us (23%)
  local copies, waits for them, and re-layouts  16.2 us (14%)
  waiting for transfers between devices  8.24 us (7%)
  starting transfers between devices  4.13 us (4%)
  between operations  1.41 us (1%)
    all_to_all x1, blocking collectives, body(): mine = lax.all_to_all(parcel, 'feat', 0, 0, tiled=True)  36.1 us
    pallas_call x5, Pallas kernels, call(): pl.pallas_call(kernel, out_shape=tuple((jax.ShapeDtypeStruct(shape, dtype...  25.8 us
    all_to_all x1, blocking collectives, body(): lax.all_to_all(shares.reshape(n_feat, seed_count, width), 'feat', 0, 0, t...  18.2 us
    unnamed x32, local copies, waits for them, and re-layouts  16.1 us
    all_to_all x1, waiting for transfers between devices, body(): got = lax.all_to_all(sent, 'feat', 0, 0, tiled=True)  6.34 us
    all_to_all x1, starting transfers between devices, body(): got = lax.all_to_all(sent, 'feat', 0, 0, tiled=True)  4.06 us
  transfers between devices with their start and end apart: 3, of which 2 were waited for; matrix products, arithmetic and copies ran while one was open for 0% of the time, Pallas kernels for 18%

profile of v3, /device:TPU:0, one launch (start us, length us, event | category | flops | bytes accessed | tf_op | source)
XLA Modules:
  0.0 111.1 jit_solution(8584317534599202024)
XLA Ops:
  0.6 0.0 copy-start.2
  0.6 1.7 %copy-done.2 = bf16[96,12288]{1,0:T(8,128)(2,1)S(1)} copy-done((bf16[96,12288]{1,0:T(8,128)(2,1)S(1)}, bf16[96,12288]{1,0:T(8,128)(2,1)}, u32[]{:S(2)}) %copy-start.2) | copy-done | bytes 2359320
  2.3 0.0 copy-start.9
  2.3 0.9 copy-done.9
  3.2 0.0 copy-start.10
  3.2 0.9 copy-done.10
  4.1 0.0 copy-start.11
  4.1 0.7 copy-done.11
  4.8 0.0 copy-start.13
  4.8 0.7 copy-done.13
  5.4 2.9 %turn.1 = (f32[12288,128]{1,0:T(8,128)S(1)}, bf16[8,144,512]{2,1,0:T(8,128)(2,1)S(1)}) custom-call(bf16[96,12288]{1,0:T(8,128)(2,1)S(1)} %copy-done.2, s32[1,64]{1,0:T(1,128)S(1)} %bitcast.8, s32[15,64]{1,0:T(8,128)S(1)} %bitcast.6, bf16[96,512]{1,0:T(8,128)(2,1)S(1)} %copy-done.9, bf16[96,512]{1,0:T(8,128)(2,1)S(1)} %copy-done.10), custom_call_target="tpu_custom_call" | custom-call | bytes 10800000 | tf_op jit(solution)/shard_map/turn/pallas_call | solution.py:223
  8.4 0.0 copy-start
  8.4 2.7 %copy-done = f32[12288,128]{1,0:T(8,128)} copy-done((f32[12288,128]{1,0:T(8,128)}, f32[12288,128]{1,0:T(8,128)S(1)}, u32[]{:S(2)}) %copy-start) | copy-done | bytes 6291480
  11.0 0.0 copy-start.14
  11.0 36.1 %all_to_all.15.mine_ref = bf16[8,144,512]{2,1,0:T(8,128)(2,1)S(1)} all-to-all(bf16[8,144,512]{2,1,0:T(8,128)(2,1)S(1)} %get-tuple-element.12), channel_id=1, replica_groups=mesh['groups'=2,'feat'=8,'rep'=2] {'feat'}, dimensions={0} | all-to-all | bytes 2359296 | tf_op jit(solution)/shard_map/all_to_all | solution.py:248
  47.2 0.0 collective-permute-start
  47.2 0.0 copy-done.14
  47.2 0.2 reduce
  47.4 0.1 reshape.11.nbr_ref
  47.5 0.0 copy-start.1
  47.5 2.8 %copy-done.1 = f32[12288,128]{1,0:T(8,128)S(1)} copy-done((f32[12288,128]{1,0:T(8,128)S(1)}, f32[12288,128]{1,0:T(8,128)}, u32[]{:S(2)}) %copy-start.1) | copy-done | bytes 6291480
  50.3 0.0 copy-start.12
  50.3 18.4 %mean.1 = bf16[8,144,128]{2,1,0:T(8,128)(2,1)} custom-call(s32[15360]{0:T(1024)S(1)} %reshape.11.nbr_ref, f32[12288,128]{1,0:T(8,128)S(1)} %copy-done.1), custom_call_target="tpu_custom_call" | custom-call | bytes 72000000 | tf_op jit(solution)/shard_map/mean/pallas_call | solution.py:223
  68.7 4.1 %all-to-all-start = ((bf16[8,144,128]{2,1,0:T(8,128)(2,1)}), bf16[8,144,128]{2,1,0:T(8,128)(2,1)}, u32[]{:S(2)}, u32[]{:S(2)}) async-start(bf16[8,144,128]{2,1,0:T(8,128)(2,1)} %mean.1), calls=%async_computation | async-start | bytes 589824 | tf_op jit(solution)/shard_map/all_to_all | solution.py:261
  73.4 0.0 collective-permute-done.other_ref
  73.4 0.0 copy-done.12
  73.4 1.9 %prepare.1 = (f32[192,512]{1,0:T(8,128)S(1)}, bf16[8,96,512]{2,1,0:T(8,128)(2,1)S(1)}, bf16[2,512,192]{2,1,0:T(8,128)(2,1)S(1)}, bf16[2,512,192]{2,1,0:T(8,128)(2,1)S(1)}) custom-call(bf16[8,144,512]{2,1,0:T(8,128)(2,1)S(1)} %all_to_all.15.mine_ref, bf16[8,144,512]{2,1,0:T(8,128)(2,1)S(1)} %collective-permute-done.other_ref, f32[1,512]{1,0:T(1,128)S(1)} %bitcast.7), custom_call_target="tpu_custom_call" | custom-call | bytes 10800000 | tf_op jit(solution)/shard_map/prepare/pallas_call | solution.py:223
  75.3 0.0 copy-start.3
  75.3 0.9 copy-done.3
  76.2 0.0 copy-start.7
  76.2 0.8 copy-done.7
  76.9 6.3 %all-to-all-done.got_ref = bf16[8,144,128]{2,1,0:T(8,128)(2,1)} async-done(((bf16[8,144,128]{2,1,0:T(8,128)(2,1)}), bf16[8,144,128]{2,1,0:T(8,128)(2,1)}, u32[]{:S(2)}, u32[]{:S(2)}) %all-to-all-start) | async-done | bytes 294944 | tf_op jit(solution)/shard_map/all_to_all | solution.py:261
  83.3 0.0 copy-start.4
  83.3 1.1 %copy-done.4 = bf16[8,96,512]{2,1,0:T(8,128)(2,1)S(1)} copy-done((bf16[8,96,512]{2,1,0:T(8,128)(2,1)S(1)}, bf16[8,96,512]{2,1,0:T(8,128)(2,1)}, u32[]{:S(2)}) %copy-start.4) | copy-done | bytes 786456
  84.4 0.0 copy-start.5
  84.4 1.0 copy-done.5
  85.4 0.0 copy-start.6
  85.4 1.0 copy-done.6
  86.5 0.0 copy-start.8
  86.5 1.0 copy-done.8
  87.5 2.2 %layers.1 = (bf16[192,512]{1,0:T(8,128)(2,1)}, bf16[2,192,512]{2,1,0:T(8,128)(2,1)S(1)}, bf16[512,512]{1,0:T(8,128)(2,1)S(1)}) custom-call(s32[1,1]{1,0:T(1,128)S(6)} %copy.13.count_ref, bf16[8,144,128]{2,1,0:T(8,128)(2,1)} %all-to-all-done.got_ref, f32[192,512]{1,0:T(8,128)S(1)} %copy-done.8, bf16[8,96,512]{2,1,0:T(8,128)(2,1)S(1)} %copy-done.4, ...), custom_call_target="tpu_custom_call" | custom-call | bytes 3600000 | tf_op jit(solution)/shard_map/layers/pallas_call | solution.py:223
  89.7 0.1 collective-permute-start.1
  89.8 1.9 %collective-permute-done.1.got_ref = bf16[512,512]{1,0:T(8,128)(2,1)S(1)} collective-permute-done((bf16[512,512]{1,0:T(8,128)(2,1)S(1)}, bf16[512,512]{1,0:T(8,128)(2,1)S(1)}, u32[]{:S(2)}, u32[]{:S(2)}) %collective-permute-start.1) | collective-permute-done | bytes 524320 | tf_op jit(solution)/shard_map/ppermute | solution.py:195
  91.7 0.4 share.1
  92.1 0.0 copy-start.15
  92.1 18.2 %all_to_all.16 = bf16[8,64,512]{2,1,0:T(8,128)(2,1)S(1)} all-to-all(bf16[8,64,512]{2,1,0:T(8,128)(2,1)S(1)} %bitcast.5), channel_id=1, replica_groups=mesh['groups'=2,'feat'=8,'rep'=2] {'feat'}, dimensions={0} | all-to-all | bytes 1048576 | tf_op jit(solution)/shard_map/all_to_all | solution.py:296
  110.3 0.1 convert_reduce_fusion
  110.4 0.0 copy-done.15
  110.4 0.6 maximum_convert_fusion
Async XLA Ops:
  0.6 1.7 %copy-start.2 = (bf16[96,12288]{1,0:T(8,128)(2,1)S(1)}, bf16[96,12288]{1,0:T(8,128)(2,1)}, u32[]{:S(2)}) copy-start(bf16[96,12288]{1,0:T(8,128)(2,1)} %src_ref.1) | copy-start | bytes 7077892
  2.3 0.9 copy-start.9
  3.2 0.9 copy-start.10
  4.1 0.7 copy-start.11
  4.8 0.7 copy-start.13
  8.4 2.7 %copy-start = (f32[12288,128]{1,0:T(8,128)}, f32[12288,128]{1,0:T(8,128)S(1)}, u32[]{:S(2)}) copy-start(f32[12288,128]{1,0:T(8,128)S(1)} %get-tuple-element.11.table_ref) | copy-start | bytes 18874372
  11.0 36.2 %copy-start.14 = (s32[8,1,10,192]{3,1,2,0:T(1,128)S(1)}, s32[8,1,10,192]{3,1,2,0:T(1,128)}, u32[]{:S(2)}) copy-start(s32[8,1,10,192]{3,1,2,0:T(1,128)} %param.12) | copy-start | bytes 184324
  47.2 26.2 %collective-permute-start = (bf16[8,144,512]{2,1,0:T(8,128)(2,1)S(1)}, bf16[8,144,512]{2,1,0:T(8,128)(2,1)S(1)}, u32[]{:S(2)}, u32[]{:S(2)}) collective-permute-start(bf16[8,144,512]{2,1,0:T(8,128)(2,1)S(1)} %all_to_all.15.mine_ref), channel_id=1, source_target_pairs={{0,1},{1,0},{2,3},{3,2},{4,5},{5,4},{6,7},{7,6},{8,9},{9,8},{10,11... | collective-permute-start | bytes 3538952 | tf_op jit(solution)/shard_map/ppermute | solution.py:195
  47.5 2.8 %copy-start.1 = (f32[12288,128]{1,0:T(8,128)S(1)}, f32[12288,128]{1,0:T(8,128)}, u32[]{:S(2)}) copy-start(f32[12288,128]{1,0:T(8,128)} %copy-done) | copy-start | bytes 18874372
  50.3 23.1 %copy-start.12 = (f32[512]{0:T(512)S(1)}, f32[512]{0:T(512)}, u32[]{:S(2)}) copy-start(f32[512]{0:T(512)} %param.18) | copy-start | bytes 6148
  68.7 14.6 %all-to-all-start = ((bf16[8,144,128]{2,1,0:T(8,128)(2,1)}), bf16[8,144,128]{2,1,0:T(8,128)(2,1)}, u32[]{:S(2)}, u32[]{:S(2)}) async-start(bf16[8,144,128]{2,1,0:T(8,128)(2,1)} %mean.1), calls=%async_computation | async-start | bytes 589824 | tf_op jit(solution)/shard_map/all_to_all | solution.py:261
  75.3 0.9 copy-start.3
  76.2 0.8 copy-start.7
  83.3 1.1 %copy-start.4 = (bf16[8,96,512]{2,1,0:T(8,128)(2,1)S(1)}, bf16[8,96,512]{2,1,0:T(8,128)(2,1)}, u32[]{:S(2)}) copy-start(bf16[8,96,512]{2,1,0:T(8,128)(2,1)} %copy-done.3) | copy-start | bytes 2359300
  84.4 1.0 copy-start.5
  85.4 1.0 copy-start.6
  86.5 1.0 copy-start.8
  89.7 2.0 %collective-permute-start.1 = (bf16[512,512]{1,0:T(8,128)(2,1)S(1)}, bf16[512,512]{1,0:T(8,128)(2,1)S(1)}, u32[]{:S(2)}, u32[]{:S(2)}) collective-permute-start(bf16[512,512]{1,0:T(8,128)(2,1)S(1)} %get-tuple-element.19), channel_id=1, source_target_pairs={{0,1},{1,0},{2,3},{3,2},{4,5},{5,4},{6,7},{7,6},{8,9},{9,8},{10,11... | collective-permute-start | bytes 1572872 | tf_op jit(solution)/shard_map/ppermute | solution.py:195
  92.1 18.3 %copy-start.15 = (f32[512]{0:T(512)S(1)}, f32[512]{0:T(512)}, u32[]{:S(2)}) copy-start(f32[512]{0:T(512)} %param.21) | copy-start | bytes 6148

commit v4 on v0

v4 whole, which is shorter than its diff:
```python
import functools

import jax
import jax.numpy as jnp
from jax import lax
from jax.experimental import pallas as pl
from jax.experimental.pallas import tpu as pltpu
from jax.sharding import PartitionSpec as P

LANES = 128
MIB = 1024 * 1024


def folds(fslice, pcap):
    return 4 * fslice == 3 * LANES and pcap % 64 == 0


def pack_kernel(
    n_feat,
    pcap,
    src_hbm,
    seed_hbm,
    nbr_hbm,
    w_self_hbm,
    w_nbr_hbm,
    *refs,
):
    half = n_feat // 2
    parcel_refs = refs[:half]
    src_ref, seed_ref, nbr_ref, w_self_ref, w_nbr_ref, sems = refs[half:]
    fslice = w_self_ref.shape[0]
    copies = [
        pltpu.make_async_copy(a, b, sems.at[i])
        for i, (a, b) in enumerate(
            (
                (src_hbm.at[:, pl.ds(0, src_ref.shape[1])], src_ref),
                (seed_hbm, seed_ref),
                (nbr_hbm, nbr_ref),
                (w_self_hbm, w_self_ref),
                (w_nbr_hbm, w_nbr_ref),
            )
        )
    ]
    for copy in copies:
        copy.start()
    for copy in copies:
        copy.wait()
    feat_pos = lax.axis_index("feat")
    first_core = lax.axis_index("rep") == 0
    idx = jnp.concatenate([seed_ref[...], nbr_ref[...]], axis=0)
    high = lax.shift_right_logical(idx, 7)
    digits = jnp.concatenate([high, idx - high * 128], axis=1).astype(jnp.float32)
    digits = digits.astype(jnp.bfloat16)
    weight = jnp.where(first_core, w_self_ref[...], w_nbr_ref[...])
    for s, parcel_ref in enumerate(parcel_refs):
        parcel_ref[:fslice, :] = weight
        for place, step in enumerate((s, s ^ half)):
            at = pl.multiple_of(jnp.bitwise_xor(feat_pos, step) * (2 * pcap), LANES)
            block = src_ref[:, pl.ds(at, 2 * pcap)].astype(jnp.float32)
            own = jnp.where(first_core, block[:, :pcap], block[:, pcap:])
            if place == 0:
                near_side = own
        both = jnp.concatenate([near_side, own], axis=1)
        parcel_ref[fslice:, : 2 * pcap] = both.astype(jnp.bfloat16)
        parcel_ref[fslice : fslice + idx.shape[0], 2 * pcap :] = digits


def turn_kernel(src_hbm, table_ref, src_ref, sems):
    fslice, nodes = src_hbm.shape
    pieces = sems.shape[0]
    piece = nodes // pieces
    width = 512
    copies = [
        pltpu.make_async_copy(
            src_hbm.at[:, pl.ds(i * piece, piece)], src_ref.at[:, pl.ds(i * piece, piece)], sems.at[i]
        )
        for i in range(pieces)
    ]
    for copy in copies:
        copy.start()
    for i, copy in enumerate(copies):
        copy.wait()

        def turn(step, carry):
            at = pl.multiple_of(i * piece + step * width, width)
            block = src_ref[:, pl.ds(at, width)].astype(jnp.float32)
            table_ref[pl.ds(at, width), :fslice] = block.T
            return carry

        lax.fori_loop(0, piece // width, turn, 0)


def mean_kernel(steps, fanout, pcap, fslice, nbr_hbm, table_ref, *refs):
    out_refs, (total, nbr_ref, sems) = refs[: len(steps)], refs[len(steps) :]
    feat_pos = lax.axis_index("feat")
    copies = [
        pltpu.make_async_copy(nbr_hbm.at[jnp.bitwise_xor(feat_pos, step)], nbr_ref.at[i], sems.at[i])
        for i, step in enumerate(steps)
    ]
    for copy in copies:
        copy.start()
    for i, out_ref in enumerate(out_refs):
        copies[i].wait()

        def group(g, carry):
            at = pl.multiple_of(g * 8, 8)
            for u in range(8):
                rows = [table_ref[nbr_ref[i, 0, at + (k * pcap + u)]] for k in range(fanout)]
                while len(rows) > 1:
                    rows = [a + b for a, b in zip(rows[::2], rows[1::2])] + (
                        [rows[-1]] if len(rows) % 2 else []
                    )
                total[pl.ds(at + u, 1), :] = rows[0]
            return carry

        lax.fori_loop(0, pcap // 8, group, 0)
        mean = total[...] / fanout
        if folds(fslice, pcap):
            part = pcap // 4
            lane = lax.broadcasted_iota(jnp.int32, (part, LANES), 1)
            tail = mean[3 * part :]
            for b in range(3):
                shift = (fslice - 32 * b) % LANES
                moved = pltpu.roll(tail, shift, 1) if shift else tail
                out_ref[pl.ds(b * part, part), :] = jnp.where(
                    lane < fslice, mean[b * part : (b + 1) * part], moved
                ).astype(jnp.bfloat16)
        else:
            out_ref[...] = mean[:, :fslice].astype(jnp.bfloat16)


def unfold(block, fslice, pcap):
    if block.shape[0] == pcap:
        return block
    part = block.shape[0] // 3
    wide = block.astype(jnp.float32)
    lane = lax.broadcasted_iota(jnp.int32, (part, LANES), 1)
    tail = pltpu.roll(wide[:part], LANES - fslice, 1)
    for b in (1, 2):
        shift = (32 * b - fslice) % LANES
        moved = wide[b * part : (b + 1) * part]
        moved = pltpu.roll(moved, shift, 1) if shift else moved
        tail = jnp.where(lane // 32 == b, moved, tail)
    return jnp.concatenate([wide, tail], axis=0)[:, :fslice].astype(jnp.bfloat16)


def halves_kernel(*refs):
    out_ref = refs[-1]
    for s, ref in enumerate(refs[:-1]):
        out_ref[s] = ref[: out_ref.shape[1], :]


def prepare_kernel(half, n_idx, *refs):
    parcel_refs, mean_refs = refs[:half], refs[half : 2 * half]
    other_ref, bias_ref, w_ref, pre_ref, cross_ref = refs[2 * half :]
    fslice = w_ref.shape[1]
    pcap, width = pre_ref.shape
    first_core = lax.axis_index("rep") == 0
    both = jnp.zeros((2 * pcap, width), jnp.float32)
    far = jnp.zeros((pcap, width), jnp.float32)
    for s in range(half):
        mine, other = parcel_refs[s][:fslice, :], other_ref[s]
        w_nbr = jnp.where(first_core, other, mine)
        w_ref[s] = w_nbr
        feats = parcel_refs[s][fslice:, : 2 * pcap].astype(jnp.float32).T.astype(jnp.bfloat16)
        both = both + jnp.dot(
            feats, jnp.where(first_core, mine, other), preferred_element_type=jnp.float32
        )
        far = far + jnp.dot(
            unfold(mean_refs[s][...], fslice, pcap), w_nbr, preferred_element_type=jnp.float32
        )
        rows = pl.ds(pcap + s // 4 * n_idx, n_idx)
        cross_ref[rows, s % 4 * LANES : (s % 4 + 1) * LANES] = parcel_refs[s][
            fslice : fslice + n_idx, 2 * pcap :
        ]
    pre_ref[...] = both[:pcap] + bias_ref[...]
    cross_ref[:pcap, :] = (both[pcap:] + far).astype(jnp.bfloat16)


def store_times(pcap, blocks, out_ref):
    n_idx, pair = blocks[0].shape
    seed_count = pair // 2
    core_rows = lax.axis_index("feat") * (2 * pcap)
    rep_pos = lax.axis_index("rep")
    row = lax.broadcasted_iota(jnp.int32, (2 * pcap, pair), 0)
    slot = jnp.where(
        row < pcap, row + core_rows + rep_pos * pcap, row + core_rows - rep_pos * pcap
    ).astype(jnp.float32)
    low = lax.broadcasted_iota(jnp.int32, (n_idx, pair), 1) < seed_count
    for s in range(0, len(blocks), 2):
        first, second = blocks[s].astype(jnp.float32), blocks[s + 1].astype(jnp.float32)
        high_part = jnp.where(low, first, pltpu.roll(second, seed_count, 1))
        low_part = jnp.where(low, pltpu.roll(first, seed_count, 1), second)
        name = high_part * 128.0 + low_part
        own = jnp.where(slot == name[:1], 1.0, 0.0)
        near = jnp.zeros((2 * pcap, pair), jnp.float32)
        for k in range(1, n_idx):
            near = near + jnp.where(slot == name[k : k + 1], 1.0, 0.0)
        place = pl.ds(s * seed_count, pair)
        out_ref[place, : 2 * pcap] = own.T.astype(jnp.bfloat16)
        out_ref[place, 2 * pcap :] = near.T.astype(jnp.bfloat16)


def near_times_kernel(half, fslice, pcap, n_idx, *refs):
    blocks = [ref[fslice : fslice + n_idx, 2 * pcap :] for ref in refs[:half]]
    store_times(pcap, blocks, refs[half])


def far_times_kernel(
    half, n_idx, fanout_two, cross_ref, hidden_ref, ws_ref, wn_ref, out_ref, value_ref
):
    pcap = hidden_ref.shape[0]
    blocks = [
        cross_ref[
            pl.ds(pcap + s // 4 * n_idx, n_idx), s % 4 * LANES : (s % 4 + 1) * LANES
        ]
        for s in range(half)
    ]
    store_times(pcap, blocks, out_ref)
    store_values(hidden_ref[...], ws_ref, wn_ref, fanout_two, value_ref)


def store_values(hidden, ws_ref, wn_ref, fanout_two, value_ref):
    value_ref[0] = jnp.dot(hidden, ws_ref[...], preferred_element_type=jnp.float32).astype(
        jnp.bfloat16
    )
    value_ref[1] = (
        jnp.dot(hidden, wn_ref[...], preferred_element_type=jnp.float32) / fanout_two
    ).astype(jnp.bfloat16)


def layer_kernel(half, count_ref, *refs):
    mean_refs = refs[:half]
    pre_ref, w_ref, cross_ref, hidden_ref = refs[half:]
    pcap, width = hidden_ref.shape
    fslice = w_ref.shape[1]
    pre = pre_ref[...] + cross_ref[:pcap, :].astype(jnp.float32)
    for s in range(half):
        pre = pre + jnp.dot(
            unfold(mean_refs[s][...], fslice, pcap), w_ref[s], preferred_element_type=jnp.float32
        )
    live = lax.broadcasted_iota(jnp.int32, (pcap, width), 0) < count_ref[0, 0]
    hidden_ref[...] = jnp.where(live, jnp.maximum(pre, 0.0), 0.0).astype(jnp.bfloat16)


def share_kernel(
    half, fanout_two, near_ref, far_ref, value_ref, hidden_ref, ws_ref, wn_ref, *refs
):
    out_refs, other_ref = refs[:half], refs[half]
    store_values(hidden_ref[...], ws_ref, wn_ref, fanout_two, other_ref)
    values = jnp.concatenate(
        [value_ref[0], other_ref[0], value_ref[1], other_ref[1]], axis=0
    )
    near = jnp.dot(near_ref[...], values, preferred_element_type=jnp.float32)
    far = jnp.dot(far_ref[...], values, preferred_element_type=jnp.float32)
    rows = out_refs[0].shape[0] // 2
    for s, out_ref in enumerate(out_refs):
        out_ref[:rows, :] = near[s * rows : (s + 1) * rows].astype(jnp.bfloat16)
        out_ref[rows:, :] = far[s * rows : (s + 1) * rows].astype(jnp.bfloat16)


def side_sum_kernel(*refs):
    near_ref, far_ref = refs[-2:]
    rows = near_ref.shape[0]
    total = refs[0][...].astype(jnp.float32)
    for ref in refs[1:-2]:
        total = total + ref[...].astype(jnp.float32)
    near_ref[...] = total[:rows]
    far_ref[...] = total[rows:].astype(jnp.bfloat16)


def swap(value, axis, step):
    size = lax.axis_size(axis)
    return lax.ppermute(value, axis, [(i, i ^ step) for i in range(size)])


def body(
    src_feats,
    nbr_one,
    counts,
    seed_rows,
    nbr_two,
    w1_self,
    w1_nbr,
    bias_one,
    w2_self,
    w2_nbr,
    bias_two,
):
    n_feat = lax.axis_size("feat")
    half = n_feat // 2
    fslice, nodes = src_feats.shape
    fanout_one, pcap = nbr_one.shape[2:]
    width = w1_self.shape[1]
    seed_count, fanout_two = nbr_two.shape
    n_idx = fanout_two + 1
    bf16 = jnp.bfloat16
    vmem = pl.BlockSpec(memory_space=pltpu.VMEM)
    smem = pl.BlockSpec(memory_space=pltpu.SMEM)
    hbm = pl.BlockSpec(memory_space=pltpu.HBM)
    anywhere = pl.BlockSpec(memory_space=pl.ANY)
    table_bytes = nodes * LANES * 4

    def call(kernel, name, shapes, ins, args, after=(), scratch=(), limit=16 * MIB, cost_us=1):
        def wrapped(*refs):
            kernel(*refs[: len(args)], *refs[len(args) + len(after) :])

        return pl.pallas_call(
            wrapped,
            out_shape=tuple(jax.ShapeDtypeStruct(shape, dtype) for shape, dtype in shapes),
            in_specs=[*ins, *([anywhere] * len(after))],
            out_specs=(vmem,) * len(shapes),
            scratch_shapes=scratch,
            compiler_params=pltpu.CompilerParams(vmem_limit_bytes=limit),
            cost_estimate=pl.CostEstimate(
                flops=int(cost_us * 1_100_000_000), bytes_accessed=0, transcendentals=0
            ),
            name=name,
        )(*args, *after)

    def send(chunks):
        return [chunk if s == 0 else swap(chunk, "feat", s) for s, chunk in enumerate(chunks)]

    parcels = call(
        functools.partial(pack_kernel, n_feat, pcap),
        "pack",
        [((2 * fslice, width), bf16)] * half,
        [hbm] * 5,
        (src_feats, seed_rows[None], nbr_two.T, w1_self, w1_nbr),
        scratch=[
            pltpu.VMEM((fslice, n_feat * 2 * pcap), bf16),
            pltpu.VMEM((1, seed_count), jnp.int32),
            pltpu.VMEM((fanout_two, seed_count), jnp.int32),
            pltpu.VMEM((fslice, width), bf16),
            pltpu.VMEM((fslice, width), bf16),
            pltpu.SemaphoreType.DMA((5,)),
        ],
        cost_us=2,
    )
    arrived = send(parcels)
    (table,) = call(
        turn_kernel,
        "turn",
        [((nodes, LANES), jnp.float32)],
        [hbm],
        (src_feats,),
        after=(parcels[0],),
        scratch=[pltpu.VMEM((fslice, nodes), bf16), pltpu.SemaphoreType.DMA((6,))],
        limit=table_bytes + 12 * MIB,
        cost_us=3,
    )
    table = table.reshape(nodes, 1, LANES)
    neighbors = nbr_one.reshape(n_feat, 1, fanout_one * pcap)
    chunk_shape = (pcap // 4 * 3, LANES) if folds(fslice, pcap) else (pcap, fslice)

    def means(steps, after):
        return call(
            functools.partial(mean_kernel, steps, fanout_one, pcap, fslice),
            "mean",
            [(chunk_shape, bf16)] * len(steps),
            [anywhere, vmem],
            (neighbors, table),
            after=after,
            scratch=[
                pltpu.VMEM((pcap, LANES), jnp.float32),
                pltpu.SMEM((len(steps), 1, fanout_one * pcap), jnp.int32),
                pltpu.SemaphoreType.DMA((len(steps),)),
            ],
            limit=table_bytes + 8 * MIB,
            cost_us=2.3 * len(steps),
        )

    far_means = means([s + half for s in range(half)], ())
    far_arrived = send(far_means)
    (halves,) = call(
        halves_kernel,
        "halves",
        [((half, fslice, width), bf16)],
        [vmem] * half,
        arrived,
        after=far_means[:1],
    )
    other_halves = swap(halves, "rep", 1)
    (last_mean,) = means([half - 1], far_means[:1])
    w_nbr, pre, cross = call(
        functools.partial(prepare_kernel, half, n_idx),
        "prepare",
        [
            ((half, fslice, width), bf16),
            ((pcap, width), jnp.float32),
            ((pcap + -(-half // 4) * n_idx, width), bf16),
        ],
        [vmem] * (2 * half + 2),
        (*arrived, *far_arrived, other_halves, bias_one[None]),
        after=(last_mean,),
        cost_us=2,
    )
    cross_arrived = swap(cross, "feat", half)
    near_means = means(list(range(half - 1)), (cross,))
    near_arrived = send([*near_means, last_mean])
    (near_times,) = call(
        functools.partial(near_times_kernel, half, fslice, pcap, n_idx),
        "near_times",
        [((half * seed_count, 4 * pcap), bf16)],
        [vmem] * half,
        arrived,
        after=near_means[:1],
    )
    (hidden,) = call(
        functools.partial(layer_kernel, half),
        "hidden",
        [((pcap, width), bf16)],
        [smem] + [vmem] * (half + 3),
        (counts, *near_arrived, pre, w_nbr, cross_arrived),
    )
    other_hidden = swap(hidden, "rep", 1)
    far_times, value = call(
        functools.partial(far_times_kernel, half, n_idx, fanout_two),
        "far_times",
        [((half * seed_count, 4 * pcap), bf16), ((2, pcap, width), bf16)],
        [vmem] * 4,
        (cross_arrived, hidden, w2_self, w2_nbr),
    )
    shares = call(
        functools.partial(share_kernel, half, fanout_two),
        "share",
        [((2 * seed_count, width), bf16)] * half,
        [vmem] * 6,
        (near_times, far_times, value, other_hidden, w2_self, w2_nbr),
        scratch=[pltpu.VMEM((2, pcap, width), bf16)],
        limit=32 * MIB,
    )
    near_sum, far_sum = call(
        side_sum_kernel,
        "side_sum",
        [((seed_count, width), jnp.float32), ((seed_count, width), bf16)],
        [vmem] * half,
        send(shares),
    )
    pre_two = near_sum + swap(far_sum, "feat", half).astype(jnp.float32) + bias_two
    seed_out = jnp.maximum(pre_two, 0.0).astype(bf16)
    return (hidden[None, None], seed_out)


def solution(mesh):
    placed = (
        P("feat", "groups"),
        P("groups", "rep", None, None),
        P(("groups", "feat"), "rep"),
        P(("groups", "feat", "rep")),
        P(("groups", "feat", "rep"), None),
        P("feat", None),
        P("feat", None),
        P(),
        P(),
        P(),
        P(),
    )
    return jax.shard_map(
        body,
        mesh=mesh,
        in_specs=placed,
        out_specs=(P(("groups", "feat"), "rep", None, None), P(("groups", "feat", "rep"), None)),
        check_vma=False,
    )
```

time: 209 us -> 84.3 us (0.40)
  waiting for transfers between devices: 110 us -> 14.7 us
  local copies, waits for them, and re-layouts: 68.6 us -> 11.3 us
  Pallas kernels: 0 us -> 36.7 us
  starting transfers between devices: 0.08 us -> 18.9 us
  between operations: 15 us -> 1.53 us
  other arithmetic: 12.1 us -> 0.85 us
  matrix products: 2.83 us -> 0 us
    reduce_scatter x1 -> x0, waiting for transfers between devices: 67 us -> none  [body(): lax.psum_scatter(partial_value.astype(jnp.bfloat16), 'feat', scatter_dime...]
    gather x2 -> x0, local copies, waits for them, and re-layouts: 60.6 us -> none  [the longest x1 54.3 us: body(): jnp.take(node_major, nbr_one[:, 0].reshape(-1), axis=0)]
    all_gather x1 -> x0, waiting for transfers between devices: 43 us -> none  [body(): table = lax.all_gather(hidden, ('feat', 'rep'), axis=0, tiled=True)]
    pallas_call x0 -> x12, Pallas kernels: none -> 36.7 us  [call(): pl.pallas_call(wrapped, out_shape=tuple((jax.ShapeDtypeStruct(shape, dtyp...]
    ppermute x0 -> x16, starting transfers between devices: none -> 18.9 us  [swap(): return lax.ppermute(value, axis, [(i, i ^ step) for i in range(size)])]
    ppermute x0 -> x16, waiting for transfers between devices: none -> 14.7 us  [swap(): return lax.ppermute(value, axis, [(i, i ^ step) for i in range(size)])]
    reduce_sum x2 -> x0, other arithmetic: 7.08 us -> none  [the longest x1 6.94 us: body(): jnp.sum(picked.astype(jnp.float32), axis=1) / fanout_one]
    unnamed x20 -> x30, local copies, waits for them, and re-layouts: 5.9 us -> 11.2 us
  transfers between devices with their start and end apart: 2 -> 16, of which waited for: 2 -> 6; matrix products, arithmetic and copies ran while one was open for 1% -> 0% of each run, Pallas kernels for 0% -> 41%
where the time goes in v4:
time: 84.3 us; the launch traced here: 84 us
  Pallas kernels  36.7 us (44%)
  starting transfers between devices  18.9 us (22%)
  waiting for transfers between devices  14.7 us (17%)
  local copies, waits for them, and re-layouts  11.3 us (13%)
  between operations  1.53 us (2%)
  other arithmetic  0.85 us (1%)
    pallas_call x12, Pallas kernels, call(): pl.pallas_call(wrapped, out_shape=tuple((jax.ShapeDtypeStruct(shape, dtyp...  36.7 us
    ppermute x16, starting transfers between devices, swap(): return lax.ppermute(value, axis, [(i, i ^ step) for i in range(size)])  18.9 us
    ppermute x16, waiting for transfers between devices, swap(): return lax.ppermute(value, axis, [(i, i ^ step) for i in range(size)])  14.7 us
    unnamed x30, local copies, waits for them, and re-layouts  11.2 us
  transfers between devices with their start and end apart: 16, of which 6 were waited for; matrix products, arithmetic and copies ran while one was open for 0% of the time, Pallas kernels for 41%

profile of v4, /device:TPU:0, one launch (start us, length us, event | category | flops | bytes accessed | tf_op | source)
XLA Modules:
  0.0 84.0 jit_solution(9557150170460986616)
XLA Ops:
  0.6 0.0 copy-start
  0.6 1.7 %copy-done = bf16[96,12288]{1,0:T(8,128)(2,1)S(1)} copy-done((bf16[96,12288]{1,0:T(8,128)(2,1)S(1)}, bf16[96,12288]{1,0:T(8,128)(2,1)}, u32[]{:S(2)}) %copy-start) | copy-done | bytes 2359320
  2.3 0.9 %copy-done.5 = bf16[96,512]{1,0:T(8,128)(2,1)S(1)} copy-done((bf16[96,512]{1,0:T(8,128)(2,1)S(1)}, bf16[96,512]{1,0:T(8,128)(2,1)}, u32[]{:S(2)}) %copy-start.5) | copy-done | bytes 98328
  3.2 0.9 %copy-done.6 = bf16[96,512]{1,0:T(8,128)(2,1)S(1)} copy-done((bf16[96,512]{1,0:T(8,128)(2,1)S(1)}, bf16[96,512]{1,0:T(8,128)(2,1)}, u32[]{:S(2)}) %copy-start.6) | copy-done | bytes 98328
  4.1 0.7 copy-done.7
  4.8 0.7 copy-done.9
  5.4 0.8 pack.1
  6.2 0.0 copy-start.13
  6.2 3.0 %collective-permute-start = (bf16[192,512]{1,0:T(8,128)(2,1)S(1)}, bf16[192,512]{1,0:T(8,128)(2,1)S(1)}, u32[]{:S(2)}, u32[]{:S(2)}) collective-permute-start(bf16[192,512]{1,0:T(8,128)(2,1)S(1)} %get-tuple-element.25), channel_id=1, source_target_pairs={{0,2},{2,0},{4,6},{6,4},{8,10},{10,8},{12,14},{14,12},{1,3},{3,1},... | collective-permute-start | bytes 589832 | tf_op jit(solution)/shard_map/ppermute | solution.py:274
  9.2 1.6 %collective-permute-start.1 = (bf16[192,512]{1,0:T(8,128)(2,1)S(1)}, bf16[192,512]{1,0:T(8,128)(2,1)S(1)}, u32[]{:S(2)}, u32[]{:S(2)}) collective-permute-start(bf16[192,512]{1,0:T(8,128)(2,1)S(1)} %get-tuple-element.26), channel_id=1, source_target_pairs={{0,4},{2,6},{4,0},{6,2},{8,12},{10,14},{12,8},{14,10},{1,5},{3,7},... | collective-permute-start | bytes 589832 | tf_op jit(solution)/shard_map/ppermute | solution.py:274
  10.8 0.0 collective-permute-start.2
  10.8 0.0 copy-done.1
  10.8 2.7 %turn.1 = f32[12288,128]{1,0:T(8,128)S(1)} custom-call(bf16[96,12288]{1,0:T(8,128)(2,1)S(1)} %copy-done.1, bf16[192,512]{1,0:T(8,128)(2,1)S(1)} %get-tuple-element.24.refs_1_.refs_0_), custom_call_target="tpu_custom_call" | custom-call | flops 3300000000 | tf_op jit(solution)/shard_map/turn/pallas_call | solution.py:308
  13.5 0.0 copy-start.10
  13.6 2.6 %copy-done.10 = f32[12288,128]{1,0:T(8,128)} copy-done((f32[12288,128]{1,0:T(8,128)}, f32[12288,128]{1,0:T(8,128)S(1)}, u32[]{:S(2)}) %copy-start.10) | copy-done | bytes 6291480
  16.2 0.0 copy-done.13
  16.2 0.2 reduce
  16.4 0.1 reshape.11.refs_0_
  16.5 0.0 copy-start.11
  16.5 2.8 %copy-done.11 = f32[12288,128]{1,0:T(8,128)S(1)} copy-done((f32[12288,128]{1,0:T(8,128)S(1)}, f32[12288,128]{1,0:T(8,128)}, u32[]{:S(2)}) %copy-start.11) | copy-done | bytes 6291480
  19.3 15.4 %mean.3 = (bf16[144,128]{1,0:T(8,128)(2,1)S(1)}, bf16[144,128]{1,0:T(8,128)(2,1)S(1)}, bf16[144,128]{1,0:T(8,128)(2,1)S(1)}, bf16[144,128]{1,0:T(8,128)(2,1)S(1)}) custom-call(s32[8,1,1920]{2,1,0:T(1,128)S(1)} %reshape.11.refs_0_, f32[12288,1,128]{2,1,0:T(1,128)S(1)} %bitcast.9), custom_call_target="tpu_custom_call" | custom-call | flops 10119999488 | tf_op jit(solution)/shard_map/mean/pallas_call | solution.py:308
  34.7 0.0 collective-permute-done.refs_1_
  34.7 0.0 collective-permute-done.1.refs_2_
  34.7 0.0 collective-permute-done.2.refs_3_
  34.7 0.0 copy-start.8
  34.8 0.1 collective-permute-start.6
  34.9 2.0 %collective-permute-start.3 = (bf16[144,128]{1,0:T(8,128)(2,1)S(1)}, bf16[144,128]{1,0:T(8,128)(2,1)S(1)}, u32[]{:S(2)}, u32[]{:S(2)}) collective-permute-start(bf16[144,128]{1,0:T(8,128)(2,1)S(1)} %get-tuple-element.29), channel_id=1, source_target_pairs={{0,2},{2,0},{4,6},{6,4},{8,10},{10,8},{12,14},{14,12},{1,3},{3,1},... | collective-permute-start | bytes 110600 | tf_op jit(solution)/shard_map/ppermute | solution.py:274
  36.8 1.6 %collective-permute-start.4 = (bf16[144,128]{1,0:T(8,128)(2,1)S(1)}, bf16[144,128]{1,0:T(8,128)(2,1)S(1)}, u32[]{:S(2)}, u32[]{:S(2)}) collective-permute-start(bf16[144,128]{1,0:T(8,128)(2,1)S(1)} %get-tuple-element.30), channel_id=1, source_target_pairs={{0,4},{2,6},{4,0},{6,2},{8,12},{10,14},{12,8},{14,10},{1,5},{3,7},... | collective-permute-start | bytes 110600 | tf_op jit(solution)/shard_map/ppermute | solution.py:274
  38.4 0.0 collective-permute-start.5
  38.4 2.4 %mean.4.refs_10_ = bf16[144,128]{1,0:T(8,128)(2,1)S(1)} custom-call(s32[8,1,1920]{2,1,0:T(1,128)S(1)} %reshape.11.refs_0_, f32[12288,1,128]{2,1,0:T(1,128)S(1)} %bitcast.10, bf16[144,128]{1,0:T(8,128)(2,1)S(1)} %get-tuple-element.28.refs_4_.refs_2_), custom_call_target="tpu_custom_call" | custom-call | flops 2529999872 | tf_op jit(solution)/shard_map/mean/pallas_call | solution.py:308
  40.9 3.0 %collective-permute-start.9 = (bf16[144,128]{1,0:T(8,128)(2,1)S(1)}, bf16[144,128]{1,0:T(8,128)(2,1)S(1)}, u32[]{:S(2)}, u32[]{:S(2)}) collective-permute-start(bf16[144,128]{1,0:T(8,128)(2,1)S(1)} %mean.4.refs_10_), channel_id=1, source_target_pairs={{0,6},{2,4},{4,2},{6,0},{8,14},{10,12},{12,10},{14,8},{1,7},{3,5},... | collective-permute-start | bytes 110600 | tf_op jit(solution)/shard_map/ppermute | solution.py:274
  43.8 0.0 collective-permute-done.3.refs_5_
  43.9 0.0 collective-permute-done.4.refs_6_
  43.9 0.0 collective-permute-done.5.refs_7_
  43.9 0.0 collective-permute-done.6.refs_8_
  43.9 0.8 prepare.1
  44.7 2.7 %collective-permute-start.10 = (bf16[208,512]{1,0:T(8,128)(2,1)S(1)}, bf16[208,512]{1,0:T(8,128)(2,1)S(1)}, u32[]{:S(2)}, u32[]{:S(2)}) collective-permute-start(bf16[208,512]{1,0:T(8,128)(2,1)S(1)} %get-tuple-element.32.refs_2_), channel_id=1, source_target_pairs={{0,8},{2,10},{4,12},{6,14},{8,0},{10,2},{12,4},{14,6},{1,9},{3,11}... | collective-permute-start | bytes 638984 | tf_op jit(solution)/shard_map/ppermute | solution.py:274
  47.4 11.1 %mean.5 = (bf16[144,128]{1,0:T(8,128)(2,1)S(1)}, bf16[144,128]{1,0:T(8,128)(2,1)S(1)}, bf16[144,128]{1,0:T(8,128)(2,1)S(1)}) custom-call(s32[8,1,1920]{2,1,0:T(1,128)S(1)} %reshape.11.refs_0_, f32[12288,1,128]{2,1,0:T(1,128)S(1)} %bitcast.11, bf16[208,512]{1,0:T(8,128)(2,1)S(1)} %get-tuple-element.32.refs_2_), custom_call_target="tpu_custom_call" | custom-call | flops 7590000128 | tf_op jit(solution)/shard_map/mean/pallas_call | solution.py:308
  58.5 0.0 copy-start.2
  58.5 0.0 copy-start.3
  58.5 0.6 collective-permute-start.7
  59.1 0.4 collective-permute-start.8
  60.2 0.0 collective-permute-done.9.refs_4_
  60.2 2.3 %collective-permute-done.7.refs_2_ = bf16[144,128]{1,0:T(8,128)(2,1)S(1)} collective-permute-done((bf16[144,128]{1,0:T(8,128)(2,1)S(1)}, bf16[144,128]{1,0:T(8,128)(2,1)S(1)}, u32[]{:S(2)}, u32[]{:S(2)}) %collective-permute-start.7) | collective-permute-done | bytes 36896 | tf_op jit(solution)/shard_map/ppermute | solution.py:274
  62.5 0.5 collective-permute-done.8.refs_3_
  63.0 0.0 collective-permute-done.10.refs_7_.refs_0_
  63.0 1.1 %hidden.1.refs_1_ = bf16[192,512]{1,0:T(8,128)(2,1)} custom-call(s32[1,1]{1,0:T(1,128)S(6)} %copy.13.refs_0_, bf16[144,128]{1,0:T(8,128)(2,1)S(1)} %get-tuple-element.33.refs_1_.refs_4_, bf16[144,128]{1,0:T(8,128)(2,1)S(1)} %collective-permute-done.7.refs_2_, bf16[144,128]{1,0:T(8,128)(2,1)S(1)} %collective-permute-done.8.refs_3_, ...), custom_call_target="tpu_custom_call" | custom-call | flops 1100000000 | tf_op jit(solution)/shard_map/hidden/pallas_call | solution.py:308
  64.1 0.0 collective-permute-start.11
  64.1 0.8 near_times.1.refs_0_
  64.9 0.0 copy-start.4
  64.9 0.9 %copy-done.4 = bf16[192,512]{1,0:T(8,128)(2,1)S(1)} copy-done((bf16[192,512]{1,0:T(8,128)(2,1)S(1)}, bf16[192,512]{1,0:T(8,128)(2,1)}, u32[]{:S(2)}) %copy-start.4) | copy-done | bytes 196632
  65.8 0.8 %far_times.1 = (bf16[256,768]{1,0:T(8,128)(2,1)S(1)}, bf16[2,192,512]{2,1,0:T(8,128)(2,1)S(1)}) custom-call(bf16[208,512]{1,0:T(8,128)(2,1)S(1)} %collective-permute-done.10.refs_7_.refs_0_, bf16[192,512]{1,0:T(8,128)(2,1)S(1)} %copy-done.4, bf16[512,512]{1,0:T(8,128)(2,1)S(1)} %copy-done.2, bf16[512,512]{1,0:T(8,128)(2,1)S(1)} %copy-done.3), custom_call_target="tpu_custom_call" | custom-call | flops 1100000000 | tf_op jit(solution)/shard_map/far_times/pallas_call | solution.py:308
  66.7 0.0 collective-permute-done.11.refs_3_
  66.7 0.8 share.1
  67.5 1.6 %collective-permute-start.12 = (bf16[128,512]{1,0:T(8,128)(2,1)S(1)}, bf16[128,512]{1,0:T(8,128)(2,1)S(1)}, u32[]{:S(2)}, u32[]{:S(2)}) collective-permute-start(bf16[128,512]{1,0:T(8,128)(2,1)S(1)} %get-tuple-element.41), channel_id=1, source_target_pairs={{0,2},{2,0},{4,6},{6,4},{8,10},{10,8},{12,14},{14,12},{1,3},{3,1},... | collective-permute-start | bytes 393224 | tf_op jit(solution)/shard_map/ppermute | solution.py:274
  69.0 0.4 collective-permute-start.13
  69.5 1.5 %collective-permute-start.14 = (bf16[128,512]{1,0:T(8,128)(2,1)S(1)}, bf16[128,512]{1,0:T(8,128)(2,1)S(1)}, u32[]{:S(2)}, u32[]{:S(2)}) collective-permute-start(bf16[128,512]{1,0:T(8,128)(2,1)S(1)} %get-tuple-element.43), channel_id=1, source_target_pairs={{0,6},{2,4},{4,2},{6,0},{8,14},{10,12},{12,10},{14,8},{1,7},{3,5},... | collective-permute-start | bytes 393224 | tf_op jit(solution)/shard_map/ppermute | solution.py:274
  71.0 2.4 %collective-permute-done.12.refs_1_ = bf16[128,512]{1,0:T(8,128)(2,1)S(1)} collective-permute-done((bf16[128,512]{1,0:T(8,128)(2,1)S(1)}, bf16[128,512]{1,0:T(8,128)(2,1)S(1)}, u32[]{:S(2)}, u32[]{:S(2)}) %collective-permute-start.12) | collective-permute-done | bytes 131104 | tf_op jit(solution)/shard_map/ppermute | solution.py:274
  73.4 1.9 %collective-permute-done.13.refs_2_ = bf16[128,512]{1,0:T(8,128)(2,1)S(1)} collective-permute-done((bf16[128,512]{1,0:T(8,128)(2,1)S(1)}, bf16[128,512]{1,0:T(8,128)(2,1)S(1)}, u32[]{:S(2)}, u32[]{:S(2)}) %collective-permute-start.13) | collective-permute-done | bytes 131104 | tf_op jit(solution)/shard_map/ppermute | solution.py:274
  75.4 2.1 %collective-permute-done.14.refs_3_ = bf16[128,512]{1,0:T(8,128)(2,1)S(1)} collective-permute-done((bf16[128,512]{1,0:T(8,128)(2,1)S(1)}, bf16[128,512]{1,0:T(8,128)(2,1)S(1)}, u32[]{:S(2)}, u32[]{:S(2)}) %collective-permute-start.14) | collective-permute-done | bytes 131104 | tf_op jit(solution)/shard_map/ppermute | solution.py:274
  77.4 0.1 side_sum.1
  77.5 0.4 collective-permute-start.15
  77.9 5.4 %collective-permute-done.15 = bf16[64,512]{1,0:T(8,128)(2,1)S(1)} collective-permute-done((bf16[64,512]{1,0:T(8,128)(2,1)S(1)}, bf16[64,512]{1,0:T(8,128)(2,1)S(1)}, u32[]{:S(2)}, u32[]{:S(2)}) %collective-permute-start.15) | collective-permute-done | bytes 65568 | tf_op jit(solution)/shard_map/ppermute | solution.py:274
  83.3 0.7 maximum_convert_fusion
  (13 shorter events, 0.0 us)
Async XLA Ops:
  0.6 1.7 %copy-start = (bf16[96,12288]{1,0:T(8,128)(2,1)S(1)}, bf16[96,12288]{1,0:T(8,128)(2,1)}, u32[]{:S(2)}) copy-start(bf16[96,12288]{1,0:T(8,128)(2,1)} %refs_0_.4) | copy-start | bytes 7077892
  2.3 0.9 %copy-start.5 = (bf16[96,512]{1,0:T(8,128)(2,1)S(1)}, bf16[96,512]{1,0:T(8,128)(2,1)}, u32[]{:S(2)}) copy-start(bf16[96,512]{1,0:T(8,128)(2,1)} %refs_3_.2) | copy-start | bytes 294916
  3.2 0.9 %copy-start.6 = (bf16[96,512]{1,0:T(8,128)(2,1)S(1)}, bf16[96,512]{1,0:T(8,128)(2,1)}, u32[]{:S(2)}) copy-start(bf16[96,512]{1,0:T(8,128)(2,1)} %refs_4_.2) | copy-start | bytes 294916
  4.1 0.7 copy-start.7
  4.8 0.7 copy-start.9
  5.4 5.4 %copy-start.1 = (bf16[96,12288]{1,0:T(8,128)(2,1)S(1)}, bf16[96,12288]{1,0:T(8,128)(2,1)}, u32[]{:S(2)}) copy-start(bf16[96,12288]{1,0:T(8,128)(2,1)} %refs_0_.4) | copy-start | bytes 7077892
  6.2 10.0 %copy-start.13 = (s32[8,1,10,192]{3,1,2,0:T(1,128)S(1)}, s32[8,1,10,192]{3,1,2,0:T(1,128)}, u32[]{:S(2)}) copy-start(s32[8,1,10,192]{3,1,2,0:T(1,128)} %param.12) | copy-start | bytes 184324
  6.2 28.5 %collective-permute-start = (bf16[192,512]{1,0:T(8,128)(2,1)S(1)}, bf16[192,512]{1,0:T(8,128)(2,1)S(1)}, u32[]{:S(2)}, u32[]{:S(2)}) collective-permute-start(bf16[192,512]{1,0:T(8,128)(2,1)S(1)} %get-tuple-element.25), channel_id=1, source_target_pairs={{0,2},{2,0},{4,6},{6,4},{8,10},{10,8},{12,14},{14,12},{1,3},{3,1},... | collective-permute-start | bytes 589832 | tf_op jit(solution)/shard_map/ppermute | solution.py:274
  9.2 25.5 %collective-permute-start.1 = (bf16[192,512]{1,0:T(8,128)(2,1)S(1)}, bf16[192,512]{1,0:T(8,128)(2,1)S(1)}, u32[]{:S(2)}, u32[]{:S(2)}) collective-permute-start(bf16[192,512]{1,0:T(8,128)(2,1)S(1)} %get-tuple-element.26), channel_id=1, source_target_pairs={{0,4},{2,6},{4,0},{6,2},{8,12},{10,14},{12,8},{14,10},{1,5},{3,7},... | collective-permute-start | bytes 589832 | tf_op jit(solution)/shard_map/ppermute | solution.py:274
  10.8 23.9 %collective-permute-start.2 = (bf16[192,512]{1,0:T(8,128)(2,1)S(1)}, bf16[192,512]{1,0:T(8,128)(2,1)S(1)}, u32[]{:S(2)}, u32[]{:S(2)}) collective-permute-start(bf16[192,512]{1,0:T(8,128)(2,1)S(1)} %get-tuple-element.27), channel_id=1, source_target_pairs={{0,6},{2,4},{4,2},{6,0},{8,14},{10,12},{12,10},{14,8},{1,7},{3,5},... | collective-permute-start | bytes 589832 | tf_op jit(solution)/shard_map/ppermute | solution.py:274
  13.5 2.6 %copy-start.10 = (f32[12288,128]{1,0:T(8,128)}, f32[12288,128]{1,0:T(8,128)S(1)}, u32[]{:S(2)}) copy-start(f32[12288,128]{1,0:T(8,128)S(1)} %turn.1) | copy-start | bytes 18874372
  16.5 2.8 %copy-start.11 = (f32[12288,128]{1,0:T(8,128)S(1)}, f32[12288,128]{1,0:T(8,128)}, u32[]{:S(2)}) copy-start(f32[12288,128]{1,0:T(8,128)} %copy-done.10) | copy-start | bytes 18874372
  19.3 19.1 %copy-start.12 = (f32[12288,128]{1,0:T(8,128)S(1)}, f32[12288,128]{1,0:T(8,128)}, u32[]{:S(2)}) copy-start(f32[12288,128]{1,0:T(8,128)} %copy-done.10) | copy-start | bytes 18874372
  34.7 9.1 %copy-start.8 = (f32[512]{0:T(512)S(1)}, f32[512]{0:T(512)}, u32[]{:S(2)}) copy-start(f32[512]{0:T(512)} %param.18) | copy-start | bytes 6148
  34.8 9.1 %collective-permute-start.6 = (bf16[4,96,512]{2,1,0:T(8,128)(2,1)S(1)}, bf16[4,96,512]{2,1,0:T(8,128)(2,1)S(1)}, u32[]{:S(2)}, u32[]{:S(2)}) collective-permute-start(bf16[4,96,512]{2,1,0:T(8,128)(2,1)S(1)} %halves.1), channel_id=1, source_target_pairs={{0,1},{1,0},{2,3},{3,2},{4,5},{5,4},{6,7},{7,6},{8,9},{9,8},{10,11... | collective-permute-start | bytes 1179656 | tf_op jit(solution)/shard_map/ppermute | solution.py:274
  34.9 9.0 %collective-permute-start.3 = (bf16[144,128]{1,0:T(8,128)(2,1)S(1)}, bf16[144,128]{1,0:T(8,128)(2,1)S(1)}, u32[]{:S(2)}, u32[]{:S(2)}) collective-permute-start(bf16[144,128]{1,0:T(8,128)(2,1)S(1)} %get-tuple-element.29), channel_id=1, source_target_pairs={{0,2},{2,0},{4,6},{6,4},{8,10},{10,8},{12,14},{14,12},{1,3},{3,1},... | collective-permute-start | bytes 110600 | tf_op jit(solution)/shard_map/ppermute | solution.py:274
  36.8 7.0 %collective-permute-start.4 = (bf16[144,128]{1,0:T(8,128)(2,1)S(1)}, bf16[144,128]{1,0:T(8,128)(2,1)S(1)}, u32[]{:S(2)}, u32[]{:S(2)}) collective-permute-start(bf16[144,128]{1,0:T(8,128)(2,1)S(1)} %get-tuple-element.30), channel_id=1, source_target_pairs={{0,4},{2,6},{4,0},{6,2},{8,12},{10,14},{12,8},{14,10},{1,5},{3,7},... | collective-permute-start | bytes 110600 | tf_op jit(solution)/shard_map/ppermute | solution.py:274
  38.4 5.4 %collective-permute-start.5 = (bf16[144,128]{1,0:T(8,128)(2,1)S(1)}, bf16[144,128]{1,0:T(8,128)(2,1)S(1)}, u32[]{:S(2)}, u32[]{:S(2)}) collective-permute-start(bf16[144,128]{1,0:T(8,128)(2,1)S(1)} %get-tuple-element.31), channel_id=1, source_target_pairs={{0,6},{2,4},{4,2},{6,0},{8,14},{10,12},{12,10},{14,8},{1,7},{3,5},... | collective-permute-start | bytes 110600 | tf_op jit(solution)/shard_map/ppermute | solution.py:274
  40.9 19.3 %collective-permute-start.9 = (bf16[144,128]{1,0:T(8,128)(2,1)S(1)}, bf16[144,128]{1,0:T(8,128)(2,1)S(1)}, u32[]{:S(2)}, u32[]{:S(2)}) collective-permute-start(bf16[144,128]{1,0:T(8,128)(2,1)S(1)} %mean.4.refs_10_), channel_id=1, source_target_pairs={{0,6},{2,4},{4,2},{6,0},{8,14},{10,12},{12,10},{14,8},{1,7},{3,5},... | collective-permute-start | bytes 110600 | tf_op jit(solution)/shard_map/ppermute | solution.py:274
  44.7 18.3 %collective-permute-start.10 = (bf16[208,512]{1,0:T(8,128)(2,1)S(1)}, bf16[208,512]{1,0:T(8,128)(2,1)S(1)}, u32[]{:S(2)}, u32[]{:S(2)}) collective-permute-start(bf16[208,512]{1,0:T(8,128)(2,1)S(1)} %get-tuple-element.32.refs_2_), channel_id=1, source_target_pairs={{0,8},{2,10},{4,12},{6,14},{8,0},{10,2},{12,4},{14,6},{1,9},{3,11}... | collective-permute-start | bytes 638984 | tf_op jit(solution)/shard_map/ppermute | solution.py:274
  58.5 6.4 %copy-start.2 = (bf16[512,512]{1,0:T(8,128)(2,1)S(1)}, bf16[512,512]{1,0:T(8,128)(2,1)}, u32[]{:S(2)}) copy-start(bf16[512,512]{1,0:T(8,128)(2,1)} %refs_4_.3) | copy-start | bytes 1572868
  58.5 6.4 %copy-start.3 = (bf16[512,512]{1,0:T(8,128)(2,1)S(1)}, bf16[512,512]{1,0:T(8,128)(2,1)}, u32[]{:S(2)}) copy-start(bf16[512,512]{1,0:T(8,128)(2,1)} %refs_5_.1) | copy-start | bytes 1572868
  58.5 4.0 %collective-permute-start.7 = (bf16[144,128]{1,0:T(8,128)(2,1)S(1)}, bf16[144,128]{1,0:T(8,128)(2,1)S(1)}, u32[]{:S(2)}, u32[]{:S(2)}) collective-permute-start(bf16[144,128]{1,0:T(8,128)(2,1)S(1)} %get-tuple-element.34), channel_id=1, source_target_pairs={{0,2},{2,0},{4,6},{6,4},{8,10},{10,8},{12,14},{14,12},{1,3},{3,1},... | collective-permute-start | bytes 110600 | tf_op jit(solution)/shard_map/ppermute | solution.py:274
  59.1 4.0 %collective-permute-start.8 = (bf16[144,128]{1,0:T(8,128)(2,1)S(1)}, bf16[144,128]{1,0:T(8,128)(2,1)S(1)}, u32[]{:S(2)}, u32[]{:S(2)}) collective-permute-start(bf16[144,128]{1,0:T(8,128)(2,1)S(1)} %get-tuple-element.35), channel_id=1, source_target_pairs={{0,4},{2,6},{4,0},{6,2},{8,12},{10,14},{12,8},{14,10},{1,5},{3,7},... | collective-permute-start | bytes 110600 | tf_op jit(solution)/shard_map/ppermute | solution.py:274
  64.1 2.6 %collective-permute-start.11 = (bf16[192,512]{1,0:T(8,128)(2,1)}, bf16[192,512]{1,0:T(8,128)(2,1)S(1)}, u32[]{:S(2)}, u32[]{:S(2)}) collective-permute-start(bf16[192,512]{1,0:T(8,128)(2,1)} %hidden.1.refs_1_), channel_id=1, source_target_pairs={{0,1},{1,0},{2,3},{3,2},{4,5},{5,4},{6,7},{7,6},{8,9},{9,8},{10,11... | collective-permute-start | bytes 589832 | tf_op jit(solution)/shard_map/ppermute | solution.py:274
  64.9 0.9 %copy-start.4 = (bf16[192,512]{1,0:T(8,128)(2,1)S(1)}, bf16[192,512]{1,0:T(8,128)(2,1)}, u32[]{:S(2)}) copy-start(bf16[192,512]{1,0:T(8,128)(2,1)} %hidden.1.refs_1_) | copy-start | bytes 589828
  65.8 17.5 %copy-start.14 = (f32[512]{0:T(512)S(1)}, f32[512]{0:T(512)}, u32[]{:S(2)}) copy-start(f32[512]{0:T(512)} %param.21) | copy-start | bytes 6148
  67.5 6.0 %collective-permute-start.12 = (bf16[128,512]{1,0:T(8,128)(2,1)S(1)}, bf16[128,512]{1,0:T(8,128)(2,1)S(1)}, u32[]{:S(2)}, u32[]{:S(2)}) collective-permute-start(bf16[128,512]{1,0:T(8,128)(2,1)S(1)} %get-tuple-element.41), channel_id=1, source_target_pairs={{0,2},{2,0},{4,6},{6,4},{8,10},{10,8},{12,14},{14,12},{1,3},{3,1},... | collective-permute-start | bytes 393224 | tf_op jit(solution)/shard_map/ppermute | solution.py:274
  69.0 6.3 %collective-permute-start.13 = (bf16[128,512]{1,0:T(8,128)(2,1)S(1)}, bf16[128,512]{1,0:T(8,128)(2,1)S(1)}, u32[]{:S(2)}, u32[]{:S(2)}) collective-permute-start(bf16[128,512]{1,0:T(8,128)(2,1)S(1)} %get-tuple-element.42), channel_id=1, source_target_pairs={{0,4},{2,6},{4,0},{6,2},{8,12},{10,14},{12,8},{14,10},{1,5},{3,7},... | collective-permute-start | bytes 393224 | tf_op jit(solution)/shard_map/ppermute | solution.py:274
  69.5 7.9 %collective-permute-start.14 = (bf16[128,512]{1,0:T(8,128)(2,1)S(1)}, bf16[128,512]{1,0:T(8,128)(2,1)S(1)}, u32[]{:S(2)}, u32[]{:S(2)}) collective-permute-start(bf16[128,512]{1,0:T(8,128)(2,1)S(1)} %get-tuple-element.43), channel_id=1, source_target_pairs={{0,6},{2,4},{4,2},{6,0},{8,14},{10,12},{12,10},{14,8},{1,7},{3,5},... | collective-permute-start | bytes 393224 | tf_op jit(solution)/shard_map/ppermute | solution.py:274
  77.5 5.8 %collective-permute-start.15 = (bf16[64,512]{1,0:T(8,128)(2,1)S(1)}, bf16[64,512]{1,0:T(8,128)(2,1)S(1)}, u32[]{:S(2)}, u32[]{:S(2)}) collective-permute-start(bf16[64,512]{1,0:T(8,128)(2,1)S(1)} %get-tuple-element.45), channel_id=1, source_target_pairs={{0,8},{2,10},{4,12},{6,14},{8,0},{10,2},{12,4},{14,6},{1,9},{3,11}... | collective-permute-start | bytes 196616 | tf_op jit(solution)/shard_map/ppermute | solution.py:274

commit v5 on v4

--- a/solution.py
+++ b/solution.py
@@ -90,28 +90,22 @@
         lax.fori_loop(0, piece // width, turn, 0)
 
 
-def mean_kernel(steps, fanout, pcap, fslice, nbr_hbm, table_ref, *refs):
-    out_refs, (total, nbr_ref, sems) = refs[: len(steps)], refs[len(steps) :]
+def mean_kernel(base, fanout, pcap, fslice, nbr_ref, table_ref, out_ref, total):
     feat_pos = lax.axis_index("feat")
-    copies = [
-        pltpu.make_async_copy(nbr_hbm.at[jnp.bitwise_xor(feat_pos, step)], nbr_ref.at[i], sems.at[i])
-        for i, step in enumerate(steps)
-    ]
-    for copy in copies:
-        copy.start()
-    for i, out_ref in enumerate(out_refs):
-        copies[i].wait()
-
-        def group(g, carry):
+
+    def partition(i, carry):
+        first = jnp.bitwise_xor(feat_pos, base + i) * (fanout * pcap)
+
+        def group(g, inner):
             at = pl.multiple_of(g * 8, 8)
             for u in range(8):
-                rows = [table_ref[nbr_ref[i, 0, at + (k * pcap + u)]] for k in range(fanout)]
+                rows = [table_ref[nbr_ref[first + k * pcap + at + u]] for k in range(fanout)]
                 while len(rows) > 1:
                     rows = [a + b for a, b in zip(rows[::2], rows[1::2])] + (
                         [rows[-1]] if len(rows) % 2 else []
                     )
                 total[pl.ds(at + u, 1), :] = rows[0]
-            return carry
+            return inner
 
         lax.fori_loop(0, pcap // 8, group, 0)
         mean = total[...] / fanout
@@ -122,11 +116,14 @@
             for b in range(3):
                 shift = (fslice - 32 * b) % LANES
                 moved = pltpu.roll(tail, shift, 1) if shift else tail
-                out_ref[pl.ds(b * part, part), :] = jnp.where(
+                out_ref[i, pl.ds(b * part, part), :] = jnp.where(
                     lane < fslice, mean[b * part : (b + 1) * part], moved
                 ).astype(jnp.bfloat16)
         else:
-            out_ref[...] = mean[:, :fslice].astype(jnp.bfloat16)
+            out_ref[i] = mean[:, :fslice].astype(jnp.bfloat16)
+        return carry
+
+    lax.fori_loop(0, out_ref.shape[0], partition, 0)
 
 
 def unfold(block, fslice, pcap):
@@ -231,7 +228,7 @@
 
 def layer_kernel(half, count_ref, *refs):
     mean_refs = refs[:half]
-    pre_ref, w_ref, cross_ref, hidden_ref = refs[half:]
+    pre_ref, w_ref, cross_ref, hidden_ref, result_ref = refs[half:]
     pcap, width = hidden_ref.shape
     fslice = w_ref.shape[1]
     pre = pre_ref[...] + cross_ref[:pcap, :].astype(jnp.float32)
@@ -240,7 +237,9 @@
             unfold(mean_refs[s][...], fslice, pcap), w_ref[s], preferred_element_type=jnp.float32
         )
     live = lax.broadcasted_iota(jnp.int32, (pcap, width), 0) < count_ref[0, 0]
-    hidden_ref[...] = jnp.where(live, jnp.maximum(pre, 0.0), 0.0).astype(jnp.bfloat16)
+    hidden = jnp.where(live, jnp.maximum(pre, 0.0), 0.0).astype(jnp.bfloat16)
+    hidden_ref[...] = hidden
+    result_ref[...] = hidden
 
 
 def share_kernel(
@@ -301,7 +300,7 @@
     anywhere = pl.BlockSpec(memory_space=pl.ANY)
     table_bytes = nodes * LANES * 4
 
-    def call(kernel, name, shapes, ins, args, after=(), scratch=(), limit=16 * MIB, cost_us=1):
+    def call(kernel, name, shapes, ins, args, after=(), scratch=(), limit=16 * MIB):
         def wrapped(*refs):
             kernel(*refs[: len(args)], *refs[len(args) + len(after) :])
 
@@ -312,11 +311,11 @@
             out_specs=(vmem,) * len(shapes),
             scratch_shapes=scratch,
             compiler_params=pltpu.CompilerParams(vmem_limit_bytes=limit),
-            cost_estimate=pl.CostEstimate(
-                flops=int(cost_us * 1_100_000_000), bytes_accessed=0, transcendentals=0
-            ),
             name=name,
         )(*args, *after)
+
+    def pinned(value):
+        return pltpu.with_memory_space_constraint(value, pltpu.HBM)
 
     def send(chunks):
         return [chunk if s == 0 else swap(chunk, "feat", s) for s, chunk in enumerate(chunks)]
@@ -326,7 +325,7 @@
         "pack",
         [((2 * fslice, width), bf16)] * half,
         [hbm] * 5,
-        (src_feats, seed_rows[None], nbr_two.T, w1_self, w1_nbr),
+        [pinned(x) for x in (src_feats, seed_rows[None], nbr_two.T, w1_self, w1_nbr)],
         scratch=[
             pltpu.VMEM((fslice, n_feat * 2 * pcap), bf16),
             pltpu.VMEM((1, seed_count), jnp.int32),
@@ -335,7 +334,6 @@
             pltpu.VMEM((fslice, width), bf16),
             pltpu.SemaphoreType.DMA((5,)),
         ],
-        cost_us=2,
     )
     arrived = send(parcels)
     (table,) = call(
@@ -343,34 +341,29 @@
         "turn",
         [((nodes, LANES), jnp.float32)],
         [hbm],
-        (src_feats,),
+        (pinned(src_feats),),
         after=(parcels[0],),
         scratch=[pltpu.VMEM((fslice, nodes), bf16), pltpu.SemaphoreType.DMA((6,))],
         limit=table_bytes + 12 * MIB,
-        cost_us=3,
     )
     table = table.reshape(nodes, 1, LANES)
-    neighbors = nbr_one.reshape(n_feat, 1, fanout_one * pcap)
+    neighbors = nbr_one.reshape(-1)
     chunk_shape = (pcap // 4 * 3, LANES) if folds(fslice, pcap) else (pcap, fslice)
 
-    def means(steps, after):
-        return call(
-            functools.partial(mean_kernel, steps, fanout_one, pcap, fslice),
+    def means(base, count, after):
+        (chunks,) = call(
+            functools.partial(mean_kernel, base, fanout_one, pcap, fslice),
             "mean",
-            [(chunk_shape, bf16)] * len(steps),
-            [anywhere, vmem],
+            [((count, *chunk_shape), bf16)],
+            [smem, vmem],
             (neighbors, table),
             after=after,
-            scratch=[
-                pltpu.VMEM((pcap, LANES), jnp.float32),
-                pltpu.SMEM((len(steps), 1, fanout_one * pcap), jnp.int32),
-                pltpu.SemaphoreType.DMA((len(steps),)),
-            ],
+            scratch=[pltpu.VMEM((pcap, LANES), jnp.float32)],
             limit=table_bytes + 8 * MIB,
-            cost_us=2.3 * len(steps),
-        )
-
-    far_means = means([s + half for s in range(half)], ())
+        )
+        return [chunks[i] for i in range(count)]
+
+    far_means = means(half, half, ())
     far_arrived = send(far_means)
     (halves,) = call(
         halves_kernel,
@@ -381,7 +374,7 @@
         after=far_means[:1],
     )
     other_halves = swap(halves, "rep", 1)
-    (last_mean,) = means([half - 1], far_means[:1])
+    (last_mean,) = means(half - 1, 1, far_means[:1])
     w_nbr, pre, cross = call(
         functools.partial(prepare_kernel, half, n_idx),
         "prepare",
@@ -393,10 +386,9 @@
         [vmem] * (2 * half + 2),
         (*arrived, *far_arrived, other_halves, bias_one[None]),
         after=(last_mean,),
-        cost_us=2,
     )
     cross_arrived = swap(cross, "feat", half)
-    near_means = means(list(range(half - 1)), (cross,))
+    near_means = means(0, half - 1, (cross,))
     near_arrived = send([*near_means, last_mean])
     (near_times,) = call(
         functools.partial(near_times_kernel, half, fslice, pcap, n_idx),
@@ -406,10 +398,10 @@
         arrived,
         after=near_means[:1],
     )
-    (hidden,) = call(
+    hidden, result = call(
         functools.partial(layer_kernel, half),
         "hidden",
-        [((pcap, width), bf16)],
+        [((pcap, width), bf16)] * 2,
         [smem] + [vmem] * (half + 3),
         (counts, *near_arrived, pre, w_nbr, cross_arrived),
     )
@@ -439,7 +431,7 @@
     )
     pre_two = near_sum + swap(far_sum, "feat", half).astype(jnp.float32) + bias_two
     seed_out = jnp.maximum(pre_two, 0.0).astype(bf16)
-    return (hidden[None, None], seed_out)
+    return (result[None, None], seed_out)
 
 
 def solution(mesh):

time: 84.3 us -> 76.6 us (0.909)
  Pallas kernels: 36.7 us -> 30.3 us
  local copies, waits for them, and re-layouts: 11.3 us -> 5.55 us
  waiting for transfers between devices: 14.7 us -> 18.2 us
  starting transfers between devices: 18.9 us -> 20 us
    pallas_call x12, Pallas kernels: 36.7 us -> 30.3 us  [call(): pl.pallas_call(wrapped, out_shape=tuple((jax.ShapeDtypeStruct(shape, dtyp...]
    unnamed x30 -> x16, local copies, waits for them, and re-layouts: 11.2 us -> 5.44 us
    ppermute x16, waiting for transfers between devices: 14.7 us -> 18.2 us  [swap(): return lax.ppermute(value, axis, [(i, i ^ step) for i in range(size)])]
    ppermute x16, starting transfers between devices: 18.9 us -> 20 us  [swap(): return lax.ppermute(value, axis, [(i, i ^ step) for i in range(size)])]
  transfers between devices with their start and end apart: 16 -> 16, of which waited for: 6 -> 7; matrix products, arithmetic and copies ran while one was open for 0% -> 0% of each run, Pallas kernels for 41% -> 35%
where the time goes in v5:
time: 76.6 us; the launch traced here: 76.4 us
  Pallas kernels  30.3 us (40%)
  starting transfers between devices  20 us (26%)
  waiting for transfers between devices  18.2 us (24%)
  local copies, waits for them, and re-layouts  5.55 us (7%)
  between operations  1.52 us (2%)
  other arithmetic  0.85 us (1%)
    pallas_call x12, Pallas kernels, call(): pl.pallas_call(wrapped, out_shape=tuple((jax.ShapeDtypeStruct(shape, dtyp...  30.3 us
    ppermute x16, starting transfers between devices, swap(): return lax.ppermute(value, axis, [(i, i ^ step) for i in range(size)])  20 us
    ppermute x16, waiting for transfers between devices, swap(): return lax.ppermute(value, axis, [(i, i ^ step) for i in range(size)])  18.2 us
    unnamed x16, local copies, waits for them, and re-layouts  5.44 us
  transfers between devices with their start and end apart: 16, of which 7 were waited for; matrix products, arithmetic and copies ran while one was open for 0% of the time, Pallas kernels for 35%

profile of v5, /device:TPU:0, one launch (start us, length us, event | category | flops | bytes accessed | tf_op | source)
XLA Modules:
  0.0 76.4 jit_solution(4285294962855626705)
XLA Ops:
  0.6 0.0 copy-start.6
  0.6 1.6 %pack.1 = (bf16[192,512]{1,0:T(8,128)(2,1)S(1)}, bf16[192,512]{1,0:T(8,128)(2,1)S(1)}, bf16[192,512]{1,0:T(8,128)(2,1)S(1)}, bf16[192,512]{1,0:T(8,128)(2,1)S(1)}) custom-call(bf16[96,12288]{1,0:T(8,128)(2,1)} %refs_0_.4, s32[1,64]{1,0:T(1,128)} %bitcast.27, s32[15,64]{1,0:T(8,128)} %bitcast.26, bf16[96,512]{1,0:T(8,128)(2,1)} %refs_3_.2, ...), custom_call_target="tpu_custom_call" | custom-call | tf_op jit(solution)/shard_map/pack/pallas_call | solution.py:307
  2.3 3.0 %collective-permute-start = (bf16[192,512]{1,0:T(8,128)(2,1)S(1)}, bf16[192,512]{1,0:T(8,128)(2,1)S(1)}, u32[]{:S(2)}, u32[]{:S(2)}) collective-permute-start(bf16[192,512]{1,0:T(8,128)(2,1)S(1)} %get-tuple-element.20), channel_id=1, source_target_pairs={{0,2},{2,0},{4,6},{6,4},{8,10},{10,8},{12,14},{14,12},{1,3},{3,1},... | collective-permute-start | bytes 589832 | tf_op jit(solution)/shard_map/ppermute | solution.py:273
  5.3 1.6 %collective-permute-start.1 = (bf16[192,512]{1,0:T(8,128)(2,1)S(1)}, bf16[192,512]{1,0:T(8,128)(2,1)S(1)}, u32[]{:S(2)}, u32[]{:S(2)}) collective-permute-start(bf16[192,512]{1,0:T(8,128)(2,1)S(1)} %get-tuple-element.21), channel_id=1, source_target_pairs={{0,4},{2,6},{4,0},{6,2},{8,12},{10,14},{12,8},{14,10},{1,5},{3,7},... | collective-permute-start | bytes 589832 | tf_op jit(solution)/shard_map/ppermute | solution.py:273
  6.9 0.0 collective-permute-start.2
  6.9 3.5 %turn.1 = f32[12288,128]{1,0:T(8,128)S(1)} custom-call(bf16[96,12288]{1,0:T(8,128)(2,1)} %refs_0_.4, bf16[192,512]{1,0:T(8,128)(2,1)S(1)} %get-tuple-element.19.refs_1_.refs_0_), custom_call_target="tpu_custom_call" | custom-call | tf_op jit(solution)/shard_map/turn/pallas_call | solution.py:307
  10.4 0.0 copy-start
  10.4 2.6 %copy-done = f32[12288,128]{1,0:T(8,128)} copy-done((f32[12288,128]{1,0:T(8,128)}, f32[12288,128]{1,0:T(8,128)S(1)}, u32[]{:S(2)}) %copy-start) | copy-done | bytes 6291480
  13.1 0.0 copy-done.6
  13.1 0.2 reduce
  13.3 0.1 reshape.11.refs_0_
  13.4 0.0 copy-start.1
  13.4 2.8 %copy-done.1 = f32[12288,128]{1,0:T(8,128)S(1)} copy-done((f32[12288,128]{1,0:T(8,128)S(1)}, f32[12288,128]{1,0:T(8,128)}, u32[]{:S(2)}) %copy-start.1) | copy-done | bytes 6291480
  16.1 0.0 copy-start.2
  16.2 0.0 copy-start.5
  16.2 9.6 %mean.3 = bf16[4,144,128]{2,1,0:T(8,128)(2,1)S(1)} custom-call(s32[15360]{0:T(1024)S(1)} %reshape.11.refs_0_, f32[12288,1,128]{2,1,0:T(1,128)S(1)} %bitcast.20), custom_call_target="tpu_custom_call" | custom-call | tf_op jit(solution)/shard_map/mean/pallas_call | solution.py:307
  25.8 0.0 collective-permute-done.refs_1_
  25.8 0.0 collective-permute-done.1.refs_2_
  25.8 0.0 collective-permute-done.2.refs_3_
  25.9 0.1 collective-permute-start.6
  26.0 2.0 %collective-permute-start.3 = (bf16[144,128]{1,0:T(8,128)(2,1)S(1)}, bf16[144,128]{1,0:T(8,128)(2,1)S(1)}, u32[]{:S(2)}, u32[]{:S(2)}) collective-permute-start(bf16[144,128]{1,0:T(8,128)(2,1)S(1)} %get-tuple-element.38), channel_id=1, source_target_pairs={{0,2},{2,0},{4,6},{6,4},{8,10},{10,8},{12,14},{14,12},{1,3},{3,1},... | collective-permute-start | bytes 110600 | tf_op jit(solution)/shard_map/ppermute | solution.py:273
  27.9 1.6 %collective-permute-start.4 = (bf16[144,128]{1,0:T(8,128)(2,1)S(1)}, bf16[144,128]{1,0:T(8,128)(2,1)S(1)}, u32[]{:S(2)}, u32[]{:S(2)}) collective-permute-start(bf16[144,128]{1,0:T(8,128)(2,1)S(1)} %get-tuple-element.37), channel_id=1, source_target_pairs={{0,4},{2,6},{4,0},{6,2},{8,12},{10,14},{12,8},{14,10},{1,5},{3,7},... | collective-permute-start | bytes 110600 | tf_op jit(solution)/shard_map/ppermute | solution.py:273
  29.5 0.0 collective-permute-start.5
  29.5 0.0 copy-done.2
  29.5 3.6 %mean.4 = bf16[1,144,128]{2,1,0:T(8,128)(2,1)S(1)} custom-call(s32[15360]{0:T(1024)S(1)} %reshape.11.refs_0_, f32[12288,1,128]{2,1,0:T(1,128)S(1)} %bitcast.21, bf16[144,128]{1,0:T(8,128)(2,1)S(1)} %get-tuple-element.39.refs_4_.refs_2_), custom_call_target="tpu_custom_call" | custom-call | tf_op jit(solution)/shard_map/mean/pallas_call | solution.py:307
  33.1 0.0 copy-start.3
  33.1 0.0 copy-start.4
  33.1 3.0 %collective-permute-start.9 = (bf16[144,128]{1,0:T(8,128)(2,1)S(1)}, bf16[144,128]{1,0:T(8,128)(2,1)S(1)}, u32[]{:S(2)}, u32[]{:S(2)}) collective-permute-start(bf16[144,128]{1,0:T(8,128)(2,1)S(1)} %bitcast.23), channel_id=1, source_target_pairs={{0,6},{2,4},{4,2},{6,0},{8,14},{10,12},{12,10},{14,8},{1,7},{3,5},... | collective-permute-start | bytes 110600 | tf_op jit(solution)/shard_map/ppermute | solution.py:273
  36.1 0.0 collective-permute-done.3.refs_5_
  36.1 0.0 collective-permute-done.4.refs_6_
  36.1 0.0 collective-permute-done.5.refs_7_
  36.1 0.0 collective-permute-done.6.refs_8_
  36.1 0.0 copy-done.5
  36.1 0.8 %prepare.1 = (bf16[4,96,512]{2,1,0:T(8,128)(2,1)S(1)}, f32[192,512]{1,0:T(8,128)S(1)}, bf16[208,512]{1,0:T(8,128)(2,1)S(1)}) custom-call(bf16[192,512]{1,0:T(8,128)(2,1)S(1)} %get-tuple-element.19.refs_1_.refs_0_, bf16[192,512]{1,0:T(8,128)(2,1)S(1)} %collective-permute-done.refs_1_, bf16[192,512]{1,0:T(8,128)(2,1)S(1)} %collective-permute-done.1.refs_2_, ...), custom_call_target="tpu_custom_call" | custom-call | tf_op jit(solution)/shard_map/prepare/pallas_call | solution.py:307
  37.0 0.0 copy-start.7
  37.0 7.6 %mean.5 = bf16[3,144,128]{2,1,0:T(8,128)(2,1)S(1)} custom-call(s32[15360]{0:T(1024)S(1)} %reshape.11.refs_0_, f32[12288,1,128]{2,1,0:T(1,128)S(1)} %bitcast.22, bf16[208,512]{1,0:T(8,128)(2,1)S(1)} %get-tuple-element.23.refs_2_), custom_call_target="tpu_custom_call" | custom-call | tf_op jit(solution)/shard_map/mean/pallas_call | solution.py:307
  44.6 2.7 %collective-permute-start.10 = (bf16[208,512]{1,0:T(8,128)(2,1)S(1)}, bf16[208,512]{1,0:T(8,128)(2,1)S(1)}, u32[]{:S(2)}, u32[]{:S(2)}) collective-permute-start(bf16[208,512]{1,0:T(8,128)(2,1)S(1)} %get-tuple-element.23.refs_2_), channel_id=1, source_target_pairs={{0,8},{2,10},{4,12},{6,14},{8,0},{10,2},{12,4},{14,6},{1,9},{3,11}... | collective-permute-start | bytes 638984 | tf_op jit(solution)/shard_map/ppermute | solution.py:273
  47.3 0.6 collective-permute-start.7
  47.8 0.4 collective-permute-start.8
  48.9 0.0 collective-permute-done.9.refs_4_
  48.9 2.3 %collective-permute-done.7.refs_2_ = bf16[144,128]{1,0:T(8,128)(2,1)S(1)} collective-permute-done((bf16[144,128]{1,0:T(8,128)(2,1)S(1)}, bf16[144,128]{1,0:T(8,128)(2,1)S(1)}, u32[]{:S(2)}, u32[]{:S(2)}) %collective-permute-start.7) | collective-permute-done | bytes 36896 | tf_op jit(solution)/shard_map/ppermute | solution.py:273
  51.3 0.8 %collective-permute-done.8.refs_3_ = bf16[144,128]{1,0:T(8,128)(2,1)S(1)} collective-permute-done((bf16[144,128]{1,0:T(8,128)(2,1)S(1)}, bf16[144,128]{1,0:T(8,128)(2,1)S(1)}, u32[]{:S(2)}, u32[]{:S(2)}) %collective-permute-start.8) | collective-permute-done | bytes 36896 | tf_op jit(solution)/shard_map/ppermute | solution.py:273
  52.1 4.4 %collective-permute-done.10.refs_7_.refs_0_ = bf16[208,512]{1,0:T(8,128)(2,1)S(1)} collective-permute-done((bf16[208,512]{1,0:T(8,128)(2,1)S(1)}, bf16[208,512]{1,0:T(8,128)(2,1)S(1)}, u32[]{:S(2)}, u32[]{:S(2)}) %collective-permute-start.10) | collective-permute-done | bytes 213024 | tf_op jit(solution)/shard_map/ppermute | solution.py:273
  56.5 1.1 %hidden.1 = (bf16[192,512]{1,0:T(8,128)(2,1)S(1)}, bf16[192,512]{1,0:T(8,128)(2,1)}) custom-call(s32[1,1]{1,0:T(1,128)S(6)} %copy.13.refs_0_, bf16[144,128]{1,0:T(8,128)(2,1)S(1)} %get-tuple-element.42.refs_1_.refs_4_, bf16[144,128]{1,0:T(8,128)(2,1)S(1)} %collective-permute-done.7.refs_2_, bf16[144,128]{1,0:T(8,128)(2,1)S(1)} %collective-permute-done.8.refs_3_, ...), custom_call_target="tpu_custom_call" | custom-call | tf_op jit(solution)/shard_map/hidden/pallas_call | solution.py:307
  57.5 0.0 collective-permute-start.11
  57.6 0.8 %near_times.1.refs_0_ = bf16[256,768]{1,0:T(8,128)(2,1)S(1)} custom-call(bf16[192,512]{1,0:T(8,128)(2,1)S(1)} %get-tuple-element.19.refs_1_.refs_0_, bf16[192,512]{1,0:T(8,128)(2,1)S(1)} %collective-permute-done.refs_1_, bf16[192,512]{1,0:T(8,128)(2,1)S(1)} %collective-permute-done.1.refs_2_, bf16[192,512]{1,0:T(8,128)(2,1)S(1)} %collective-permute-done.2.refs_3_, ...), custom_call_target="tpu_custom_call" | custom-call | tf_op jit(solution)/shard_map/near_times/pallas_call | solution.py:307
  58.3 0.0 copy-done.3
  58.3 0.0 copy-done.4
  58.4 0.8 %far_times.1 = (bf16[256,768]{1,0:T(8,128)(2,1)S(1)}, bf16[2,192,512]{2,1,0:T(8,128)(2,1)S(1)}) custom-call(bf16[208,512]{1,0:T(8,128)(2,1)S(1)} %collective-permute-done.10.refs_7_.refs_0_, bf16[192,512]{1,0:T(8,128)(2,1)S(1)} %get-tuple-element.27.refs_1_, bf16[512,512]{1,0:T(8,128)(2,1)S(1)} %copy-done.3, bf16[512,512]{1,0:T(8,128)(2,1)S(1)} %copy-done.4), custom_call_target="tpu_custom_call" | custom-call | tf_op jit(solution)/shard_map/far_times/pallas_call | solution.py:307
  59.2 0.0 collective-permute-done.11.refs_3_
  59.2 0.8 %share.1 = (bf16[128,512]{1,0:T(8,128)(2,1)S(1)}, bf16[128,512]{1,0:T(8,128)(2,1)S(1)}, bf16[128,512]{1,0:T(8,128)(2,1)S(1)}, bf16[128,512]{1,0:T(8,128)(2,1)S(1)}) custom-call(bf16[256,768]{1,0:T(8,128)(2,1)S(1)} %near_times.1.refs_0_, bf16[256,768]{1,0:T(8,128)(2,1)S(1)} %get-tuple-element.28.refs_1_, bf16[2,192,512]{2,1,0:T(8,128)(2,1)S(1)} %get-tuple-element.29.refs_2_, ...), custom_call_target="tpu_custom_call" | custom-call | tf_op jit(solution)/shard_map/share/pallas_call | solution.py:307
  60.0 0.9 %collective-permute-start.12 = (bf16[128,512]{1,0:T(8,128)(2,1)S(1)}, bf16[128,512]{1,0:T(8,128)(2,1)S(1)}, u32[]{:S(2)}, u32[]{:S(2)}) collective-permute-start(bf16[128,512]{1,0:T(8,128)(2,1)S(1)} %get-tuple-element.31), channel_id=1, source_target_pairs={{0,2},{2,0},{4,6},{6,4},{8,10},{10,8},{12,14},{14,12},{1,3},{3,1},... | collective-permute-start | bytes 393224 | tf_op jit(solution)/shard_map/ppermute | solution.py:273
  60.9 0.0 collective-permute-start.13
  60.9 2.6 %collective-permute-start.14 = (bf16[128,512]{1,0:T(8,128)(2,1)S(1)}, bf16[128,512]{1,0:T(8,128)(2,1)S(1)}, u32[]{:S(2)}, u32[]{:S(2)}) collective-permute-start(bf16[128,512]{1,0:T(8,128)(2,1)S(1)} %get-tuple-element.33), channel_id=1, source_target_pairs={{0,6},{2,4},{4,2},{6,0},{8,14},{10,12},{12,10},{14,8},{1,7},{3,5},... | collective-permute-start | bytes 393224 | tf_op jit(solution)/shard_map/ppermute | solution.py:273
  63.6 2.4 %collective-permute-done.12.refs_1_ = bf16[128,512]{1,0:T(8,128)(2,1)S(1)} collective-permute-done((bf16[128,512]{1,0:T(8,128)(2,1)S(1)}, bf16[128,512]{1,0:T(8,128)(2,1)S(1)}, u32[]{:S(2)}, u32[]{:S(2)}) %collective-permute-start.12) | collective-permute-done | bytes 131104 | tf_op jit(solution)/shard_map/ppermute | solution.py:273
  66.0 1.3 %collective-permute-done.13.refs_2_ = bf16[128,512]{1,0:T(8,128)(2,1)S(1)} collective-permute-done((bf16[128,512]{1,0:T(8,128)(2,1)S(1)}, bf16[128,512]{1,0:T(8,128)(2,1)S(1)}, u32[]{:S(2)}, u32[]{:S(2)}) %collective-permute-start.13) | collective-permute-done | bytes 131104 | tf_op jit(solution)/shard_map/ppermute | solution.py:273
  67.2 2.7 %collective-permute-done.14.refs_3_ = bf16[128,512]{1,0:T(8,128)(2,1)S(1)} collective-permute-done((bf16[128,512]{1,0:T(8,128)(2,1)S(1)}, bf16[128,512]{1,0:T(8,128)(2,1)S(1)}, u32[]{:S(2)}, u32[]{:S(2)}) %collective-permute-start.14) | collective-permute-done | bytes 131104 | tf_op jit(solution)/shard_map/ppermute | solution.py:273
  70.0 0.1 side_sum.1
  70.0 1.5 %collective-permute-start.15 = (bf16[64,512]{1,0:T(8,128)(2,1)S(1)}, bf16[64,512]{1,0:T(8,128)(2,1)S(1)}, u32[]{:S(2)}, u32[]{:S(2)}) collective-permute-start(bf16[64,512]{1,0:T(8,128)(2,1)S(1)} %get-tuple-element.35), channel_id=1, source_target_pairs={{0,8},{2,10},{4,12},{6,14},{8,0},{10,2},{12,4},{14,6},{1,9},{3,11}... | collective-permute-start | bytes 196616 | tf_op jit(solution)/shard_map/ppermute | solution.py:273
  71.5 4.3 %collective-permute-done.15 = bf16[64,512]{1,0:T(8,128)(2,1)S(1)} collective-permute-done((bf16[64,512]{1,0:T(8,128)(2,1)S(1)}, bf16[64,512]{1,0:T(8,128)(2,1)S(1)}, u32[]{:S(2)}, u32[]{:S(2)}) %collective-permute-start.15) | collective-permute-done | bytes 65568 | tf_op jit(solution)/shard_map/ppermute | solution.py:273
  75.8 0.0 copy-done.7
  75.8 0.7 maximum_convert_fusion
  (3 shorter events, 0.0 us)
Async XLA Ops:
  0.6 12.4 %copy-start.6 = (s32[8,1,10,192]{3,1,2,0:T(1,128)S(1)}, s32[8,1,10,192]{3,1,2,0:T(1,128)}, u32[]{:S(2)}) copy-start(s32[8,1,10,192]{3,1,2,0:T(1,128)} %param.12) | copy-start | bytes 184324
  2.3 23.6 %collective-permute-start = (bf16[192,512]{1,0:T(8,128)(2,1)S(1)}, bf16[192,512]{1,0:T(8,128)(2,1)S(1)}, u32[]{:S(2)}, u32[]{:S(2)}) collective-permute-start(bf16[192,512]{1,0:T(8,128)(2,1)S(1)} %get-tuple-element.20), channel_id=1, source_target_pairs={{0,2},{2,0},{4,6},{6,4},{8,10},{10,8},{12,14},{14,12},{1,3},{3,1},... | collective-permute-start | bytes 589832 | tf_op jit(solution)/shard_map/ppermute | solution.py:273
  5.3 20.5 %collective-permute-start.1 = (bf16[192,512]{1,0:T(8,128)(2,1)S(1)}, bf16[192,512]{1,0:T(8,128)(2,1)S(1)}, u32[]{:S(2)}, u32[]{:S(2)}) collective-permute-start(bf16[192,512]{1,0:T(8,128)(2,1)S(1)} %get-tuple-element.21), channel_id=1, source_target_pairs={{0,4},{2,6},{4,0},{6,2},{8,12},{10,14},{12,8},{14,10},{1,5},{3,7},... | collective-permute-start | bytes 589832 | tf_op jit(solution)/shard_map/ppermute | solution.py:273
  6.9 19.0 %collective-permute-start.2 = (bf16[192,512]{1,0:T(8,128)(2,1)S(1)}, bf16[192,512]{1,0:T(8,128)(2,1)S(1)}, u32[]{:S(2)}, u32[]{:S(2)}) collective-permute-start(bf16[192,512]{1,0:T(8,128)(2,1)S(1)} %get-tuple-element.22), channel_id=1, source_target_pairs={{0,6},{2,4},{4,2},{6,0},{8,14},{10,12},{12,10},{14,8},{1,7},{3,5},... | collective-permute-start | bytes 589832 | tf_op jit(solution)/shard_map/ppermute | solution.py:273
  10.4 2.6 %copy-start = (f32[12288,128]{1,0:T(8,128)}, f32[12288,128]{1,0:T(8,128)S(1)}, u32[]{:S(2)}) copy-start(f32[12288,128]{1,0:T(8,128)S(1)} %turn.1) | copy-start | bytes 18874372
  13.4 2.8 %copy-start.1 = (f32[12288,128]{1,0:T(8,128)S(1)}, f32[12288,128]{1,0:T(8,128)}, u32[]{:S(2)}) copy-start(f32[12288,128]{1,0:T(8,128)} %copy-done) | copy-start | bytes 18874372
  16.1 13.4 %copy-start.2 = (f32[12288,128]{1,0:T(8,128)S(1)}, f32[12288,128]{1,0:T(8,128)}, u32[]{:S(2)}) copy-start(f32[12288,128]{1,0:T(8,128)} %copy-done) | copy-start | bytes 18874372
  16.2 20.0 %copy-start.5 = (f32[512]{0:T(512)S(1)}, f32[512]{0:T(512)}, u32[]{:S(2)}) copy-start(f32[512]{0:T(512)} %param.18) | copy-start | bytes 6148
  25.9 10.2 %collective-permute-start.6 = (bf16[4,96,512]{2,1,0:T(8,128)(2,1)S(1)}, bf16[4,96,512]{2,1,0:T(8,128)(2,1)S(1)}, u32[]{:S(2)}, u32[]{:S(2)}) collective-permute-start(bf16[4,96,512]{2,1,0:T(8,128)(2,1)S(1)} %halves.1), channel_id=1, source_target_pairs={{0,1},{1,0},{2,3},{3,2},{4,5},{5,4},{6,7},{7,6},{8,9},{9,8},{10,11... | collective-permute-start | bytes 1179656 | tf_op jit(solution)/shard_map/ppermute | solution.py:273
  26.0 10.1 %collective-permute-start.3 = (bf16[144,128]{1,0:T(8,128)(2,1)S(1)}, bf16[144,128]{1,0:T(8,128)(2,1)S(1)}, u32[]{:S(2)}, u32[]{:S(2)}) collective-permute-start(bf16[144,128]{1,0:T(8,128)(2,1)S(1)} %get-tuple-element.38), channel_id=1, source_target_pairs={{0,2},{2,0},{4,6},{6,4},{8,10},{10,8},{12,14},{14,12},{1,3},{3,1},... | collective-permute-start | bytes 110600 | tf_op jit(solution)/shard_map/ppermute | solution.py:273
  27.9 8.2 %collective-permute-start.4 = (bf16[144,128]{1,0:T(8,128)(2,1)S(1)}, bf16[144,128]{1,0:T(8,128)(2,1)S(1)}, u32[]{:S(2)}, u32[]{:S(2)}) collective-permute-start(bf16[144,128]{1,0:T(8,128)(2,1)S(1)} %get-tuple-element.37), channel_id=1, source_target_pairs={{0,4},{2,6},{4,0},{6,2},{8,12},{10,14},{12,8},{14,10},{1,5},{3,7},... | collective-permute-start | bytes 110600 | tf_op jit(solution)/shard_map/ppermute | solution.py:273
  29.5 6.6 %collective-permute-start.5 = (bf16[144,128]{1,0:T(8,128)(2,1)S(1)}, bf16[144,128]{1,0:T(8,128)(2,1)S(1)}, u32[]{:S(2)}, u32[]{:S(2)}) collective-permute-start(bf16[144,128]{1,0:T(8,128)(2,1)S(1)} %get-tuple-element.36), channel_id=1, source_target_pairs={{0,6},{2,4},{4,2},{6,0},{8,14},{10,12},{12,10},{14,8},{1,7},{3,5},... | collective-permute-start | bytes 110600 | tf_op jit(solution)/shard_map/ppermute | solution.py:273
  33.1 25.3 %copy-start.3 = (bf16[512,512]{1,0:T(8,128)(2,1)S(1)}, bf16[512,512]{1,0:T(8,128)(2,1)}, u32[]{:S(2)}) copy-start(bf16[512,512]{1,0:T(8,128)(2,1)} %refs_4_.3) | copy-start | bytes 1572868
  33.1 25.3 %copy-start.4 = (bf16[512,512]{1,0:T(8,128)(2,1)S(1)}, bf16[512,512]{1,0:T(8,128)(2,1)}, u32[]{:S(2)}) copy-start(bf16[512,512]{1,0:T(8,128)(2,1)} %refs_5_.1) | copy-start | bytes 1572868
  33.1 15.8 %collective-permute-start.9 = (bf16[144,128]{1,0:T(8,128)(2,1)S(1)}, bf16[144,128]{1,0:T(8,128)(2,1)S(1)}, u32[]{:S(2)}, u32[]{:S(2)}) collective-permute-start(bf16[144,128]{1,0:T(8,128)(2,1)S(1)} %bitcast.23), channel_id=1, source_target_pairs={{0,6},{2,4},{4,2},{6,0},{8,14},{10,12},{12,10},{14,8},{1,7},{3,5},... | collective-permute-start | bytes 110600 | tf_op jit(solution)/shard_map/ppermute | solution.py:273
  37.0 38.8 %copy-start.7 = (f32[512]{0:T(512)S(1)}, f32[512]{0:T(512)}, u32[]{:S(2)}) copy-start(f32[512]{0:T(512)} %param.21) | copy-start | bytes 6148
  44.6 11.9 %collective-permute-start.10 = (bf16[208,512]{1,0:T(8,128)(2,1)S(1)}, bf16[208,512]{1,0:T(8,128)(2,1)S(1)}, u32[]{:S(2)}, u32[]{:S(2)}) collective-permute-start(bf16[208,512]{1,0:T(8,128)(2,1)S(1)} %get-tuple-element.23.refs_2_), channel_id=1, source_target_pairs={{0,8},{2,10},{4,12},{6,14},{8,0},{10,2},{12,4},{14,6},{1,9},{3,11}... | collective-permute-start | bytes 638984 | tf_op jit(solution)/shard_map/ppermute | solution.py:273
  47.3 4.0 %collective-permute-start.7 = (bf16[144,128]{1,0:T(8,128)(2,1)S(1)}, bf16[144,128]{1,0:T(8,128)(2,1)S(1)}, u32[]{:S(2)}, u32[]{:S(2)}) collective-permute-start(bf16[144,128]{1,0:T(8,128)(2,1)S(1)} %get-tuple-element.41), channel_id=1, source_target_pairs={{0,2},{2,0},{4,6},{6,4},{8,10},{10,8},{12,14},{14,12},{1,3},{3,1},... | collective-permute-start | bytes 110600 | tf_op jit(solution)/shard_map/ppermute | solution.py:273
  47.8 4.3 %collective-permute-start.8 = (bf16[144,128]{1,0:T(8,128)(2,1)S(1)}, bf16[144,128]{1,0:T(8,128)(2,1)S(1)}, u32[]{:S(2)}, u32[]{:S(2)}) collective-permute-start(bf16[144,128]{1,0:T(8,128)(2,1)S(1)} %get-tuple-element.40), channel_id=1, source_target_pairs={{0,4},{2,6},{4,0},{6,2},{8,12},{10,14},{12,8},{14,10},{1,5},{3,7},... | collective-permute-start | bytes 110600 | tf_op jit(solution)/shard_map/ppermute | solution.py:273
  57.5 1.7 %collective-permute-start.11 = (bf16[192,512]{1,0:T(8,128)(2,1)S(1)}, bf16[192,512]{1,0:T(8,128)(2,1)S(1)}, u32[]{:S(2)}, u32[]{:S(2)}) collective-permute-start(bf16[192,512]{1,0:T(8,128)(2,1)S(1)} %get-tuple-element.27.refs_1_), channel_id=1, source_target_pairs={{0,1},{1,0},{2,3},{3,2},{4,5},{5,4},{6,7},{7,6},{8,9},{9,8},{10,11... | collective-permute-start | bytes 589832 | tf_op jit(solution)/shard_map/ppermute | solution.py:273
  60.0 6.0 %collective-permute-start.12 = (bf16[128,512]{1,0:T(8,128)(2,1)S(1)}, bf16[128,512]{1,0:T(8,128)(2,1)S(1)}, u32[]{:S(2)}, u32[]{:S(2)}) collective-permute-start(bf16[128,512]{1,0:T(8,128)(2,1)S(1)} %get-tuple-element.31), channel_id=1, source_target_pairs={{0,2},{2,0},{4,6},{6,4},{8,10},{10,8},{12,14},{14,12},{1,3},{3,1},... | collective-permute-start | bytes 393224 | tf_op jit(solution)/shard_map/ppermute | solution.py:273
  60.9 6.3 %collective-permute-start.13 = (bf16[128,512]{1,0:T(8,128)(2,1)S(1)}, bf16[128,512]{1,0:T(8,128)(2,1)S(1)}, u32[]{:S(2)}, u32[]{:S(2)}) collective-permute-start(bf16[128,512]{1,0:T(8,128)(2,1)S(1)} %get-tuple-element.32), channel_id=1, source_target_pairs={{0,4},{2,6},{4,0},{6,2},{8,12},{10,14},{12,8},{14,10},{1,5},{3,7},... | collective-permute-start | bytes 393224 | tf_op jit(solution)/shard_map/ppermute | solution.py:273
  60.9 9.0 %collective-permute-start.14 = (bf16[128,512]{1,0:T(8,128)(2,1)S(1)}, bf16[128,512]{1,0:T(8,128)(2,1)S(1)}, u32[]{:S(2)}, u32[]{:S(2)}) collective-permute-start(bf16[128,512]{1,0:T(8,128)(2,1)S(1)} %get-tuple-element.33), channel_id=1, source_target_pairs={{0,6},{2,4},{4,2},{6,0},{8,14},{10,12},{12,10},{14,8},{1,7},{3,5},... | collective-permute-start | bytes 393224 | tf_op jit(solution)/shard_map/ppermute | solution.py:273
  70.0 5.7 %collective-permute-start.15 = (bf16[64,512]{1,0:T(8,128)(2,1)S(1)}, bf16[64,512]{1,0:T(8,128)(2,1)S(1)}, u32[]{:S(2)}, u32[]{:S(2)}) collective-permute-start(bf16[64,512]{1,0:T(8,128)(2,1)S(1)} %get-tuple-element.35), channel_id=1, source_target_pairs={{0,8},{2,10},{4,12},{6,14},{8,0},{10,2},{12,4},{14,6},{1,9},{3,11}... | collective-permute-start | bytes 196616 | tf_op jit(solution)/shard_map/ppermute | solution.py:273

commit v6 on v5

--- a/solution.py
+++ b/solution.py
@@ -90,11 +90,26 @@
         lax.fori_loop(0, piece // width, turn, 0)
 
 
-def mean_kernel(base, fanout, pcap, fslice, nbr_ref, table_ref, out_ref, total):
+def mean_kernel(
+    base, count, fanout, pcap, fslice, nbr_hbm, table_ref, out_ref, total, nbr_ref, sems
+):
     feat_pos = lax.axis_index("feat")
+    stride = nbr_ref.shape[0] // count
+    copies = [
+        pltpu.make_async_copy(
+            nbr_hbm.at[pl.ds(pl.multiple_of((feat_pos ^ (base + i)) * stride, stride), stride)],
+            nbr_ref.at[pl.ds(i * stride, stride)],
+            sems.at[i],
+        )
+        for i in range(count)
+    ]
+    for copy in copies:
+        copy.start()
+    for copy in copies:
+        copy.wait()
 
     def partition(i, carry):
-        first = jnp.bitwise_xor(feat_pos, base + i) * (fanout * pcap)
+        first = i * stride
 
         def group(g, inner):
             at = pl.multiple_of(g * 8, 8)
@@ -123,7 +138,7 @@
             out_ref[i] = mean[:, :fslice].astype(jnp.bfloat16)
         return carry
 
-    lax.fori_loop(0, out_ref.shape[0], partition, 0)
+    lax.fori_loop(0, count, partition, 0)
 
 
 def unfold(block, fslice, pcap):
@@ -149,7 +164,8 @@
 
 def prepare_kernel(half, n_idx, *refs):
     parcel_refs, mean_refs = refs[:half], refs[half : 2 * half]
-    other_ref, bias_ref, w_ref, pre_ref, cross_ref = refs[2 * half :]
+    other_ref, bias_ref, last_ref, w_ref, pre_ref, cross_ref, moved_ref = refs[2 * half :]
+    moved_ref[...] = last_ref[0]
     fslice = w_ref.shape[1]
     pcap, width = pre_ref.shape
     first_core = lax.axis_index("rep") == 0
@@ -245,27 +261,30 @@
 def share_kernel(
     half, fanout_two, near_ref, far_ref, value_ref, hidden_ref, ws_ref, wn_ref, *refs
 ):
-    out_refs, other_ref = refs[:half], refs[half]
+    near_refs, far_refs, other_ref = refs[:half], refs[half : 2 * half], refs[2 * half]
     store_values(hidden_ref[...], ws_ref, wn_ref, fanout_two, other_ref)
     values = jnp.concatenate(
         [value_ref[0], other_ref[0], value_ref[1], other_ref[1]], axis=0
     )
-    near = jnp.dot(near_ref[...], values, preferred_element_type=jnp.float32)
-    far = jnp.dot(far_ref[...], values, preferred_element_type=jnp.float32)
-    rows = out_refs[0].shape[0] // 2
-    for s, out_ref in enumerate(out_refs):
-        out_ref[:rows, :] = near[s * rows : (s + 1) * rows].astype(jnp.bfloat16)
-        out_ref[rows:, :] = far[s * rows : (s + 1) * rows].astype(jnp.bfloat16)
+    for times_ref, out_refs in ((far_ref, far_refs), (near_ref, near_refs)):
+        part = jnp.dot(times_ref[...], values, preferred_element_type=jnp.float32)
+        rows = out_refs[0].shape[0]
+        for s, out_ref in enumerate(out_refs):
+            out_ref[...] = part[s * rows : (s + 1) * rows].astype(jnp.bfloat16)
 
 
 def side_sum_kernel(*refs):
-    near_ref, far_ref = refs[-2:]
-    rows = near_ref.shape[0]
     total = refs[0][...].astype(jnp.float32)
-    for ref in refs[1:-2]:
+    for ref in refs[1:-1]:
         total = total + ref[...].astype(jnp.float32)
-    near_ref[...] = total[:rows]
-    far_ref[...] = total[rows:].astype(jnp.bfloat16)
+    refs[-1][...] = total.astype(jnp.bfloat16)
+
+
+def last_kernel(bias_ref, *refs):
+    total = bias_ref[...] + refs[0][...].astype(jnp.float32)
+    for ref in refs[1:-1]:
+        total = total + ref[...].astype(jnp.float32)
+    refs[-1][...] = jnp.maximum(total, 0.0).astype(jnp.bfloat16)
 
 
 def swap(value, axis, step):
@@ -300,22 +319,30 @@
     anywhere = pl.BlockSpec(memory_space=pl.ANY)
     table_bytes = nodes * LANES * 4
 
-    def call(kernel, name, shapes, ins, args, after=(), scratch=(), limit=16 * MIB):
+    def spaced(shape):
+        return shape if len(shape) == 3 else (*shape, jax.ShapeDtypeStruct)
+
+    def call(kernel, name, shapes, ins, args, after=(), scratch=(), limit=16 * MIB, cost_us=1):
         def wrapped(*refs):
             kernel(*refs[: len(args)], *refs[len(args) + len(after) :])
 
         return pl.pallas_call(
             wrapped,
-            out_shape=tuple(jax.ShapeDtypeStruct(shape, dtype) for shape, dtype in shapes),
+            out_shape=tuple(
+                space(shape, dtype) for shape, dtype, space in map(spaced, shapes)
+            ),
             in_specs=[*ins, *([anywhere] * len(after))],
             out_specs=(vmem,) * len(shapes),
             scratch_shapes=scratch,
             compiler_params=pltpu.CompilerParams(vmem_limit_bytes=limit),
+            cost_estimate=pl.CostEstimate(
+                flops=int(cost_us * 1_100_000_000), bytes_accessed=0, transcendentals=0
+            ),
             name=name,
         )(*args, *after)
 
-    def pinned(value):
-        return pltpu.with_memory_space_constraint(value, pltpu.HBM)
+    def pinned(value, space=pltpu.HBM):
+        return pltpu.with_memory_space_constraint(value, space)
 
     def send(chunks):
         return [chunk if s == 0 else swap(chunk, "feat", s) for s, chunk in enumerate(chunks)]
@@ -339,65 +366,77 @@
     (table,) = call(
         turn_kernel,
         "turn",
-        [((nodes, LANES), jnp.float32)],
+        [((nodes, LANES), jnp.float32, pltpu.VMEM)],
         [hbm],
         (pinned(src_feats),),
         after=(parcels[0],),
         scratch=[pltpu.VMEM((fslice, nodes), bf16), pltpu.SemaphoreType.DMA((6,))],
         limit=table_bytes + 12 * MIB,
+        cost_us=3,
     )
     table = table.reshape(nodes, 1, LANES)
-    neighbors = nbr_one.reshape(-1)
+    stride = -(-fanout_one * pcap // 1024) * 1024
+    neighbors = jnp.pad(
+        nbr_one.reshape(n_feat, fanout_one * pcap), ((0, 0), (0, stride - fanout_one * pcap))
+    ).reshape(-1)
     chunk_shape = (pcap // 4 * 3, LANES) if folds(fslice, pcap) else (pcap, fslice)
 
     def means(base, count, after):
         (chunks,) = call(
-            functools.partial(mean_kernel, base, fanout_one, pcap, fslice),
+            functools.partial(mean_kernel, base, count, fanout_one, pcap, fslice),
             "mean",
             [((count, *chunk_shape), bf16)],
-            [smem, vmem],
-            (neighbors, table),
+            [anywhere, vmem],
+            (neighbors, pinned(table, pltpu.VMEM)),
             after=after,
-            scratch=[pltpu.VMEM((pcap, LANES), jnp.float32)],
+            scratch=[
+                pltpu.VMEM((pcap, LANES), jnp.float32),
+                pltpu.SMEM((count * stride,), jnp.int32),
+                pltpu.SemaphoreType.DMA((count,)),
+            ],
             limit=table_bytes + 8 * MIB,
-        )
-        return [chunks[i] for i in range(count)]
+            cost_us=2 * count,
+        )
+        return chunks
+
+    def split(chunks):
+        return [chunks[i] for i in range(chunks.shape[0])]
 
     far_means = means(half, half, ())
-    far_arrived = send(far_means)
+    far_arrived = send(split(far_means))
     (halves,) = call(
         halves_kernel,
         "halves",
         [((half, fslice, width), bf16)],
         [vmem] * half,
         arrived,
-        after=far_means[:1],
+        after=(far_means,),
     )
     other_halves = swap(halves, "rep", 1)
-    (last_mean,) = means(half - 1, 1, far_means[:1])
-    w_nbr, pre, cross = call(
+    last_mean = means(half - 1, 1, (far_means,))
+    w_nbr, pre, cross, moved = call(
         functools.partial(prepare_kernel, half, n_idx),
         "prepare",
         [
             ((half, fslice, width), bf16),
             ((pcap, width), jnp.float32),
             ((pcap + -(-half // 4) * n_idx, width), bf16),
+            (chunk_shape, bf16),
         ],
-        [vmem] * (2 * half + 2),
-        (*arrived, *far_arrived, other_halves, bias_one[None]),
-        after=(last_mean,),
+        [vmem] * (2 * half + 3),
+        (*arrived, *far_arrived, other_halves, bias_one[None], last_mean),
     )
     cross_arrived = swap(cross, "feat", half)
-    near_means = means(0, half - 1, (cross,))
-    near_arrived = send([*near_means, last_mean])
     (near_times,) = call(
         functools.partial(near_times_kernel, half, fslice, pcap, n_idx),
         "near_times",
         [((half * seed_count, 4 * pcap), bf16)],
         [vmem] * half,
         arrived,
-        after=near_means[:1],
-    )
+        after=(far_means,),
+    )
+    near_means = means(0, half - 1, (cross, near_times))
+    near_arrived = send([*split(near_means), moved])
     hidden, result = call(
         functools.partial(layer_kernel, half),
         "hidden",
@@ -416,21 +455,24 @@
     shares = call(
         functools.partial(share_kernel, half, fanout_two),
         "share",
-        [((2 * seed_count, width), bf16)] * half,
+        [((seed_count, width), bf16)] * (2 * half),
         [vmem] * 6,
         (near_times, far_times, value, other_hidden, w2_self, w2_nbr),
         scratch=[pltpu.VMEM((2, pcap, width), bf16)],
         limit=32 * MIB,
     )
-    near_sum, far_sum = call(
-        side_sum_kernel,
-        "side_sum",
-        [((seed_count, width), jnp.float32), ((seed_count, width), bf16)],
-        [vmem] * half,
-        send(shares),
-    )
-    pre_two = near_sum + swap(far_sum, "feat", half).astype(jnp.float32) + bias_two
-    seed_out = jnp.maximum(pre_two, 0.0).astype(bf16)
+    far_shares = send(shares[half:])
+    near_shares = send(shares[:half])
+    (far_sum,) = call(
+        side_sum_kernel, "side_sum", [((seed_count, width), bf16)], [vmem] * half, far_shares
+    )
+    (seed_out,) = call(
+        last_kernel,
+        "seeds",
+        [((seed_count, width), bf16)],
+        [vmem] * (half + 2),
+        (bias_two[None], *near_shares, swap(far_sum, "feat", half)),
+    )
     return (result[None, None], seed_out)
 
 

time: 76.6 us -> 69.3 us (0.905)
  waiting for transfers between devices: 18.2 us -> 11.2 us
  starting transfers between devices: 20 us -> 21.9 us
  Pallas kernels: 30.3 us -> 28.7 us
    ppermute x16 -> x19, waiting for transfers between devices: 18.2 us -> 11.2 us  [swap(): return lax.ppermute(value, axis, [(i, i ^ step) for i in range(size)])]
    ppermute x16 -> x19, starting transfers between devices: 20 us -> 21.9 us  [swap(): return lax.ppermute(value, axis, [(i, i ^ step) for i in range(size)])]
    pallas_call x12 -> x13, Pallas kernels: 30.3 us -> 28.7 us  [call(): pl.pallas_call(wrapped, out_shape=tuple((space(shape, dtype) for shape, d...]
    unnamed x16 -> x18, local copies, waits for them, and re-layouts: 5.44 us -> 5.46 us
  transfers between devices with their start and end apart: 16 -> 19, of which waited for: 7 -> 8; matrix products, arithmetic and copies ran while one was open for 0% -> 0% of each run, Pallas kernels for 35% -> 34%
where the time goes in v6:
time: 69.3 us; the launch traced here: 69.1 us
  Pallas kernels  28.7 us (41%)
  starting transfers between devices  21.9 us (32%)
  waiting for transfers between devices  11.2 us (16%)
  local copies, waits for them, and re-layouts  5.57 us (8%)
  between operations  1.52 us (2%)
    pallas_call x13, Pallas kernels, call(): pl.pallas_call(wrapped, out_shape=tuple((space(shape, dtype) for shape, d...  28.7 us
    ppermute x19, starting transfers between devices, swap(): return lax.ppermute(value, axis, [(i, i ^ step) for i in range(size)])  21.9 us
    ppermute x19, waiting for transfers between devices, swap(): return lax.ppermute(value, axis, [(i, i ^ step) for i in range(size)])  11.2 us
    unnamed x18, local copies, waits for them, and re-layouts  5.46 us
  transfers between devices with their start and end apart: 19, of which 8 were waited for; matrix products, arithmetic and copies ran while one was open for 0% of the time, Pallas kernels for 34%

profile of v6, /device:TPU:0, one launch (start us, length us, event | category | flops | bytes accessed | tf_op | source)
XLA Modules:
  0.0 69.1 jit_solution(10147300056301635087)
XLA Ops:
  0.6 1.6 %pack.1 = (bf16[192,512]{1,0:T(8,128)(2,1)S(1)}, bf16[192,512]{1,0:T(8,128)(2,1)S(1)}, bf16[192,512]{1,0:T(8,128)(2,1)S(1)}, bf16[192,512]{1,0:T(8,128)(2,1)S(1)}) custom-call(bf16[96,12288]{1,0:T(8,128)(2,1)} %refs_0_.4, s32[1,64]{1,0:T(1,128)} %bitcast.32, s32[15,64]{1,0:T(8,128)} %bitcast.31, bf16[96,512]{1,0:T(8,128)(2,1)} %refs_3_.2, ...), custom_call_target="tpu_custom_call" | custom-call | flops 1100000000 | tf_op jit(solution)/shard_map/pack/pallas_call | solution.py:329
  2.2 0.0 copy-start.7
  2.2 3.0 %collective-permute-start = (bf16[192,512]{1,0:T(8,128)(2,1)S(1)}, bf16[192,512]{1,0:T(8,128)(2,1)S(1)}, u32[]{:S(2)}, u32[]{:S(2)}) collective-permute-start(bf16[192,512]{1,0:T(8,128)(2,1)S(1)} %get-tuple-element.23), channel_id=1, source_target_pairs={{0,2},{2,0},{4,6},{6,4},{8,10},{10,8},{12,14},{14,12},{1,3},{3,1},... | collective-permute-start | bytes 589832 | tf_op jit(solution)/shard_map/ppermute | solution.py:292
  5.3 1.6 %collective-permute-start.1 = (bf16[192,512]{1,0:T(8,128)(2,1)S(1)}, bf16[192,512]{1,0:T(8,128)(2,1)S(1)}, u32[]{:S(2)}, u32[]{:S(2)}) collective-permute-start(bf16[192,512]{1,0:T(8,128)(2,1)S(1)} %get-tuple-element.24), channel_id=1, source_target_pairs={{0,4},{2,6},{4,0},{6,2},{8,12},{10,14},{12,8},{14,10},{1,5},{3,7},... | collective-permute-start | bytes 589832 | tf_op jit(solution)/shard_map/ppermute | solution.py:292
  6.8 0.0 collective-permute-start.2
  6.8 3.5 %turn.1 = f32[12288,128]{1,0:T(8,128)S(1)} custom-call(bf16[96,12288]{1,0:T(8,128)(2,1)} %refs_0_.4, bf16[192,512]{1,0:T(8,128)(2,1)S(1)} %get-tuple-element.22.refs_1_.refs_0_), custom_call_target="tpu_custom_call" | custom-call | flops 3300000000 | tf_op jit(solution)/shard_map/turn/pallas_call | solution.py:329
  10.4 0.0 copy-start.4
  10.4 2.6 %copy-done.4 = f32[12288,128]{1,0:T(8,128)} copy-done((f32[12288,128]{1,0:T(8,128)}, f32[12288,128]{1,0:T(8,128)S(1)}, u32[]{:S(2)}) %copy-start.4) | copy-done | bytes 6291480
  13.0 0.0 copy-done.7
  13.0 0.2 reduce
  13.2 0.1 reshape.13
  13.4 0.0 copy-start.5
  13.4 2.8 %copy-done.5 = f32[12288,128]{1,0:T(8,128)S(1)} copy-done((f32[12288,128]{1,0:T(8,128)S(1)}, f32[12288,128]{1,0:T(8,128)}, u32[]{:S(2)}) %copy-start.5) | copy-done | bytes 6291480
  16.1 9.2 %mean.3.refs_4_.refs_2_ = bf16[4,144,128]{2,1,0:T(8,128)(2,1)S(1)} custom-call(s32[16384]{0:T(1024)S(1)} %bitcast.23, f32[12288,1,128]{2,1,0:T(1,128)S(1)} %bitcast.28), custom_call_target="tpu_custom_call" | custom-call | flops 8800000000 | tf_op jit(solution)/shard_map/mean/pallas_call | solution.py:329
  25.3 0.0 collective-permute-done.refs_1_
  25.3 0.0 collective-permute-done.1.refs_2_
  25.3 0.0 collective-permute-done.2.refs_3_
  25.4 0.0 copy-start.2
  25.4 0.1 collective-permute-start.6
  25.5 2.0 %collective-permute-start.3 = (bf16[144,128]{1,0:T(8,128)(2,1)S(1)}, bf16[144,128]{1,0:T(8,128)(2,1)S(1)}, u32[]{:S(2)}, u32[]{:S(2)}) collective-permute-start(bf16[144,128]{1,0:T(8,128)(2,1)S(1)} %get-tuple-element.44), channel_id=1, source_target_pairs={{0,2},{2,0},{4,6},{6,4},{8,10},{10,8},{12,14},{14,12},{1,3},{3,1},... | collective-permute-start | bytes 110600 | tf_op jit(solution)/shard_map/ppermute | solution.py:292
  27.5 1.6 %collective-permute-start.4 = (bf16[144,128]{1,0:T(8,128)(2,1)S(1)}, bf16[144,128]{1,0:T(8,128)(2,1)S(1)}, u32[]{:S(2)}, u32[]{:S(2)}) collective-permute-start(bf16[144,128]{1,0:T(8,128)(2,1)S(1)} %get-tuple-element.43), channel_id=1, source_target_pairs={{0,4},{2,6},{4,0},{6,2},{8,12},{10,14},{12,8},{14,10},{1,5},{3,7},... | collective-permute-start | bytes 110600 | tf_op jit(solution)/shard_map/ppermute | solution.py:292
  29.0 0.0 collective-permute-start.5
  29.0 0.0 copy-done.6
  29.0 2.4 %mean.4.refs_10_ = bf16[1,144,128]{2,1,0:T(8,128)(2,1)S(1)} custom-call(s32[16384]{0:T(1024)S(1)} %bitcast.24, f32[12288,1,128]{2,1,0:T(1,128)S(1)} %bitcast.29, bf16[4,144,128]{2,1,0:T(8,128)(2,1)S(1)} %mean.3.refs_4_.refs_2_), custom_call_target="tpu_custom_call" | custom-call | flops 2200000000 | tf_op jit(solution)/shard_map/mean/pallas_call | solution.py:329
  31.5 0.8 %near_times.1.refs_3_.refs_0_ = bf16[256,768]{1,0:T(8,128)(2,1)S(1)} custom-call(bf16[192,512]{1,0:T(8,128)(2,1)S(1)} %get-tuple-element.22.refs_1_.refs_0_, bf16[192,512]{1,0:T(8,128)(2,1)S(1)} %collective-permute-done.refs_1_, bf16[192,512]{1,0:T(8,128)(2,1)S(1)} %collective-permute-done.1.refs_2_, bf16[192,512]{1,0:T(8,128)(2,1)S(1)} %collective-permute-done.2.refs_3_, ...), custom_call_target="tpu_custom_call" | custom-call | flops 1100000000 | tf_op jit(solution)/shard_map/near_times/pallas_call | solution.py:329
  32.3 0.0 collective-permute-done.3.refs_5_
  32.3 0.0 collective-permute-done.4.refs_6_
  32.3 1.6 %collective-permute-done.5.refs_7_ = bf16[144,128]{1,0:T(8,128)(2,1)S(1)} collective-permute-done((bf16[144,128]{1,0:T(8,128)(2,1)S(1)}, bf16[144,128]{1,0:T(8,128)(2,1)S(1)}, u32[]{:S(2)}, u32[]{:S(2)}) %collective-permute-start.5) | collective-permute-done | bytes 36896 | tf_op jit(solution)/shard_map/ppermute | solution.py:292
  33.9 0.0 collective-permute-done.6.refs_8_
  33.9 0.0 copy-done.2
  33.9 0.8 %prepare.1 = (bf16[4,96,512]{2,1,0:T(8,128)(2,1)S(1)}, f32[192,512]{1,0:T(8,128)S(1)}, bf16[208,512]{1,0:T(8,128)(2,1)S(1)}, bf16[144,128]{1,0:T(8,128)(2,1)S(1)}) custom-call(bf16[192,512]{1,0:T(8,128)(2,1)S(1)} %get-tuple-element.22.refs_1_.refs_0_, bf16[192,512]{1,0:T(8,128)(2,1)S(1)} %collective-permute-done.refs_1_, ...), custom_call_target="tpu_custom_call" | custom-call | flops 1100000000 | tf_op jit(solution)/shard_map/prepare/pallas_call | solution.py:329
  34.7 0.0 copy-start
  34.7 0.0 copy-start.1
  34.8 2.7 %collective-permute-start.10 = (bf16[208,512]{1,0:T(8,128)(2,1)S(1)}, bf16[208,512]{1,0:T(8,128)(2,1)S(1)}, u32[]{:S(2)}, u32[]{:S(2)}) collective-permute-start(bf16[208,512]{1,0:T(8,128)(2,1)S(1)} %get-tuple-element.26.refs_2_), channel_id=1, source_target_pairs={{0,8},{2,10},{4,12},{6,14},{8,0},{10,2},{12,4},{14,6},{1,9},{3,11}... | collective-permute-start | bytes 638984 | tf_op jit(solution)/shard_map/ppermute | solution.py:292
  37.4 7.0 %mean.5 = bf16[3,144,128]{2,1,0:T(8,128)(2,1)S(1)} custom-call(s32[16384]{0:T(1024)S(1)} %bitcast.25, f32[12288,1,128]{2,1,0:T(1,128)S(1)} %bitcast.30, bf16[208,512]{1,0:T(8,128)(2,1)S(1)} %get-tuple-element.26.refs_2_, bf16[256,768]{1,0:T(8,128)(2,1)S(1)} %near_times.1.refs_3_.refs_0_), custom_call_target="tpu_custom_call" | custom-call | flops 6600000000 | tf_op jit(solution)/shard_map/mean/pallas_call | solution.py:329
  44.4 0.6 collective-permute-start.7
  45.0 1.4 %collective-permute-start.8 = (bf16[144,128]{1,0:T(8,128)(2,1)S(1)}, bf16[144,128]{1,0:T(8,128)(2,1)S(1)}, u32[]{:S(2)}, u32[]{:S(2)}) collective-permute-start(bf16[144,128]{1,0:T(8,128)(2,1)S(1)} %get-tuple-element.46), channel_id=1, source_target_pairs={{0,4},{2,6},{4,0},{6,2},{8,12},{10,14},{12,8},{14,10},{1,5},{3,7},... | collective-permute-start | bytes 110600 | tf_op jit(solution)/shard_map/ppermute | solution.py:292
  46.4 1.6 %collective-permute-start.9 = (bf16[144,128]{1,0:T(8,128)(2,1)S(1)}, bf16[144,128]{1,0:T(8,128)(2,1)S(1)}, u32[]{:S(2)}, u32[]{:S(2)}) collective-permute-start(bf16[144,128]{1,0:T(8,128)(2,1)S(1)} %get-tuple-element.27), channel_id=1, source_target_pairs={{0,6},{2,4},{4,2},{6,0},{8,14},{10,12},{12,10},{14,8},{1,7},{3,5},... | collective-permute-start | bytes 110600 | tf_op jit(solution)/shard_map/ppermute | solution.py:292
  48.6 0.0 collective-permute-done.7.refs_2_
  48.7 0.3 collective-permute-done.8.refs_3_
  49.0 2.3 %collective-permute-done.9.refs_4_ = bf16[144,128]{1,0:T(8,128)(2,1)S(1)} collective-permute-done((bf16[144,128]{1,0:T(8,128)(2,1)S(1)}, bf16[144,128]{1,0:T(8,128)(2,1)S(1)}, u32[]{:S(2)}, u32[]{:S(2)}) %collective-permute-start.9) | collective-permute-done | bytes 36896 | tf_op jit(solution)/shard_map/ppermute | solution.py:292
  51.3 0.0 collective-permute-done.10.refs_7_.refs_0_
  51.3 1.1 %hidden.1 = (bf16[192,512]{1,0:T(8,128)(2,1)S(1)}, bf16[192,512]{1,0:T(8,128)(2,1)}) custom-call(s32[1,1]{1,0:T(1,128)S(6)} %copy.14.refs_0_, bf16[144,128]{1,0:T(8,128)(2,1)S(1)} %get-tuple-element.48.refs_1_, bf16[144,128]{1,0:T(8,128)(2,1)S(1)} %collective-permute-done.7.refs_2_, bf16[144,128]{1,0:T(8,128)(2,1)S(1)} %collective-permute-done.8.refs_3_, ...), custom_call_target="tpu_custom_call" | custom-call | flops 1100000000 | tf_op jit(solution)/shard_map/hidden/pallas_call | solution.py:329
  52.3 0.0 collective-permute-start.11
  52.3 0.0 copy-done
  52.3 0.0 copy-done.1
  52.3 0.8 %far_times.1 = (bf16[256,768]{1,0:T(8,128)(2,1)S(1)}, bf16[2,192,512]{2,1,0:T(8,128)(2,1)S(1)}) custom-call(bf16[208,512]{1,0:T(8,128)(2,1)S(1)} %collective-permute-done.10.refs_7_.refs_0_, bf16[192,512]{1,0:T(8,128)(2,1)S(1)} %get-tuple-element.31.refs_1_, bf16[512,512]{1,0:T(8,128)(2,1)S(1)} %copy-done, bf16[512,512]{1,0:T(8,128)(2,1)S(1)} %copy-done.1), custom_call_target="tpu_custom_call" | custom-call | flops 1100000000 | tf_op jit(solution)/shard_map/far_times/pallas_call | solution.py:329
  53.2 0.6 collective-permute-done.11.refs_3_
  53.8 0.8 %share.1 = (bf16[64,512]{1,0:T(8,128)(2,1)S(1)}, bf16[64,512]{1,0:T(8,128)(2,1)S(1)}, bf16[64,512]{1,0:T(8,128)(2,1)S(1)}, bf16[64,512]{1,0:T(8,128)(2,1)S(1)}, ...) custom-call(bf16[256,768]{1,0:T(8,128)(2,1)S(1)} %near_times.1.refs_, ...), custom_call_target="tpu_custom_call" | custom-call | flops 1100000000 | tf_op jit(solution)/shard_map/share/pallas_call | solution.py:329
  54.5 0.6 collective-permute-start.15
  55.2 1.6 %collective-permute-start.16 = (bf16[64,512]{1,0:T(8,128)(2,1)S(1)}, bf16[64,512]{1,0:T(8,128)(2,1)S(1)}, u32[]{:S(2)}, u32[]{:S(2)}) collective-permute-start(bf16[64,512]{1,0:T(8,128)(2,1)S(1)} %get-tuple-element.40), channel_id=1, source_target_pairs={{0,4},{2,6},{4,0},{6,2},{8,12},{10,14},{12,8},{14,10},{1,5},{3,7},... | collective-permute-start | bytes 196616 | tf_op jit(solution)/shard_map/ppermute | solution.py:292
  56.8 1.3 %collective-permute-start.17 = (bf16[64,512]{1,0:T(8,128)(2,1)S(1)}, bf16[64,512]{1,0:T(8,128)(2,1)S(1)}, u32[]{:S(2)}, u32[]{:S(2)}) collective-permute-start(bf16[64,512]{1,0:T(8,128)(2,1)S(1)} %get-tuple-element.41), channel_id=1, source_target_pairs={{0,6},{2,4},{4,2},{6,0},{8,14},{10,12},{12,10},{14,8},{1,7},{3,5},... | collective-permute-start | bytes 196616 | tf_op jit(solution)/shard_map/ppermute | solution.py:292
  58.1 0.6 collective-permute-start.12
  58.7 1.6 %collective-permute-start.13 = (bf16[64,512]{1,0:T(8,128)(2,1)S(1)}, bf16[64,512]{1,0:T(8,128)(2,1)S(1)}, u32[]{:S(2)}, u32[]{:S(2)}) collective-permute-start(bf16[64,512]{1,0:T(8,128)(2,1)S(1)} %get-tuple-element.36), channel_id=1, source_target_pairs={{0,4},{2,6},{4,0},{6,2},{8,12},{10,14},{12,8},{14,10},{1,5},{3,7},... | collective-permute-start | bytes 196616 | tf_op jit(solution)/shard_map/ppermute | solution.py:292
  60.3 0.0 collective-permute-done.15.refs_1_
  60.3 1.3 %collective-permute-start.14 = (bf16[64,512]{1,0:T(8,128)(2,1)S(1)}, bf16[64,512]{1,0:T(8,128)(2,1)S(1)}, u32[]{:S(2)}, u32[]{:S(2)}) collective-permute-start(bf16[64,512]{1,0:T(8,128)(2,1)S(1)} %get-tuple-element.37), channel_id=1, source_target_pairs={{0,6},{2,4},{4,2},{6,0},{8,14},{10,12},{12,10},{14,8},{1,7},{3,5},... | collective-permute-start | bytes 196616 | tf_op jit(solution)/shard_map/ppermute | solution.py:292
  61.6 0.0 collective-permute-done.16.refs_2_
  61.6 1.1 %collective-permute-done.17.refs_3_ = bf16[64,512]{1,0:T(8,128)(2,1)S(1)} collective-permute-done((bf16[64,512]{1,0:T(8,128)(2,1)S(1)}, bf16[64,512]{1,0:T(8,128)(2,1)S(1)}, u32[]{:S(2)}, u32[]{:S(2)}) %collective-permute-start.17) | collective-permute-done | bytes 65568 | tf_op jit(solution)/shard_map/ppermute | solution.py:292
  62.7 0.4 collective-permute-start.18
  63.1 0.5 collective-permute-done.12.refs_2_
  63.6 0.0 collective-permute-done.13.refs_3_
  63.6 2.4 %collective-permute-done.14.refs_4_ = bf16[64,512]{1,0:T(8,128)(2,1)S(1)} collective-permute-done((bf16[64,512]{1,0:T(8,128)(2,1)S(1)}, bf16[64,512]{1,0:T(8,128)(2,1)S(1)}, u32[]{:S(2)}, u32[]{:S(2)}) %collective-permute-start.14) | collective-permute-done | bytes 65568 | tf_op jit(solution)/shard_map/ppermute | solution.py:292
  66.0 2.4 %collective-permute-done.18.refs_5_ = bf16[64,512]{1,0:T(8,128)(2,1)S(1)} collective-permute-done((bf16[64,512]{1,0:T(8,128)(2,1)S(1)}, bf16[64,512]{1,0:T(8,128)(2,1)S(1)}, u32[]{:S(2)}, u32[]{:S(2)}) %collective-permute-start.18) | collective-permute-done | bytes 65568 | tf_op jit(solution)/shard_map/ppermute | solution.py:292
  68.4 0.7 seeds.1
  (9 shorter events, 0.1 us)
Async XLA Ops:
  2.2 10.8 %copy-start.7 = (s32[8,1,10,192]{3,1,2,0:T(1,128)S(1)}, s32[8,1,10,192]{3,1,2,0:T(1,128)}, u32[]{:S(2)}) copy-start(s32[8,1,10,192]{3,1,2,0:T(1,128)} %param.12) | copy-start | bytes 184324
  2.2 23.1 %collective-permute-start = (bf16[192,512]{1,0:T(8,128)(2,1)S(1)}, bf16[192,512]{1,0:T(8,128)(2,1)S(1)}, u32[]{:S(2)}, u32[]{:S(2)}) collective-permute-start(bf16[192,512]{1,0:T(8,128)(2,1)S(1)} %get-tuple-element.23), channel_id=1, source_target_pairs={{0,2},{2,0},{4,6},{6,4},{8,10},{10,8},{12,14},{14,12},{1,3},{3,1},... | collective-permute-start | bytes 589832 | tf_op jit(solution)/shard_map/ppermute | solution.py:292
  5.3 20.1 %collective-permute-start.1 = (bf16[192,512]{1,0:T(8,128)(2,1)S(1)}, bf16[192,512]{1,0:T(8,128)(2,1)S(1)}, u32[]{:S(2)}, u32[]{:S(2)}) collective-permute-start(bf16[192,512]{1,0:T(8,128)(2,1)S(1)} %get-tuple-element.24), channel_id=1, source_target_pairs={{0,4},{2,6},{4,0},{6,2},{8,12},{10,14},{12,8},{14,10},{1,5},{3,7},... | collective-permute-start | bytes 589832 | tf_op jit(solution)/shard_map/ppermute | solution.py:292
  6.8 18.5 %collective-permute-start.2 = (bf16[192,512]{1,0:T(8,128)(2,1)S(1)}, bf16[192,512]{1,0:T(8,128)(2,1)S(1)}, u32[]{:S(2)}, u32[]{:S(2)}) collective-permute-start(bf16[192,512]{1,0:T(8,128)(2,1)S(1)} %get-tuple-element.25), channel_id=1, source_target_pairs={{0,6},{2,4},{4,2},{6,0},{8,14},{10,12},{12,10},{14,8},{1,7},{3,5},... | collective-permute-start | bytes 589832 | tf_op jit(solution)/shard_map/ppermute | solution.py:292
  10.4 2.6 %copy-start.4 = (f32[12288,128]{1,0:T(8,128)}, f32[12288,128]{1,0:T(8,128)S(1)}, u32[]{:S(2)}) copy-start(f32[12288,128]{1,0:T(8,128)S(1)} %turn.1) | copy-start | bytes 18874372
  13.4 2.8 %copy-start.5 = (f32[12288,128]{1,0:T(8,128)S(1)}, f32[12288,128]{1,0:T(8,128)}, u32[]{:S(2)}) copy-start(f32[12288,128]{1,0:T(8,128)} %copy-done.4) | copy-start | bytes 18874372
  16.1 12.9 %copy-start.6 = (f32[12288,128]{1,0:T(8,128)S(1)}, f32[12288,128]{1,0:T(8,128)}, u32[]{:S(2)}) copy-start(f32[12288,128]{1,0:T(8,128)} %copy-done.4) | copy-start | bytes 18874372
  25.4 8.5 %copy-start.2 = (f32[512]{0:T(512)S(1)}, f32[512]{0:T(512)}, u32[]{:S(2)}) copy-start(f32[512]{0:T(512)} %param.18) | copy-start | bytes 6148
  25.4 8.5 %collective-permute-start.6 = (bf16[4,96,512]{2,1,0:T(8,128)(2,1)S(1)}, bf16[4,96,512]{2,1,0:T(8,128)(2,1)S(1)}, u32[]{:S(2)}, u32[]{:S(2)}) collective-permute-start(bf16[4,96,512]{2,1,0:T(8,128)(2,1)S(1)} %halves.1), channel_id=1, source_target_pairs={{0,1},{1,0},{2,3},{3,2},{4,5},{5,4},{6,7},{7,6},{8,9},{9,8},{10,11... | collective-permute-start | bytes 1179656 | tf_op jit(solution)/shard_map/ppermute | solution.py:292
  25.5 6.8 %collective-permute-start.3 = (bf16[144,128]{1,0:T(8,128)(2,1)S(1)}, bf16[144,128]{1,0:T(8,128)(2,1)S(1)}, u32[]{:S(2)}, u32[]{:S(2)}) collective-permute-start(bf16[144,128]{1,0:T(8,128)(2,1)S(1)} %get-tuple-element.44), channel_id=1, source_target_pairs={{0,2},{2,0},{4,6},{6,4},{8,10},{10,8},{12,14},{14,12},{1,3},{3,1},... | collective-permute-start | bytes 110600 | tf_op jit(solution)/shard_map/ppermute | solution.py:292
  27.5 4.8 %collective-permute-start.4 = (bf16[144,128]{1,0:T(8,128)(2,1)S(1)}, bf16[144,128]{1,0:T(8,128)(2,1)S(1)}, u32[]{:S(2)}, u32[]{:S(2)}) collective-permute-start(bf16[144,128]{1,0:T(8,128)(2,1)S(1)} %get-tuple-element.43), channel_id=1, source_target_pairs={{0,4},{2,6},{4,0},{6,2},{8,12},{10,14},{12,8},{14,10},{1,5},{3,7},... | collective-permute-start | bytes 110600 | tf_op jit(solution)/shard_map/ppermute | solution.py:292
  29.0 4.9 %collective-permute-start.5 = (bf16[144,128]{1,0:T(8,128)(2,1)S(1)}, bf16[144,128]{1,0:T(8,128)(2,1)S(1)}, u32[]{:S(2)}, u32[]{:S(2)}) collective-permute-start(bf16[144,128]{1,0:T(8,128)(2,1)S(1)} %get-tuple-element.42), channel_id=1, source_target_pairs={{0,6},{2,4},{4,2},{6,0},{8,14},{10,12},{12,10},{14,8},{1,7},{3,5},... | collective-permute-start | bytes 110600 | tf_op jit(solution)/shard_map/ppermute | solution.py:292
  34.7 17.6 %copy-start = (bf16[512,512]{1,0:T(8,128)(2,1)S(1)}, bf16[512,512]{1,0:T(8,128)(2,1)}, u32[]{:S(2)}) copy-start(bf16[512,512]{1,0:T(8,128)(2,1)} %refs_4_.3) | copy-start | bytes 1572868
  34.7 17.6 %copy-start.1 = (bf16[512,512]{1,0:T(8,128)(2,1)S(1)}, bf16[512,512]{1,0:T(8,128)(2,1)}, u32[]{:S(2)}) copy-start(bf16[512,512]{1,0:T(8,128)(2,1)} %refs_5_.1) | copy-start | bytes 1572868
  34.8 16.5 %collective-permute-start.10 = (bf16[208,512]{1,0:T(8,128)(2,1)S(1)}, bf16[208,512]{1,0:T(8,128)(2,1)S(1)}, u32[]{:S(2)}, u32[]{:S(2)}) collective-permute-start(bf16[208,512]{1,0:T(8,128)(2,1)S(1)} %get-tuple-element.26.refs_2_), channel_id=1, source_target_pairs={{0,8},{2,10},{4,12},{6,14},{8,0},{10,2},{12,4},{14,6},{1,9},{3,11}... | collective-permute-start | bytes 638984 | tf_op jit(solution)/shard_map/ppermute | solution.py:292
  44.4 4.2 %collective-permute-start.7 = (bf16[144,128]{1,0:T(8,128)(2,1)S(1)}, bf16[144,128]{1,0:T(8,128)(2,1)S(1)}, u32[]{:S(2)}, u32[]{:S(2)}) collective-permute-start(bf16[144,128]{1,0:T(8,128)(2,1)S(1)} %get-tuple-element.47), channel_id=1, source_target_pairs={{0,2},{2,0},{4,6},{6,4},{8,10},{10,8},{12,14},{14,12},{1,3},{3,1},... | collective-permute-start | bytes 110600 | tf_op jit(solution)/shard_map/ppermute | solution.py:292
  45.0 4.0 %collective-permute-start.8 = (bf16[144,128]{1,0:T(8,128)(2,1)S(1)}, bf16[144,128]{1,0:T(8,128)(2,1)S(1)}, u32[]{:S(2)}, u32[]{:S(2)}) collective-permute-start(bf16[144,128]{1,0:T(8,128)(2,1)S(1)} %get-tuple-element.46), channel_id=1, source_target_pairs={{0,4},{2,6},{4,0},{6,2},{8,12},{10,14},{12,8},{14,10},{1,5},{3,7},... | collective-permute-start | bytes 110600 | tf_op jit(solution)/shard_map/ppermute | solution.py:292
  46.4 4.9 %collective-permute-start.9 = (bf16[144,128]{1,0:T(8,128)(2,1)S(1)}, bf16[144,128]{1,0:T(8,128)(2,1)S(1)}, u32[]{:S(2)}, u32[]{:S(2)}) collective-permute-start(bf16[144,128]{1,0:T(8,128)(2,1)S(1)} %get-tuple-element.27), channel_id=1, source_target_pairs={{0,6},{2,4},{4,2},{6,0},{8,14},{10,12},{12,10},{14,8},{1,7},{3,5},... | collective-permute-start | bytes 110600 | tf_op jit(solution)/shard_map/ppermute | solution.py:292
  52.3 16.1 %copy-start.3 = (f32[512]{0:T(512)S(1)}, f32[512]{0:T(512)}, u32[]{:S(2)}) copy-start(f32[512]{0:T(512)} %param.21) | copy-start | bytes 6148
  52.3 1.4 %collective-permute-start.11 = (bf16[192,512]{1,0:T(8,128)(2,1)S(1)}, bf16[192,512]{1,0:T(8,128)(2,1)S(1)}, u32[]{:S(2)}, u32[]{:S(2)}) collective-permute-start(bf16[192,512]{1,0:T(8,128)(2,1)S(1)} %get-tuple-element.31.refs_1_), channel_id=1, source_target_pairs={{0,1},{1,0},{2,3},{3,2},{4,5},{5,4},{6,7},{7,6},{8,9},{9,8},{10,11... | collective-permute-start | bytes 589832 | tf_op jit(solution)/shard_map/ppermute | solution.py:292
  54.5 5.7 %collective-permute-start.15 = (bf16[64,512]{1,0:T(8,128)(2,1)S(1)}, bf16[64,512]{1,0:T(8,128)(2,1)S(1)}, u32[]{:S(2)}, u32[]{:S(2)}) collective-permute-start(bf16[64,512]{1,0:T(8,128)(2,1)S(1)} %get-tuple-element.39), channel_id=1, source_target_pairs={{0,2},{2,0},{4,6},{6,4},{8,10},{10,8},{12,14},{14,12},{1,3},{3,1},... | collective-permute-start | bytes 196616 | tf_op jit(solution)/shard_map/ppermute | solution.py:292
  55.2 6.4 %collective-permute-start.16 = (bf16[64,512]{1,0:T(8,128)(2,1)S(1)}, bf16[64,512]{1,0:T(8,128)(2,1)S(1)}, u32[]{:S(2)}, u32[]{:S(2)}) collective-permute-start(bf16[64,512]{1,0:T(8,128)(2,1)S(1)} %get-tuple-element.40), channel_id=1, source_target_pairs={{0,4},{2,6},{4,0},{6,2},{8,12},{10,14},{12,8},{14,10},{1,5},{3,7},... | collective-permute-start | bytes 196616 | tf_op jit(solution)/shard_map/ppermute | solution.py:292
  56.8 5.9 %collective-permute-start.17 = (bf16[64,512]{1,0:T(8,128)(2,1)S(1)}, bf16[64,512]{1,0:T(8,128)(2,1)S(1)}, u32[]{:S(2)}, u32[]{:S(2)}) collective-permute-start(bf16[64,512]{1,0:T(8,128)(2,1)S(1)} %get-tuple-element.41), channel_id=1, source_target_pairs={{0,6},{2,4},{4,2},{6,0},{8,14},{10,12},{12,10},{14,8},{1,7},{3,5},... | collective-permute-start | bytes 196616 | tf_op jit(solution)/shard_map/ppermute | solution.py:292
  58.1 5.5 %collective-permute-start.12 = (bf16[64,512]{1,0:T(8,128)(2,1)S(1)}, bf16[64,512]{1,0:T(8,128)(2,1)S(1)}, u32[]{:S(2)}, u32[]{:S(2)}) collective-permute-start(bf16[64,512]{1,0:T(8,128)(2,1)S(1)} %get-tuple-element.35), channel_id=1, source_target_pairs={{0,2},{2,0},{4,6},{6,4},{8,10},{10,8},{12,14},{14,12},{1,3},{3,1},... | collective-permute-start | bytes 196616 | tf_op jit(solution)/shard_map/ppermute | solution.py:292
  58.7 4.9 %collective-permute-start.13 = (bf16[64,512]{1,0:T(8,128)(2,1)S(1)}, bf16[64,512]{1,0:T(8,128)(2,1)S(1)}, u32[]{:S(2)}, u32[]{:S(2)}) collective-permute-start(bf16[64,512]{1,0:T(8,128)(2,1)S(1)} %get-tuple-element.36), channel_id=1, source_target_pairs={{0,4},{2,6},{4,0},{6,2},{8,12},{10,14},{12,8},{14,10},{1,5},{3,7},... | collective-permute-start | bytes 196616 | tf_op jit(solution)/shard_map/ppermute | solution.py:292
  60.3 5.7 %collective-permute-start.14 = (bf16[64,512]{1,0:T(8,128)(2,1)S(1)}, bf16[64,512]{1,0:T(8,128)(2,1)S(1)}, u32[]{:S(2)}, u32[]{:S(2)}) collective-permute-start(bf16[64,512]{1,0:T(8,128)(2,1)S(1)} %get-tuple-element.37), channel_id=1, source_target_pairs={{0,6},{2,4},{4,2},{6,0},{8,14},{10,12},{12,10},{14,8},{1,7},{3,5},... | collective-permute-start | bytes 196616 | tf_op jit(solution)/shard_map/ppermute | solution.py:292
  62.7 5.7 %collective-permute-start.18 = (bf16[64,512]{1,0:T(8,128)(2,1)S(1)}, bf16[64,512]{1,0:T(8,128)(2,1)S(1)}, u32[]{:S(2)}, u32[]{:S(2)}) collective-permute-start(bf16[64,512]{1,0:T(8,128)(2,1)S(1)} %side_sum.1), channel_id=1, source_target_pairs={{0,8},{2,10},{4,12},{6,14},{8,0},{10,2},{12,4},{14,6},{1,9},{3,11}... | collective-permute-start | bytes 196616 | tf_op jit(solution)/shard_map/ppermute | solution.py:292

commit v7 on v6

--- a/solution.py
+++ b/solution.py
@@ -23,6 +23,7 @@
     nbr_hbm,
     w_self_hbm,
     w_nbr_hbm,
+    count_ref,
     *refs,
 ):
     half = n_feat // 2
@@ -52,6 +53,8 @@
     digits = jnp.concatenate([high, idx - high * 128], axis=1).astype(jnp.float32)
     digits = digits.astype(jnp.bfloat16)
     weight = jnp.where(first_core, w_self_ref[...], w_nbr_ref[...])
+    live = jnp.full((8, LANES), count_ref[0, 0].astype(jnp.float32)).astype(jnp.bfloat16)
+    tags = jnp.concatenate([digits, live], axis=0)
     for s, parcel_ref in enumerate(parcel_refs):
         parcel_ref[:fslice, :] = weight
         for place, step in enumerate((s, s ^ half)):
@@ -62,7 +65,7 @@
                 near_side = own
         both = jnp.concatenate([near_side, own], axis=1)
         parcel_ref[fslice:, : 2 * pcap] = both.astype(jnp.bfloat16)
-        parcel_ref[fslice : fslice + idx.shape[0], 2 * pcap :] = digits
+        parcel_ref[fslice : fslice + tags.shape[0], 2 * pcap :] = tags
 
 
 def turn_kernel(src_hbm, table_ref, src_ref, sems):
@@ -83,16 +86,16 @@
 
         def turn(step, carry):
             at = pl.multiple_of(i * piece + step * width, width)
-            block = src_ref[:, pl.ds(at, width)].astype(jnp.float32)
-            table_ref[pl.ds(at, width), :fslice] = block.T
+            table_ref[pl.ds(at, width), :fslice] = src_ref[:, pl.ds(at, width)].T.astype(
+                jnp.float32
+            )
             return carry
 
         lax.fori_loop(0, piece // width, turn, 0)
 
 
-def mean_kernel(
-    base, count, fanout, pcap, fslice, nbr_hbm, table_ref, out_ref, total, nbr_ref, sems
-):
+def mean_kernel(base, count, fanout, pcap, fslice, n_idx, nbr_hbm, table_ref, *refs):
+    parcel_refs, (out_ref, total, nbr_ref, live_ref, sems) = refs[:-5], refs[-5:]
     feat_pos = lax.axis_index("feat")
     stride = nbr_ref.shape[0] // count
     copies = [
@@ -105,6 +108,11 @@
     ]
     for copy in copies:
         copy.start()
+    for i in range(count):
+        live_ref[i] = pcap
+    for i, ref in enumerate(parcel_refs):
+        tag = ref[fslice + n_idx : fslice + n_idx + 8, 2 * pcap :]
+        live_ref[i] = jnp.max(tag.astype(jnp.float32)).astype(jnp.int32)
     for copy in copies:
         copy.wait()
 
@@ -112,8 +120,8 @@
         first = i * stride
 
         def group(g, inner):
-            at = pl.multiple_of(g * 8, 8)
-            for u in range(8):
+            at = pl.multiple_of(g * 16, 16)
+            for u in range(16):
                 rows = [table_ref[nbr_ref[first + k * pcap + at + u]] for k in range(fanout)]
                 while len(rows) > 1:
                     rows = [a + b for a, b in zip(rows[::2], rows[1::2])] + (
@@ -122,7 +130,7 @@
                 total[pl.ds(at + u, 1), :] = rows[0]
             return inner
 
-        lax.fori_loop(0, pcap // 8, group, 0)
+        lax.fori_loop(0, lax.div(live_ref[i] + 15, 16), group, 0)
         mean = total[...] / fanout
         if folds(fslice, pcap):
             part = pcap // 4
@@ -156,10 +164,16 @@
     return jnp.concatenate([wide, tail], axis=0)[:, :fslice].astype(jnp.bfloat16)
 
 
-def halves_kernel(*refs):
-    out_ref = refs[-1]
-    for s, ref in enumerate(refs[:-1]):
-        out_ref[s] = ref[: out_ref.shape[1], :]
+def halves_kernel(half, *refs):
+    parcel_refs, chunks_ref, out_ref, chunk_refs = (
+        refs[:half],
+        refs[half],
+        refs[half + 1],
+        refs[half + 2 :],
+    )
+    for s in range(half):
+        out_ref[s] = parcel_refs[s][: out_ref.shape[1], :]
+        chunk_refs[s][...] = chunks_ref[s]
 
 
 def prepare_kernel(half, n_idx, *refs):
@@ -258,32 +272,40 @@
     result_ref[...] = hidden
 
 
-def share_kernel(
-    half, fanout_two, near_ref, far_ref, value_ref, hidden_ref, ws_ref, wn_ref, *refs
+def far_share_kernel(
+    half, fanout_two, far_ref, value_ref, hidden_ref, ws_ref, wn_ref, *refs
 ):
-    near_refs, far_refs, other_ref = refs[:half], refs[half : 2 * half], refs[2 * half]
+    out_refs, values_ref, other_ref = refs[:half], refs[half], refs[half + 1]
+    pcap = hidden_ref.shape[0]
     store_values(hidden_ref[...], ws_ref, wn_ref, fanout_two, other_ref)
-    values = jnp.concatenate(
-        [value_ref[0], other_ref[0], value_ref[1], other_ref[1]], axis=0
-    )
-    for times_ref, out_refs in ((far_ref, far_refs), (near_ref, near_refs)):
-        part = jnp.dot(times_ref[...], values, preferred_element_type=jnp.float32)
-        rows = out_refs[0].shape[0]
-        for s, out_ref in enumerate(out_refs):
-            out_ref[...] = part[s * rows : (s + 1) * rows].astype(jnp.bfloat16)
+    for i in range(2):
+        values_ref[pl.ds(2 * i * pcap, pcap), :] = value_ref[i]
+        values_ref[pl.ds((2 * i + 1) * pcap, pcap), :] = other_ref[i]
+    store_shares(far_ref, values_ref, out_refs)
+
+
+def store_shares(times_ref, values_ref, out_refs):
+    rows = out_refs[0].shape[0]
+    part = jnp.dot(times_ref[...], values_ref[...], preferred_element_type=jnp.float32)
+    for s, out_ref in enumerate(out_refs):
+        out_ref[...] = part[s * rows : (s + 1) * rows].astype(jnp.bfloat16)
+
+
+def near_share_kernel(near_ref, values_ref, *out_refs):
+    store_shares(near_ref, values_ref, out_refs)
 
 
 def side_sum_kernel(*refs):
     total = refs[0][...].astype(jnp.float32)
     for ref in refs[1:-1]:
         total = total + ref[...].astype(jnp.float32)
-    refs[-1][...] = total.astype(jnp.bfloat16)
+    refs[-1][: total.shape[0], :] = total.astype(jnp.bfloat16)
 
 
 def last_kernel(bias_ref, *refs):
-    total = bias_ref[...] + refs[0][...].astype(jnp.float32)
-    for ref in refs[1:-1]:
-        total = total + ref[...].astype(jnp.float32)
+    total = bias_ref[...]
+    for ref in refs[:-1]:
+        total = total + ref[: refs[-1].shape[0], :].astype(jnp.float32)
     refs[-1][...] = jnp.maximum(total, 0.0).astype(jnp.bfloat16)
 
 
@@ -319,18 +341,13 @@
     anywhere = pl.BlockSpec(memory_space=pl.ANY)
     table_bytes = nodes * LANES * 4
 
-    def spaced(shape):
-        return shape if len(shape) == 3 else (*shape, jax.ShapeDtypeStruct)
-
     def call(kernel, name, shapes, ins, args, after=(), scratch=(), limit=16 * MIB, cost_us=1):
         def wrapped(*refs):
             kernel(*refs[: len(args)], *refs[len(args) + len(after) :])
 
         return pl.pallas_call(
             wrapped,
-            out_shape=tuple(
-                space(shape, dtype) for shape, dtype, space in map(spaced, shapes)
-            ),
+            out_shape=tuple(jax.ShapeDtypeStruct(shape, dtype) for shape, dtype in shapes),
             in_specs=[*ins, *([anywhere] * len(after))],
             out_specs=(vmem,) * len(shapes),
             scratch_shapes=scratch,
@@ -341,18 +358,22 @@
             name=name,
         )(*args, *after)
 
-    def pinned(value, space=pltpu.HBM):
-        return pltpu.with_memory_space_constraint(value, space)
+    def pinned(value):
+        return pltpu.with_memory_space_constraint(value, pltpu.HBM)
 
     def send(chunks):
         return [chunk if s == 0 else swap(chunk, "feat", s) for s, chunk in enumerate(chunks)]
 
+    stride = -(-fanout_one * pcap // 1024) * 1024
+    neighbors = jnp.pad(
+        nbr_one.reshape(n_feat, fanout_one * pcap), ((0, 0), (0, stride - fanout_one * pcap))
+    ).reshape(-1)
     parcels = call(
         functools.partial(pack_kernel, n_feat, pcap),
         "pack",
         [((2 * fslice, width), bf16)] * half,
-        [hbm] * 5,
-        [pinned(x) for x in (src_feats, seed_rows[None], nbr_two.T, w1_self, w1_nbr)],
+        [hbm] * 5 + [smem],
+        [pinned(x) for x in (src_feats, seed_rows[None], nbr_two.T, w1_self, w1_nbr)] + [counts],
         scratch=[
             pltpu.VMEM((fslice, n_feat * 2 * pcap), bf16),
             pltpu.VMEM((1, seed_count), jnp.int32),
@@ -366,32 +387,29 @@
     (table,) = call(
         turn_kernel,
         "turn",
-        [((nodes, LANES), jnp.float32, pltpu.VMEM)],
+        [((nodes, LANES), jnp.float32)],
         [hbm],
         (pinned(src_feats),),
-        after=(parcels[0],),
+        after=(parcels[0], neighbors),
         scratch=[pltpu.VMEM((fslice, nodes), bf16), pltpu.SemaphoreType.DMA((6,))],
         limit=table_bytes + 12 * MIB,
         cost_us=3,
     )
     table = table.reshape(nodes, 1, LANES)
-    stride = -(-fanout_one * pcap // 1024) * 1024
-    neighbors = jnp.pad(
-        nbr_one.reshape(n_feat, fanout_one * pcap), ((0, 0), (0, stride - fanout_one * pcap))
-    ).reshape(-1)
     chunk_shape = (pcap // 4 * 3, LANES) if folds(fslice, pcap) else (pcap, fslice)
 
-    def means(base, count, after):
+    def means(base, count, parcels=(), after=()):
         (chunks,) = call(
-            functools.partial(mean_kernel, base, count, fanout_one, pcap, fslice),
+            functools.partial(mean_kernel, base, count, fanout_one, pcap, fslice, n_idx),
             "mean",
             [((count, *chunk_shape), bf16)],
-            [anywhere, vmem],
-            (neighbors, pinned(table, pltpu.VMEM)),
+            [anywhere] + [vmem] * (1 + len(parcels)),
+            (neighbors, table, *parcels),
             after=after,
             scratch=[
                 pltpu.VMEM((pcap, LANES), jnp.float32),
                 pltpu.SMEM((count * stride,), jnp.int32),
+                pltpu.SMEM((count,), jnp.int32),
                 pltpu.SemaphoreType.DMA((count,)),
             ],
             limit=table_bytes + 8 * MIB,
@@ -399,21 +417,17 @@
         )
         return chunks
 
-    def split(chunks):
-        return [chunks[i] for i in range(chunks.shape[0])]
-
-    far_means = means(half, half, ())
-    far_arrived = send(split(far_means))
-    (halves,) = call(
-        halves_kernel,
+    far_means = means(half, half)
+    halves, *far_chunks = call(
+        functools.partial(halves_kernel, half),
         "halves",
-        [((half, fslice, width), bf16)],
-        [vmem] * half,
-        arrived,
-        after=(far_means,),
-    )
+        [((half, fslice, width), bf16)] + [(chunk_shape, bf16)] * half,
+        [vmem] * (half + 1),
+        (*arrived, far_means),
+    )
+    far_arrived = send(far_chunks)
     other_halves = swap(halves, "rep", 1)
-    last_mean = means(half - 1, 1, (far_means,))
+    last_mean = means(half - 1, 1, arrived[half - 1 :], (far_chunks[0],))
     w_nbr, pre, cross, moved = call(
         functools.partial(prepare_kernel, half, n_idx),
         "prepare",
@@ -435,8 +449,8 @@
         arrived,
         after=(far_means,),
     )
-    near_means = means(0, half - 1, (cross, near_times))
-    near_arrived = send([*split(near_means), moved])
+    near_means = means(0, half - 1, arrived[: half - 1], (cross, near_times))
+    near_arrived = send([*(near_means[i] for i in range(half - 1)), moved])
     hidden, result = call(
         functools.partial(layer_kernel, half),
         "hidden",
@@ -452,26 +466,35 @@
         [vmem] * 4,
         (cross_arrived, hidden, w2_self, w2_nbr),
     )
-    shares = call(
-        functools.partial(share_kernel, half, fanout_two),
-        "share",
-        [((seed_count, width), bf16)] * (2 * half),
-        [vmem] * 6,
-        (near_times, far_times, value, other_hidden, w2_self, w2_nbr),
+    *far_shares, values = call(
+        functools.partial(far_share_kernel, half, fanout_two),
+        "far_share",
+        [((seed_count, width), bf16)] * half + [((4 * pcap, width), bf16)],
+        [vmem] * 5,
+        (far_times, value, other_hidden, w2_self, w2_nbr),
         scratch=[pltpu.VMEM((2, pcap, width), bf16)],
         limit=32 * MIB,
     )
-    far_shares = send(shares[half:])
-    near_shares = send(shares[:half])
     (far_sum,) = call(
-        side_sum_kernel, "side_sum", [((seed_count, width), bf16)], [vmem] * half, far_shares
+        side_sum_kernel, "side_sum", [((seed_count + 8, width), bf16)], [vmem] * half, send(far_shares)
+    )
+    near_shares = send(
+        call(
+            near_share_kernel,
+            "near_share",
+            [((seed_count, width), bf16)] * half,
+            [vmem] * 2,
+            (near_times, values),
+            after=(far_sum,),
+            limit=32 * MIB,
+        )
     )
     (seed_out,) = call(
         last_kernel,
         "seeds",
         [((seed_count, width), bf16)],
         [vmem] * (half + 2),
-        (bias_two[None], *near_shares, swap(far_sum, "feat", half)),
+        (bias_two[None], swap(far_sum, "feat", half), *near_shares),
     )
     return (result[None, None], seed_out)
 

time: 69.3 us -> 64.1 us (0.925)
  local copies, waits for them, and re-layouts: 5.57 us -> 0.15 us
  Pallas kernels: 28.7 us -> 25.7 us
  waiting for transfers between devices: 11.2 us -> 13 us
  starting transfers between devices: 21.9 us -> 22.9 us
  other arithmetic: 0.2 us -> 1.09 us
    unnamed x18 -> x10, local copies, waits for them, and re-layouts: 5.46 us -> 0.05 us
    pallas_call x13 -> x14, Pallas kernels: 28.7 us -> 25.7 us  [call(): pl.pallas_call(wrapped, out_shape=tuple((jax.ShapeDtypeStruct(shape, dtyp...]
    ppermute x19, waiting for transfers between devices: 11.2 us -> 13 us  [swap(): return lax.ppermute(value, axis, [(i, i ^ step) for i in range(size)])]
    ppermute x19, starting transfers between devices: 21.9 us -> 22.9 us  [swap(): return lax.ppermute(value, axis, [(i, i ^ step) for i in range(size)])]
    unnamed x1, other arithmetic: 0.2 us -> 1.09 us
  transfers between devices with their start and end apart: 19 -> 19, of which waited for: 8 -> 11; matrix products, arithmetic and copies ran while one was open for 0% -> 2% of each run, Pallas kernels for 34% -> 32%
where the time goes in v7:
time: 64.1 us; the launch traced here: 64.3 us
  Pallas kernels  25.7 us (40%)
  starting transfers between devices  22.9 us (36%)
  waiting for transfers between devices  13 us (20%)
  between operations  1.48 us (2%)
  other arithmetic  1.09 us (2%)
    pallas_call x14, Pallas kernels, call(): pl.pallas_call(wrapped, out_shape=tuple((jax.ShapeDtypeStruct(shape, dtyp...  25.7 us
    ppermute x19, starting transfers between devices, swap(): return lax.ppermute(value, axis, [(i, i ^ step) for i in range(size)])  22.9 us
    ppermute x19, waiting for transfers between devices, swap(): return lax.ppermute(value, axis, [(i, i ^ step) for i in range(size)])  13 us
  transfers between devices with their start and end apart: 19, of which 11 were waited for; matrix products, arithmetic and copies ran while one was open for 2% of the time, Pallas kernels for 32%

profile of v7, /device:TPU:0, one launch (start us, length us, event | category | flops | bytes accessed | tf_op | source)
XLA Modules:
  0.0 64.3 jit_solution(7639999608292708963)
XLA Ops:
  1.3 1.6 %pack.1 = (bf16[192,512]{1,0:T(8,128)(2,1)S(1)}, bf16[192,512]{1,0:T(8,128)(2,1)S(1)}, bf16[192,512]{1,0:T(8,128)(2,1)S(1)}, bf16[192,512]{1,0:T(8,128)(2,1)S(1)}) custom-call(bf16[96,12288]{1,0:T(8,128)(2,1)} %refs_0_.4, s32[1,64]{1,0:T(1,128)} %bitcast.25, s32[15,64]{1,0:T(8,128)} %bitcast.24, bf16[96,512]{1,0:T(8,128)(2,1)} %refs_3_.3, ...), custom_call_target="tpu_custom_call" | custom-call | flops 1100000000 | tf_op jit(solution)/shard_map/pack/pallas_call | solution.py:348
  2.9 3.0 %collective-permute-start = (bf16[192,512]{1,0:T(8,128)(2,1)S(1)}, bf16[192,512]{1,0:T(8,128)(2,1)S(1)}, u32[]{:S(2)}, u32[]{:S(2)}) collective-permute-start(bf16[192,512]{1,0:T(8,128)(2,1)S(1)} %get-tuple-element.29), channel_id=1, source_target_pairs={{0,2},{2,0},{4,6},{6,4},{8,10},{10,8},{12,14},{14,12},{1,3},{3,1},... | collective-permute-start | bytes 589832 | tf_op jit(solution)/shard_map/ppermute | solution.py:314
  5.9 1.6 %collective-permute-start.1 = (bf16[192,512]{1,0:T(8,128)(2,1)S(1)}, bf16[192,512]{1,0:T(8,128)(2,1)S(1)}, u32[]{:S(2)}, u32[]{:S(2)}) collective-permute-start(bf16[192,512]{1,0:T(8,128)(2,1)S(1)} %get-tuple-element.30), channel_id=1, source_target_pairs={{0,4},{2,6},{4,0},{6,2},{8,12},{10,14},{12,8},{14,10},{1,5},{3,7},... | collective-permute-start | bytes 589832 | tf_op jit(solution)/shard_map/ppermute | solution.py:314
  7.5 0.0 collective-permute-start.2
  7.5 1.1 %reduce = s32[8,10,192]{2,1,0:T(8,128)S(1)} reduce(s32[8,1,10,192]{3,1,2,0:T(1,128)} %param.12, s32[]{:T(128)} %constant.0.clone.1), dimensions={1}, to_apply=%param.12.reduce_sub_computation | reduce | bytes 122884 | tf_op args[1]
  8.6 0.1 reshape.13
  8.7 3.2 %turn.1 = f32[12288,128]{1,0:T(8,128)S(1)} custom-call(bf16[96,12288]{1,0:T(8,128)(2,1)} %refs_0_.4, bf16[192,512]{1,0:T(8,128)(2,1)S(1)} %get-tuple-element.28.refs_1_.refs_0_.refs_2_, s32[16384]{0:T(1024)S(1)} %bitcast.15), custom_call_target="tpu_custom_call" | custom-call | flops 3300000000 | tf_op jit(solution)/shard_map/turn/pallas_call | solution.py:348
  11.9 8.5 %mean.3.refs_4_ = bf16[4,144,128]{2,1,0:T(8,128)(2,1)S(1)} custom-call(s32[16384]{0:T(1024)S(1)} %bitcast.16, f32[12288,1,128]{2,1,0:T(1,128)S(1)} %bitcast.21), custom_call_target="tpu_custom_call" | custom-call | flops 8800000000 | tf_op jit(solution)/shard_map/mean/pallas_call | solution.py:348
  20.5 0.0 collective-permute-done.refs_1_.refs_3_
  20.5 0.0 collective-permute-done.1.refs_2_.refs_4_
  20.5 0.0 collective-permute-done.2.refs_3_.refs_2_
  20.5 0.0 copy-start.2
  20.6 0.1 collective-permute-start.6
  20.6 2.0 %collective-permute-start.3 = (bf16[144,128]{1,0:T(8,128)(2,1)S(1)}, bf16[144,128]{1,0:T(8,128)(2,1)S(1)}, u32[]{:S(2)}, u32[]{:S(2)}) collective-permute-start(bf16[144,128]{1,0:T(8,128)(2,1)S(1)} %get-tuple-element.33), channel_id=1, source_target_pairs={{0,2},{2,0},{4,6},{6,4},{8,10},{10,8},{12,14},{14,12},{1,3},{3,1},... | collective-permute-start | bytes 110600 | tf_op jit(solution)/shard_map/ppermute | solution.py:314
  22.6 1.6 %collective-permute-start.4 = (bf16[144,128]{1,0:T(8,128)(2,1)S(1)}, bf16[144,128]{1,0:T(8,128)(2,1)S(1)}, u32[]{:S(2)}, u32[]{:S(2)}) collective-permute-start(bf16[144,128]{1,0:T(8,128)(2,1)S(1)} %get-tuple-element.34), channel_id=1, source_target_pairs={{0,4},{2,6},{4,0},{6,2},{8,12},{10,14},{12,8},{14,10},{1,5},{3,7},... | collective-permute-start | bytes 110600 | tf_op jit(solution)/shard_map/ppermute | solution.py:314
  24.2 0.0 collective-permute-start.5
  24.2 2.4 %mean.4.refs_10_ = bf16[1,144,128]{2,1,0:T(8,128)(2,1)S(1)} custom-call(s32[16384]{0:T(1024)S(1)} %bitcast.17, f32[12288,1,128]{2,1,0:T(1,128)S(1)} %bitcast.22, bf16[192,512]{1,0:T(8,128)(2,1)S(1)} %collective-permute-done.2.refs_3_.refs_2_, bf16[144,128]{1,0:T(8,128)(2,1)S(1)} %get-tuple-element.32.refs_3_.refs_4_), custom_call_target="tpu_custom_call" | custom-call | flops 2200000000 | tf_op jit(solution)/shard_map/mean/pallas_call | solution.py:348
  26.6 0.8 %near_times.1.refs_6_.refs_0_ = bf16[256,768]{1,0:T(8,128)(2,1)S(1)} custom-call(bf16[192,512]{1,0:T(8,128)(2,1)S(1)} %get-tuple-element.28.refs_1_.refs_0_.refs_2_, bf16[192,512]{1,0:T(8,128)(2,1)S(1)} %collective-permute-done.refs_1_.refs_3_, bf16[192,512]{1,0:T(8,128)(2,1)S(1)} %collective-permute-done.1.refs_2_.refs_4_, ...), custom_call_target="tpu_custom_call" | custom-call | flops 1100000000 | tf_op jit(solution)/shard_map/near_times/pallas_call | solution.py:348
  27.3 0.0 collective-permute-done.3.refs_5_
  27.3 0.0 collective-permute-done.4.refs_6_
  27.3 1.7 %collective-permute-done.5.refs_7_ = bf16[144,128]{1,0:T(8,128)(2,1)S(1)} collective-permute-done((bf16[144,128]{1,0:T(8,128)(2,1)S(1)}, bf16[144,128]{1,0:T(8,128)(2,1)S(1)}, u32[]{:S(2)}, u32[]{:S(2)}) %collective-permute-start.5) | collective-permute-done | bytes 36896 | tf_op jit(solution)/shard_map/ppermute | solution.py:314
  29.0 0.0 collective-permute-done.6.refs_8_
  29.0 0.0 copy-done.2
  29.0 0.8 %prepare.1 = (bf16[4,96,512]{2,1,0:T(8,128)(2,1)S(1)}, f32[192,512]{1,0:T(8,128)S(1)}, bf16[208,512]{1,0:T(8,128)(2,1)S(1)}, bf16[144,128]{1,0:T(8,128)(2,1)S(1)}) custom-call(bf16[192,512]{1,0:T(8,128)(2,1)S(1)} %get-tuple-element.28.refs_1_.refs_0_.refs_2_, bf16[192,512]{1,0:T(8,128)(2,1)S(1)} %collective-permute-done.refs_1_.refs_3_, ...), custom_call_target="tpu_custom_call" | custom-call | flops 1100000000 | tf_op jit(solution)/shard_map/prepare/pallas_call | solution.py:348
  29.9 0.0 copy-start
  29.9 0.0 copy-start.1
  29.9 2.7 %collective-permute-start.10 = (bf16[208,512]{1,0:T(8,128)(2,1)S(1)}, bf16[208,512]{1,0:T(8,128)(2,1)S(1)}, u32[]{:S(2)}, u32[]{:S(2)}) collective-permute-start(bf16[208,512]{1,0:T(8,128)(2,1)S(1)} %get-tuple-element.37.refs_5_), channel_id=1, source_target_pairs={{0,8},{2,10},{4,12},{6,14},{8,0},{10,2},{12,4},{14,6},{1,9},{3,11}... | collective-permute-start | bytes 638984 | tf_op jit(solution)/shard_map/ppermute | solution.py:314
  32.6 4.8 %mean.5 = bf16[3,144,128]{2,1,0:T(8,128)(2,1)S(1)} custom-call(s32[16384]{0:T(1024)S(1)} %bitcast.18, f32[12288,1,128]{2,1,0:T(1,128)S(1)} %bitcast.23, bf16[192,512]{1,0:T(8,128)(2,1)S(1)} %get-tuple-element.28.refs_1_.refs_0_.refs_2_, bf16[192,512]{1,0:T(8,128)(2,1)S(1)} %collective-permute-done.refs_1_.refs_3_, ...), custom_call_target="tpu_custom_call" | custom-call | flops 6600000000 | tf_op jit(solution)/shard_map/mean/pallas_call | solution.py:348
  37.4 1.3 %collective-permute-start.7 = (bf16[144,128]{1,0:T(8,128)(2,1)S(1)}, bf16[144,128]{1,0:T(8,128)(2,1)S(1)}, u32[]{:S(2)}, u32[]{:S(2)}) collective-permute-start(bf16[144,128]{1,0:T(8,128)(2,1)S(1)} %get-tuple-element.55), channel_id=1, source_target_pairs={{0,2},{2,0},{4,6},{6,4},{8,10},{10,8},{12,14},{14,12},{1,3},{3,1},... | collective-permute-start | bytes 110600 | tf_op jit(solution)/shard_map/ppermute | solution.py:314
  38.7 0.9 %collective-permute-start.8 = (bf16[144,128]{1,0:T(8,128)(2,1)S(1)}, bf16[144,128]{1,0:T(8,128)(2,1)S(1)}, u32[]{:S(2)}, u32[]{:S(2)}) collective-permute-start(bf16[144,128]{1,0:T(8,128)(2,1)S(1)} %get-tuple-element.54), channel_id=1, source_target_pairs={{0,4},{2,6},{4,0},{6,2},{8,12},{10,14},{12,8},{14,10},{1,5},{3,7},... | collective-permute-start | bytes 110600 | tf_op jit(solution)/shard_map/ppermute | solution.py:314
  39.6 1.4 %collective-permute-start.9 = (bf16[144,128]{1,0:T(8,128)(2,1)S(1)}, bf16[144,128]{1,0:T(8,128)(2,1)S(1)}, u32[]{:S(2)}, u32[]{:S(2)}) collective-permute-start(bf16[144,128]{1,0:T(8,128)(2,1)S(1)} %get-tuple-element.38), channel_id=1, source_target_pairs={{0,6},{2,4},{4,2},{6,0},{8,14},{10,12},{12,10},{14,8},{1,7},{3,5},... | collective-permute-start | bytes 110600 | tf_op jit(solution)/shard_map/ppermute | solution.py:314
  40.9 0.5 collective-permute-done.7.refs_2_
  41.4 1.2 %collective-permute-done.8.refs_3_ = bf16[144,128]{1,0:T(8,128)(2,1)S(1)} collective-permute-done((bf16[144,128]{1,0:T(8,128)(2,1)S(1)}, bf16[144,128]{1,0:T(8,128)(2,1)S(1)}, u32[]{:S(2)}, u32[]{:S(2)}) %collective-permute-start.8) | collective-permute-done | bytes 36896 | tf_op jit(solution)/shard_map/ppermute | solution.py:314
  42.6 1.8 %collective-permute-done.9.refs_4_ = bf16[144,128]{1,0:T(8,128)(2,1)S(1)} collective-permute-done((bf16[144,128]{1,0:T(8,128)(2,1)S(1)}, bf16[144,128]{1,0:T(8,128)(2,1)S(1)}, u32[]{:S(2)}, u32[]{:S(2)}) %collective-permute-start.9) | collective-permute-done | bytes 36896 | tf_op jit(solution)/shard_map/ppermute | solution.py:314
  44.4 0.0 collective-permute-done.10.refs_7_.refs_0_
  44.4 1.1 %hidden.1 = (bf16[192,512]{1,0:T(8,128)(2,1)S(1)}, bf16[192,512]{1,0:T(8,128)(2,1)}) custom-call(s32[1,1]{1,0:T(1,128)S(6)} %copy.14.refs_5_.refs_0_, bf16[144,128]{1,0:T(8,128)(2,1)S(1)} %get-tuple-element.56.refs_1_, bf16[144,128]{1,0:T(8,128)(2,1)S(1)} %collective-permute-done.7.refs_2_, bf16[144,128]{1,0:T(8,128)(2,1)S(1)} %collective-permute-done.8.refs_3_, ...), custom_call_target="tpu_custom_call" | custom-call | flops 1100000000 | tf_op jit(solution)/shard_map/hidden/pallas_call | solution.py:348
  45.5 0.0 collective-permute-start.11
  45.5 0.0 copy-done
  45.5 0.0 copy-done.1
  45.5 0.8 %far_times.1 = (bf16[256,768]{1,0:T(8,128)(2,1)S(1)}, bf16[2,192,512]{2,1,0:T(8,128)(2,1)S(1)}) custom-call(bf16[208,512]{1,0:T(8,128)(2,1)S(1)} %collective-permute-done.10.refs_7_.refs_0_, bf16[192,512]{1,0:T(8,128)(2,1)S(1)} %get-tuple-element.42.refs_1_, bf16[512,512]{1,0:T(8,128)(2,1)S(1)} %copy-done, bf16[512,512]{1,0:T(8,128)(2,1)S(1)} %copy-done.1), custom_call_target="tpu_custom_call" | custom-call | flops 1100000000 | tf_op jit(solution)/shard_map/far_times/pallas_call | solution.py:348
  46.3 0.0 copy-start.3
  46.3 0.6 collective-permute-done.11.refs_2_
  46.9 0.6 far_share.1
  47.5 1.0 %collective-permute-start.12 = (bf16[64,512]{1,0:T(8,128)(2,1)S(1)}, bf16[64,512]{1,0:T(8,128)(2,1)S(1)}, u32[]{:S(2)}, u32[]{:S(2)}) collective-permute-start(bf16[64,512]{1,0:T(8,128)(2,1)S(1)} %get-tuple-element.46), channel_id=1, source_target_pairs={{0,2},{2,0},{4,6},{6,4},{8,10},{10,8},{12,14},{14,12},{1,3},{3,1},... | collective-permute-start | bytes 196616 | tf_op jit(solution)/shard_map/ppermute | solution.py:314
  48.5 1.0 %collective-permute-start.13 = (bf16[64,512]{1,0:T(8,128)(2,1)S(1)}, bf16[64,512]{1,0:T(8,128)(2,1)S(1)}, u32[]{:S(2)}, u32[]{:S(2)}) collective-permute-start(bf16[64,512]{1,0:T(8,128)(2,1)S(1)} %get-tuple-element.47), channel_id=1, source_target_pairs={{0,4},{2,6},{4,0},{6,2},{8,12},{10,14},{12,8},{14,10},{1,5},{3,7},... | collective-permute-start | bytes 196616 | tf_op jit(solution)/shard_map/ppermute | solution.py:314
  49.5 1.6 %collective-permute-start.14 = (bf16[64,512]{1,0:T(8,128)(2,1)S(1)}, bf16[64,512]{1,0:T(8,128)(2,1)S(1)}, u32[]{:S(2)}, u32[]{:S(2)}) collective-permute-start(bf16[64,512]{1,0:T(8,128)(2,1)S(1)} %get-tuple-element.48), channel_id=1, source_target_pairs={{0,6},{2,4},{4,2},{6,0},{8,14},{10,12},{12,10},{14,8},{1,7},{3,5},... | collective-permute-start | bytes 196616 | tf_op jit(solution)/shard_map/ppermute | solution.py:314
  51.1 0.8 %collective-permute-done.12.refs_1_ = bf16[64,512]{1,0:T(8,128)(2,1)S(1)} collective-permute-done((bf16[64,512]{1,0:T(8,128)(2,1)S(1)}, bf16[64,512]{1,0:T(8,128)(2,1)S(1)}, u32[]{:S(2)}, u32[]{:S(2)}) %collective-permute-start.12) | collective-permute-done | bytes 65568 | tf_op jit(solution)/shard_map/ppermute | solution.py:314
  51.8 1.4 %collective-permute-done.13.refs_2_ = bf16[64,512]{1,0:T(8,128)(2,1)S(1)} collective-permute-done((bf16[64,512]{1,0:T(8,128)(2,1)S(1)}, bf16[64,512]{1,0:T(8,128)(2,1)S(1)}, u32[]{:S(2)}, u32[]{:S(2)}) %collective-permute-start.13) | collective-permute-done | bytes 65568 | tf_op jit(solution)/shard_map/ppermute | solution.py:314
  53.2 1.5 %collective-permute-done.14.refs_3_ = bf16[64,512]{1,0:T(8,128)(2,1)S(1)} collective-permute-done((bf16[64,512]{1,0:T(8,128)(2,1)S(1)}, bf16[64,512]{1,0:T(8,128)(2,1)S(1)}, u32[]{:S(2)}, u32[]{:S(2)}) %collective-permute-start.14) | collective-permute-done | bytes 65568 | tf_op jit(solution)/shard_map/ppermute | solution.py:314
  54.7 1.3 %collective-permute-start.15 = (bf16[72,512]{1,0:T(8,128)(2,1)S(1)}, bf16[72,512]{1,0:T(8,128)(2,1)S(1)}, u32[]{:S(2)}, u32[]{:S(2)}) collective-permute-start(bf16[72,512]{1,0:T(8,128)(2,1)S(1)} %side_sum.1.refs_2_), channel_id=1, source_target_pairs={{0,8},{2,10},{4,12},{6,14},{8,0},{10,2},{12,4},{14,6},{1,9},{3,11}... | collective-permute-start | bytes 221192 | tf_op jit(solution)/shard_map/ppermute | solution.py:314
  56.0 0.4 near_share.1
  56.4 1.7 %collective-permute-start.16 = (bf16[64,512]{1,0:T(8,128)(2,1)S(1)}, bf16[64,512]{1,0:T(8,128)(2,1)S(1)}, u32[]{:S(2)}, u32[]{:S(2)}) collective-permute-start(bf16[64,512]{1,0:T(8,128)(2,1)S(1)} %get-tuple-element.51), channel_id=1, source_target_pairs={{0,2},{2,0},{4,6},{6,4},{8,10},{10,8},{12,14},{14,12},{1,3},{3,1},... | collective-permute-start | bytes 196616 | tf_op jit(solution)/shard_map/ppermute | solution.py:314
  58.1 0.3 collective-permute-start.17
  58.4 1.5 %collective-permute-start.18 = (bf16[64,512]{1,0:T(8,128)(2,1)S(1)}, bf16[64,512]{1,0:T(8,128)(2,1)S(1)}, u32[]{:S(2)}, u32[]{:S(2)}) collective-permute-start(bf16[64,512]{1,0:T(8,128)(2,1)S(1)} %get-tuple-element.53), channel_id=1, source_target_pairs={{0,6},{2,4},{4,2},{6,0},{8,14},{10,12},{12,10},{14,8},{1,7},{3,5},... | collective-permute-start | bytes 196616 | tf_op jit(solution)/shard_map/ppermute | solution.py:314
  59.9 1.3 %collective-permute-done.16.refs_3_ = bf16[64,512]{1,0:T(8,128)(2,1)S(1)} collective-permute-done((bf16[64,512]{1,0:T(8,128)(2,1)S(1)}, bf16[64,512]{1,0:T(8,128)(2,1)S(1)}, u32[]{:S(2)}, u32[]{:S(2)}) %collective-permute-start.16) | collective-permute-done | bytes 65568 | tf_op jit(solution)/shard_map/ppermute | solution.py:314
  61.2 1.2 %collective-permute-done.17.refs_4_ = bf16[64,512]{1,0:T(8,128)(2,1)S(1)} collective-permute-done((bf16[64,512]{1,0:T(8,128)(2,1)S(1)}, bf16[64,512]{1,0:T(8,128)(2,1)S(1)}, u32[]{:S(2)}, u32[]{:S(2)}) %collective-permute-start.17) | collective-permute-done | bytes 65568 | tf_op jit(solution)/shard_map/ppermute | solution.py:314
  62.4 1.2 %collective-permute-done.18.refs_5_ = bf16[64,512]{1,0:T(8,128)(2,1)S(1)} collective-permute-done((bf16[64,512]{1,0:T(8,128)(2,1)S(1)}, bf16[64,512]{1,0:T(8,128)(2,1)S(1)}, u32[]{:S(2)}, u32[]{:S(2)}) %collective-permute-start.18) | collective-permute-done | bytes 65568 | tf_op jit(solution)/shard_map/ppermute | solution.py:314
  63.6 0.0 collective-permute-done.15.refs_1_
  63.6 0.0 copy-done.3
  63.6 0.7 %seeds.1 = bf16[64,512]{1,0:T(8,128)(2,1)} custom-call(f32[1,512]{1,0:T(1,128)S(1)} %bitcast.20, bf16[72,512]{1,0:T(8,128)(2,1)S(1)} %collective-permute-done.15.refs_1_, bf16[64,512]{1,0:T(8,128)(2,1)S(1)} %get-tuple-element.50.refs_2_, bf16[64,512]{1,0:T(8,128)(2,1)S(1)} %collective-permute-done.16.refs_3_, ...), custom_call_target="tpu_custom_call" | custom-call | flops 1100000000 | tf_op jit(solution)/shard_map/seeds/pallas_call | solution.py:348
  (5 shorter events, 0.1 us)
Async XLA Ops:
  2.9 17.6 %collective-permute-start = (bf16[192,512]{1,0:T(8,128)(2,1)S(1)}, bf16[192,512]{1,0:T(8,128)(2,1)S(1)}, u32[]{:S(2)}, u32[]{:S(2)}) collective-permute-start(bf16[192,512]{1,0:T(8,128)(2,1)S(1)} %get-tuple-element.29), channel_id=1, source_target_pairs={{0,2},{2,0},{4,6},{6,4},{8,10},{10,8},{12,14},{14,12},{1,3},{3,1},... | collective-permute-start | bytes 589832 | tf_op jit(solution)/shard_map/ppermute | solution.py:314
  5.9 14.6 %collective-permute-start.1 = (bf16[192,512]{1,0:T(8,128)(2,1)S(1)}, bf16[192,512]{1,0:T(8,128)(2,1)S(1)}, u32[]{:S(2)}, u32[]{:S(2)}) collective-permute-start(bf16[192,512]{1,0:T(8,128)(2,1)S(1)} %get-tuple-element.30), channel_id=1, source_target_pairs={{0,4},{2,6},{4,0},{6,2},{8,12},{10,14},{12,8},{14,10},{1,5},{3,7},... | collective-permute-start | bytes 589832 | tf_op jit(solution)/shard_map/ppermute | solution.py:314
  7.5 13.0 %collective-permute-start.2 = (bf16[192,512]{1,0:T(8,128)(2,1)S(1)}, bf16[192,512]{1,0:T(8,128)(2,1)S(1)}, u32[]{:S(2)}, u32[]{:S(2)}) collective-permute-start(bf16[192,512]{1,0:T(8,128)(2,1)S(1)} %get-tuple-element.31), channel_id=1, source_target_pairs={{0,6},{2,4},{4,2},{6,0},{8,14},{10,12},{12,10},{14,8},{1,7},{3,5},... | collective-permute-start | bytes 589832 | tf_op jit(solution)/shard_map/ppermute | solution.py:314
  20.5 8.5 %copy-start.2 = (f32[512]{0:T(512)S(1)}, f32[512]{0:T(512)}, u32[]{:S(2)}) copy-start(f32[512]{0:T(512)} %param.18) | copy-start | bytes 6148
  20.6 8.5 %collective-permute-start.6 = (bf16[4,96,512]{2,1,0:T(8,128)(2,1)S(1)}, bf16[4,96,512]{2,1,0:T(8,128)(2,1)S(1)}, u32[]{:S(2)}, u32[]{:S(2)}) collective-permute-start(bf16[4,96,512]{2,1,0:T(8,128)(2,1)S(1)} %get-tuple-element.36), channel_id=1, source_target_pairs={{0,1},{1,0},{2,3},{3,2},{4,5},{5,4},{6,7},{7,6},{8,9},{9,8},{10,11... | collective-permute-start | bytes 1179656 | tf_op jit(solution)/shard_map/ppermute | solution.py:314
  20.6 6.7 %collective-permute-start.3 = (bf16[144,128]{1,0:T(8,128)(2,1)S(1)}, bf16[144,128]{1,0:T(8,128)(2,1)S(1)}, u32[]{:S(2)}, u32[]{:S(2)}) collective-permute-start(bf16[144,128]{1,0:T(8,128)(2,1)S(1)} %get-tuple-element.33), channel_id=1, source_target_pairs={{0,2},{2,0},{4,6},{6,4},{8,10},{10,8},{12,14},{14,12},{1,3},{3,1},... | collective-permute-start | bytes 110600 | tf_op jit(solution)/shard_map/ppermute | solution.py:314
  22.6 4.7 %collective-permute-start.4 = (bf16[144,128]{1,0:T(8,128)(2,1)S(1)}, bf16[144,128]{1,0:T(8,128)(2,1)S(1)}, u32[]{:S(2)}, u32[]{:S(2)}) collective-permute-start(bf16[144,128]{1,0:T(8,128)(2,1)S(1)} %get-tuple-element.34), channel_id=1, source_target_pairs={{0,4},{2,6},{4,0},{6,2},{8,12},{10,14},{12,8},{14,10},{1,5},{3,7},... | collective-permute-start | bytes 110600 | tf_op jit(solution)/shard_map/ppermute | solution.py:314
  24.2 4.9 %collective-permute-start.5 = (bf16[144,128]{1,0:T(8,128)(2,1)S(1)}, bf16[144,128]{1,0:T(8,128)(2,1)S(1)}, u32[]{:S(2)}, u32[]{:S(2)}) collective-permute-start(bf16[144,128]{1,0:T(8,128)(2,1)S(1)} %get-tuple-element.35), channel_id=1, source_target_pairs={{0,6},{2,4},{4,2},{6,0},{8,14},{10,12},{12,10},{14,8},{1,7},{3,5},... | collective-permute-start | bytes 110600 | tf_op jit(solution)/shard_map/ppermute | solution.py:314
  29.9 15.6 %copy-start = (bf16[512,512]{1,0:T(8,128)(2,1)S(1)}, bf16[512,512]{1,0:T(8,128)(2,1)}, u32[]{:S(2)}) copy-start(bf16[512,512]{1,0:T(8,128)(2,1)} %refs_3_.5) | copy-start | bytes 1572868
  29.9 15.6 %copy-start.1 = (bf16[512,512]{1,0:T(8,128)(2,1)S(1)}, bf16[512,512]{1,0:T(8,128)(2,1)}, u32[]{:S(2)}) copy-start(bf16[512,512]{1,0:T(8,128)(2,1)} %refs_4_.3) | copy-start | bytes 1572868
  29.9 14.5 %collective-permute-start.10 = (bf16[208,512]{1,0:T(8,128)(2,1)S(1)}, bf16[208,512]{1,0:T(8,128)(2,1)S(1)}, u32[]{:S(2)}, u32[]{:S(2)}) collective-permute-start(bf16[208,512]{1,0:T(8,128)(2,1)S(1)} %get-tuple-element.37.refs_5_), channel_id=1, source_target_pairs={{0,8},{2,10},{4,12},{6,14},{8,0},{10,2},{12,4},{14,6},{1,9},{3,11}... | collective-permute-start | bytes 638984 | tf_op jit(solution)/shard_map/ppermute | solution.py:314
  37.4 4.0 %collective-permute-start.7 = (bf16[144,128]{1,0:T(8,128)(2,1)S(1)}, bf16[144,128]{1,0:T(8,128)(2,1)S(1)}, u32[]{:S(2)}, u32[]{:S(2)}) collective-permute-start(bf16[144,128]{1,0:T(8,128)(2,1)S(1)} %get-tuple-element.55), channel_id=1, source_target_pairs={{0,2},{2,0},{4,6},{6,4},{8,10},{10,8},{12,14},{14,12},{1,3},{3,1},... | collective-permute-start | bytes 110600 | tf_op jit(solution)/shard_map/ppermute | solution.py:314
  38.7 4.0 %collective-permute-start.8 = (bf16[144,128]{1,0:T(8,128)(2,1)S(1)}, bf16[144,128]{1,0:T(8,128)(2,1)S(1)}, u32[]{:S(2)}, u32[]{:S(2)}) collective-permute-start(bf16[144,128]{1,0:T(8,128)(2,1)S(1)} %get-tuple-element.54), channel_id=1, source_target_pairs={{0,4},{2,6},{4,0},{6,2},{8,12},{10,14},{12,8},{14,10},{1,5},{3,7},... | collective-permute-start | bytes 110600 | tf_op jit(solution)/shard_map/ppermute | solution.py:314
  39.6 4.9 %collective-permute-start.9 = (bf16[144,128]{1,0:T(8,128)(2,1)S(1)}, bf16[144,128]{1,0:T(8,128)(2,1)S(1)}, u32[]{:S(2)}, u32[]{:S(2)}) collective-permute-start(bf16[144,128]{1,0:T(8,128)(2,1)S(1)} %get-tuple-element.38), channel_id=1, source_target_pairs={{0,6},{2,4},{4,2},{6,0},{8,14},{10,12},{12,10},{14,8},{1,7},{3,5},... | collective-permute-start | bytes 110600 | tf_op jit(solution)/shard_map/ppermute | solution.py:314
  45.5 1.4 %collective-permute-start.11 = (bf16[192,512]{1,0:T(8,128)(2,1)S(1)}, bf16[192,512]{1,0:T(8,128)(2,1)S(1)}, u32[]{:S(2)}, u32[]{:S(2)}) collective-permute-start(bf16[192,512]{1,0:T(8,128)(2,1)S(1)} %get-tuple-element.42.refs_1_), channel_id=1, source_target_pairs={{0,1},{1,0},{2,3},{3,2},{4,5},{5,4},{6,7},{7,6},{8,9},{9,8},{10,11... | collective-permute-start | bytes 589832 | tf_op jit(solution)/shard_map/ppermute | solution.py:314
  46.3 17.3 %copy-start.3 = (f32[512]{0:T(512)S(1)}, f32[512]{0:T(512)}, u32[]{:S(2)}) copy-start(f32[512]{0:T(512)} %param.21) | copy-start | bytes 6148
  47.5 4.3 %collective-permute-start.12 = (bf16[64,512]{1,0:T(8,128)(2,1)S(1)}, bf16[64,512]{1,0:T(8,128)(2,1)S(1)}, u32[]{:S(2)}, u32[]{:S(2)}) collective-permute-start(bf16[64,512]{1,0:T(8,128)(2,1)S(1)} %get-tuple-element.46), channel_id=1, source_target_pairs={{0,2},{2,0},{4,6},{6,4},{8,10},{10,8},{12,14},{14,12},{1,3},{3,1},... | collective-permute-start | bytes 196616 | tf_op jit(solution)/shard_map/ppermute | solution.py:314
  48.5 4.7 %collective-permute-start.13 = (bf16[64,512]{1,0:T(8,128)(2,1)S(1)}, bf16[64,512]{1,0:T(8,128)(2,1)S(1)}, u32[]{:S(2)}, u32[]{:S(2)}) collective-permute-start(bf16[64,512]{1,0:T(8,128)(2,1)S(1)} %get-tuple-element.47), channel_id=1, source_target_pairs={{0,4},{2,6},{4,0},{6,2},{8,12},{10,14},{12,8},{14,10},{1,5},{3,7},... | collective-permute-start | bytes 196616 | tf_op jit(solution)/shard_map/ppermute | solution.py:314
  49.5 5.2 %collective-permute-start.14 = (bf16[64,512]{1,0:T(8,128)(2,1)S(1)}, bf16[64,512]{1,0:T(8,128)(2,1)S(1)}, u32[]{:S(2)}, u32[]{:S(2)}) collective-permute-start(bf16[64,512]{1,0:T(8,128)(2,1)S(1)} %get-tuple-element.48), channel_id=1, source_target_pairs={{0,6},{2,4},{4,2},{6,0},{8,14},{10,12},{12,10},{14,8},{1,7},{3,5},... | collective-permute-start | bytes 196616 | tf_op jit(solution)/shard_map/ppermute | solution.py:314
  54.7 8.9 %collective-permute-start.15 = (bf16[72,512]{1,0:T(8,128)(2,1)S(1)}, bf16[72,512]{1,0:T(8,128)(2,1)S(1)}, u32[]{:S(2)}, u32[]{:S(2)}) collective-permute-start(bf16[72,512]{1,0:T(8,128)(2,1)S(1)} %side_sum.1.refs_2_), channel_id=1, source_target_pairs={{0,8},{2,10},{4,12},{6,14},{8,0},{10,2},{12,4},{14,6},{1,9},{3,11}... | collective-permute-start | bytes 221192 | tf_op jit(solution)/shard_map/ppermute | solution.py:314
  56.4 4.8 %collective-permute-start.16 = (bf16[64,512]{1,0:T(8,128)(2,1)S(1)}, bf16[64,512]{1,0:T(8,128)(2,1)S(1)}, u32[]{:S(2)}, u32[]{:S(2)}) collective-permute-start(bf16[64,512]{1,0:T(8,128)(2,1)S(1)} %get-tuple-element.51), channel_id=1, source_target_pairs={{0,2},{2,0},{4,6},{6,4},{8,10},{10,8},{12,14},{14,12},{1,3},{3,1},... | collective-permute-start | bytes 196616 | tf_op jit(solution)/shard_map/ppermute | solution.py:314
  58.1 4.3 %collective-permute-start.17 = (bf16[64,512]{1,0:T(8,128)(2,1)S(1)}, bf16[64,512]{1,0:T(8,128)(2,1)S(1)}, u32[]{:S(2)}, u32[]{:S(2)}) collective-permute-start(bf16[64,512]{1,0:T(8,128)(2,1)S(1)} %get-tuple-element.52), channel_id=1, source_target_pairs={{0,4},{2,6},{4,0},{6,2},{8,12},{10,14},{12,8},{14,10},{1,5},{3,7},... | collective-permute-start | bytes 196616 | tf_op jit(solution)/shard_map/ppermute | solution.py:314
  58.4 5.2 %collective-permute-start.18 = (bf16[64,512]{1,0:T(8,128)(2,1)S(1)}, bf16[64,512]{1,0:T(8,128)(2,1)S(1)}, u32[]{:S(2)}, u32[]{:S(2)}) collective-permute-start(bf16[64,512]{1,0:T(8,128)(2,1)S(1)} %get-tuple-element.53), channel_id=1, source_target_pairs={{0,6},{2,4},{4,2},{6,0},{8,14},{10,12},{12,10},{14,8},{1,7},{3,5},... | collective-permute-start | bytes 196616 | tf_op jit(solution)/shard_map/ppermute | solution.py:314

commit v8 on v6

--- a/solution.py
+++ b/solution.py
@@ -23,11 +23,13 @@
     nbr_hbm,
     w_self_hbm,
     w_nbr_hbm,
+    pick_hbm,
+    live_ref,
     *refs,
 ):
     half = n_feat // 2
-    parcel_refs = refs[:half]
-    src_ref, seed_ref, nbr_ref, w_self_ref, w_nbr_ref, sems = refs[half:]
+    parcel_refs, pick_ref = refs[:half], refs[half]
+    src_ref, seed_ref, nbr_ref, w_self_ref, w_nbr_ref, sems = refs[half + 1 :]
     fslice = w_self_ref.shape[0]
     copies = [
         pltpu.make_async_copy(a, b, sems.at[i])
@@ -38,6 +40,7 @@
                 (nbr_hbm, nbr_ref),
                 (w_self_hbm, w_self_ref),
                 (w_nbr_hbm, w_nbr_ref),
+                (pick_hbm, pick_ref),
             )
         )
     ]
@@ -52,7 +55,9 @@
     digits = jnp.concatenate([high, idx - high * 128], axis=1).astype(jnp.float32)
     digits = digits.astype(jnp.bfloat16)
     weight = jnp.where(first_core, w_self_ref[...], w_nbr_ref[...])
-    for s, parcel_ref in enumerate(parcel_refs):
+    live = jnp.full((8, LANES), live_ref[0, 0].astype(jnp.float32)).astype(jnp.bfloat16)
+    tags = jnp.concatenate([digits, live], axis=0)
+    for s, parcel_ref in enumerate(reversed(parcel_refs)):
         parcel_ref[:fslice, :] = weight
         for place, step in enumerate((s, s ^ half)):
             at = pl.multiple_of(jnp.bitwise_xor(feat_pos, step) * (2 * pcap), LANES)
@@ -62,7 +67,7 @@
                 near_side = own
         both = jnp.concatenate([near_side, own], axis=1)
         parcel_ref[fslice:, : 2 * pcap] = both.astype(jnp.bfloat16)
-        parcel_ref[fslice : fslice + idx.shape[0], 2 * pcap :] = digits
+        parcel_ref[fslice : fslice + tags.shape[0], 2 * pcap :] = tags
 
 
 def turn_kernel(src_hbm, table_ref, src_ref, sems):
@@ -83,28 +88,37 @@
 
         def turn(step, carry):
             at = pl.multiple_of(i * piece + step * width, width)
-            block = src_ref[:, pl.ds(at, width)].astype(jnp.float32)
-            table_ref[pl.ds(at, width), :fslice] = block.T
+            table_ref[pl.ds(at, width), :fslice] = src_ref[:, pl.ds(at, width)].T.astype(
+                jnp.float32
+            )
             return carry
 
         lax.fori_loop(0, piece // width, turn, 0)
 
 
-def mean_kernel(
-    base, count, fanout, pcap, fslice, nbr_hbm, table_ref, out_ref, total, nbr_ref, sems
-):
+def live_rows(parcel_ref, row, lane):
+    return jnp.max(parcel_ref[row : row + 8, lane:].astype(jnp.float32)).astype(jnp.int32)
+
+
+def mean_kernel(chosen, fanout, pcap, fslice, n_idx, nbr_hbm, table_ref, *refs):
+    parcel_refs, (out_ref, total, nbr_ref, live_ref, sems) = refs[:-5], refs[-5:]
     feat_pos = lax.axis_index("feat")
+    count = len(chosen)
     stride = nbr_ref.shape[0] // count
     copies = [
         pltpu.make_async_copy(
-            nbr_hbm.at[pl.ds(pl.multiple_of((feat_pos ^ (base + i)) * stride, stride), stride)],
+            nbr_hbm.at[pl.ds(pl.multiple_of((feat_pos ^ step) * stride, stride), stride)],
             nbr_ref.at[pl.ds(i * stride, stride)],
             sems.at[i],
         )
-        for i in range(count)
+        for i, step in enumerate(chosen)
     ]
     for copy in copies:
         copy.start()
+    for i in range(count):
+        live_ref[i] = pcap
+    for i, ref in enumerate(parcel_refs):
+        live_ref[i] = live_rows(ref, fslice + n_idx, 2 * pcap)
     for copy in copies:
         copy.wait()
 
@@ -112,8 +126,8 @@
         first = i * stride
 
         def group(g, inner):
-            at = pl.multiple_of(g * 8, 8)
-            for u in range(8):
+            at = pl.multiple_of(g * 16, 16)
+            for u in range(16):
                 rows = [table_ref[nbr_ref[first + k * pcap + at + u]] for k in range(fanout)]
                 while len(rows) > 1:
                     rows = [a + b for a, b in zip(rows[::2], rows[1::2])] + (
@@ -122,7 +136,7 @@
                 total[pl.ds(at + u, 1), :] = rows[0]
             return inner
 
-        lax.fori_loop(0, pcap // 8, group, 0)
+        lax.fori_loop(0, lax.div(live_ref[i] + 15, 16), group, 0)
         mean = total[...] / fanout
         if folds(fslice, pcap):
             part = pcap // 4
@@ -156,16 +170,22 @@
     return jnp.concatenate([wide, tail], axis=0)[:, :fslice].astype(jnp.bfloat16)
 
 
-def halves_kernel(*refs):
-    out_ref = refs[-1]
-    for s, ref in enumerate(refs[:-1]):
-        out_ref[s] = ref[: out_ref.shape[1], :]
+def halves_kernel(half, *refs):
+    parcel_refs, chunks_ref, out_ref, chunk_refs = (
+        refs[:half],
+        refs[half],
+        refs[half + 1],
+        refs[half + 2 :],
+    )
+    for s in range(half):
+        out_ref[s] = parcel_refs[s][: out_ref.shape[1], :]
+        chunk_refs[s][...] = chunks_ref[s]
 
 
 def prepare_kernel(half, n_idx, *refs):
     parcel_refs, mean_refs = refs[:half], refs[half : 2 * half]
-    other_ref, bias_ref, last_ref, w_ref, pre_ref, cross_ref, moved_ref = refs[2 * half :]
-    moved_ref[...] = last_ref[0]
+    other_ref, bias_ref, first_ref, w_ref, pre_ref, cross_ref, moved_ref = refs[2 * half :]
+    moved_ref[...] = first_ref[0]
     fslice = w_ref.shape[1]
     pcap, width = pre_ref.shape
     first_core = lax.axis_index("rep") == 0
@@ -242,7 +262,7 @@
     ).astype(jnp.bfloat16)
 
 
-def layer_kernel(half, count_ref, *refs):
+def layer_kernel(half, n_idx, parcel_ref, *refs):
     mean_refs = refs[:half]
     pre_ref, w_ref, cross_ref, hidden_ref, result_ref = refs[half:]
     pcap, width = hidden_ref.shape
@@ -252,7 +272,8 @@
         pre = pre + jnp.dot(
             unfold(mean_refs[s][...], fslice, pcap), w_ref[s], preferred_element_type=jnp.float32
         )
-    live = lax.broadcasted_iota(jnp.int32, (pcap, width), 0) < count_ref[0, 0]
+    count = live_rows(parcel_ref, fslice + n_idx, 2 * pcap)
+    live = lax.broadcasted_iota(jnp.int32, (pcap, width), 0) < count
     hidden = jnp.where(live, jnp.maximum(pre, 0.0), 0.0).astype(jnp.bfloat16)
     hidden_ref[...] = hidden
     result_ref[...] = hidden
@@ -307,6 +328,7 @@
 ):
     n_feat = lax.axis_size("feat")
     half = n_feat // 2
+    steps = range(half - 1, -1, -1)
     fslice, nodes = src_feats.shape
     fanout_one, pcap = nbr_one.shape[2:]
     width = w1_self.shape[1]
@@ -319,18 +341,13 @@
     anywhere = pl.BlockSpec(memory_space=pl.ANY)
     table_bytes = nodes * LANES * 4
 
-    def spaced(shape):
-        return shape if len(shape) == 3 else (*shape, jax.ShapeDtypeStruct)
-
     def call(kernel, name, shapes, ins, args, after=(), scratch=(), limit=16 * MIB, cost_us=1):
         def wrapped(*refs):
             kernel(*refs[: len(args)], *refs[len(args) + len(after) :])
 
         return pl.pallas_call(
             wrapped,
-            out_shape=tuple(
-                space(shape, dtype) for shape, dtype, space in map(spaced, shapes)
-            ),
+            out_shape=tuple(jax.ShapeDtypeStruct(shape, dtype) for shape, dtype in shapes),
             in_specs=[*ins, *([anywhere] * len(after))],
             out_specs=(vmem,) * len(shapes),
             scratch_shapes=scratch,
@@ -341,57 +358,63 @@
             name=name,
         )(*args, *after)
 
-    def pinned(value, space=pltpu.HBM):
-        return pltpu.with_memory_space_constraint(value, space)
+    def pinned(value):
+        return pltpu.with_memory_space_constraint(value, pltpu.HBM)
 
     def send(chunks):
-        return [chunk if s == 0 else swap(chunk, "feat", s) for s, chunk in enumerate(chunks)]
-
-    parcels = call(
+        return [swap(chunk, "feat", s) if s else chunk for s, chunk in zip(steps, chunks)]
+
+    picks = jnp.transpose(nbr_one, (0, 2, 1, 3))
+    *parcels, picks = call(
         functools.partial(pack_kernel, n_feat, pcap),
         "pack",
-        [((2 * fslice, width), bf16)] * half,
-        [hbm] * 5,
-        [pinned(x) for x in (src_feats, seed_rows[None], nbr_two.T, w1_self, w1_nbr)],
+        [((2 * fslice, width), bf16)] * half + [(picks.shape, jnp.int32)],
+        [hbm] * 6 + [smem],
+        [
+            *(pinned(x) for x in (src_feats, seed_rows[None], nbr_two.T, w1_self, w1_nbr, picks)),
+            counts,
+        ],
         scratch=[
             pltpu.VMEM((fslice, n_feat * 2 * pcap), bf16),
             pltpu.VMEM((1, seed_count), jnp.int32),
             pltpu.VMEM((fanout_two, seed_count), jnp.int32),
             pltpu.VMEM((fslice, width), bf16),
             pltpu.VMEM((fslice, width), bf16),
-            pltpu.SemaphoreType.DMA((5,)),
+            pltpu.SemaphoreType.DMA((6,)),
         ],
     )
+    stride = -(-fanout_one * pcap // 1024) * 1024
+    neighbors = jnp.pad(
+        picks.reshape(n_feat, fanout_one * pcap), ((0, 0), (0, stride - fanout_one * pcap))
+    ).reshape(-1)
     arrived = send(parcels)
     (table,) = call(
         turn_kernel,
         "turn",
-        [((nodes, LANES), jnp.float32, pltpu.VMEM)],
+        [((nodes, LANES), jnp.float32)],
         [hbm],
         (pinned(src_feats),),
-        after=(parcels[0],),
+        after=(parcels[-1], neighbors),
         scratch=[pltpu.VMEM((fslice, nodes), bf16), pltpu.SemaphoreType.DMA((6,))],
         limit=table_bytes + 12 * MIB,
         cost_us=3,
     )
     table = table.reshape(nodes, 1, LANES)
-    stride = -(-fanout_one * pcap // 1024) * 1024
-    neighbors = jnp.pad(
-        nbr_one.reshape(n_feat, fanout_one * pcap), ((0, 0), (0, stride - fanout_one * pcap))
-    ).reshape(-1)
     chunk_shape = (pcap // 4 * 3, LANES) if folds(fslice, pcap) else (pcap, fslice)
 
-    def means(base, count, after):
+    def means(chosen, parcels=(), after=()):
+        count = len(chosen)
         (chunks,) = call(
-            functools.partial(mean_kernel, base, count, fanout_one, pcap, fslice),
+            functools.partial(mean_kernel, tuple(chosen), fanout_one, pcap, fslice, n_idx),
             "mean",
             [((count, *chunk_shape), bf16)],
-            [anywhere, vmem],
-            (neighbors, pinned(table, pltpu.VMEM)),
+            [anywhere] + [vmem] * (1 + len(parcels)),
+            (neighbors, table, *parcels),
             after=after,
             scratch=[
                 pltpu.VMEM((pcap, LANES), jnp.float32),
                 pltpu.SMEM((count * stride,), jnp.int32),
+                pltpu.SMEM((count,), jnp.int32),
                 pltpu.SemaphoreType.DMA((count,)),
             ],
             limit=table_bytes + 8 * MIB,
@@ -399,21 +422,17 @@
         )
         return chunks
 
-    def split(chunks):
-        return [chunks[i] for i in range(chunks.shape[0])]
-
-    far_means = means(half, half, ())
-    far_arrived = send(split(far_means))
-    (halves,) = call(
-        halves_kernel,
+    far_means = means([s + half for s in steps])
+    halves, *far_chunks = call(
+        functools.partial(halves_kernel, half),
         "halves",
-        [((half, fslice, width), bf16)],
-        [vmem] * half,
-        arrived,
-        after=(far_means,),
-    )
+        [((half, fslice, width), bf16)] + [(chunk_shape, bf16)] * half,
+        [vmem] * (half + 1),
+        (*arrived, far_means),
+    )
+    far_arrived = send(far_chunks)
     other_halves = swap(halves, "rep", 1)
-    last_mean = means(half - 1, 1, (far_means,))
+    first_mean = means([1], arrived[-2:-1], (far_chunks[-1],))
     w_nbr, pre, cross, moved = call(
         functools.partial(prepare_kernel, half, n_idx),
         "prepare",
@@ -424,7 +443,7 @@
             (chunk_shape, bf16),
         ],
         [vmem] * (2 * half + 3),
-        (*arrived, *far_arrived, other_halves, bias_one[None], last_mean),
+        (*arrived, *far_arrived, other_halves, bias_one[None], first_mean),
     )
     cross_arrived = swap(cross, "feat", half)
     (near_times,) = call(
@@ -435,14 +454,17 @@
         arrived,
         after=(far_means,),
     )
-    near_means = means(0, half - 1, (cross, near_times))
-    near_arrived = send([*split(near_means), moved])
+    near_means = means(
+        [s for s in steps if s != 1], [*arrived[:-2], arrived[-1]], (cross, near_times)
+    )
+    near_means = [near_means[i] for i in range(half - 1)]
+    near_arrived = send([*near_means[:-1], moved, near_means[-1]])
     hidden, result = call(
-        functools.partial(layer_kernel, half),
+        functools.partial(layer_kernel, half, n_idx),
         "hidden",
         [((pcap, width), bf16)] * 2,
-        [smem] + [vmem] * (half + 3),
-        (counts, *near_arrived, pre, w_nbr, cross_arrived),
+        [vmem] * (half + 4),
+        (parcels[-1], *near_arrived, pre, w_nbr, cross_arrived),
     )
     other_hidden = swap(hidden, "rep", 1)
     far_times, value = call(

time: 69.3 us -> 59.5 us (0.86)
  local copies, waits for them, and re-layouts: 5.57 us -> 0.14 us
  Pallas kernels: 28.7 us -> 24.7 us
  waiting for transfers between devices: 11.2 us -> 9.56 us
  starting transfers between devices: 21.9 us -> 22.9 us
    unnamed x18 -> x10, local copies, waits for them, and re-layouts: 5.46 us -> 0.04 us
    pallas_call x13, Pallas kernels: 28.7 us -> 24.7 us  [call(): pl.pallas_call(wrapped, out_shape=tuple((jax.ShapeDtypeStruct(shape, dtyp...]
    ppermute x19, waiting for transfers between devices: 11.2 us -> 9.56 us  [swap(): return lax.ppermute(value, axis, [(i, i ^ step) for i in range(size)])]
    ppermute x19, starting transfers between devices: 21.9 us -> 22.9 us  [swap(): return lax.ppermute(value, axis, [(i, i ^ step) for i in range(size)])]
  transfers between devices with their start and end apart: 19 -> 19, of which waited for: 8 -> 10; matrix products, arithmetic and copies ran while one was open for 0% -> 1% of each run, Pallas kernels for 34% -> 33%
where the time goes in v8:
time: 59.5 us; the launch traced here: 58.9 us
  Pallas kernels  24.7 us (42%)
  starting transfers between devices  22.9 us (38%)
  waiting for transfers between devices  9.56 us (16%)
  between operations  1.46 us (2%)
    pallas_call x13, Pallas kernels, call(): pl.pallas_call(wrapped, out_shape=tuple((jax.ShapeDtypeStruct(shape, dtyp...  24.7 us
    ppermute x19, starting transfers between devices, swap(): return lax.ppermute(value, axis, [(i, i ^ step) for i in range(size)])  22.9 us
    ppermute x19, waiting for transfers between devices, swap(): return lax.ppermute(value, axis, [(i, i ^ step) for i in range(size)])  9.56 us
  transfers between devices with their start and end apart: 19, of which 10 were waited for; matrix products, arithmetic and copies ran while one was open for 1% of the time, Pallas kernels for 33%

profile of v8, /device:TPU:0, one launch (start us, length us, event | category | flops | bytes accessed | tf_op | source)
XLA Modules:
  0.0 58.9 jit_solution(6140878506073569562)
XLA Ops:
  1.3 1.6 %pack.1 = (bf16[192,512]{1,0:T(8,128)(2,1)S(1)}, bf16[192,512]{1,0:T(8,128)(2,1)S(1)}, bf16[192,512]{1,0:T(8,128)(2,1)S(1)}, bf16[192,512]{1,0:T(8,128)(2,1)S(1)}, s32[8,10,1,192]{3,2,1,0:T(1,128)S(1)}) custom-call(bf16[96,12288]{1,0:T(8,128)(2,1)} %refs_0_.3, s32[1,64]{1,0:T(1,128)} %bitcast.27, s32[15,64]{1,0:T(8,128)} %bitcast.26, ...), custom_call_target="tpu_custom_call" | custom-call | flops 1100000000 | tf_op jit(solution)/shard_map/pack/pallas_call | solution.py:348
  2.9 4.0 %collective-permute-start = (bf16[192,512]{1,0:T(8,128)(2,1)S(1)}, bf16[192,512]{1,0:T(8,128)(2,1)S(1)}, u32[]{:S(2)}, u32[]{:S(2)}) collective-permute-start(bf16[192,512]{1,0:T(8,128)(2,1)S(1)} %get-tuple-element.30), channel_id=1, source_target_pairs={{0,6},{2,4},{4,2},{6,0},{8,14},{10,12},{12,10},{14,8},{1,7},{3,5},... | collective-permute-start | bytes 589832 | tf_op jit(solution)/shard_map/ppermute | solution.py:313
  6.9 0.4 collective-permute-start.1
  7.4 0.2 collective-permute-start.2
  7.6 0.2 reduce
  7.8 0.1 reshape.13
  7.9 3.2 %turn.1 = f32[12288,128]{1,0:T(8,128)S(1)} custom-call(bf16[96,12288]{1,0:T(8,128)(2,1)} %refs_0_.3, bf16[192,512]{1,0:T(8,128)(2,1)S(1)} %get-tuple-element.28.refs_1_.refs_3_.refs_4_.refs_0_, s32[16384]{0:T(1024)S(1)} %bitcast.16), custom_call_target="tpu_custom_call" | custom-call | flops 3300000000 | tf_op jit(solution)/shard_map/turn/pallas_call | solution.py:348
  11.1 8.5 %mean.3.refs_4_ = bf16[4,144,128]{2,1,0:T(8,128)(2,1)S(1)} custom-call(s32[16384]{0:T(1024)S(1)} %bitcast.17, f32[12288,1,128]{2,1,0:T(1,128)S(1)} %bitcast.22), custom_call_target="tpu_custom_call" | custom-call | flops 8800000000 | tf_op jit(solution)/shard_map/mean/pallas_call | solution.py:348
  19.7 0.0 collective-permute-done.refs_0_.refs_2_
  19.7 0.0 collective-permute-done.1.refs_1_.refs_3_
  19.7 0.0 collective-permute-done.2.refs_2_
  19.8 0.0 copy-start.2
  19.8 0.1 collective-permute-start.6
  19.8 2.9 %collective-permute-start.3 = (bf16[144,128]{1,0:T(8,128)(2,1)S(1)}, bf16[144,128]{1,0:T(8,128)(2,1)S(1)}, u32[]{:S(2)}, u32[]{:S(2)}) collective-permute-start(bf16[144,128]{1,0:T(8,128)(2,1)S(1)} %get-tuple-element.33), channel_id=1, source_target_pairs={{0,6},{2,4},{4,2},{6,0},{8,14},{10,12},{12,10},{14,8},{1,7},{3,5},... | collective-permute-start | bytes 110600 | tf_op jit(solution)/shard_map/ppermute | solution.py:313
  22.8 0.4 collective-permute-start.4
  23.2 0.2 collective-permute-start.5
  23.4 2.4 %mean.4.refs_10_ = bf16[1,144,128]{2,1,0:T(8,128)(2,1)S(1)} custom-call(s32[16384]{0:T(1024)S(1)} %bitcast.18, f32[12288,1,128]{2,1,0:T(1,128)S(1)} %bitcast.23, bf16[192,512]{1,0:T(8,128)(2,1)S(1)} %collective-permute-done.2.refs_2_, bf16[144,128]{1,0:T(8,128)(2,1)S(1)} %get-tuple-element.36.refs_3_.refs_7_), custom_call_target="tpu_custom_call" | custom-call | flops 2200000000 | tf_op jit(solution)/shard_map/mean/pallas_call | solution.py:348
  25.8 0.8 %near_times.1.refs_6_.refs_0_ = bf16[256,768]{1,0:T(8,128)(2,1)S(1)} custom-call(bf16[192,512]{1,0:T(8,128)(2,1)S(1)} %collective-permute-done.refs_0_.refs_2_, bf16[192,512]{1,0:T(8,128)(2,1)S(1)} %collective-permute-done.1.refs_1_.refs_3_, bf16[192,512]{1,0:T(8,128)(2,1)S(1)} %collective-permute-done.2.refs_2_, ...), custom_call_target="tpu_custom_call" | custom-call | flops 1100000000 | tf_op jit(solution)/shard_map/near_times/pallas_call | solution.py:348
  26.5 0.0 collective-permute-done.3.refs_4_
  26.6 0.2 collective-permute-done.4.refs_5_
  26.7 0.4 collective-permute-done.5.refs_6_
  27.2 0.0 collective-permute-done.6.refs_8_
  27.2 0.0 copy-done.2
  27.2 0.8 %prepare.1 = (bf16[4,96,512]{2,1,0:T(8,128)(2,1)S(1)}, f32[192,512]{1,0:T(8,128)S(1)}, bf16[208,512]{1,0:T(8,128)(2,1)S(1)}, bf16[144,128]{1,0:T(8,128)(2,1)S(1)}) custom-call(bf16[192,512]{1,0:T(8,128)(2,1)S(1)} %collective-permute-done.refs_0_.refs_2_, bf16[192,512]{1,0:T(8,128)(2,1)S(1)} %collective-permute-done.1.refs_1_.refs_3_, ...), custom_call_target="tpu_custom_call" | custom-call | flops 1100000000 | tf_op jit(solution)/shard_map/prepare/pallas_call | solution.py:348
  28.0 0.0 copy-start
  28.0 0.0 copy-start.1
  28.0 2.6 %collective-permute-start.10 = (bf16[208,512]{1,0:T(8,128)(2,1)S(1)}, bf16[208,512]{1,0:T(8,128)(2,1)S(1)}, u32[]{:S(2)}, u32[]{:S(2)}) collective-permute-start(bf16[208,512]{1,0:T(8,128)(2,1)S(1)} %get-tuple-element.38.refs_5_), channel_id=1, source_target_pairs={{0,8},{2,10},{4,12},{6,14},{8,0},{10,2},{12,4},{14,6},{1,9},{3,11}... | collective-permute-start | bytes 638984 | tf_op jit(solution)/shard_map/ppermute | solution.py:313
  30.7 3.9 %mean.5 = bf16[3,144,128]{2,1,0:T(8,128)(2,1)S(1)} custom-call(s32[16384]{0:T(1024)S(1)} %bitcast.19, f32[12288,1,128]{2,1,0:T(1,128)S(1)} %bitcast.24, bf16[192,512]{1,0:T(8,128)(2,1)S(1)} %collective-permute-done.refs_0_.refs_2_, bf16[192,512]{1,0:T(8,128)(2,1)S(1)} %collective-permute-done.1.refs_1_.refs_3_, ...), custom_call_target="tpu_custom_call" | custom-call | flops 6600000000 | tf_op jit(solution)/shard_map/mean/pallas_call | solution.py:348
  34.6 3.0 %collective-permute-start.7 = (bf16[144,128]{1,0:T(8,128)(2,1)S(1)}, bf16[144,128]{1,0:T(8,128)(2,1)S(1)}, u32[]{:S(2)}, u32[]{:S(2)}) collective-permute-start(bf16[144,128]{1,0:T(8,128)(2,1)S(1)} %get-tuple-element.56), channel_id=1, source_target_pairs={{0,6},{2,4},{4,2},{6,0},{8,14},{10,12},{12,10},{14,8},{1,7},{3,5},... | collective-permute-start | bytes 110600 | tf_op jit(solution)/shard_map/ppermute | solution.py:313
  37.6 0.3 collective-permute-start.8
  37.9 0.6 collective-permute-start.9
  38.4 3.4 %collective-permute-done.7.refs_1_ = bf16[144,128]{1,0:T(8,128)(2,1)S(1)} collective-permute-done((bf16[144,128]{1,0:T(8,128)(2,1)S(1)}, bf16[144,128]{1,0:T(8,128)(2,1)S(1)}, u32[]{:S(2)}, u32[]{:S(2)}) %collective-permute-start.7) | collective-permute-done | bytes 36896 | tf_op jit(solution)/shard_map/ppermute | solution.py:313
  41.9 0.0 collective-permute-done.8.refs_2_
  41.9 0.3 collective-permute-done.9.refs_3_
  42.2 0.0 collective-permute-done.10.refs_7_.refs_0_
  42.2 1.1 %hidden.1 = (bf16[192,512]{1,0:T(8,128)(2,1)S(1)}, bf16[192,512]{1,0:T(8,128)(2,1)}) custom-call(bf16[192,512]{1,0:T(8,128)(2,1)S(1)} %get-tuple-element.28.refs_1_.refs_3_.refs_4_.refs_0_, bf16[144,128]{1,0:T(8,128)(2,1)S(1)} %collective-permute-done.7.refs_1_, bf16[144,128]{1,0:T(8,128)(2,1)S(1)} %collective-permute-done.8.refs_2_, ...), custom_call_target="tpu_custom_call" | custom-call | flops 1100000000 | tf_op jit(solution)/shard_map/hidden/pallas_call | solution.py:348
  43.2 0.0 copy-start.3
  43.2 0.0 collective-permute-start.11
  43.2 0.0 copy-done
  43.2 0.0 copy-done.1
  43.2 0.8 %far_times.1 = (bf16[256,768]{1,0:T(8,128)(2,1)S(1)}, bf16[2,192,512]{2,1,0:T(8,128)(2,1)S(1)}) custom-call(bf16[208,512]{1,0:T(8,128)(2,1)S(1)} %collective-permute-done.10.refs_7_.refs_0_, bf16[192,512]{1,0:T(8,128)(2,1)S(1)} %get-tuple-element.43.refs_1_, bf16[512,512]{1,0:T(8,128)(2,1)S(1)} %copy-done, bf16[512,512]{1,0:T(8,128)(2,1)S(1)} %copy-done.1), custom_call_target="tpu_custom_call" | custom-call | flops 1100000000 | tf_op jit(solution)/shard_map/far_times/pallas_call | solution.py:348
  44.1 0.6 collective-permute-done.11.refs_3_
  44.7 0.8 %share.1 = (bf16[64,512]{1,0:T(8,128)(2,1)S(1)}, bf16[64,512]{1,0:T(8,128)(2,1)S(1)}, bf16[64,512]{1,0:T(8,128)(2,1)S(1)}, bf16[64,512]{1,0:T(8,128)(2,1)S(1)}, ...) custom-call(bf16[256,768]{1,0:T(8,128)(2,1)S(1)} %near_times.1.refs_, ...), custom_call_target="tpu_custom_call" | custom-call | flops 1100000000 | tf_op jit(solution)/shard_map/share/pallas_call | solution.py:348
  45.5 1.8 %collective-permute-start.15 = (bf16[64,512]{1,0:T(8,128)(2,1)S(1)}, bf16[64,512]{1,0:T(8,128)(2,1)S(1)}, u32[]{:S(2)}, u32[]{:S(2)}) collective-permute-start(bf16[64,512]{1,0:T(8,128)(2,1)S(1)} %get-tuple-element.50), channel_id=1, source_target_pairs={{0,6},{2,4},{4,2},{6,0},{8,14},{10,12},{12,10},{14,8},{1,7},{3,5},... | collective-permute-start | bytes 196616 | tf_op jit(solution)/shard_map/ppermute | solution.py:313
  47.2 0.7 %collective-permute-start.16 = (bf16[64,512]{1,0:T(8,128)(2,1)S(1)}, bf16[64,512]{1,0:T(8,128)(2,1)S(1)}, u32[]{:S(2)}, u32[]{:S(2)}) collective-permute-start(bf16[64,512]{1,0:T(8,128)(2,1)S(1)} %get-tuple-element.51), channel_id=1, source_target_pairs={{0,4},{2,6},{4,0},{6,2},{8,12},{10,14},{12,8},{14,10},{1,5},{3,7},... | collective-permute-start | bytes 196616 | tf_op jit(solution)/shard_map/ppermute | solution.py:313
  47.9 1.1 %collective-permute-start.17 = (bf16[64,512]{1,0:T(8,128)(2,1)S(1)}, bf16[64,512]{1,0:T(8,128)(2,1)S(1)}, u32[]{:S(2)}, u32[]{:S(2)}) collective-permute-start(bf16[64,512]{1,0:T(8,128)(2,1)S(1)} %get-tuple-element.52), channel_id=1, source_target_pairs={{0,2},{2,0},{4,6},{6,4},{8,10},{10,8},{12,14},{14,12},{1,3},{3,1},... | collective-permute-start | bytes 196616 | tf_op jit(solution)/shard_map/ppermute | solution.py:313
  49.0 1.7 %collective-permute-start.12 = (bf16[64,512]{1,0:T(8,128)(2,1)S(1)}, bf16[64,512]{1,0:T(8,128)(2,1)S(1)}, u32[]{:S(2)}, u32[]{:S(2)}) collective-permute-start(bf16[64,512]{1,0:T(8,128)(2,1)S(1)} %get-tuple-element.46), channel_id=1, source_target_pairs={{0,6},{2,4},{4,2},{6,0},{8,14},{10,12},{12,10},{14,8},{1,7},{3,5},... | collective-permute-start | bytes 196616 | tf_op jit(solution)/shard_map/ppermute | solution.py:313
  50.7 0.7 %collective-permute-start.13 = (bf16[64,512]{1,0:T(8,128)(2,1)S(1)}, bf16[64,512]{1,0:T(8,128)(2,1)S(1)}, u32[]{:S(2)}, u32[]{:S(2)}) collective-permute-start(bf16[64,512]{1,0:T(8,128)(2,1)S(1)} %get-tuple-element.47), channel_id=1, source_target_pairs={{0,4},{2,6},{4,0},{6,2},{8,12},{10,14},{12,8},{14,10},{1,5},{3,7},... | collective-permute-start | bytes 196616 | tf_op jit(solution)/shard_map/ppermute | solution.py:313
  51.4 0.0 collective-permute-done.15.refs_0_
  51.4 1.1 %collective-permute-start.14 = (bf16[64,512]{1,0:T(8,128)(2,1)S(1)}, bf16[64,512]{1,0:T(8,128)(2,1)S(1)}, u32[]{:S(2)}, u32[]{:S(2)}) collective-permute-start(bf16[64,512]{1,0:T(8,128)(2,1)S(1)} %get-tuple-element.48), channel_id=1, source_target_pairs={{0,2},{2,0},{4,6},{6,4},{8,10},{10,8},{12,14},{14,12},{1,3},{3,1},... | collective-permute-start | bytes 196616 | tf_op jit(solution)/shard_map/ppermute | solution.py:313
  52.5 0.0 collective-permute-done.16.refs_1_
  52.5 0.5 collective-permute-done.17.refs_2_
  53.0 1.1 %collective-permute-start.18 = (bf16[64,512]{1,0:T(8,128)(2,1)S(1)}, bf16[64,512]{1,0:T(8,128)(2,1)S(1)}, u32[]{:S(2)}, u32[]{:S(2)}) collective-permute-start(bf16[64,512]{1,0:T(8,128)(2,1)S(1)} %side_sum.1), channel_id=1, source_target_pairs={{0,8},{2,10},{4,12},{6,14},{8,0},{10,2},{12,4},{14,6},{1,9},{3,11}... | collective-permute-start | bytes 196616 | tf_op jit(solution)/shard_map/ppermute | solution.py:313
  54.1 0.2 collective-permute-done.12.refs_1_
  54.3 0.7 %collective-permute-done.13.refs_2_ = bf16[64,512]{1,0:T(8,128)(2,1)S(1)} collective-permute-done((bf16[64,512]{1,0:T(8,128)(2,1)S(1)}, bf16[64,512]{1,0:T(8,128)(2,1)S(1)}, u32[]{:S(2)}, u32[]{:S(2)}) %collective-permute-start.13) | collective-permute-done | bytes 65568 | tf_op jit(solution)/shard_map/ppermute | solution.py:313
  55.0 0.7 %collective-permute-done.14.refs_3_ = bf16[64,512]{1,0:T(8,128)(2,1)S(1)} collective-permute-done((bf16[64,512]{1,0:T(8,128)(2,1)S(1)}, bf16[64,512]{1,0:T(8,128)(2,1)S(1)}, u32[]{:S(2)}, u32[]{:S(2)}) %collective-permute-start.14) | collective-permute-done | bytes 65568 | tf_op jit(solution)/shard_map/ppermute | solution.py:313
  55.7 2.5 %collective-permute-done.18.refs_5_ = bf16[64,512]{1,0:T(8,128)(2,1)S(1)} collective-permute-done((bf16[64,512]{1,0:T(8,128)(2,1)S(1)}, bf16[64,512]{1,0:T(8,128)(2,1)S(1)}, u32[]{:S(2)}, u32[]{:S(2)}) %collective-permute-start.18) | collective-permute-done | bytes 65568 | tf_op jit(solution)/shard_map/ppermute | solution.py:313
  58.2 0.0 copy-done.3
  58.2 0.7 %seeds.1 = bf16[64,512]{1,0:T(8,128)(2,1)} custom-call(f32[1,512]{1,0:T(1,128)S(1)} %bitcast.21, bf16[64,512]{1,0:T(8,128)(2,1)S(1)} %collective-permute-done.12.refs_1_, bf16[64,512]{1,0:T(8,128)(2,1)S(1)} %collective-permute-done.13.refs_2_, bf16[64,512]{1,0:T(8,128)(2,1)S(1)} %collective-permute-done.14.refs_3_, ...), custom_call_target="tpu_custom_call" | custom-call | flops 1100000000 | tf_op jit(solution)/shard_map/seeds/pallas_call | solution.py:348
  (5 shorter events, 0.1 us)
Async XLA Ops:
  2.9 16.8 %collective-permute-start = (bf16[192,512]{1,0:T(8,128)(2,1)S(1)}, bf16[192,512]{1,0:T(8,128)(2,1)S(1)}, u32[]{:S(2)}, u32[]{:S(2)}) collective-permute-start(bf16[192,512]{1,0:T(8,128)(2,1)S(1)} %get-tuple-element.30), channel_id=1, source_target_pairs={{0,6},{2,4},{4,2},{6,0},{8,14},{10,12},{12,10},{14,8},{1,7},{3,5},... | collective-permute-start | bytes 589832 | tf_op jit(solution)/shard_map/ppermute | solution.py:313
  6.9 12.8 %collective-permute-start.1 = (bf16[192,512]{1,0:T(8,128)(2,1)S(1)}, bf16[192,512]{1,0:T(8,128)(2,1)S(1)}, u32[]{:S(2)}, u32[]{:S(2)}) collective-permute-start(bf16[192,512]{1,0:T(8,128)(2,1)S(1)} %get-tuple-element.31), channel_id=1, source_target_pairs={{0,4},{2,6},{4,0},{6,2},{8,12},{10,14},{12,8},{14,10},{1,5},{3,7},... | collective-permute-start | bytes 589832 | tf_op jit(solution)/shard_map/ppermute | solution.py:313
  7.4 12.3 %collective-permute-start.2 = (bf16[192,512]{1,0:T(8,128)(2,1)S(1)}, bf16[192,512]{1,0:T(8,128)(2,1)S(1)}, u32[]{:S(2)}, u32[]{:S(2)}) collective-permute-start(bf16[192,512]{1,0:T(8,128)(2,1)S(1)} %get-tuple-element.32), channel_id=1, source_target_pairs={{0,2},{2,0},{4,6},{6,4},{8,10},{10,8},{12,14},{14,12},{1,3},{3,1},... | collective-permute-start | bytes 589832 | tf_op jit(solution)/shard_map/ppermute | solution.py:313
  19.8 7.4 %copy-start.2 = (f32[512]{0:T(512)S(1)}, f32[512]{0:T(512)}, u32[]{:S(2)}) copy-start(f32[512]{0:T(512)} %param.18) | copy-start | bytes 6148
  19.8 7.4 %collective-permute-start.6 = (bf16[4,96,512]{2,1,0:T(8,128)(2,1)S(1)}, bf16[4,96,512]{2,1,0:T(8,128)(2,1)S(1)}, u32[]{:S(2)}, u32[]{:S(2)}) collective-permute-start(bf16[4,96,512]{2,1,0:T(8,128)(2,1)S(1)} %get-tuple-element.37), channel_id=1, source_target_pairs={{0,1},{1,0},{2,3},{3,2},{4,5},{5,4},{6,7},{7,6},{8,9},{9,8},{10,11... | collective-permute-start | bytes 1179656 | tf_op jit(solution)/shard_map/ppermute | solution.py:313
  19.8 6.7 %collective-permute-start.3 = (bf16[144,128]{1,0:T(8,128)(2,1)S(1)}, bf16[144,128]{1,0:T(8,128)(2,1)S(1)}, u32[]{:S(2)}, u32[]{:S(2)}) collective-permute-start(bf16[144,128]{1,0:T(8,128)(2,1)S(1)} %get-tuple-element.33), channel_id=1, source_target_pairs={{0,6},{2,4},{4,2},{6,0},{8,14},{10,12},{12,10},{14,8},{1,7},{3,5},... | collective-permute-start | bytes 110600 | tf_op jit(solution)/shard_map/ppermute | solution.py:313
  22.8 4.0 %collective-permute-start.4 = (bf16[144,128]{1,0:T(8,128)(2,1)S(1)}, bf16[144,128]{1,0:T(8,128)(2,1)S(1)}, u32[]{:S(2)}, u32[]{:S(2)}) collective-permute-start(bf16[144,128]{1,0:T(8,128)(2,1)S(1)} %get-tuple-element.34), channel_id=1, source_target_pairs={{0,4},{2,6},{4,0},{6,2},{8,12},{10,14},{12,8},{14,10},{1,5},{3,7},... | collective-permute-start | bytes 110600 | tf_op jit(solution)/shard_map/ppermute | solution.py:313
  23.2 4.0 %collective-permute-start.5 = (bf16[144,128]{1,0:T(8,128)(2,1)S(1)}, bf16[144,128]{1,0:T(8,128)(2,1)S(1)}, u32[]{:S(2)}, u32[]{:S(2)}) collective-permute-start(bf16[144,128]{1,0:T(8,128)(2,1)S(1)} %get-tuple-element.35), channel_id=1, source_target_pairs={{0,2},{2,0},{4,6},{6,4},{8,10},{10,8},{12,14},{14,12},{1,3},{3,1},... | collective-permute-start | bytes 110600 | tf_op jit(solution)/shard_map/ppermute | solution.py:313
  28.0 15.2 %copy-start = (bf16[512,512]{1,0:T(8,128)(2,1)S(1)}, bf16[512,512]{1,0:T(8,128)(2,1)}, u32[]{:S(2)}) copy-start(bf16[512,512]{1,0:T(8,128)(2,1)} %refs_4_.3) | copy-start | bytes 1572868
  28.0 15.2 %copy-start.1 = (bf16[512,512]{1,0:T(8,128)(2,1)S(1)}, bf16[512,512]{1,0:T(8,128)(2,1)}, u32[]{:S(2)}) copy-start(bf16[512,512]{1,0:T(8,128)(2,1)} %refs_5_.1) | copy-start | bytes 1572868
  28.0 14.1 %collective-permute-start.10 = (bf16[208,512]{1,0:T(8,128)(2,1)S(1)}, bf16[208,512]{1,0:T(8,128)(2,1)S(1)}, u32[]{:S(2)}, u32[]{:S(2)}) collective-permute-start(bf16[208,512]{1,0:T(8,128)(2,1)S(1)} %get-tuple-element.38.refs_5_), channel_id=1, source_target_pairs={{0,8},{2,10},{4,12},{6,14},{8,0},{10,2},{12,4},{14,6},{1,9},{3,11}... | collective-permute-start | bytes 638984 | tf_op jit(solution)/shard_map/ppermute | solution.py:313
  34.6 7.3 %collective-permute-start.7 = (bf16[144,128]{1,0:T(8,128)(2,1)S(1)}, bf16[144,128]{1,0:T(8,128)(2,1)S(1)}, u32[]{:S(2)}, u32[]{:S(2)}) collective-permute-start(bf16[144,128]{1,0:T(8,128)(2,1)S(1)} %get-tuple-element.56), channel_id=1, source_target_pairs={{0,6},{2,4},{4,2},{6,0},{8,14},{10,12},{12,10},{14,8},{1,7},{3,5},... | collective-permute-start | bytes 110600 | tf_op jit(solution)/shard_map/ppermute | solution.py:313
  37.6 4.3 %collective-permute-start.8 = (bf16[144,128]{1,0:T(8,128)(2,1)S(1)}, bf16[144,128]{1,0:T(8,128)(2,1)S(1)}, u32[]{:S(2)}, u32[]{:S(2)}) collective-permute-start(bf16[144,128]{1,0:T(8,128)(2,1)S(1)} %get-tuple-element.55), channel_id=1, source_target_pairs={{0,4},{2,6},{4,0},{6,2},{8,12},{10,14},{12,8},{14,10},{1,5},{3,7},... | collective-permute-start | bytes 110600 | tf_op jit(solution)/shard_map/ppermute | solution.py:313
  37.9 4.3 %collective-permute-start.9 = (bf16[144,128]{1,0:T(8,128)(2,1)S(1)}, bf16[144,128]{1,0:T(8,128)(2,1)S(1)}, u32[]{:S(2)}, u32[]{:S(2)}) collective-permute-start(bf16[144,128]{1,0:T(8,128)(2,1)S(1)} %get-tuple-element.39), channel_id=1, source_target_pairs={{0,2},{2,0},{4,6},{6,4},{8,10},{10,8},{12,14},{14,12},{1,3},{3,1},... | collective-permute-start | bytes 110600 | tf_op jit(solution)/shard_map/ppermute | solution.py:313
  43.2 15.0 %copy-start.3 = (f32[512]{0:T(512)S(1)}, f32[512]{0:T(512)}, u32[]{:S(2)}) copy-start(f32[512]{0:T(512)} %param.21) | copy-start | bytes 6148
  43.2 1.4 %collective-permute-start.11 = (bf16[192,512]{1,0:T(8,128)(2,1)S(1)}, bf16[192,512]{1,0:T(8,128)(2,1)S(1)}, u32[]{:S(2)}, u32[]{:S(2)}) collective-permute-start(bf16[192,512]{1,0:T(8,128)(2,1)S(1)} %get-tuple-element.43.refs_1_), channel_id=1, source_target_pairs={{0,1},{1,0},{2,3},{3,2},{4,5},{5,4},{6,7},{7,6},{8,9},{9,8},{10,11... | collective-permute-start | bytes 589832 | tf_op jit(solution)/shard_map/ppermute | solution.py:313
  45.5 6.0 %collective-permute-start.15 = (bf16[64,512]{1,0:T(8,128)(2,1)S(1)}, bf16[64,512]{1,0:T(8,128)(2,1)S(1)}, u32[]{:S(2)}, u32[]{:S(2)}) collective-permute-start(bf16[64,512]{1,0:T(8,128)(2,1)S(1)} %get-tuple-element.50), channel_id=1, source_target_pairs={{0,6},{2,4},{4,2},{6,0},{8,14},{10,12},{12,10},{14,8},{1,7},{3,5},... | collective-permute-start | bytes 196616 | tf_op jit(solution)/shard_map/ppermute | solution.py:313
  47.2 5.3 %collective-permute-start.16 = (bf16[64,512]{1,0:T(8,128)(2,1)S(1)}, bf16[64,512]{1,0:T(8,128)(2,1)S(1)}, u32[]{:S(2)}, u32[]{:S(2)}) collective-permute-start(bf16[64,512]{1,0:T(8,128)(2,1)S(1)} %get-tuple-element.51), channel_id=1, source_target_pairs={{0,4},{2,6},{4,0},{6,2},{8,12},{10,14},{12,8},{14,10},{1,5},{3,7},... | collective-permute-start | bytes 196616 | tf_op jit(solution)/shard_map/ppermute | solution.py:313
  47.9 5.0 %collective-permute-start.17 = (bf16[64,512]{1,0:T(8,128)(2,1)S(1)}, bf16[64,512]{1,0:T(8,128)(2,1)S(1)}, u32[]{:S(2)}, u32[]{:S(2)}) collective-permute-start(bf16[64,512]{1,0:T(8,128)(2,1)S(1)} %get-tuple-element.52), channel_id=1, source_target_pairs={{0,2},{2,0},{4,6},{6,4},{8,10},{10,8},{12,14},{14,12},{1,3},{3,1},... | collective-permute-start | bytes 196616 | tf_op jit(solution)/shard_map/ppermute | solution.py:313
  49.0 5.3 %collective-permute-start.12 = (bf16[64,512]{1,0:T(8,128)(2,1)S(1)}, bf16[64,512]{1,0:T(8,128)(2,1)S(1)}, u32[]{:S(2)}, u32[]{:S(2)}) collective-permute-start(bf16[64,512]{1,0:T(8,128)(2,1)S(1)} %get-tuple-element.46), channel_id=1, source_target_pairs={{0,6},{2,4},{4,2},{6,0},{8,14},{10,12},{12,10},{14,8},{1,7},{3,5},... | collective-permute-start | bytes 196616 | tf_op jit(solution)/shard_map/ppermute | solution.py:313
  50.7 4.3 %collective-permute-start.13 = (bf16[64,512]{1,0:T(8,128)(2,1)S(1)}, bf16[64,512]{1,0:T(8,128)(2,1)S(1)}, u32[]{:S(2)}, u32[]{:S(2)}) collective-permute-start(bf16[64,512]{1,0:T(8,128)(2,1)S(1)} %get-tuple-element.47), channel_id=1, source_target_pairs={{0,4},{2,6},{4,0},{6,2},{8,12},{10,14},{12,8},{14,10},{1,5},{3,7},... | collective-permute-start | bytes 196616 | tf_op jit(solution)/shard_map/ppermute | solution.py:313
  51.4 4.3 %collective-permute-start.14 = (bf16[64,512]{1,0:T(8,128)(2,1)S(1)}, bf16[64,512]{1,0:T(8,128)(2,1)S(1)}, u32[]{:S(2)}, u32[]{:S(2)}) collective-permute-start(bf16[64,512]{1,0:T(8,128)(2,1)S(1)} %get-tuple-element.48), channel_id=1, source_target_pairs={{0,2},{2,0},{4,6},{6,4},{8,10},{10,8},{12,14},{14,12},{1,3},{3,1},... | collective-permute-start | bytes 196616 | tf_op jit(solution)/shard_map/ppermute | solution.py:313
  53.0 5.2 %collective-permute-start.18 = (bf16[64,512]{1,0:T(8,128)(2,1)S(1)}, bf16[64,512]{1,0:T(8,128)(2,1)S(1)}, u32[]{:S(2)}, u32[]{:S(2)}) collective-permute-start(bf16[64,512]{1,0:T(8,128)(2,1)S(1)} %side_sum.1), channel_id=1, source_target_pairs={{0,8},{2,10},{4,12},{6,14},{8,0},{10,2},{12,4},{14,6},{1,9},{3,11}... | collective-permute-start | bytes 196616 | tf_op jit(solution)/shard_map/ppermute | solution.py:313

commit v9 on v8

--- a/solution.py
+++ b/solution.py
@@ -101,9 +101,10 @@
 
 
 def mean_kernel(chosen, fanout, pcap, fslice, n_idx, nbr_hbm, table_ref, *refs):
-    parcel_refs, (out_ref, total, nbr_ref, live_ref, sems) = refs[:-5], refs[-5:]
+    count = len(chosen)
+    out_ref, total, nbr_ref, live_ref, sems = refs[-5:]
+    chunk_refs, parcel_refs = refs[-5 - count : -5], refs[: -5 - count]
     feat_pos = lax.axis_index("feat")
-    count = len(chosen)
     stride = nbr_ref.shape[0] // count
     copies = [
         pltpu.make_async_copy(
@@ -127,13 +128,16 @@
 
         def group(g, inner):
             at = pl.multiple_of(g * 16, 16)
+            sums = []
             for u in range(16):
                 rows = [table_ref[nbr_ref[first + k * pcap + at + u]] for k in range(fanout)]
                 while len(rows) > 1:
                     rows = [a + b for a, b in zip(rows[::2], rows[1::2])] + (
                         [rows[-1]] if len(rows) % 2 else []
                     )
-                total[pl.ds(at + u, 1), :] = rows[0]
+                sums.append(rows[0])
+            for u, row in enumerate(sums):
+                total[pl.ds(at + u, 1), :] = row
             return inner
 
         lax.fori_loop(0, lax.div(live_ref[i] + 15, 16), group, 0)
@@ -153,6 +157,8 @@
         return carry
 
     lax.fori_loop(0, count, partition, 0)
+    for i, ref in enumerate(chunk_refs):
+        ref[...] = out_ref[i]
 
 
 def unfold(block, fslice, pcap):
@@ -171,21 +177,13 @@
 
 
 def halves_kernel(half, *refs):
-    parcel_refs, chunks_ref, out_ref, chunk_refs = (
-        refs[:half],
-        refs[half],
-        refs[half + 1],
-        refs[half + 2 :],
-    )
     for s in range(half):
-        out_ref[s] = parcel_refs[s][: out_ref.shape[1], :]
-        chunk_refs[s][...] = chunks_ref[s]
+        refs[half][s] = refs[s][: refs[half].shape[1], :]
 
 
 def prepare_kernel(half, n_idx, *refs):
     parcel_refs, mean_refs = refs[:half], refs[half : 2 * half]
-    other_ref, bias_ref, first_ref, w_ref, pre_ref, cross_ref, moved_ref = refs[2 * half :]
-    moved_ref[...] = first_ref[0]
+    other_ref, bias_ref, w_ref, pre_ref, cross_ref = refs[2 * half :]
     fslice = w_ref.shape[1]
     pcap, width = pre_ref.shape
     first_core = lax.axis_index("rep") == 0
@@ -404,46 +402,46 @@
 
     def means(chosen, parcels=(), after=()):
         count = len(chosen)
-        (chunks,) = call(
+        return call(
             functools.partial(mean_kernel, tuple(chosen), fanout_one, pcap, fslice, n_idx),
             "mean",
-            [((count, *chunk_shape), bf16)],
+            [(chunk_shape, bf16)] * count,
             [anywhere] + [vmem] * (1 + len(parcels)),
             (neighbors, table, *parcels),
             after=after,
             scratch=[
+                pltpu.VMEM((count, *chunk_shape), bf16),
                 pltpu.VMEM((pcap, LANES), jnp.float32),
                 pltpu.SMEM((count * stride,), jnp.int32),
                 pltpu.SMEM((count,), jnp.int32),
                 pltpu.SemaphoreType.DMA((count,)),
             ],
             limit=table_bytes + 8 * MIB,
-            cost_us=2 * count,
-        )
-        return chunks
-
-    far_means = means([s + half for s in steps])
-    halves, *far_chunks = call(
+            cost_us=2 * count if count > 1 else 0.5,
+        )
+
+    far_means = means([s + half for s in steps if s])
+    (halves,) = call(
         functools.partial(halves_kernel, half),
         "halves",
-        [((half, fslice, width), bf16)] + [(chunk_shape, bf16)] * half,
-        [vmem] * (half + 1),
-        (*arrived, far_means),
-    )
-    far_arrived = send(far_chunks)
+        [((half, fslice, width), bf16)],
+        [vmem] * half,
+        arrived,
+        after=far_means[:1],
+    )
+    far_arrived = send(far_means)
     other_halves = swap(halves, "rep", 1)
-    first_mean = means([1], arrived[-2:-1], (far_chunks[-1],))
-    w_nbr, pre, cross, moved = call(
+    (far_own,) = means([half], after=(halves,))
+    w_nbr, pre, cross = call(
         functools.partial(prepare_kernel, half, n_idx),
         "prepare",
         [
             ((half, fslice, width), bf16),
             ((pcap, width), jnp.float32),
             ((pcap + -(-half // 4) * n_idx, width), bf16),
-            (chunk_shape, bf16),
         ],
-        [vmem] * (2 * half + 3),
-        (*arrived, *far_arrived, other_halves, bias_one[None], first_mean),
+        [vmem] * (2 * half + 2),
+        (*arrived, *far_arrived, far_own, other_halves, bias_one[None]),
     )
     cross_arrived = swap(cross, "feat", half)
     (near_times,) = call(
@@ -452,19 +450,17 @@
         [((half * seed_count, 4 * pcap), bf16)],
         [vmem] * half,
         arrived,
-        after=(far_means,),
-    )
-    near_means = means(
-        [s for s in steps if s != 1], [*arrived[:-2], arrived[-1]], (cross, near_times)
-    )
-    near_means = [near_means[i] for i in range(half - 1)]
-    near_arrived = send([*near_means[:-1], moved, near_means[-1]])
+        after=far_means[:1],
+    )
+    near_means = means([s for s in steps if s], arrived[:-1], (cross, near_times))
+    near_arrived = send(near_means)
+    (near_own,) = means([0], arrived[-1:], near_means[:1])
     hidden, result = call(
         functools.partial(layer_kernel, half, n_idx),
         "hidden",
         [((pcap, width), bf16)] * 2,
         [vmem] * (half + 4),
-        (parcels[-1], *near_arrived, pre, w_nbr, cross_arrived),
+        (parcels[-1], *near_arrived, near_own, pre, w_nbr, cross_arrived),
     )
     other_hidden = swap(hidden, "rep", 1)
     far_times, value = call(

time: 59.5 us -> 57.9 us (0.973)
  waiting for transfers between devices: 9.56 us -> 6.75 us
  Pallas kernels: 24.7 us -> 26 us
    ppermute x19, waiting for transfers between devices: 9.56 us -> 6.75 us  [swap(): return lax.ppermute(value, axis, [(i, i ^ step) for i in range(size)])]
    pallas_call x13 -> x14, Pallas kernels: 24.7 us -> 26 us  [call(): pl.pallas_call(wrapped, out_shape=tuple((jax.ShapeDtypeStruct(shape, dtyp...]
  transfers between devices with their start and end apart: 19 -> 19, of which waited for: 10 -> 7; matrix products, arithmetic and copies ran while one was open for 1% -> 1% of each run, Pallas kernels for 33% -> 36%
where the time goes in v9:
time: 57.9 us
  Pallas kernels  26 us (45%)
  starting transfers between devices  23.4 us (40%)
  waiting for transfers between devices  6.75 us (12%)
  between operations  1.47 us (3%)
    pallas_call x14, Pallas kernels, call(): pl.pallas_call(wrapped, out_shape=tuple((jax.ShapeDtypeStruct(shape, dtyp...  26 us
    ppermute x19, starting transfers between devices, swap(): return lax.ppermute(value, axis, [(i, i ^ step) for i in range(size)])  23.4 us
    ppermute x19, waiting for transfers between devices, swap(): return lax.ppermute(value, axis, [(i, i ^ step) for i in range(size)])  6.75 us
  transfers between devices with their start and end apart: 19, of which 7 were waited for; matrix products, arithmetic and copies ran while one was open for 1% of the time, Pallas kernels for 36%

profile of v9, /device:TPU:0, one launch (start us, length us, event | category | flops | bytes accessed | tf_op | source)
XLA Modules:
  0.0 57.9 jit_solution(8710801645096952635)
XLA Ops:
  1.3 1.6 %pack.1 = (bf16[192,512]{1,0:T(8,128)(2,1)S(1)}, bf16[192,512]{1,0:T(8,128)(2,1)S(1)}, bf16[192,512]{1,0:T(8,128)(2,1)S(1)}, bf16[192,512]{1,0:T(8,128)(2,1)S(1)}, s32[8,10,1,192]{3,2,1,0:T(1,128)S(1)}) custom-call(bf16[96,12288]{1,0:T(8,128)(2,1)} %refs_0_.3, s32[1,64]{1,0:T(1,128)} %bitcast.23, s32[15,64]{1,0:T(8,128)} %bitcast.22, ...), custom_call_target="tpu_custom_call" | custom-call | flops 1100000000 | tf_op jit(solution)/shard_map/pack/pallas_call | solution.py:346
  2.9 4.0 %collective-permute-start = (bf16[192,512]{1,0:T(8,128)(2,1)S(1)}, bf16[192,512]{1,0:T(8,128)(2,1)S(1)}, u32[]{:S(2)}, u32[]{:S(2)}) collective-permute-start(bf16[192,512]{1,0:T(8,128)(2,1)S(1)} %get-tuple-element.30), channel_id=1, source_target_pairs={{0,6},{2,4},{4,2},{6,0},{8,14},{10,12},{12,10},{14,8},{1,7},{3,5},... | collective-permute-start | bytes 589832 | tf_op jit(solution)/shard_map/ppermute | solution.py:311
  6.9 0.4 collective-permute-start.1
  7.4 0.2 collective-permute-start.2
  7.6 0.2 reduce
  7.8 0.1 reshape.13
  7.9 3.2 %turn.1 = f32[12288,128]{1,0:T(8,128)S(1)} custom-call(bf16[96,12288]{1,0:T(8,128)(2,1)} %refs_0_.3, bf16[192,512]{1,0:T(8,128)(2,1)S(1)} %get-tuple-element.28.refs_1_.refs_3_.refs_2_.refs_0_, s32[16384]{0:T(1024)S(1)} %bitcast.14), custom_call_target="tpu_custom_call" | custom-call | flops 3300000000 | tf_op jit(solution)/shard_map/turn/pallas_call | solution.py:346
  11.1 6.6 %mean.4 = (bf16[144,128]{1,0:T(8,128)(2,1)S(1)}, bf16[144,128]{1,0:T(8,128)(2,1)S(1)}, bf16[144,128]{1,0:T(8,128)(2,1)S(1)}) custom-call(s32[16384]{0:T(1024)S(1)} %bitcast.15, f32[12288,1,128]{2,1,0:T(1,128)S(1)} %bitcast.10), custom_call_target="tpu_custom_call" | custom-call | flops 6600000000 | tf_op jit(solution)/shard_map/mean/pallas_call | solution.py:346
  17.7 0.0 collective-permute-done.refs_0_.refs_2_
  17.7 0.0 collective-permute-done.1.refs_1_.refs_3_
  17.7 0.0 collective-permute-done.2.refs_2_.refs_4_
  17.8 0.0 copy-start.2
  17.8 0.1 collective-permute-start.6
  17.8 2.9 %collective-permute-start.3 = (bf16[144,128]{1,0:T(8,128)(2,1)S(1)}, bf16[144,128]{1,0:T(8,128)(2,1)S(1)}, u32[]{:S(2)}, u32[]{:S(2)}) collective-permute-start(bf16[144,128]{1,0:T(8,128)(2,1)S(1)} %get-tuple-element.33.refs_4_), channel_id=1, source_target_pairs={{0,6},{2,4},{4,2},{6,0},{8,14},{10,12},{12,10},{14,8},{1,7},{3,5},... | collective-permute-start | bytes 110600 | tf_op jit(solution)/shard_map/ppermute | solution.py:311
  20.8 0.4 collective-permute-start.4
  21.2 0.2 collective-permute-start.5
  21.4 0.8 %near_times.1.refs_6_.refs_0_ = bf16[256,768]{1,0:T(8,128)(2,1)S(1)} custom-call(bf16[192,512]{1,0:T(8,128)(2,1)S(1)} %collective-permute-done.refs_0_.refs_2_, bf16[192,512]{1,0:T(8,128)(2,1)S(1)} %collective-permute-done.1.refs_1_.refs_3_, bf16[192,512]{1,0:T(8,128)(2,1)S(1)} %collective-permute-done.2.refs_2_.refs_4_, ...), custom_call_target="tpu_custom_call" | custom-call | flops 1100000000 | tf_op jit(solution)/shard_map/near_times/pallas_call | solution.py:346
  22.2 2.4 %mean.5.refs_7_ = bf16[144,128]{1,0:T(8,128)(2,1)S(1)} custom-call(s32[16384]{0:T(1024)S(1)} %bitcast.16, f32[12288,1,128]{2,1,0:T(1,128)S(1)} %bitcast.11, bf16[4,96,512]{2,1,0:T(8,128)(2,1)S(1)} %halves.1.refs_2_), custom_call_target="tpu_custom_call" | custom-call | flops 550000000 | tf_op jit(solution)/shard_map/mean/pallas_call | solution.py:346
  24.6 0.0 collective-permute-done.3.refs_4_
  24.6 0.1 collective-permute-done.4.refs_5_
  24.7 0.4 collective-permute-done.5.refs_6_
  25.2 0.0 collective-permute-done.6.refs_8_
  25.2 0.0 copy-done.2
  25.2 0.8 %prepare.1 = (bf16[4,96,512]{2,1,0:T(8,128)(2,1)S(1)}, f32[192,512]{1,0:T(8,128)S(1)}, bf16[208,512]{1,0:T(8,128)(2,1)S(1)}) custom-call(bf16[192,512]{1,0:T(8,128)(2,1)S(1)} %collective-permute-done.refs_0_.refs_2_, bf16[192,512]{1,0:T(8,128)(2,1)S(1)} %collective-permute-done.1.refs_1_.refs_3_, ...), custom_call_target="tpu_custom_call" | custom-call | flops 1100000000 | tf_op jit(solution)/shard_map/prepare/pallas_call | solution.py:346
  26.0 2.7 %collective-permute-start.10 = (bf16[208,512]{1,0:T(8,128)(2,1)S(1)}, bf16[208,512]{1,0:T(8,128)(2,1)S(1)}, u32[]{:S(2)}, u32[]{:S(2)}) collective-permute-start(bf16[208,512]{1,0:T(8,128)(2,1)S(1)} %get-tuple-element.36.refs_5_), channel_id=1, source_target_pairs={{0,8},{2,10},{4,12},{6,14},{8,0},{10,2},{12,4},{14,6},{1,9},{3,11}... | collective-permute-start | bytes 638984 | tf_op jit(solution)/shard_map/ppermute | solution.py:311
  28.7 5.1 %mean.6 = (bf16[144,128]{1,0:T(8,128)(2,1)S(1)}, bf16[144,128]{1,0:T(8,128)(2,1)S(1)}, bf16[144,128]{1,0:T(8,128)(2,1)S(1)}) custom-call(s32[16384]{0:T(1024)S(1)} %bitcast.17, f32[12288,1,128]{2,1,0:T(1,128)S(1)} %bitcast.12, bf16[192,512]{1,0:T(8,128)(2,1)S(1)} %collective-permute-done.refs_0_.refs_2_, ...), custom_call_target="tpu_custom_call" | custom-call | flops 6600000000 | tf_op jit(solution)/shard_map/mean/pallas_call | solution.py:346
  33.7 0.0 copy-start
  33.8 0.0 copy-start.1
  33.8 3.5 %collective-permute-start.7 = (bf16[144,128]{1,0:T(8,128)(2,1)S(1)}, bf16[144,128]{1,0:T(8,128)(2,1)S(1)}, u32[]{:S(2)}, u32[]{:S(2)}) collective-permute-start(bf16[144,128]{1,0:T(8,128)(2,1)S(1)} %get-tuple-element.37.refs_3_), channel_id=1, source_target_pairs={{0,6},{2,4},{4,2},{6,0},{8,14},{10,12},{12,10},{14,8},{1,7},{3,5},... | collective-permute-start | bytes 110600 | tf_op jit(solution)/shard_map/ppermute | solution.py:311
  37.3 0.0 collective-permute-start.8
  37.3 0.6 %collective-permute-start.9 = (bf16[144,128]{1,0:T(8,128)(2,1)S(1)}, bf16[144,128]{1,0:T(8,128)(2,1)S(1)}, u32[]{:S(2)}, u32[]{:S(2)}) collective-permute-start(bf16[144,128]{1,0:T(8,128)(2,1)S(1)} %get-tuple-element.39), channel_id=1, source_target_pairs={{0,2},{2,0},{4,6},{6,4},{8,10},{10,8},{12,14},{14,12},{1,3},{3,1},... | collective-permute-start | bytes 110600 | tf_op jit(solution)/shard_map/ppermute | solution.py:311
  37.9 2.1 %mean.7.refs_4_ = bf16[144,128]{1,0:T(8,128)(2,1)S(1)} custom-call(s32[16384]{0:T(1024)S(1)} %bitcast.18, f32[12288,1,128]{2,1,0:T(1,128)S(1)} %bitcast.13, bf16[192,512]{1,0:T(8,128)(2,1)S(1)} %get-tuple-element.28.refs_1_.refs_3_.refs_2_.refs_0_, bf16[144,128]{1,0:T(8,128)(2,1)S(1)} %get-tuple-element.37.refs_3_), custom_call_target="tpu_custom_call" | custom-call | flops 550000000 | tf_op jit(solution)/shard_map/mean/pallas_call | solution.py:346
  40.1 0.0 collective-permute-done.7.refs_1_
  40.1 1.2 %collective-permute-done.8.refs_2_ = bf16[144,128]{1,0:T(8,128)(2,1)S(1)} collective-permute-done((bf16[144,128]{1,0:T(8,128)(2,1)S(1)}, bf16[144,128]{1,0:T(8,128)(2,1)S(1)}, u32[]{:S(2)}, u32[]{:S(2)}) %collective-permute-start.8) | collective-permute-done | bytes 36896 | tf_op jit(solution)/shard_map/ppermute | solution.py:311
  41.3 0.0 collective-permute-done.9.refs_3_
  41.3 0.0 collective-permute-done.10.refs_7_.refs_0_
  41.3 1.1 %hidden.1 = (bf16[192,512]{1,0:T(8,128)(2,1)S(1)}, bf16[192,512]{1,0:T(8,128)(2,1)}) custom-call(bf16[192,512]{1,0:T(8,128)(2,1)S(1)} %get-tuple-element.28.refs_1_.refs_3_.refs_2_.refs_0_, bf16[144,128]{1,0:T(8,128)(2,1)S(1)} %collective-permute-done.7.refs_1_, bf16[144,128]{1,0:T(8,128)(2,1)S(1)} %collective-permute-done.8.refs_2_, ...), custom_call_target="tpu_custom_call" | custom-call | flops 1100000000 | tf_op jit(solution)/shard_map/hidden/pallas_call | solution.py:346
  42.3 0.0 copy-start.3
  42.3 0.0 collective-permute-start.11
  42.3 0.0 copy-done
  42.3 0.0 copy-done.1
  42.3 0.8 %far_times.1 = (bf16[256,768]{1,0:T(8,128)(2,1)S(1)}, bf16[2,192,512]{2,1,0:T(8,128)(2,1)S(1)}) custom-call(bf16[208,512]{1,0:T(8,128)(2,1)S(1)} %collective-permute-done.10.refs_7_.refs_0_, bf16[192,512]{1,0:T(8,128)(2,1)S(1)} %get-tuple-element.43.refs_1_, bf16[512,512]{1,0:T(8,128)(2,1)S(1)} %copy-done, bf16[512,512]{1,0:T(8,128)(2,1)S(1)} %copy-done.1), custom_call_target="tpu_custom_call" | custom-call | flops 1100000000 | tf_op jit(solution)/shard_map/far_times/pallas_call | solution.py:346
  43.2 0.6 collective-permute-done.11.refs_3_
  43.8 0.8 %share.1 = (bf16[64,512]{1,0:T(8,128)(2,1)S(1)}, bf16[64,512]{1,0:T(8,128)(2,1)S(1)}, bf16[64,512]{1,0:T(8,128)(2,1)S(1)}, bf16[64,512]{1,0:T(8,128)(2,1)S(1)}, ...) custom-call(bf16[256,768]{1,0:T(8,128)(2,1)S(1)} %near_times.1.refs_, ...), custom_call_target="tpu_custom_call" | custom-call | flops 1100000000 | tf_op jit(solution)/shard_map/share/pallas_call | solution.py:346
  44.6 1.5 %collective-permute-start.15 = (bf16[64,512]{1,0:T(8,128)(2,1)S(1)}, bf16[64,512]{1,0:T(8,128)(2,1)S(1)}, u32[]{:S(2)}, u32[]{:S(2)}) collective-permute-start(bf16[64,512]{1,0:T(8,128)(2,1)S(1)} %get-tuple-element.50), channel_id=1, source_target_pairs={{0,6},{2,4},{4,2},{6,0},{8,14},{10,12},{12,10},{14,8},{1,7},{3,5},... | collective-permute-start | bytes 196616 | tf_op jit(solution)/shard_map/ppermute | solution.py:311
  46.1 0.6 %collective-permute-start.16 = (bf16[64,512]{1,0:T(8,128)(2,1)S(1)}, bf16[64,512]{1,0:T(8,128)(2,1)S(1)}, u32[]{:S(2)}, u32[]{:S(2)}) collective-permute-start(bf16[64,512]{1,0:T(8,128)(2,1)S(1)} %get-tuple-element.51), channel_id=1, source_target_pairs={{0,4},{2,6},{4,0},{6,2},{8,12},{10,14},{12,8},{14,10},{1,5},{3,7},... | collective-permute-start | bytes 196616 | tf_op jit(solution)/shard_map/ppermute | solution.py:311
  46.7 1.4 %collective-permute-start.17 = (bf16[64,512]{1,0:T(8,128)(2,1)S(1)}, bf16[64,512]{1,0:T(8,128)(2,1)S(1)}, u32[]{:S(2)}, u32[]{:S(2)}) collective-permute-start(bf16[64,512]{1,0:T(8,128)(2,1)S(1)} %get-tuple-element.52), channel_id=1, source_target_pairs={{0,2},{2,0},{4,6},{6,4},{8,10},{10,8},{12,14},{14,12},{1,3},{3,1},... | collective-permute-start | bytes 196616 | tf_op jit(solution)/shard_map/ppermute | solution.py:311
  48.1 1.5 %collective-permute-start.12 = (bf16[64,512]{1,0:T(8,128)(2,1)S(1)}, bf16[64,512]{1,0:T(8,128)(2,1)S(1)}, u32[]{:S(2)}, u32[]{:S(2)}) collective-permute-start(bf16[64,512]{1,0:T(8,128)(2,1)S(1)} %get-tuple-element.46), channel_id=1, source_target_pairs={{0,6},{2,4},{4,2},{6,0},{8,14},{10,12},{12,10},{14,8},{1,7},{3,5},... | collective-permute-start | bytes 196616 | tf_op jit(solution)/shard_map/ppermute | solution.py:311
  49.6 0.6 %collective-permute-start.13 = (bf16[64,512]{1,0:T(8,128)(2,1)S(1)}, bf16[64,512]{1,0:T(8,128)(2,1)S(1)}, u32[]{:S(2)}, u32[]{:S(2)}) collective-permute-start(bf16[64,512]{1,0:T(8,128)(2,1)S(1)} %get-tuple-element.47), channel_id=1, source_target_pairs={{0,4},{2,6},{4,0},{6,2},{8,12},{10,14},{12,8},{14,10},{1,5},{3,7},... | collective-permute-start | bytes 196616 | tf_op jit(solution)/shard_map/ppermute | solution.py:311
  50.2 0.0 collective-permute-done.15.refs_0_
  50.2 1.4 %collective-permute-start.14 = (bf16[64,512]{1,0:T(8,128)(2,1)S(1)}, bf16[64,512]{1,0:T(8,128)(2,1)S(1)}, u32[]{:S(2)}, u32[]{:S(2)}) collective-permute-start(bf16[64,512]{1,0:T(8,128)(2,1)S(1)} %get-tuple-element.48), channel_id=1, source_target_pairs={{0,2},{2,0},{4,6},{6,4},{8,10},{10,8},{12,14},{14,12},{1,3},{3,1},... | collective-permute-start | bytes 196616 | tf_op jit(solution)/shard_map/ppermute | solution.py:311
  51.6 0.0 collective-permute-done.16.refs_1_
  51.6 0.0 collective-permute-done.17.refs_2_
  51.7 1.2 %collective-permute-start.18 = (bf16[64,512]{1,0:T(8,128)(2,1)S(1)}, bf16[64,512]{1,0:T(8,128)(2,1)S(1)}, u32[]{:S(2)}, u32[]{:S(2)}) collective-permute-start(bf16[64,512]{1,0:T(8,128)(2,1)S(1)} %side_sum.1), channel_id=1, source_target_pairs={{0,8},{2,10},{4,12},{6,14},{8,0},{10,2},{12,4},{14,6},{1,9},{3,11}... | collective-permute-start | bytes 196616 | tf_op jit(solution)/shard_map/ppermute | solution.py:311
  52.9 1.0 %collective-permute-done.12.refs_1_ = bf16[64,512]{1,0:T(8,128)(2,1)S(1)} collective-permute-done((bf16[64,512]{1,0:T(8,128)(2,1)S(1)}, bf16[64,512]{1,0:T(8,128)(2,1)S(1)}, u32[]{:S(2)}, u32[]{:S(2)}) %collective-permute-start.12) | collective-permute-done | bytes 65568 | tf_op jit(solution)/shard_map/ppermute | solution.py:311
  53.9 0.0 collective-permute-done.13.refs_2_
  53.9 0.6 %collective-permute-done.14.refs_3_ = bf16[64,512]{1,0:T(8,128)(2,1)S(1)} collective-permute-done((bf16[64,512]{1,0:T(8,128)(2,1)S(1)}, bf16[64,512]{1,0:T(8,128)(2,1)S(1)}, u32[]{:S(2)}, u32[]{:S(2)}) %collective-permute-start.14) | collective-permute-done | bytes 65568 | tf_op jit(solution)/shard_map/ppermute | solution.py:311
  54.6 2.7 %collective-permute-done.18.refs_5_ = bf16[64,512]{1,0:T(8,128)(2,1)S(1)} collective-permute-done((bf16[64,512]{1,0:T(8,128)(2,1)S(1)}, bf16[64,512]{1,0:T(8,128)(2,1)S(1)}, u32[]{:S(2)}, u32[]{:S(2)}) %collective-permute-start.18) | collective-permute-done | bytes 65568 | tf_op jit(solution)/shard_map/ppermute | solution.py:311
  57.2 0.0 copy-done.3
  57.2 0.7 %seeds.1 = bf16[64,512]{1,0:T(8,128)(2,1)} custom-call(f32[1,512]{1,0:T(1,128)S(1)} %bitcast.20, bf16[64,512]{1,0:T(8,128)(2,1)S(1)} %collective-permute-done.12.refs_1_, bf16[64,512]{1,0:T(8,128)(2,1)S(1)} %collective-permute-done.13.refs_2_, bf16[64,512]{1,0:T(8,128)(2,1)S(1)} %collective-permute-done.14.refs_3_, ...), custom_call_target="tpu_custom_call" | custom-call | flops 1100000000 | tf_op jit(solution)/shard_map/seeds/pallas_call | solution.py:346
  (4 shorter events, 0.1 us)
Async XLA Ops:
  2.9 14.8 %collective-permute-start = (bf16[192,512]{1,0:T(8,128)(2,1)S(1)}, bf16[192,512]{1,0:T(8,128)(2,1)S(1)}, u32[]{:S(2)}, u32[]{:S(2)}) collective-permute-start(bf16[192,512]{1,0:T(8,128)(2,1)S(1)} %get-tuple-element.30), channel_id=1, source_target_pairs={{0,6},{2,4},{4,2},{6,0},{8,14},{10,12},{12,10},{14,8},{1,7},{3,5},... | collective-permute-start | bytes 589832 | tf_op jit(solution)/shard_map/ppermute | solution.py:311
  6.9 10.8 %collective-permute-start.1 = (bf16[192,512]{1,0:T(8,128)(2,1)S(1)}, bf16[192,512]{1,0:T(8,128)(2,1)S(1)}, u32[]{:S(2)}, u32[]{:S(2)}) collective-permute-start(bf16[192,512]{1,0:T(8,128)(2,1)S(1)} %get-tuple-element.31), channel_id=1, source_target_pairs={{0,4},{2,6},{4,0},{6,2},{8,12},{10,14},{12,8},{14,10},{1,5},{3,7},... | collective-permute-start | bytes 589832 | tf_op jit(solution)/shard_map/ppermute | solution.py:311
  7.4 10.3 %collective-permute-start.2 = (bf16[192,512]{1,0:T(8,128)(2,1)S(1)}, bf16[192,512]{1,0:T(8,128)(2,1)S(1)}, u32[]{:S(2)}, u32[]{:S(2)}) collective-permute-start(bf16[192,512]{1,0:T(8,128)(2,1)S(1)} %get-tuple-element.32), channel_id=1, source_target_pairs={{0,2},{2,0},{4,6},{6,4},{8,10},{10,8},{12,14},{14,12},{1,3},{3,1},... | collective-permute-start | bytes 589832 | tf_op jit(solution)/shard_map/ppermute | solution.py:311
  17.8 7.4 %copy-start.2 = (f32[512]{0:T(512)S(1)}, f32[512]{0:T(512)}, u32[]{:S(2)}) copy-start(f32[512]{0:T(512)} %param.18) | copy-start | bytes 6148
  17.8 7.4 %collective-permute-start.6 = (bf16[4,96,512]{2,1,0:T(8,128)(2,1)S(1)}, bf16[4,96,512]{2,1,0:T(8,128)(2,1)S(1)}, u32[]{:S(2)}, u32[]{:S(2)}) collective-permute-start(bf16[4,96,512]{2,1,0:T(8,128)(2,1)S(1)} %halves.1.refs_2_), channel_id=1, source_target_pairs={{0,1},{1,0},{2,3},{3,2},{4,5},{5,4},{6,7},{7,6},{8,9},{9,8},{10,11... | collective-permute-start | bytes 1179656 | tf_op jit(solution)/shard_map/ppermute | solution.py:311
  17.8 6.7 %collective-permute-start.3 = (bf16[144,128]{1,0:T(8,128)(2,1)S(1)}, bf16[144,128]{1,0:T(8,128)(2,1)S(1)}, u32[]{:S(2)}, u32[]{:S(2)}) collective-permute-start(bf16[144,128]{1,0:T(8,128)(2,1)S(1)} %get-tuple-element.33.refs_4_), channel_id=1, source_target_pairs={{0,6},{2,4},{4,2},{6,0},{8,14},{10,12},{12,10},{14,8},{1,7},{3,5},... | collective-permute-start | bytes 110600 | tf_op jit(solution)/shard_map/ppermute | solution.py:311
  20.8 4.0 %collective-permute-start.4 = (bf16[144,128]{1,0:T(8,128)(2,1)S(1)}, bf16[144,128]{1,0:T(8,128)(2,1)S(1)}, u32[]{:S(2)}, u32[]{:S(2)}) collective-permute-start(bf16[144,128]{1,0:T(8,128)(2,1)S(1)} %get-tuple-element.34), channel_id=1, source_target_pairs={{0,4},{2,6},{4,0},{6,2},{8,12},{10,14},{12,8},{14,10},{1,5},{3,7},... | collective-permute-start | bytes 110600 | tf_op jit(solution)/shard_map/ppermute | solution.py:311
  21.2 4.0 %collective-permute-start.5 = (bf16[144,128]{1,0:T(8,128)(2,1)S(1)}, bf16[144,128]{1,0:T(8,128)(2,1)S(1)}, u32[]{:S(2)}, u32[]{:S(2)}) collective-permute-start(bf16[144,128]{1,0:T(8,128)(2,1)S(1)} %get-tuple-element.35), channel_id=1, source_target_pairs={{0,2},{2,0},{4,6},{6,4},{8,10},{10,8},{12,14},{14,12},{1,3},{3,1},... | collective-permute-start | bytes 110600 | tf_op jit(solution)/shard_map/ppermute | solution.py:311
  26.0 15.3 %collective-permute-start.10 = (bf16[208,512]{1,0:T(8,128)(2,1)S(1)}, bf16[208,512]{1,0:T(8,128)(2,1)S(1)}, u32[]{:S(2)}, u32[]{:S(2)}) collective-permute-start(bf16[208,512]{1,0:T(8,128)(2,1)S(1)} %get-tuple-element.36.refs_5_), channel_id=1, source_target_pairs={{0,8},{2,10},{4,12},{6,14},{8,0},{10,2},{12,4},{14,6},{1,9},{3,11}... | collective-permute-start | bytes 638984 | tf_op jit(solution)/shard_map/ppermute | solution.py:311
  33.7 8.6 %copy-start = (bf16[512,512]{1,0:T(8,128)(2,1)S(1)}, bf16[512,512]{1,0:T(8,128)(2,1)}, u32[]{:S(2)}) copy-start(bf16[512,512]{1,0:T(8,128)(2,1)} %refs_4_.3) | copy-start | bytes 1572868
  33.8 8.6 %copy-start.1 = (bf16[512,512]{1,0:T(8,128)(2,1)S(1)}, bf16[512,512]{1,0:T(8,128)(2,1)}, u32[]{:S(2)}) copy-start(bf16[512,512]{1,0:T(8,128)(2,1)} %refs_5_.1) | copy-start | bytes 1572868
  33.8 6.3 %collective-permute-start.7 = (bf16[144,128]{1,0:T(8,128)(2,1)S(1)}, bf16[144,128]{1,0:T(8,128)(2,1)S(1)}, u32[]{:S(2)}, u32[]{:S(2)}) collective-permute-start(bf16[144,128]{1,0:T(8,128)(2,1)S(1)} %get-tuple-element.37.refs_3_), channel_id=1, source_target_pairs={{0,6},{2,4},{4,2},{6,0},{8,14},{10,12},{12,10},{14,8},{1,7},{3,5},... | collective-permute-start | bytes 110600 | tf_op jit(solution)/shard_map/ppermute | solution.py:311
  37.3 4.0 %collective-permute-start.8 = (bf16[144,128]{1,0:T(8,128)(2,1)S(1)}, bf16[144,128]{1,0:T(8,128)(2,1)S(1)}, u32[]{:S(2)}, u32[]{:S(2)}) collective-permute-start(bf16[144,128]{1,0:T(8,128)(2,1)S(1)} %get-tuple-element.38), channel_id=1, source_target_pairs={{0,4},{2,6},{4,0},{6,2},{8,12},{10,14},{12,8},{14,10},{1,5},{3,7},... | collective-permute-start | bytes 110600 | tf_op jit(solution)/shard_map/ppermute | solution.py:311
  37.3 4.0 %collective-permute-start.9 = (bf16[144,128]{1,0:T(8,128)(2,1)S(1)}, bf16[144,128]{1,0:T(8,128)(2,1)S(1)}, u32[]{:S(2)}, u32[]{:S(2)}) collective-permute-start(bf16[144,128]{1,0:T(8,128)(2,1)S(1)} %get-tuple-element.39), channel_id=1, source_target_pairs={{0,2},{2,0},{4,6},{6,4},{8,10},{10,8},{12,14},{14,12},{1,3},{3,1},... | collective-permute-start | bytes 110600 | tf_op jit(solution)/shard_map/ppermute | solution.py:311
  42.3 14.9 %copy-start.3 = (f32[512]{0:T(512)S(1)}, f32[512]{0:T(512)}, u32[]{:S(2)}) copy-start(f32[512]{0:T(512)} %param.21) | copy-start | bytes 6148
  42.3 1.4 %collective-permute-start.11 = (bf16[192,512]{1,0:T(8,128)(2,1)S(1)}, bf16[192,512]{1,0:T(8,128)(2,1)S(1)}, u32[]{:S(2)}, u32[]{:S(2)}) collective-permute-start(bf16[192,512]{1,0:T(8,128)(2,1)S(1)} %get-tuple-element.43.refs_1_), channel_id=1, source_target_pairs={{0,1},{1,0},{2,3},{3,2},{4,5},{5,4},{6,7},{7,6},{8,9},{9,8},{10,11... | collective-permute-start | bytes 589832 | tf_op jit(solution)/shard_map/ppermute | solution.py:311
  44.6 5.7 %collective-permute-start.15 = (bf16[64,512]{1,0:T(8,128)(2,1)S(1)}, bf16[64,512]{1,0:T(8,128)(2,1)S(1)}, u32[]{:S(2)}, u32[]{:S(2)}) collective-permute-start(bf16[64,512]{1,0:T(8,128)(2,1)S(1)} %get-tuple-element.50), channel_id=1, source_target_pairs={{0,6},{2,4},{4,2},{6,0},{8,14},{10,12},{12,10},{14,8},{1,7},{3,5},... | collective-permute-start | bytes 196616 | tf_op jit(solution)/shard_map/ppermute | solution.py:311
  46.1 5.5 %collective-permute-start.16 = (bf16[64,512]{1,0:T(8,128)(2,1)S(1)}, bf16[64,512]{1,0:T(8,128)(2,1)S(1)}, u32[]{:S(2)}, u32[]{:S(2)}) collective-permute-start(bf16[64,512]{1,0:T(8,128)(2,1)S(1)} %get-tuple-element.51), channel_id=1, source_target_pairs={{0,4},{2,6},{4,0},{6,2},{8,12},{10,14},{12,8},{14,10},{1,5},{3,7},... | collective-permute-start | bytes 196616 | tf_op jit(solution)/shard_map/ppermute | solution.py:311
  46.7 4.9 %collective-permute-start.17 = (bf16[64,512]{1,0:T(8,128)(2,1)S(1)}, bf16[64,512]{1,0:T(8,128)(2,1)S(1)}, u32[]{:S(2)}, u32[]{:S(2)}) collective-permute-start(bf16[64,512]{1,0:T(8,128)(2,1)S(1)} %get-tuple-element.52), channel_id=1, source_target_pairs={{0,2},{2,0},{4,6},{6,4},{8,10},{10,8},{12,14},{14,12},{1,3},{3,1},... | collective-permute-start | bytes 196616 | tf_op jit(solution)/shard_map/ppermute | solution.py:311
  48.1 5.8 %collective-permute-start.12 = (bf16[64,512]{1,0:T(8,128)(2,1)S(1)}, bf16[64,512]{1,0:T(8,128)(2,1)S(1)}, u32[]{:S(2)}, u32[]{:S(2)}) collective-permute-start(bf16[64,512]{1,0:T(8,128)(2,1)S(1)} %get-tuple-element.46), channel_id=1, source_target_pairs={{0,6},{2,4},{4,2},{6,0},{8,14},{10,12},{12,10},{14,8},{1,7},{3,5},... | collective-permute-start | bytes 196616 | tf_op jit(solution)/shard_map/ppermute | solution.py:311
  49.6 4.3 %collective-permute-start.13 = (bf16[64,512]{1,0:T(8,128)(2,1)S(1)}, bf16[64,512]{1,0:T(8,128)(2,1)S(1)}, u32[]{:S(2)}, u32[]{:S(2)}) collective-permute-start(bf16[64,512]{1,0:T(8,128)(2,1)S(1)} %get-tuple-element.47), channel_id=1, source_target_pairs={{0,4},{2,6},{4,0},{6,2},{8,12},{10,14},{12,8},{14,10},{1,5},{3,7},... | collective-permute-start | bytes 196616 | tf_op jit(solution)/shard_map/ppermute | solution.py:311
  50.2 4.3 %collective-permute-start.14 = (bf16[64,512]{1,0:T(8,128)(2,1)S(1)}, bf16[64,512]{1,0:T(8,128)(2,1)S(1)}, u32[]{:S(2)}, u32[]{:S(2)}) collective-permute-start(bf16[64,512]{1,0:T(8,128)(2,1)S(1)} %get-tuple-element.48), channel_id=1, source_target_pairs={{0,2},{2,0},{4,6},{6,4},{8,10},{10,8},{12,14},{14,12},{1,3},{3,1},... | collective-permute-start | bytes 196616 | tf_op jit(solution)/shard_map/ppermute | solution.py:311
  51.7 5.6 %collective-permute-start.18 = (bf16[64,512]{1,0:T(8,128)(2,1)S(1)}, bf16[64,512]{1,0:T(8,128)(2,1)S(1)}, u32[]{:S(2)}, u32[]{:S(2)}) collective-permute-start(bf16[64,512]{1,0:T(8,128)(2,1)S(1)} %side_sum.1), channel_id=1, source_target_pairs={{0,8},{2,10},{4,12},{6,14},{8,0},{10,2},{12,4},{14,6},{1,9},{3,11}... | collective-permute-start | bytes 196616 | tf_op jit(solution)/shard_map/ppermute | solution.py:311

commit v10 on v9

--- a/solution.py
+++ b/solution.py
@@ -29,7 +29,7 @@
 ):
     half = n_feat // 2
     parcel_refs, pick_ref = refs[:half], refs[half]
-    src_ref, seed_ref, nbr_ref, w_self_ref, w_nbr_ref, sems = refs[half + 1 :]
+    src_ref, seed_ref, nbr_ref, w_self_ref, w_nbr_ref, fetched_ref, sems = refs[half + 1 :]
     fslice = w_self_ref.shape[0]
     copies = [
         pltpu.make_async_copy(a, b, sems.at[i])
@@ -40,7 +40,7 @@
                 (nbr_hbm, nbr_ref),
                 (w_self_hbm, w_self_ref),
                 (w_nbr_hbm, w_nbr_ref),
-                (pick_hbm, pick_ref),
+                (pick_hbm, fetched_ref),
             )
         )
     ]
@@ -48,6 +48,11 @@
         copy.start()
     for copy in copies:
         copy.wait()
+    words = pick_ref.shape[1]
+    if fetched_ref.shape[1] == words:
+        pick_ref[...] = fetched_ref[...]
+    else:
+        pick_ref[...] = fetched_ref[:, :words] | (fetched_ref[:, words:] << 16)
     feat_pos = lax.axis_index("feat")
     first_core = lax.axis_index("rep") == 0
     idx = jnp.concatenate([seed_ref[...], nbr_ref[...]], axis=0)
@@ -74,7 +79,7 @@
     fslice, nodes = src_hbm.shape
     pieces = sems.shape[0]
     piece = nodes // pieces
-    width = 512
+    width = piece if piece <= 2048 else 512
     copies = [
         pltpu.make_async_copy(
             src_hbm.at[:, pl.ds(i * piece, piece)], src_ref.at[:, pl.ds(i * piece, piece)], sems.at[i]
@@ -100,7 +105,7 @@
     return jnp.max(parcel_ref[row : row + 8, lane:].astype(jnp.float32)).astype(jnp.int32)
 
 
-def mean_kernel(chosen, fanout, pcap, fslice, n_idx, nbr_hbm, table_ref, *refs):
+def mean_kernel(chosen, packed, fanout, pcap, fslice, n_idx, nbr_hbm, table_ref, *refs):
     count = len(chosen)
     out_ref, total, nbr_ref, live_ref, sems = refs[-5:]
     chunk_refs, parcel_refs = refs[-5 - count : -5], refs[: -5 - count]
@@ -128,9 +133,17 @@
 
         def group(g, inner):
             at = pl.multiple_of(g * 16, 16)
+            start = first + at
             sums = []
             for u in range(16):
-                rows = [table_ref[nbr_ref[first + k * pcap + at + u]] for k in range(fanout)]
+                names = [nbr_ref[start + (k * pcap + u)] for k in range(fanout // packed)]
+                if packed == 2:
+                    names = [
+                        part
+                        for name in names
+                        for part in (name & 0xFFFF, lax.shift_right_logical(name, 16))
+                    ]
+                rows = [table_ref[name] for name in names]
                 while len(rows) > 1:
                     rows = [a + b for a, b in zip(rows[::2], rows[1::2])] + (
                         [rows[-1]] if len(rows) % 2 else []
@@ -181,31 +194,43 @@
         refs[half][s] = refs[s][: refs[half].shape[1], :]
 
 
-def prepare_kernel(half, n_idx, *refs):
-    parcel_refs, mean_refs = refs[:half], refs[half : 2 * half]
-    other_ref, bias_ref, w_ref, pre_ref, cross_ref = refs[2 * half :]
+def own_kernel(half, n_idx, *refs):
+    parcel_refs = refs[:half]
+    other_ref, bias_ref, w_ref, pre_ref, far_ref, idx_ref = refs[half:]
     fslice = w_ref.shape[1]
     pcap, width = pre_ref.shape
     first_core = lax.axis_index("rep") == 0
     both = jnp.zeros((2 * pcap, width), jnp.float32)
-    far = jnp.zeros((pcap, width), jnp.float32)
     for s in range(half):
         mine, other = parcel_refs[s][:fslice, :], other_ref[s]
-        w_nbr = jnp.where(first_core, other, mine)
-        w_ref[s] = w_nbr
+        w_ref[s] = jnp.where(first_core, other, mine)
         feats = parcel_refs[s][fslice:, : 2 * pcap].astype(jnp.float32).T.astype(jnp.bfloat16)
         both = both + jnp.dot(
             feats, jnp.where(first_core, mine, other), preferred_element_type=jnp.float32
         )
-        far = far + jnp.dot(
-            unfold(mean_refs[s][...], fslice, pcap), w_nbr, preferred_element_type=jnp.float32
-        )
-        rows = pl.ds(pcap + s // 4 * n_idx, n_idx)
-        cross_ref[rows, s % 4 * LANES : (s % 4 + 1) * LANES] = parcel_refs[s][
+        rows = pl.ds(s // 4 * n_idx, n_idx)
+        idx_ref[rows, s % 4 * LANES : (s % 4 + 1) * LANES] = parcel_refs[s][
             fslice : fslice + n_idx, 2 * pcap :
         ]
     pre_ref[...] = both[:pcap] + bias_ref[...]
-    cross_ref[:pcap, :] = (both[pcap:] + far).astype(jnp.bfloat16)
+    far_ref[...] = both[pcap:]
+
+
+def add_means(half, pre, mean_refs, w_ref):
+    for s in range(half):
+        pre = pre + jnp.dot(
+            unfold(mean_refs[s][...], w_ref.shape[1], pre.shape[0]),
+            w_ref[s],
+            preferred_element_type=jnp.float32,
+        )
+    return pre
+
+
+def far_kernel(half, *refs):
+    far_ref, w_ref, idx_ref, cross_ref = refs[half:]
+    pcap = far_ref.shape[0]
+    cross_ref[:pcap, :] = add_means(half, far_ref[...], refs[:half], w_ref).astype(jnp.bfloat16)
+    cross_ref[pcap:, :] = idx_ref[...]
 
 
 def store_times(pcap, blocks, out_ref):
@@ -260,16 +285,14 @@
     ).astype(jnp.bfloat16)
 
 
-def layer_kernel(half, n_idx, parcel_ref, *refs):
-    mean_refs = refs[:half]
-    pre_ref, w_ref, cross_ref, hidden_ref, result_ref = refs[half:]
+def near_kernel(half, *refs):
+    pre_ref, w_ref, out_ref = refs[half:]
+    out_ref[...] = add_means(half, pre_ref[...], refs[:half], w_ref)
+
+
+def hidden_kernel(fslice, n_idx, parcel_ref, pre_ref, cross_ref, hidden_ref, result_ref):
     pcap, width = hidden_ref.shape
-    fslice = w_ref.shape[1]
     pre = pre_ref[...] + cross_ref[:pcap, :].astype(jnp.float32)
-    for s in range(half):
-        pre = pre + jnp.dot(
-            unfold(mean_refs[s][...], fslice, pcap), w_ref[s], preferred_element_type=jnp.float32
-        )
     count = live_rows(parcel_ref, fslice + n_idx, 2 * pcap)
     live = lax.broadcasted_iota(jnp.int32, (pcap, width), 0) < count
     hidden = jnp.where(live, jnp.maximum(pre, 0.0), 0.0).astype(jnp.bfloat16)
@@ -280,29 +303,38 @@
 def share_kernel(
     half, fanout_two, near_ref, far_ref, value_ref, hidden_ref, ws_ref, wn_ref, *refs
 ):
-    near_refs, far_refs, other_ref = refs[:half], refs[half : 2 * half], refs[2 * half]
+    *out_refs, other_ref = refs
     store_values(hidden_ref[...], ws_ref, wn_ref, fanout_two, other_ref)
     values = jnp.concatenate(
         [value_ref[0], other_ref[0], value_ref[1], other_ref[1]], axis=0
     )
-    for times_ref, out_refs in ((far_ref, far_refs), (near_ref, near_refs)):
+    rows = far_ref.shape[0] // half
+    both_ref, far_refs, near_refs = out_refs[0], out_refs[1:half], out_refs[half:]
+    for times_ref, refs, low in ((far_ref, far_refs, 0), (near_ref, near_refs, rows)):
         part = jnp.dot(times_ref[...], values, preferred_element_type=jnp.float32)
-        rows = out_refs[0].shape[0]
-        for s, out_ref in enumerate(out_refs):
-            out_ref[...] = part[s * rows : (s + 1) * rows].astype(jnp.bfloat16)
+        part = part.astype(jnp.bfloat16)
+        both_ref[low : low + rows, :] = part[(half - 2) * rows : (half - 1) * rows]
+        for i, ref in enumerate(refs):
+            place = i if i < half - 2 else half - 1
+            ref[...] = part[place * rows : (place + 1) * rows]
+
+
+def sum_rows(first, low, refs, rows):
+    total = first
+    for i, ref in enumerate(refs):
+        at = low if i == 0 else 0
+        total = total + ref[at : at + rows, :].astype(jnp.float32)
+    return total
 
 
 def side_sum_kernel(*refs):
-    total = refs[0][...].astype(jnp.float32)
-    for ref in refs[1:-1]:
-        total = total + ref[...].astype(jnp.float32)
-    refs[-1][...] = total.astype(jnp.bfloat16)
+    rows = refs[-1].shape[0]
+    refs[-1][...] = sum_rows(0.0, 0, refs[:-1], rows).astype(jnp.bfloat16)
 
 
 def last_kernel(bias_ref, *refs):
-    total = bias_ref[...] + refs[0][...].astype(jnp.float32)
-    for ref in refs[1:-1]:
-        total = total + ref[...].astype(jnp.float32)
+    rows = refs[-1].shape[0]
+    total = sum_rows(bias_ref[...], rows, refs[:-1], rows)
     refs[-1][...] = jnp.maximum(total, 0.0).astype(jnp.bfloat16)
 
 
@@ -359,14 +391,16 @@
     def pinned(value):
         return pltpu.with_memory_space_constraint(value, pltpu.HBM)
 
-    def send(chunks):
+    def send(chunks, steps=steps):
         return [swap(chunk, "feat", s) if s else chunk for s, chunk in zip(steps, chunks)]
 
     picks = jnp.transpose(nbr_one, (0, 2, 1, 3))
+    packed = 2 if fanout_one % 2 == 0 and nodes <= 1 << 16 else 1
+    words = (n_feat, fanout_one // packed, 1, pcap)
     *parcels, picks = call(
         functools.partial(pack_kernel, n_feat, pcap),
         "pack",
-        [((2 * fslice, width), bf16)] * half + [(picks.shape, jnp.int32)],
+        [((2 * fslice, width), bf16)] * half + [(words, jnp.int32)],
         [hbm] * 6 + [smem],
         [
             *(pinned(x) for x in (src_feats, seed_rows[None], nbr_two.T, w1_self, w1_nbr, picks)),
@@ -378,13 +412,13 @@
             pltpu.VMEM((fanout_two, seed_count), jnp.int32),
             pltpu.VMEM((fslice, width), bf16),
             pltpu.VMEM((fslice, width), bf16),
+            pltpu.VMEM((n_feat, fanout_one, 1, pcap), jnp.int32),
             pltpu.SemaphoreType.DMA((6,)),
         ],
     )
-    stride = -(-fanout_one * pcap // 1024) * 1024
-    neighbors = jnp.pad(
-        picks.reshape(n_feat, fanout_one * pcap), ((0, 0), (0, stride - fanout_one * pcap))
-    ).reshape(-1)
+    picks = picks.reshape(n_feat, -1)
+    stride = -(-picks.shape[1] // 1024) * 1024
+    neighbors = jnp.pad(picks, ((0, 0), (0, stride - picks.shape[1]))).reshape(-1)
     arrived = send(parcels)
     (table,) = call(
         turn_kernel,
@@ -403,7 +437,7 @@
     def means(chosen, parcels=(), after=()):
         count = len(chosen)
         return call(
-            functools.partial(mean_kernel, tuple(chosen), fanout_one, pcap, fslice, n_idx),
+            functools.partial(mean_kernel, tuple(chosen), packed, fanout_one, pcap, fslice, n_idx),
             "mean",
             [(chunk_shape, bf16)] * count,
             [anywhere] + [vmem] * (1 + len(parcels)),
@@ -417,7 +451,7 @@
                 pltpu.SemaphoreType.DMA((count,)),
             ],
             limit=table_bytes + 8 * MIB,
-            cost_us=2 * count if count > 1 else 0.5,
+            cost_us=2 * count if count > 1 else 0,
         )
 
     far_means = means([s + half for s in steps if s])
@@ -432,35 +466,55 @@
     far_arrived = send(far_means)
     other_halves = swap(halves, "rep", 1)
     (far_own,) = means([half], after=(halves,))
-    w_nbr, pre, cross = call(
-        functools.partial(prepare_kernel, half, n_idx),
-        "prepare",
+    idx_rows = -(-half // 4) * n_idx
+    w_nbr, pre, far_pre, idx_tags = call(
+        functools.partial(own_kernel, half, n_idx),
+        "own",
         [
             ((half, fslice, width), bf16),
             ((pcap, width), jnp.float32),
-            ((pcap + -(-half // 4) * n_idx, width), bf16),
+            ((pcap, width), jnp.float32),
+            ((idx_rows, width), bf16),
         ],
-        [vmem] * (2 * half + 2),
-        (*arrived, *far_arrived, far_own, other_halves, bias_one[None]),
+        [vmem] * (half + 2),
+        (*arrived, other_halves, bias_one[None]),
+        after=(far_own,),
+    )
+    (cross,) = call(
+        functools.partial(far_kernel, half),
+        "far",
+        [((pcap + idx_rows, width), bf16)],
+        [vmem] * (half + 3),
+        (*far_arrived, far_own, far_pre, w_nbr, idx_tags),
     )
     cross_arrived = swap(cross, "feat", half)
+    near_means = means([s for s in steps if s], arrived[:-1], (cross,))
+    near_arrived = send(near_means)
+    (near_own,) = means([0], arrived[-1:], near_means[-1:])
     (near_times,) = call(
         functools.partial(near_times_kernel, half, fslice, pcap, n_idx),
         "near_times",
         [((half * seed_count, 4 * pcap), bf16)],
         [vmem] * half,
         arrived,
-        after=far_means[:1],
-    )
-    near_means = means([s for s in steps if s], arrived[:-1], (cross, near_times))
-    near_arrived = send(near_means)
-    (near_own,) = means([0], arrived[-1:], near_means[:1])
+        after=(near_own,),
+        cost_us=0,
+    )
+    (near_pre,) = call(
+        functools.partial(near_kernel, half),
+        "near",
+        [((pcap, width), jnp.float32)],
+        [vmem] * (half + 2),
+        (*near_arrived, near_own, pre, w_nbr),
+        after=(near_times,),
+        cost_us=0,
+    )
     hidden, result = call(
-        functools.partial(layer_kernel, half, n_idx),
+        functools.partial(hidden_kernel, fslice, n_idx),
         "hidden",
         [((pcap, width), bf16)] * 2,
-        [vmem] * (half + 4),
-        (parcels[-1], *near_arrived, near_own, pre, w_nbr, cross_arrived),
+        [vmem] * 3,
+        (parcels[-1], near_pre, cross_arrived),
     )
     other_hidden = swap(hidden, "rep", 1)
     far_times, value = call(
@@ -473,23 +527,29 @@
     shares = call(
         functools.partial(share_kernel, half, fanout_two),
         "share",
-        [((seed_count, width), bf16)] * (2 * half),
+        [((2 * seed_count, width), bf16)] + [((seed_count, width), bf16)] * (2 * half - 2),
         [vmem] * 6,
         (near_times, far_times, value, other_hidden, w2_self, w2_nbr),
         scratch=[pltpu.VMEM((2, pcap, width), bf16)],
         limit=32 * MIB,
     )
-    far_shares = send(shares[half:])
-    near_shares = send(shares[:half])
+    both = swap(shares[0], "feat", 1)
+    others = [*steps[: half - 2], 0]
+    far_shares = send(shares[1:half], others)
+    near_shares = send(shares[half:], others)
     (far_sum,) = call(
-        side_sum_kernel, "side_sum", [((seed_count, width), bf16)], [vmem] * half, far_shares
+        side_sum_kernel,
+        "side_sum",
+        [((seed_count, width), bf16)],
+        [vmem] * half,
+        (both, *far_shares),
     )
     (seed_out,) = call(
         last_kernel,
         "seeds",
         [((seed_count, width), bf16)],
         [vmem] * (half + 2),
-        (bias_two[None], *near_shares, swap(far_sum, "feat", half)),
+        (bias_two[None], both, *near_shares, swap(far_sum, "feat", half)),
     )
     return (result[None, None], seed_out)
 

time: 57.9 us -> 55.5 us (0.959)
  Pallas kernels: 26 us -> 22.1 us
  waiting for transfers between devices: 6.75 us -> 8.93 us
  starting transfers between devices: 23.4 us -> 22.7 us
    pallas_call x14 -> x16, Pallas kernels: 26 us -> 22.1 us  [call(): pl.pallas_call(wrapped, out_shape=tuple((jax.ShapeDtypeStruct(shape, dtyp...]
    ppermute x19 -> x18, waiting for transfers between devices: 6.75 us -> 8.93 us  [swap(): return lax.ppermute(value, axis, [(i, i ^ step) for i in range(size)])]
    ppermute x19 -> x18, starting transfers between devices: 23.4 us -> 22.7 us  [swap(): return lax.ppermute(value, axis, [(i, i ^ step) for i in range(size)])]
  transfers between devices with their start and end apart: 19 -> 18, of which waited for: 7 -> 10; matrix products, arithmetic and copies ran while one was open for 1% -> 0% of each run, Pallas kernels for 36% -> 32%
where the time goes in v10:
time: 55.5 us; the launch traced here: 55.4 us
  starting transfers between devices  22.7 us (41%)
  Pallas kernels  22.1 us (40%)
  waiting for transfers between devices  8.93 us (16%)
  between operations  1.44 us (3%)
    ppermute x18, starting transfers between devices, swap(): return lax.ppermute(value, axis, [(i, i ^ step) for i in range(size)])  22.7 us
    pallas_call x16, Pallas kernels, call(): pl.pallas_call(wrapped, out_shape=tuple((jax.ShapeDtypeStruct(shape, dtyp...  22.1 us
    ppermute x18, waiting for transfers between devices, swap(): return lax.ppermute(value, axis, [(i, i ^ step) for i in range(size)])  8.93 us
  transfers between devices with their start and end apart: 18, of which 10 were waited for; matrix products, arithmetic and copies ran while one was open for 0% of the time, Pallas kernels for 32%

profile of v10, /device:TPU:0, one launch (start us, length us, event | category | flops | bytes accessed | tf_op | source)
XLA Modules:
  0.0 55.4 jit_solution(5305991250912558615)
XLA Ops:
  1.3 1.6 %pack.1 = (bf16[192,512]{1,0:T(8,128)(2,1)S(1)}, bf16[192,512]{1,0:T(8,128)(2,1)S(1)}, bf16[192,512]{1,0:T(8,128)(2,1)S(1)}, bf16[192,512]{1,0:T(8,128)(2,1)S(1)}, s32[8,5,1,192]{3,2,1,0:T(1,128)S(1)}) custom-call(bf16[96,12288]{1,0:T(8,128)(2,1)} %refs_0_.3, s32[1,64]{1,0:T(1,128)} %bitcast.25, s32[15,64]{1,0:T(8,128)} %bitcast.24, ...), custom_call_target="tpu_custom_call" | custom-call | flops 1100000000 | tf_op jit(solution)/shard_map/pack/pallas_call | solution.py:378
  2.9 4.0 %collective-permute-start = (bf16[192,512]{1,0:T(8,128)(2,1)S(1)}, bf16[192,512]{1,0:T(8,128)(2,1)S(1)}, u32[]{:S(2)}, u32[]{:S(2)}) collective-permute-start(bf16[192,512]{1,0:T(8,128)(2,1)S(1)} %get-tuple-element.30), channel_id=1, source_target_pairs={{0,6},{2,4},{4,2},{6,0},{8,14},{10,12},{12,10},{14,8},{1,7},{3,5},... | collective-permute-start | bytes 589832 | tf_op jit(solution)/shard_map/ppermute | solution.py:343
  7.0 0.4 collective-permute-start.1
  7.4 0.2 collective-permute-start.2
  7.6 0.1 reduce
  7.7 0.1 reshape.13
  7.8 2.3 %turn.1 = f32[12288,128]{1,0:T(8,128)S(1)} custom-call(bf16[96,12288]{1,0:T(8,128)(2,1)} %refs_0_.3, bf16[192,512]{1,0:T(8,128)(2,1)S(1)} %get-tuple-element.28.refs_1_.refs_3_.refs_2_.refs_0_, s32[8192]{0:T(1024)S(1)} %bitcast.16), custom_call_target="tpu_custom_call" | custom-call | flops 3300000000 | tf_op jit(solution)/shard_map/turn/pallas_call | solution.py:378
  10.1 5.9 %mean.4 = (bf16[144,128]{1,0:T(8,128)(2,1)S(1)}, bf16[144,128]{1,0:T(8,128)(2,1)S(1)}, bf16[144,128]{1,0:T(8,128)(2,1)S(1)}) custom-call(s32[8192]{0:T(1024)S(1)} %bitcast.17, f32[12288,1,128]{2,1,0:T(1,128)S(1)} %bitcast.12), custom_call_target="tpu_custom_call" | custom-call | flops 6600000000 | tf_op jit(solution)/shard_map/mean/pallas_call | solution.py:378
  16.0 0.0 copy-start.2
  16.0 0.0 collective-permute-done.refs_0_.refs_2_
  16.0 0.3 collective-permute-done.1.refs_1_.refs_3_
  16.3 0.0 collective-permute-done.2.refs_2_.refs_4_
  16.3 0.1 collective-permute-start.6
  16.4 2.7 %collective-permute-start.3 = (bf16[144,128]{1,0:T(8,128)(2,1)S(1)}, bf16[144,128]{1,0:T(8,128)(2,1)S(1)}, u32[]{:S(2)}, u32[]{:S(2)}) collective-permute-start(bf16[144,128]{1,0:T(8,128)(2,1)S(1)} %get-tuple-element.33.refs_4_), channel_id=1, source_target_pairs={{0,6},{2,4},{4,2},{6,0},{8,14},{10,12},{12,10},{14,8},{1,7},{3,5},... | collective-permute-start | bytes 110600 | tf_op jit(solution)/shard_map/ppermute | solution.py:343
  19.1 0.4 collective-permute-start.4
  19.5 0.4 collective-permute-start.5
  19.9 2.3 %mean.5.refs_6_.refs_3_ = bf16[144,128]{1,0:T(8,128)(2,1)S(1)} custom-call(s32[8192]{0:T(1024)S(1)} %bitcast.18, f32[12288,1,128]{2,1,0:T(1,128)S(1)} %bitcast.13, bf16[4,96,512]{2,1,0:T(8,128)(2,1)S(1)} %halves.1.refs_2_), custom_call_target="tpu_custom_call" | custom-call | tf_op jit(solution)/shard_map/mean/pallas_call | solution.py:378
  22.3 0.0 collective-permute-done.6.refs_4_
  22.3 0.0 copy-done.2
  22.3 0.6 %own.1 = (bf16[4,96,512]{2,1,0:T(8,128)(2,1)S(1)}, f32[192,512]{1,0:T(8,128)S(1)}, f32[192,512]{1,0:T(8,128)S(1)}, bf16[16,512]{1,0:T(8,128)(2,1)S(1)}) custom-call(bf16[192,512]{1,0:T(8,128)(2,1)S(1)} %collective-permute-done.refs_0_.refs_2_, bf16[192,512]{1,0:T(8,128)(2,1)S(1)} %collective-permute-done.1.refs_1_.refs_3_, ...), custom_call_target="tpu_custom_call" | custom-call | flops 1100000000 | tf_op jit(solution)/shard_map/own/pallas_call | solution.py:378
  22.9 0.1 collective-permute-done.4.refs_1_
  23.0 0.4 collective-permute-done.5.refs_2_
  23.5 0.0 collective-permute-done.3.refs_0_
  23.5 0.4 far.1.refs_5_
  23.8 2.7 %collective-permute-start.10 = (bf16[208,512]{1,0:T(8,128)(2,1)S(1)}, bf16[208,512]{1,0:T(8,128)(2,1)S(1)}, u32[]{:S(2)}, u32[]{:S(2)}) collective-permute-start(bf16[208,512]{1,0:T(8,128)(2,1)S(1)} %far.1.refs_5_), channel_id=1, source_target_pairs={{0,8},{2,10},{4,12},{6,14},{8,0},{10,2},{12,4},{14,6},{1,9},{3,11}... | collective-permute-start | bytes 638984 | tf_op jit(solution)/shard_map/ppermute | solution.py:343
  26.5 3.1 %mean.6 = (bf16[144,128]{1,0:T(8,128)(2,1)S(1)}, bf16[144,128]{1,0:T(8,128)(2,1)S(1)}, bf16[144,128]{1,0:T(8,128)(2,1)S(1)}) custom-call(s32[8192]{0:T(1024)S(1)} %bitcast.19, f32[12288,1,128]{2,1,0:T(1,128)S(1)} %bitcast.14, bf16[192,512]{1,0:T(8,128)(2,1)S(1)} %collective-permute-done.refs_0_.refs_2_, ...), custom_call_target="tpu_custom_call" | custom-call | flops 6600000000 | tf_op jit(solution)/shard_map/mean/pallas_call | solution.py:378
  29.6 2.2 %collective-permute-start.7 = (bf16[144,128]{1,0:T(8,128)(2,1)S(1)}, bf16[144,128]{1,0:T(8,128)(2,1)S(1)}, u32[]{:S(2)}, u32[]{:S(2)}) collective-permute-start(bf16[144,128]{1,0:T(8,128)(2,1)S(1)} %get-tuple-element.39), channel_id=1, source_target_pairs={{0,6},{2,4},{4,2},{6,0},{8,14},{10,12},{12,10},{14,8},{1,7},{3,5},... | collective-permute-start | bytes 110600 | tf_op jit(solution)/shard_map/ppermute | solution.py:343
  31.7 0.6 %collective-permute-start.8 = (bf16[144,128]{1,0:T(8,128)(2,1)S(1)}, bf16[144,128]{1,0:T(8,128)(2,1)S(1)}, u32[]{:S(2)}, u32[]{:S(2)}) collective-permute-start(bf16[144,128]{1,0:T(8,128)(2,1)S(1)} %get-tuple-element.40), channel_id=1, source_target_pairs={{0,4},{2,6},{4,0},{6,2},{8,12},{10,14},{12,8},{14,10},{1,5},{3,7},... | collective-permute-start | bytes 110600 | tf_op jit(solution)/shard_map/ppermute | solution.py:343
  32.3 0.0 copy-start
  32.3 0.0 copy-start.1
  32.3 0.8 %collective-permute-start.9 = (bf16[144,128]{1,0:T(8,128)(2,1)S(1)}, bf16[144,128]{1,0:T(8,128)(2,1)S(1)}, u32[]{:S(2)}, u32[]{:S(2)}) collective-permute-start(bf16[144,128]{1,0:T(8,128)(2,1)S(1)} %get-tuple-element.41.refs_3_), channel_id=1, source_target_pairs={{0,2},{2,0},{4,6},{6,4},{8,10},{10,8},{12,14},{14,12},{1,3},{3,1},... | collective-permute-start | bytes 110600 | tf_op jit(solution)/shard_map/ppermute | solution.py:343
  33.1 1.5 %mean.7.refs_4_.refs_3_ = bf16[144,128]{1,0:T(8,128)(2,1)S(1)} custom-call(s32[8192]{0:T(1024)S(1)} %bitcast.20, f32[12288,1,128]{2,1,0:T(1,128)S(1)} %bitcast.15, bf16[192,512]{1,0:T(8,128)(2,1)S(1)} %get-tuple-element.28.refs_1_.refs_3_.refs_2_.refs_0_, bf16[144,128]{1,0:T(8,128)(2,1)S(1)} %get-tuple-element.41.refs_3_), custom_call_target="tpu_custom_call" | custom-call | tf_op jit(solution)/shard_map/mean/pallas_call | solution.py:378
  34.7 0.8 %near_times.1.refs_6_.refs_0_ = bf16[256,768]{1,0:T(8,128)(2,1)S(1)} custom-call(bf16[192,512]{1,0:T(8,128)(2,1)S(1)} %collective-permute-done.refs_0_.refs_2_, bf16[192,512]{1,0:T(8,128)(2,1)S(1)} %collective-permute-done.1.refs_1_.refs_3_, bf16[192,512]{1,0:T(8,128)(2,1)S(1)} %collective-permute-done.2.refs_2_.refs_4_, ...), custom_call_target="tpu_custom_call" | custom-call | tf_op jit(solution)/shard_map/near_times/pallas_call | solution.py:378
  35.4 2.1 %collective-permute-done.7.refs_0_ = bf16[144,128]{1,0:T(8,128)(2,1)S(1)} collective-permute-done((bf16[144,128]{1,0:T(8,128)(2,1)S(1)}, bf16[144,128]{1,0:T(8,128)(2,1)S(1)}, u32[]{:S(2)}, u32[]{:S(2)}) %collective-permute-start.7) | collective-permute-done | bytes 36896 | tf_op jit(solution)/shard_map/ppermute | solution.py:343
  37.5 0.0 collective-permute-done.8.refs_1_
  37.5 0.0 collective-permute-done.9.refs_2_
  37.5 0.4 near.1.refs_1_
  37.9 0.0 collective-permute-done.10.refs_2_.refs_0_
  37.9 0.9 %hidden.1 = (bf16[192,512]{1,0:T(8,128)(2,1)S(1)}, bf16[192,512]{1,0:T(8,128)(2,1)}) custom-call(bf16[192,512]{1,0:T(8,128)(2,1)S(1)} %get-tuple-element.28.refs_1_.refs_3_.refs_2_.refs_0_, f32[192,512]{1,0:T(8,128)S(1)} %near.1.refs_1_, bf16[208,512]{1,0:T(8,128)(2,1)S(1)} %collective-permute-done.10.refs_2_.refs_0_), custom_call_target="tpu_custom_call" | custom-call | flops 1100000000 | tf_op jit(solution)/shard_map/hidden/pallas_call | solution.py:378
  38.8 0.0 copy-start.3
  38.8 0.0 collective-permute-start.11
  38.8 0.0 copy-done
  38.8 0.0 copy-done.1
  38.8 0.8 %far_times.1 = (bf16[256,768]{1,0:T(8,128)(2,1)S(1)}, bf16[2,192,512]{2,1,0:T(8,128)(2,1)S(1)}) custom-call(bf16[208,512]{1,0:T(8,128)(2,1)S(1)} %collective-permute-done.10.refs_2_.refs_0_, bf16[192,512]{1,0:T(8,128)(2,1)S(1)} %get-tuple-element.44.refs_1_, bf16[512,512]{1,0:T(8,128)(2,1)S(1)} %copy-done, bf16[512,512]{1,0:T(8,128)(2,1)S(1)} %copy-done.1), custom_call_target="tpu_custom_call" | custom-call | flops 1100000000 | tf_op jit(solution)/shard_map/far_times/pallas_call | solution.py:378
  39.6 0.6 %collective-permute-done.11.refs_3_ = bf16[192,512]{1,0:T(8,128)(2,1)S(1)} collective-permute-done((bf16[192,512]{1,0:T(8,128)(2,1)S(1)}, bf16[192,512]{1,0:T(8,128)(2,1)S(1)}, u32[]{:S(2)}, u32[]{:S(2)}) %collective-permute-start.11) | collective-permute-done | bytes 196640 | tf_op jit(solution)/shard_map/ppermute | solution.py:343
  40.2 0.8 %share.1 = (bf16[128,512]{1,0:T(8,128)(2,1)S(1)}, bf16[64,512]{1,0:T(8,128)(2,1)S(1)}, bf16[64,512]{1,0:T(8,128)(2,1)S(1)}, bf16[64,512]{1,0:T(8,128)(2,1)S(1)},...) custom-call(bf16[256,768]{1,0:T(8,128)(2,1)S(1)} %near_times.1.refs_6_.refs_0_, ...), custom_call_target="tpu_custom_call" | custom-call | flops 1100000000 | tf_op jit(solution)/shard_map/share/pallas_call | solution.py:378
  41.0 1.2 %collective-permute-start.12 = (bf16[128,512]{1,0:T(8,128)(2,1)S(1)}, bf16[128,512]{1,0:T(8,128)(2,1)S(1)}, u32[]{:S(2)}, u32[]{:S(2)}) collective-permute-start(bf16[128,512]{1,0:T(8,128)(2,1)S(1)} %get-tuple-element.47), channel_id=1, source_target_pairs={{0,2},{2,0},{4,6},{6,4},{8,10},{10,8},{12,14},{14,12},{1,3},{3,1},... | collective-permute-start | bytes 393224 | tf_op jit(solution)/shard_map/ppermute | solution.py:343
  42.2 0.5 collective-permute-start.15
  42.7 1.9 %collective-permute-start.16 = (bf16[64,512]{1,0:T(8,128)(2,1)S(1)}, bf16[64,512]{1,0:T(8,128)(2,1)S(1)}, u32[]{:S(2)}, u32[]{:S(2)}) collective-permute-start(bf16[64,512]{1,0:T(8,128)(2,1)S(1)} %get-tuple-element.52), channel_id=1, source_target_pairs={{0,4},{2,6},{4,0},{6,2},{8,12},{10,14},{12,8},{14,10},{1,5},{3,7},... | collective-permute-start | bytes 196616 | tf_op jit(solution)/shard_map/ppermute | solution.py:343
  44.6 0.8 %collective-permute-start.13 = (bf16[64,512]{1,0:T(8,128)(2,1)S(1)}, bf16[64,512]{1,0:T(8,128)(2,1)S(1)}, u32[]{:S(2)}, u32[]{:S(2)}) collective-permute-start(bf16[64,512]{1,0:T(8,128)(2,1)S(1)} %get-tuple-element.48), channel_id=1, source_target_pairs={{0,6},{2,4},{4,2},{6,0},{8,14},{10,12},{12,10},{14,8},{1,7},{3,5},... | collective-permute-start | bytes 196616 | tf_op jit(solution)/shard_map/ppermute | solution.py:343
  45.4 1.8 %collective-permute-start.14 = (bf16[64,512]{1,0:T(8,128)(2,1)S(1)}, bf16[64,512]{1,0:T(8,128)(2,1)S(1)}, u32[]{:S(2)}, u32[]{:S(2)}) collective-permute-start(bf16[64,512]{1,0:T(8,128)(2,1)S(1)} %get-tuple-element.49), channel_id=1, source_target_pairs={{0,4},{2,6},{4,0},{6,2},{8,12},{10,14},{12,8},{14,10},{1,5},{3,7},... | collective-permute-start | bytes 196616 | tf_op jit(solution)/shard_map/ppermute | solution.py:343
  47.2 0.9 %collective-permute-done.15.refs_1_ = bf16[64,512]{1,0:T(8,128)(2,1)S(1)} collective-permute-done((bf16[64,512]{1,0:T(8,128)(2,1)S(1)}, bf16[64,512]{1,0:T(8,128)(2,1)S(1)}, u32[]{:S(2)}, u32[]{:S(2)}) %collective-permute-start.15) | collective-permute-done | bytes 65568 | tf_op jit(solution)/shard_map/ppermute | solution.py:343
  48.1 0.5 collective-permute-done.16.refs_2_
  48.6 0.1 collective-permute-done.12.refs_0_.refs_1_
  48.8 2.1 %collective-permute-start.17 = (bf16[64,512]{1,0:T(8,128)(2,1)S(1)}, bf16[64,512]{1,0:T(8,128)(2,1)S(1)}, u32[]{:S(2)}, u32[]{:S(2)}) collective-permute-start(bf16[64,512]{1,0:T(8,128)(2,1)S(1)} %side_sum.1), channel_id=1, source_target_pairs={{0,8},{2,10},{4,12},{6,14},{8,0},{10,2},{12,4},{14,6},{1,9},{3,11}... | collective-permute-start | bytes 196616 | tf_op jit(solution)/shard_map/ppermute | solution.py:343
  50.8 0.0 collective-permute-done.13.refs_2_
  50.8 0.5 collective-permute-done.14.refs_3_
  51.3 3.4 %collective-permute-done.17.refs_5_ = bf16[64,512]{1,0:T(8,128)(2,1)S(1)} collective-permute-done((bf16[64,512]{1,0:T(8,128)(2,1)S(1)}, bf16[64,512]{1,0:T(8,128)(2,1)S(1)}, u32[]{:S(2)}, u32[]{:S(2)}) %collective-permute-start.17) | collective-permute-done | bytes 65568 | tf_op jit(solution)/shard_map/ppermute | solution.py:343
  54.7 0.0 copy-done.3
  54.7 0.7 %seeds.1 = bf16[64,512]{1,0:T(8,128)(2,1)} custom-call(f32[1,512]{1,0:T(1,128)S(1)} %bitcast.22, bf16[128,512]{1,0:T(8,128)(2,1)S(1)} %collective-permute-done.12.refs_0_.refs_1_, bf16[64,512]{1,0:T(8,128)(2,1)S(1)} %collective-permute-done.13.refs_2_, bf16[64,512]{1,0:T(8,128)(2,1)S(1)} %collective-permute-done.14.refs_3_, ...), custom_call_target="tpu_custom_call" | custom-call | flops 1100000000 | tf_op jit(solution)/shard_map/seeds/pallas_call | solution.py:378
  (4 shorter events, 0.1 us)
Async XLA Ops:
  2.9 13.1 %collective-permute-start = (bf16[192,512]{1,0:T(8,128)(2,1)S(1)}, bf16[192,512]{1,0:T(8,128)(2,1)S(1)}, u32[]{:S(2)}, u32[]{:S(2)}) collective-permute-start(bf16[192,512]{1,0:T(8,128)(2,1)S(1)} %get-tuple-element.30), channel_id=1, source_target_pairs={{0,6},{2,4},{4,2},{6,0},{8,14},{10,12},{12,10},{14,8},{1,7},{3,5},... | collective-permute-start | bytes 589832 | tf_op jit(solution)/shard_map/ppermute | solution.py:343
  7.0 9.3 %collective-permute-start.1 = (bf16[192,512]{1,0:T(8,128)(2,1)S(1)}, bf16[192,512]{1,0:T(8,128)(2,1)S(1)}, u32[]{:S(2)}, u32[]{:S(2)}) collective-permute-start(bf16[192,512]{1,0:T(8,128)(2,1)S(1)} %get-tuple-element.31), channel_id=1, source_target_pairs={{0,4},{2,6},{4,0},{6,2},{8,12},{10,14},{12,8},{14,10},{1,5},{3,7},... | collective-permute-start | bytes 589832 | tf_op jit(solution)/shard_map/ppermute | solution.py:343
  7.4 8.9 %collective-permute-start.2 = (bf16[192,512]{1,0:T(8,128)(2,1)S(1)}, bf16[192,512]{1,0:T(8,128)(2,1)S(1)}, u32[]{:S(2)}, u32[]{:S(2)}) collective-permute-start(bf16[192,512]{1,0:T(8,128)(2,1)S(1)} %get-tuple-element.32), channel_id=1, source_target_pairs={{0,2},{2,0},{4,6},{6,4},{8,10},{10,8},{12,14},{14,12},{1,3},{3,1},... | collective-permute-start | bytes 589832 | tf_op jit(solution)/shard_map/ppermute | solution.py:343
  16.0 6.3 %copy-start.2 = (f32[512]{0:T(512)S(1)}, f32[512]{0:T(512)}, u32[]{:S(2)}) copy-start(f32[512]{0:T(512)} %param.18) | copy-start | bytes 6148
  16.3 6.0 %collective-permute-start.6 = (bf16[4,96,512]{2,1,0:T(8,128)(2,1)S(1)}, bf16[4,96,512]{2,1,0:T(8,128)(2,1)S(1)}, u32[]{:S(2)}, u32[]{:S(2)}) collective-permute-start(bf16[4,96,512]{2,1,0:T(8,128)(2,1)S(1)} %halves.1.refs_2_), channel_id=1, source_target_pairs={{0,1},{1,0},{2,3},{3,2},{4,5},{5,4},{6,7},{7,6},{8,9},{9,8},{10,11... | collective-permute-start | bytes 1179656 | tf_op jit(solution)/shard_map/ppermute | solution.py:343
  16.4 7.1 %collective-permute-start.3 = (bf16[144,128]{1,0:T(8,128)(2,1)S(1)}, bf16[144,128]{1,0:T(8,128)(2,1)S(1)}, u32[]{:S(2)}, u32[]{:S(2)}) collective-permute-start(bf16[144,128]{1,0:T(8,128)(2,1)S(1)} %get-tuple-element.33.refs_4_), channel_id=1, source_target_pairs={{0,6},{2,4},{4,2},{6,0},{8,14},{10,12},{12,10},{14,8},{1,7},{3,5},... | collective-permute-start | bytes 110600 | tf_op jit(solution)/shard_map/ppermute | solution.py:343
  19.1 4.0 %collective-permute-start.4 = (bf16[144,128]{1,0:T(8,128)(2,1)S(1)}, bf16[144,128]{1,0:T(8,128)(2,1)S(1)}, u32[]{:S(2)}, u32[]{:S(2)}) collective-permute-start(bf16[144,128]{1,0:T(8,128)(2,1)S(1)} %get-tuple-element.34), channel_id=1, source_target_pairs={{0,4},{2,6},{4,0},{6,2},{8,12},{10,14},{12,8},{14,10},{1,5},{3,7},... | collective-permute-start | bytes 110600 | tf_op jit(solution)/shard_map/ppermute | solution.py:343
  19.5 4.0 %collective-permute-start.5 = (bf16[144,128]{1,0:T(8,128)(2,1)S(1)}, bf16[144,128]{1,0:T(8,128)(2,1)S(1)}, u32[]{:S(2)}, u32[]{:S(2)}) collective-permute-start(bf16[144,128]{1,0:T(8,128)(2,1)S(1)} %get-tuple-element.35), channel_id=1, source_target_pairs={{0,2},{2,0},{4,6},{6,4},{8,10},{10,8},{12,14},{14,12},{1,3},{3,1},... | collective-permute-start | bytes 110600 | tf_op jit(solution)/shard_map/ppermute | solution.py:343
  23.8 14.1 %collective-permute-start.10 = (bf16[208,512]{1,0:T(8,128)(2,1)S(1)}, bf16[208,512]{1,0:T(8,128)(2,1)S(1)}, u32[]{:S(2)}, u32[]{:S(2)}) collective-permute-start(bf16[208,512]{1,0:T(8,128)(2,1)S(1)} %far.1.refs_5_), channel_id=1, source_target_pairs={{0,8},{2,10},{4,12},{6,14},{8,0},{10,2},{12,4},{14,6},{1,9},{3,11}... | collective-permute-start | bytes 638984 | tf_op jit(solution)/shard_map/ppermute | solution.py:343
  29.6 8.0 %collective-permute-start.7 = (bf16[144,128]{1,0:T(8,128)(2,1)S(1)}, bf16[144,128]{1,0:T(8,128)(2,1)S(1)}, u32[]{:S(2)}, u32[]{:S(2)}) collective-permute-start(bf16[144,128]{1,0:T(8,128)(2,1)S(1)} %get-tuple-element.39), channel_id=1, source_target_pairs={{0,6},{2,4},{4,2},{6,0},{8,14},{10,12},{12,10},{14,8},{1,7},{3,5},... | collective-permute-start | bytes 110600 | tf_op jit(solution)/shard_map/ppermute | solution.py:343
  31.7 5.8 %collective-permute-start.8 = (bf16[144,128]{1,0:T(8,128)(2,1)S(1)}, bf16[144,128]{1,0:T(8,128)(2,1)S(1)}, u32[]{:S(2)}, u32[]{:S(2)}) collective-permute-start(bf16[144,128]{1,0:T(8,128)(2,1)S(1)} %get-tuple-element.40), channel_id=1, source_target_pairs={{0,4},{2,6},{4,0},{6,2},{8,12},{10,14},{12,8},{14,10},{1,5},{3,7},... | collective-permute-start | bytes 110600 | tf_op jit(solution)/shard_map/ppermute | solution.py:343
  32.3 6.5 %copy-start = (bf16[512,512]{1,0:T(8,128)(2,1)S(1)}, bf16[512,512]{1,0:T(8,128)(2,1)}, u32[]{:S(2)}) copy-start(bf16[512,512]{1,0:T(8,128)(2,1)} %refs_4_.3) | copy-start | bytes 1572868
  32.3 6.5 %copy-start.1 = (bf16[512,512]{1,0:T(8,128)(2,1)S(1)}, bf16[512,512]{1,0:T(8,128)(2,1)}, u32[]{:S(2)}) copy-start(bf16[512,512]{1,0:T(8,128)(2,1)} %refs_5_.1) | copy-start | bytes 1572868
  32.3 5.2 %collective-permute-start.9 = (bf16[144,128]{1,0:T(8,128)(2,1)S(1)}, bf16[144,128]{1,0:T(8,128)(2,1)S(1)}, u32[]{:S(2)}, u32[]{:S(2)}) collective-permute-start(bf16[144,128]{1,0:T(8,128)(2,1)S(1)} %get-tuple-element.41.refs_3_), channel_id=1, source_target_pairs={{0,2},{2,0},{4,6},{6,4},{8,10},{10,8},{12,14},{14,12},{1,3},{3,1},... | collective-permute-start | bytes 110600 | tf_op jit(solution)/shard_map/ppermute | solution.py:343
  38.8 15.9 %copy-start.3 = (f32[512]{0:T(512)S(1)}, f32[512]{0:T(512)}, u32[]{:S(2)}) copy-start(f32[512]{0:T(512)} %param.21) | copy-start | bytes 6148
  38.8 1.4 %collective-permute-start.11 = (bf16[192,512]{1,0:T(8,128)(2,1)S(1)}, bf16[192,512]{1,0:T(8,128)(2,1)S(1)}, u32[]{:S(2)}, u32[]{:S(2)}) collective-permute-start(bf16[192,512]{1,0:T(8,128)(2,1)S(1)} %get-tuple-element.44.refs_1_), channel_id=1, source_target_pairs={{0,1},{1,0},{2,3},{3,2},{4,5},{5,4},{6,7},{7,6},{8,9},{9,8},{10,11... | collective-permute-start | bytes 589832 | tf_op jit(solution)/shard_map/ppermute | solution.py:343
  41.0 7.7 %collective-permute-start.12 = (bf16[128,512]{1,0:T(8,128)(2,1)S(1)}, bf16[128,512]{1,0:T(8,128)(2,1)S(1)}, u32[]{:S(2)}, u32[]{:S(2)}) collective-permute-start(bf16[128,512]{1,0:T(8,128)(2,1)S(1)} %get-tuple-element.47), channel_id=1, source_target_pairs={{0,2},{2,0},{4,6},{6,4},{8,10},{10,8},{12,14},{14,12},{1,3},{3,1},... | collective-permute-start | bytes 393224 | tf_op jit(solution)/shard_map/ppermute | solution.py:343
  42.2 5.9 %collective-permute-start.15 = (bf16[64,512]{1,0:T(8,128)(2,1)S(1)}, bf16[64,512]{1,0:T(8,128)(2,1)S(1)}, u32[]{:S(2)}, u32[]{:S(2)}) collective-permute-start(bf16[64,512]{1,0:T(8,128)(2,1)S(1)} %get-tuple-element.51), channel_id=1, source_target_pairs={{0,6},{2,4},{4,2},{6,0},{8,14},{10,12},{12,10},{14,8},{1,7},{3,5},... | collective-permute-start | bytes 196616 | tf_op jit(solution)/shard_map/ppermute | solution.py:343
  42.7 5.9 %collective-permute-start.16 = (bf16[64,512]{1,0:T(8,128)(2,1)S(1)}, bf16[64,512]{1,0:T(8,128)(2,1)S(1)}, u32[]{:S(2)}, u32[]{:S(2)}) collective-permute-start(bf16[64,512]{1,0:T(8,128)(2,1)S(1)} %get-tuple-element.52), channel_id=1, source_target_pairs={{0,4},{2,6},{4,0},{6,2},{8,12},{10,14},{12,8},{14,10},{1,5},{3,7},... | collective-permute-start | bytes 196616 | tf_op jit(solution)/shard_map/ppermute | solution.py:343
  44.6 6.3 %collective-permute-start.13 = (bf16[64,512]{1,0:T(8,128)(2,1)S(1)}, bf16[64,512]{1,0:T(8,128)(2,1)S(1)}, u32[]{:S(2)}, u32[]{:S(2)}) collective-permute-start(bf16[64,512]{1,0:T(8,128)(2,1)S(1)} %get-tuple-element.48), channel_id=1, source_target_pairs={{0,6},{2,4},{4,2},{6,0},{8,14},{10,12},{12,10},{14,8},{1,7},{3,5},... | collective-permute-start | bytes 196616 | tf_op jit(solution)/shard_map/ppermute | solution.py:343
  45.4 5.9 %collective-permute-start.14 = (bf16[64,512]{1,0:T(8,128)(2,1)S(1)}, bf16[64,512]{1,0:T(8,128)(2,1)S(1)}, u32[]{:S(2)}, u32[]{:S(2)}) collective-permute-start(bf16[64,512]{1,0:T(8,128)(2,1)S(1)} %get-tuple-element.49), channel_id=1, source_target_pairs={{0,4},{2,6},{4,0},{6,2},{8,12},{10,14},{12,8},{14,10},{1,5},{3,7},... | collective-permute-start | bytes 196616 | tf_op jit(solution)/shard_map/ppermute | solution.py:343
  48.8 5.9 %collective-permute-start.17 = (bf16[64,512]{1,0:T(8,128)(2,1)S(1)}, bf16[64,512]{1,0:T(8,128)(2,1)S(1)}, u32[]{:S(2)}, u32[]{:S(2)}) collective-permute-start(bf16[64,512]{1,0:T(8,128)(2,1)S(1)} %side_sum.1), channel_id=1, source_target_pairs={{0,8},{2,10},{4,12},{6,14},{8,0},{10,2},{12,4},{14,6},{1,9},{3,11}... | collective-permute-start | bytes 196616 | tf_op jit(solution)/shard_map/ppermute | solution.py:343

commit v11 on v10

--- a/solution.py
+++ b/solution.py
@@ -13,6 +13,53 @@
 
 def folds(fslice, pcap):
     return 4 * fslice == 3 * LANES and pcap % 64 == 0
+
+
+def is_dense(fslice, n_idx):
+    return fslice % 32 == 0 and n_idx == 16
+
+
+def parcel_rows(fslice, n_idx):
+    return 2 * fslice - fslice // 4 + 8 if is_dense(fslice, n_idx) else 2 * fslice
+
+
+def write_parcel(ref, weight, feats, digits, live):
+    fslice, lanes = feats.shape
+    ref[:fslice, :] = weight
+    if is_dense(fslice, digits.shape[0]):
+        cut = fslice // 4 * 3
+        tail = jnp.concatenate([feats[cut:, i : i + LANES] for i in range(0, lanes, LANES)], axis=0)
+        tags = jnp.concatenate([digits[:8], digits[8:], live, live], axis=1)
+        body = jnp.concatenate([feats[:cut], tail], axis=1)
+        ref[fslice:, :] = jnp.concatenate([body, tags], axis=0).astype(jnp.bfloat16)
+    else:
+        tags = jnp.concatenate([digits, live], axis=0).astype(jnp.bfloat16)
+        ref[fslice:, :lanes] = feats.astype(jnp.bfloat16)
+        ref[fslice : fslice + tags.shape[0], lanes:] = tags
+
+
+def read_feats(ref, fslice, n_idx, lanes):
+    if not is_dense(fslice, n_idx):
+        return ref[fslice:, :lanes].astype(jnp.float32)
+    cut, part = fslice // 4 * 3, fslice // 4
+    tail = ref[fslice : fslice + cut, lanes:].astype(jnp.float32)
+    tail = jnp.concatenate([tail[i : i + part] for i in range(0, cut, part)], axis=1)
+    return jnp.concatenate([ref[fslice : fslice + cut, :lanes].astype(jnp.float32), tail], axis=0)
+
+
+def read_digits(ref, fslice, n_idx, lanes):
+    if not is_dense(fslice, n_idx):
+        return ref[fslice : fslice + n_idx, lanes:].astype(jnp.float32)
+    tags = ref[-8:, : 2 * LANES].astype(jnp.float32)
+    return jnp.concatenate([tags[:, :LANES], tags[:, LANES:]], axis=0)
+
+
+def live_rows(ref, fslice, n_idx, lanes):
+    if is_dense(fslice, n_idx):
+        tag = ref[-8:, 2 * LANES : 3 * LANES]
+    else:
+        tag = ref[fslice + n_idx : fslice + n_idx + 8, lanes:]
+    return jnp.max(tag.astype(jnp.float32)).astype(jnp.int32)
 
 
 def pack_kernel(
@@ -28,115 +75,96 @@
     *refs,
 ):
     half = n_feat // 2
-    parcel_refs, pick_ref = refs[:half], refs[half]
-    src_ref, seed_ref, nbr_ref, w_self_ref, w_nbr_ref, fetched_ref, sems = refs[half + 1 :]
-    fslice = w_self_ref.shape[0]
+    parcel_refs, pick_ref, src_ref = refs[:half], refs[half], refs[half + 1]
+    seed_ref, nbr_ref, w_self_ref, w_nbr_ref, fetched_ref, sems = refs[half + 2 :]
+    owned = n_feat * 2 * pcap
+    first, rest = pl.ds(0, owned), pl.ds(owned, src_ref.shape[1] - owned)
     copies = [
         pltpu.make_async_copy(a, b, sems.at[i])
         for i, (a, b) in enumerate(
             (
-                (src_hbm.at[:, pl.ds(0, src_ref.shape[1])], src_ref),
+                (src_hbm.at[:, first], src_ref.at[:, first]),
+                (w_self_hbm, w_self_ref),
+                (w_nbr_hbm, w_nbr_ref),
                 (seed_hbm, seed_ref),
                 (nbr_hbm, nbr_ref),
-                (w_self_hbm, w_self_ref),
-                (w_nbr_hbm, w_nbr_ref),
                 (pick_hbm, fetched_ref),
+                (src_hbm.at[:, rest], src_ref.at[:, rest]),
             )
         )
     ]
     for copy in copies:
         copy.start()
-    for copy in copies:
+    for copy in copies[:-1]:
         copy.wait()
     words = pick_ref.shape[1]
     if fetched_ref.shape[1] == words:
-        pick_ref[...] = fetched_ref[...]
+        pick_ref[:, :, :, :pcap] = fetched_ref[...]
     else:
-        pick_ref[...] = fetched_ref[:, :words] | (fetched_ref[:, words:] << 16)
+        pick_ref[:, :, :, :pcap] = fetched_ref[:, :words] | (fetched_ref[:, words:] << 16)
     feat_pos = lax.axis_index("feat")
     first_core = lax.axis_index("rep") == 0
     idx = jnp.concatenate([seed_ref[...], nbr_ref[...]], axis=0)
     high = lax.shift_right_logical(idx, 7)
     digits = jnp.concatenate([high, idx - high * 128], axis=1).astype(jnp.float32)
-    digits = digits.astype(jnp.bfloat16)
     weight = jnp.where(first_core, w_self_ref[...], w_nbr_ref[...])
-    live = jnp.full((8, LANES), live_ref[0, 0].astype(jnp.float32)).astype(jnp.bfloat16)
-    tags = jnp.concatenate([digits, live], axis=0)
+    live = jnp.full((8, LANES), live_ref[0, 0].astype(jnp.float32))
     for s, parcel_ref in enumerate(reversed(parcel_refs)):
-        parcel_ref[:fslice, :] = weight
-        for place, step in enumerate((s, s ^ half)):
+        sides = []
+        for step in (s, s ^ half):
             at = pl.multiple_of(jnp.bitwise_xor(feat_pos, step) * (2 * pcap), LANES)
             block = src_ref[:, pl.ds(at, 2 * pcap)].astype(jnp.float32)
-            own = jnp.where(first_core, block[:, :pcap], block[:, pcap:])
-            if place == 0:
-                near_side = own
-        both = jnp.concatenate([near_side, own], axis=1)
-        parcel_ref[fslice:, : 2 * pcap] = both.astype(jnp.bfloat16)
-        parcel_ref[fslice : fslice + tags.shape[0], 2 * pcap :] = tags
-
-
-def turn_kernel(src_hbm, table_ref, src_ref, sems):
-    fslice, nodes = src_hbm.shape
-    pieces = sems.shape[0]
-    piece = nodes // pieces
-    width = piece if piece <= 2048 else 512
-    copies = [
-        pltpu.make_async_copy(
-            src_hbm.at[:, pl.ds(i * piece, piece)], src_ref.at[:, pl.ds(i * piece, piece)], sems.at[i]
-        )
-        for i in range(pieces)
-    ]
-    for copy in copies:
-        copy.start()
-    for i, copy in enumerate(copies):
-        copy.wait()
-
-        def turn(step, carry):
-            at = pl.multiple_of(i * piece + step * width, width)
-            table_ref[pl.ds(at, width), :fslice] = src_ref[:, pl.ds(at, width)].T.astype(
-                jnp.float32
-            )
-            return carry
-
-        lax.fori_loop(0, piece // width, turn, 0)
-
-
-def live_rows(parcel_ref, row, lane):
-    return jnp.max(parcel_ref[row : row + 8, lane:].astype(jnp.float32)).astype(jnp.int32)
-
-
-def mean_kernel(chosen, packed, fanout, pcap, fslice, n_idx, nbr_hbm, table_ref, *refs):
+            sides.append(jnp.where(first_core, block[:, :pcap], block[:, pcap:]))
+        write_parcel(parcel_ref, weight, jnp.concatenate(sides, axis=1), digits, live)
+    copies[-1].wait()
+
+
+def turn_kernel(src_ref, table_ref):
+    fslice, nodes = src_ref.shape
+    width = 2048 if nodes % 2048 == 0 else 512
+
+    def turn(step, carry):
+        at = pl.multiple_of(step * width, width)
+        table_ref[pl.ds(at, width), :fslice] = src_ref[:, pl.ds(at, width)].T.astype(jnp.float32)
+        return carry
+
+    lax.fori_loop(0, nodes // width, turn, 0)
+
+
+def mean_kernel(chosen, packed, fanout, pcap, fslice, n_idx, nbr_any, table_ref, *refs):
     count = len(chosen)
     out_ref, total, nbr_ref, live_ref, sems = refs[-5:]
     chunk_refs, parcel_refs = refs[-5 - count : -5], refs[: -5 - count]
     feat_pos = lax.axis_index("feat")
-    stride = nbr_ref.shape[0] // count
+    words = fanout // packed
+    stride = -(-pcap // LANES) * LANES
     copies = [
         pltpu.make_async_copy(
-            nbr_hbm.at[pl.ds(pl.multiple_of((feat_pos ^ step) * stride, stride), stride)],
-            nbr_ref.at[pl.ds(i * stride, stride)],
-            sems.at[i],
+            nbr_any.at[feat_pos ^ step, k, 0],
+            nbr_ref.at[pl.ds((i * words + k) * stride, stride)],
+            sems.at[i * words + k],
         )
         for i, step in enumerate(chosen)
+        for k in range(words)
     ]
     for copy in copies:
         copy.start()
     for i in range(count):
         live_ref[i] = pcap
     for i, ref in enumerate(parcel_refs):
-        live_ref[i] = live_rows(ref, fslice + n_idx, 2 * pcap)
+        live_ref[i] = live_rows(ref, fslice, n_idx, 2 * pcap)
     for copy in copies:
         copy.wait()
 
     def partition(i, carry):
-        first = i * stride
+        first = i * (words * stride)
 
         def group(g, inner):
             at = pl.multiple_of(g * 16, 16)
             start = first + at
             sums = []
             for u in range(16):
-                names = [nbr_ref[start + (k * pcap + u)] for k in range(fanout // packed)]
+                names = [nbr_ref[start + (k * stride + u)] for k in range(words)]
                 if packed == 2:
                     names = [
                         part
@@ -204,14 +232,13 @@
     for s in range(half):
         mine, other = parcel_refs[s][:fslice, :], other_ref[s]
         w_ref[s] = jnp.where(first_core, other, mine)
-        feats = parcel_refs[s][fslice:, : 2 * pcap].astype(jnp.float32).T.astype(jnp.bfloat16)
+        feats = read_feats(parcel_refs[s], fslice, n_idx, 2 * pcap).T.astype(jnp.bfloat16)
         both = both + jnp.dot(
             feats, jnp.where(first_core, mine, other), preferred_element_type=jnp.float32
         )
         rows = pl.ds(s // 4 * n_idx, n_idx)
-        idx_ref[rows, s % 4 * LANES : (s % 4 + 1) * LANES] = parcel_refs[s][
-            fslice : fslice + n_idx, 2 * pcap :
-        ]
+        digits = read_digits(parcel_refs[s], fslice, n_idx, 2 * pcap)
+        idx_ref[rows, s % 4 * LANES : (s % 4 + 1) * LANES] = digits.astype(jnp.bfloat16)
     pre_ref[...] = both[:pcap] + bias_ref[...]
     far_ref[...] = both[pcap:]
 
@@ -258,13 +285,25 @@
 
 
 def near_times_kernel(half, fslice, pcap, n_idx, *refs):
-    blocks = [ref[fslice : fslice + n_idx, 2 * pcap :] for ref in refs[:half]]
+    blocks = [read_digits(ref, fslice, n_idx, 2 * pcap) for ref in refs[:half]]
     store_times(pcap, blocks, refs[half])
 
 
 def far_times_kernel(
-    half, n_idx, fanout_two, cross_ref, hidden_ref, ws_ref, wn_ref, out_ref, value_ref
+    half,
+    n_idx,
+    fanout_two,
+    cross_ref,
+    hidden_ref,
+    ws_ref,
+    wn_ref,
+    out_ref,
+    value_ref,
+    result_ref,
+    sem,
 ):
+    copy = pltpu.make_async_copy(hidden_ref, result_ref, sem)
+    copy.start()
     pcap = hidden_ref.shape[0]
     blocks = [
         cross_ref[
@@ -274,6 +313,7 @@
     ]
     store_times(pcap, blocks, out_ref)
     store_values(hidden_ref[...], ws_ref, wn_ref, fanout_two, value_ref)
+    copy.wait()
 
 
 def store_values(hidden, ws_ref, wn_ref, fanout_two, value_ref):
@@ -290,14 +330,12 @@
     out_ref[...] = add_means(half, pre_ref[...], refs[:half], w_ref)
 
 
-def hidden_kernel(fslice, n_idx, parcel_ref, pre_ref, cross_ref, hidden_ref, result_ref):
+def hidden_kernel(fslice, n_idx, parcel_ref, pre_ref, cross_ref, hidden_ref):
     pcap, width = hidden_ref.shape
     pre = pre_ref[...] + cross_ref[:pcap, :].astype(jnp.float32)
-    count = live_rows(parcel_ref, fslice + n_idx, 2 * pcap)
+    count = live_rows(parcel_ref, fslice, n_idx, 2 * pcap)
     live = lax.broadcasted_iota(jnp.int32, (pcap, width), 0) < count
-    hidden = jnp.where(live, jnp.maximum(pre, 0.0), 0.0).astype(jnp.bfloat16)
-    hidden_ref[...] = hidden
-    result_ref[...] = hidden
+    hidden_ref[...] = jnp.where(live, jnp.maximum(pre, 0.0), 0.0).astype(jnp.bfloat16)
 
 
 def share_kernel(
@@ -371,7 +409,7 @@
     anywhere = pl.BlockSpec(memory_space=pl.ANY)
     table_bytes = nodes * LANES * 4
 
-    def call(kernel, name, shapes, ins, args, after=(), scratch=(), limit=16 * MIB, cost_us=1):
+    def call(kernel, name, shapes, ins, args, after=(), scratch=(), limit=16 * MIB, cost_us=1, outs=None):
         def wrapped(*refs):
             kernel(*refs[: len(args)], *refs[len(args) + len(after) :])
 
@@ -379,7 +417,7 @@
             wrapped,
             out_shape=tuple(jax.ShapeDtypeStruct(shape, dtype) for shape, dtype in shapes),
             in_specs=[*ins, *([anywhere] * len(after))],
-            out_specs=(vmem,) * len(shapes),
+            out_specs=outs or (vmem,) * len(shapes),
             scratch_shapes=scratch,
             compiler_params=pltpu.CompilerParams(vmem_limit_bytes=limit),
             cost_estimate=pl.CostEstimate(
@@ -396,38 +434,34 @@
 
     picks = jnp.transpose(nbr_one, (0, 2, 1, 3))
     packed = 2 if fanout_one % 2 == 0 and nodes <= 1 << 16 else 1
-    words = (n_feat, fanout_one // packed, 1, pcap)
-    *parcels, picks = call(
+    words = (n_feat, fanout_one // packed, 1, -(-pcap // LANES) * LANES)
+    *parcels, picks, feats = call(
         functools.partial(pack_kernel, n_feat, pcap),
         "pack",
-        [((2 * fslice, width), bf16)] * half + [(words, jnp.int32)],
+        [((parcel_rows(fslice, n_idx), width), bf16)] * half
+        + [(words, jnp.int32), ((fslice, nodes), bf16)],
         [hbm] * 6 + [smem],
         [
             *(pinned(x) for x in (src_feats, seed_rows[None], nbr_two.T, w1_self, w1_nbr, picks)),
             counts,
         ],
         scratch=[
-            pltpu.VMEM((fslice, n_feat * 2 * pcap), bf16),
             pltpu.VMEM((1, seed_count), jnp.int32),
             pltpu.VMEM((fanout_two, seed_count), jnp.int32),
             pltpu.VMEM((fslice, width), bf16),
             pltpu.VMEM((fslice, width), bf16),
             pltpu.VMEM((n_feat, fanout_one, 1, pcap), jnp.int32),
-            pltpu.SemaphoreType.DMA((6,)),
+            pltpu.SemaphoreType.DMA((7,)),
         ],
-    )
-    picks = picks.reshape(n_feat, -1)
-    stride = -(-picks.shape[1] // 1024) * 1024
-    neighbors = jnp.pad(picks, ((0, 0), (0, stride - picks.shape[1]))).reshape(-1)
+        limit=32 * MIB,
+    )
     arrived = send(parcels)
     (table,) = call(
         turn_kernel,
         "turn",
         [((nodes, LANES), jnp.float32)],
-        [hbm],
-        (pinned(src_feats),),
-        after=(parcels[-1], neighbors),
-        scratch=[pltpu.VMEM((fslice, nodes), bf16), pltpu.SemaphoreType.DMA((6,))],
+        [vmem],
+        (feats,),
         limit=table_bytes + 12 * MIB,
         cost_us=3,
     )
@@ -441,14 +475,14 @@
             "mean",
             [(chunk_shape, bf16)] * count,
             [anywhere] + [vmem] * (1 + len(parcels)),
-            (neighbors, table, *parcels),
+            (picks, table, *parcels),
             after=after,
             scratch=[
                 pltpu.VMEM((count, *chunk_shape), bf16),
                 pltpu.VMEM((pcap, LANES), jnp.float32),
-                pltpu.SMEM((count * stride,), jnp.int32),
+                pltpu.SMEM((count * words[1] * words[3],), jnp.int32),
                 pltpu.SMEM((count,), jnp.int32),
-                pltpu.SemaphoreType.DMA((count,)),
+                pltpu.SemaphoreType.DMA((count * words[1],)),
             ],
             limit=table_bytes + 8 * MIB,
             cost_us=2 * count if count > 1 else 0,
@@ -509,20 +543,26 @@
         after=(near_times,),
         cost_us=0,
     )
-    hidden, result = call(
+    (hidden,) = call(
         functools.partial(hidden_kernel, fslice, n_idx),
         "hidden",
-        [((pcap, width), bf16)] * 2,
+        [((pcap, width), bf16)],
         [vmem] * 3,
         (parcels[-1], near_pre, cross_arrived),
     )
     other_hidden = swap(hidden, "rep", 1)
-    far_times, value = call(
+    far_times, value, result = call(
         functools.partial(far_times_kernel, half, n_idx, fanout_two),
         "far_times",
-        [((half * seed_count, 4 * pcap), bf16), ((2, pcap, width), bf16)],
+        [
+            ((half * seed_count, 4 * pcap), bf16),
+            ((2, pcap, width), bf16),
+            ((pcap, width), bf16),
+        ],
         [vmem] * 4,
         (cross_arrived, hidden, w2_self, w2_nbr),
+        scratch=[pltpu.SemaphoreType.DMA],
+        outs=(vmem, vmem, anywhere),
     )
     shares = call(
         functools.partial(share_kernel, half, fanout_two),

time: 55.5 us -> 54.8 us (0.987)
  waiting for transfers between devices: 8.93 us -> 6.83 us
  local copies, waits for them, and re-layouts: 0.11 us -> 0.93 us
  starting transfers between devices: 22.7 us -> 23.5 us
    ppermute x18, waiting for transfers between devices: 8.93 us -> 6.83 us  [swap(): return lax.ppermute(value, axis, [(i, i ^ step) for i in range(size)])]
    unnamed x10 -> x8, local copies, waits for them, and re-layouts: 0.04 us -> 0.93 us
    ppermute x18, starting transfers between devices: 22.7 us -> 23.5 us  [swap(): return lax.ppermute(value, axis, [(i, i ^ step) for i in range(size)])]
  transfers between devices with their start and end apart: 18 -> 18, of which waited for: 10 -> 8; matrix products, arithmetic and copies ran while one was open for 0% -> 0% of each run, Pallas kernels for 32% -> 33%
where the time goes in v11:
time: 54.8 us; the launch traced here: 54.4 us
  starting transfers between devices  23.5 us (43%)
  Pallas kernels  21.7 us (40%)
  waiting for transfers between devices  6.83 us (12%)
  between operations  1.48 us (3%)
  local copies, waits for them, and re-layouts  0.93 us (2%)
    ppermute x18, starting transfers between devices, swap(): return lax.ppermute(value, axis, [(i, i ^ step) for i in range(size)])  23.5 us
    pallas_call x16, Pallas kernels, call(): pl.pallas_call(wrapped, out_shape=tuple((jax.ShapeDtypeStruct(shape, dtyp...  21.7 us
    ppermute x18, waiting for transfers between devices, swap(): return lax.ppermute(value, axis, [(i, i ^ step) for i in range(size)])  6.83 us
  transfers between devices with their start and end apart: 18, of which 8 were waited for; matrix products, arithmetic and copies ran while one was open for 0% of the time, Pallas kernels for 33%

profile of v11, /device:TPU:0, one launch (start us, length us, event | category | flops | bytes accessed | tf_op | source)
XLA Modules:
  0.0 54.4 jit_solution(9799061578205205466)
XLA Ops:
  1.3 1.8 %pack.1 = (bf16[176,512]{1,0:T(8,128)(2,1)S(1)}, bf16[176,512]{1,0:T(8,128)(2,1)S(1)}, bf16[176,512]{1,0:T(8,128)(2,1)S(1)}, bf16[176,512]{1,0:T(8,128)(2,1)S(1)...) custom-call(bf16[96,12288]{1,0:T(8,128)(2,1)} %refs_0_.1, s32[1,64]{1,0:T(1,128)} %bitcast.15, ...), custom_call_target="tpu_custom_call" | custom-call | flops 1100000000 | tf_op jit(solution)/shard_map/pack/pallas_call | solution.py:416
  3.1 4.0 %collective-permute-start.3 = (bf16[176,512]{1,0:T(8,128)(2,1)S(1)}, bf16[176,512]{1,0:T(8,128)(2,1)S(1)}, u32[]{:S(2)}, u32[]{:S(2)}) collective-permute-start(bf16[176,512]{1,0:T(8,128)(2,1)S(1)} %get-tuple-element.33), channel_id=1, source_target_pairs={{0,6},{2,4},{4,2},{6,0},{8,14},{10,12},{12,10},{14,8},{1,7},{3,5},... | collective-permute-start | bytes 540680 | tf_op jit(solution)/shard_map/ppermute | solution.py:381
  7.2 0.4 collective-permute-start.4
  7.6 0.2 collective-permute-start.5
  7.8 1.2 %turn.1 = f32[12288,128]{1,0:T(8,128)S(1)} custom-call(bf16[96,12288]{1,0:T(8,128)(2,1)S(1)} %get-tuple-element.29.refs_0_), custom_call_target="tpu_custom_call" | custom-call | flops 3300000000 | tf_op jit(solution)/shard_map/turn/pallas_call | solution.py:416
  9.0 6.1 %mean.4 = (bf16[144,128]{1,0:T(8,128)(2,1)S(1)}, bf16[144,128]{1,0:T(8,128)(2,1)S(1)}, bf16[144,128]{1,0:T(8,128)(2,1)S(1)}) custom-call(s32[8,5,1,256]{3,2,1,0:T(1,128)S(1)} %get-tuple-element.28.refs_0_, f32[12288,1,128]{2,1,0:T(1,128)S(1)} %bitcast.7), custom_call_target="tpu_custom_call" | custom-call | flops 6600000000 | tf_op jit(solution)/shard_map/mean/pallas_call | solution.py:416
  15.1 0.0 collective-permute-done.3.refs_0_.refs_2_
  15.1 0.7 %collective-permute-done.4.refs_1_.refs_3_ = bf16[176,512]{1,0:T(8,128)(2,1)S(1)} collective-permute-done((bf16[176,512]{1,0:T(8,128)(2,1)S(1)}, bf16[176,512]{1,0:T(8,128)(2,1)S(1)}, u32[]{:S(2)}, u32[]{:S(2)}) %collective-permute-start.4) | collective-permute-done | bytes 180256 | tf_op jit(solution)/shard_map/ppermute | solution.py:381
  15.8 0.0 collective-permute-done.5.refs_2_.refs_4_
  15.8 0.1 collective-permute-start.6
  15.9 2.5 %collective-permute-start = (bf16[144,128]{1,0:T(8,128)(2,1)S(1)}, bf16[144,128]{1,0:T(8,128)(2,1)S(1)}, u32[]{:S(2)}, u32[]{:S(2)}) collective-permute-start(bf16[144,128]{1,0:T(8,128)(2,1)S(1)} %get-tuple-element.30.refs_4_), channel_id=1, source_target_pairs={{0,6},{2,4},{4,2},{6,0},{8,14},{10,12},{12,10},{14,8},{1,7},{3,5},... | collective-permute-start | bytes 110600 | tf_op jit(solution)/shard_map/ppermute | solution.py:381
  18.4 0.4 collective-permute-start.1
  18.9 0.0 copy-start.2
  18.9 0.6 %collective-permute-start.2 = (bf16[144,128]{1,0:T(8,128)(2,1)S(1)}, bf16[144,128]{1,0:T(8,128)(2,1)S(1)}, u32[]{:S(2)}, u32[]{:S(2)}) collective-permute-start(bf16[144,128]{1,0:T(8,128)(2,1)S(1)} %get-tuple-element.32), channel_id=1, source_target_pairs={{0,2},{2,0},{4,6},{6,4},{8,10},{10,8},{12,14},{14,12},{1,3},{3,1},... | collective-permute-start | bytes 110600 | tf_op jit(solution)/shard_map/ppermute | solution.py:381
  19.5 2.4 %mean.5.refs_6_.refs_3_ = bf16[144,128]{1,0:T(8,128)(2,1)S(1)} custom-call(s32[8,5,1,256]{3,2,1,0:T(1,128)S(1)} %get-tuple-element.28.refs_0_, f32[12288,1,128]{2,1,0:T(1,128)S(1)} %bitcast.8, bf16[4,96,512]{2,1,0:T(8,128)(2,1)S(1)} %halves.1.refs_2_), custom_call_target="tpu_custom_call" | custom-call | tf_op jit(solution)/shard_map/mean/pallas_call | solution.py:416
  21.8 0.0 collective-permute-done.6.refs_4_
  21.9 0.0 copy-done.2
  21.9 0.6 %own.1 = (bf16[4,96,512]{2,1,0:T(8,128)(2,1)S(1)}, f32[192,512]{1,0:T(8,128)S(1)}, f32[192,512]{1,0:T(8,128)S(1)}, bf16[16,512]{1,0:T(8,128)(2,1)S(1)}) custom-call(bf16[176,512]{1,0:T(8,128)(2,1)S(1)} %collective-permute-done.3.refs_0_.refs_2_, bf16[176,512]{1,0:T(8,128)(2,1)S(1)} %collective-permute-done.4.refs_1_.refs_3_, ...), custom_call_target="tpu_custom_call" | custom-call | flops 1100000000 | tf_op jit(solution)/shard_map/own/pallas_call | solution.py:416
  22.5 0.0 collective-permute-done.1.refs_1_
  22.5 0.3 collective-permute-done.2.refs_2_
  22.8 0.0 collective-permute-done.refs_0_
  22.8 0.4 far.1.refs_5_
  23.2 2.6 %collective-permute-start.7 = (bf16[208,512]{1,0:T(8,128)(2,1)S(1)}, bf16[208,512]{1,0:T(8,128)(2,1)S(1)}, u32[]{:S(2)}, u32[]{:S(2)}) collective-permute-start(bf16[208,512]{1,0:T(8,128)(2,1)S(1)} %far.1.refs_5_), channel_id=1, source_target_pairs={{0,8},{2,10},{4,12},{6,14},{8,0},{10,2},{12,4},{14,6},{1,9},{3,11}... | collective-permute-start | bytes 638984 | tf_op jit(solution)/shard_map/ppermute | solution.py:381
  25.8 3.4 %mean.6 = (bf16[144,128]{1,0:T(8,128)(2,1)S(1)}, bf16[144,128]{1,0:T(8,128)(2,1)S(1)}, bf16[144,128]{1,0:T(8,128)(2,1)S(1)}) custom-call(s32[8,5,1,256]{3,2,1,0:T(1,128)S(1)} %get-tuple-element.28.refs_0_, f32[12288,1,128]{2,1,0:T(1,128)S(1)} %bitcast.9, bf16[176,512]{1,0:T(8,128)(2,1)S(1)} %collective-permute-done.3.refs_0_.refs_2_, ...), custom_call_target="tpu_custom_call" | custom-call | flops 6600000000 | tf_op jit(solution)/shard_map/mean/pallas_call | solution.py:416
  29.2 2.7 %collective-permute-start.8 = (bf16[144,128]{1,0:T(8,128)(2,1)S(1)}, bf16[144,128]{1,0:T(8,128)(2,1)S(1)}, u32[]{:S(2)}, u32[]{:S(2)}) collective-permute-start(bf16[144,128]{1,0:T(8,128)(2,1)S(1)} %get-tuple-element.40), channel_id=1, source_target_pairs={{0,6},{2,4},{4,2},{6,0},{8,14},{10,12},{12,10},{14,8},{1,7},{3,5},... | collective-permute-start | bytes 110600 | tf_op jit(solution)/shard_map/ppermute | solution.py:381
  32.0 0.4 collective-permute-start.9
  32.4 0.8 %collective-permute-start.10 = (bf16[144,128]{1,0:T(8,128)(2,1)S(1)}, bf16[144,128]{1,0:T(8,128)(2,1)S(1)}, u32[]{:S(2)}, u32[]{:S(2)}) collective-permute-start(bf16[144,128]{1,0:T(8,128)(2,1)S(1)} %get-tuple-element.42.refs_3_), channel_id=1, source_target_pairs={{0,2},{2,0},{4,6},{6,4},{8,10},{10,8},{12,14},{14,12},{1,3},{3,1},... | collective-permute-start | bytes 110600 | tf_op jit(solution)/shard_map/ppermute | solution.py:381
  33.2 2.1 %mean.7.refs_4_.refs_3_ = bf16[144,128]{1,0:T(8,128)(2,1)S(1)} custom-call(s32[8,5,1,256]{3,2,1,0:T(1,128)S(1)} %get-tuple-element.28.refs_0_, f32[12288,1,128]{2,1,0:T(1,128)S(1)} %bitcast.10, bf16[176,512]{1,0:T(8,128)(2,1)S(1)} %get-tuple-element.36.refs_3_.refs_2_.refs_0_, bf16[144,128]{1,0:T(8,128)(2,1)S(1)} %get-tuple-element.42.refs_3_), custom_call_target="tpu_custom_call" | custom-call | tf_op jit(solution)/shard_map/mean/pallas_call | solution.py:416
  35.3 0.8 %near_times.1.refs_6_.refs_0_ = bf16[256,768]{1,0:T(8,128)(2,1)S(1)} custom-call(bf16[176,512]{1,0:T(8,128)(2,1)S(1)} %collective-permute-done.3.refs_0_.refs_2_, bf16[176,512]{1,0:T(8,128)(2,1)S(1)} %collective-permute-done.4.refs_1_.refs_3_, bf16[176,512]{1,0:T(8,128)(2,1)S(1)} %collective-permute-done.5.refs_2_.refs_4_, ...), custom_call_target="tpu_custom_call" | custom-call | tf_op jit(solution)/shard_map/near_times/pallas_call | solution.py:416
  36.1 0.8 %collective-permute-done.8.refs_0_ = bf16[144,128]{1,0:T(8,128)(2,1)S(1)} collective-permute-done((bf16[144,128]{1,0:T(8,128)(2,1)S(1)}, bf16[144,128]{1,0:T(8,128)(2,1)S(1)}, u32[]{:S(2)}, u32[]{:S(2)}) %collective-permute-start.8) | collective-permute-done | bytes 36896 | tf_op jit(solution)/shard_map/ppermute | solution.py:381
  36.9 0.0 collective-permute-done.9.refs_1_
  36.9 0.2 collective-permute-done.10.refs_2_
  37.1 0.4 near.1.refs_1_
  37.5 0.0 copy-start
  37.5 0.0 copy-start.1
  37.5 0.0 collective-permute-done.7.refs_2_.refs_0_
  37.5 0.2 hidden.1.refs_1_
  37.7 0.1 collective-permute-start.11
  37.8 0.8 %copy-done = bf16[512,512]{1,0:T(8,128)(2,1)S(1)} copy-done((bf16[512,512]{1,0:T(8,128)(2,1)S(1)}, bf16[512,512]{1,0:T(8,128)(2,1)}, u32[]{:S(2)}) %copy-start) | copy-done | bytes 524312
  38.6 0.2 copy-done.1
  38.7 0.9 %far_times.1 = (bf16[256,768]{1,0:T(8,128)(2,1)S(1)}, bf16[2,192,512]{2,1,0:T(8,128)(2,1)S(1)}, bf16[192,512]{1,0:T(8,128)(2,1)}) custom-call(bf16[208,512]{1,0:T(8,128)(2,1)S(1)} %collective-permute-done.7.refs_2_.refs_0_, bf16[192,512]{1,0:T(8,128)(2,1)S(1)} %hidden.1.refs_1_, bf16[512,512]{1,0:T(8,128)(2,1)S(1)} %copy-done, bf16[512,512]{1,0:T(8,128)(2,1)S(1)} %copy-done.1), custom_call_target="tpu_custom_call" | custom-call | flops 1100000000 | tf_op jit(solution)/shard_map/far_times/pallas_call | solution.py:416
  39.6 0.0 collective-permute-done.11.refs_3_
  39.6 0.8 %share.1 = (bf16[128,512]{1,0:T(8,128)(2,1)S(1)}, bf16[64,512]{1,0:T(8,128)(2,1)S(1)}, bf16[64,512]{1,0:T(8,128)(2,1)S(1)}, bf16[64,512]{1,0:T(8,128)(2,1)S(1)},...) custom-call(bf16[256,768]{1,0:T(8,128)(2,1)S(1)} %near_times.1.refs_6_.refs_0_, ...), custom_call_target="tpu_custom_call" | custom-call | flops 1100000000 | tf_op jit(solution)/shard_map/share/pallas_call | solution.py:416
  40.4 0.0 copy-start.3
  40.4 1.1 %collective-permute-start.12 = (bf16[128,512]{1,0:T(8,128)(2,1)S(1)}, bf16[128,512]{1,0:T(8,128)(2,1)S(1)}, u32[]{:S(2)}, u32[]{:S(2)}) collective-permute-start(bf16[128,512]{1,0:T(8,128)(2,1)S(1)} %get-tuple-element.47), channel_id=1, source_target_pairs={{0,2},{2,0},{4,6},{6,4},{8,10},{10,8},{12,14},{14,12},{1,3},{3,1},... | collective-permute-start | bytes 393224 | tf_op jit(solution)/shard_map/ppermute | solution.py:381
  41.5 1.3 %collective-permute-start.15 = (bf16[64,512]{1,0:T(8,128)(2,1)S(1)}, bf16[64,512]{1,0:T(8,128)(2,1)S(1)}, u32[]{:S(2)}, u32[]{:S(2)}) collective-permute-start(bf16[64,512]{1,0:T(8,128)(2,1)S(1)} %get-tuple-element.51), channel_id=1, source_target_pairs={{0,6},{2,4},{4,2},{6,0},{8,14},{10,12},{12,10},{14,8},{1,7},{3,5},... | collective-permute-start | bytes 196616 | tf_op jit(solution)/shard_map/ppermute | solution.py:381
  42.8 1.2 %collective-permute-start.16 = (bf16[64,512]{1,0:T(8,128)(2,1)S(1)}, bf16[64,512]{1,0:T(8,128)(2,1)S(1)}, u32[]{:S(2)}, u32[]{:S(2)}) collective-permute-start(bf16[64,512]{1,0:T(8,128)(2,1)S(1)} %get-tuple-element.52), channel_id=1, source_target_pairs={{0,4},{2,6},{4,0},{6,2},{8,12},{10,14},{12,8},{14,10},{1,5},{3,7},... | collective-permute-start | bytes 196616 | tf_op jit(solution)/shard_map/ppermute | solution.py:381
  44.0 1.4 %collective-permute-start.13 = (bf16[64,512]{1,0:T(8,128)(2,1)S(1)}, bf16[64,512]{1,0:T(8,128)(2,1)S(1)}, u32[]{:S(2)}, u32[]{:S(2)}) collective-permute-start(bf16[64,512]{1,0:T(8,128)(2,1)S(1)} %get-tuple-element.48), channel_id=1, source_target_pairs={{0,6},{2,4},{4,2},{6,0},{8,14},{10,12},{12,10},{14,8},{1,7},{3,5},... | collective-permute-start | bytes 196616 | tf_op jit(solution)/shard_map/ppermute | solution.py:381
  45.4 1.1 %collective-permute-start.14 = (bf16[64,512]{1,0:T(8,128)(2,1)S(1)}, bf16[64,512]{1,0:T(8,128)(2,1)S(1)}, u32[]{:S(2)}, u32[]{:S(2)}) collective-permute-start(bf16[64,512]{1,0:T(8,128)(2,1)S(1)} %get-tuple-element.49), channel_id=1, source_target_pairs={{0,4},{2,6},{4,0},{6,2},{8,12},{10,14},{12,8},{14,10},{1,5},{3,7},... | collective-permute-start | bytes 196616 | tf_op jit(solution)/shard_map/ppermute | solution.py:381
  46.4 0.9 %collective-permute-done.15.refs_1_ = bf16[64,512]{1,0:T(8,128)(2,1)S(1)} collective-permute-done((bf16[64,512]{1,0:T(8,128)(2,1)S(1)}, bf16[64,512]{1,0:T(8,128)(2,1)S(1)}, u32[]{:S(2)}, u32[]{:S(2)}) %collective-permute-start.15) | collective-permute-done | bytes 65568 | tf_op jit(solution)/shard_map/ppermute | solution.py:381
  47.3 0.5 collective-permute-done.16.refs_2_
  47.8 0.0 collective-permute-done.12.refs_0_.refs_1_
  47.8 2.5 %collective-permute-start.17 = (bf16[64,512]{1,0:T(8,128)(2,1)S(1)}, bf16[64,512]{1,0:T(8,128)(2,1)S(1)}, u32[]{:S(2)}, u32[]{:S(2)}) collective-permute-start(bf16[64,512]{1,0:T(8,128)(2,1)S(1)} %side_sum.1), channel_id=1, source_target_pairs={{0,8},{2,10},{4,12},{6,14},{8,0},{10,2},{12,4},{14,6},{1,9},{3,11}... | collective-permute-start | bytes 196616 | tf_op jit(solution)/shard_map/ppermute | solution.py:381
  50.3 0.0 collective-permute-done.13.refs_2_
  50.3 0.2 collective-permute-done.14.refs_3_
  50.5 3.2 %collective-permute-done.17.refs_5_ = bf16[64,512]{1,0:T(8,128)(2,1)S(1)} collective-permute-done((bf16[64,512]{1,0:T(8,128)(2,1)S(1)}, bf16[64,512]{1,0:T(8,128)(2,1)S(1)}, u32[]{:S(2)}, u32[]{:S(2)}) %collective-permute-start.17) | collective-permute-done | bytes 65568 | tf_op jit(solution)/shard_map/ppermute | solution.py:381
  53.7 0.0 copy-done.3
  53.7 0.7 %seeds.1 = bf16[64,512]{1,0:T(8,128)(2,1)} custom-call(f32[1,512]{1,0:T(1,128)S(1)} %bitcast.12, bf16[128,512]{1,0:T(8,128)(2,1)S(1)} %collective-permute-done.12.refs_0_.refs_1_, bf16[64,512]{1,0:T(8,128)(2,1)S(1)} %collective-permute-done.13.refs_2_, bf16[64,512]{1,0:T(8,128)(2,1)S(1)} %collective-permute-done.14.refs_3_, ...), custom_call_target="tpu_custom_call" | custom-call | flops 1100000000 | tf_op jit(solution)/shard_map/seeds/pallas_call | solution.py:416
  (2 shorter events, 0.1 us)
Async XLA Ops:
  3.1 12.0 %collective-permute-start.3 = (bf16[176,512]{1,0:T(8,128)(2,1)S(1)}, bf16[176,512]{1,0:T(8,128)(2,1)S(1)}, u32[]{:S(2)}, u32[]{:S(2)}) collective-permute-start(bf16[176,512]{1,0:T(8,128)(2,1)S(1)} %get-tuple-element.33), channel_id=1, source_target_pairs={{0,6},{2,4},{4,2},{6,0},{8,14},{10,12},{12,10},{14,8},{1,7},{3,5},... | collective-permute-start | bytes 540680 | tf_op jit(solution)/shard_map/ppermute | solution.py:381
  7.2 8.6 %collective-permute-start.4 = (bf16[176,512]{1,0:T(8,128)(2,1)S(1)}, bf16[176,512]{1,0:T(8,128)(2,1)S(1)}, u32[]{:S(2)}, u32[]{:S(2)}) collective-permute-start(bf16[176,512]{1,0:T(8,128)(2,1)S(1)} %get-tuple-element.34), channel_id=1, source_target_pairs={{0,4},{2,6},{4,0},{6,2},{8,12},{10,14},{12,8},{14,10},{1,5},{3,7},... | collective-permute-start | bytes 540680 | tf_op jit(solution)/shard_map/ppermute | solution.py:381
  7.6 8.2 %collective-permute-start.5 = (bf16[176,512]{1,0:T(8,128)(2,1)S(1)}, bf16[176,512]{1,0:T(8,128)(2,1)S(1)}, u32[]{:S(2)}, u32[]{:S(2)}) collective-permute-start(bf16[176,512]{1,0:T(8,128)(2,1)S(1)} %get-tuple-element.35), channel_id=1, source_target_pairs={{0,2},{2,0},{4,6},{6,4},{8,10},{10,8},{12,14},{14,12},{1,3},{3,1},... | collective-permute-start | bytes 540680 | tf_op jit(solution)/shard_map/ppermute | solution.py:381
  15.8 6.0 %collective-permute-start.6 = (bf16[4,96,512]{2,1,0:T(8,128)(2,1)S(1)}, bf16[4,96,512]{2,1,0:T(8,128)(2,1)S(1)}, u32[]{:S(2)}, u32[]{:S(2)}) collective-permute-start(bf16[4,96,512]{2,1,0:T(8,128)(2,1)S(1)} %halves.1.refs_2_), channel_id=1, source_target_pairs={{0,1},{1,0},{2,3},{3,2},{4,5},{5,4},{6,7},{7,6},{8,9},{9,8},{10,11... | collective-permute-start | bytes 1179656 | tf_op jit(solution)/shard_map/ppermute | solution.py:381
  15.9 6.9 %collective-permute-start = (bf16[144,128]{1,0:T(8,128)(2,1)S(1)}, bf16[144,128]{1,0:T(8,128)(2,1)S(1)}, u32[]{:S(2)}, u32[]{:S(2)}) collective-permute-start(bf16[144,128]{1,0:T(8,128)(2,1)S(1)} %get-tuple-element.30.refs_4_), channel_id=1, source_target_pairs={{0,6},{2,4},{4,2},{6,0},{8,14},{10,12},{12,10},{14,8},{1,7},{3,5},... | collective-permute-start | bytes 110600 | tf_op jit(solution)/shard_map/ppermute | solution.py:381
  18.4 4.1 %collective-permute-start.1 = (bf16[144,128]{1,0:T(8,128)(2,1)S(1)}, bf16[144,128]{1,0:T(8,128)(2,1)S(1)}, u32[]{:S(2)}, u32[]{:S(2)}) collective-permute-start(bf16[144,128]{1,0:T(8,128)(2,1)S(1)} %get-tuple-element.31), channel_id=1, source_target_pairs={{0,4},{2,6},{4,0},{6,2},{8,12},{10,14},{12,8},{14,10},{1,5},{3,7},... | collective-permute-start | bytes 110600 | tf_op jit(solution)/shard_map/ppermute | solution.py:381
  18.9 3.0 %copy-start.2 = (f32[512]{0:T(512)S(1)}, f32[512]{0:T(512)}, u32[]{:S(2)}) copy-start(f32[512]{0:T(512)} %param.18) | copy-start | bytes 6148
  18.9 4.0 %collective-permute-start.2 = (bf16[144,128]{1,0:T(8,128)(2,1)S(1)}, bf16[144,128]{1,0:T(8,128)(2,1)S(1)}, u32[]{:S(2)}, u32[]{:S(2)}) collective-permute-start(bf16[144,128]{1,0:T(8,128)(2,1)S(1)} %get-tuple-element.32), channel_id=1, source_target_pairs={{0,2},{2,0},{4,6},{6,4},{8,10},{10,8},{12,14},{14,12},{1,3},{3,1},... | collective-permute-start | bytes 110600 | tf_op jit(solution)/shard_map/ppermute | solution.py:381
  23.2 14.3 %collective-permute-start.7 = (bf16[208,512]{1,0:T(8,128)(2,1)S(1)}, bf16[208,512]{1,0:T(8,128)(2,1)S(1)}, u32[]{:S(2)}, u32[]{:S(2)}) collective-permute-start(bf16[208,512]{1,0:T(8,128)(2,1)S(1)} %far.1.refs_5_), channel_id=1, source_target_pairs={{0,8},{2,10},{4,12},{6,14},{8,0},{10,2},{12,4},{14,6},{1,9},{3,11}... | collective-permute-start | bytes 638984 | tf_op jit(solution)/shard_map/ppermute | solution.py:381
  29.2 7.7 %collective-permute-start.8 = (bf16[144,128]{1,0:T(8,128)(2,1)S(1)}, bf16[144,128]{1,0:T(8,128)(2,1)S(1)}, u32[]{:S(2)}, u32[]{:S(2)}) collective-permute-start(bf16[144,128]{1,0:T(8,128)(2,1)S(1)} %get-tuple-element.40), channel_id=1, source_target_pairs={{0,6},{2,4},{4,2},{6,0},{8,14},{10,12},{12,10},{14,8},{1,7},{3,5},... | collective-permute-start | bytes 110600 | tf_op jit(solution)/shard_map/ppermute | solution.py:381
  32.0 5.0 %collective-permute-start.9 = (bf16[144,128]{1,0:T(8,128)(2,1)S(1)}, bf16[144,128]{1,0:T(8,128)(2,1)S(1)}, u32[]{:S(2)}, u32[]{:S(2)}) collective-permute-start(bf16[144,128]{1,0:T(8,128)(2,1)S(1)} %get-tuple-element.41), channel_id=1, source_target_pairs={{0,4},{2,6},{4,0},{6,2},{8,12},{10,14},{12,8},{14,10},{1,5},{3,7},... | collective-permute-start | bytes 110600 | tf_op jit(solution)/shard_map/ppermute | solution.py:381
  32.4 4.7 %collective-permute-start.10 = (bf16[144,128]{1,0:T(8,128)(2,1)S(1)}, bf16[144,128]{1,0:T(8,128)(2,1)S(1)}, u32[]{:S(2)}, u32[]{:S(2)}) collective-permute-start(bf16[144,128]{1,0:T(8,128)(2,1)S(1)} %get-tuple-element.42.refs_3_), channel_id=1, source_target_pairs={{0,2},{2,0},{4,6},{6,4},{8,10},{10,8},{12,14},{14,12},{1,3},{3,1},... | collective-permute-start | bytes 110600 | tf_op jit(solution)/shard_map/ppermute | solution.py:381
  37.5 1.0 %copy-start = (bf16[512,512]{1,0:T(8,128)(2,1)S(1)}, bf16[512,512]{1,0:T(8,128)(2,1)}, u32[]{:S(2)}) copy-start(bf16[512,512]{1,0:T(8,128)(2,1)} %refs_4_.3) | copy-start | bytes 1572868
  37.5 1.2 %copy-start.1 = (bf16[512,512]{1,0:T(8,128)(2,1)S(1)}, bf16[512,512]{1,0:T(8,128)(2,1)}, u32[]{:S(2)}) copy-start(bf16[512,512]{1,0:T(8,128)(2,1)} %refs_5_.1) | copy-start | bytes 1572868
  37.7 1.9 %collective-permute-start.11 = (bf16[192,512]{1,0:T(8,128)(2,1)S(1)}, bf16[192,512]{1,0:T(8,128)(2,1)S(1)}, u32[]{:S(2)}, u32[]{:S(2)}) collective-permute-start(bf16[192,512]{1,0:T(8,128)(2,1)S(1)} %hidden.1.refs_1_), channel_id=1, source_target_pairs={{0,1},{1,0},{2,3},{3,2},{4,5},{5,4},{6,7},{7,6},{8,9},{9,8},{10,11... | collective-permute-start | bytes 589832 | tf_op jit(solution)/shard_map/ppermute | solution.py:381
  40.4 13.4 %copy-start.3 = (f32[512]{0:T(512)S(1)}, f32[512]{0:T(512)}, u32[]{:S(2)}) copy-start(f32[512]{0:T(512)} %param.21) | copy-start | bytes 6148
  40.4 7.4 %collective-permute-start.12 = (bf16[128,512]{1,0:T(8,128)(2,1)S(1)}, bf16[128,512]{1,0:T(8,128)(2,1)S(1)}, u32[]{:S(2)}, u32[]{:S(2)}) collective-permute-start(bf16[128,512]{1,0:T(8,128)(2,1)S(1)} %get-tuple-element.47), channel_id=1, source_target_pairs={{0,2},{2,0},{4,6},{6,4},{8,10},{10,8},{12,14},{14,12},{1,3},{3,1},... | collective-permute-start | bytes 393224 | tf_op jit(solution)/shard_map/ppermute | solution.py:381
  41.5 5.8 %collective-permute-start.15 = (bf16[64,512]{1,0:T(8,128)(2,1)S(1)}, bf16[64,512]{1,0:T(8,128)(2,1)S(1)}, u32[]{:S(2)}, u32[]{:S(2)}) collective-permute-start(bf16[64,512]{1,0:T(8,128)(2,1)S(1)} %get-tuple-element.51), channel_id=1, source_target_pairs={{0,6},{2,4},{4,2},{6,0},{8,14},{10,12},{12,10},{14,8},{1,7},{3,5},... | collective-permute-start | bytes 196616 | tf_op jit(solution)/shard_map/ppermute | solution.py:381
  42.8 5.0 %collective-permute-start.16 = (bf16[64,512]{1,0:T(8,128)(2,1)S(1)}, bf16[64,512]{1,0:T(8,128)(2,1)S(1)}, u32[]{:S(2)}, u32[]{:S(2)}) collective-permute-start(bf16[64,512]{1,0:T(8,128)(2,1)S(1)} %get-tuple-element.52), channel_id=1, source_target_pairs={{0,4},{2,6},{4,0},{6,2},{8,12},{10,14},{12,8},{14,10},{1,5},{3,7},... | collective-permute-start | bytes 196616 | tf_op jit(solution)/shard_map/ppermute | solution.py:381
  44.0 6.3 %collective-permute-start.13 = (bf16[64,512]{1,0:T(8,128)(2,1)S(1)}, bf16[64,512]{1,0:T(8,128)(2,1)S(1)}, u32[]{:S(2)}, u32[]{:S(2)}) collective-permute-start(bf16[64,512]{1,0:T(8,128)(2,1)S(1)} %get-tuple-element.48), channel_id=1, source_target_pairs={{0,6},{2,4},{4,2},{6,0},{8,14},{10,12},{12,10},{14,8},{1,7},{3,5},... | collective-permute-start | bytes 196616 | tf_op jit(solution)/shard_map/ppermute | solution.py:381
  45.4 5.1 %collective-permute-start.14 = (bf16[64,512]{1,0:T(8,128)(2,1)S(1)}, bf16[64,512]{1,0:T(8,128)(2,1)S(1)}, u32[]{:S(2)}, u32[]{:S(2)}) collective-permute-start(bf16[64,512]{1,0:T(8,128)(2,1)S(1)} %get-tuple-element.49), channel_id=1, source_target_pairs={{0,4},{2,6},{4,0},{6,2},{8,12},{10,14},{12,8},{14,10},{1,5},{3,7},... | collective-permute-start | bytes 196616 | tf_op jit(solution)/shard_map/ppermute | solution.py:381
  47.8 5.9 %collective-permute-start.17 = (bf16[64,512]{1,0:T(8,128)(2,1)S(1)}, bf16[64,512]{1,0:T(8,128)(2,1)S(1)}, u32[]{:S(2)}, u32[]{:S(2)}) collective-permute-start(bf16[64,512]{1,0:T(8,128)(2,1)S(1)} %side_sum.1), channel_id=1, source_target_pairs={{0,8},{2,10},{4,12},{6,14},{8,0},{10,2},{12,4},{14,6},{1,9},{3,11}... | collective-permute-start | bytes 196616 | tf_op jit(solution)/shard_map/ppermute | solution.py:381

commit v12 on v11

--- a/solution.py
+++ b/solution.py
@@ -23,19 +23,18 @@
     return 2 * fslice - fslice // 4 + 8 if is_dense(fslice, n_idx) else 2 * fslice
 
 
-def write_parcel(ref, weight, feats, digits, live):
+def write_parcel(ref, weight, feats, digits):
     fslice, lanes = feats.shape
     ref[:fslice, :] = weight
     if is_dense(fslice, digits.shape[0]):
         cut = fslice // 4 * 3
         tail = jnp.concatenate([feats[cut:, i : i + LANES] for i in range(0, lanes, LANES)], axis=0)
-        tags = jnp.concatenate([digits[:8], digits[8:], live, live], axis=1)
+        tags = jnp.concatenate([digits[:8], digits[8:]] * 2, axis=1)
         body = jnp.concatenate([feats[:cut], tail], axis=1)
         ref[fslice:, :] = jnp.concatenate([body, tags], axis=0).astype(jnp.bfloat16)
     else:
-        tags = jnp.concatenate([digits, live], axis=0).astype(jnp.bfloat16)
         ref[fslice:, :lanes] = feats.astype(jnp.bfloat16)
-        ref[fslice : fslice + tags.shape[0], lanes:] = tags
+        ref[fslice : fslice + digits.shape[0], lanes:] = digits.astype(jnp.bfloat16)
 
 
 def read_feats(ref, fslice, n_idx, lanes):
@@ -54,12 +53,11 @@
     return jnp.concatenate([tags[:, :LANES], tags[:, LANES:]], axis=0)
 
 
-def live_rows(ref, fslice, n_idx, lanes):
-    if is_dense(fslice, n_idx):
-        tag = ref[-8:, 2 * LANES : 3 * LANES]
-    else:
-        tag = ref[fslice + n_idx : fslice + n_idx + 8, lanes:]
-    return jnp.max(tag.astype(jnp.float32)).astype(jnp.int32)
+TAG_ROWS = 16
+
+
+def live_rows(ref):
+    return jnp.max(ref[-TAG_ROWS:, :].astype(jnp.float32)).astype(jnp.int32)
 
 
 def pack_kernel(
@@ -71,7 +69,6 @@
     w_self_hbm,
     w_nbr_hbm,
     pick_hbm,
-    live_ref,
     *refs,
 ):
     half = n_feat // 2
@@ -108,14 +105,13 @@
     high = lax.shift_right_logical(idx, 7)
     digits = jnp.concatenate([high, idx - high * 128], axis=1).astype(jnp.float32)
     weight = jnp.where(first_core, w_self_ref[...], w_nbr_ref[...])
-    live = jnp.full((8, LANES), live_ref[0, 0].astype(jnp.float32))
     for s, parcel_ref in enumerate(reversed(parcel_refs)):
         sides = []
         for step in (s, s ^ half):
             at = pl.multiple_of(jnp.bitwise_xor(feat_pos, step) * (2 * pcap), LANES)
             block = src_ref[:, pl.ds(at, 2 * pcap)].astype(jnp.float32)
             sides.append(jnp.where(first_core, block[:, :pcap], block[:, pcap:]))
-        write_parcel(parcel_ref, weight, jnp.concatenate(sides, axis=1), digits, live)
+        write_parcel(parcel_ref, weight, jnp.concatenate(sides, axis=1), digits)
     copies[-1].wait()
 
 
@@ -131,10 +127,11 @@
     lax.fori_loop(0, nodes // width, turn, 0)
 
 
-def mean_kernel(chosen, packed, fanout, pcap, fslice, n_idx, nbr_any, table_ref, *refs):
+def mean_kernel(chosen, packed, fanout, pcap, fslice, nbr_any, table_ref, *refs):
     count = len(chosen)
-    out_ref, total, nbr_ref, live_ref, sems = refs[-5:]
-    chunk_refs, parcel_refs = refs[-5 - count : -5], refs[: -5 - count]
+    token_ref, out_ref, total, nbr_ref, live_ref, sems = refs[-6:]
+    chunk_refs, tagged_refs = refs[-6 - count : -6], refs[: -6 - count]
+    token_ref[...] = jnp.zeros(token_ref.shape, jnp.float32)
     feat_pos = lax.axis_index("feat")
     words = fanout // packed
     stride = -(-pcap // LANES) * LANES
@@ -151,8 +148,8 @@
         copy.start()
     for i in range(count):
         live_ref[i] = pcap
-    for i, ref in enumerate(parcel_refs):
-        live_ref[i] = live_rows(ref, fslice, n_idx, 2 * pcap)
+    for i, ref in enumerate(tagged_refs):
+        live_ref[i] = live_rows(ref)
     for copy in copies:
         copy.wait()
 
@@ -202,11 +199,11 @@
         ref[...] = out_ref[i]
 
 
-def unfold(block, fslice, pcap):
-    if block.shape[0] == pcap:
-        return block
-    part = block.shape[0] // 3
-    wide = block.astype(jnp.float32)
+def unfold(ref, fslice, pcap):
+    if not folds(fslice, pcap):
+        return ref[:pcap, :]
+    part = pcap // 4
+    wide = ref[: 3 * part, :].astype(jnp.float32)
     lane = lax.broadcasted_iota(jnp.int32, (part, LANES), 1)
     tail = pltpu.roll(wide[:part], LANES - fslice, 1)
     for b in (1, 2):
@@ -217,9 +214,16 @@
     return jnp.concatenate([wide, tail], axis=0)[:, :fslice].astype(jnp.bfloat16)
 
 
-def halves_kernel(half, *refs):
-    for s in range(half):
-        refs[half][s] = refs[s][: refs[half].shape[1], :]
+def halves_kernel(half, count_ref, *refs):
+    parcel_refs, chunk_refs = refs[:half], refs[half : 2 * half - 1]
+    out_ref, *tagged_refs, live_ref = refs[2 * half - 1 :]
+    for s, ref in enumerate(parcel_refs):
+        out_ref[s] = ref[: out_ref.shape[1], :]
+    live = jnp.full(live_ref.shape, count_ref[0, 0].astype(jnp.float32)).astype(jnp.bfloat16)
+    live_ref[...] = live
+    for chunk_ref, ref in zip(chunk_refs, tagged_refs):
+        ref[:-TAG_ROWS, :] = chunk_ref[...]
+        ref[-TAG_ROWS:, :] = live
 
 
 def own_kernel(half, n_idx, *refs):
@@ -243,11 +247,11 @@
     far_ref[...] = both[pcap:]
 
 
-def add_means(half, pre, mean_refs, w_ref):
-    for s in range(half):
+def add_means(half, pre, mean_refs, w_ref, turn=0):
+    for s, ref in enumerate(mean_refs):
         pre = pre + jnp.dot(
-            unfold(mean_refs[s][...], w_ref.shape[1], pre.shape[0]),
-            w_ref[s],
+            unfold(ref, w_ref.shape[1], pre.shape[0]),
+            w_ref[(s + turn) % (half - 1) if s < half - 1 else s],
             preferred_element_type=jnp.float32,
         )
     return pre
@@ -284,7 +288,7 @@
         out_ref[place, 2 * pcap :] = near.T.astype(jnp.bfloat16)
 
 
-def near_times_kernel(half, fslice, pcap, n_idx, *refs):
+def near_times_kernel(half, fslice, pcap, n_idx, _, __, *refs):
     blocks = [read_digits(ref, fslice, n_idx, 2 * pcap) for ref in refs[:half]]
     store_times(pcap, blocks, refs[half])
 
@@ -327,14 +331,13 @@
 
 def near_kernel(half, *refs):
     pre_ref, w_ref, out_ref = refs[half:]
-    out_ref[...] = add_means(half, pre_ref[...], refs[:half], w_ref)
-
-
-def hidden_kernel(fslice, n_idx, parcel_ref, pre_ref, cross_ref, hidden_ref):
+    out_ref[...] = add_means(half, pre_ref[...], refs[:half], w_ref, 1)
+
+
+def hidden_kernel(live_ref, pre_ref, cross_ref, hidden_ref):
     pcap, width = hidden_ref.shape
     pre = pre_ref[...] + cross_ref[:pcap, :].astype(jnp.float32)
-    count = live_rows(parcel_ref, fslice, n_idx, 2 * pcap)
-    live = lax.broadcasted_iota(jnp.int32, (pcap, width), 0) < count
+    live = lax.broadcasted_iota(jnp.int32, (pcap, width), 0) < live_rows(live_ref)
     hidden_ref[...] = jnp.where(live, jnp.maximum(pre, 0.0), 0.0).astype(jnp.bfloat16)
 
 
@@ -440,11 +443,8 @@
         "pack",
         [((parcel_rows(fslice, n_idx), width), bf16)] * half
         + [(words, jnp.int32), ((fslice, nodes), bf16)],
-        [hbm] * 6 + [smem],
-        [
-            *(pinned(x) for x in (src_feats, seed_rows[None], nbr_two.T, w1_self, w1_nbr, picks)),
-            counts,
-        ],
+        [hbm] * 6,
+        [pinned(x) for x in (src_feats, seed_rows[None], nbr_two.T, w1_self, w1_nbr, picks)],
         scratch=[
             pltpu.VMEM((1, seed_count), jnp.int32),
             pltpu.VMEM((fanout_two, seed_count), jnp.int32),
@@ -468,14 +468,14 @@
     table = table.reshape(nodes, 1, LANES)
     chunk_shape = (pcap // 4 * 3, LANES) if folds(fslice, pcap) else (pcap, fslice)
 
-    def means(chosen, parcels=(), after=()):
+    def means(chosen, tagged=(), after=()):
         count = len(chosen)
         return call(
-            functools.partial(mean_kernel, tuple(chosen), packed, fanout_one, pcap, fslice, n_idx),
+            functools.partial(mean_kernel, tuple(chosen), packed, fanout_one, pcap, fslice),
             "mean",
-            [(chunk_shape, bf16)] * count,
-            [anywhere] + [vmem] * (1 + len(parcels)),
-            (picks, table, *parcels),
+            [(chunk_shape, bf16)] * count + [((8, LANES), jnp.float32)],
+            [anywhere] + [vmem] * (1 + len(tagged)),
+            (picks, table, *tagged),
             after=after,
             scratch=[
                 pltpu.VMEM((count, *chunk_shape), bf16),
@@ -488,18 +488,22 @@
             cost_us=2 * count if count > 1 else 0,
         )
 
-    far_means = means([s + half for s in steps if s])
-    (halves,) = call(
+    *far_means, _ = means([s + half for s in steps if s])
+    tagged_shape = (chunk_shape[0] + TAG_ROWS, chunk_shape[1])
+    halves, *tagged, live = call(
         functools.partial(halves_kernel, half),
         "halves",
-        [((half, fslice, width), bf16)],
-        [vmem] * half,
-        arrived,
-        after=far_means[:1],
-    )
-    far_arrived = send(far_means)
+        [
+            ((half, fslice, width), bf16),
+            *([(tagged_shape, bf16)] * (half - 1)),
+            ((TAG_ROWS, chunk_shape[1]), bf16),
+        ],
+        [smem] + [vmem] * (2 * half - 1),
+        (counts, *arrived, *far_means),
+    )
+    far_arrived = send(tagged)
     other_halves = swap(halves, "rep", 1)
-    (far_own,) = means([half], after=(halves,))
+    far_own, _ = means([half], after=(halves,))
     idx_rows = -(-half // 4) * n_idx
     w_nbr, pre, far_pre, idx_tags = call(
         functools.partial(own_kernel, half, n_idx),
@@ -513,6 +517,7 @@
         [vmem] * (half + 2),
         (*arrived, other_halves, bias_one[None]),
         after=(far_own,),
+        cost_us=0,
     )
     (cross,) = call(
         functools.partial(far_kernel, half),
@@ -522,15 +527,16 @@
         (*far_arrived, far_own, far_pre, w_nbr, idx_tags),
     )
     cross_arrived = swap(cross, "feat", half)
-    near_means = means([s for s in steps if s], arrived[:-1], (cross,))
-    near_arrived = send(near_means)
-    (near_own,) = means([0], arrived[-1:], near_means[-1:])
+    turned = [*steps[1:-1], steps[0]]
+    *near_means, token = means(turned, [*far_arrived[1:], far_arrived[0]], (cross,))
+    near_arrived = send(near_means, turned)
+    near_own, _ = means([0], [live], (token,))
     (near_times,) = call(
         functools.partial(near_times_kernel, half, fslice, pcap, n_idx),
         "near_times",
         [((half * seed_count, 4 * pcap), bf16)],
-        [vmem] * half,
-        arrived,
+        [vmem] * (half + 2),
+        (w2_self, w2_nbr, *arrived),
         after=(near_own,),
         cost_us=0,
     )
@@ -544,11 +550,11 @@
         cost_us=0,
     )
     (hidden,) = call(
-        functools.partial(hidden_kernel, fslice, n_idx),
+        hidden_kernel,
         "hidden",
         [((pcap, width), bf16)],
         [vmem] * 3,
-        (parcels[-1], near_pre, cross_arrived),
+        (live, near_pre, cross_arrived),
     )
     other_hidden = swap(hidden, "rep", 1)
     far_times, value, result = call(

time: 54.8 us -> 55.2 us (level)
  Pallas kernels: 21.7 us -> 23 us
  local copies, waits for them, and re-layouts: 0.93 us -> 0.02 us
    pallas_call x16, Pallas kernels: 21.7 us -> 23 us  [call(): pl.pallas_call(wrapped, out_shape=tuple((jax.ShapeDtypeStruct(shape, dtyp...]
    unnamed x8, local copies, waits for them, and re-layouts: 0.93 us -> 0.02 us
  transfers between devices with their start and end apart: 18 -> 18, of which waited for: 8 -> 7; matrix products, arithmetic and copies ran while one was open for 0% -> 0% of each run, Pallas kernels for 33% -> 35%
where the time goes in v12:
time: 55.2 us; the launch traced here: 55 us
  starting transfers between devices  23.3 us (42%)
  Pallas kernels  23 us (42%)
  waiting for transfers between devices  7.19 us (13%)
  between operations  1.5 us (3%)
    ppermute x18, starting transfers between devices, swap(): return lax.ppermute(value, axis, [(i, i ^ step) for i in range(size)])  23.3 us
    pallas_call x16, Pallas kernels, call(): pl.pallas_call(wrapped, out_shape=tuple((jax.ShapeDtypeStruct(shape, dtyp...  23 us
    ppermute x18, waiting for transfers between devices, swap(): return lax.ppermute(value, axis, [(i, i ^ step) for i in range(size)])  7.19 us
  transfers between devices with their start and end apart: 18, of which 7 were waited for; matrix products, arithmetic and copies ran while one was open for 0% of the time, Pallas kernels for 35%

profile of v12, /device:TPU:0, one launch (start us, length us, event | category | flops | bytes accessed | tf_op | source)
XLA Modules:
  0.0 55.0 jit_solution(16070647059317093478)
XLA Ops:
  0.6 1.8 %pack.1 = (bf16[176,512]{1,0:T(8,128)(2,1)S(1)}, bf16[176,512]{1,0:T(8,128)(2,1)S(1)}, bf16[176,512]{1,0:T(8,128)(2,1)S(1)}, bf16[176,512]{1,0:T(8,128)(2,1)S(1)...) custom-call(bf16[96,12288]{1,0:T(8,128)(2,1)} %refs_0_.3, s32[1,64]{1,0:T(1,128)} %bitcast.15, ...), custom_call_target="tpu_custom_call" | custom-call | flops 1100000000 | tf_op jit(solution)/shard_map/pack/pallas_call | solution.py:419
  2.5 4.0 %collective-permute-start = (bf16[176,512]{1,0:T(8,128)(2,1)S(1)}, bf16[176,512]{1,0:T(8,128)(2,1)S(1)}, u32[]{:S(2)}, u32[]{:S(2)}) collective-permute-start(bf16[176,512]{1,0:T(8,128)(2,1)S(1)} %get-tuple-element.36), channel_id=1, source_target_pairs={{0,6},{2,4},{4,2},{6,0},{8,14},{10,12},{12,10},{14,8},{1,7},{3,5},... | collective-permute-start | bytes 540680 | tf_op jit(solution)/shard_map/ppermute | solution.py:384
  6.5 0.4 collective-permute-start.1
  7.0 0.2 collective-permute-start.2
  7.2 1.2 %turn.1 = f32[12288,128]{1,0:T(8,128)S(1)} custom-call(bf16[96,12288]{1,0:T(8,128)(2,1)S(1)} %get-tuple-element.41.refs_0_), custom_call_target="tpu_custom_call" | custom-call | flops 3300000000 | tf_op jit(solution)/shard_map/turn/pallas_call | solution.py:419
  8.4 6.6 %mean.4 = (bf16[144,128]{1,0:T(8,128)(2,1)S(1)}, bf16[144,128]{1,0:T(8,128)(2,1)S(1)}, bf16[144,128]{1,0:T(8,128)(2,1)S(1)}, f32[8,128]{1,0:T(8,128)}) custom-call(s32[8,5,1,256]{3,2,1,0:T(1,128)S(1)} %get-tuple-element.40.refs_0_, f32[12288,1,128]{2,1,0:T(1,128)S(1)} %bitcast.7), custom_call_target="tpu_custom_call" | custom-call | flops 6600000000 | tf_op jit(solution)/shard_map/mean/pallas_call | solution.py:419
  15.6 0.0 collective-permute-done.refs_1_.refs_0_.refs_2_
  15.6 0.0 collective-permute-done.1.refs_2_.refs_1_.refs_3_
  15.7 0.0 collective-permute-done.2.refs_3_.refs_2_.refs_4_
  15.7 0.1 collective-permute-start.6
  15.8 2.9 %collective-permute-start.3 = (bf16[160,128]{1,0:T(8,128)(2,1)S(1)}, bf16[160,128]{1,0:T(8,128)(2,1)S(1)}, u32[]{:S(2)}, u32[]{:S(2)}) collective-permute-start(bf16[160,128]{1,0:T(8,128)(2,1)S(1)} %get-tuple-element.45), channel_id=1, source_target_pairs={{0,6},{2,4},{4,2},{6,0},{8,14},{10,12},{12,10},{14,8},{1,7},{3,5},... | collective-permute-start | bytes 122888 | tf_op jit(solution)/shard_map/ppermute | solution.py:384
  18.7 0.4 collective-permute-start.4
  19.2 0.0 copy-start.2
  19.2 0.2 collective-permute-start.5
  19.4 2.9 %mean.5 = (bf16[144,128]{1,0:T(8,128)(2,1)S(1)}, f32[8,128]{1,0:T(8,128)}) custom-call(s32[8,5,1,256]{3,2,1,0:T(1,128)S(1)} %get-tuple-element.40.refs_0_, f32[12288,1,128]{2,1,0:T(1,128)S(1)} %bitcast.8, bf16[4,96,512]{2,1,0:T(8,128)(2,1)S(1)} %get-tuple-element.48.refs_2_), custom_call_target="tpu_custom_call" | custom-call | tf_op jit(solution)/shard_map/mean/pallas_call | solution.py:419
  22.3 0.0 collective-permute-done.6.refs_4_
  22.3 0.0 copy-done.2
  22.3 0.6 %own.1 = (bf16[4,96,512]{2,1,0:T(8,128)(2,1)S(1)}, f32[192,512]{1,0:T(8,128)S(1)}, f32[192,512]{1,0:T(8,128)S(1)}, bf16[16,512]{1,0:T(8,128)(2,1)S(1)}) custom-call(bf16[176,512]{1,0:T(8,128)(2,1)S(1)} %collective-permute-done.refs_1_.refs_0_.refs_2_, bf16[176,512]{1,0:T(8,128)(2,1)S(1)} %collective-permute-done.1.refs_2_.refs_1_.refs_3_, ...), custom_call_target="tpu_custom_call" | custom-call | tf_op jit(solution)/shard_map/own/pallas_call | solution.py:419
  22.9 0.0 collective-permute-done.3.refs_0_.refs_4_
  22.9 0.0 collective-permute-done.4.refs_1_.refs_2_
  22.9 0.2 collective-permute-done.5.refs_2_.refs_3_
  23.2 0.4 far.1.refs_5_
  23.5 2.8 %collective-permute-start.7 = (bf16[208,512]{1,0:T(8,128)(2,1)S(1)}, bf16[208,512]{1,0:T(8,128)(2,1)S(1)}, u32[]{:S(2)}, u32[]{:S(2)}) collective-permute-start(bf16[208,512]{1,0:T(8,128)(2,1)S(1)} %far.1.refs_5_), channel_id=1, source_target_pairs={{0,8},{2,10},{4,12},{6,14},{8,0},{10,2},{12,4},{14,6},{1,9},{3,11}... | collective-permute-start | bytes 638984 | tf_op jit(solution)/shard_map/ppermute | solution.py:384
  26.3 3.5 %mean.6 = (bf16[144,128]{1,0:T(8,128)(2,1)S(1)}, bf16[144,128]{1,0:T(8,128)(2,1)S(1)}, bf16[144,128]{1,0:T(8,128)(2,1)S(1)}, f32[8,128]{1,0:T(8,128)S(1)}) custom-call(s32[8,5,1,256]{3,2,1,0:T(1,128)S(1)} %get-tuple-element.40.refs_0_, f32[12288,1,128]{2,1,0:T(1,128)S(1)} %bitcast.9, bf16[160,128]{1,0:T(8,128)(2,1)S(1)} %collective-permute-done.4.refs_1_.refs_2_, ...), custom_call_target="tpu_custom_call" | custom-call | flops 6600000000 | tf_op jit(solution)/shard_map/mean/pallas_call | solution.py:419
  29.8 2.2 %collective-permute-start.10 = (bf16[144,128]{1,0:T(8,128)(2,1)S(1)}, bf16[144,128]{1,0:T(8,128)(2,1)S(1)}, u32[]{:S(2)}, u32[]{:S(2)}) collective-permute-start(bf16[144,128]{1,0:T(8,128)(2,1)S(1)} %get-tuple-element.56), channel_id=1, source_target_pairs={{0,6},{2,4},{4,2},{6,0},{8,14},{10,12},{12,10},{14,8},{1,7},{3,5},... | collective-permute-start | bytes 110600 | tf_op jit(solution)/shard_map/ppermute | solution.py:384
  32.0 1.1 %collective-permute-start.8 = (bf16[144,128]{1,0:T(8,128)(2,1)S(1)}, bf16[144,128]{1,0:T(8,128)(2,1)S(1)}, u32[]{:S(2)}, u32[]{:S(2)}) collective-permute-start(bf16[144,128]{1,0:T(8,128)(2,1)S(1)} %get-tuple-element.54), channel_id=1, source_target_pairs={{0,4},{2,6},{4,0},{6,2},{8,12},{10,14},{12,8},{14,10},{1,5},{3,7},... | collective-permute-start | bytes 110600 | tf_op jit(solution)/shard_map/ppermute | solution.py:384
  33.1 0.5 collective-permute-start.9
  33.6 0.0 copy-start
  33.6 0.0 copy-start.1
  33.6 2.2 %mean.7 = (bf16[144,128]{1,0:T(8,128)(2,1)S(1)}, f32[8,128]{1,0:T(8,128)}) custom-call(s32[8,5,1,256]{3,2,1,0:T(1,128)S(1)} %get-tuple-element.40.refs_0_, f32[12288,1,128]{2,1,0:T(1,128)S(1)} %bitcast.10, bf16[16,128]{1,0:T(8,128)(2,1)S(1)} %get-tuple-element.53.refs_2_.refs_0_, f32[8,128]{1,0:T(8,128)S(1)} %get-tuple-element.57.refs_3_), custom_call_target="tpu_custom_call" | custom-call | tf_op jit(solution)/shard_map/mean/pallas_call | solution.py:419
  35.8 0.0 copy-done
  35.8 0.0 copy-done.1
  35.8 0.8 %near_times.1.refs_6_.refs_0_ = bf16[256,768]{1,0:T(8,128)(2,1)S(1)} custom-call(bf16[512,512]{1,0:T(8,128)(2,1)S(1)} %copy-done, bf16[512,512]{1,0:T(8,128)(2,1)S(1)} %copy-done.1, bf16[176,512]{1,0:T(8,128)(2,1)S(1)} %collective-permute-done.refs_1_.refs_0_.refs_2_, bf16[176,512]{1,0:T(8,128)(2,1)S(1)} %collective-permute-done.1.refs_2_.refs_1_.refs_3_, ...), custom_call_target="tpu_custom_call" | custom-call | tf_op jit(solution)/shard_map/near_times/pallas_call | solution.py:419
  36.6 1.1 %collective-permute-done.10.refs_2_ = bf16[144,128]{1,0:T(8,128)(2,1)S(1)} collective-permute-done((bf16[144,128]{1,0:T(8,128)(2,1)S(1)}, bf16[144,128]{1,0:T(8,128)(2,1)S(1)}, u32[]{:S(2)}, u32[]{:S(2)}) %collective-permute-start.10) | collective-permute-done | bytes 36896 | tf_op jit(solution)/shard_map/ppermute | solution.py:384
  37.7 0.0 collective-permute-done.8.refs_0_
  37.7 0.0 collective-permute-done.9.refs_1_
  37.7 0.4 near.1.refs_1_
  38.1 0.0 collective-permute-done.7.refs_2_.refs_0_
  38.1 0.2 hidden.1.refs_1_
  38.2 0.1 collective-permute-start.11
  38.3 0.9 %far_times.1 = (bf16[256,768]{1,0:T(8,128)(2,1)S(1)}, bf16[2,192,512]{2,1,0:T(8,128)(2,1)S(1)}, bf16[192,512]{1,0:T(8,128)(2,1)}) custom-call(bf16[208,512]{1,0:T(8,128)(2,1)S(1)} %collective-permute-done.7.refs_2_.refs_0_, bf16[192,512]{1,0:T(8,128)(2,1)S(1)} %hidden.1.refs_1_, bf16[512,512]{1,0:T(8,128)(2,1)S(1)} %copy-done, bf16[512,512]{1,0:T(8,128)(2,1)S(1)} %copy-done.1), custom_call_target="tpu_custom_call" | custom-call | flops 1100000000 | tf_op jit(solution)/shard_map/far_times/pallas_call | solution.py:419
  39.2 0.6 %collective-permute-done.11.refs_3_ = bf16[192,512]{1,0:T(8,128)(2,1)S(1)} collective-permute-done((bf16[192,512]{1,0:T(8,128)(2,1)S(1)}, bf16[192,512]{1,0:T(8,128)(2,1)S(1)}, u32[]{:S(2)}, u32[]{:S(2)}) %collective-permute-start.11) | collective-permute-done | bytes 196640 | tf_op jit(solution)/shard_map/ppermute | solution.py:384
  39.8 0.8 %share.1 = (bf16[128,512]{1,0:T(8,128)(2,1)S(1)}, bf16[64,512]{1,0:T(8,128)(2,1)S(1)}, bf16[64,512]{1,0:T(8,128)(2,1)S(1)}, bf16[64,512]{1,0:T(8,128)(2,1)S(1)},...) custom-call(bf16[256,768]{1,0:T(8,128)(2,1)S(1)} %near_times.1.refs_6_.refs_0_, ...), custom_call_target="tpu_custom_call" | custom-call | flops 1100000000 | tf_op jit(solution)/shard_map/share/pallas_call | solution.py:419
  40.5 0.0 copy-start.3
  40.5 1.0 %collective-permute-start.12 = (bf16[128,512]{1,0:T(8,128)(2,1)S(1)}, bf16[128,512]{1,0:T(8,128)(2,1)S(1)}, u32[]{:S(2)}, u32[]{:S(2)}) collective-permute-start(bf16[128,512]{1,0:T(8,128)(2,1)S(1)} %get-tuple-element.63), channel_id=1, source_target_pairs={{0,2},{2,0},{4,6},{6,4},{8,10},{10,8},{12,14},{14,12},{1,3},{3,1},... | collective-permute-start | bytes 393224 | tf_op jit(solution)/shard_map/ppermute | solution.py:384
  41.6 0.8 %collective-permute-start.15 = (bf16[64,512]{1,0:T(8,128)(2,1)S(1)}, bf16[64,512]{1,0:T(8,128)(2,1)S(1)}, u32[]{:S(2)}, u32[]{:S(2)}) collective-permute-start(bf16[64,512]{1,0:T(8,128)(2,1)S(1)} %get-tuple-element.67), channel_id=1, source_target_pairs={{0,6},{2,4},{4,2},{6,0},{8,14},{10,12},{12,10},{14,8},{1,7},{3,5},... | collective-permute-start | bytes 196616 | tf_op jit(solution)/shard_map/ppermute | solution.py:384
  42.4 1.7 %collective-permute-start.16 = (bf16[64,512]{1,0:T(8,128)(2,1)S(1)}, bf16[64,512]{1,0:T(8,128)(2,1)S(1)}, u32[]{:S(2)}, u32[]{:S(2)}) collective-permute-start(bf16[64,512]{1,0:T(8,128)(2,1)S(1)} %get-tuple-element.68), channel_id=1, source_target_pairs={{0,4},{2,6},{4,0},{6,2},{8,12},{10,14},{12,8},{14,10},{1,5},{3,7},... | collective-permute-start | bytes 196616 | tf_op jit(solution)/shard_map/ppermute | solution.py:384
  44.1 1.3 %collective-permute-start.13 = (bf16[64,512]{1,0:T(8,128)(2,1)S(1)}, bf16[64,512]{1,0:T(8,128)(2,1)S(1)}, u32[]{:S(2)}, u32[]{:S(2)}) collective-permute-start(bf16[64,512]{1,0:T(8,128)(2,1)S(1)} %get-tuple-element.64), channel_id=1, source_target_pairs={{0,6},{2,4},{4,2},{6,0},{8,14},{10,12},{12,10},{14,8},{1,7},{3,5},... | collective-permute-start | bytes 196616 | tf_op jit(solution)/shard_map/ppermute | solution.py:384
  45.4 1.1 %collective-permute-start.14 = (bf16[64,512]{1,0:T(8,128)(2,1)S(1)}, bf16[64,512]{1,0:T(8,128)(2,1)S(1)}, u32[]{:S(2)}, u32[]{:S(2)}) collective-permute-start(bf16[64,512]{1,0:T(8,128)(2,1)S(1)} %get-tuple-element.65), channel_id=1, source_target_pairs={{0,4},{2,6},{4,0},{6,2},{8,12},{10,14},{12,8},{14,10},{1,5},{3,7},... | collective-permute-start | bytes 196616 | tf_op jit(solution)/shard_map/ppermute | solution.py:384
  46.5 0.7 %collective-permute-done.15.refs_1_ = bf16[64,512]{1,0:T(8,128)(2,1)S(1)} collective-permute-done((bf16[64,512]{1,0:T(8,128)(2,1)S(1)}, bf16[64,512]{1,0:T(8,128)(2,1)S(1)}, u32[]{:S(2)}, u32[]{:S(2)}) %collective-permute-start.15) | collective-permute-done | bytes 65568 | tf_op jit(solution)/shard_map/ppermute | solution.py:384
  47.2 1.1 %collective-permute-done.16.refs_2_ = bf16[64,512]{1,0:T(8,128)(2,1)S(1)} collective-permute-done((bf16[64,512]{1,0:T(8,128)(2,1)S(1)}, bf16[64,512]{1,0:T(8,128)(2,1)S(1)}, u32[]{:S(2)}, u32[]{:S(2)}) %collective-permute-start.16) | collective-permute-done | bytes 65568 | tf_op jit(solution)/shard_map/ppermute | solution.py:384
  48.3 0.0 collective-permute-done.12.refs_0_.refs_1_
  48.4 2.4 %collective-permute-start.17 = (bf16[64,512]{1,0:T(8,128)(2,1)S(1)}, bf16[64,512]{1,0:T(8,128)(2,1)S(1)}, u32[]{:S(2)}, u32[]{:S(2)}) collective-permute-start(bf16[64,512]{1,0:T(8,128)(2,1)S(1)} %side_sum.1), channel_id=1, source_target_pairs={{0,8},{2,10},{4,12},{6,14},{8,0},{10,2},{12,4},{14,6},{1,9},{3,11}... | collective-permute-start | bytes 196616 | tf_op jit(solution)/shard_map/ppermute | solution.py:384
  50.8 0.0 collective-permute-done.13.refs_2_
  50.8 0.1 collective-permute-done.14.refs_3_
  50.8 3.5 %collective-permute-done.17.refs_5_ = bf16[64,512]{1,0:T(8,128)(2,1)S(1)} collective-permute-done((bf16[64,512]{1,0:T(8,128)(2,1)S(1)}, bf16[64,512]{1,0:T(8,128)(2,1)S(1)}, u32[]{:S(2)}, u32[]{:S(2)}) %collective-permute-start.17) | collective-permute-done | bytes 65568 | tf_op jit(solution)/shard_map/ppermute | solution.py:384
  54.3 0.0 copy-done.3
  54.3 0.7 %seeds.1 = bf16[64,512]{1,0:T(8,128)(2,1)} custom-call(f32[1,512]{1,0:T(1,128)S(1)} %bitcast.12, bf16[128,512]{1,0:T(8,128)(2,1)S(1)} %collective-permute-done.12.refs_0_.refs_1_, bf16[64,512]{1,0:T(8,128)(2,1)S(1)} %collective-permute-done.13.refs_2_, bf16[64,512]{1,0:T(8,128)(2,1)S(1)} %collective-permute-done.14.refs_3_, ...), custom_call_target="tpu_custom_call" | custom-call | flops 1100000000 | tf_op jit(solution)/shard_map/seeds/pallas_call | solution.py:419
  (2 shorter events, 0.1 us)
Async XLA Ops:
  2.5 13.2 %collective-permute-start = (bf16[176,512]{1,0:T(8,128)(2,1)S(1)}, bf16[176,512]{1,0:T(8,128)(2,1)S(1)}, u32[]{:S(2)}, u32[]{:S(2)}) collective-permute-start(bf16[176,512]{1,0:T(8,128)(2,1)S(1)} %get-tuple-element.36), channel_id=1, source_target_pairs={{0,6},{2,4},{4,2},{6,0},{8,14},{10,12},{12,10},{14,8},{1,7},{3,5},... | collective-permute-start | bytes 540680 | tf_op jit(solution)/shard_map/ppermute | solution.py:384
  6.5 9.1 %collective-permute-start.1 = (bf16[176,512]{1,0:T(8,128)(2,1)S(1)}, bf16[176,512]{1,0:T(8,128)(2,1)S(1)}, u32[]{:S(2)}, u32[]{:S(2)}) collective-permute-start(bf16[176,512]{1,0:T(8,128)(2,1)S(1)} %get-tuple-element.37), channel_id=1, source_target_pairs={{0,4},{2,6},{4,0},{6,2},{8,12},{10,14},{12,8},{14,10},{1,5},{3,7},... | collective-permute-start | bytes 540680 | tf_op jit(solution)/shard_map/ppermute | solution.py:384
  7.0 8.7 %collective-permute-start.2 = (bf16[176,512]{1,0:T(8,128)(2,1)S(1)}, bf16[176,512]{1,0:T(8,128)(2,1)S(1)}, u32[]{:S(2)}, u32[]{:S(2)}) collective-permute-start(bf16[176,512]{1,0:T(8,128)(2,1)S(1)} %get-tuple-element.38), channel_id=1, source_target_pairs={{0,2},{2,0},{4,6},{6,4},{8,10},{10,8},{12,14},{14,12},{1,3},{3,1},... | collective-permute-start | bytes 540680 | tf_op jit(solution)/shard_map/ppermute | solution.py:384
  15.7 6.5 %collective-permute-start.6 = (bf16[4,96,512]{2,1,0:T(8,128)(2,1)S(1)}, bf16[4,96,512]{2,1,0:T(8,128)(2,1)S(1)}, u32[]{:S(2)}, u32[]{:S(2)}) collective-permute-start(bf16[4,96,512]{2,1,0:T(8,128)(2,1)S(1)} %get-tuple-element.48.refs_2_), channel_id=1, source_target_pairs={{0,1},{1,0},{2,3},{3,2},{4,5},{5,4},{6,7},{7,6},{8,9},{9,8},{10,11... | collective-permute-start | bytes 1179656 | tf_op jit(solution)/shard_map/ppermute | solution.py:384
  15.8 7.1 %collective-permute-start.3 = (bf16[160,128]{1,0:T(8,128)(2,1)S(1)}, bf16[160,128]{1,0:T(8,128)(2,1)S(1)}, u32[]{:S(2)}, u32[]{:S(2)}) collective-permute-start(bf16[160,128]{1,0:T(8,128)(2,1)S(1)} %get-tuple-element.45), channel_id=1, source_target_pairs={{0,6},{2,4},{4,2},{6,0},{8,14},{10,12},{12,10},{14,8},{1,7},{3,5},... | collective-permute-start | bytes 122888 | tf_op jit(solution)/shard_map/ppermute | solution.py:384
  18.7 4.2 %collective-permute-start.4 = (bf16[160,128]{1,0:T(8,128)(2,1)S(1)}, bf16[160,128]{1,0:T(8,128)(2,1)S(1)}, u32[]{:S(2)}, u32[]{:S(2)}) collective-permute-start(bf16[160,128]{1,0:T(8,128)(2,1)S(1)} %get-tuple-element.46), channel_id=1, source_target_pairs={{0,4},{2,6},{4,0},{6,2},{8,12},{10,14},{12,8},{14,10},{1,5},{3,7},... | collective-permute-start | bytes 122888 | tf_op jit(solution)/shard_map/ppermute | solution.py:384
  19.2 3.1 %copy-start.2 = (f32[512]{0:T(512)S(1)}, f32[512]{0:T(512)}, u32[]{:S(2)}) copy-start(f32[512]{0:T(512)} %param.18) | copy-start | bytes 6148
  19.2 4.0 %collective-permute-start.5 = (bf16[160,128]{1,0:T(8,128)(2,1)S(1)}, bf16[160,128]{1,0:T(8,128)(2,1)S(1)}, u32[]{:S(2)}, u32[]{:S(2)}) collective-permute-start(bf16[160,128]{1,0:T(8,128)(2,1)S(1)} %get-tuple-element.47), channel_id=1, source_target_pairs={{0,2},{2,0},{4,6},{6,4},{8,10},{10,8},{12,14},{14,12},{1,3},{3,1},... | collective-permute-start | bytes 122888 | tf_op jit(solution)/shard_map/ppermute | solution.py:384
  23.5 14.5 %collective-permute-start.7 = (bf16[208,512]{1,0:T(8,128)(2,1)S(1)}, bf16[208,512]{1,0:T(8,128)(2,1)S(1)}, u32[]{:S(2)}, u32[]{:S(2)}) collective-permute-start(bf16[208,512]{1,0:T(8,128)(2,1)S(1)} %far.1.refs_5_), channel_id=1, source_target_pairs={{0,8},{2,10},{4,12},{6,14},{8,0},{10,2},{12,4},{14,6},{1,9},{3,11}... | collective-permute-start | bytes 638984 | tf_op jit(solution)/shard_map/ppermute | solution.py:384
  29.8 7.9 %collective-permute-start.10 = (bf16[144,128]{1,0:T(8,128)(2,1)S(1)}, bf16[144,128]{1,0:T(8,128)(2,1)S(1)}, u32[]{:S(2)}, u32[]{:S(2)}) collective-permute-start(bf16[144,128]{1,0:T(8,128)(2,1)S(1)} %get-tuple-element.56), channel_id=1, source_target_pairs={{0,6},{2,4},{4,2},{6,0},{8,14},{10,12},{12,10},{14,8},{1,7},{3,5},... | collective-permute-start | bytes 110600 | tf_op jit(solution)/shard_map/ppermute | solution.py:384
  32.0 5.7 %collective-permute-start.8 = (bf16[144,128]{1,0:T(8,128)(2,1)S(1)}, bf16[144,128]{1,0:T(8,128)(2,1)S(1)}, u32[]{:S(2)}, u32[]{:S(2)}) collective-permute-start(bf16[144,128]{1,0:T(8,128)(2,1)S(1)} %get-tuple-element.54), channel_id=1, source_target_pairs={{0,4},{2,6},{4,0},{6,2},{8,12},{10,14},{12,8},{14,10},{1,5},{3,7},... | collective-permute-start | bytes 110600 | tf_op jit(solution)/shard_map/ppermute | solution.py:384
  33.1 4.6 %collective-permute-start.9 = (bf16[144,128]{1,0:T(8,128)(2,1)S(1)}, bf16[144,128]{1,0:T(8,128)(2,1)S(1)}, u32[]{:S(2)}, u32[]{:S(2)}) collective-permute-start(bf16[144,128]{1,0:T(8,128)(2,1)S(1)} %get-tuple-element.55), channel_id=1, source_target_pairs={{0,2},{2,0},{4,6},{6,4},{8,10},{10,8},{12,14},{14,12},{1,3},{3,1},... | collective-permute-start | bytes 110600 | tf_op jit(solution)/shard_map/ppermute | solution.py:384
  33.6 2.2 %copy-start = (bf16[512,512]{1,0:T(8,128)(2,1)S(1)}, bf16[512,512]{1,0:T(8,128)(2,1)}, u32[]{:S(2)}) copy-start(bf16[512,512]{1,0:T(8,128)(2,1)} %refs_4_.3) | copy-start | bytes 1572868
  33.6 2.2 %copy-start.1 = (bf16[512,512]{1,0:T(8,128)(2,1)S(1)}, bf16[512,512]{1,0:T(8,128)(2,1)}, u32[]{:S(2)}) copy-start(bf16[512,512]{1,0:T(8,128)(2,1)} %refs_5_.1) | copy-start | bytes 1572868
  38.2 1.5 %collective-permute-start.11 = (bf16[192,512]{1,0:T(8,128)(2,1)S(1)}, bf16[192,512]{1,0:T(8,128)(2,1)S(1)}, u32[]{:S(2)}, u32[]{:S(2)}) collective-permute-start(bf16[192,512]{1,0:T(8,128)(2,1)S(1)} %hidden.1.refs_1_), channel_id=1, source_target_pairs={{0,1},{1,0},{2,3},{3,2},{4,5},{5,4},{6,7},{7,6},{8,9},{9,8},{10,11... | collective-permute-start | bytes 589832 | tf_op jit(solution)/shard_map/ppermute | solution.py:384
  40.5 13.8 %copy-start.3 = (f32[512]{0:T(512)S(1)}, f32[512]{0:T(512)}, u32[]{:S(2)}) copy-start(f32[512]{0:T(512)} %param.21) | copy-start | bytes 6148
  40.5 7.8 %collective-permute-start.12 = (bf16[128,512]{1,0:T(8,128)(2,1)S(1)}, bf16[128,512]{1,0:T(8,128)(2,1)S(1)}, u32[]{:S(2)}, u32[]{:S(2)}) collective-permute-start(bf16[128,512]{1,0:T(8,128)(2,1)S(1)} %get-tuple-element.63), channel_id=1, source_target_pairs={{0,2},{2,0},{4,6},{6,4},{8,10},{10,8},{12,14},{14,12},{1,3},{3,1},... | collective-permute-start | bytes 393224 | tf_op jit(solution)/shard_map/ppermute | solution.py:384
  41.6 5.7 %collective-permute-start.15 = (bf16[64,512]{1,0:T(8,128)(2,1)S(1)}, bf16[64,512]{1,0:T(8,128)(2,1)S(1)}, u32[]{:S(2)}, u32[]{:S(2)}) collective-permute-start(bf16[64,512]{1,0:T(8,128)(2,1)S(1)} %get-tuple-element.67), channel_id=1, source_target_pairs={{0,6},{2,4},{4,2},{6,0},{8,14},{10,12},{12,10},{14,8},{1,7},{3,5},... | collective-permute-start | bytes 196616 | tf_op jit(solution)/shard_map/ppermute | solution.py:384
  42.4 6.0 %collective-permute-start.16 = (bf16[64,512]{1,0:T(8,128)(2,1)S(1)}, bf16[64,512]{1,0:T(8,128)(2,1)S(1)}, u32[]{:S(2)}, u32[]{:S(2)}) collective-permute-start(bf16[64,512]{1,0:T(8,128)(2,1)S(1)} %get-tuple-element.68), channel_id=1, source_target_pairs={{0,4},{2,6},{4,0},{6,2},{8,12},{10,14},{12,8},{14,10},{1,5},{3,7},... | collective-permute-start | bytes 196616 | tf_op jit(solution)/shard_map/ppermute | solution.py:384
  44.1 6.7 %collective-permute-start.13 = (bf16[64,512]{1,0:T(8,128)(2,1)S(1)}, bf16[64,512]{1,0:T(8,128)(2,1)S(1)}, u32[]{:S(2)}, u32[]{:S(2)}) collective-permute-start(bf16[64,512]{1,0:T(8,128)(2,1)S(1)} %get-tuple-element.64), channel_id=1, source_target_pairs={{0,6},{2,4},{4,2},{6,0},{8,14},{10,12},{12,10},{14,8},{1,7},{3,5},... | collective-permute-start | bytes 196616 | tf_op jit(solution)/shard_map/ppermute | solution.py:384
  45.4 5.4 %collective-permute-start.14 = (bf16[64,512]{1,0:T(8,128)(2,1)S(1)}, bf16[64,512]{1,0:T(8,128)(2,1)S(1)}, u32[]{:S(2)}, u32[]{:S(2)}) collective-permute-start(bf16[64,512]{1,0:T(8,128)(2,1)S(1)} %get-tuple-element.65), channel_id=1, source_target_pairs={{0,4},{2,6},{4,0},{6,2},{8,12},{10,14},{12,8},{14,10},{1,5},{3,7},... | collective-permute-start | bytes 196616 | tf_op jit(solution)/shard_map/ppermute | solution.py:384
  48.4 5.9 %collective-permute-start.17 = (bf16[64,512]{1,0:T(8,128)(2,1)S(1)}, bf16[64,512]{1,0:T(8,128)(2,1)S(1)}, u32[]{:S(2)}, u32[]{:S(2)}) collective-permute-start(bf16[64,512]{1,0:T(8,128)(2,1)S(1)} %side_sum.1), channel_id=1, source_target_pairs={{0,8},{2,10},{4,12},{6,14},{8,0},{10,2},{12,4},{14,6},{1,9},{3,11}... | collective-permute-start | bytes 196616 | tf_op jit(solution)/shard_map/ppermute | solution.py:384

commit v13 on v12

--- a/solution.py
+++ b/solution.py
@@ -92,19 +92,22 @@
     ]
     for copy in copies:
         copy.start()
-    for copy in copies[:-1]:
+    for copy in copies[1:-1]:
         copy.wait()
-    words = pick_ref.shape[1]
-    if fetched_ref.shape[1] == words:
-        pick_ref[:, :, :, :pcap] = fetched_ref[...]
-    else:
-        pick_ref[:, :, :, :pcap] = fetched_ref[:, :words] | (fetched_ref[:, words:] << 16)
+    stride = -(-pcap // LANES) * LANES
+    words = pick_ref.shape[2] // stride
+    for k in range(words):
+        word = fetched_ref[:, k]
+        if words < fetched_ref.shape[1]:
+            word = word | (fetched_ref[:, words + k] << 16)
+        pick_ref[:, :, k * stride : k * stride + pcap] = word
     feat_pos = lax.axis_index("feat")
     first_core = lax.axis_index("rep") == 0
     idx = jnp.concatenate([seed_ref[...], nbr_ref[...]], axis=0)
     high = lax.shift_right_logical(idx, 7)
     digits = jnp.concatenate([high, idx - high * 128], axis=1).astype(jnp.float32)
     weight = jnp.where(first_core, w_self_ref[...], w_nbr_ref[...])
+    copies[0].wait()
     for s, parcel_ref in enumerate(reversed(parcel_refs)):
         sides = []
         for step in (s, s ^ half):
@@ -127,22 +130,24 @@
     lax.fori_loop(0, nodes // width, turn, 0)
 
 
-def mean_kernel(chosen, packed, fanout, pcap, fslice, nbr_any, table_ref, *refs):
+def mean_kernel(chosen, packed, fanout, pcap, fslice, before, n_before, *refs):
     count = len(chosen)
-    token_ref, out_ref, total, nbr_ref, live_ref, sems = refs[-6:]
-    chunk_refs, tagged_refs = refs[-6 - count : -6], refs[: -6 - count]
-    token_ref[...] = jnp.zeros(token_ref.shape, jnp.float32)
+    before_in, refs = refs[: n_before[0]], refs[n_before[0] :]
+    nbr_any, table_ref, *refs = refs
+    out_ref, total, nbr_ref, live_ref, sems = refs[-5:]
+    refs = refs[:-5]
+    before_out = refs[len(refs) - n_before[1] :]
+    refs = refs[: len(refs) - n_before[1]]
+    chunk_refs, tagged_refs = refs[len(refs) - count :], refs[: len(refs) - count]
     feat_pos = lax.axis_index("feat")
     words = fanout // packed
     stride = -(-pcap // LANES) * LANES
+    length = words * stride
     copies = [
         pltpu.make_async_copy(
-            nbr_any.at[feat_pos ^ step, k, 0],
-            nbr_ref.at[pl.ds((i * words + k) * stride, stride)],
-            sems.at[i * words + k],
+            nbr_any.at[feat_pos ^ step, 0], nbr_ref.at[pl.ds(i * length, length)], sems.at[i]
         )
         for i, step in enumerate(chosen)
-        for k in range(words)
     ]
     for copy in copies:
         copy.start()
@@ -150,11 +155,13 @@
         live_ref[i] = pcap
     for i, ref in enumerate(tagged_refs):
         live_ref[i] = live_rows(ref)
+    if before is not None:
+        before(*before_in, *before_out)
     for copy in copies:
         copy.wait()
 
     def partition(i, carry):
-        first = i * (words * stride)
+        first = i * length
 
         def group(g, inner):
             at = pl.multiple_of(g * 16, 16)
@@ -232,17 +239,20 @@
     fslice = w_ref.shape[1]
     pcap, width = pre_ref.shape
     first_core = lax.axis_index("rep") == 0
-    both = jnp.zeros((2 * pcap, width), jnp.float32)
+    feats, weights = [], []
     for s in range(half):
         mine, other = parcel_refs[s][:fslice, :], other_ref[s]
         w_ref[s] = jnp.where(first_core, other, mine)
-        feats = read_feats(parcel_refs[s], fslice, n_idx, 2 * pcap).T.astype(jnp.bfloat16)
-        both = both + jnp.dot(
-            feats, jnp.where(first_core, mine, other), preferred_element_type=jnp.float32
-        )
+        weights.append(jnp.where(first_core, mine, other))
+        feats.append(read_feats(parcel_refs[s], fslice, n_idx, 2 * pcap))
         rows = pl.ds(s // 4 * n_idx, n_idx)
         digits = read_digits(parcel_refs[s], fslice, n_idx, 2 * pcap)
         idx_ref[rows, s % 4 * LANES : (s % 4 + 1) * LANES] = digits.astype(jnp.bfloat16)
+    both = jnp.dot(
+        jnp.concatenate(feats, axis=0).T.astype(jnp.bfloat16),
+        jnp.concatenate(weights, axis=0),
+        preferred_element_type=jnp.float32,
+    )
     pre_ref[...] = both[:pcap] + bias_ref[...]
     far_ref[...] = both[pcap:]
 
@@ -437,7 +447,7 @@
 
     picks = jnp.transpose(nbr_one, (0, 2, 1, 3))
     packed = 2 if fanout_one % 2 == 0 and nodes <= 1 << 16 else 1
-    words = (n_feat, fanout_one // packed, 1, -(-pcap // LANES) * LANES)
+    words = (n_feat, 1, fanout_one // packed * (-(-pcap // LANES) * LANES))
     *parcels, picks, feats = call(
         functools.partial(pack_kernel, n_feat, pcap),
         "pack",
@@ -468,27 +478,36 @@
     table = table.reshape(nodes, 1, LANES)
     chunk_shape = (pcap // 4 * 3, LANES) if folds(fslice, pcap) else (pcap, fslice)
 
-    def means(chosen, tagged=(), after=()):
+    def means(chosen, tagged=(), after=(), before=None, ins=(), outs=()):
         count = len(chosen)
         return call(
-            functools.partial(mean_kernel, tuple(chosen), packed, fanout_one, pcap, fslice),
+            functools.partial(
+                mean_kernel,
+                tuple(chosen),
+                packed,
+                fanout_one,
+                pcap,
+                fslice,
+                before,
+                (len(ins), len(outs)),
+            ),
             "mean",
-            [(chunk_shape, bf16)] * count + [((8, LANES), jnp.float32)],
-            [anywhere] + [vmem] * (1 + len(tagged)),
-            (picks, table, *tagged),
+            [(chunk_shape, bf16)] * count + list(outs),
+            [vmem] * len(ins) + [anywhere] + [vmem] * (1 + len(tagged)),
+            (*ins, picks, table, *tagged),
             after=after,
             scratch=[
                 pltpu.VMEM((count, *chunk_shape), bf16),
                 pltpu.VMEM((pcap, LANES), jnp.float32),
-                pltpu.SMEM((count * words[1] * words[3],), jnp.int32),
+                pltpu.SMEM((count * words[2],), jnp.int32),
                 pltpu.SMEM((count,), jnp.int32),
-                pltpu.SemaphoreType.DMA((count * words[1],)),
+                pltpu.SemaphoreType.DMA((count,)),
             ],
             limit=table_bytes + 8 * MIB,
             cost_us=2 * count if count > 1 else 0,
         )
 
-    *far_means, _ = means([s + half for s in steps if s])
+    far_means = means([s + half for s in steps if s])
     tagged_shape = (chunk_shape[0] + TAG_ROWS, chunk_shape[1])
     halves, *tagged, live = call(
         functools.partial(halves_kernel, half),
@@ -503,21 +522,17 @@
     )
     far_arrived = send(tagged)
     other_halves = swap(halves, "rep", 1)
-    far_own, _ = means([half], after=(halves,))
     idx_rows = -(-half // 4) * n_idx
-    w_nbr, pre, far_pre, idx_tags = call(
-        functools.partial(own_kernel, half, n_idx),
-        "own",
-        [
+    far_own, w_nbr, pre, far_pre, idx_tags = means(
+        [half],
+        before=functools.partial(own_kernel, half, n_idx),
+        ins=(*arrived, other_halves, bias_one[None]),
+        outs=[
             ((half, fslice, width), bf16),
             ((pcap, width), jnp.float32),
             ((pcap, width), jnp.float32),
             ((idx_rows, width), bf16),
         ],
-        [vmem] * (half + 2),
-        (*arrived, other_halves, bias_one[None]),
-        after=(far_own,),
-        cost_us=0,
     )
     (cross,) = call(
         functools.partial(far_kernel, half),
@@ -528,17 +543,15 @@
     )
     cross_arrived = swap(cross, "feat", half)
     turned = [*steps[1:-1], steps[0]]
-    *near_means, token = means(turned, [*far_arrived[1:], far_arrived[0]], (cross,))
+    near_means = means(turned, [*far_arrived[1:], far_arrived[0]], (cross,))
     near_arrived = send(near_means, turned)
-    near_own, _ = means([0], [live], (token,))
-    (near_times,) = call(
-        functools.partial(near_times_kernel, half, fslice, pcap, n_idx),
-        "near_times",
-        [((half * seed_count, 4 * pcap), bf16)],
-        [vmem] * (half + 2),
-        (w2_self, w2_nbr, *arrived),
-        after=(near_own,),
-        cost_us=0,
+    near_own, near_times = means(
+        [0],
+        [live],
+        after=(cross,),
+        before=functools.partial(near_times_kernel, half, fslice, pcap, n_idx),
+        ins=(w2_self, w2_nbr, *arrived),
+        outs=[((half * seed_count, 4 * pcap), bf16)],
     )
     (near_pre,) = call(
         functools.partial(near_kernel, half),
@@ -546,7 +559,6 @@
         [((pcap, width), jnp.float32)],
         [vmem] * (half + 2),
         (*near_arrived, near_own, pre, w_nbr),
-        after=(near_times,),
         cost_us=0,
     )
     (hidden,) = call(

time: 55.2 us -> 53.4 us (0.967)
  Pallas kernels: 23 us -> 20.5 us
  waiting for transfers between devices: 7.19 us -> 7.81 us
    pallas_call x16 -> x14, Pallas kernels: 23 us -> 20.5 us  [call(): pl.pallas_call(wrapped, out_shape=tuple((jax.ShapeDtypeStruct(shape, dtyp...]
    ppermute x18, waiting for transfers between devices: 7.19 us -> 7.81 us  [swap(): return lax.ppermute(value, axis, [(i, i ^ step) for i in range(size)])]
  transfers between devices with their start and end apart: 18 -> 18, of which waited for: 7 -> 9; matrix products, arithmetic and copies ran while one was open for 0% -> 0% of each run, Pallas kernels for 35% -> 32%
where the time goes in v13:
time: 53.4 us; the launch traced here: 52.8 us
  starting transfers between devices  23 us (43%)
  Pallas kernels  20.5 us (38%)
  waiting for transfers between devices  7.81 us (15%)
  between operations  1.47 us (3%)
    ppermute x18, starting transfers between devices, swap(): return lax.ppermute(value, axis, [(i, i ^ step) for i in range(size)])  23 us
    pallas_call x14, Pallas kernels, call(): pl.pallas_call(wrapped, out_shape=tuple((jax.ShapeDtypeStruct(shape, dtyp...  20.5 us
    ppermute x18, waiting for transfers between devices, swap(): return lax.ppermute(value, axis, [(i, i ^ step) for i in range(size)])  7.81 us
  transfers between devices with their start and end apart: 18, of which 9 were waited for; matrix products, arithmetic and copies ran while one was open for 0% of the time, Pallas kernels for 32%

profile of v13, /device:TPU:0, one launch (start us, length us, event | category | flops | bytes accessed | tf_op | source)
XLA Modules:
  0.0 52.8 jit_solution(447043259276858011)
XLA Ops:
  0.6 1.8 %pack.1 = (bf16[176,512]{1,0:T(8,128)(2,1)S(1)}, bf16[176,512]{1,0:T(8,128)(2,1)S(1)}, bf16[176,512]{1,0:T(8,128)(2,1)S(1)}, bf16[176,512]{1,0:T(8,128)(2,1)S(1)...) custom-call(bf16[96,12288]{1,0:T(8,128)(2,1)} %refs_0_.3, s32[1,64]{1,0:T(1,128)} %bitcast.15, ...), custom_call_target="tpu_custom_call" | custom-call | flops 1100000000 | tf_op jit(solution)/shard_map/pack/pallas_call | solution.py:429
  2.5 4.0 %collective-permute-start = (bf16[176,512]{1,0:T(8,128)(2,1)S(1)}, bf16[176,512]{1,0:T(8,128)(2,1)S(1)}, u32[]{:S(2)}, u32[]{:S(2)}) collective-permute-start(bf16[176,512]{1,0:T(8,128)(2,1)S(1)} %get-tuple-element.36), channel_id=1, source_target_pairs={{0,6},{2,4},{4,2},{6,0},{8,14},{10,12},{12,10},{14,8},{1,7},{3,5},... | collective-permute-start | bytes 540680 | tf_op jit(solution)/shard_map/ppermute | solution.py:394
  6.5 0.4 collective-permute-start.1
  7.0 0.2 collective-permute-start.2
  7.2 1.2 %turn.1 = f32[12288,128]{1,0:T(8,128)S(1)} custom-call(bf16[96,12288]{1,0:T(8,128)(2,1)S(1)} %get-tuple-element.41.refs_0_), custom_call_target="tpu_custom_call" | custom-call | flops 3300000000 | tf_op jit(solution)/shard_map/turn/pallas_call | solution.py:429
  8.4 6.0 %mean.4 = (bf16[144,128]{1,0:T(8,128)(2,1)S(1)}, bf16[144,128]{1,0:T(8,128)(2,1)S(1)}, bf16[144,128]{1,0:T(8,128)(2,1)S(1)}) custom-call(s32[8,1,1280]{2,1,0:T(1,128)S(1)} %get-tuple-element.40.refs_0_.refs_6_, f32[12288,1,128]{2,1,0:T(1,128)S(1)} %bitcast.7), custom_call_target="tpu_custom_call" | custom-call | flops 6600000000 | tf_op jit(solution)/shard_map/mean/pallas_call | solution.py:429
  14.4 0.0 copy-start.2
  15.0 0.0 collective-permute-done.refs_1_.refs_0_.refs_2_
  15.1 0.1 collective-permute-done.1.refs_2_.refs_1_.refs_3_
  15.2 0.0 collective-permute-done.2.refs_3_.refs_2_.refs_4_
  15.2 0.1 collective-permute-start.6
  15.3 2.8 %collective-permute-start.3 = (bf16[160,128]{1,0:T(8,128)(2,1)S(1)}, bf16[160,128]{1,0:T(8,128)(2,1)S(1)}, u32[]{:S(2)}, u32[]{:S(2)}) collective-permute-start(bf16[160,128]{1,0:T(8,128)(2,1)S(1)} %get-tuple-element.45), channel_id=1, source_target_pairs={{0,6},{2,4},{4,2},{6,0},{8,14},{10,12},{12,10},{14,8},{1,7},{3,5},... | collective-permute-start | bytes 122888 | tf_op jit(solution)/shard_map/ppermute | solution.py:394
  18.1 0.4 collective-permute-start.4
  18.6 0.3 collective-permute-start.5
  18.8 0.0 collective-permute-done.6.refs_4_
  18.8 0.0 copy-done.2
  18.8 2.7 %mean.5 = (bf16[144,128]{1,0:T(8,128)(2,1)S(1)}, bf16[4,96,512]{2,1,0:T(8,128)(2,1)S(1)}, f32[192,512]{1,0:T(8,128)S(1)}, f32[192,512]{1,0:T(8,128)S(1)}, bf16[16,512]{1,0:T(8,128)(2,1)S(1)}) custom-call(bf16[176,512]{1,0:T(8,128)(2,1)S(1)} %collective-permute-done.refs_1_.refs_0_.refs_2_, ...), custom_call_target="tpu_custom_call" | custom-call | tf_op jit(solution)/shard_map/mean/pallas_call | solution.py:429
  21.5 0.0 collective-permute-done.3.refs_0_.refs_4_
  21.5 0.6 %collective-permute-done.4.refs_1_.refs_2_ = bf16[160,128]{1,0:T(8,128)(2,1)S(1)} collective-permute-done((bf16[160,128]{1,0:T(8,128)(2,1)S(1)}, bf16[160,128]{1,0:T(8,128)(2,1)S(1)}, u32[]{:S(2)}, u32[]{:S(2)}) %collective-permute-start.4) | collective-permute-done | bytes 40992 | tf_op jit(solution)/shard_map/ppermute | solution.py:394
  22.1 0.4 collective-permute-done.5.refs_2_.refs_3_
  22.6 0.4 far.1.refs_5_.refs_9_
  22.9 0.0 copy-start
  23.0 0.0 copy-start.1
  23.0 2.6 %collective-permute-start.7 = (bf16[208,512]{1,0:T(8,128)(2,1)S(1)}, bf16[208,512]{1,0:T(8,128)(2,1)S(1)}, u32[]{:S(2)}, u32[]{:S(2)}) collective-permute-start(bf16[208,512]{1,0:T(8,128)(2,1)S(1)} %far.1.refs_5_.refs_9_), channel_id=1, source_target_pairs={{0,8},{2,10},{4,12},{6,14},{8,0},{10,2},{12,4},{14,6},{1,9},{3,11}... | collective-permute-start | bytes 638984 | tf_op jit(solution)/shard_map/ppermute | solution.py:394
  25.6 4.2 %mean.6 = (bf16[144,128]{1,0:T(8,128)(2,1)S(1)}, bf16[144,128]{1,0:T(8,128)(2,1)S(1)}, bf16[144,128]{1,0:T(8,128)(2,1)S(1)}) custom-call(s32[8,1,1280]{2,1,0:T(1,128)S(1)} %get-tuple-element.40.refs_0_.refs_6_, f32[12288,1,128]{2,1,0:T(1,128)S(1)} %bitcast.9, bf16[160,128]{1,0:T(8,128)(2,1)S(1)} %collective-permute-done.4.refs_1_.refs_2_, ...), custom_call_target="tpu_custom_call" | custom-call | flops 6600000000 | tf_op jit(solution)/shard_map/mean/pallas_call | solution.py:429
  29.8 1.6 %collective-permute-start.10 = (bf16[144,128]{1,0:T(8,128)(2,1)S(1)}, bf16[144,128]{1,0:T(8,128)(2,1)S(1)}, u32[]{:S(2)}, u32[]{:S(2)}) collective-permute-start(bf16[144,128]{1,0:T(8,128)(2,1)S(1)} %get-tuple-element.56), channel_id=1, source_target_pairs={{0,6},{2,4},{4,2},{6,0},{8,14},{10,12},{12,10},{14,8},{1,7},{3,5},... | collective-permute-start | bytes 110600 | tf_op jit(solution)/shard_map/ppermute | solution.py:394
  31.4 0.0 collective-permute-start.8
  31.4 2.0 %collective-permute-start.9 = (bf16[144,128]{1,0:T(8,128)(2,1)S(1)}, bf16[144,128]{1,0:T(8,128)(2,1)S(1)}, u32[]{:S(2)}, u32[]{:S(2)}) collective-permute-start(bf16[144,128]{1,0:T(8,128)(2,1)S(1)} %get-tuple-element.55), channel_id=1, source_target_pairs={{0,2},{2,0},{4,6},{6,4},{8,10},{10,8},{12,14},{14,12},{1,3},{3,1},... | collective-permute-start | bytes 110600 | tf_op jit(solution)/shard_map/ppermute | solution.py:394
  33.4 0.0 copy-done
  33.4 0.0 copy-done.1
  33.4 1.3 %mean.7 = (bf16[144,128]{1,0:T(8,128)(2,1)S(1)}, bf16[256,768]{1,0:T(8,128)(2,1)S(1)}) custom-call(bf16[512,512]{1,0:T(8,128)(2,1)S(1)} %copy-done, bf16[512,512]{1,0:T(8,128)(2,1)S(1)} %copy-done.1, bf16[176,512]{1,0:T(8,128)(2,1)S(1)} %collective-permute-done.refs_1_.refs_0_.refs_2_, bf16[176,512]{1,0:T(8,128)(2,1)S(1)} %collective-permute-done.1.refs_2_.refs_1_.refs_3_, ...), custom_call_target="tpu_custom_call" | custom-call | tf_op jit(solution)/shard_map/mean/pallas_call | solution.py:429
  34.7 1.6 %collective-permute-done.10.refs_2_ = bf16[144,128]{1,0:T(8,128)(2,1)S(1)} collective-permute-done((bf16[144,128]{1,0:T(8,128)(2,1)S(1)}, bf16[144,128]{1,0:T(8,128)(2,1)S(1)}, u32[]{:S(2)}, u32[]{:S(2)}) %collective-permute-start.10) | collective-permute-done | bytes 36896 | tf_op jit(solution)/shard_map/ppermute | solution.py:394
  36.3 0.0 collective-permute-done.8.refs_0_
  36.3 0.0 collective-permute-done.9.refs_1_
  36.3 0.4 near.1.refs_1_
  36.7 0.0 collective-permute-done.7.refs_2_.refs_0_
  36.7 0.2 hidden.1.refs_1_
  36.9 0.1 collective-permute-start.11
  37.0 0.9 %far_times.1 = (bf16[256,768]{1,0:T(8,128)(2,1)S(1)}, bf16[2,192,512]{2,1,0:T(8,128)(2,1)S(1)}, bf16[192,512]{1,0:T(8,128)(2,1)}) custom-call(bf16[208,512]{1,0:T(8,128)(2,1)S(1)} %collective-permute-done.7.refs_2_.refs_0_, bf16[192,512]{1,0:T(8,128)(2,1)S(1)} %hidden.1.refs_1_, bf16[512,512]{1,0:T(8,128)(2,1)S(1)} %copy-done, bf16[512,512]{1,0:T(8,128)(2,1)S(1)} %copy-done.1), custom_call_target="tpu_custom_call" | custom-call | flops 1100000000 | tf_op jit(solution)/shard_map/far_times/pallas_call | solution.py:429
  37.8 0.6 %collective-permute-done.11.refs_3_ = bf16[192,512]{1,0:T(8,128)(2,1)S(1)} collective-permute-done((bf16[192,512]{1,0:T(8,128)(2,1)S(1)}, bf16[192,512]{1,0:T(8,128)(2,1)S(1)}, u32[]{:S(2)}, u32[]{:S(2)}) %collective-permute-start.11) | collective-permute-done | bytes 196640 | tf_op jit(solution)/shard_map/ppermute | solution.py:394
  38.4 0.8 %share.1 = (bf16[128,512]{1,0:T(8,128)(2,1)S(1)}, bf16[64,512]{1,0:T(8,128)(2,1)S(1)}, bf16[64,512]{1,0:T(8,128)(2,1)S(1)}, bf16[64,512]{1,0:T(8,128)(2,1)S(1)},...) custom-call(bf16[256,768]{1,0:T(8,128)(2,1)S(1)} %get-tuple-element.60.refs_0_, ...), custom_call_target="tpu_custom_call" | custom-call | flops 1100000000 | tf_op jit(solution)/shard_map/share/pallas_call | solution.py:429
  39.2 0.0 copy-start.3
  39.2 1.3 %collective-permute-start.12 = (bf16[128,512]{1,0:T(8,128)(2,1)S(1)}, bf16[128,512]{1,0:T(8,128)(2,1)S(1)}, u32[]{:S(2)}, u32[]{:S(2)}) collective-permute-start(bf16[128,512]{1,0:T(8,128)(2,1)S(1)} %get-tuple-element.63), channel_id=1, source_target_pairs={{0,2},{2,0},{4,6},{6,4},{8,10},{10,8},{12,14},{14,12},{1,3},{3,1},... | collective-permute-start | bytes 393224 | tf_op jit(solution)/shard_map/ppermute | solution.py:394
  40.5 1.2 %collective-permute-start.15 = (bf16[64,512]{1,0:T(8,128)(2,1)S(1)}, bf16[64,512]{1,0:T(8,128)(2,1)S(1)}, u32[]{:S(2)}, u32[]{:S(2)}) collective-permute-start(bf16[64,512]{1,0:T(8,128)(2,1)S(1)} %get-tuple-element.67), channel_id=1, source_target_pairs={{0,6},{2,4},{4,2},{6,0},{8,14},{10,12},{12,10},{14,8},{1,7},{3,5},... | collective-permute-start | bytes 196616 | tf_op jit(solution)/shard_map/ppermute | solution.py:394
  41.8 1.0 %collective-permute-start.16 = (bf16[64,512]{1,0:T(8,128)(2,1)S(1)}, bf16[64,512]{1,0:T(8,128)(2,1)S(1)}, u32[]{:S(2)}, u32[]{:S(2)}) collective-permute-start(bf16[64,512]{1,0:T(8,128)(2,1)S(1)} %get-tuple-element.68), channel_id=1, source_target_pairs={{0,4},{2,6},{4,0},{6,2},{8,12},{10,14},{12,8},{14,10},{1,5},{3,7},... | collective-permute-start | bytes 196616 | tf_op jit(solution)/shard_map/ppermute | solution.py:394
  42.8 1.2 %collective-permute-start.13 = (bf16[64,512]{1,0:T(8,128)(2,1)S(1)}, bf16[64,512]{1,0:T(8,128)(2,1)S(1)}, u32[]{:S(2)}, u32[]{:S(2)}) collective-permute-start(bf16[64,512]{1,0:T(8,128)(2,1)S(1)} %get-tuple-element.64), channel_id=1, source_target_pairs={{0,6},{2,4},{4,2},{6,0},{8,14},{10,12},{12,10},{14,8},{1,7},{3,5},... | collective-permute-start | bytes 196616 | tf_op jit(solution)/shard_map/ppermute | solution.py:394
  44.0 1.5 %collective-permute-start.14 = (bf16[64,512]{1,0:T(8,128)(2,1)S(1)}, bf16[64,512]{1,0:T(8,128)(2,1)S(1)}, u32[]{:S(2)}, u32[]{:S(2)}) collective-permute-start(bf16[64,512]{1,0:T(8,128)(2,1)S(1)} %get-tuple-element.65), channel_id=1, source_target_pairs={{0,4},{2,6},{4,0},{6,2},{8,12},{10,14},{12,8},{14,10},{1,5},{3,7},... | collective-permute-start | bytes 196616 | tf_op jit(solution)/shard_map/ppermute | solution.py:394
  45.5 1.0 %collective-permute-done.15.refs_1_ = bf16[64,512]{1,0:T(8,128)(2,1)S(1)} collective-permute-done((bf16[64,512]{1,0:T(8,128)(2,1)S(1)}, bf16[64,512]{1,0:T(8,128)(2,1)S(1)}, u32[]{:S(2)}, u32[]{:S(2)}) %collective-permute-start.15) | collective-permute-done | bytes 65568 | tf_op jit(solution)/shard_map/ppermute | solution.py:394
  46.5 0.3 collective-permute-done.16.refs_2_
  46.8 0.1 collective-permute-done.12.refs_0_.refs_1_
  46.9 2.1 %collective-permute-start.17 = (bf16[64,512]{1,0:T(8,128)(2,1)S(1)}, bf16[64,512]{1,0:T(8,128)(2,1)S(1)}, u32[]{:S(2)}, u32[]{:S(2)}) collective-permute-start(bf16[64,512]{1,0:T(8,128)(2,1)S(1)} %side_sum.1), channel_id=1, source_target_pairs={{0,8},{2,10},{4,12},{6,14},{8,0},{10,2},{12,4},{14,6},{1,9},{3,11}... | collective-permute-start | bytes 196616 | tf_op jit(solution)/shard_map/ppermute | solution.py:394
  49.0 0.0 collective-permute-done.13.refs_2_
  49.0 0.0 collective-permute-done.14.refs_3_
  49.0 3.1 %collective-permute-done.17.refs_5_ = bf16[64,512]{1,0:T(8,128)(2,1)S(1)} collective-permute-done((bf16[64,512]{1,0:T(8,128)(2,1)S(1)}, bf16[64,512]{1,0:T(8,128)(2,1)S(1)}, u32[]{:S(2)}, u32[]{:S(2)}) %collective-permute-start.17) | collective-permute-done | bytes 65568 | tf_op jit(solution)/shard_map/ppermute | solution.py:394
  52.1 0.0 copy-done.3
  52.1 0.7 %seeds.1 = bf16[64,512]{1,0:T(8,128)(2,1)} custom-call(f32[1,512]{1,0:T(1,128)S(1)} %bitcast.12, bf16[128,512]{1,0:T(8,128)(2,1)S(1)} %collective-permute-done.12.refs_0_.refs_1_, bf16[64,512]{1,0:T(8,128)(2,1)S(1)} %collective-permute-done.13.refs_2_, bf16[64,512]{1,0:T(8,128)(2,1)S(1)} %collective-permute-done.14.refs_3_, ...), custom_call_target="tpu_custom_call" | custom-call | flops 1100000000 | tf_op jit(solution)/shard_map/seeds/pallas_call | solution.py:429
  (2 shorter events, 0.1 us)
Async XLA Ops:
  2.5 12.6 %collective-permute-start = (bf16[176,512]{1,0:T(8,128)(2,1)S(1)}, bf16[176,512]{1,0:T(8,128)(2,1)S(1)}, u32[]{:S(2)}, u32[]{:S(2)}) collective-permute-start(bf16[176,512]{1,0:T(8,128)(2,1)S(1)} %get-tuple-element.36), channel_id=1, source_target_pairs={{0,6},{2,4},{4,2},{6,0},{8,14},{10,12},{12,10},{14,8},{1,7},{3,5},... | collective-permute-start | bytes 540680 | tf_op jit(solution)/shard_map/ppermute | solution.py:394
  6.5 8.6 %collective-permute-start.1 = (bf16[176,512]{1,0:T(8,128)(2,1)S(1)}, bf16[176,512]{1,0:T(8,128)(2,1)S(1)}, u32[]{:S(2)}, u32[]{:S(2)}) collective-permute-start(bf16[176,512]{1,0:T(8,128)(2,1)S(1)} %get-tuple-element.37), channel_id=1, source_target_pairs={{0,4},{2,6},{4,0},{6,2},{8,12},{10,14},{12,8},{14,10},{1,5},{3,7},... | collective-permute-start | bytes 540680 | tf_op jit(solution)/shard_map/ppermute | solution.py:394
  7.0 8.2 %collective-permute-start.2 = (bf16[176,512]{1,0:T(8,128)(2,1)S(1)}, bf16[176,512]{1,0:T(8,128)(2,1)S(1)}, u32[]{:S(2)}, u32[]{:S(2)}) collective-permute-start(bf16[176,512]{1,0:T(8,128)(2,1)S(1)} %get-tuple-element.38), channel_id=1, source_target_pairs={{0,2},{2,0},{4,6},{6,4},{8,10},{10,8},{12,14},{14,12},{1,3},{3,1},... | collective-permute-start | bytes 540680 | tf_op jit(solution)/shard_map/ppermute | solution.py:394
  14.4 4.5 %copy-start.2 = (f32[512]{0:T(512)S(1)}, f32[512]{0:T(512)}, u32[]{:S(2)}) copy-start(f32[512]{0:T(512)} %param.18) | copy-start | bytes 6148
  15.2 3.6 %collective-permute-start.6 = (bf16[4,96,512]{2,1,0:T(8,128)(2,1)S(1)}, bf16[4,96,512]{2,1,0:T(8,128)(2,1)S(1)}, u32[]{:S(2)}, u32[]{:S(2)}) collective-permute-start(bf16[4,96,512]{2,1,0:T(8,128)(2,1)S(1)} %get-tuple-element.48), channel_id=1, source_target_pairs={{0,1},{1,0},{2,3},{3,2},{4,5},{5,4},{6,7},{7,6},{8,9},{9,8},{10,11... | collective-permute-start | bytes 1179656 | tf_op jit(solution)/shard_map/ppermute | solution.py:394
  15.3 6.3 %collective-permute-start.3 = (bf16[160,128]{1,0:T(8,128)(2,1)S(1)}, bf16[160,128]{1,0:T(8,128)(2,1)S(1)}, u32[]{:S(2)}, u32[]{:S(2)}) collective-permute-start(bf16[160,128]{1,0:T(8,128)(2,1)S(1)} %get-tuple-element.45), channel_id=1, source_target_pairs={{0,6},{2,4},{4,2},{6,0},{8,14},{10,12},{12,10},{14,8},{1,7},{3,5},... | collective-permute-start | bytes 122888 | tf_op jit(solution)/shard_map/ppermute | solution.py:394
  18.1 4.0 %collective-permute-start.4 = (bf16[160,128]{1,0:T(8,128)(2,1)S(1)}, bf16[160,128]{1,0:T(8,128)(2,1)S(1)}, u32[]{:S(2)}, u32[]{:S(2)}) collective-permute-start(bf16[160,128]{1,0:T(8,128)(2,1)S(1)} %get-tuple-element.46), channel_id=1, source_target_pairs={{0,4},{2,6},{4,0},{6,2},{8,12},{10,14},{12,8},{14,10},{1,5},{3,7},... | collective-permute-start | bytes 122888 | tf_op jit(solution)/shard_map/ppermute | solution.py:394
  18.6 4.0 %collective-permute-start.5 = (bf16[160,128]{1,0:T(8,128)(2,1)S(1)}, bf16[160,128]{1,0:T(8,128)(2,1)S(1)}, u32[]{:S(2)}, u32[]{:S(2)}) collective-permute-start(bf16[160,128]{1,0:T(8,128)(2,1)S(1)} %get-tuple-element.47), channel_id=1, source_target_pairs={{0,2},{2,0},{4,6},{6,4},{8,10},{10,8},{12,14},{14,12},{1,3},{3,1},... | collective-permute-start | bytes 122888 | tf_op jit(solution)/shard_map/ppermute | solution.py:394
  22.9 10.4 %copy-start = (bf16[512,512]{1,0:T(8,128)(2,1)S(1)}, bf16[512,512]{1,0:T(8,128)(2,1)}, u32[]{:S(2)}) copy-start(bf16[512,512]{1,0:T(8,128)(2,1)} %refs_4_.3) | copy-start | bytes 1572868
  23.0 10.4 %copy-start.1 = (bf16[512,512]{1,0:T(8,128)(2,1)S(1)}, bf16[512,512]{1,0:T(8,128)(2,1)}, u32[]{:S(2)}) copy-start(bf16[512,512]{1,0:T(8,128)(2,1)} %refs_5_.1) | copy-start | bytes 1572868
  23.0 13.7 %collective-permute-start.7 = (bf16[208,512]{1,0:T(8,128)(2,1)S(1)}, bf16[208,512]{1,0:T(8,128)(2,1)S(1)}, u32[]{:S(2)}, u32[]{:S(2)}) collective-permute-start(bf16[208,512]{1,0:T(8,128)(2,1)S(1)} %far.1.refs_5_.refs_9_), channel_id=1, source_target_pairs={{0,8},{2,10},{4,12},{6,14},{8,0},{10,2},{12,4},{14,6},{1,9},{3,11}... | collective-permute-start | bytes 638984 | tf_op jit(solution)/shard_map/ppermute | solution.py:394
  29.8 6.5 %collective-permute-start.10 = (bf16[144,128]{1,0:T(8,128)(2,1)S(1)}, bf16[144,128]{1,0:T(8,128)(2,1)S(1)}, u32[]{:S(2)}, u32[]{:S(2)}) collective-permute-start(bf16[144,128]{1,0:T(8,128)(2,1)S(1)} %get-tuple-element.56), channel_id=1, source_target_pairs={{0,6},{2,4},{4,2},{6,0},{8,14},{10,12},{12,10},{14,8},{1,7},{3,5},... | collective-permute-start | bytes 110600 | tf_op jit(solution)/shard_map/ppermute | solution.py:394
  31.4 4.9 %collective-permute-start.8 = (bf16[144,128]{1,0:T(8,128)(2,1)S(1)}, bf16[144,128]{1,0:T(8,128)(2,1)S(1)}, u32[]{:S(2)}, u32[]{:S(2)}) collective-permute-start(bf16[144,128]{1,0:T(8,128)(2,1)S(1)} %get-tuple-element.54), channel_id=1, source_target_pairs={{0,4},{2,6},{4,0},{6,2},{8,12},{10,14},{12,8},{14,10},{1,5},{3,7},... | collective-permute-start | bytes 110600 | tf_op jit(solution)/shard_map/ppermute | solution.py:394
  31.4 4.9 %collective-permute-start.9 = (bf16[144,128]{1,0:T(8,128)(2,1)S(1)}, bf16[144,128]{1,0:T(8,128)(2,1)S(1)}, u32[]{:S(2)}, u32[]{:S(2)}) collective-permute-start(bf16[144,128]{1,0:T(8,128)(2,1)S(1)} %get-tuple-element.55), channel_id=1, source_target_pairs={{0,2},{2,0},{4,6},{6,4},{8,10},{10,8},{12,14},{14,12},{1,3},{3,1},... | collective-permute-start | bytes 110600 | tf_op jit(solution)/shard_map/ppermute | solution.py:394
  36.9 1.5 %collective-permute-start.11 = (bf16[192,512]{1,0:T(8,128)(2,1)S(1)}, bf16[192,512]{1,0:T(8,128)(2,1)S(1)}, u32[]{:S(2)}, u32[]{:S(2)}) collective-permute-start(bf16[192,512]{1,0:T(8,128)(2,1)S(1)} %hidden.1.refs_1_), channel_id=1, source_target_pairs={{0,1},{1,0},{2,3},{3,2},{4,5},{5,4},{6,7},{7,6},{8,9},{9,8},{10,11... | collective-permute-start | bytes 589832 | tf_op jit(solution)/shard_map/ppermute | solution.py:394
  39.2 12.9 %copy-start.3 = (f32[512]{0:T(512)S(1)}, f32[512]{0:T(512)}, u32[]{:S(2)}) copy-start(f32[512]{0:T(512)} %param.21) | copy-start | bytes 6148
  39.2 7.7 %collective-permute-start.12 = (bf16[128,512]{1,0:T(8,128)(2,1)S(1)}, bf16[128,512]{1,0:T(8,128)(2,1)S(1)}, u32[]{:S(2)}, u32[]{:S(2)}) collective-permute-start(bf16[128,512]{1,0:T(8,128)(2,1)S(1)} %get-tuple-element.63), channel_id=1, source_target_pairs={{0,2},{2,0},{4,6},{6,4},{8,10},{10,8},{12,14},{14,12},{1,3},{3,1},... | collective-permute-start | bytes 393224 | tf_op jit(solution)/shard_map/ppermute | solution.py:394
  40.5 5.9 %collective-permute-start.15 = (bf16[64,512]{1,0:T(8,128)(2,1)S(1)}, bf16[64,512]{1,0:T(8,128)(2,1)S(1)}, u32[]{:S(2)}, u32[]{:S(2)}) collective-permute-start(bf16[64,512]{1,0:T(8,128)(2,1)S(1)} %get-tuple-element.67), channel_id=1, source_target_pairs={{0,6},{2,4},{4,2},{6,0},{8,14},{10,12},{12,10},{14,8},{1,7},{3,5},... | collective-permute-start | bytes 196616 | tf_op jit(solution)/shard_map/ppermute | solution.py:394
  41.8 5.0 %collective-permute-start.16 = (bf16[64,512]{1,0:T(8,128)(2,1)S(1)}, bf16[64,512]{1,0:T(8,128)(2,1)S(1)}, u32[]{:S(2)}, u32[]{:S(2)}) collective-permute-start(bf16[64,512]{1,0:T(8,128)(2,1)S(1)} %get-tuple-element.68), channel_id=1, source_target_pairs={{0,4},{2,6},{4,0},{6,2},{8,12},{10,14},{12,8},{14,10},{1,5},{3,7},... | collective-permute-start | bytes 196616 | tf_op jit(solution)/shard_map/ppermute | solution.py:394
  42.8 6.3 %collective-permute-start.13 = (bf16[64,512]{1,0:T(8,128)(2,1)S(1)}, bf16[64,512]{1,0:T(8,128)(2,1)S(1)}, u32[]{:S(2)}, u32[]{:S(2)}) collective-permute-start(bf16[64,512]{1,0:T(8,128)(2,1)S(1)} %get-tuple-element.64), channel_id=1, source_target_pairs={{0,6},{2,4},{4,2},{6,0},{8,14},{10,12},{12,10},{14,8},{1,7},{3,5},... | collective-permute-start | bytes 196616 | tf_op jit(solution)/shard_map/ppermute | solution.py:394
  44.0 5.0 %collective-permute-start.14 = (bf16[64,512]{1,0:T(8,128)(2,1)S(1)}, bf16[64,512]{1,0:T(8,128)(2,1)S(1)}, u32[]{:S(2)}, u32[]{:S(2)}) collective-permute-start(bf16[64,512]{1,0:T(8,128)(2,1)S(1)} %get-tuple-element.65), channel_id=1, source_target_pairs={{0,4},{2,6},{4,0},{6,2},{8,12},{10,14},{12,8},{14,10},{1,5},{3,7},... | collective-permute-start | bytes 196616 | tf_op jit(solution)/shard_map/ppermute | solution.py:394
  46.9 5.2 %collective-permute-start.17 = (bf16[64,512]{1,0:T(8,128)(2,1)S(1)}, bf16[64,512]{1,0:T(8,128)(2,1)S(1)}, u32[]{:S(2)}, u32[]{:S(2)}) collective-permute-start(bf16[64,512]{1,0:T(8,128)(2,1)S(1)} %side_sum.1), channel_id=1, source_target_pairs={{0,8},{2,10},{4,12},{6,14},{8,0},{10,2},{12,4},{14,6},{1,9},{3,11}... | collective-permute-start | bytes 196616 | tf_op jit(solution)/shard_map/ppermute | solution.py:394

commit v14 on v13

--- a/solution.py
+++ b/solution.py
@@ -257,21 +257,23 @@
     far_ref[...] = both[pcap:]
 
 
-def add_means(half, pre, mean_refs, w_ref, turn=0):
+def add_means(pre, mean_refs, w_ref):
     for s, ref in enumerate(mean_refs):
         pre = pre + jnp.dot(
             unfold(ref, w_ref.shape[1], pre.shape[0]),
-            w_ref[(s + turn) % (half - 1) if s < half - 1 else s],
+            w_ref[s],
             preferred_element_type=jnp.float32,
         )
     return pre
 
 
 def far_kernel(half, *refs):
-    far_ref, w_ref, idx_ref, cross_ref = refs[half:]
-    pcap = far_ref.shape[0]
-    cross_ref[:pcap, :] = add_means(half, far_ref[...], refs[:half], w_ref).astype(jnp.bfloat16)
-    cross_ref[pcap:, :] = idx_ref[...]
+    far_ref, w_ref, cross_ref = refs[half:]
+    cross_ref[...] = add_means(far_ref[...], refs[:half], w_ref).astype(jnp.bfloat16)
+
+
+def copy_kernel(in_ref, out_ref):
+    out_ref[...] = in_ref[...]
 
 
 def store_times(pcap, blocks, out_ref):
@@ -294,8 +296,11 @@
         for k in range(1, n_idx):
             near = near + jnp.where(slot == name[k : k + 1], 1.0, 0.0)
         place = pl.ds(s * seed_count, pair)
-        out_ref[place, : 2 * pcap] = own.T.astype(jnp.bfloat16)
-        out_ref[place, 2 * pcap :] = near.T.astype(jnp.bfloat16)
+        for core in range(2):
+            rows = slice(core * pcap, (core + 1) * pcap)
+            counts = jnp.concatenate([own[rows], near[rows]], axis=0)
+            lanes = slice(2 * core * pcap, 2 * (core + 1) * pcap)
+            out_ref[place, lanes] = counts.T.astype(jnp.bfloat16)
 
 
 def near_times_kernel(half, fslice, pcap, n_idx, _, __, *refs):
@@ -303,45 +308,39 @@
     store_times(pcap, blocks, refs[half])
 
 
-def far_times_kernel(
-    half,
-    n_idx,
-    fanout_two,
-    cross_ref,
-    hidden_ref,
-    ws_ref,
-    wn_ref,
-    out_ref,
-    value_ref,
-    result_ref,
-    sem,
+def far_times_kernel(half, pcap, n_idx, idx_ref, out_ref):
+    blocks = [
+        idx_ref[pl.ds(s // 4 * n_idx, n_idx), s % 4 * LANES : (s % 4 + 1) * LANES]
+        for s in range(half)
+    ]
+    store_times(pcap, blocks, out_ref)
+
+
+def values_of(hidden, ws_ref, wn_ref, fanout_two):
+    return jnp.concatenate(
+        [
+            jnp.dot(hidden, ws_ref[...], preferred_element_type=jnp.float32),
+            jnp.dot(hidden, wn_ref[...], preferred_element_type=jnp.float32) / fanout_two,
+        ],
+        axis=0,
+    ).astype(jnp.bfloat16)
+
+
+def own_share_kernel(
+    fanout_two, near_ref, far_ref, hidden_ref, ws_ref, wn_ref, part_ref, result_ref, sem
 ):
     copy = pltpu.make_async_copy(hidden_ref, result_ref, sem)
     copy.start()
-    pcap = hidden_ref.shape[0]
-    blocks = [
-        cross_ref[
-            pl.ds(pcap + s // 4 * n_idx, n_idx), s % 4 * LANES : (s % 4 + 1) * LANES
-        ]
-        for s in range(half)
-    ]
-    store_times(pcap, blocks, out_ref)
-    store_values(hidden_ref[...], ws_ref, wn_ref, fanout_two, value_ref)
+    values = values_of(hidden_ref[...], ws_ref, wn_ref, fanout_two)
+    lanes = values.shape[0]
+    for i, ref in enumerate((far_ref, near_ref)):
+        part_ref[i] = jnp.dot(ref[:, :lanes], values, preferred_element_type=jnp.float32)
     copy.wait()
-
-
-def store_values(hidden, ws_ref, wn_ref, fanout_two, value_ref):
-    value_ref[0] = jnp.dot(hidden, ws_ref[...], preferred_element_type=jnp.float32).astype(
-        jnp.bfloat16
-    )
-    value_ref[1] = (
-        jnp.dot(hidden, wn_ref[...], preferred_element_type=jnp.float32) / fanout_two
-    ).astype(jnp.bfloat16)
 
 
 def near_kernel(half, *refs):
     pre_ref, w_ref, out_ref = refs[half:]
-    out_ref[...] = add_means(half, pre_ref[...], refs[:half], w_ref, 1)
+    out_ref[...] = add_means(pre_ref[...], refs[:half], w_ref)
 
 
 def hidden_kernel(live_ref, pre_ref, cross_ref, hidden_ref):
@@ -351,41 +350,27 @@
     hidden_ref[...] = jnp.where(live, jnp.maximum(pre, 0.0), 0.0).astype(jnp.bfloat16)
 
 
-def share_kernel(
-    half, fanout_two, near_ref, far_ref, value_ref, hidden_ref, ws_ref, wn_ref, *refs
-):
-    *out_refs, other_ref = refs
-    store_values(hidden_ref[...], ws_ref, wn_ref, fanout_two, other_ref)
-    values = jnp.concatenate(
-        [value_ref[0], other_ref[0], value_ref[1], other_ref[1]], axis=0
-    )
-    rows = far_ref.shape[0] // half
-    both_ref, far_refs, near_refs = out_refs[0], out_refs[1:half], out_refs[half:]
-    for times_ref, refs, low in ((far_ref, far_refs, 0), (near_ref, near_refs, rows)):
-        part = jnp.dot(times_ref[...], values, preferred_element_type=jnp.float32)
-        part = part.astype(jnp.bfloat16)
-        both_ref[low : low + rows, :] = part[(half - 2) * rows : (half - 1) * rows]
-        for i, ref in enumerate(refs):
-            place = i if i < half - 2 else half - 1
-            ref[...] = part[place * rows : (place + 1) * rows]
-
-
-def sum_rows(first, low, refs, rows):
-    total = first
-    for i, ref in enumerate(refs):
-        at = low if i == 0 else 0
-        total = total + ref[at : at + rows, :].astype(jnp.float32)
-    return total
+def share_kernel(half, fanout_two, near_ref, far_ref, part_ref, hidden_ref, ws_ref, wn_ref, *refs):
+    values = values_of(hidden_ref[...], ws_ref, wn_ref, fanout_two)
+    lanes = values.shape[0]
+    for i, ref in enumerate((far_ref, near_ref)):
+        part = part_ref[i] + jnp.dot(ref[:, lanes:], values, preferred_element_type=jnp.float32)
+        rows = part.shape[0] // half
+        for s, out_ref in enumerate(refs[i * half : (i + 1) * half]):
+            out_ref[...] = part[s * rows : (s + 1) * rows].astype(jnp.bfloat16)
 
 
 def side_sum_kernel(*refs):
-    rows = refs[-1].shape[0]
-    refs[-1][...] = sum_rows(0.0, 0, refs[:-1], rows).astype(jnp.bfloat16)
+    total = refs[0][...].astype(jnp.float32)
+    for ref in refs[1:-1]:
+        total = total + ref[...].astype(jnp.float32)
+    refs[-1][...] = total.astype(jnp.bfloat16)
 
 
 def last_kernel(bias_ref, *refs):
-    rows = refs[-1].shape[0]
-    total = sum_rows(bias_ref[...], rows, refs[:-1], rows)
+    total = bias_ref[...]
+    for ref in refs[:-1]:
+        total = total + ref[...].astype(jnp.float32)
     refs[-1][...] = jnp.maximum(total, 0.0).astype(jnp.bfloat16)
 
 
@@ -442,7 +427,7 @@
     def pinned(value):
         return pltpu.with_memory_space_constraint(value, pltpu.HBM)
 
-    def send(chunks, steps=steps):
+    def send(chunks):
         return [swap(chunk, "feat", s) if s else chunk for s, chunk in zip(steps, chunks)]
 
     picks = jnp.transpose(nbr_one, (0, 2, 1, 3))
@@ -537,14 +522,21 @@
     (cross,) = call(
         functools.partial(far_kernel, half),
         "far",
-        [((pcap + idx_rows, width), bf16)],
-        [vmem] * (half + 3),
-        (*far_arrived, far_own, far_pre, w_nbr, idx_tags),
+        [((pcap, width), bf16)],
+        [vmem] * (half + 2),
+        (*far_arrived, far_own, far_pre, w_nbr),
     )
     cross_arrived = swap(cross, "feat", half)
-    turned = [*steps[1:-1], steps[0]]
-    near_means = means(turned, [*far_arrived[1:], far_arrived[0]], (cross,))
-    near_arrived = send(near_means, turned)
+    *near_means, idx_tags = means(
+        [s for s in steps if s],
+        far_arrived,
+        (cross,),
+        before=copy_kernel,
+        ins=(idx_tags,),
+        outs=[((idx_rows, width), bf16)],
+    )
+    near_arrived = send(near_means)
+    idx_arrived = swap(idx_tags, "feat", half)
     near_own, near_times = means(
         [0],
         [live],
@@ -553,12 +545,22 @@
         ins=(w2_self, w2_nbr, *arrived),
         outs=[((half * seed_count, 4 * pcap), bf16)],
     )
+    (far_times,) = call(
+        functools.partial(far_times_kernel, half, pcap, n_idx),
+        "far_times",
+        [((half * seed_count, 4 * pcap), bf16)],
+        [vmem],
+        (idx_arrived,),
+        after=(near_own,),
+        cost_us=0,
+    )
     (near_pre,) = call(
         functools.partial(near_kernel, half),
         "near",
         [((pcap, width), jnp.float32)],
         [vmem] * (half + 2),
         (*near_arrived, near_own, pre, w_nbr),
+        after=(far_times,),
         cost_us=0,
     )
     (hidden,) = call(
@@ -569,45 +571,34 @@
         (live, near_pre, cross_arrived),
     )
     other_hidden = swap(hidden, "rep", 1)
-    far_times, value, result = call(
-        functools.partial(far_times_kernel, half, n_idx, fanout_two),
-        "far_times",
-        [
-            ((half * seed_count, 4 * pcap), bf16),
-            ((2, pcap, width), bf16),
-            ((pcap, width), bf16),
-        ],
-        [vmem] * 4,
-        (cross_arrived, hidden, w2_self, w2_nbr),
+    own_part, result = call(
+        functools.partial(own_share_kernel, fanout_two),
+        "own_share",
+        [((2, half * seed_count, width), jnp.float32), ((pcap, width), bf16)],
+        [vmem] * 5,
+        (near_times, far_times, hidden, w2_self, w2_nbr),
         scratch=[pltpu.SemaphoreType.DMA],
-        outs=(vmem, vmem, anywhere),
+        outs=(vmem, anywhere),
     )
     shares = call(
         functools.partial(share_kernel, half, fanout_two),
         "share",
-        [((2 * seed_count, width), bf16)] + [((seed_count, width), bf16)] * (2 * half - 2),
+        [((seed_count, width), bf16)] * (2 * half),
         [vmem] * 6,
-        (near_times, far_times, value, other_hidden, w2_self, w2_nbr),
-        scratch=[pltpu.VMEM((2, pcap, width), bf16)],
+        (near_times, far_times, own_part, other_hidden, w2_self, w2_nbr),
         limit=32 * MIB,
     )
-    both = swap(shares[0], "feat", 1)
-    others = [*steps[: half - 2], 0]
-    far_shares = send(shares[1:half], others)
-    near_shares = send(shares[half:], others)
+    far_shares = send(shares[:half])
+    near_shares = send(shares[half:])
     (far_sum,) = call(
-        side_sum_kernel,
-        "side_sum",
-        [((seed_count, width), bf16)],
-        [vmem] * half,
-        (both, *far_shares),
+        side_sum_kernel, "side_sum", [((seed_count, width), bf16)], [vmem] * half, far_shares
     )
     (seed_out,) = call(
         last_kernel,
         "seeds",
         [((seed_count, width), bf16)],
         [vmem] * (half + 2),
-        (bias_two[None], both, *near_shares, swap(far_sum, "feat", half)),
+        (bias_two[None], *near_shares, swap(far_sum, "feat", half)),
     )
     return (result[None, None], seed_out)
 

time: 53.4 us -> 54.5 us (1.021)
  starting transfers between devices: 23 us -> 26.1 us
  waiting for transfers between devices: 7.81 us -> 5.78 us
    ppermute x18 -> x20, starting transfers between devices: 23 us -> 26.1 us  [swap(): return lax.ppermute(value, axis, [(i, i ^ step) for i in range(size)])]
    ppermute x18 -> x20, waiting for transfers between devices: 7.81 us -> 5.78 us  [swap(): return lax.ppermute(value, axis, [(i, i ^ step) for i in range(size)])]
    pallas_call x14 -> x15, Pallas kernels: 20.5 us -> 20.7 us  [call(): pl.pallas_call(wrapped, out_shape=tuple((jax.ShapeDtypeStruct(shape, dtyp...]
  transfers between devices with their start and end apart: 18 -> 20, of which waited for: 9 -> 7; matrix products, arithmetic and copies ran while one was open for 0% -> 0% of each run, Pallas kernels for 32% -> 31%
where the time goes in v14:
time: 54.5 us; the launch traced here: 54 us
  starting transfers between devices  26.1 us (48%)
  Pallas kernels  20.7 us (38%)
  waiting for transfers between devices  5.78 us (11%)
  between operations  1.48 us (3%)
    ppermute x20, starting transfers between devices, swap(): return lax.ppermute(value, axis, [(i, i ^ step) for i in range(size)])  26.1 us
    pallas_call x15, Pallas kernels, call(): pl.pallas_call(wrapped, out_shape=tuple((jax.ShapeDtypeStruct(shape, dtyp...  20.7 us
    ppermute x20, waiting for transfers between devices, swap(): return lax.ppermute(value, axis, [(i, i ^ step) for i in range(size)])  5.78 us
  transfers between devices with their start and end apart: 20, of which 7 were waited for; matrix products, arithmetic and copies ran while one was open for 0% of the time, Pallas kernels for 31%

profile of v14, /device:TPU:0, one launch (start us, length us, event | category | flops | bytes accessed | tf_op | source)
XLA Modules:
  0.0 54.0 jit_solution(1233377139596206161)
XLA Ops:
  0.6 1.8 %pack.1 = (bf16[176,512]{1,0:T(8,128)(2,1)S(1)}, bf16[176,512]{1,0:T(8,128)(2,1)S(1)}, bf16[176,512]{1,0:T(8,128)(2,1)S(1)}, bf16[176,512]{1,0:T(8,128)(2,1)S(1)...) custom-call(bf16[96,12288]{1,0:T(8,128)(2,1)} %refs_0_.3, s32[1,64]{1,0:T(1,128)} %bitcast.15, ...), custom_call_target="tpu_custom_call" | custom-call | flops 1100000000 | tf_op jit(solution)/shard_map/pack/pallas_call | solution.py:414
  2.5 4.0 %collective-permute-start = (bf16[176,512]{1,0:T(8,128)(2,1)S(1)}, bf16[176,512]{1,0:T(8,128)(2,1)S(1)}, u32[]{:S(2)}, u32[]{:S(2)}) collective-permute-start(bf16[176,512]{1,0:T(8,128)(2,1)S(1)} %get-tuple-element.37), channel_id=1, source_target_pairs={{0,6},{2,4},{4,2},{6,0},{8,14},{10,12},{12,10},{14,8},{1,7},{3,5},... | collective-permute-start | bytes 540680 | tf_op jit(solution)/shard_map/ppermute | solution.py:379
  6.5 0.4 collective-permute-start.1
  7.0 0.2 collective-permute-start.2
  7.2 1.2 %turn.1 = f32[12288,128]{1,0:T(8,128)S(1)} custom-call(bf16[96,12288]{1,0:T(8,128)(2,1)S(1)} %get-tuple-element.42.refs_0_), custom_call_target="tpu_custom_call" | custom-call | flops 3300000000 | tf_op jit(solution)/shard_map/turn/pallas_call | solution.py:414
  8.4 6.0 %mean.4 = (bf16[144,128]{1,0:T(8,128)(2,1)S(1)}, bf16[144,128]{1,0:T(8,128)(2,1)S(1)}, bf16[144,128]{1,0:T(8,128)(2,1)S(1)}) custom-call(s32[8,1,1280]{2,1,0:T(1,128)S(1)} %get-tuple-element.41.refs_0_.refs_6_.refs_1_, f32[12288,1,128]{2,1,0:T(1,128)S(1)} %bitcast.7), custom_call_target="tpu_custom_call" | custom-call | flops 6600000000 | tf_op jit(solution)/shard_map/mean/pallas_call | solution.py:414
  14.4 0.0 copy-start.2
  15.0 0.0 collective-permute-done.refs_1_.refs_0_.refs_2_
  15.1 0.1 collective-permute-done.1.refs_2_.refs_1_.refs_3_
  15.2 0.0 collective-permute-done.2.refs_3_.refs_2_.refs_4_
  15.2 0.1 collective-permute-start.6
  15.3 2.8 %collective-permute-start.3 = (bf16[160,128]{1,0:T(8,128)(2,1)S(1)}, bf16[160,128]{1,0:T(8,128)(2,1)S(1)}, u32[]{:S(2)}, u32[]{:S(2)}) collective-permute-start(bf16[160,128]{1,0:T(8,128)(2,1)S(1)} %get-tuple-element.47), channel_id=1, source_target_pairs={{0,6},{2,4},{4,2},{6,0},{8,14},{10,12},{12,10},{14,8},{1,7},{3,5},... | collective-permute-start | bytes 122888 | tf_op jit(solution)/shard_map/ppermute | solution.py:379
  18.1 0.4 collective-permute-start.4
  18.6 0.3 collective-permute-start.5
  18.8 0.0 collective-permute-done.6.refs_4_
  18.8 0.0 copy-done.2
  18.8 2.7 %mean.5 = (bf16[144,128]{1,0:T(8,128)(2,1)S(1)}, bf16[4,96,512]{2,1,0:T(8,128)(2,1)S(1)}, f32[192,512]{1,0:T(8,128)S(1)}, f32[192,512]{1,0:T(8,128)S(1)}, bf16[16,512]{1,0:T(8,128)(2,1)S(1)}) custom-call(bf16[176,512]{1,0:T(8,128)(2,1)S(1)} %collective-permute-done.refs_1_.refs_0_.refs_2_, ...), custom_call_target="tpu_custom_call" | custom-call | tf_op jit(solution)/shard_map/mean/pallas_call | solution.py:414
  21.5 0.0 collective-permute-done.3.refs_0_.refs_3_
  21.5 0.6 %collective-permute-done.4.refs_1_.refs_4_ = bf16[160,128]{1,0:T(8,128)(2,1)S(1)} collective-permute-done((bf16[160,128]{1,0:T(8,128)(2,1)S(1)}, bf16[160,128]{1,0:T(8,128)(2,1)S(1)}, u32[]{:S(2)}, u32[]{:S(2)}) %collective-permute-start.4) | collective-permute-done | bytes 40992 | tf_op jit(solution)/shard_map/ppermute | solution.py:379
  22.1 0.4 collective-permute-done.5.refs_2_.refs_5_
  22.6 0.4 far.1.refs_9_.refs_6_
  22.9 2.7 %collective-permute-start.11 = (bf16[192,512]{1,0:T(8,128)(2,1)S(1)}, bf16[192,512]{1,0:T(8,128)(2,1)S(1)}, u32[]{:S(2)}, u32[]{:S(2)}) collective-permute-start(bf16[192,512]{1,0:T(8,128)(2,1)S(1)} %far.1.refs_9_.refs_6_), channel_id=1, source_target_pairs={{0,8},{2,10},{4,12},{6,14},{8,0},{10,2},{12,4},{14,6},{1,9},{3,11}... | collective-permute-start | bytes 589832 | tf_op jit(solution)/shard_map/ppermute | solution.py:379
  25.6 0.0 copy-start
  25.6 0.0 copy-start.1
  25.6 3.3 %mean.7 = (bf16[144,128]{1,0:T(8,128)(2,1)S(1)}, bf16[144,128]{1,0:T(8,128)(2,1)S(1)}, bf16[144,128]{1,0:T(8,128)(2,1)S(1)}, bf16[16,512]{1,0:T(8,128)(2,1)S(1)}) custom-call(bf16[16,512]{1,0:T(8,128)(2,1)S(1)} %get-tuple-element.55.refs_0_, s32[8,1,1280]{2,1,0:T(1,128)S(1)} %get-tuple-element.41.refs_0_.refs_6_.refs_1_, f32[12288,1,128]{2,1,0:T(1,128)S(1)} %bitcast.9, ...), custom_call_target="tpu_custom_call" | custom-call | flops 6600000000 | tf_op jit(solution)/shard_map/mean/pallas_call | solution.py:414
  28.9 1.4 %collective-permute-start.8 = (bf16[144,128]{1,0:T(8,128)(2,1)S(1)}, bf16[144,128]{1,0:T(8,128)(2,1)S(1)}, u32[]{:S(2)}, u32[]{:S(2)}) collective-permute-start(bf16[144,128]{1,0:T(8,128)(2,1)S(1)} %get-tuple-element.58), channel_id=1, source_target_pairs={{0,6},{2,4},{4,2},{6,0},{8,14},{10,12},{12,10},{14,8},{1,7},{3,5},... | collective-permute-start | bytes 110600 | tf_op jit(solution)/shard_map/ppermute | solution.py:379
  30.3 1.1 %collective-permute-start.9 = (bf16[144,128]{1,0:T(8,128)(2,1)S(1)}, bf16[144,128]{1,0:T(8,128)(2,1)S(1)}, u32[]{:S(2)}, u32[]{:S(2)}) collective-permute-start(bf16[144,128]{1,0:T(8,128)(2,1)S(1)} %get-tuple-element.59), channel_id=1, source_target_pairs={{0,4},{2,6},{4,0},{6,2},{8,12},{10,14},{12,8},{14,10},{1,5},{3,7},... | collective-permute-start | bytes 110600 | tf_op jit(solution)/shard_map/ppermute | solution.py:379
  31.4 1.0 %collective-permute-start.10 = (bf16[144,128]{1,0:T(8,128)(2,1)S(1)}, bf16[144,128]{1,0:T(8,128)(2,1)S(1)}, u32[]{:S(2)}, u32[]{:S(2)}) collective-permute-start(bf16[144,128]{1,0:T(8,128)(2,1)S(1)} %get-tuple-element.60), channel_id=1, source_target_pairs={{0,2},{2,0},{4,6},{6,4},{8,10},{10,8},{12,14},{14,12},{1,3},{3,1},... | collective-permute-start | bytes 110600 | tf_op jit(solution)/shard_map/ppermute | solution.py:379
  32.4 2.2 %collective-permute-start.7 = (bf16[16,512]{1,0:T(8,128)(2,1)S(1)}, bf16[16,512]{1,0:T(8,128)(2,1)S(1)}, u32[]{:S(2)}, u32[]{:S(2)}) collective-permute-start(bf16[16,512]{1,0:T(8,128)(2,1)S(1)} %get-tuple-element.56), channel_id=1, source_target_pairs={{0,8},{2,10},{4,12},{6,14},{8,0},{10,2},{12,4},{14,6},{1,9},{3,11}... | collective-permute-start | bytes 49160 | tf_op jit(solution)/shard_map/ppermute | solution.py:379
  34.6 0.0 copy-done
  34.6 0.0 copy-done.1
  34.6 1.7 %mean.6 = (bf16[144,128]{1,0:T(8,128)(2,1)S(1)}, bf16[256,768]{1,0:T(8,128)(2,1)S(1)}) custom-call(bf16[512,512]{1,0:T(8,128)(2,1)S(1)} %copy-done, bf16[512,512]{1,0:T(8,128)(2,1)S(1)} %copy-done.1, bf16[176,512]{1,0:T(8,128)(2,1)S(1)} %collective-permute-done.refs_1_.refs_0_.refs_2_, bf16[176,512]{1,0:T(8,128)(2,1)S(1)} %collective-permute-done.1.refs_2_.refs_1_.refs_3_, ...), custom_call_target="tpu_custom_call" | custom-call | tf_op jit(solution)/shard_map/mean/pallas_call | solution.py:414
  36.4 0.7 %collective-permute-done.7.refs_0_ = bf16[16,512]{1,0:T(8,128)(2,1)S(1)} collective-permute-done((bf16[16,512]{1,0:T(8,128)(2,1)S(1)}, bf16[16,512]{1,0:T(8,128)(2,1)S(1)}, u32[]{:S(2)}, u32[]{:S(2)}) %collective-permute-start.7) | collective-permute-done | bytes 16416 | tf_op jit(solution)/shard_map/ppermute | solution.py:379
  37.1 0.8 %far_times.1.refs_6_.refs_1_ = bf16[256,768]{1,0:T(8,128)(2,1)S(1)} custom-call(bf16[16,512]{1,0:T(8,128)(2,1)S(1)} %collective-permute-done.7.refs_0_, bf16[144,128]{1,0:T(8,128)(2,1)S(1)} %get-tuple-element.57.refs_1_.refs_3_), custom_call_target="tpu_custom_call" | custom-call | tf_op jit(solution)/shard_map/far_times/pallas_call | solution.py:414
  37.8 0.0 collective-permute-done.8.refs_0_
  37.8 0.0 collective-permute-done.9.refs_1_
  37.9 0.0 collective-permute-done.10.refs_2_
  37.9 0.4 near.1.refs_1_
  38.2 0.0 collective-permute-done.11.refs_2_
  38.3 0.2 hidden.1.refs_2_
  38.4 0.1 collective-permute-start.12
  38.5 0.8 %own_share.1 = (f32[2,256,512]{2,1,0:T(8,128)S(1)}, bf16[192,512]{1,0:T(8,128)(2,1)}) custom-call(bf16[256,768]{1,0:T(8,128)(2,1)S(1)} %get-tuple-element.54.refs_0_, bf16[256,768]{1,0:T(8,128)(2,1)S(1)} %far_times.1.refs_6_.refs_1_, bf16[192,512]{1,0:T(8,128)(2,1)S(1)} %hidden.1.refs_2_, bf16[512,512]{1,0:T(8,128)(2,1)S(1)} %copy-done, ...), custom_call_target="tpu_custom_call" | custom-call | flops 1100000000 | tf_op jit(solution)/shard_map/own_share/pallas_call | solution.py:414
  39.3 0.7 %collective-permute-done.12.refs_3_ = bf16[192,512]{1,0:T(8,128)(2,1)S(1)} collective-permute-done((bf16[192,512]{1,0:T(8,128)(2,1)S(1)}, bf16[192,512]{1,0:T(8,128)(2,1)S(1)}, u32[]{:S(2)}, u32[]{:S(2)}) %collective-permute-start.12) | collective-permute-done | bytes 196640 | tf_op jit(solution)/shard_map/ppermute | solution.py:379
  39.9 0.8 %share.1 = (bf16[64,512]{1,0:T(8,128)(2,1)S(1)}, bf16[64,512]{1,0:T(8,128)(2,1)S(1)}, bf16[64,512]{1,0:T(8,128)(2,1)S(1)}, bf16[64,512]{1,0:T(8,128)(2,1)S(1)}, ...) custom-call(bf16[256,768]{1,0:T(8,128)(2,1)S(1)} %get-tuple-element., ...), custom_call_target="tpu_custom_call" | custom-call | flops 1100000000 | tf_op jit(solution)/shard_map/share/pallas_call | solution.py:414
  40.7 0.0 copy-start.3
  40.7 1.5 %collective-permute-start.16 = (bf16[64,512]{1,0:T(8,128)(2,1)S(1)}, bf16[64,512]{1,0:T(8,128)(2,1)S(1)}, u32[]{:S(2)}, u32[]{:S(2)}) collective-permute-start(bf16[64,512]{1,0:T(8,128)(2,1)S(1)} %get-tuple-element.68), channel_id=1, source_target_pairs={{0,6},{2,4},{4,2},{6,0},{8,14},{10,12},{12,10},{14,8},{1,7},{3,5},... | collective-permute-start | bytes 196616 | tf_op jit(solution)/shard_map/ppermute | solution.py:379
  42.2 1.1 %collective-permute-start.17 = (bf16[64,512]{1,0:T(8,128)(2,1)S(1)}, bf16[64,512]{1,0:T(8,128)(2,1)S(1)}, u32[]{:S(2)}, u32[]{:S(2)}) collective-permute-start(bf16[64,512]{1,0:T(8,128)(2,1)S(1)} %get-tuple-element.69), channel_id=1, source_target_pairs={{0,4},{2,6},{4,0},{6,2},{8,12},{10,14},{12,8},{14,10},{1,5},{3,7},... | collective-permute-start | bytes 196616 | tf_op jit(solution)/shard_map/ppermute | solution.py:379
  43.3 1.0 %collective-permute-start.18 = (bf16[64,512]{1,0:T(8,128)(2,1)S(1)}, bf16[64,512]{1,0:T(8,128)(2,1)S(1)}, u32[]{:S(2)}, u32[]{:S(2)}) collective-permute-start(bf16[64,512]{1,0:T(8,128)(2,1)S(1)} %get-tuple-element.70), channel_id=1, source_target_pairs={{0,2},{2,0},{4,6},{6,4},{8,10},{10,8},{12,14},{14,12},{1,3},{3,1},... | collective-permute-start | bytes 196616 | tf_op jit(solution)/shard_map/ppermute | solution.py:379
  44.3 1.4 %collective-permute-start.13 = (bf16[64,512]{1,0:T(8,128)(2,1)S(1)}, bf16[64,512]{1,0:T(8,128)(2,1)S(1)}, u32[]{:S(2)}, u32[]{:S(2)}) collective-permute-start(bf16[64,512]{1,0:T(8,128)(2,1)S(1)} %get-tuple-element.64), channel_id=1, source_target_pairs={{0,6},{2,4},{4,2},{6,0},{8,14},{10,12},{12,10},{14,8},{1,7},{3,5},... | collective-permute-start | bytes 196616 | tf_op jit(solution)/shard_map/ppermute | solution.py:379
  45.7 1.1 %collective-permute-start.14 = (bf16[64,512]{1,0:T(8,128)(2,1)S(1)}, bf16[64,512]{1,0:T(8,128)(2,1)S(1)}, u32[]{:S(2)}, u32[]{:S(2)}) collective-permute-start(bf16[64,512]{1,0:T(8,128)(2,1)S(1)} %get-tuple-element.65), channel_id=1, source_target_pairs={{0,4},{2,6},{4,0},{6,2},{8,12},{10,14},{12,8},{14,10},{1,5},{3,7},... | collective-permute-start | bytes 196616 | tf_op jit(solution)/shard_map/ppermute | solution.py:379
  46.8 0.0 collective-permute-done.16.refs_0_
  46.8 1.0 %collective-permute-start.15 = (bf16[64,512]{1,0:T(8,128)(2,1)S(1)}, bf16[64,512]{1,0:T(8,128)(2,1)S(1)}, u32[]{:S(2)}, u32[]{:S(2)}) collective-permute-start(bf16[64,512]{1,0:T(8,128)(2,1)S(1)} %get-tuple-element.66), channel_id=1, source_target_pairs={{0,2},{2,0},{4,6},{6,4},{8,10},{10,8},{12,14},{14,12},{1,3},{3,1},... | collective-permute-start | bytes 196616 | tf_op jit(solution)/shard_map/ppermute | solution.py:379
  47.8 0.0 collective-permute-done.17.refs_1_
  47.8 0.0 collective-permute-done.18.refs_2_
  47.8 2.2 %collective-permute-start.19 = (bf16[64,512]{1,0:T(8,128)(2,1)S(1)}, bf16[64,512]{1,0:T(8,128)(2,1)S(1)}, u32[]{:S(2)}, u32[]{:S(2)}) collective-permute-start(bf16[64,512]{1,0:T(8,128)(2,1)S(1)} %side_sum.1), channel_id=1, source_target_pairs={{0,8},{2,10},{4,12},{6,14},{8,0},{10,2},{12,4},{14,6},{1,9},{3,11}... | collective-permute-start | bytes 196616 | tf_op jit(solution)/shard_map/ppermute | solution.py:379
  50.1 0.0 collective-permute-done.13.refs_1_
  50.1 0.0 collective-permute-done.14.refs_2_
  50.1 0.9 %collective-permute-done.15.refs_3_ = bf16[64,512]{1,0:T(8,128)(2,1)S(1)} collective-permute-done((bf16[64,512]{1,0:T(8,128)(2,1)S(1)}, bf16[64,512]{1,0:T(8,128)(2,1)S(1)}, u32[]{:S(2)}, u32[]{:S(2)}) %collective-permute-start.15) | collective-permute-done | bytes 65568 | tf_op jit(solution)/shard_map/ppermute | solution.py:379
  51.0 2.3 %collective-permute-done.19.refs_5_ = bf16[64,512]{1,0:T(8,128)(2,1)S(1)} collective-permute-done((bf16[64,512]{1,0:T(8,128)(2,1)S(1)}, bf16[64,512]{1,0:T(8,128)(2,1)S(1)}, u32[]{:S(2)}, u32[]{:S(2)}) %collective-permute-start.19) | collective-permute-done | bytes 65568 | tf_op jit(solution)/shard_map/ppermute | solution.py:379
  53.3 0.0 copy-done.3
  53.3 0.7 %seeds.1 = bf16[64,512]{1,0:T(8,128)(2,1)} custom-call(f32[1,512]{1,0:T(1,128)S(1)} %bitcast.12, bf16[64,512]{1,0:T(8,128)(2,1)S(1)} %collective-permute-done.13.refs_1_, bf16[64,512]{1,0:T(8,128)(2,1)S(1)} %collective-permute-done.14.refs_2_, bf16[64,512]{1,0:T(8,128)(2,1)S(1)} %collective-permute-done.15.refs_3_, ...), custom_call_target="tpu_custom_call" | custom-call | flops 1100000000 | tf_op jit(solution)/shard_map/seeds/pallas_call | solution.py:414
  (2 shorter events, 0.1 us)
Async XLA Ops:
  2.5 12.6 %collective-permute-start = (bf16[176,512]{1,0:T(8,128)(2,1)S(1)}, bf16[176,512]{1,0:T(8,128)(2,1)S(1)}, u32[]{:S(2)}, u32[]{:S(2)}) collective-permute-start(bf16[176,512]{1,0:T(8,128)(2,1)S(1)} %get-tuple-element.37), channel_id=1, source_target_pairs={{0,6},{2,4},{4,2},{6,0},{8,14},{10,12},{12,10},{14,8},{1,7},{3,5},... | collective-permute-start | bytes 540680 | tf_op jit(solution)/shard_map/ppermute | solution.py:379
  6.5 8.6 %collective-permute-start.1 = (bf16[176,512]{1,0:T(8,128)(2,1)S(1)}, bf16[176,512]{1,0:T(8,128)(2,1)S(1)}, u32[]{:S(2)}, u32[]{:S(2)}) collective-permute-start(bf16[176,512]{1,0:T(8,128)(2,1)S(1)} %get-tuple-element.38), channel_id=1, source_target_pairs={{0,4},{2,6},{4,0},{6,2},{8,12},{10,14},{12,8},{14,10},{1,5},{3,7},... | collective-permute-start | bytes 540680 | tf_op jit(solution)/shard_map/ppermute | solution.py:379
  7.0 8.2 %collective-permute-start.2 = (bf16[176,512]{1,0:T(8,128)(2,1)S(1)}, bf16[176,512]{1,0:T(8,128)(2,1)S(1)}, u32[]{:S(2)}, u32[]{:S(2)}) collective-permute-start(bf16[176,512]{1,0:T(8,128)(2,1)S(1)} %get-tuple-element.39), channel_id=1, source_target_pairs={{0,2},{2,0},{4,6},{6,4},{8,10},{10,8},{12,14},{14,12},{1,3},{3,1},... | collective-permute-start | bytes 540680 | tf_op jit(solution)/shard_map/ppermute | solution.py:379
  14.4 4.5 %copy-start.2 = (f32[512]{0:T(512)S(1)}, f32[512]{0:T(512)}, u32[]{:S(2)}) copy-start(f32[512]{0:T(512)} %param.18) | copy-start | bytes 6148
  15.2 3.6 %collective-permute-start.6 = (bf16[4,96,512]{2,1,0:T(8,128)(2,1)S(1)}, bf16[4,96,512]{2,1,0:T(8,128)(2,1)S(1)}, u32[]{:S(2)}, u32[]{:S(2)}) collective-permute-start(bf16[4,96,512]{2,1,0:T(8,128)(2,1)S(1)} %get-tuple-element.50), channel_id=1, source_target_pairs={{0,1},{1,0},{2,3},{3,2},{4,5},{5,4},{6,7},{7,6},{8,9},{9,8},{10,11... | collective-permute-start | bytes 1179656 | tf_op jit(solution)/shard_map/ppermute | solution.py:379
  15.3 6.3 %collective-permute-start.3 = (bf16[160,128]{1,0:T(8,128)(2,1)S(1)}, bf16[160,128]{1,0:T(8,128)(2,1)S(1)}, u32[]{:S(2)}, u32[]{:S(2)}) collective-permute-start(bf16[160,128]{1,0:T(8,128)(2,1)S(1)} %get-tuple-element.47), channel_id=1, source_target_pairs={{0,6},{2,4},{4,2},{6,0},{8,14},{10,12},{12,10},{14,8},{1,7},{3,5},... | collective-permute-start | bytes 122888 | tf_op jit(solution)/shard_map/ppermute | solution.py:379
  18.1 4.0 %collective-permute-start.4 = (bf16[160,128]{1,0:T(8,128)(2,1)S(1)}, bf16[160,128]{1,0:T(8,128)(2,1)S(1)}, u32[]{:S(2)}, u32[]{:S(2)}) collective-permute-start(bf16[160,128]{1,0:T(8,128)(2,1)S(1)} %get-tuple-element.48), channel_id=1, source_target_pairs={{0,4},{2,6},{4,0},{6,2},{8,12},{10,14},{12,8},{14,10},{1,5},{3,7},... | collective-permute-start | bytes 122888 | tf_op jit(solution)/shard_map/ppermute | solution.py:379
  18.6 4.0 %collective-permute-start.5 = (bf16[160,128]{1,0:T(8,128)(2,1)S(1)}, bf16[160,128]{1,0:T(8,128)(2,1)S(1)}, u32[]{:S(2)}, u32[]{:S(2)}) collective-permute-start(bf16[160,128]{1,0:T(8,128)(2,1)S(1)} %get-tuple-element.49), channel_id=1, source_target_pairs={{0,2},{2,0},{4,6},{6,4},{8,10},{10,8},{12,14},{14,12},{1,3},{3,1},... | collective-permute-start | bytes 122888 | tf_op jit(solution)/shard_map/ppermute | solution.py:379
  22.9 15.3 %collective-permute-start.11 = (bf16[192,512]{1,0:T(8,128)(2,1)S(1)}, bf16[192,512]{1,0:T(8,128)(2,1)S(1)}, u32[]{:S(2)}, u32[]{:S(2)}) collective-permute-start(bf16[192,512]{1,0:T(8,128)(2,1)S(1)} %far.1.refs_9_.refs_6_), channel_id=1, source_target_pairs={{0,8},{2,10},{4,12},{6,14},{8,0},{10,2},{12,4},{14,6},{1,9},{3,11}... | collective-permute-start | bytes 589832 | tf_op jit(solution)/shard_map/ppermute | solution.py:379
  25.6 9.0 %copy-start = (bf16[512,512]{1,0:T(8,128)(2,1)S(1)}, bf16[512,512]{1,0:T(8,128)(2,1)}, u32[]{:S(2)}) copy-start(bf16[512,512]{1,0:T(8,128)(2,1)} %refs_4_.5) | copy-start | bytes 1572868
  25.6 9.0 %copy-start.1 = (bf16[512,512]{1,0:T(8,128)(2,1)S(1)}, bf16[512,512]{1,0:T(8,128)(2,1)}, u32[]{:S(2)}) copy-start(bf16[512,512]{1,0:T(8,128)(2,1)} %refs_5_.1) | copy-start | bytes 1572868
  28.9 9.0 %collective-permute-start.8 = (bf16[144,128]{1,0:T(8,128)(2,1)S(1)}, bf16[144,128]{1,0:T(8,128)(2,1)S(1)}, u32[]{:S(2)}, u32[]{:S(2)}) collective-permute-start(bf16[144,128]{1,0:T(8,128)(2,1)S(1)} %get-tuple-element.58), channel_id=1, source_target_pairs={{0,6},{2,4},{4,2},{6,0},{8,14},{10,12},{12,10},{14,8},{1,7},{3,5},... | collective-permute-start | bytes 110600 | tf_op jit(solution)/shard_map/ppermute | solution.py:379
  30.3 7.5 %collective-permute-start.9 = (bf16[144,128]{1,0:T(8,128)(2,1)S(1)}, bf16[144,128]{1,0:T(8,128)(2,1)S(1)}, u32[]{:S(2)}, u32[]{:S(2)}) collective-permute-start(bf16[144,128]{1,0:T(8,128)(2,1)S(1)} %get-tuple-element.59), channel_id=1, source_target_pairs={{0,4},{2,6},{4,0},{6,2},{8,12},{10,14},{12,8},{14,10},{1,5},{3,7},... | collective-permute-start | bytes 110600 | tf_op jit(solution)/shard_map/ppermute | solution.py:379
  31.4 6.4 %collective-permute-start.10 = (bf16[144,128]{1,0:T(8,128)(2,1)S(1)}, bf16[144,128]{1,0:T(8,128)(2,1)S(1)}, u32[]{:S(2)}, u32[]{:S(2)}) collective-permute-start(bf16[144,128]{1,0:T(8,128)(2,1)S(1)} %get-tuple-element.60), channel_id=1, source_target_pairs={{0,2},{2,0},{4,6},{6,4},{8,10},{10,8},{12,14},{14,12},{1,3},{3,1},... | collective-permute-start | bytes 110600 | tf_op jit(solution)/shard_map/ppermute | solution.py:379
  32.4 4.6 %collective-permute-start.7 = (bf16[16,512]{1,0:T(8,128)(2,1)S(1)}, bf16[16,512]{1,0:T(8,128)(2,1)S(1)}, u32[]{:S(2)}, u32[]{:S(2)}) collective-permute-start(bf16[16,512]{1,0:T(8,128)(2,1)S(1)} %get-tuple-element.56), channel_id=1, source_target_pairs={{0,8},{2,10},{4,12},{6,14},{8,0},{10,2},{12,4},{14,6},{1,9},{3,11}... | collective-permute-start | bytes 49160 | tf_op jit(solution)/shard_map/ppermute | solution.py:379
  38.4 1.5 %collective-permute-start.12 = (bf16[192,512]{1,0:T(8,128)(2,1)S(1)}, bf16[192,512]{1,0:T(8,128)(2,1)S(1)}, u32[]{:S(2)}, u32[]{:S(2)}) collective-permute-start(bf16[192,512]{1,0:T(8,128)(2,1)S(1)} %hidden.1.refs_2_), channel_id=1, source_target_pairs={{0,1},{1,0},{2,3},{3,2},{4,5},{5,4},{6,7},{7,6},{8,9},{9,8},{10,11... | collective-permute-start | bytes 589832 | tf_op jit(solution)/shard_map/ppermute | solution.py:379
  40.7 12.6 %copy-start.3 = (f32[512]{0:T(512)S(1)}, f32[512]{0:T(512)}, u32[]{:S(2)}) copy-start(f32[512]{0:T(512)} %param.21) | copy-start | bytes 6148
  40.7 6.1 %collective-permute-start.16 = (bf16[64,512]{1,0:T(8,128)(2,1)S(1)}, bf16[64,512]{1,0:T(8,128)(2,1)S(1)}, u32[]{:S(2)}, u32[]{:S(2)}) collective-permute-start(bf16[64,512]{1,0:T(8,128)(2,1)S(1)} %get-tuple-element.68), channel_id=1, source_target_pairs={{0,6},{2,4},{4,2},{6,0},{8,14},{10,12},{12,10},{14,8},{1,7},{3,5},... | collective-permute-start | bytes 196616 | tf_op jit(solution)/shard_map/ppermute | solution.py:379
  42.2 5.6 %collective-permute-start.17 = (bf16[64,512]{1,0:T(8,128)(2,1)S(1)}, bf16[64,512]{1,0:T(8,128)(2,1)S(1)}, u32[]{:S(2)}, u32[]{:S(2)}) collective-permute-start(bf16[64,512]{1,0:T(8,128)(2,1)S(1)} %get-tuple-element.69), channel_id=1, source_target_pairs={{0,4},{2,6},{4,0},{6,2},{8,12},{10,14},{12,8},{14,10},{1,5},{3,7},... | collective-permute-start | bytes 196616 | tf_op jit(solution)/shard_map/ppermute | solution.py:379
  43.3 4.5 %collective-permute-start.18 = (bf16[64,512]{1,0:T(8,128)(2,1)S(1)}, bf16[64,512]{1,0:T(8,128)(2,1)S(1)}, u32[]{:S(2)}, u32[]{:S(2)}) collective-permute-start(bf16[64,512]{1,0:T(8,128)(2,1)S(1)} %get-tuple-element.70), channel_id=1, source_target_pairs={{0,2},{2,0},{4,6},{6,4},{8,10},{10,8},{12,14},{14,12},{1,3},{3,1},... | collective-permute-start | bytes 196616 | tf_op jit(solution)/shard_map/ppermute | solution.py:379
  44.3 5.8 %collective-permute-start.13 = (bf16[64,512]{1,0:T(8,128)(2,1)S(1)}, bf16[64,512]{1,0:T(8,128)(2,1)S(1)}, u32[]{:S(2)}, u32[]{:S(2)}) collective-permute-start(bf16[64,512]{1,0:T(8,128)(2,1)S(1)} %get-tuple-element.64), channel_id=1, source_target_pairs={{0,6},{2,4},{4,2},{6,0},{8,14},{10,12},{12,10},{14,8},{1,7},{3,5},... | collective-permute-start | bytes 196616 | tf_op jit(solution)/shard_map/ppermute | solution.py:379
  45.7 4.4 %collective-permute-start.14 = (bf16[64,512]{1,0:T(8,128)(2,1)S(1)}, bf16[64,512]{1,0:T(8,128)(2,1)S(1)}, u32[]{:S(2)}, u32[]{:S(2)}) collective-permute-start(bf16[64,512]{1,0:T(8,128)(2,1)S(1)} %get-tuple-element.65), channel_id=1, source_target_pairs={{0,4},{2,6},{4,0},{6,2},{8,12},{10,14},{12,8},{14,10},{1,5},{3,7},... | collective-permute-start | bytes 196616 | tf_op jit(solution)/shard_map/ppermute | solution.py:379
  46.8 4.3 %collective-permute-start.15 = (bf16[64,512]{1,0:T(8,128)(2,1)S(1)}, bf16[64,512]{1,0:T(8,128)(2,1)S(1)}, u32[]{:S(2)}, u32[]{:S(2)}) collective-permute-start(bf16[64,512]{1,0:T(8,128)(2,1)S(1)} %get-tuple-element.66), channel_id=1, source_target_pairs={{0,2},{2,0},{4,6},{6,4},{8,10},{10,8},{12,14},{14,12},{1,3},{3,1},... | collective-permute-start | bytes 196616 | tf_op jit(solution)/shard_map/ppermute | solution.py:379
  47.8 5.5 %collective-permute-start.19 = (bf16[64,512]{1,0:T(8,128)(2,1)S(1)}, bf16[64,512]{1,0:T(8,128)(2,1)S(1)}, u32[]{:S(2)}, u32[]{:S(2)}) collective-permute-start(bf16[64,512]{1,0:T(8,128)(2,1)S(1)} %side_sum.1), channel_id=1, source_target_pairs={{0,8},{2,10},{4,12},{6,14},{8,0},{10,2},{12,4},{14,6},{1,9},{3,11}... | collective-permute-start | bytes 196616 | tf_op jit(solution)/shard_map/ppermute | solution.py:379

commit v15 on v13

--- a/solution.py
+++ b/solution.py
@@ -351,41 +351,45 @@
     hidden_ref[...] = jnp.where(live, jnp.maximum(pre, 0.0), 0.0).astype(jnp.bfloat16)
 
 
-def share_kernel(
-    half, fanout_two, near_ref, far_ref, value_ref, hidden_ref, ws_ref, wn_ref, *refs
+def far_share_kernel(
+    half, fanout_two, far_ref, value_ref, hidden_ref, ws_ref, wn_ref, *refs
 ):
-    *out_refs, other_ref = refs
-    store_values(hidden_ref[...], ws_ref, wn_ref, fanout_two, other_ref)
-    values = jnp.concatenate(
-        [value_ref[0], other_ref[0], value_ref[1], other_ref[1]], axis=0
-    )
-    rows = far_ref.shape[0] // half
-    both_ref, far_refs, near_refs = out_refs[0], out_refs[1:half], out_refs[half:]
-    for times_ref, refs, low in ((far_ref, far_refs, 0), (near_ref, near_refs, rows)):
-        part = jnp.dot(times_ref[...], values, preferred_element_type=jnp.float32)
-        part = part.astype(jnp.bfloat16)
-        both_ref[low : low + rows, :] = part[(half - 2) * rows : (half - 1) * rows]
-        for i, ref in enumerate(refs):
-            place = i if i < half - 2 else half - 1
-            ref[...] = part[place * rows : (place + 1) * rows]
-
-
-def sum_rows(first, low, refs, rows):
-    total = first
-    for i, ref in enumerate(refs):
-        at = low if i == 0 else 0
-        total = total + ref[at : at + rows, :].astype(jnp.float32)
-    return total
+    *out_refs, values_ref = refs
+    pcap = hidden_ref.shape[0]
+    for i in range(2):
+        values_ref[2 * i * pcap : (2 * i + 1) * pcap, :] = value_ref[i]
+    hidden = hidden_ref[...]
+    values_ref[pcap : 2 * pcap, :] = jnp.dot(
+        hidden, ws_ref[...], preferred_element_type=jnp.float32
+    ).astype(jnp.bfloat16)
+    values_ref[3 * pcap :, :] = (
+        jnp.dot(hidden, wn_ref[...], preferred_element_type=jnp.float32) / fanout_two
+    ).astype(jnp.bfloat16)
+    store_shares(far_ref, values_ref, out_refs)
+
+
+def store_shares(times_ref, values_ref, out_refs):
+    rows = times_ref.shape[0] // len(out_refs)
+    part = jnp.dot(times_ref[...], values_ref[...], preferred_element_type=jnp.float32)
+    for s, ref in enumerate(out_refs):
+        ref[...] = part[s * rows : (s + 1) * rows].astype(jnp.bfloat16)
+
+
+def near_share_kernel(near_ref, values_ref, *out_refs):
+    store_shares(near_ref, values_ref, out_refs)
 
 
 def side_sum_kernel(*refs):
-    rows = refs[-1].shape[0]
-    refs[-1][...] = sum_rows(0.0, 0, refs[:-1], rows).astype(jnp.bfloat16)
+    total = refs[0][...].astype(jnp.float32)
+    for ref in refs[1:-1]:
+        total = total + ref[...].astype(jnp.float32)
+    refs[-1][...] = total.astype(jnp.bfloat16)
 
 
 def last_kernel(bias_ref, *refs):
-    rows = refs[-1].shape[0]
-    total = sum_rows(bias_ref[...], rows, refs[:-1], rows)
+    total = bias_ref[...]
+    for ref in refs[:-1]:
+        total = total + ref[...].astype(jnp.float32)
     refs[-1][...] = jnp.maximum(total, 0.0).astype(jnp.bfloat16)
 
 
@@ -582,32 +586,33 @@
         scratch=[pltpu.SemaphoreType.DMA],
         outs=(vmem, vmem, anywhere),
     )
-    shares = call(
-        functools.partial(share_kernel, half, fanout_two),
-        "share",
-        [((2 * seed_count, width), bf16)] + [((seed_count, width), bf16)] * (2 * half - 2),
-        [vmem] * 6,
-        (near_times, far_times, value, other_hidden, w2_self, w2_nbr),
-        scratch=[pltpu.VMEM((2, pcap, width), bf16)],
+    *far_shares, values = call(
+        functools.partial(far_share_kernel, half, fanout_two),
+        "far_share",
+        [((seed_count, width), bf16)] * half + [((4 * pcap, width), bf16)],
+        [vmem] * 5,
+        (far_times, value, other_hidden, w2_self, w2_nbr),
         limit=32 * MIB,
     )
-    both = swap(shares[0], "feat", 1)
-    others = [*steps[: half - 2], 0]
-    far_shares = send(shares[1:half], others)
-    near_shares = send(shares[half:], others)
+    far_shares = send(far_shares)
+    near_shares = call(
+        near_share_kernel,
+        "near_share",
+        [((seed_count, width), bf16)] * half,
+        [vmem] * 2,
+        (near_times, values),
+        limit=32 * MIB,
+    )
+    near_shares = send(near_shares)
     (far_sum,) = call(
-        side_sum_kernel,
-        "side_sum",
-        [((seed_count, width), bf16)],
-        [vmem] * half,
-        (both, *far_shares),
+        side_sum_kernel, "side_sum", [((seed_count, width), bf16)], [vmem] * half, far_shares
     )
     (seed_out,) = call(
         last_kernel,
         "seeds",
         [((seed_count, width), bf16)],
         [vmem] * (half + 2),
-        (bias_two[None], both, *near_shares, swap(far_sum, "feat", half)),
+        (bias_two[None], *near_shares, swap(far_sum, "feat", half)),
     )
     return (result[None, None], seed_out)
 

time: 53.4 us -> 53.1 us (level); the launches traced: 52.8 us -> 53.1 us
    pallas_call x14 -> x15, Pallas kernels: 20.5 us -> 20 us  [call(): pl.pallas_call(wrapped, out_shape=tuple((jax.ShapeDtypeStruct(shape, dtyp...]
    ppermute x18 -> x19, starting transfers between devices: 23 us -> 23.4 us  [swap(): return lax.ppermute(value, axis, [(i, i ^ step) for i in range(size)])]
    ppermute x18 -> x19, waiting for transfers between devices: 7.81 us -> 8.11 us  [swap(): return lax.ppermute(value, axis, [(i, i ^ step) for i in range(size)])]
  transfers between devices with their start and end apart: 18 -> 19, of which waited for: 9 -> 8; matrix products, arithmetic and copies ran while one was open for 0% -> 0% of each run, Pallas kernels for 32% -> 31%
where the time goes in v15:
time: 53.1 us
  starting transfers between devices  23.4 us (44%)
  Pallas kernels  20 us (38%)
  waiting for transfers between devices  8.11 us (15%)
  between operations  1.48 us (3%)
    ppermute x19, starting transfers between devices, swap(): return lax.ppermute(value, axis, [(i, i ^ step) for i in range(size)])  23.4 us
    pallas_call x15, Pallas kernels, call(): pl.pallas_call(wrapped, out_shape=tuple((jax.ShapeDtypeStruct(shape, dtyp...  20 us
    ppermute x19, waiting for transfers between devices, swap(): return lax.ppermute(value, axis, [(i, i ^ step) for i in range(size)])  8.11 us
  transfers between devices with their start and end apart: 19, of which 8 were waited for; matrix products, arithmetic and copies ran while one was open for 0% of the time, Pallas kernels for 31%

profile of v15, /device:TPU:0, one launch (start us, length us, event | category | flops | bytes accessed | tf_op | source)
XLA Modules:
  0.0 53.1 jit_solution(7285414831150379690)
XLA Ops:
  0.6 1.8 %pack.1 = (bf16[176,512]{1,0:T(8,128)(2,1)S(1)}, bf16[176,512]{1,0:T(8,128)(2,1)S(1)}, bf16[176,512]{1,0:T(8,128)(2,1)S(1)}, bf16[176,512]{1,0:T(8,128)(2,1)S(1)...) custom-call(bf16[96,12288]{1,0:T(8,128)(2,1)} %refs_0_.3, s32[1,64]{1,0:T(1,128)} %bitcast.15, ...), custom_call_target="tpu_custom_call" | custom-call | flops 1100000000 | tf_op jit(solution)/shard_map/pack/pallas_call | solution.py:433
  2.5 4.0 %collective-permute-start = (bf16[176,512]{1,0:T(8,128)(2,1)S(1)}, bf16[176,512]{1,0:T(8,128)(2,1)S(1)}, u32[]{:S(2)}, u32[]{:S(2)}) collective-permute-start(bf16[176,512]{1,0:T(8,128)(2,1)S(1)} %get-tuple-element.38), channel_id=1, source_target_pairs={{0,6},{2,4},{4,2},{6,0},{8,14},{10,12},{12,10},{14,8},{1,7},{3,5},... | collective-permute-start | bytes 540680 | tf_op jit(solution)/shard_map/ppermute | solution.py:398
  6.5 0.4 collective-permute-start.1
  7.0 0.2 collective-permute-start.2
  7.2 1.2 %turn.1 = f32[12288,128]{1,0:T(8,128)S(1)} custom-call(bf16[96,12288]{1,0:T(8,128)(2,1)S(1)} %get-tuple-element.43.refs_0_), custom_call_target="tpu_custom_call" | custom-call | flops 3300000000 | tf_op jit(solution)/shard_map/turn/pallas_call | solution.py:433
  8.4 6.0 %mean.4 = (bf16[144,128]{1,0:T(8,128)(2,1)S(1)}, bf16[144,128]{1,0:T(8,128)(2,1)S(1)}, bf16[144,128]{1,0:T(8,128)(2,1)S(1)}) custom-call(s32[8,1,1280]{2,1,0:T(1,128)S(1)} %get-tuple-element.42.refs_0_.refs_6_, f32[12288,1,128]{2,1,0:T(1,128)S(1)} %bitcast.7), custom_call_target="tpu_custom_call" | custom-call | flops 6600000000 | tf_op jit(solution)/shard_map/mean/pallas_call | solution.py:433
  14.4 0.0 copy-start.2
  15.0 0.0 collective-permute-done.refs_1_.refs_0_.refs_2_
  15.1 0.1 collective-permute-done.1.refs_2_.refs_1_.refs_3_
  15.2 0.0 collective-permute-done.2.refs_3_.refs_2_.refs_4_
  15.2 0.1 collective-permute-start.6
  15.3 2.8 %collective-permute-start.3 = (bf16[160,128]{1,0:T(8,128)(2,1)S(1)}, bf16[160,128]{1,0:T(8,128)(2,1)S(1)}, u32[]{:S(2)}, u32[]{:S(2)}) collective-permute-start(bf16[160,128]{1,0:T(8,128)(2,1)S(1)} %get-tuple-element.47), channel_id=1, source_target_pairs={{0,6},{2,4},{4,2},{6,0},{8,14},{10,12},{12,10},{14,8},{1,7},{3,5},... | collective-permute-start | bytes 122888 | tf_op jit(solution)/shard_map/ppermute | solution.py:398
  18.1 0.4 collective-permute-start.4
  18.6 0.3 collective-permute-start.5
  18.8 0.0 collective-permute-done.6.refs_4_
  18.8 0.0 copy-done.2
  18.8 2.7 %mean.5 = (bf16[144,128]{1,0:T(8,128)(2,1)S(1)}, bf16[4,96,512]{2,1,0:T(8,128)(2,1)S(1)}, f32[192,512]{1,0:T(8,128)S(1)}, f32[192,512]{1,0:T(8,128)S(1)}, bf16[16,512]{1,0:T(8,128)(2,1)S(1)}) custom-call(bf16[176,512]{1,0:T(8,128)(2,1)S(1)} %collective-permute-done.refs_1_.refs_0_.refs_2_, ...), custom_call_target="tpu_custom_call" | custom-call | tf_op jit(solution)/shard_map/mean/pallas_call | solution.py:433
  21.5 0.0 collective-permute-done.3.refs_0_.refs_4_
  21.5 0.6 %collective-permute-done.4.refs_1_.refs_2_ = bf16[160,128]{1,0:T(8,128)(2,1)S(1)} collective-permute-done((bf16[160,128]{1,0:T(8,128)(2,1)S(1)}, bf16[160,128]{1,0:T(8,128)(2,1)S(1)}, u32[]{:S(2)}, u32[]{:S(2)}) %collective-permute-start.4) | collective-permute-done | bytes 40992 | tf_op jit(solution)/shard_map/ppermute | solution.py:398
  22.1 0.4 collective-permute-done.5.refs_2_.refs_3_
  22.6 0.4 far.1.refs_5_.refs_9_
  22.9 0.0 copy-start
  23.0 0.0 copy-start.1
  23.0 2.6 %collective-permute-start.7 = (bf16[208,512]{1,0:T(8,128)(2,1)S(1)}, bf16[208,512]{1,0:T(8,128)(2,1)S(1)}, u32[]{:S(2)}, u32[]{:S(2)}) collective-permute-start(bf16[208,512]{1,0:T(8,128)(2,1)S(1)} %far.1.refs_5_.refs_9_), channel_id=1, source_target_pairs={{0,8},{2,10},{4,12},{6,14},{8,0},{10,2},{12,4},{14,6},{1,9},{3,11}... | collective-permute-start | bytes 638984 | tf_op jit(solution)/shard_map/ppermute | solution.py:398
  25.6 3.3 %mean.6 = (bf16[144,128]{1,0:T(8,128)(2,1)S(1)}, bf16[144,128]{1,0:T(8,128)(2,1)S(1)}, bf16[144,128]{1,0:T(8,128)(2,1)S(1)}) custom-call(s32[8,1,1280]{2,1,0:T(1,128)S(1)} %get-tuple-element.42.refs_0_.refs_6_, f32[12288,1,128]{2,1,0:T(1,128)S(1)} %bitcast.9, bf16[160,128]{1,0:T(8,128)(2,1)S(1)} %collective-permute-done.4.refs_1_.refs_2_, ...), custom_call_target="tpu_custom_call" | custom-call | flops 6600000000 | tf_op jit(solution)/shard_map/mean/pallas_call | solution.py:433
  28.9 2.1 %collective-permute-start.10 = (bf16[144,128]{1,0:T(8,128)(2,1)S(1)}, bf16[144,128]{1,0:T(8,128)(2,1)S(1)}, u32[]{:S(2)}, u32[]{:S(2)}) collective-permute-start(bf16[144,128]{1,0:T(8,128)(2,1)S(1)} %get-tuple-element.58), channel_id=1, source_target_pairs={{0,6},{2,4},{4,2},{6,0},{8,14},{10,12},{12,10},{14,8},{1,7},{3,5},... | collective-permute-start | bytes 110600 | tf_op jit(solution)/shard_map/ppermute | solution.py:398
  31.0 0.0 collective-permute-start.8
  31.0 1.4 %collective-permute-start.9 = (bf16[144,128]{1,0:T(8,128)(2,1)S(1)}, bf16[144,128]{1,0:T(8,128)(2,1)S(1)}, u32[]{:S(2)}, u32[]{:S(2)}) collective-permute-start(bf16[144,128]{1,0:T(8,128)(2,1)S(1)} %get-tuple-element.57), channel_id=1, source_target_pairs={{0,2},{2,0},{4,6},{6,4},{8,10},{10,8},{12,14},{14,12},{1,3},{3,1},... | collective-permute-start | bytes 110600 | tf_op jit(solution)/shard_map/ppermute | solution.py:398
  32.4 0.0 copy-done
  32.4 0.0 copy-done.1
  32.4 1.6 %mean.7 = (bf16[144,128]{1,0:T(8,128)(2,1)S(1)}, bf16[256,768]{1,0:T(8,128)(2,1)S(1)}) custom-call(bf16[512,512]{1,0:T(8,128)(2,1)S(1)} %copy-done, bf16[512,512]{1,0:T(8,128)(2,1)S(1)} %copy-done.1, bf16[176,512]{1,0:T(8,128)(2,1)S(1)} %collective-permute-done.refs_1_.refs_0_.refs_2_, bf16[176,512]{1,0:T(8,128)(2,1)S(1)} %collective-permute-done.1.refs_2_.refs_1_.refs_3_, ...), custom_call_target="tpu_custom_call" | custom-call | tf_op jit(solution)/shard_map/mean/pallas_call | solution.py:433
  34.0 2.2 %collective-permute-done.10.refs_2_ = bf16[144,128]{1,0:T(8,128)(2,1)S(1)} collective-permute-done((bf16[144,128]{1,0:T(8,128)(2,1)S(1)}, bf16[144,128]{1,0:T(8,128)(2,1)S(1)}, u32[]{:S(2)}, u32[]{:S(2)}) %collective-permute-start.10) | collective-permute-done | bytes 36896 | tf_op jit(solution)/shard_map/ppermute | solution.py:398
  36.2 0.0 collective-permute-done.8.refs_0_
  36.2 0.0 collective-permute-done.9.refs_1_
  36.2 0.4 near.1.refs_1_
  36.6 0.0 collective-permute-done.7.refs_2_.refs_0_
  36.6 0.2 hidden.1.refs_1_
  36.8 0.1 collective-permute-start.11
  36.9 0.9 %far_times.1 = (bf16[256,768]{1,0:T(8,128)(2,1)S(1)}, bf16[2,192,512]{2,1,0:T(8,128)(2,1)S(1)}, bf16[192,512]{1,0:T(8,128)(2,1)}) custom-call(bf16[208,512]{1,0:T(8,128)(2,1)S(1)} %collective-permute-done.7.refs_2_.refs_0_, bf16[192,512]{1,0:T(8,128)(2,1)S(1)} %hidden.1.refs_1_, bf16[512,512]{1,0:T(8,128)(2,1)S(1)} %copy-done, bf16[512,512]{1,0:T(8,128)(2,1)S(1)} %copy-done.1), custom_call_target="tpu_custom_call" | custom-call | flops 1100000000 | tf_op jit(solution)/shard_map/far_times/pallas_call | solution.py:433
  37.7 0.6 %collective-permute-done.11.refs_2_ = bf16[192,512]{1,0:T(8,128)(2,1)S(1)} collective-permute-done((bf16[192,512]{1,0:T(8,128)(2,1)S(1)}, bf16[192,512]{1,0:T(8,128)(2,1)S(1)}, u32[]{:S(2)}, u32[]{:S(2)}) %collective-permute-start.11) | collective-permute-done | bytes 196640 | tf_op jit(solution)/shard_map/ppermute | solution.py:398
  38.3 0.6 %far_share.1 = (bf16[64,512]{1,0:T(8,128)(2,1)S(1)}, bf16[64,512]{1,0:T(8,128)(2,1)S(1)}, bf16[64,512]{1,0:T(8,128)(2,1)S(1)}, bf16[64,512]{1,0:T(8,128)(2,1)S(1)}, bf16[768,512]{1,0:T(8,128)(2,1)S(1)}) custom-call(bf16[256,768]{1,0:T(8,128)(2,1)S(1)} %get-tuple-element.63.refs_0_, bf16[2,192,512]{2,1,0:T(8,128)(2,1)S(1)} %get-tuple-element.64.refs_1_, ...), custom_call_target="tpu_custom_call" | custom-call | flops 1100000000 | tf_op jit(solution)/shard_map/far_share/pallas_call | solution.py:433
  38.9 1.5 %collective-permute-start.15 = (bf16[64,512]{1,0:T(8,128)(2,1)S(1)}, bf16[64,512]{1,0:T(8,128)(2,1)S(1)}, u32[]{:S(2)}, u32[]{:S(2)}) collective-permute-start(bf16[64,512]{1,0:T(8,128)(2,1)S(1)} %get-tuple-element.70), channel_id=1, source_target_pairs={{0,6},{2,4},{4,2},{6,0},{8,14},{10,12},{12,10},{14,8},{1,7},{3,5},... | collective-permute-start | bytes 196616 | tf_op jit(solution)/shard_map/ppermute | solution.py:398
  40.4 1.0 %collective-permute-start.16 = (bf16[64,512]{1,0:T(8,128)(2,1)S(1)}, bf16[64,512]{1,0:T(8,128)(2,1)S(1)}, u32[]{:S(2)}, u32[]{:S(2)}) collective-permute-start(bf16[64,512]{1,0:T(8,128)(2,1)S(1)} %get-tuple-element.71), channel_id=1, source_target_pairs={{0,4},{2,6},{4,0},{6,2},{8,12},{10,14},{12,8},{14,10},{1,5},{3,7},... | collective-permute-start | bytes 196616 | tf_op jit(solution)/shard_map/ppermute | solution.py:398
  41.4 1.1 %collective-permute-start.17 = (bf16[64,512]{1,0:T(8,128)(2,1)S(1)}, bf16[64,512]{1,0:T(8,128)(2,1)S(1)}, u32[]{:S(2)}, u32[]{:S(2)}) collective-permute-start(bf16[64,512]{1,0:T(8,128)(2,1)S(1)} %get-tuple-element.72), channel_id=1, source_target_pairs={{0,2},{2,0},{4,6},{6,4},{8,10},{10,8},{12,14},{14,12},{1,3},{3,1},... | collective-permute-start | bytes 196616 | tf_op jit(solution)/shard_map/ppermute | solution.py:398
  42.5 0.4 near_share.1
  42.8 0.0 copy-start.3
  42.8 1.5 %collective-permute-start.12 = (bf16[64,512]{1,0:T(8,128)(2,1)S(1)}, bf16[64,512]{1,0:T(8,128)(2,1)S(1)}, u32[]{:S(2)}, u32[]{:S(2)}) collective-permute-start(bf16[64,512]{1,0:T(8,128)(2,1)S(1)} %get-tuple-element.66), channel_id=1, source_target_pairs={{0,6},{2,4},{4,2},{6,0},{8,14},{10,12},{12,10},{14,8},{1,7},{3,5},... | collective-permute-start | bytes 196616 | tf_op jit(solution)/shard_map/ppermute | solution.py:398
  44.3 1.0 %collective-permute-start.13 = (bf16[64,512]{1,0:T(8,128)(2,1)S(1)}, bf16[64,512]{1,0:T(8,128)(2,1)S(1)}, u32[]{:S(2)}, u32[]{:S(2)}) collective-permute-start(bf16[64,512]{1,0:T(8,128)(2,1)S(1)} %get-tuple-element.67), channel_id=1, source_target_pairs={{0,4},{2,6},{4,0},{6,2},{8,12},{10,14},{12,8},{14,10},{1,5},{3,7},... | collective-permute-start | bytes 196616 | tf_op jit(solution)/shard_map/ppermute | solution.py:398
  45.3 0.0 collective-permute-done.15.refs_0_
  45.3 1.1 %collective-permute-start.14 = (bf16[64,512]{1,0:T(8,128)(2,1)S(1)}, bf16[64,512]{1,0:T(8,128)(2,1)S(1)}, u32[]{:S(2)}, u32[]{:S(2)}) collective-permute-start(bf16[64,512]{1,0:T(8,128)(2,1)S(1)} %get-tuple-element.68), channel_id=1, source_target_pairs={{0,2},{2,0},{4,6},{6,4},{8,10},{10,8},{12,14},{14,12},{1,3},{3,1},... | collective-permute-start | bytes 196616 | tf_op jit(solution)/shard_map/ppermute | solution.py:398
  46.4 0.0 collective-permute-done.16.refs_1_
  46.4 0.0 collective-permute-done.17.refs_2_
  46.4 1.7 %collective-permute-start.18 = (bf16[64,512]{1,0:T(8,128)(2,1)S(1)}, bf16[64,512]{1,0:T(8,128)(2,1)S(1)}, u32[]{:S(2)}, u32[]{:S(2)}) collective-permute-start(bf16[64,512]{1,0:T(8,128)(2,1)S(1)} %side_sum.1), channel_id=1, source_target_pairs={{0,8},{2,10},{4,12},{6,14},{8,0},{10,2},{12,4},{14,6},{1,9},{3,11}... | collective-permute-start | bytes 196616 | tf_op jit(solution)/shard_map/ppermute | solution.py:398
  48.1 0.0 collective-permute-done.12.refs_1_
  48.1 0.5 collective-permute-done.13.refs_2_
  48.6 1.0 %collective-permute-done.14.refs_3_ = bf16[64,512]{1,0:T(8,128)(2,1)S(1)} collective-permute-done((bf16[64,512]{1,0:T(8,128)(2,1)S(1)}, bf16[64,512]{1,0:T(8,128)(2,1)S(1)}, u32[]{:S(2)}, u32[]{:S(2)}) %collective-permute-start.14) | collective-permute-done | bytes 65568 | tf_op jit(solution)/shard_map/ppermute | solution.py:398
  49.6 2.8 %collective-permute-done.18.refs_5_ = bf16[64,512]{1,0:T(8,128)(2,1)S(1)} collective-permute-done((bf16[64,512]{1,0:T(8,128)(2,1)S(1)}, bf16[64,512]{1,0:T(8,128)(2,1)S(1)}, u32[]{:S(2)}, u32[]{:S(2)}) %collective-permute-start.18) | collective-permute-done | bytes 65568 | tf_op jit(solution)/shard_map/ppermute | solution.py:398
  52.4 0.0 copy-done.3
  52.4 0.7 %seeds.1 = bf16[64,512]{1,0:T(8,128)(2,1)} custom-call(f32[1,512]{1,0:T(1,128)S(1)} %bitcast.12, bf16[64,512]{1,0:T(8,128)(2,1)S(1)} %collective-permute-done.12.refs_1_, bf16[64,512]{1,0:T(8,128)(2,1)S(1)} %collective-permute-done.13.refs_2_, bf16[64,512]{1,0:T(8,128)(2,1)S(1)} %collective-permute-done.14.refs_3_, ...), custom_call_target="tpu_custom_call" | custom-call | flops 1100000000 | tf_op jit(solution)/shard_map/seeds/pallas_call | solution.py:433
  (2 shorter events, 0.1 us)
Async XLA Ops:
  2.5 12.6 %collective-permute-start = (bf16[176,512]{1,0:T(8,128)(2,1)S(1)}, bf16[176,512]{1,0:T(8,128)(2,1)S(1)}, u32[]{:S(2)}, u32[]{:S(2)}) collective-permute-start(bf16[176,512]{1,0:T(8,128)(2,1)S(1)} %get-tuple-element.38), channel_id=1, source_target_pairs={{0,6},{2,4},{4,2},{6,0},{8,14},{10,12},{12,10},{14,8},{1,7},{3,5},... | collective-permute-start | bytes 540680 | tf_op jit(solution)/shard_map/ppermute | solution.py:398
  6.5 8.6 %collective-permute-start.1 = (bf16[176,512]{1,0:T(8,128)(2,1)S(1)}, bf16[176,512]{1,0:T(8,128)(2,1)S(1)}, u32[]{:S(2)}, u32[]{:S(2)}) collective-permute-start(bf16[176,512]{1,0:T(8,128)(2,1)S(1)} %get-tuple-element.39), channel_id=1, source_target_pairs={{0,4},{2,6},{4,0},{6,2},{8,12},{10,14},{12,8},{14,10},{1,5},{3,7},... | collective-permute-start | bytes 540680 | tf_op jit(solution)/shard_map/ppermute | solution.py:398
  7.0 8.2 %collective-permute-start.2 = (bf16[176,512]{1,0:T(8,128)(2,1)S(1)}, bf16[176,512]{1,0:T(8,128)(2,1)S(1)}, u32[]{:S(2)}, u32[]{:S(2)}) collective-permute-start(bf16[176,512]{1,0:T(8,128)(2,1)S(1)} %get-tuple-element.40), channel_id=1, source_target_pairs={{0,2},{2,0},{4,6},{6,4},{8,10},{10,8},{12,14},{14,12},{1,3},{3,1},... | collective-permute-start | bytes 540680 | tf_op jit(solution)/shard_map/ppermute | solution.py:398
  14.4 4.5 %copy-start.2 = (f32[512]{0:T(512)S(1)}, f32[512]{0:T(512)}, u32[]{:S(2)}) copy-start(f32[512]{0:T(512)} %param.18) | copy-start | bytes 6148
  15.2 3.6 %collective-permute-start.6 = (bf16[4,96,512]{2,1,0:T(8,128)(2,1)S(1)}, bf16[4,96,512]{2,1,0:T(8,128)(2,1)S(1)}, u32[]{:S(2)}, u32[]{:S(2)}) collective-permute-start(bf16[4,96,512]{2,1,0:T(8,128)(2,1)S(1)} %get-tuple-element.50), channel_id=1, source_target_pairs={{0,1},{1,0},{2,3},{3,2},{4,5},{5,4},{6,7},{7,6},{8,9},{9,8},{10,11... | collective-permute-start | bytes 1179656 | tf_op jit(solution)/shard_map/ppermute | solution.py:398
  15.3 6.3 %collective-permute-start.3 = (bf16[160,128]{1,0:T(8,128)(2,1)S(1)}, bf16[160,128]{1,0:T(8,128)(2,1)S(1)}, u32[]{:S(2)}, u32[]{:S(2)}) collective-permute-start(bf16[160,128]{1,0:T(8,128)(2,1)S(1)} %get-tuple-element.47), channel_id=1, source_target_pairs={{0,6},{2,4},{4,2},{6,0},{8,14},{10,12},{12,10},{14,8},{1,7},{3,5},... | collective-permute-start | bytes 122888 | tf_op jit(solution)/shard_map/ppermute | solution.py:398
  18.1 4.0 %collective-permute-start.4 = (bf16[160,128]{1,0:T(8,128)(2,1)S(1)}, bf16[160,128]{1,0:T(8,128)(2,1)S(1)}, u32[]{:S(2)}, u32[]{:S(2)}) collective-permute-start(bf16[160,128]{1,0:T(8,128)(2,1)S(1)} %get-tuple-element.48), channel_id=1, source_target_pairs={{0,4},{2,6},{4,0},{6,2},{8,12},{10,14},{12,8},{14,10},{1,5},{3,7},... | collective-permute-start | bytes 122888 | tf_op jit(solution)/shard_map/ppermute | solution.py:398
  18.6 4.0 %collective-permute-start.5 = (bf16[160,128]{1,0:T(8,128)(2,1)S(1)}, bf16[160,128]{1,0:T(8,128)(2,1)S(1)}, u32[]{:S(2)}, u32[]{:S(2)}) collective-permute-start(bf16[160,128]{1,0:T(8,128)(2,1)S(1)} %get-tuple-element.49), channel_id=1, source_target_pairs={{0,2},{2,0},{4,6},{6,4},{8,10},{10,8},{12,14},{14,12},{1,3},{3,1},... | collective-permute-start | bytes 122888 | tf_op jit(solution)/shard_map/ppermute | solution.py:398
  22.9 9.5 %copy-start = (bf16[512,512]{1,0:T(8,128)(2,1)S(1)}, bf16[512,512]{1,0:T(8,128)(2,1)}, u32[]{:S(2)}) copy-start(bf16[512,512]{1,0:T(8,128)(2,1)} %refs_3_.5) | copy-start | bytes 1572868
  23.0 9.5 %copy-start.1 = (bf16[512,512]{1,0:T(8,128)(2,1)S(1)}, bf16[512,512]{1,0:T(8,128)(2,1)}, u32[]{:S(2)}) copy-start(bf16[512,512]{1,0:T(8,128)(2,1)} %refs_4_.3) | copy-start | bytes 1572868
  23.0 13.6 %collective-permute-start.7 = (bf16[208,512]{1,0:T(8,128)(2,1)S(1)}, bf16[208,512]{1,0:T(8,128)(2,1)S(1)}, u32[]{:S(2)}, u32[]{:S(2)}) collective-permute-start(bf16[208,512]{1,0:T(8,128)(2,1)S(1)} %far.1.refs_5_.refs_9_), channel_id=1, source_target_pairs={{0,8},{2,10},{4,12},{6,14},{8,0},{10,2},{12,4},{14,6},{1,9},{3,11}... | collective-permute-start | bytes 638984 | tf_op jit(solution)/shard_map/ppermute | solution.py:398
  28.9 7.3 %collective-permute-start.10 = (bf16[144,128]{1,0:T(8,128)(2,1)S(1)}, bf16[144,128]{1,0:T(8,128)(2,1)S(1)}, u32[]{:S(2)}, u32[]{:S(2)}) collective-permute-start(bf16[144,128]{1,0:T(8,128)(2,1)S(1)} %get-tuple-element.58), channel_id=1, source_target_pairs={{0,6},{2,4},{4,2},{6,0},{8,14},{10,12},{12,10},{14,8},{1,7},{3,5},... | collective-permute-start | bytes 110600 | tf_op jit(solution)/shard_map/ppermute | solution.py:398
  31.0 5.2 %collective-permute-start.8 = (bf16[144,128]{1,0:T(8,128)(2,1)S(1)}, bf16[144,128]{1,0:T(8,128)(2,1)S(1)}, u32[]{:S(2)}, u32[]{:S(2)}) collective-permute-start(bf16[144,128]{1,0:T(8,128)(2,1)S(1)} %get-tuple-element.56), channel_id=1, source_target_pairs={{0,4},{2,6},{4,0},{6,2},{8,12},{10,14},{12,8},{14,10},{1,5},{3,7},... | collective-permute-start | bytes 110600 | tf_op jit(solution)/shard_map/ppermute | solution.py:398
  31.0 5.2 %collective-permute-start.9 = (bf16[144,128]{1,0:T(8,128)(2,1)S(1)}, bf16[144,128]{1,0:T(8,128)(2,1)S(1)}, u32[]{:S(2)}, u32[]{:S(2)}) collective-permute-start(bf16[144,128]{1,0:T(8,128)(2,1)S(1)} %get-tuple-element.57), channel_id=1, source_target_pairs={{0,2},{2,0},{4,6},{6,4},{8,10},{10,8},{12,14},{14,12},{1,3},{3,1},... | collective-permute-start | bytes 110600 | tf_op jit(solution)/shard_map/ppermute | solution.py:398
  36.8 1.5 %collective-permute-start.11 = (bf16[192,512]{1,0:T(8,128)(2,1)S(1)}, bf16[192,512]{1,0:T(8,128)(2,1)S(1)}, u32[]{:S(2)}, u32[]{:S(2)}) collective-permute-start(bf16[192,512]{1,0:T(8,128)(2,1)S(1)} %hidden.1.refs_1_), channel_id=1, source_target_pairs={{0,1},{1,0},{2,3},{3,2},{4,5},{5,4},{6,7},{7,6},{8,9},{9,8},{10,11... | collective-permute-start | bytes 589832 | tf_op jit(solution)/shard_map/ppermute | solution.py:398
  38.9 6.4 %collective-permute-start.15 = (bf16[64,512]{1,0:T(8,128)(2,1)S(1)}, bf16[64,512]{1,0:T(8,128)(2,1)S(1)}, u32[]{:S(2)}, u32[]{:S(2)}) collective-permute-start(bf16[64,512]{1,0:T(8,128)(2,1)S(1)} %get-tuple-element.70), channel_id=1, source_target_pairs={{0,6},{2,4},{4,2},{6,0},{8,14},{10,12},{12,10},{14,8},{1,7},{3,5},... | collective-permute-start | bytes 196616 | tf_op jit(solution)/shard_map/ppermute | solution.py:398
  40.4 6.0 %collective-permute-start.16 = (bf16[64,512]{1,0:T(8,128)(2,1)S(1)}, bf16[64,512]{1,0:T(8,128)(2,1)S(1)}, u32[]{:S(2)}, u32[]{:S(2)}) collective-permute-start(bf16[64,512]{1,0:T(8,128)(2,1)S(1)} %get-tuple-element.71), channel_id=1, source_target_pairs={{0,4},{2,6},{4,0},{6,2},{8,12},{10,14},{12,8},{14,10},{1,5},{3,7},... | collective-permute-start | bytes 196616 | tf_op jit(solution)/shard_map/ppermute | solution.py:398
  41.4 5.0 %collective-permute-start.17 = (bf16[64,512]{1,0:T(8,128)(2,1)S(1)}, bf16[64,512]{1,0:T(8,128)(2,1)S(1)}, u32[]{:S(2)}, u32[]{:S(2)}) collective-permute-start(bf16[64,512]{1,0:T(8,128)(2,1)S(1)} %get-tuple-element.72), channel_id=1, source_target_pairs={{0,2},{2,0},{4,6},{6,4},{8,10},{10,8},{12,14},{14,12},{1,3},{3,1},... | collective-permute-start | bytes 196616 | tf_op jit(solution)/shard_map/ppermute | solution.py:398
  42.8 9.6 %copy-start.3 = (f32[512]{0:T(512)S(1)}, f32[512]{0:T(512)}, u32[]{:S(2)}) copy-start(f32[512]{0:T(512)} %param.21) | copy-start | bytes 6148
  42.8 5.3 %collective-permute-start.12 = (bf16[64,512]{1,0:T(8,128)(2,1)S(1)}, bf16[64,512]{1,0:T(8,128)(2,1)S(1)}, u32[]{:S(2)}, u32[]{:S(2)}) collective-permute-start(bf16[64,512]{1,0:T(8,128)(2,1)S(1)} %get-tuple-element.66), channel_id=1, source_target_pairs={{0,6},{2,4},{4,2},{6,0},{8,14},{10,12},{12,10},{14,8},{1,7},{3,5},... | collective-permute-start | bytes 196616 | tf_op jit(solution)/shard_map/ppermute | solution.py:398
  44.3 4.3 %collective-permute-start.13 = (bf16[64,512]{1,0:T(8,128)(2,1)S(1)}, bf16[64,512]{1,0:T(8,128)(2,1)S(1)}, u32[]{:S(2)}, u32[]{:S(2)}) collective-permute-start(bf16[64,512]{1,0:T(8,128)(2,1)S(1)} %get-tuple-element.67), channel_id=1, source_target_pairs={{0,4},{2,6},{4,0},{6,2},{8,12},{10,14},{12,8},{14,10},{1,5},{3,7},... | collective-permute-start | bytes 196616 | tf_op jit(solution)/shard_map/ppermute | solution.py:398
  45.3 4.3 %collective-permute-start.14 = (bf16[64,512]{1,0:T(8,128)(2,1)S(1)}, bf16[64,512]{1,0:T(8,128)(2,1)S(1)}, u32[]{:S(2)}, u32[]{:S(2)}) collective-permute-start(bf16[64,512]{1,0:T(8,128)(2,1)S(1)} %get-tuple-element.68), channel_id=1, source_target_pairs={{0,2},{2,0},{4,6},{6,4},{8,10},{10,8},{12,14},{14,12},{1,3},{3,1},... | collective-permute-start | bytes 196616 | tf_op jit(solution)/shard_map/ppermute | solution.py:398
  46.4 5.9 %collective-permute-start.18 = (bf16[64,512]{1,0:T(8,128)(2,1)S(1)}, bf16[64,512]{1,0:T(8,128)(2,1)S(1)}, u32[]{:S(2)}, u32[]{:S(2)}) collective-permute-start(bf16[64,512]{1,0:T(8,128)(2,1)S(1)} %side_sum.1), channel_id=1, source_target_pairs={{0,8},{2,10},{4,12},{6,14},{8,0},{10,2},{12,4},{14,6},{1,9},{3,11}... | collective-permute-start | bytes 196616 | tf_op jit(solution)/shard_map/ppermute | solution.py:398

commit v16 on v15

--- a/solution.py
+++ b/solution.py
@@ -141,6 +141,7 @@
     chunk_refs, tagged_refs = refs[len(refs) - count :], refs[: len(refs) - count]
     feat_pos = lax.axis_index("feat")
     words = fanout // packed
+    size = 16 if len(tagged_refs) or pcap % 64 else 64
     stride = -(-pcap // LANES) * LANES
     length = words * stride
     copies = [
@@ -164,10 +165,10 @@
         first = i * length
 
         def group(g, inner):
-            at = pl.multiple_of(g * 16, 16)
+            at = pl.multiple_of(g * size, 16)
             start = first + at
             sums = []
-            for u in range(16):
+            for u in range(size):
                 names = [nbr_ref[start + (k * stride + u)] for k in range(words)]
                 if packed == 2:
                     names = [
@@ -181,11 +182,13 @@
                         [rows[-1]] if len(rows) % 2 else []
                     )
                 sums.append(rows[0])
-            for u, row in enumerate(sums):
-                total[pl.ds(at + u, 1), :] = row
+                if len(sums) == 16:
+                    for v, row in enumerate(sums):
+                        total[pl.ds(at + (u - 15 + v), 1), :] = row
+                    sums = []
             return inner
 
-        lax.fori_loop(0, lax.div(live_ref[i] + 15, 16), group, 0)
+        lax.fori_loop(0, lax.div(live_ref[i] + size - 1, size), group, 0)
         mean = total[...] / fanout
         if folds(fslice, pcap):
             part = pcap // 4
@@ -376,7 +379,25 @@
 
 
 def near_share_kernel(near_ref, values_ref, *out_refs):
-    store_shares(near_ref, values_ref, out_refs)
+    rows = near_ref.shape[0]
+    pairs = len(out_refs)
+    count = 2 * (pairs - 1)
+    each = rows // count
+    part = jnp.dot(near_ref[...], values_ref[...], preferred_element_type=jnp.float32)
+    part = part.astype(jnp.bfloat16)
+    for i in range(pairs - 1):
+        out_refs[0][i * each : (i + 1) * each, :] = part[2 * i * each : (2 * i + 1) * each]
+        out_refs[i + 1][...] = part[(2 * i + 1) * each : (2 * i + 2) * each]
+
+
+def relay_kernel(relay_ref, *refs):
+    count = len(refs) // 2
+    for i in range(count):
+        rows = refs[i].shape[0]
+        refs[count + i][...] = (
+            refs[i][...].astype(jnp.float32)
+            + relay_ref[i * rows : (i + 1) * rows, :].astype(jnp.float32)
+        ).astype(jnp.bfloat16)
 
 
 def side_sum_kernel(*refs):
@@ -595,24 +616,36 @@
         limit=32 * MIB,
     )
     far_shares = send(far_shares)
-    near_shares = call(
+    column, *near_shares = call(
         near_share_kernel,
         "near_share",
-        [((seed_count, width), bf16)] * half,
+        [((half // 2 * seed_count, width), bf16)] + [((seed_count, width), bf16)] * (half // 2),
         [vmem] * 2,
         (near_times, values),
         limit=32 * MIB,
     )
-    near_shares = send(near_shares)
+    column = swap(column, "feat", 1)
     (far_sum,) = call(
         side_sum_kernel, "side_sum", [((seed_count, width), bf16)], [vmem] * half, far_shares
     )
+    far_sum = swap(far_sum, "feat", half)
+    near_shares = call(
+        relay_kernel,
+        "relay",
+        [((seed_count, width), bf16)] * (half // 2),
+        [vmem] * (half // 2 + 1),
+        (column, *near_shares),
+        after=far_shares[:1],
+    )
+    near_shares = [
+        swap(share, "feat", s) if s else share for share, s in zip(near_shares, steps[1::2])
+    ]
     (seed_out,) = call(
         last_kernel,
         "seeds",
         [((seed_count, width), bf16)],
-        [vmem] * (half + 2),
-        (bias_two[None], *near_shares, swap(far_sum, "feat", half)),
+        [vmem] * (half // 2 + 2),
+        (bias_two[None], *near_shares, far_sum),
     )
     return (result[None, None], seed_out)
 

time: 53.1 us -> 53.8 us (1.013)
  Pallas kernels: 20 us -> 21.2 us
  starting transfers between devices: 23.4 us -> 22.7 us
    pallas_call x15 -> x16, Pallas kernels: 20 us -> 21.2 us  [call(): pl.pallas_call(wrapped, out_shape=tuple((jax.ShapeDtypeStruct(shape, dtyp...]
    ppermute x19 -> x18, starting transfers between devices: 23.4 us -> 22.7 us  [swap(): return lax.ppermute(value, axis, [(i, i ^ step) for i in range(size)])]
    ppermute x19 -> x18, waiting for transfers between devices: 8.11 us -> 8.13 us  [swap(): return lax.ppermute(value, axis, [(i, i ^ step) for i in range(size)])]
  transfers between devices with their start and end apart: 19 -> 18, of which waited for: 8 -> 12; matrix products, arithmetic and copies ran while one was open for 0% -> 0% of each run, Pallas kernels for 31% -> 33%
where the time goes in v16:
time: 53.8 us; the launch traced here: 53.6 us
  starting transfers between devices  22.7 us (42%)
  Pallas kernels  21.2 us (39%)
  waiting for transfers between devices  8.13 us (15%)
  between operations  1.48 us (3%)
    ppermute x18, starting transfers between devices, swap(): return lax.ppermute(value, axis, [(i, i ^ step) for i in range(size)])  22.7 us
    pallas_call x16, Pallas kernels, call(): pl.pallas_call(wrapped, out_shape=tuple((jax.ShapeDtypeStruct(shape, dtyp...  21.2 us
    ppermute x18, waiting for transfers between devices, swap(): return lax.ppermute(value, axis, [(i, i ^ step) for i in range(size)])  8.13 us
  transfers between devices with their start and end apart: 18, of which 12 were waited for; matrix products, arithmetic and copies ran while one was open for 0% of the time, Pallas kernels for 33%

profile of v16, /device:TPU:0, one launch (start us, length us, event | category | flops | bytes accessed | tf_op | source)
XLA Modules:
  0.0 53.6 jit_solution(18308324643813703713)
XLA Ops:
  0.6 1.8 %pack.1 = (bf16[176,512]{1,0:T(8,128)(2,1)S(1)}, bf16[176,512]{1,0:T(8,128)(2,1)S(1)}, bf16[176,512]{1,0:T(8,128)(2,1)S(1)}, bf16[176,512]{1,0:T(8,128)(2,1)S(1)...) custom-call(bf16[96,12288]{1,0:T(8,128)(2,1)} %refs_0_.3, s32[1,64]{1,0:T(1,128)} %bitcast.15, ...), custom_call_target="tpu_custom_call" | custom-call | flops 1100000000 | tf_op jit(solution)/shard_map/pack/pallas_call | solution.py:454
  2.5 4.0 %collective-permute-start = (bf16[176,512]{1,0:T(8,128)(2,1)S(1)}, bf16[176,512]{1,0:T(8,128)(2,1)S(1)}, u32[]{:S(2)}, u32[]{:S(2)}) collective-permute-start(bf16[176,512]{1,0:T(8,128)(2,1)S(1)} %get-tuple-element.39), channel_id=1, source_target_pairs={{0,6},{2,4},{4,2},{6,0},{8,14},{10,12},{12,10},{14,8},{1,7},{3,5},... | collective-permute-start | bytes 540680 | tf_op jit(solution)/shard_map/ppermute | solution.py:419
  6.5 0.4 collective-permute-start.1
  7.0 0.2 collective-permute-start.2
  7.2 1.2 %turn.1 = f32[12288,128]{1,0:T(8,128)S(1)} custom-call(bf16[96,12288]{1,0:T(8,128)(2,1)S(1)} %get-tuple-element.44.refs_0_), custom_call_target="tpu_custom_call" | custom-call | flops 3300000000 | tf_op jit(solution)/shard_map/turn/pallas_call | solution.py:454
  8.4 5.7 %mean.4 = (bf16[144,128]{1,0:T(8,128)(2,1)S(1)}, bf16[144,128]{1,0:T(8,128)(2,1)S(1)}, bf16[144,128]{1,0:T(8,128)(2,1)S(1)}) custom-call(s32[8,1,1280]{2,1,0:T(1,128)S(1)} %get-tuple-element.43.refs_0_.refs_6_, f32[12288,1,128]{2,1,0:T(1,128)S(1)} %bitcast.7), custom_call_target="tpu_custom_call" | custom-call | flops 6600000000 | tf_op jit(solution)/shard_map/mean/pallas_call | solution.py:454
  14.1 0.0 copy-start.2
  14.8 0.0 collective-permute-done.refs_1_.refs_0_.refs_2_
  14.8 0.3 collective-permute-done.1.refs_2_.refs_1_.refs_3_
  15.2 0.0 collective-permute-done.2.refs_3_.refs_2_.refs_4_
  15.2 0.1 collective-permute-start.6
  15.3 2.6 %collective-permute-start.3 = (bf16[160,128]{1,0:T(8,128)(2,1)S(1)}, bf16[160,128]{1,0:T(8,128)(2,1)S(1)}, u32[]{:S(2)}, u32[]{:S(2)}) collective-permute-start(bf16[160,128]{1,0:T(8,128)(2,1)S(1)} %get-tuple-element.48), channel_id=1, source_target_pairs={{0,6},{2,4},{4,2},{6,0},{8,14},{10,12},{12,10},{14,8},{1,7},{3,5},... | collective-permute-start | bytes 122888 | tf_op jit(solution)/shard_map/ppermute | solution.py:419
  17.9 0.4 collective-permute-start.4
  18.3 0.5 collective-permute-start.5
  18.8 0.0 collective-permute-done.6.refs_4_
  18.8 0.0 copy-done.2
  18.8 2.6 %mean.5 = (bf16[144,128]{1,0:T(8,128)(2,1)S(1)}, bf16[4,96,512]{2,1,0:T(8,128)(2,1)S(1)}, f32[192,512]{1,0:T(8,128)S(1)}, f32[192,512]{1,0:T(8,128)S(1)}, bf16[16,512]{1,0:T(8,128)(2,1)S(1)}) custom-call(bf16[176,512]{1,0:T(8,128)(2,1)S(1)} %collective-permute-done.refs_1_.refs_0_.refs_2_, ...), custom_call_target="tpu_custom_call" | custom-call | tf_op jit(solution)/shard_map/mean/pallas_call | solution.py:454
  21.4 0.0 collective-permute-done.3.refs_0_.refs_4_
  21.5 0.4 collective-permute-done.4.refs_1_.refs_2_
  21.9 0.4 collective-permute-done.5.refs_2_.refs_3_
  22.3 0.4 far.1.refs_5_.refs_9_
  22.7 0.0 copy-start
  22.7 0.0 copy-start.1
  22.7 2.6 %collective-permute-start.7 = (bf16[208,512]{1,0:T(8,128)(2,1)S(1)}, bf16[208,512]{1,0:T(8,128)(2,1)S(1)}, u32[]{:S(2)}, u32[]{:S(2)}) collective-permute-start(bf16[208,512]{1,0:T(8,128)(2,1)S(1)} %far.1.refs_5_.refs_9_), channel_id=1, source_target_pairs={{0,8},{2,10},{4,12},{6,14},{8,0},{10,2},{12,4},{14,6},{1,9},{3,11}... | collective-permute-start | bytes 638984 | tf_op jit(solution)/shard_map/ppermute | solution.py:419
  25.4 4.1 %mean.6 = (bf16[144,128]{1,0:T(8,128)(2,1)S(1)}, bf16[144,128]{1,0:T(8,128)(2,1)S(1)}, bf16[144,128]{1,0:T(8,128)(2,1)S(1)}) custom-call(s32[8,1,1280]{2,1,0:T(1,128)S(1)} %get-tuple-element.43.refs_0_.refs_6_, f32[12288,1,128]{2,1,0:T(1,128)S(1)} %bitcast.9, bf16[160,128]{1,0:T(8,128)(2,1)S(1)} %collective-permute-done.4.refs_1_.refs_2_, ...), custom_call_target="tpu_custom_call" | custom-call | flops 6600000000 | tf_op jit(solution)/shard_map/mean/pallas_call | solution.py:454
  29.5 1.5 %collective-permute-start.10 = (bf16[144,128]{1,0:T(8,128)(2,1)S(1)}, bf16[144,128]{1,0:T(8,128)(2,1)S(1)}, u32[]{:S(2)}, u32[]{:S(2)}) collective-permute-start(bf16[144,128]{1,0:T(8,128)(2,1)S(1)} %get-tuple-element.59), channel_id=1, source_target_pairs={{0,6},{2,4},{4,2},{6,0},{8,14},{10,12},{12,10},{14,8},{1,7},{3,5},... | collective-permute-start | bytes 110600 | tf_op jit(solution)/shard_map/ppermute | solution.py:419
  30.9 1.4 %collective-permute-start.8 = (bf16[144,128]{1,0:T(8,128)(2,1)S(1)}, bf16[144,128]{1,0:T(8,128)(2,1)S(1)}, u32[]{:S(2)}, u32[]{:S(2)}) collective-permute-start(bf16[144,128]{1,0:T(8,128)(2,1)S(1)} %get-tuple-element.57), channel_id=1, source_target_pairs={{0,4},{2,6},{4,0},{6,2},{8,12},{10,14},{12,8},{14,10},{1,5},{3,7},... | collective-permute-start | bytes 110600 | tf_op jit(solution)/shard_map/ppermute | solution.py:419
  32.3 0.9 %collective-permute-start.9 = (bf16[144,128]{1,0:T(8,128)(2,1)S(1)}, bf16[144,128]{1,0:T(8,128)(2,1)S(1)}, u32[]{:S(2)}, u32[]{:S(2)}) collective-permute-start(bf16[144,128]{1,0:T(8,128)(2,1)S(1)} %get-tuple-element.58), channel_id=1, source_target_pairs={{0,2},{2,0},{4,6},{6,4},{8,10},{10,8},{12,14},{14,12},{1,3},{3,1},... | collective-permute-start | bytes 110600 | tf_op jit(solution)/shard_map/ppermute | solution.py:419
  33.2 0.0 copy-done
  33.2 0.0 copy-done.1
  33.2 2.3 %mean.7 = (bf16[144,128]{1,0:T(8,128)(2,1)S(1)}, bf16[256,768]{1,0:T(8,128)(2,1)S(1)}) custom-call(bf16[512,512]{1,0:T(8,128)(2,1)S(1)} %copy-done, bf16[512,512]{1,0:T(8,128)(2,1)S(1)} %copy-done.1, bf16[176,512]{1,0:T(8,128)(2,1)S(1)} %collective-permute-done.refs_1_.refs_0_.refs_2_, bf16[176,512]{1,0:T(8,128)(2,1)S(1)} %collective-permute-done.1.refs_2_.refs_1_.refs_3_, ...), custom_call_target="tpu_custom_call" | custom-call | tf_op jit(solution)/shard_map/mean/pallas_call | solution.py:454
  35.5 0.4 collective-permute-done.10.refs_2_
  35.9 0.0 collective-permute-done.8.refs_0_
  35.9 0.4 collective-permute-done.9.refs_1_
  36.3 0.4 near.1.refs_1_
  36.7 0.0 collective-permute-done.7.refs_2_.refs_0_
  36.7 0.2 hidden.1.refs_1_
  36.9 0.1 collective-permute-start.11
  37.0 0.9 %far_times.1 = (bf16[256,768]{1,0:T(8,128)(2,1)S(1)}, bf16[2,192,512]{2,1,0:T(8,128)(2,1)S(1)}, bf16[192,512]{1,0:T(8,128)(2,1)}) custom-call(bf16[208,512]{1,0:T(8,128)(2,1)S(1)} %collective-permute-done.7.refs_2_.refs_0_, bf16[192,512]{1,0:T(8,128)(2,1)S(1)} %hidden.1.refs_1_, bf16[512,512]{1,0:T(8,128)(2,1)S(1)} %copy-done, bf16[512,512]{1,0:T(8,128)(2,1)S(1)} %copy-done.1), custom_call_target="tpu_custom_call" | custom-call | flops 1100000000 | tf_op jit(solution)/shard_map/far_times/pallas_call | solution.py:454
  37.8 0.6 %collective-permute-done.11.refs_2_ = bf16[192,512]{1,0:T(8,128)(2,1)S(1)} collective-permute-done((bf16[192,512]{1,0:T(8,128)(2,1)S(1)}, bf16[192,512]{1,0:T(8,128)(2,1)S(1)}, u32[]{:S(2)}, u32[]{:S(2)}) %collective-permute-start.11) | collective-permute-done | bytes 196640 | tf_op jit(solution)/shard_map/ppermute | solution.py:419
  38.4 0.6 %far_share.1 = (bf16[64,512]{1,0:T(8,128)(2,1)S(1)}, bf16[64,512]{1,0:T(8,128)(2,1)S(1)}, bf16[64,512]{1,0:T(8,128)(2,1)S(1)}, bf16[64,512]{1,0:T(8,128)(2,1)S(1)}, bf16[768,512]{1,0:T(8,128)(2,1)S(1)}) custom-call(bf16[256,768]{1,0:T(8,128)(2,1)S(1)} %get-tuple-element.64.refs_0_, bf16[2,192,512]{2,1,0:T(8,128)(2,1)S(1)} %get-tuple-element.65.refs_1_, ...), custom_call_target="tpu_custom_call" | custom-call | flops 1100000000 | tf_op jit(solution)/shard_map/far_share/pallas_call | solution.py:454
  39.0 2.4 %collective-permute-start.13 = (bf16[64,512]{1,0:T(8,128)(2,1)S(1)}, bf16[64,512]{1,0:T(8,128)(2,1)S(1)}, u32[]{:S(2)}, u32[]{:S(2)}) collective-permute-start(bf16[64,512]{1,0:T(8,128)(2,1)S(1)} %get-tuple-element.70), channel_id=1, source_target_pairs={{0,6},{2,4},{4,2},{6,0},{8,14},{10,12},{12,10},{14,8},{1,7},{3,5},... | collective-permute-start | bytes 196616 | tf_op jit(solution)/shard_map/ppermute | solution.py:419
  41.4 0.0 collective-permute-start.15
  41.4 1.1 %collective-permute-start.16 = (bf16[64,512]{1,0:T(8,128)(2,1)S(1)}, bf16[64,512]{1,0:T(8,128)(2,1)S(1)}, u32[]{:S(2)}, u32[]{:S(2)}) collective-permute-start(bf16[64,512]{1,0:T(8,128)(2,1)S(1)} %get-tuple-element.74), channel_id=1, source_target_pairs={{0,2},{2,0},{4,6},{6,4},{8,10},{10,8},{12,14},{14,12},{1,3},{3,1},... | collective-permute-start | bytes 196616 | tf_op jit(solution)/shard_map/ppermute | solution.py:419
  42.5 0.4 near_share.1
  42.9 1.0 %collective-permute-start.12 = (bf16[128,512]{1,0:T(8,128)(2,1)S(1)}, bf16[128,512]{1,0:T(8,128)(2,1)S(1)}, u32[]{:S(2)}, u32[]{:S(2)}) collective-permute-start(bf16[128,512]{1,0:T(8,128)(2,1)S(1)} %get-tuple-element.67), channel_id=1, source_target_pairs={{0,2},{2,0},{4,6},{6,4},{8,10},{10,8},{12,14},{14,12},{1,3},{3,1},... | collective-permute-start | bytes 393224 | tf_op jit(solution)/shard_map/ppermute | solution.py:419
  43.9 1.0 %collective-permute-done.13.refs_3_.refs_0_ = bf16[64,512]{1,0:T(8,128)(2,1)S(1)} collective-permute-done((bf16[64,512]{1,0:T(8,128)(2,1)S(1)}, bf16[64,512]{1,0:T(8,128)(2,1)S(1)}, u32[]{:S(2)}, u32[]{:S(2)}) %collective-permute-start.13) | collective-permute-done | bytes 65568 | tf_op jit(solution)/shard_map/ppermute | solution.py:419
  44.9 0.8 %collective-permute-done.15.refs_1_ = bf16[64,512]{1,0:T(8,128)(2,1)S(1)} collective-permute-done((bf16[64,512]{1,0:T(8,128)(2,1)S(1)}, bf16[64,512]{1,0:T(8,128)(2,1)S(1)}, u32[]{:S(2)}, u32[]{:S(2)}) %collective-permute-start.15) | collective-permute-done | bytes 65568 | tf_op jit(solution)/shard_map/ppermute | solution.py:419
  45.7 0.7 %collective-permute-done.16.refs_2_ = bf16[64,512]{1,0:T(8,128)(2,1)S(1)} collective-permute-done((bf16[64,512]{1,0:T(8,128)(2,1)S(1)}, bf16[64,512]{1,0:T(8,128)(2,1)S(1)}, u32[]{:S(2)}, u32[]{:S(2)}) %collective-permute-start.16) | collective-permute-done | bytes 65568 | tf_op jit(solution)/shard_map/ppermute | solution.py:419
  46.4 0.0 copy-start.3
  46.4 1.6 %collective-permute-start.17 = (bf16[64,512]{1,0:T(8,128)(2,1)S(1)}, bf16[64,512]{1,0:T(8,128)(2,1)S(1)}, u32[]{:S(2)}, u32[]{:S(2)}) collective-permute-start(bf16[64,512]{1,0:T(8,128)(2,1)S(1)} %side_sum.1), channel_id=1, source_target_pairs={{0,8},{2,10},{4,12},{6,14},{8,0},{10,2},{12,4},{14,6},{1,9},{3,11}... | collective-permute-start | bytes 196616 | tf_op jit(solution)/shard_map/ppermute | solution.py:419
  48.1 0.5 collective-permute-done.12.refs_0_
  48.6 1.8 %collective-permute-start.14 = (bf16[64,512]{1,0:T(8,128)(2,1)S(1)}, bf16[64,512]{1,0:T(8,128)(2,1)S(1)}, u32[]{:S(2)}, u32[]{:S(2)}) collective-permute-start(bf16[64,512]{1,0:T(8,128)(2,1)S(1)} %get-tuple-element.71), channel_id=1, source_target_pairs={{0,4},{2,6},{4,0},{6,2},{8,12},{10,14},{12,8},{14,10},{1,5},{3,7},... | collective-permute-start | bytes 196616 | tf_op jit(solution)/shard_map/ppermute | solution.py:419
  50.4 1.4 %collective-permute-done.17.refs_3_ = bf16[64,512]{1,0:T(8,128)(2,1)S(1)} collective-permute-done((bf16[64,512]{1,0:T(8,128)(2,1)S(1)}, bf16[64,512]{1,0:T(8,128)(2,1)S(1)}, u32[]{:S(2)}, u32[]{:S(2)}) %collective-permute-start.17) | collective-permute-done | bytes 65568 | tf_op jit(solution)/shard_map/ppermute | solution.py:419
  51.8 1.2 %collective-permute-done.14.refs_1_ = bf16[64,512]{1,0:T(8,128)(2,1)S(1)} collective-permute-done((bf16[64,512]{1,0:T(8,128)(2,1)S(1)}, bf16[64,512]{1,0:T(8,128)(2,1)S(1)}, u32[]{:S(2)}, u32[]{:S(2)}) %collective-permute-start.14) | collective-permute-done | bytes 65568 | tf_op jit(solution)/shard_map/ppermute | solution.py:419
  52.9 0.0 copy-done.3
  52.9 0.7 %seeds.1 = bf16[64,512]{1,0:T(8,128)(2,1)} custom-call(f32[1,512]{1,0:T(1,128)S(1)} %bitcast.12, bf16[64,512]{1,0:T(8,128)(2,1)S(1)} %collective-permute-done.14.refs_1_, bf16[64,512]{1,0:T(8,128)(2,1)S(1)} %get-tuple-element.72.refs_2_, bf16[64,512]{1,0:T(8,128)(2,1)S(1)} %collective-permute-done.17.refs_3_), custom_call_target="tpu_custom_call" | custom-call | flops 1100000000 | tf_op jit(solution)/shard_map/seeds/pallas_call | solution.py:454
  (3 shorter events, 0.1 us)
Async XLA Ops:
  2.5 12.3 %collective-permute-start = (bf16[176,512]{1,0:T(8,128)(2,1)S(1)}, bf16[176,512]{1,0:T(8,128)(2,1)S(1)}, u32[]{:S(2)}, u32[]{:S(2)}) collective-permute-start(bf16[176,512]{1,0:T(8,128)(2,1)S(1)} %get-tuple-element.39), channel_id=1, source_target_pairs={{0,6},{2,4},{4,2},{6,0},{8,14},{10,12},{12,10},{14,8},{1,7},{3,5},... | collective-permute-start | bytes 540680 | tf_op jit(solution)/shard_map/ppermute | solution.py:419
  6.5 8.6 %collective-permute-start.1 = (bf16[176,512]{1,0:T(8,128)(2,1)S(1)}, bf16[176,512]{1,0:T(8,128)(2,1)S(1)}, u32[]{:S(2)}, u32[]{:S(2)}) collective-permute-start(bf16[176,512]{1,0:T(8,128)(2,1)S(1)} %get-tuple-element.40), channel_id=1, source_target_pairs={{0,4},{2,6},{4,0},{6,2},{8,12},{10,14},{12,8},{14,10},{1,5},{3,7},... | collective-permute-start | bytes 540680 | tf_op jit(solution)/shard_map/ppermute | solution.py:419
  7.0 8.2 %collective-permute-start.2 = (bf16[176,512]{1,0:T(8,128)(2,1)S(1)}, bf16[176,512]{1,0:T(8,128)(2,1)S(1)}, u32[]{:S(2)}, u32[]{:S(2)}) collective-permute-start(bf16[176,512]{1,0:T(8,128)(2,1)S(1)} %get-tuple-element.41), channel_id=1, source_target_pairs={{0,2},{2,0},{4,6},{6,4},{8,10},{10,8},{12,14},{14,12},{1,3},{3,1},... | collective-permute-start | bytes 540680 | tf_op jit(solution)/shard_map/ppermute | solution.py:419
  14.1 4.7 %copy-start.2 = (f32[512]{0:T(512)S(1)}, f32[512]{0:T(512)}, u32[]{:S(2)}) copy-start(f32[512]{0:T(512)} %param.18) | copy-start | bytes 6148
  15.2 3.6 %collective-permute-start.6 = (bf16[4,96,512]{2,1,0:T(8,128)(2,1)S(1)}, bf16[4,96,512]{2,1,0:T(8,128)(2,1)S(1)}, u32[]{:S(2)}, u32[]{:S(2)}) collective-permute-start(bf16[4,96,512]{2,1,0:T(8,128)(2,1)S(1)} %get-tuple-element.51), channel_id=1, source_target_pairs={{0,1},{1,0},{2,3},{3,2},{4,5},{5,4},{6,7},{7,6},{8,9},{9,8},{10,11... | collective-permute-start | bytes 1179656 | tf_op jit(solution)/shard_map/ppermute | solution.py:419
  15.3 6.2 %collective-permute-start.3 = (bf16[160,128]{1,0:T(8,128)(2,1)S(1)}, bf16[160,128]{1,0:T(8,128)(2,1)S(1)}, u32[]{:S(2)}, u32[]{:S(2)}) collective-permute-start(bf16[160,128]{1,0:T(8,128)(2,1)S(1)} %get-tuple-element.48), channel_id=1, source_target_pairs={{0,6},{2,4},{4,2},{6,0},{8,14},{10,12},{12,10},{14,8},{1,7},{3,5},... | collective-permute-start | bytes 122888 | tf_op jit(solution)/shard_map/ppermute | solution.py:419
  17.9 4.0 %collective-permute-start.4 = (bf16[160,128]{1,0:T(8,128)(2,1)S(1)}, bf16[160,128]{1,0:T(8,128)(2,1)S(1)}, u32[]{:S(2)}, u32[]{:S(2)}) collective-permute-start(bf16[160,128]{1,0:T(8,128)(2,1)S(1)} %get-tuple-element.49), channel_id=1, source_target_pairs={{0,4},{2,6},{4,0},{6,2},{8,12},{10,14},{12,8},{14,10},{1,5},{3,7},... | collective-permute-start | bytes 122888 | tf_op jit(solution)/shard_map/ppermute | solution.py:419
  18.3 4.0 %collective-permute-start.5 = (bf16[160,128]{1,0:T(8,128)(2,1)S(1)}, bf16[160,128]{1,0:T(8,128)(2,1)S(1)}, u32[]{:S(2)}, u32[]{:S(2)}) collective-permute-start(bf16[160,128]{1,0:T(8,128)(2,1)S(1)} %get-tuple-element.50), channel_id=1, source_target_pairs={{0,2},{2,0},{4,6},{6,4},{8,10},{10,8},{12,14},{14,12},{1,3},{3,1},... | collective-permute-start | bytes 122888 | tf_op jit(solution)/shard_map/ppermute | solution.py:419
  22.7 10.5 %copy-start = (bf16[512,512]{1,0:T(8,128)(2,1)S(1)}, bf16[512,512]{1,0:T(8,128)(2,1)}, u32[]{:S(2)}) copy-start(bf16[512,512]{1,0:T(8,128)(2,1)} %refs_3_.5) | copy-start | bytes 1572868
  22.7 10.5 %copy-start.1 = (bf16[512,512]{1,0:T(8,128)(2,1)S(1)}, bf16[512,512]{1,0:T(8,128)(2,1)}, u32[]{:S(2)}) copy-start(bf16[512,512]{1,0:T(8,128)(2,1)} %refs_4_.3) | copy-start | bytes 1572868
  22.7 13.9 %collective-permute-start.7 = (bf16[208,512]{1,0:T(8,128)(2,1)S(1)}, bf16[208,512]{1,0:T(8,128)(2,1)S(1)}, u32[]{:S(2)}, u32[]{:S(2)}) collective-permute-start(bf16[208,512]{1,0:T(8,128)(2,1)S(1)} %far.1.refs_5_.refs_9_), channel_id=1, source_target_pairs={{0,8},{2,10},{4,12},{6,14},{8,0},{10,2},{12,4},{14,6},{1,9},{3,11}... | collective-permute-start | bytes 638984 | tf_op jit(solution)/shard_map/ppermute | solution.py:419
  29.5 6.5 %collective-permute-start.10 = (bf16[144,128]{1,0:T(8,128)(2,1)S(1)}, bf16[144,128]{1,0:T(8,128)(2,1)S(1)}, u32[]{:S(2)}, u32[]{:S(2)}) collective-permute-start(bf16[144,128]{1,0:T(8,128)(2,1)S(1)} %get-tuple-element.59), channel_id=1, source_target_pairs={{0,6},{2,4},{4,2},{6,0},{8,14},{10,12},{12,10},{14,8},{1,7},{3,5},... | collective-permute-start | bytes 110600 | tf_op jit(solution)/shard_map/ppermute | solution.py:419
  30.9 5.0 %collective-permute-start.8 = (bf16[144,128]{1,0:T(8,128)(2,1)S(1)}, bf16[144,128]{1,0:T(8,128)(2,1)S(1)}, u32[]{:S(2)}, u32[]{:S(2)}) collective-permute-start(bf16[144,128]{1,0:T(8,128)(2,1)S(1)} %get-tuple-element.57), channel_id=1, source_target_pairs={{0,4},{2,6},{4,0},{6,2},{8,12},{10,14},{12,8},{14,10},{1,5},{3,7},... | collective-permute-start | bytes 110600 | tf_op jit(solution)/shard_map/ppermute | solution.py:419
  32.3 4.0 %collective-permute-start.9 = (bf16[144,128]{1,0:T(8,128)(2,1)S(1)}, bf16[144,128]{1,0:T(8,128)(2,1)S(1)}, u32[]{:S(2)}, u32[]{:S(2)}) collective-permute-start(bf16[144,128]{1,0:T(8,128)(2,1)S(1)} %get-tuple-element.58), channel_id=1, source_target_pairs={{0,2},{2,0},{4,6},{6,4},{8,10},{10,8},{12,14},{14,12},{1,3},{3,1},... | collective-permute-start | bytes 110600 | tf_op jit(solution)/shard_map/ppermute | solution.py:419
  36.9 1.5 %collective-permute-start.11 = (bf16[192,512]{1,0:T(8,128)(2,1)S(1)}, bf16[192,512]{1,0:T(8,128)(2,1)S(1)}, u32[]{:S(2)}, u32[]{:S(2)}) collective-permute-start(bf16[192,512]{1,0:T(8,128)(2,1)S(1)} %hidden.1.refs_1_), channel_id=1, source_target_pairs={{0,1},{1,0},{2,3},{3,2},{4,5},{5,4},{6,7},{7,6},{8,9},{9,8},{10,11... | collective-permute-start | bytes 589832 | tf_op jit(solution)/shard_map/ppermute | solution.py:419
  39.0 5.9 %collective-permute-start.13 = (bf16[64,512]{1,0:T(8,128)(2,1)S(1)}, bf16[64,512]{1,0:T(8,128)(2,1)S(1)}, u32[]{:S(2)}, u32[]{:S(2)}) collective-permute-start(bf16[64,512]{1,0:T(8,128)(2,1)S(1)} %get-tuple-element.70), channel_id=1, source_target_pairs={{0,6},{2,4},{4,2},{6,0},{8,14},{10,12},{12,10},{14,8},{1,7},{3,5},... | collective-permute-start | bytes 196616 | tf_op jit(solution)/shard_map/ppermute | solution.py:419
  41.4 4.3 %collective-permute-start.15 = (bf16[64,512]{1,0:T(8,128)(2,1)S(1)}, bf16[64,512]{1,0:T(8,128)(2,1)S(1)}, u32[]{:S(2)}, u32[]{:S(2)}) collective-permute-start(bf16[64,512]{1,0:T(8,128)(2,1)S(1)} %get-tuple-element.73), channel_id=1, source_target_pairs={{0,4},{2,6},{4,0},{6,2},{8,12},{10,14},{12,8},{14,10},{1,5},{3,7},... | collective-permute-start | bytes 196616 | tf_op jit(solution)/shard_map/ppermute | solution.py:419
  41.4 5.0 %collective-permute-start.16 = (bf16[64,512]{1,0:T(8,128)(2,1)S(1)}, bf16[64,512]{1,0:T(8,128)(2,1)S(1)}, u32[]{:S(2)}, u32[]{:S(2)}) collective-permute-start(bf16[64,512]{1,0:T(8,128)(2,1)S(1)} %get-tuple-element.74), channel_id=1, source_target_pairs={{0,2},{2,0},{4,6},{6,4},{8,10},{10,8},{12,14},{14,12},{1,3},{3,1},... | collective-permute-start | bytes 196616 | tf_op jit(solution)/shard_map/ppermute | solution.py:419
  42.9 5.7 %collective-permute-start.12 = (bf16[128,512]{1,0:T(8,128)(2,1)S(1)}, bf16[128,512]{1,0:T(8,128)(2,1)S(1)}, u32[]{:S(2)}, u32[]{:S(2)}) collective-permute-start(bf16[128,512]{1,0:T(8,128)(2,1)S(1)} %get-tuple-element.67), channel_id=1, source_target_pairs={{0,2},{2,0},{4,6},{6,4},{8,10},{10,8},{12,14},{14,12},{1,3},{3,1},... | collective-permute-start | bytes 393224 | tf_op jit(solution)/shard_map/ppermute | solution.py:419
  46.4 6.5 %copy-start.3 = (f32[512]{0:T(512)S(1)}, f32[512]{0:T(512)}, u32[]{:S(2)}) copy-start(f32[512]{0:T(512)} %param.21) | copy-start | bytes 6148
  46.4 5.3 %collective-permute-start.17 = (bf16[64,512]{1,0:T(8,128)(2,1)S(1)}, bf16[64,512]{1,0:T(8,128)(2,1)S(1)}, u32[]{:S(2)}, u32[]{:S(2)}) collective-permute-start(bf16[64,512]{1,0:T(8,128)(2,1)S(1)} %side_sum.1), channel_id=1, source_target_pairs={{0,8},{2,10},{4,12},{6,14},{8,0},{10,2},{12,4},{14,6},{1,9},{3,11}... | collective-permute-start | bytes 196616 | tf_op jit(solution)/shard_map/ppermute | solution.py:419
  48.6 4.3 %collective-permute-start.14 = (bf16[64,512]{1,0:T(8,128)(2,1)S(1)}, bf16[64,512]{1,0:T(8,128)(2,1)S(1)}, u32[]{:S(2)}, u32[]{:S(2)}) collective-permute-start(bf16[64,512]{1,0:T(8,128)(2,1)S(1)} %get-tuple-element.71), channel_id=1, source_target_pairs={{0,4},{2,6},{4,0},{6,2},{8,12},{10,14},{12,8},{14,10},{1,5},{3,7},... | collective-permute-start | bytes 196616 | tf_op jit(solution)/shard_map/ppermute | solution.py:419

commit v17 on v15

--- a/solution.py
+++ b/solution.py
@@ -61,6 +61,7 @@
 
 
 def pack_kernel(
+    steps,
     n_feat,
     pcap,
     src_hbm,
@@ -108,7 +109,7 @@
     digits = jnp.concatenate([high, idx - high * 128], axis=1).astype(jnp.float32)
     weight = jnp.where(first_core, w_self_ref[...], w_nbr_ref[...])
     copies[0].wait()
-    for s, parcel_ref in enumerate(reversed(parcel_refs)):
+    for s, parcel_ref in zip(steps, parcel_refs):
         sides = []
         for step in (s, s ^ half):
             at = pl.multiple_of(jnp.bitwise_xor(feat_pos, step) * (2 * pcap), LANES)
@@ -130,10 +131,12 @@
     lax.fori_loop(0, nodes // width, turn, 0)
 
 
-def mean_kernel(chosen, packed, fanout, pcap, fslice, before, n_before, *refs):
+def mean_kernel(chosen, packed, fanout, pcap, fslice, turns, before, n_before, *refs):
     count = len(chosen)
     before_in, refs = refs[: n_before[0]], refs[n_before[0] :]
-    nbr_any, table_ref, *refs = refs
+    nbr_any, *refs = refs
+    if not turns:
+        table_ref, *refs = refs
     out_ref, total, nbr_ref, live_ref, sems = refs[-5:]
     refs = refs[:-5]
     before_out = refs[len(refs) - n_before[1] :]
@@ -141,6 +144,7 @@
     chunk_refs, tagged_refs = refs[len(refs) - count :], refs[: len(refs) - count]
     feat_pos = lax.axis_index("feat")
     words = fanout // packed
+    size = 16 if len(tagged_refs) or pcap % 64 else 64
     stride = -(-pcap // LANES) * LANES
     length = words * stride
     copies = [
@@ -157,6 +161,8 @@
         live_ref[i] = live_rows(ref)
     if before is not None:
         before(*before_in, *before_out)
+    if turns:
+        table_ref = before_out[0].reshape(before_out[0].shape[0], 1, LANES)
     for copy in copies:
         copy.wait()
 
@@ -164,10 +170,10 @@
         first = i * length
 
         def group(g, inner):
-            at = pl.multiple_of(g * 16, 16)
+            at = pl.multiple_of(g * size, 16)
             start = first + at
             sums = []
-            for u in range(16):
+            for u in range(size):
                 names = [nbr_ref[start + (k * stride + u)] for k in range(words)]
                 if packed == 2:
                     names = [
@@ -181,11 +187,13 @@
                         [rows[-1]] if len(rows) % 2 else []
                     )
                 sums.append(rows[0])
-            for u, row in enumerate(sums):
-                total[pl.ds(at + u, 1), :] = row
+                if len(sums) == 16:
+                    for v, row in enumerate(sums):
+                        total[pl.ds(at + (u - 15 + v), 1), :] = row
+                    sums = []
             return inner
 
-        lax.fori_loop(0, lax.div(live_ref[i] + 15, 16), group, 0)
+        lax.fori_loop(0, lax.div(live_ref[i] + size - 1, size), group, 0)
         mean = total[...] / fanout
         if folds(fslice, pcap):
             part = pcap // 4
@@ -413,7 +421,8 @@
 ):
     n_feat = lax.axis_size("feat")
     half = n_feat // 2
-    steps = range(half - 1, -1, -1)
+    first = half // 2
+    steps = [first, *(s for s in range(half - 1, -1, -1) if s != first)]
     fslice, nodes = src_feats.shape
     fanout_one, pcap = nbr_one.shape[2:]
     width = w1_self.shape[1]
@@ -453,7 +462,7 @@
     packed = 2 if fanout_one % 2 == 0 and nodes <= 1 << 16 else 1
     words = (n_feat, 1, fanout_one // packed * (-(-pcap // LANES) * LANES))
     *parcels, picks, feats = call(
-        functools.partial(pack_kernel, n_feat, pcap),
+        functools.partial(pack_kernel, steps, n_feat, pcap),
         "pack",
         [((parcel_rows(fslice, n_idx), width), bf16)] * half
         + [(words, jnp.int32), ((fslice, nodes), bf16)],
@@ -470,20 +479,11 @@
         limit=32 * MIB,
     )
     arrived = send(parcels)
-    (table,) = call(
-        turn_kernel,
-        "turn",
-        [((nodes, LANES), jnp.float32)],
-        [vmem],
-        (feats,),
-        limit=table_bytes + 12 * MIB,
-        cost_us=3,
-    )
-    table = table.reshape(nodes, 1, LANES)
     chunk_shape = (pcap // 4 * 3, LANES) if folds(fslice, pcap) else (pcap, fslice)
 
-    def means(chosen, tagged=(), after=(), before=None, ins=(), outs=()):
+    def means(chosen, tagged=(), after=(), before=None, ins=(), outs=(), table=None):
         count = len(chosen)
+        tables = () if table is None else (table,)
         return call(
             functools.partial(
                 mean_kernel,
@@ -492,13 +492,14 @@
                 fanout_one,
                 pcap,
                 fslice,
+                table is None,
                 before,
                 (len(ins), len(outs)),
             ),
             "mean",
             [(chunk_shape, bf16)] * count + list(outs),
-            [vmem] * len(ins) + [anywhere] + [vmem] * (1 + len(tagged)),
-            (*ins, picks, table, *tagged),
+            [vmem] * len(ins) + [anywhere] + [vmem] * (len(tables) + len(tagged)),
+            (*ins, picks, *tables, *tagged),
             after=after,
             scratch=[
                 pltpu.VMEM((count, *chunk_shape), bf16),
@@ -511,7 +512,13 @@
             cost_us=2 * count if count > 1 else 0,
         )
 
-    far_means = means([s + half for s in steps if s])
+    *far_means, table = means(
+        [s + half for s in steps if s],
+        before=turn_kernel,
+        ins=(feats,),
+        outs=[((nodes, LANES), jnp.float32)],
+    )
+    table = table.reshape(nodes, 1, LANES)
     tagged_shape = (chunk_shape[0] + TAG_ROWS, chunk_shape[1])
     halves, *tagged, live = call(
         functools.partial(halves_kernel, half),
@@ -529,6 +536,7 @@
     idx_rows = -(-half // 4) * n_idx
     far_own, w_nbr, pre, far_pre, idx_tags = means(
         [half],
+        table=table,
         before=functools.partial(own_kernel, half, n_idx),
         ins=(*arrived, other_halves, bias_one[None]),
         outs=[
@@ -547,11 +555,12 @@
     )
     cross_arrived = swap(cross, "feat", half)
     turned = [*steps[1:-1], steps[0]]
-    near_means = means(turned, [*far_arrived[1:], far_arrived[0]], (cross,))
+    near_means = means(turned, [*far_arrived[1:], far_arrived[0]], (cross,), table=table)
     near_arrived = send(near_means, turned)
     near_own, near_times = means(
         [0],
         [live],
+        table=table,
         after=(cross,),
         before=functools.partial(near_times_kernel, half, fslice, pcap, n_idx),
         ins=(w2_self, w2_nbr, *arrived),

time: 53.1 us -> 54.8 us (1.032)
  waiting for transfers between devices: 8.11 us -> 10.6 us
  Pallas kernels: 20 us -> 19.1 us
    ppermute x19, waiting for transfers between devices: 8.11 us -> 10.6 us  [swap(): return lax.ppermute(value, axis, [(i, i ^ step) for i in range(size)])]
    pallas_call x15 -> x14, Pallas kernels: 20 us -> 19.1 us  [call(): pl.pallas_call(wrapped, out_shape=tuple((jax.ShapeDtypeStruct(shape, dtyp...]
  transfers between devices with their start and end apart: 19 -> 19, of which waited for: 8 -> 9; matrix products, arithmetic and copies ran while one was open for 0% -> 0% of each run, Pallas kernels for 31% -> 28%
where the time goes in v17:
time: 54.8 us; the launch traced here: 54.5 us
  starting transfers between devices  23.3 us (43%)
  Pallas kernels  19.1 us (35%)
  waiting for transfers between devices  10.6 us (19%)
  between operations  1.48 us (3%)
    ppermute x19, starting transfers between devices, swap(): return lax.ppermute(value, axis, [(i, i ^ step) for i in range(size)])  23.3 us
    pallas_call x14, Pallas kernels, call(): pl.pallas_call(wrapped, out_shape=tuple((jax.ShapeDtypeStruct(shape, dtyp...  19.1 us
    ppermute x19, waiting for transfers between devices, swap(): return lax.ppermute(value, axis, [(i, i ^ step) for i in range(size)])  10.6 us
  transfers between devices with their start and end apart: 19, of which 9 were waited for; matrix products, arithmetic and copies ran while one was open for 0% of the time, Pallas kernels for 28%

profile of v17, /device:TPU:0, one launch (start us, length us, event | category | flops | bytes accessed | tf_op | source)
XLA Modules:
  0.0 54.5 jit_solution(3331840456515427073)
XLA Ops:
  0.6 1.8 %pack.1 = (bf16[176,512]{1,0:T(8,128)(2,1)S(1)}, bf16[176,512]{1,0:T(8,128)(2,1)S(1)}, bf16[176,512]{1,0:T(8,128)(2,1)S(1)}, bf16[176,512]{1,0:T(8,128)(2,1)S(1)...) custom-call(bf16[96,12288]{1,0:T(8,128)(2,1)} %refs_0_.3, s32[1,64]{1,0:T(1,128)} %bitcast.14, ...), custom_call_target="tpu_custom_call" | custom-call | flops 1100000000 | tf_op jit(solution)/shard_map/pack/pallas_call | solution.py:442
  2.5 3.1 %collective-permute-start = (bf16[176,512]{1,0:T(8,128)(2,1)S(1)}, bf16[176,512]{1,0:T(8,128)(2,1)S(1)}, u32[]{:S(2)}, u32[]{:S(2)}) collective-permute-start(bf16[176,512]{1,0:T(8,128)(2,1)S(1)} %get-tuple-element.39), channel_id=1, source_target_pairs={{0,4},{2,6},{4,0},{6,2},{8,12},{10,14},{12,8},{14,10},{1,5},{3,7},... | collective-permute-start | bytes 540680 | tf_op jit(solution)/shard_map/ppermute | solution.py:406
  5.6 1.4 %collective-permute-start.1 = (bf16[176,512]{1,0:T(8,128)(2,1)S(1)}, bf16[176,512]{1,0:T(8,128)(2,1)S(1)}, u32[]{:S(2)}, u32[]{:S(2)}) collective-permute-start(bf16[176,512]{1,0:T(8,128)(2,1)S(1)} %get-tuple-element.40), channel_id=1, source_target_pairs={{0,6},{2,4},{4,2},{6,0},{8,14},{10,12},{12,10},{14,8},{1,7},{3,5},... | collective-permute-start | bytes 540680 | tf_op jit(solution)/shard_map/ppermute | solution.py:406
  7.0 0.1 collective-permute-start.2
  7.1 6.2 %mean.4 = (bf16[144,128]{1,0:T(8,128)(2,1)S(1)}, bf16[144,128]{1,0:T(8,128)(2,1)S(1)}, bf16[144,128]{1,0:T(8,128)(2,1)S(1)}, f32[12288,128]{1,0:T(8,128)S(1)}) custom-call(bf16[96,12288]{1,0:T(8,128)(2,1)S(1)} %get-tuple-element.43.refs_0_, s32[8,1,1280]{2,1,0:T(1,128)S(1)} %get-tuple-element.44.refs_1_.refs_6_.refs_0_), custom_call_target="tpu_custom_call" | custom-call | flops 6600000000 | tf_op jit(solution)/shard_map/mean/pallas_call | solution.py:442
  13.3 0.0 copy-start.2
  14.0 0.0 collective-permute-done.refs_1_.refs_0_.refs_2_
  14.0 1.2 %collective-permute-done.1.refs_2_.refs_1_.refs_3_ = bf16[176,512]{1,0:T(8,128)(2,1)S(1)} collective-permute-done((bf16[176,512]{1,0:T(8,128)(2,1)S(1)}, bf16[176,512]{1,0:T(8,128)(2,1)S(1)}, u32[]{:S(2)}, u32[]{:S(2)}) %collective-permute-start.1) | collective-permute-done | bytes 180256 | tf_op jit(solution)/shard_map/ppermute | solution.py:406
  15.2 1.4 %collective-permute-done.2.refs_3_.refs_2_.refs_4_ = bf16[176,512]{1,0:T(8,128)(2,1)S(1)} collective-permute-done((bf16[176,512]{1,0:T(8,128)(2,1)S(1)}, bf16[176,512]{1,0:T(8,128)(2,1)S(1)}, u32[]{:S(2)}, u32[]{:S(2)}) %collective-permute-start.2) | collective-permute-done | bytes 180256 | tf_op jit(solution)/shard_map/ppermute | solution.py:406
  16.6 0.1 collective-permute-start.6
  16.7 1.6 %collective-permute-start.3 = (bf16[160,128]{1,0:T(8,128)(2,1)S(1)}, bf16[160,128]{1,0:T(8,128)(2,1)S(1)}, u32[]{:S(2)}, u32[]{:S(2)}) collective-permute-start(bf16[160,128]{1,0:T(8,128)(2,1)S(1)} %get-tuple-element.48), channel_id=1, source_target_pairs={{0,4},{2,6},{4,0},{6,2},{8,12},{10,14},{12,8},{14,10},{1,5},{3,7},... | collective-permute-start | bytes 122888 | tf_op jit(solution)/shard_map/ppermute | solution.py:406
  18.3 0.3 collective-permute-start.4
  18.6 1.6 %collective-permute-start.5 = (bf16[160,128]{1,0:T(8,128)(2,1)S(1)}, bf16[160,128]{1,0:T(8,128)(2,1)S(1)}, u32[]{:S(2)}, u32[]{:S(2)}) collective-permute-start(bf16[160,128]{1,0:T(8,128)(2,1)S(1)} %get-tuple-element.50), channel_id=1, source_target_pairs={{0,2},{2,0},{4,6},{6,4},{8,10},{10,8},{12,14},{14,12},{1,3},{3,1},... | collective-permute-start | bytes 122888 | tf_op jit(solution)/shard_map/ppermute | solution.py:406
  20.2 0.0 collective-permute-done.6.refs_4_
  20.3 0.0 copy-done.2
  20.3 2.6 %mean.5 = (bf16[144,128]{1,0:T(8,128)(2,1)S(1)}, bf16[4,96,512]{2,1,0:T(8,128)(2,1)S(1)}, f32[192,512]{1,0:T(8,128)S(1)}, f32[192,512]{1,0:T(8,128)S(1)}, bf16[16,512]{1,0:T(8,128)(2,1)S(1)}) custom-call(bf16[176,512]{1,0:T(8,128)(2,1)S(1)} %collective-permute-done.refs_1_.refs_0_.refs_2_, ...), custom_call_target="tpu_custom_call" | custom-call | tf_op jit(solution)/shard_map/mean/pallas_call | solution.py:442
  22.9 0.0 collective-permute-done.3.refs_0_.refs_4_
  22.9 0.4 collective-permute-done.4.refs_1_.refs_2_
  23.3 0.0 collective-permute-done.5.refs_2_.refs_3_
  23.3 0.4 far.1.refs_5_.refs_9_
  23.7 0.0 copy-start
  23.7 0.0 copy-start.1
  23.7 2.7 %collective-permute-start.7 = (bf16[208,512]{1,0:T(8,128)(2,1)S(1)}, bf16[208,512]{1,0:T(8,128)(2,1)S(1)}, u32[]{:S(2)}, u32[]{:S(2)}) collective-permute-start(bf16[208,512]{1,0:T(8,128)(2,1)S(1)} %far.1.refs_5_.refs_9_), channel_id=1, source_target_pairs={{0,8},{2,10},{4,12},{6,14},{8,0},{10,2},{12,4},{14,6},{1,9},{3,11}... | collective-permute-start | bytes 638984 | tf_op jit(solution)/shard_map/ppermute | solution.py:406
  26.4 3.8 %mean.6 = (bf16[144,128]{1,0:T(8,128)(2,1)S(1)}, bf16[144,128]{1,0:T(8,128)(2,1)S(1)}, bf16[144,128]{1,0:T(8,128)(2,1)S(1)}) custom-call(s32[8,1,1280]{2,1,0:T(1,128)S(1)} %get-tuple-element.44.refs_1_.refs_6_.refs_0_, f32[12288,1,128]{2,1,0:T(1,128)S(1)} %bitcast.8, bf16[160,128]{1,0:T(8,128)(2,1)S(1)} %collective-permute-done.4.refs_1_.refs_2_, ...), custom_call_target="tpu_custom_call" | custom-call | flops 6600000000 | tf_op jit(solution)/shard_map/mean/pallas_call | solution.py:442
  30.2 0.7 %collective-permute-start.10 = (bf16[144,128]{1,0:T(8,128)(2,1)S(1)}, bf16[144,128]{1,0:T(8,128)(2,1)S(1)}, u32[]{:S(2)}, u32[]{:S(2)}) collective-permute-start(bf16[144,128]{1,0:T(8,128)(2,1)S(1)} %get-tuple-element.60), channel_id=1, source_target_pairs={{0,4},{2,6},{4,0},{6,2},{8,12},{10,14},{12,8},{14,10},{1,5},{3,7},... | collective-permute-start | bytes 110600 | tf_op jit(solution)/shard_map/ppermute | solution.py:406
  30.9 1.4 %collective-permute-start.8 = (bf16[144,128]{1,0:T(8,128)(2,1)S(1)}, bf16[144,128]{1,0:T(8,128)(2,1)S(1)}, u32[]{:S(2)}, u32[]{:S(2)}) collective-permute-start(bf16[144,128]{1,0:T(8,128)(2,1)S(1)} %get-tuple-element.58), channel_id=1, source_target_pairs={{0,6},{2,4},{4,2},{6,0},{8,14},{10,12},{12,10},{14,8},{1,7},{3,5},... | collective-permute-start | bytes 110600 | tf_op jit(solution)/shard_map/ppermute | solution.py:406
  32.2 1.5 %collective-permute-start.9 = (bf16[144,128]{1,0:T(8,128)(2,1)S(1)}, bf16[144,128]{1,0:T(8,128)(2,1)S(1)}, u32[]{:S(2)}, u32[]{:S(2)}) collective-permute-start(bf16[144,128]{1,0:T(8,128)(2,1)S(1)} %get-tuple-element.59), channel_id=1, source_target_pairs={{0,2},{2,0},{4,6},{6,4},{8,10},{10,8},{12,14},{14,12},{1,3},{3,1},... | collective-permute-start | bytes 110600 | tf_op jit(solution)/shard_map/ppermute | solution.py:406
  33.7 0.0 copy-done
  33.7 0.0 copy-done.1
  33.7 1.2 %mean.7 = (bf16[144,128]{1,0:T(8,128)(2,1)S(1)}, bf16[256,768]{1,0:T(8,128)(2,1)S(1)}) custom-call(bf16[512,512]{1,0:T(8,128)(2,1)S(1)} %copy-done, bf16[512,512]{1,0:T(8,128)(2,1)S(1)} %copy-done.1, bf16[176,512]{1,0:T(8,128)(2,1)S(1)} %collective-permute-done.refs_1_.refs_0_.refs_2_, bf16[176,512]{1,0:T(8,128)(2,1)S(1)} %collective-permute-done.1.refs_2_.refs_1_.refs_3_, ...), custom_call_target="tpu_custom_call" | custom-call | tf_op jit(solution)/shard_map/mean/pallas_call | solution.py:442
  34.9 1.5 %collective-permute-done.10.refs_2_ = bf16[144,128]{1,0:T(8,128)(2,1)S(1)} collective-permute-done((bf16[144,128]{1,0:T(8,128)(2,1)S(1)}, bf16[144,128]{1,0:T(8,128)(2,1)S(1)}, u32[]{:S(2)}, u32[]{:S(2)}) %collective-permute-start.10) | collective-permute-done | bytes 36896 | tf_op jit(solution)/shard_map/ppermute | solution.py:406
  36.4 1.6 %collective-permute-done.8.refs_0_ = bf16[144,128]{1,0:T(8,128)(2,1)S(1)} collective-permute-done((bf16[144,128]{1,0:T(8,128)(2,1)S(1)}, bf16[144,128]{1,0:T(8,128)(2,1)S(1)}, u32[]{:S(2)}, u32[]{:S(2)}) %collective-permute-start.8) | collective-permute-done | bytes 36896 | tf_op jit(solution)/shard_map/ppermute | solution.py:406
  38.0 0.0 collective-permute-done.9.refs_1_
  38.0 0.4 near.1.refs_1_
  38.3 0.0 collective-permute-done.7.refs_2_.refs_0_
  38.3 0.2 hidden.1.refs_1_
  38.5 0.2 collective-permute-start.11
  38.7 0.9 %far_times.1 = (bf16[256,768]{1,0:T(8,128)(2,1)S(1)}, bf16[2,192,512]{2,1,0:T(8,128)(2,1)S(1)}, bf16[192,512]{1,0:T(8,128)(2,1)}) custom-call(bf16[208,512]{1,0:T(8,128)(2,1)S(1)} %collective-permute-done.7.refs_2_.refs_0_, bf16[192,512]{1,0:T(8,128)(2,1)S(1)} %hidden.1.refs_1_, bf16[512,512]{1,0:T(8,128)(2,1)S(1)} %copy-done, bf16[512,512]{1,0:T(8,128)(2,1)S(1)} %copy-done.1), custom_call_target="tpu_custom_call" | custom-call | flops 1100000000 | tf_op jit(solution)/shard_map/far_times/pallas_call | solution.py:442
  39.5 0.5 collective-permute-done.11.refs_2_
  40.0 0.6 %far_share.1 = (bf16[64,512]{1,0:T(8,128)(2,1)S(1)}, bf16[64,512]{1,0:T(8,128)(2,1)S(1)}, bf16[64,512]{1,0:T(8,128)(2,1)S(1)}, bf16[64,512]{1,0:T(8,128)(2,1)S(1)}, bf16[768,512]{1,0:T(8,128)(2,1)S(1)}) custom-call(bf16[256,768]{1,0:T(8,128)(2,1)S(1)} %get-tuple-element.65.refs_0_, bf16[2,192,512]{2,1,0:T(8,128)(2,1)S(1)} %get-tuple-element.66.refs_1_, ...), custom_call_target="tpu_custom_call" | custom-call | flops 1100000000 | tf_op jit(solution)/shard_map/far_share/pallas_call | solution.py:442
  40.6 0.1 collective-permute-start.15
  40.7 1.8 %collective-permute-start.16 = (bf16[64,512]{1,0:T(8,128)(2,1)S(1)}, bf16[64,512]{1,0:T(8,128)(2,1)S(1)}, u32[]{:S(2)}, u32[]{:S(2)}) collective-permute-start(bf16[64,512]{1,0:T(8,128)(2,1)S(1)} %get-tuple-element.73), channel_id=1, source_target_pairs={{0,6},{2,4},{4,2},{6,0},{8,14},{10,12},{12,10},{14,8},{1,7},{3,5},... | collective-permute-start | bytes 196616 | tf_op jit(solution)/shard_map/ppermute | solution.py:406
  42.5 1.6 %collective-permute-start.17 = (bf16[64,512]{1,0:T(8,128)(2,1)S(1)}, bf16[64,512]{1,0:T(8,128)(2,1)S(1)}, u32[]{:S(2)}, u32[]{:S(2)}) collective-permute-start(bf16[64,512]{1,0:T(8,128)(2,1)S(1)} %get-tuple-element.74), channel_id=1, source_target_pairs={{0,2},{2,0},{4,6},{6,4},{8,10},{10,8},{12,14},{14,12},{1,3},{3,1},... | collective-permute-start | bytes 196616 | tf_op jit(solution)/shard_map/ppermute | solution.py:406
  44.2 0.4 near_share.1
  44.6 0.0 copy-start.3
  44.6 0.1 collective-permute-start.12
  44.7 1.8 %collective-permute-start.13 = (bf16[64,512]{1,0:T(8,128)(2,1)S(1)}, bf16[64,512]{1,0:T(8,128)(2,1)S(1)}, u32[]{:S(2)}, u32[]{:S(2)}) collective-permute-start(bf16[64,512]{1,0:T(8,128)(2,1)S(1)} %get-tuple-element.69), channel_id=1, source_target_pairs={{0,6},{2,4},{4,2},{6,0},{8,14},{10,12},{12,10},{14,8},{1,7},{3,5},... | collective-permute-start | bytes 196616 | tf_op jit(solution)/shard_map/ppermute | solution.py:406
  46.5 0.0 collective-permute-done.15.refs_0_
  46.5 1.6 %collective-permute-start.14 = (bf16[64,512]{1,0:T(8,128)(2,1)S(1)}, bf16[64,512]{1,0:T(8,128)(2,1)S(1)}, u32[]{:S(2)}, u32[]{:S(2)}) collective-permute-start(bf16[64,512]{1,0:T(8,128)(2,1)S(1)} %get-tuple-element.70), channel_id=1, source_target_pairs={{0,2},{2,0},{4,6},{6,4},{8,10},{10,8},{12,14},{14,12},{1,3},{3,1},... | collective-permute-start | bytes 196616 | tf_op jit(solution)/shard_map/ppermute | solution.py:406
  48.1 0.0 collective-permute-done.16.refs_1_
  48.1 0.0 collective-permute-done.17.refs_2_
  48.2 1.6 %collective-permute-start.18 = (bf16[64,512]{1,0:T(8,128)(2,1)S(1)}, bf16[64,512]{1,0:T(8,128)(2,1)S(1)}, u32[]{:S(2)}, u32[]{:S(2)}) collective-permute-start(bf16[64,512]{1,0:T(8,128)(2,1)S(1)} %side_sum.1), channel_id=1, source_target_pairs={{0,8},{2,10},{4,12},{6,14},{8,0},{10,2},{12,4},{14,6},{1,9},{3,11}... | collective-permute-start | bytes 196616 | tf_op jit(solution)/shard_map/ppermute | solution.py:406
  49.8 0.0 collective-permute-done.12.refs_1_
  49.8 0.1 collective-permute-done.13.refs_2_
  49.9 0.9 %collective-permute-done.14.refs_3_ = bf16[64,512]{1,0:T(8,128)(2,1)S(1)} collective-permute-done((bf16[64,512]{1,0:T(8,128)(2,1)S(1)}, bf16[64,512]{1,0:T(8,128)(2,1)S(1)}, u32[]{:S(2)}, u32[]{:S(2)}) %collective-permute-start.14) | collective-permute-done | bytes 65568 | tf_op jit(solution)/shard_map/ppermute | solution.py:406
  50.7 3.1 %collective-permute-done.18.refs_5_ = bf16[64,512]{1,0:T(8,128)(2,1)S(1)} collective-permute-done((bf16[64,512]{1,0:T(8,128)(2,1)S(1)}, bf16[64,512]{1,0:T(8,128)(2,1)S(1)}, u32[]{:S(2)}, u32[]{:S(2)}) %collective-permute-start.18) | collective-permute-done | bytes 65568 | tf_op jit(solution)/shard_map/ppermute | solution.py:406
  53.8 0.0 copy-done.3
  53.8 0.7 %seeds.1 = bf16[64,512]{1,0:T(8,128)(2,1)} custom-call(f32[1,512]{1,0:T(1,128)S(1)} %bitcast.11, bf16[64,512]{1,0:T(8,128)(2,1)S(1)} %collective-permute-done.12.refs_1_, bf16[64,512]{1,0:T(8,128)(2,1)S(1)} %collective-permute-done.13.refs_2_, bf16[64,512]{1,0:T(8,128)(2,1)S(1)} %collective-permute-done.14.refs_3_, ...), custom_call_target="tpu_custom_call" | custom-call | flops 1100000000 | tf_op jit(solution)/shard_map/seeds/pallas_call | solution.py:442
  (2 shorter events, 0.1 us)
Async XLA Ops:
  2.5 11.5 %collective-permute-start = (bf16[176,512]{1,0:T(8,128)(2,1)S(1)}, bf16[176,512]{1,0:T(8,128)(2,1)S(1)}, u32[]{:S(2)}, u32[]{:S(2)}) collective-permute-start(bf16[176,512]{1,0:T(8,128)(2,1)S(1)} %get-tuple-element.39), channel_id=1, source_target_pairs={{0,4},{2,6},{4,0},{6,2},{8,12},{10,14},{12,8},{14,10},{1,5},{3,7},... | collective-permute-start | bytes 540680 | tf_op jit(solution)/shard_map/ppermute | solution.py:406
  5.6 9.6 %collective-permute-start.1 = (bf16[176,512]{1,0:T(8,128)(2,1)S(1)}, bf16[176,512]{1,0:T(8,128)(2,1)S(1)}, u32[]{:S(2)}, u32[]{:S(2)}) collective-permute-start(bf16[176,512]{1,0:T(8,128)(2,1)S(1)} %get-tuple-element.40), channel_id=1, source_target_pairs={{0,6},{2,4},{4,2},{6,0},{8,14},{10,12},{12,10},{14,8},{1,7},{3,5},... | collective-permute-start | bytes 540680 | tf_op jit(solution)/shard_map/ppermute | solution.py:406
  7.0 9.6 %collective-permute-start.2 = (bf16[176,512]{1,0:T(8,128)(2,1)S(1)}, bf16[176,512]{1,0:T(8,128)(2,1)S(1)}, u32[]{:S(2)}, u32[]{:S(2)}) collective-permute-start(bf16[176,512]{1,0:T(8,128)(2,1)S(1)} %get-tuple-element.41), channel_id=1, source_target_pairs={{0,2},{2,0},{4,6},{6,4},{8,10},{10,8},{12,14},{14,12},{1,3},{3,1},... | collective-permute-start | bytes 540680 | tf_op jit(solution)/shard_map/ppermute | solution.py:406
  13.3 6.9 %copy-start.2 = (f32[512]{0:T(512)S(1)}, f32[512]{0:T(512)}, u32[]{:S(2)}) copy-start(f32[512]{0:T(512)} %param.18) | copy-start | bytes 6148
  16.6 3.6 %collective-permute-start.6 = (bf16[4,96,512]{2,1,0:T(8,128)(2,1)S(1)}, bf16[4,96,512]{2,1,0:T(8,128)(2,1)S(1)}, u32[]{:S(2)}, u32[]{:S(2)}) collective-permute-start(bf16[4,96,512]{2,1,0:T(8,128)(2,1)S(1)} %get-tuple-element.51), channel_id=1, source_target_pairs={{0,1},{1,0},{2,3},{3,2},{4,5},{5,4},{6,7},{7,6},{8,9},{9,8},{10,11... | collective-permute-start | bytes 1179656 | tf_op jit(solution)/shard_map/ppermute | solution.py:406
  16.7 6.2 %collective-permute-start.3 = (bf16[160,128]{1,0:T(8,128)(2,1)S(1)}, bf16[160,128]{1,0:T(8,128)(2,1)S(1)}, u32[]{:S(2)}, u32[]{:S(2)}) collective-permute-start(bf16[160,128]{1,0:T(8,128)(2,1)S(1)} %get-tuple-element.48), channel_id=1, source_target_pairs={{0,4},{2,6},{4,0},{6,2},{8,12},{10,14},{12,8},{14,10},{1,5},{3,7},... | collective-permute-start | bytes 122888 | tf_op jit(solution)/shard_map/ppermute | solution.py:406
  18.3 4.9 %collective-permute-start.4 = (bf16[160,128]{1,0:T(8,128)(2,1)S(1)}, bf16[160,128]{1,0:T(8,128)(2,1)S(1)}, u32[]{:S(2)}, u32[]{:S(2)}) collective-permute-start(bf16[160,128]{1,0:T(8,128)(2,1)S(1)} %get-tuple-element.49), channel_id=1, source_target_pairs={{0,6},{2,4},{4,2},{6,0},{8,14},{10,12},{12,10},{14,8},{1,7},{3,5},... | collective-permute-start | bytes 122888 | tf_op jit(solution)/shard_map/ppermute | solution.py:406
  18.6 4.7 %collective-permute-start.5 = (bf16[160,128]{1,0:T(8,128)(2,1)S(1)}, bf16[160,128]{1,0:T(8,128)(2,1)S(1)}, u32[]{:S(2)}, u32[]{:S(2)}) collective-permute-start(bf16[160,128]{1,0:T(8,128)(2,1)S(1)} %get-tuple-element.50), channel_id=1, source_target_pairs={{0,2},{2,0},{4,6},{6,4},{8,10},{10,8},{12,14},{14,12},{1,3},{3,1},... | collective-permute-start | bytes 122888 | tf_op jit(solution)/shard_map/ppermute | solution.py:406
  23.7 10.0 %copy-start = (bf16[512,512]{1,0:T(8,128)(2,1)S(1)}, bf16[512,512]{1,0:T(8,128)(2,1)}, u32[]{:S(2)}) copy-start(bf16[512,512]{1,0:T(8,128)(2,1)} %refs_3_.5) | copy-start | bytes 1572868
  23.7 10.0 %copy-start.1 = (bf16[512,512]{1,0:T(8,128)(2,1)S(1)}, bf16[512,512]{1,0:T(8,128)(2,1)}, u32[]{:S(2)}) copy-start(bf16[512,512]{1,0:T(8,128)(2,1)} %refs_4_.3) | copy-start | bytes 1572868
  23.7 14.6 %collective-permute-start.7 = (bf16[208,512]{1,0:T(8,128)(2,1)S(1)}, bf16[208,512]{1,0:T(8,128)(2,1)S(1)}, u32[]{:S(2)}, u32[]{:S(2)}) collective-permute-start(bf16[208,512]{1,0:T(8,128)(2,1)S(1)} %far.1.refs_5_.refs_9_), channel_id=1, source_target_pairs={{0,8},{2,10},{4,12},{6,14},{8,0},{10,2},{12,4},{14,6},{1,9},{3,11}... | collective-permute-start | bytes 638984 | tf_op jit(solution)/shard_map/ppermute | solution.py:406
  30.2 6.2 %collective-permute-start.10 = (bf16[144,128]{1,0:T(8,128)(2,1)S(1)}, bf16[144,128]{1,0:T(8,128)(2,1)S(1)}, u32[]{:S(2)}, u32[]{:S(2)}) collective-permute-start(bf16[144,128]{1,0:T(8,128)(2,1)S(1)} %get-tuple-element.60), channel_id=1, source_target_pairs={{0,4},{2,6},{4,0},{6,2},{8,12},{10,14},{12,8},{14,10},{1,5},{3,7},... | collective-permute-start | bytes 110600 | tf_op jit(solution)/shard_map/ppermute | solution.py:406
  30.9 7.1 %collective-permute-start.8 = (bf16[144,128]{1,0:T(8,128)(2,1)S(1)}, bf16[144,128]{1,0:T(8,128)(2,1)S(1)}, u32[]{:S(2)}, u32[]{:S(2)}) collective-permute-start(bf16[144,128]{1,0:T(8,128)(2,1)S(1)} %get-tuple-element.58), channel_id=1, source_target_pairs={{0,6},{2,4},{4,2},{6,0},{8,14},{10,12},{12,10},{14,8},{1,7},{3,5},... | collective-permute-start | bytes 110600 | tf_op jit(solution)/shard_map/ppermute | solution.py:406
  32.2 5.7 %collective-permute-start.9 = (bf16[144,128]{1,0:T(8,128)(2,1)S(1)}, bf16[144,128]{1,0:T(8,128)(2,1)S(1)}, u32[]{:S(2)}, u32[]{:S(2)}) collective-permute-start(bf16[144,128]{1,0:T(8,128)(2,1)S(1)} %get-tuple-element.59), channel_id=1, source_target_pairs={{0,2},{2,0},{4,6},{6,4},{8,10},{10,8},{12,14},{14,12},{1,3},{3,1},... | collective-permute-start | bytes 110600 | tf_op jit(solution)/shard_map/ppermute | solution.py:406
  38.5 1.5 %collective-permute-start.11 = (bf16[192,512]{1,0:T(8,128)(2,1)S(1)}, bf16[192,512]{1,0:T(8,128)(2,1)S(1)}, u32[]{:S(2)}, u32[]{:S(2)}) collective-permute-start(bf16[192,512]{1,0:T(8,128)(2,1)S(1)} %hidden.1.refs_1_), channel_id=1, source_target_pairs={{0,1},{1,0},{2,3},{3,2},{4,5},{5,4},{6,7},{7,6},{8,9},{9,8},{10,11... | collective-permute-start | bytes 589832 | tf_op jit(solution)/shard_map/ppermute | solution.py:406
  40.6 5.9 %collective-permute-start.15 = (bf16[64,512]{1,0:T(8,128)(2,1)S(1)}, bf16[64,512]{1,0:T(8,128)(2,1)S(1)}, u32[]{:S(2)}, u32[]{:S(2)}) collective-permute-start(bf16[64,512]{1,0:T(8,128)(2,1)S(1)} %get-tuple-element.72), channel_id=1, source_target_pairs={{0,4},{2,6},{4,0},{6,2},{8,12},{10,14},{12,8},{14,10},{1,5},{3,7},... | collective-permute-start | bytes 196616 | tf_op jit(solution)/shard_map/ppermute | solution.py:406
  40.7 7.4 %collective-permute-start.16 = (bf16[64,512]{1,0:T(8,128)(2,1)S(1)}, bf16[64,512]{1,0:T(8,128)(2,1)S(1)}, u32[]{:S(2)}, u32[]{:S(2)}) collective-permute-start(bf16[64,512]{1,0:T(8,128)(2,1)S(1)} %get-tuple-element.73), channel_id=1, source_target_pairs={{0,6},{2,4},{4,2},{6,0},{8,14},{10,12},{12,10},{14,8},{1,7},{3,5},... | collective-permute-start | bytes 196616 | tf_op jit(solution)/shard_map/ppermute | solution.py:406
  42.5 5.6 %collective-permute-start.17 = (bf16[64,512]{1,0:T(8,128)(2,1)S(1)}, bf16[64,512]{1,0:T(8,128)(2,1)S(1)}, u32[]{:S(2)}, u32[]{:S(2)}) collective-permute-start(bf16[64,512]{1,0:T(8,128)(2,1)S(1)} %get-tuple-element.74), channel_id=1, source_target_pairs={{0,2},{2,0},{4,6},{6,4},{8,10},{10,8},{12,14},{14,12},{1,3},{3,1},... | collective-permute-start | bytes 196616 | tf_op jit(solution)/shard_map/ppermute | solution.py:406
  44.6 9.3 %copy-start.3 = (f32[512]{0:T(512)S(1)}, f32[512]{0:T(512)}, u32[]{:S(2)}) copy-start(f32[512]{0:T(512)} %param.21) | copy-start | bytes 6148
  44.6 5.2 %collective-permute-start.12 = (bf16[64,512]{1,0:T(8,128)(2,1)S(1)}, bf16[64,512]{1,0:T(8,128)(2,1)S(1)}, u32[]{:S(2)}, u32[]{:S(2)}) collective-permute-start(bf16[64,512]{1,0:T(8,128)(2,1)S(1)} %get-tuple-element.68), channel_id=1, source_target_pairs={{0,4},{2,6},{4,0},{6,2},{8,12},{10,14},{12,8},{14,10},{1,5},{3,7},... | collective-permute-start | bytes 196616 | tf_op jit(solution)/shard_map/ppermute | solution.py:406
  44.7 5.2 %collective-permute-start.13 = (bf16[64,512]{1,0:T(8,128)(2,1)S(1)}, bf16[64,512]{1,0:T(8,128)(2,1)S(1)}, u32[]{:S(2)}, u32[]{:S(2)}) collective-permute-start(bf16[64,512]{1,0:T(8,128)(2,1)S(1)} %get-tuple-element.69), channel_id=1, source_target_pairs={{0,6},{2,4},{4,2},{6,0},{8,14},{10,12},{12,10},{14,8},{1,7},{3,5},... | collective-permute-start | bytes 196616 | tf_op jit(solution)/shard_map/ppermute | solution.py:406
  46.5 4.3 %collective-permute-start.14 = (bf16[64,512]{1,0:T(8,128)(2,1)S(1)}, bf16[64,512]{1,0:T(8,128)(2,1)S(1)}, u32[]{:S(2)}, u32[]{:S(2)}) collective-permute-start(bf16[64,512]{1,0:T(8,128)(2,1)S(1)} %get-tuple-element.70), channel_id=1, source_target_pairs={{0,2},{2,0},{4,6},{6,4},{8,10},{10,8},{12,14},{14,12},{1,3},{3,1},... | collective-permute-start | bytes 196616 | tf_op jit(solution)/shard_map/ppermute | solution.py:406
  48.2 5.6 %collective-permute-start.18 = (bf16[64,512]{1,0:T(8,128)(2,1)S(1)}, bf16[64,512]{1,0:T(8,128)(2,1)S(1)}, u32[]{:S(2)}, u32[]{:S(2)}) collective-permute-start(bf16[64,512]{1,0:T(8,128)(2,1)S(1)} %side_sum.1), channel_id=1, source_target_pairs={{0,8},{2,10},{4,12},{6,14},{8,0},{10,2},{12,4},{14,6},{1,9},{3,11}... | collective-permute-start | bytes 196616 | tf_op jit(solution)/shard_map/ppermute | solution.py:406

commit v18 on v17

--- a/solution.py
+++ b/solution.py
@@ -75,25 +75,23 @@
     half = n_feat // 2
     parcel_refs, pick_ref, src_ref = refs[:half], refs[half], refs[half + 1]
     seed_ref, nbr_ref, w_self_ref, w_nbr_ref, fetched_ref, sems = refs[half + 2 :]
-    owned = n_feat * 2 * pcap
-    first, rest = pl.ds(0, owned), pl.ds(owned, src_ref.shape[1] - owned)
+    first = pl.ds(0, src_ref.shape[1])
     copies = [
         pltpu.make_async_copy(a, b, sems.at[i])
         for i, (a, b) in enumerate(
             (
-                (src_hbm.at[:, first], src_ref.at[:, first]),
+                (src_hbm.at[:, first], src_ref),
                 (w_self_hbm, w_self_ref),
                 (w_nbr_hbm, w_nbr_ref),
                 (seed_hbm, seed_ref),
                 (nbr_hbm, nbr_ref),
                 (pick_hbm, fetched_ref),
-                (src_hbm.at[:, rest], src_ref.at[:, rest]),
             )
         )
     ]
     for copy in copies:
         copy.start()
-    for copy in copies[1:-1]:
+    for copy in copies[1:]:
         copy.wait()
     stride = -(-pcap // LANES) * LANES
     words = pick_ref.shape[2] // stride
@@ -116,19 +114,43 @@
             block = src_ref[:, pl.ds(at, 2 * pcap)].astype(jnp.float32)
             sides.append(jnp.where(first_core, block[:, :pcap], block[:, pcap:]))
         write_parcel(parcel_ref, weight, jnp.concatenate(sides, axis=1), digits)
-    copies[-1].wait()
-
-
-def turn_kernel(src_ref, table_ref):
-    fslice, nodes = src_ref.shape
-    width = 2048 if nodes % 2048 == 0 else 512
-
-    def turn(step, carry):
-        at = pl.multiple_of(step * width, width)
-        table_ref[pl.ds(at, width), :fslice] = src_ref[:, pl.ds(at, width)].T.astype(jnp.float32)
-        return carry
-
-    lax.fori_loop(0, nodes // width, turn, 0)
+
+
+def turn_kernel(owned_ref, src_hbm, table_ref):
+    fslice, owned = owned_ref.shape
+    pieces = src_hbm.shape[1] // owned - 1
+    width = next(w for w in (2048, 1536, 1024, 512, LANES) if owned % w == 0)
+
+    def turn(ref, low, place):
+        def step(i, carry):
+            at = pl.multiple_of(i * width, width)
+            rows = pl.ds(pl.multiple_of(place + at, LANES), width)
+            table_ref[rows, :fslice] = ref[:, pl.ds(low + at, width)].T.astype(jnp.float32)
+            return carry
+
+        lax.fori_loop(0, owned // width, step, 0)
+
+    def rest(buffer, sems):
+        copies = [
+            pltpu.make_async_copy(
+                src_hbm.at[:, pl.ds((i + 1) * owned, owned)],
+                buffer.at[:, pl.ds(i * owned, owned)],
+                sems.at[i],
+            )
+            for i in range(pieces)
+        ]
+        for copy in copies:
+            copy.start()
+        turn(owned_ref, 0, 0)
+        for i, copy in enumerate(copies):
+            copy.wait()
+            turn(buffer, i * owned, (i + 1) * owned)
+
+    pl.run_scoped(
+        rest,
+        pltpu.VMEM((fslice, pieces * owned), jnp.bfloat16),
+        pltpu.SemaphoreType.DMA((pieces,)),
+    )
 
 
 def mean_kernel(chosen, packed, fanout, pcap, fslice, turns, before, n_before, *refs):
@@ -349,7 +371,7 @@
 
 def near_kernel(half, *refs):
     pre_ref, w_ref, out_ref = refs[half:]
-    out_ref[...] = add_means(half, pre_ref[...], refs[:half], w_ref, 1)
+    out_ref[...] = add_means(half, pre_ref[...], refs[:half], w_ref)
 
 
 def hidden_kernel(live_ref, pre_ref, cross_ref, hidden_ref):
@@ -421,8 +443,7 @@
 ):
     n_feat = lax.axis_size("feat")
     half = n_feat // 2
-    first = half // 2
-    steps = [first, *(s for s in range(half - 1, -1, -1) if s != first)]
+    steps = list(range(half - 1, -1, -1))
     fslice, nodes = src_feats.shape
     fanout_one, pcap = nbr_one.shape[2:]
     width = w1_self.shape[1]
@@ -458,6 +479,7 @@
     def send(chunks, steps=steps):
         return [swap(chunk, "feat", s) if s else chunk for s, chunk in zip(steps, chunks)]
 
+    owned = n_feat * 2 * pcap
     picks = jnp.transpose(nbr_one, (0, 2, 1, 3))
     packed = 2 if fanout_one % 2 == 0 and nodes <= 1 << 16 else 1
     words = (n_feat, 1, fanout_one // packed * (-(-pcap // LANES) * LANES))
@@ -465,7 +487,7 @@
         functools.partial(pack_kernel, steps, n_feat, pcap),
         "pack",
         [((parcel_rows(fslice, n_idx), width), bf16)] * half
-        + [(words, jnp.int32), ((fslice, nodes), bf16)],
+        + [(words, jnp.int32), ((fslice, owned), bf16)],
         [hbm] * 6,
         [pinned(x) for x in (src_feats, seed_rows[None], nbr_two.T, w1_self, w1_nbr, picks)],
         scratch=[
@@ -474,7 +496,7 @@
             pltpu.VMEM((fslice, width), bf16),
             pltpu.VMEM((fslice, width), bf16),
             pltpu.VMEM((n_feat, fanout_one, 1, pcap), jnp.int32),
-            pltpu.SemaphoreType.DMA((7,)),
+            pltpu.SemaphoreType.DMA((6,)),
         ],
         limit=32 * MIB,
     )
@@ -498,7 +520,9 @@
             ),
             "mean",
             [(chunk_shape, bf16)] * count + list(outs),
-            [vmem] * len(ins) + [anywhere] + [vmem] * (len(tables) + len(tagged)),
+            ([vmem, hbm] if table is None else [vmem] * len(ins))
+            + [anywhere]
+            + [vmem] * (len(tables) + len(tagged)),
             (*ins, picks, *tables, *tagged),
             after=after,
             scratch=[
@@ -515,7 +539,7 @@
     *far_means, table = means(
         [s + half for s in steps if s],
         before=turn_kernel,
-        ins=(feats,),
+        ins=(feats, pinned(src_feats)),
         outs=[((nodes, LANES), jnp.float32)],
     )
     table = table.reshape(nodes, 1, LANES)
@@ -554,8 +578,8 @@
         (*far_arrived, far_own, far_pre, w_nbr, idx_tags),
     )
     cross_arrived = swap(cross, "feat", half)
-    turned = [*steps[1:-1], steps[0]]
-    near_means = means(turned, [*far_arrived[1:], far_arrived[0]], (cross,), table=table)
+    turned = steps[:-1]
+    near_means = means(turned, far_arrived, (cross,), table=table)
     near_arrived = send(near_means, turned)
     near_own, near_times = means(
         [0],

time: 54.8 us -> 53.3 us (0.973)
  waiting for transfers between devices: 10.6 us -> 6.62 us
  Pallas kernels: 19.1 us -> 21.7 us
    ppermute x19, waiting for transfers between devices: 10.6 us -> 6.62 us  [swap(): return lax.ppermute(value, axis, [(i, i ^ step) for i in range(size)])]
    pallas_call x14, Pallas kernels: 19.1 us -> 21.7 us  [call(): pl.pallas_call(wrapped, out_shape=tuple((jax.ShapeDtypeStruct(shape, dtyp...]
  transfers between devices with their start and end apart: 19 -> 19, of which waited for: 9 -> 8; matrix products, arithmetic and copies ran while one was open for 0% -> 0% of each run, Pallas kernels for 28% -> 34%
where the time goes in v18:
time: 53.3 us; the launch traced here: 52.9 us
  starting transfers between devices  23.1 us (43%)
  Pallas kernels  21.7 us (41%)
  waiting for transfers between devices  6.62 us (12%)
  between operations  1.48 us (3%)
    ppermute x19, starting transfers between devices, swap(): return lax.ppermute(value, axis, [(i, i ^ step) for i in range(size)])  23.1 us
    pallas_call x14, Pallas kernels, call(): pl.pallas_call(wrapped, out_shape=tuple((jax.ShapeDtypeStruct(shape, dtyp...  21.7 us
    ppermute x19, waiting for transfers between devices, swap(): return lax.ppermute(value, axis, [(i, i ^ step) for i in range(size)])  6.62 us
  transfers between devices with their start and end apart: 19, of which 8 were waited for; matrix products, arithmetic and copies ran while one was open for 0% of the time, Pallas kernels for 34%

profile of v18, /device:TPU:0, one launch (start us, length us, event | category | flops | bytes accessed | tf_op | source)
XLA Modules:
  0.0 52.9 jit_solution(11937706589290350633)
XLA Ops:
  0.6 1.7 %pack.1 = (bf16[176,512]{1,0:T(8,128)(2,1)S(1)}, bf16[176,512]{1,0:T(8,128)(2,1)S(1)}, bf16[176,512]{1,0:T(8,128)(2,1)S(1)}, bf16[176,512]{1,0:T(8,128)(2,1)S(1)...) custom-call(bf16[96,12288]{1,0:T(8,128)(2,1)} %refs_1_.2, s32[1,64]{1,0:T(1,128)} %bitcast.14, ...), custom_call_target="tpu_custom_call" | custom-call | flops 1100000000 | tf_op jit(solution)/shard_map/pack/pallas_call | solution.py:463
  2.3 4.0 %collective-permute-start = (bf16[176,512]{1,0:T(8,128)(2,1)S(1)}, bf16[176,512]{1,0:T(8,128)(2,1)S(1)}, u32[]{:S(2)}, u32[]{:S(2)}) collective-permute-start(bf16[176,512]{1,0:T(8,128)(2,1)S(1)} %get-tuple-element.39), channel_id=1, source_target_pairs={{0,6},{2,4},{4,2},{6,0},{8,14},{10,12},{12,10},{14,8},{1,7},{3,5},... | collective-permute-start | bytes 540680 | tf_op jit(solution)/shard_map/ppermute | solution.py:428
  6.4 0.5 collective-permute-start.1
  6.8 0.2 collective-permute-start.2
  7.0 0.0 copy-start.2
  7.0 7.1 %mean.4 = (bf16[144,128]{1,0:T(8,128)(2,1)S(1)}, bf16[144,128]{1,0:T(8,128)(2,1)S(1)}, bf16[144,128]{1,0:T(8,128)(2,1)S(1)}, f32[12288,128]{1,0:T(8,128)S(1)}) custom-call(bf16[96,3072]{1,0:T(8,128)(2,1)S(1)} %get-tuple-element.43.refs_0_, bf16[96,12288]{1,0:T(8,128)(2,1)} %refs_1_.2, s32[8,1,1280]{2,1,0:T(1,128)S(1)} %get-tuple-element.44.refs_2_.refs_6_.refs_0_), custom_call_target="tpu_custom_call" | custom-call | flops 6600000000 | tf_op jit(solution)/shard_map/mean/pallas_call | solution.py:463
  14.7 0.0 collective-permute-done.refs_1_.refs_0_.refs_2_
  14.7 0.2 collective-permute-done.1.refs_2_.refs_1_.refs_3_
  15.0 0.0 collective-permute-done.2.refs_3_.refs_2_.refs_4_
  15.0 0.1 collective-permute-start.6
  15.1 2.7 %collective-permute-start.3 = (bf16[160,128]{1,0:T(8,128)(2,1)S(1)}, bf16[160,128]{1,0:T(8,128)(2,1)S(1)}, u32[]{:S(2)}, u32[]{:S(2)}) collective-permute-start(bf16[160,128]{1,0:T(8,128)(2,1)S(1)} %get-tuple-element.48), channel_id=1, source_target_pairs={{0,6},{2,4},{4,2},{6,0},{8,14},{10,12},{12,10},{14,8},{1,7},{3,5},... | collective-permute-start | bytes 122888 | tf_op jit(solution)/shard_map/ppermute | solution.py:428
  17.8 0.5 collective-permute-start.4
  18.2 0.4 collective-permute-start.5
  18.7 0.0 collective-permute-done.6.refs_4_
  18.7 0.0 copy-done.2
  18.7 2.6 %mean.5 = (bf16[144,128]{1,0:T(8,128)(2,1)S(1)}, bf16[4,96,512]{2,1,0:T(8,128)(2,1)S(1)}, f32[192,512]{1,0:T(8,128)S(1)}, f32[192,512]{1,0:T(8,128)S(1)}, bf16[16,512]{1,0:T(8,128)(2,1)S(1)}) custom-call(bf16[176,512]{1,0:T(8,128)(2,1)S(1)} %collective-permute-done.refs_1_.refs_0_.refs_2_, ...), custom_call_target="tpu_custom_call" | custom-call | tf_op jit(solution)/shard_map/mean/pallas_call | solution.py:463
  21.3 0.0 collective-permute-done.3.refs_0_.refs_2_
  21.3 0.5 collective-permute-done.4.refs_1_.refs_3_
  21.8 0.5 collective-permute-done.5.refs_2_.refs_4_
  22.2 0.4 far.1.refs_5_.refs_9_
  22.6 0.0 copy-start
  22.6 0.0 copy-start.1
  22.6 2.7 %collective-permute-start.7 = (bf16[208,512]{1,0:T(8,128)(2,1)S(1)}, bf16[208,512]{1,0:T(8,128)(2,1)S(1)}, u32[]{:S(2)}, u32[]{:S(2)}) collective-permute-start(bf16[208,512]{1,0:T(8,128)(2,1)S(1)} %far.1.refs_5_.refs_9_), channel_id=1, source_target_pairs={{0,8},{2,10},{4,12},{6,14},{8,0},{10,2},{12,4},{14,6},{1,9},{3,11}... | collective-permute-start | bytes 638984 | tf_op jit(solution)/shard_map/ppermute | solution.py:428
  25.3 4.3 %mean.6 = (bf16[144,128]{1,0:T(8,128)(2,1)S(1)}, bf16[144,128]{1,0:T(8,128)(2,1)S(1)}, bf16[144,128]{1,0:T(8,128)(2,1)S(1)}) custom-call(s32[8,1,1280]{2,1,0:T(1,128)S(1)} %get-tuple-element.44.refs_2_.refs_6_.refs_0_, f32[12288,1,128]{2,1,0:T(1,128)S(1)} %bitcast.8, bf16[160,128]{1,0:T(8,128)(2,1)S(1)} %collective-permute-done.3.refs_0_.refs_2_, ...), custom_call_target="tpu_custom_call" | custom-call | flops 6600000000 | tf_op jit(solution)/shard_map/mean/pallas_call | solution.py:463
  29.7 2.0 %collective-permute-start.8 = (bf16[144,128]{1,0:T(8,128)(2,1)S(1)}, bf16[144,128]{1,0:T(8,128)(2,1)S(1)}, u32[]{:S(2)}, u32[]{:S(2)}) collective-permute-start(bf16[144,128]{1,0:T(8,128)(2,1)S(1)} %get-tuple-element.58), channel_id=1, source_target_pairs={{0,6},{2,4},{4,2},{6,0},{8,14},{10,12},{12,10},{14,8},{1,7},{3,5},... | collective-permute-start | bytes 110600 | tf_op jit(solution)/shard_map/ppermute | solution.py:428
  31.7 0.8 %collective-permute-start.9 = (bf16[144,128]{1,0:T(8,128)(2,1)S(1)}, bf16[144,128]{1,0:T(8,128)(2,1)S(1)}, u32[]{:S(2)}, u32[]{:S(2)}) collective-permute-start(bf16[144,128]{1,0:T(8,128)(2,1)S(1)} %get-tuple-element.59), channel_id=1, source_target_pairs={{0,4},{2,6},{4,0},{6,2},{8,12},{10,14},{12,8},{14,10},{1,5},{3,7},... | collective-permute-start | bytes 110600 | tf_op jit(solution)/shard_map/ppermute | solution.py:428
  32.5 1.4 %collective-permute-start.10 = (bf16[144,128]{1,0:T(8,128)(2,1)S(1)}, bf16[144,128]{1,0:T(8,128)(2,1)S(1)}, u32[]{:S(2)}, u32[]{:S(2)}) collective-permute-start(bf16[144,128]{1,0:T(8,128)(2,1)S(1)} %get-tuple-element.60), channel_id=1, source_target_pairs={{0,2},{2,0},{4,6},{6,4},{8,10},{10,8},{12,14},{14,12},{1,3},{3,1},... | collective-permute-start | bytes 110600 | tf_op jit(solution)/shard_map/ppermute | solution.py:428
  33.9 0.0 copy-done
  33.9 0.0 copy-done.1
  33.9 2.6 %mean.7 = (bf16[144,128]{1,0:T(8,128)(2,1)S(1)}, bf16[256,768]{1,0:T(8,128)(2,1)S(1)}) custom-call(bf16[512,512]{1,0:T(8,128)(2,1)S(1)} %copy-done, bf16[512,512]{1,0:T(8,128)(2,1)S(1)} %copy-done.1, bf16[176,512]{1,0:T(8,128)(2,1)S(1)} %collective-permute-done.refs_1_.refs_0_.refs_2_, bf16[176,512]{1,0:T(8,128)(2,1)S(1)} %collective-permute-done.1.refs_2_.refs_1_.refs_3_, ...), custom_call_target="tpu_custom_call" | custom-call | tf_op jit(solution)/shard_map/mean/pallas_call | solution.py:463
  36.4 0.0 collective-permute-done.8.refs_0_
  36.5 0.0 collective-permute-done.9.refs_1_
  36.5 0.0 collective-permute-done.10.refs_2_
  36.5 0.4 near.1.refs_1_
  36.8 0.0 collective-permute-done.7.refs_2_.refs_0_
  36.9 0.2 hidden.1.refs_1_
  37.0 0.1 collective-permute-start.11
  37.1 0.9 %far_times.1 = (bf16[256,768]{1,0:T(8,128)(2,1)S(1)}, bf16[2,192,512]{2,1,0:T(8,128)(2,1)S(1)}, bf16[192,512]{1,0:T(8,128)(2,1)}) custom-call(bf16[208,512]{1,0:T(8,128)(2,1)S(1)} %collective-permute-done.7.refs_2_.refs_0_, bf16[192,512]{1,0:T(8,128)(2,1)S(1)} %hidden.1.refs_1_, bf16[512,512]{1,0:T(8,128)(2,1)S(1)} %copy-done, bf16[512,512]{1,0:T(8,128)(2,1)S(1)} %copy-done.1), custom_call_target="tpu_custom_call" | custom-call | flops 1100000000 | tf_op jit(solution)/shard_map/far_times/pallas_call | solution.py:463
  38.0 0.0 copy-start.3
  38.0 0.5 %collective-permute-done.11.refs_2_ = bf16[192,512]{1,0:T(8,128)(2,1)S(1)} collective-permute-done((bf16[192,512]{1,0:T(8,128)(2,1)S(1)}, bf16[192,512]{1,0:T(8,128)(2,1)S(1)}, u32[]{:S(2)}, u32[]{:S(2)}) %collective-permute-start.11) | collective-permute-done | bytes 196640 | tf_op jit(solution)/shard_map/ppermute | solution.py:428
  38.5 0.6 %far_share.1 = (bf16[64,512]{1,0:T(8,128)(2,1)S(1)}, bf16[64,512]{1,0:T(8,128)(2,1)S(1)}, bf16[64,512]{1,0:T(8,128)(2,1)S(1)}, bf16[64,512]{1,0:T(8,128)(2,1)S(1)}, bf16[768,512]{1,0:T(8,128)(2,1)S(1)}) custom-call(bf16[256,768]{1,0:T(8,128)(2,1)S(1)} %get-tuple-element.65.refs_0_, bf16[2,192,512]{2,1,0:T(8,128)(2,1)S(1)} %get-tuple-element.66.refs_1_, ...), custom_call_target="tpu_custom_call" | custom-call | flops 1100000000 | tf_op jit(solution)/shard_map/far_share/pallas_call | solution.py:463
  39.1 2.9 %collective-permute-start.15 = (bf16[64,512]{1,0:T(8,128)(2,1)S(1)}, bf16[64,512]{1,0:T(8,128)(2,1)S(1)}, u32[]{:S(2)}, u32[]{:S(2)}) collective-permute-start(bf16[64,512]{1,0:T(8,128)(2,1)S(1)} %get-tuple-element.72), channel_id=1, source_target_pairs={{0,6},{2,4},{4,2},{6,0},{8,14},{10,12},{12,10},{14,8},{1,7},{3,5},... | collective-permute-start | bytes 196616 | tf_op jit(solution)/shard_map/ppermute | solution.py:428
  42.0 0.0 collective-permute-start.16
  42.0 0.7 %collective-permute-start.17 = (bf16[64,512]{1,0:T(8,128)(2,1)S(1)}, bf16[64,512]{1,0:T(8,128)(2,1)S(1)}, u32[]{:S(2)}, u32[]{:S(2)}) collective-permute-start(bf16[64,512]{1,0:T(8,128)(2,1)S(1)} %get-tuple-element.74), channel_id=1, source_target_pairs={{0,2},{2,0},{4,6},{6,4},{8,10},{10,8},{12,14},{14,12},{1,3},{3,1},... | collective-permute-start | bytes 196616 | tf_op jit(solution)/shard_map/ppermute | solution.py:428
  42.7 0.4 near_share.1
  43.1 2.9 %collective-permute-start.12 = (bf16[64,512]{1,0:T(8,128)(2,1)S(1)}, bf16[64,512]{1,0:T(8,128)(2,1)S(1)}, u32[]{:S(2)}, u32[]{:S(2)}) collective-permute-start(bf16[64,512]{1,0:T(8,128)(2,1)S(1)} %get-tuple-element.68), channel_id=1, source_target_pairs={{0,6},{2,4},{4,2},{6,0},{8,14},{10,12},{12,10},{14,8},{1,7},{3,5},... | collective-permute-start | bytes 196616 | tf_op jit(solution)/shard_map/ppermute | solution.py:428
  45.9 0.0 collective-permute-start.13
  45.9 0.0 collective-permute-done.15.refs_0_
  45.9 0.7 %collective-permute-start.14 = (bf16[64,512]{1,0:T(8,128)(2,1)S(1)}, bf16[64,512]{1,0:T(8,128)(2,1)S(1)}, u32[]{:S(2)}, u32[]{:S(2)}) collective-permute-start(bf16[64,512]{1,0:T(8,128)(2,1)S(1)} %get-tuple-element.70), channel_id=1, source_target_pairs={{0,2},{2,0},{4,6},{6,4},{8,10},{10,8},{12,14},{14,12},{1,3},{3,1},... | collective-permute-start | bytes 196616 | tf_op jit(solution)/shard_map/ppermute | solution.py:428
  46.6 0.0 collective-permute-done.16.refs_1_
  46.6 0.4 collective-permute-done.17.refs_2_
  47.0 0.7 %collective-permute-start.18 = (bf16[64,512]{1,0:T(8,128)(2,1)S(1)}, bf16[64,512]{1,0:T(8,128)(2,1)S(1)}, u32[]{:S(2)}, u32[]{:S(2)}) collective-permute-start(bf16[64,512]{1,0:T(8,128)(2,1)S(1)} %side_sum.1), channel_id=1, source_target_pairs={{0,8},{2,10},{4,12},{6,14},{8,0},{10,2},{12,4},{14,6},{1,9},{3,11}... | collective-permute-start | bytes 196616 | tf_op jit(solution)/shard_map/ppermute | solution.py:428
  47.8 1.0 %collective-permute-done.12.refs_1_ = bf16[64,512]{1,0:T(8,128)(2,1)S(1)} collective-permute-done((bf16[64,512]{1,0:T(8,128)(2,1)S(1)}, bf16[64,512]{1,0:T(8,128)(2,1)S(1)}, u32[]{:S(2)}, u32[]{:S(2)}) %collective-permute-start.12) | collective-permute-done | bytes 65568 | tf_op jit(solution)/shard_map/ppermute | solution.py:428
  48.8 1.6 %collective-permute-done.13.refs_2_ = bf16[64,512]{1,0:T(8,128)(2,1)S(1)} collective-permute-done((bf16[64,512]{1,0:T(8,128)(2,1)S(1)}, bf16[64,512]{1,0:T(8,128)(2,1)S(1)}, u32[]{:S(2)}, u32[]{:S(2)}) %collective-permute-start.13) | collective-permute-done | bytes 65568 | tf_op jit(solution)/shard_map/ppermute | solution.py:428
  50.3 0.0 collective-permute-done.14.refs_3_
  50.3 1.9 %collective-permute-done.18.refs_5_ = bf16[64,512]{1,0:T(8,128)(2,1)S(1)} collective-permute-done((bf16[64,512]{1,0:T(8,128)(2,1)S(1)}, bf16[64,512]{1,0:T(8,128)(2,1)S(1)}, u32[]{:S(2)}, u32[]{:S(2)}) %collective-permute-start.18) | collective-permute-done | bytes 65568 | tf_op jit(solution)/shard_map/ppermute | solution.py:428
  52.2 0.0 copy-done.3
  52.2 0.7 %seeds.1 = bf16[64,512]{1,0:T(8,128)(2,1)} custom-call(f32[1,512]{1,0:T(1,128)S(1)} %bitcast.11, bf16[64,512]{1,0:T(8,128)(2,1)S(1)} %collective-permute-done.12.refs_1_, bf16[64,512]{1,0:T(8,128)(2,1)S(1)} %collective-permute-done.13.refs_2_, bf16[64,512]{1,0:T(8,128)(2,1)S(1)} %collective-permute-done.14.refs_3_, ...), custom_call_target="tpu_custom_call" | custom-call | flops 1100000000 | tf_op jit(solution)/shard_map/seeds/pallas_call | solution.py:463
  (2 shorter events, 0.1 us)
Async XLA Ops:
  2.3 12.4 %collective-permute-start = (bf16[176,512]{1,0:T(8,128)(2,1)S(1)}, bf16[176,512]{1,0:T(8,128)(2,1)S(1)}, u32[]{:S(2)}, u32[]{:S(2)}) collective-permute-start(bf16[176,512]{1,0:T(8,128)(2,1)S(1)} %get-tuple-element.39), channel_id=1, source_target_pairs={{0,6},{2,4},{4,2},{6,0},{8,14},{10,12},{12,10},{14,8},{1,7},{3,5},... | collective-permute-start | bytes 540680 | tf_op jit(solution)/shard_map/ppermute | solution.py:428
  6.4 8.6 %collective-permute-start.1 = (bf16[176,512]{1,0:T(8,128)(2,1)S(1)}, bf16[176,512]{1,0:T(8,128)(2,1)S(1)}, u32[]{:S(2)}, u32[]{:S(2)}) collective-permute-start(bf16[176,512]{1,0:T(8,128)(2,1)S(1)} %get-tuple-element.40), channel_id=1, source_target_pairs={{0,4},{2,6},{4,0},{6,2},{8,12},{10,14},{12,8},{14,10},{1,5},{3,7},... | collective-permute-start | bytes 540680 | tf_op jit(solution)/shard_map/ppermute | solution.py:428
  6.8 8.2 %collective-permute-start.2 = (bf16[176,512]{1,0:T(8,128)(2,1)S(1)}, bf16[176,512]{1,0:T(8,128)(2,1)S(1)}, u32[]{:S(2)}, u32[]{:S(2)}) collective-permute-start(bf16[176,512]{1,0:T(8,128)(2,1)S(1)} %get-tuple-element.41), channel_id=1, source_target_pairs={{0,2},{2,0},{4,6},{6,4},{8,10},{10,8},{12,14},{14,12},{1,3},{3,1},... | collective-permute-start | bytes 540680 | tf_op jit(solution)/shard_map/ppermute | solution.py:428
  7.0 11.7 %copy-start.2 = (f32[512]{0:T(512)S(1)}, f32[512]{0:T(512)}, u32[]{:S(2)}) copy-start(f32[512]{0:T(512)} %param.18) | copy-start | bytes 6148
  15.0 3.6 %collective-permute-start.6 = (bf16[4,96,512]{2,1,0:T(8,128)(2,1)S(1)}, bf16[4,96,512]{2,1,0:T(8,128)(2,1)S(1)}, u32[]{:S(2)}, u32[]{:S(2)}) collective-permute-start(bf16[4,96,512]{2,1,0:T(8,128)(2,1)S(1)} %get-tuple-element.51), channel_id=1, source_target_pairs={{0,1},{1,0},{2,3},{3,2},{4,5},{5,4},{6,7},{7,6},{8,9},{9,8},{10,11... | collective-permute-start | bytes 1179656 | tf_op jit(solution)/shard_map/ppermute | solution.py:428
  15.1 6.2 %collective-permute-start.3 = (bf16[160,128]{1,0:T(8,128)(2,1)S(1)}, bf16[160,128]{1,0:T(8,128)(2,1)S(1)}, u32[]{:S(2)}, u32[]{:S(2)}) collective-permute-start(bf16[160,128]{1,0:T(8,128)(2,1)S(1)} %get-tuple-element.48), channel_id=1, source_target_pairs={{0,6},{2,4},{4,2},{6,0},{8,14},{10,12},{12,10},{14,8},{1,7},{3,5},... | collective-permute-start | bytes 122888 | tf_op jit(solution)/shard_map/ppermute | solution.py:428
  17.8 4.0 %collective-permute-start.4 = (bf16[160,128]{1,0:T(8,128)(2,1)S(1)}, bf16[160,128]{1,0:T(8,128)(2,1)S(1)}, u32[]{:S(2)}, u32[]{:S(2)}) collective-permute-start(bf16[160,128]{1,0:T(8,128)(2,1)S(1)} %get-tuple-element.49), channel_id=1, source_target_pairs={{0,4},{2,6},{4,0},{6,2},{8,12},{10,14},{12,8},{14,10},{1,5},{3,7},... | collective-permute-start | bytes 122888 | tf_op jit(solution)/shard_map/ppermute | solution.py:428
  18.2 4.0 %collective-permute-start.5 = (bf16[160,128]{1,0:T(8,128)(2,1)S(1)}, bf16[160,128]{1,0:T(8,128)(2,1)S(1)}, u32[]{:S(2)}, u32[]{:S(2)}) collective-permute-start(bf16[160,128]{1,0:T(8,128)(2,1)S(1)} %get-tuple-element.50), channel_id=1, source_target_pairs={{0,2},{2,0},{4,6},{6,4},{8,10},{10,8},{12,14},{14,12},{1,3},{3,1},... | collective-permute-start | bytes 122888 | tf_op jit(solution)/shard_map/ppermute | solution.py:428
  22.6 11.2 %copy-start = (bf16[512,512]{1,0:T(8,128)(2,1)S(1)}, bf16[512,512]{1,0:T(8,128)(2,1)}, u32[]{:S(2)}) copy-start(bf16[512,512]{1,0:T(8,128)(2,1)} %refs_3_.5) | copy-start | bytes 1572868
  22.6 11.2 %copy-start.1 = (bf16[512,512]{1,0:T(8,128)(2,1)S(1)}, bf16[512,512]{1,0:T(8,128)(2,1)}, u32[]{:S(2)}) copy-start(bf16[512,512]{1,0:T(8,128)(2,1)} %refs_4_.3) | copy-start | bytes 1572868
  22.6 14.2 %collective-permute-start.7 = (bf16[208,512]{1,0:T(8,128)(2,1)S(1)}, bf16[208,512]{1,0:T(8,128)(2,1)S(1)}, u32[]{:S(2)}, u32[]{:S(2)}) collective-permute-start(bf16[208,512]{1,0:T(8,128)(2,1)S(1)} %far.1.refs_5_.refs_9_), channel_id=1, source_target_pairs={{0,8},{2,10},{4,12},{6,14},{8,0},{10,2},{12,4},{14,6},{1,9},{3,11}... | collective-permute-start | bytes 638984 | tf_op jit(solution)/shard_map/ppermute | solution.py:428
  29.7 6.8 %collective-permute-start.8 = (bf16[144,128]{1,0:T(8,128)(2,1)S(1)}, bf16[144,128]{1,0:T(8,128)(2,1)S(1)}, u32[]{:S(2)}, u32[]{:S(2)}) collective-permute-start(bf16[144,128]{1,0:T(8,128)(2,1)S(1)} %get-tuple-element.58), channel_id=1, source_target_pairs={{0,6},{2,4},{4,2},{6,0},{8,14},{10,12},{12,10},{14,8},{1,7},{3,5},... | collective-permute-start | bytes 110600 | tf_op jit(solution)/shard_map/ppermute | solution.py:428
  31.7 4.8 %collective-permute-start.9 = (bf16[144,128]{1,0:T(8,128)(2,1)S(1)}, bf16[144,128]{1,0:T(8,128)(2,1)S(1)}, u32[]{:S(2)}, u32[]{:S(2)}) collective-permute-start(bf16[144,128]{1,0:T(8,128)(2,1)S(1)} %get-tuple-element.59), channel_id=1, source_target_pairs={{0,4},{2,6},{4,0},{6,2},{8,12},{10,14},{12,8},{14,10},{1,5},{3,7},... | collective-permute-start | bytes 110600 | tf_op jit(solution)/shard_map/ppermute | solution.py:428
  32.5 4.0 %collective-permute-start.10 = (bf16[144,128]{1,0:T(8,128)(2,1)S(1)}, bf16[144,128]{1,0:T(8,128)(2,1)S(1)}, u32[]{:S(2)}, u32[]{:S(2)}) collective-permute-start(bf16[144,128]{1,0:T(8,128)(2,1)S(1)} %get-tuple-element.60), channel_id=1, source_target_pairs={{0,2},{2,0},{4,6},{6,4},{8,10},{10,8},{12,14},{14,12},{1,3},{3,1},... | collective-permute-start | bytes 110600 | tf_op jit(solution)/shard_map/ppermute | solution.py:428
  37.0 1.5 %collective-permute-start.11 = (bf16[192,512]{1,0:T(8,128)(2,1)S(1)}, bf16[192,512]{1,0:T(8,128)(2,1)S(1)}, u32[]{:S(2)}, u32[]{:S(2)}) collective-permute-start(bf16[192,512]{1,0:T(8,128)(2,1)S(1)} %hidden.1.refs_1_), channel_id=1, source_target_pairs={{0,1},{1,0},{2,3},{3,2},{4,5},{5,4},{6,7},{7,6},{8,9},{9,8},{10,11... | collective-permute-start | bytes 589832 | tf_op jit(solution)/shard_map/ppermute | solution.py:428
  38.0 14.3 %copy-start.3 = (f32[512]{0:T(512)S(1)}, f32[512]{0:T(512)}, u32[]{:S(2)}) copy-start(f32[512]{0:T(512)} %param.21) | copy-start | bytes 6148
  39.1 6.8 %collective-permute-start.15 = (bf16[64,512]{1,0:T(8,128)(2,1)S(1)}, bf16[64,512]{1,0:T(8,128)(2,1)S(1)}, u32[]{:S(2)}, u32[]{:S(2)}) collective-permute-start(bf16[64,512]{1,0:T(8,128)(2,1)S(1)} %get-tuple-element.72), channel_id=1, source_target_pairs={{0,6},{2,4},{4,2},{6,0},{8,14},{10,12},{12,10},{14,8},{1,7},{3,5},... | collective-permute-start | bytes 196616 | tf_op jit(solution)/shard_map/ppermute | solution.py:428
  42.0 4.6 %collective-permute-start.16 = (bf16[64,512]{1,0:T(8,128)(2,1)S(1)}, bf16[64,512]{1,0:T(8,128)(2,1)S(1)}, u32[]{:S(2)}, u32[]{:S(2)}) collective-permute-start(bf16[64,512]{1,0:T(8,128)(2,1)S(1)} %get-tuple-element.73), channel_id=1, source_target_pairs={{0,4},{2,6},{4,0},{6,2},{8,12},{10,14},{12,8},{14,10},{1,5},{3,7},... | collective-permute-start | bytes 196616 | tf_op jit(solution)/shard_map/ppermute | solution.py:428
  42.0 5.0 %collective-permute-start.17 = (bf16[64,512]{1,0:T(8,128)(2,1)S(1)}, bf16[64,512]{1,0:T(8,128)(2,1)S(1)}, u32[]{:S(2)}, u32[]{:S(2)}) collective-permute-start(bf16[64,512]{1,0:T(8,128)(2,1)S(1)} %get-tuple-element.74), channel_id=1, source_target_pairs={{0,2},{2,0},{4,6},{6,4},{8,10},{10,8},{12,14},{14,12},{1,3},{3,1},... | collective-permute-start | bytes 196616 | tf_op jit(solution)/shard_map/ppermute | solution.py:428
  43.1 5.7 %collective-permute-start.12 = (bf16[64,512]{1,0:T(8,128)(2,1)S(1)}, bf16[64,512]{1,0:T(8,128)(2,1)S(1)}, u32[]{:S(2)}, u32[]{:S(2)}) collective-permute-start(bf16[64,512]{1,0:T(8,128)(2,1)S(1)} %get-tuple-element.68), channel_id=1, source_target_pairs={{0,6},{2,4},{4,2},{6,0},{8,14},{10,12},{12,10},{14,8},{1,7},{3,5},... | collective-permute-start | bytes 196616 | tf_op jit(solution)/shard_map/ppermute | solution.py:428
  45.9 4.4 %collective-permute-start.13 = (bf16[64,512]{1,0:T(8,128)(2,1)S(1)}, bf16[64,512]{1,0:T(8,128)(2,1)S(1)}, u32[]{:S(2)}, u32[]{:S(2)}) collective-permute-start(bf16[64,512]{1,0:T(8,128)(2,1)S(1)} %get-tuple-element.69), channel_id=1, source_target_pairs={{0,4},{2,6},{4,0},{6,2},{8,12},{10,14},{12,8},{14,10},{1,5},{3,7},... | collective-permute-start | bytes 196616 | tf_op jit(solution)/shard_map/ppermute | solution.py:428
  45.9 4.4 %collective-permute-start.14 = (bf16[64,512]{1,0:T(8,128)(2,1)S(1)}, bf16[64,512]{1,0:T(8,128)(2,1)S(1)}, u32[]{:S(2)}, u32[]{:S(2)}) collective-permute-start(bf16[64,512]{1,0:T(8,128)(2,1)S(1)} %get-tuple-element.70), channel_id=1, source_target_pairs={{0,2},{2,0},{4,6},{6,4},{8,10},{10,8},{12,14},{14,12},{1,3},{3,1},... | collective-permute-start | bytes 196616 | tf_op jit(solution)/shard_map/ppermute | solution.py:428
  47.0 5.2 %collective-permute-start.18 = (bf16[64,512]{1,0:T(8,128)(2,1)S(1)}, bf16[64,512]{1,0:T(8,128)(2,1)S(1)}, u32[]{:S(2)}, u32[]{:S(2)}) collective-permute-start(bf16[64,512]{1,0:T(8,128)(2,1)S(1)} %side_sum.1), channel_id=1, source_target_pairs={{0,8},{2,10},{4,12},{6,14},{8,0},{10,2},{12,4},{14,6},{1,9},{3,11}... | collective-permute-start | bytes 196616 | tf_op jit(solution)/shard_map/ppermute | solution.py:428

commit v19 on v18

--- a/solution.py
+++ b/solution.py
@@ -405,21 +405,26 @@
         ref[...] = part[s * rows : (s + 1) * rows].astype(jnp.bfloat16)
 
 
-def near_share_kernel(near_ref, values_ref, *out_refs):
-    store_shares(near_ref, values_ref, out_refs)
+def near_share_kernel(places, near_ref, values_ref, *out_refs):
+    for place, ref in zip(places, out_refs):
+        rows = ref.shape[0]
+        times = near_ref[place * rows : (place + 1) * rows, :]
+        ref[...] = jnp.dot(times, values_ref[...], preferred_element_type=jnp.float32).astype(
+            jnp.bfloat16
+        )
 
 
 def side_sum_kernel(*refs):
     total = refs[0][...].astype(jnp.float32)
     for ref in refs[1:-1]:
         total = total + ref[...].astype(jnp.float32)
-    refs[-1][...] = total.astype(jnp.bfloat16)
+    refs[-1][: total.shape[0], :] = total.astype(jnp.bfloat16)
 
 
 def last_kernel(bias_ref, *refs):
     total = bias_ref[...]
     for ref in refs[:-1]:
-        total = total + ref[...].astype(jnp.float32)
+        total = total + ref[: refs[-1].shape[0], :].astype(jnp.float32)
     refs[-1][...] = jnp.maximum(total, 0.0).astype(jnp.bfloat16)
 
 
@@ -628,24 +633,35 @@
         limit=32 * MIB,
     )
     far_shares = send(far_shares)
-    near_shares = call(
-        near_share_kernel,
-        "near_share",
-        [((seed_count, width), bf16)] * half,
-        [vmem] * 2,
-        (near_times, values),
-        limit=32 * MIB,
-    )
-    near_shares = send(near_shares)
+    def near_share(places, after=()):
+        return call(
+            functools.partial(near_share_kernel, places),
+            "near_share",
+            [((seed_count, width), bf16)] * len(places),
+            [vmem] * 2,
+            (near_times, values),
+            after=after,
+            limit=32 * MIB,
+        )
+
+    *near_shares, near_last = near_share([*range(half - 2), half - 1])
+    near_shares = [swap(share, "feat", s) for share, s in zip(near_shares, steps)]
     (far_sum,) = call(
-        side_sum_kernel, "side_sum", [((seed_count, width), bf16)], [vmem] * half, far_shares
-    )
+        side_sum_kernel, "side_sum", [((seed_count + 8, width), bf16)], [vmem] * half, far_shares
+    )
+    (near_late,) = near_share([half - 2], (far_sum,))
     (seed_out,) = call(
         last_kernel,
         "seeds",
         [((seed_count, width), bf16)],
         [vmem] * (half + 2),
-        (bias_two[None], *near_shares, swap(far_sum, "feat", half)),
+        (
+            bias_two[None],
+            *near_shares,
+            swap(near_late, "feat", 1),
+            near_last,
+            swap(far_sum, "feat", half),
+        ),
     )
     return (result[None, None], seed_out)
 

time: 53.3 us -> 52.9 us (level)
  waiting for transfers between devices: 6.62 us -> 5.73 us
    ppermute x19, waiting for transfers between devices: 6.62 us -> 5.73 us  [swap(): return lax.ppermute(value, axis, [(i, i ^ step) for i in range(size)])]
    pallas_call x14 -> x15, Pallas kernels: 21.7 us -> 21.7 us  [call(): pl.pallas_call(wrapped, out_shape=tuple((jax.ShapeDtypeStruct(shape, dtyp...]
  transfers between devices with their start and end apart: 19 -> 19, of which waited for: 8 -> 9; matrix products, arithmetic and copies ran while one was open for 0% -> 0% of each run, Pallas kernels for 34% -> 35%
where the time goes in v19:
time: 52.9 us; the launch traced here: 52.4 us
  starting transfers between devices  23.5 us (44%)
  Pallas kernels  21.7 us (41%)
  waiting for transfers between devices  5.73 us (11%)
  between operations  1.46 us (3%)
    ppermute x19, starting transfers between devices, swap(): return lax.ppermute(value, axis, [(i, i ^ step) for i in range(size)])  23.5 us
    pallas_call x15, Pallas kernels, call(): pl.pallas_call(wrapped, out_shape=tuple((jax.ShapeDtypeStruct(shape, dtyp...  21.7 us
    ppermute x19, waiting for transfers between devices, swap(): return lax.ppermute(value, axis, [(i, i ^ step) for i in range(size)])  5.73 us
  transfers between devices with their start and end apart: 19, of which 9 were waited for; matrix products, arithmetic and copies ran while one was open for 0% of the time, Pallas kernels for 35%

profile of v19, /device:TPU:0, one launch (start us, length us, event | category | flops | bytes accessed | tf_op | source)
XLA Modules:
  0.0 52.4 jit_solution(9305055003886199975)
XLA Ops:
  0.6 1.7 %pack.1 = (bf16[176,512]{1,0:T(8,128)(2,1)S(1)}, bf16[176,512]{1,0:T(8,128)(2,1)S(1)}, bf16[176,512]{1,0:T(8,128)(2,1)S(1)}, bf16[176,512]{1,0:T(8,128)(2,1)S(1)...) custom-call(bf16[96,12288]{1,0:T(8,128)(2,1)} %refs_1_.2, s32[1,64]{1,0:T(1,128)} %bitcast.14, ...), custom_call_target="tpu_custom_call" | custom-call | flops 1100000000 | tf_op jit(solution)/shard_map/pack/pallas_call | solution.py:468
  2.3 4.0 %collective-permute-start = (bf16[176,512]{1,0:T(8,128)(2,1)S(1)}, bf16[176,512]{1,0:T(8,128)(2,1)S(1)}, u32[]{:S(2)}, u32[]{:S(2)}) collective-permute-start(bf16[176,512]{1,0:T(8,128)(2,1)S(1)} %get-tuple-element.38), channel_id=1, source_target_pairs={{0,6},{2,4},{4,2},{6,0},{8,14},{10,12},{12,10},{14,8},{1,7},{3,5},... | collective-permute-start | bytes 540680 | tf_op jit(solution)/shard_map/ppermute | solution.py:433
  6.4 0.5 collective-permute-start.1
  6.8 0.2 collective-permute-start.2
  7.0 0.0 copy-start.2
  7.0 7.1 %mean.4 = (bf16[144,128]{1,0:T(8,128)(2,1)S(1)}, bf16[144,128]{1,0:T(8,128)(2,1)S(1)}, bf16[144,128]{1,0:T(8,128)(2,1)S(1)}, f32[12288,128]{1,0:T(8,128)S(1)}) custom-call(bf16[96,3072]{1,0:T(8,128)(2,1)S(1)} %get-tuple-element.42.refs_0_, bf16[96,12288]{1,0:T(8,128)(2,1)} %refs_1_.2, s32[8,1,1280]{2,1,0:T(1,128)S(1)} %get-tuple-element.43.refs_2_.refs_6_.refs_0_), custom_call_target="tpu_custom_call" | custom-call | flops 6600000000 | tf_op jit(solution)/shard_map/mean/pallas_call | solution.py:468
  14.7 0.0 collective-permute-done.refs_1_.refs_0_.refs_2_
  14.7 0.2 collective-permute-done.1.refs_2_.refs_1_.refs_3_
  15.0 0.0 collective-permute-done.2.refs_3_.refs_2_.refs_4_
  15.0 0.1 collective-permute-start.6
  15.1 2.7 %collective-permute-start.3 = (bf16[160,128]{1,0:T(8,128)(2,1)S(1)}, bf16[160,128]{1,0:T(8,128)(2,1)S(1)}, u32[]{:S(2)}, u32[]{:S(2)}) collective-permute-start(bf16[160,128]{1,0:T(8,128)(2,1)S(1)} %get-tuple-element.47), channel_id=1, source_target_pairs={{0,6},{2,4},{4,2},{6,0},{8,14},{10,12},{12,10},{14,8},{1,7},{3,5},... | collective-permute-start | bytes 122888 | tf_op jit(solution)/shard_map/ppermute | solution.py:433
  17.8 0.5 collective-permute-start.4
  18.2 0.4 collective-permute-start.5
  18.7 0.0 collective-permute-done.6.refs_4_
  18.7 0.0 copy-done.2
  18.7 2.6 %mean.5 = (bf16[144,128]{1,0:T(8,128)(2,1)S(1)}, bf16[4,96,512]{2,1,0:T(8,128)(2,1)S(1)}, f32[192,512]{1,0:T(8,128)S(1)}, f32[192,512]{1,0:T(8,128)S(1)}, bf16[16,512]{1,0:T(8,128)(2,1)S(1)}) custom-call(bf16[176,512]{1,0:T(8,128)(2,1)S(1)} %collective-permute-done.refs_1_.refs_0_.refs_2_, ...), custom_call_target="tpu_custom_call" | custom-call | tf_op jit(solution)/shard_map/mean/pallas_call | solution.py:468
  21.3 0.0 collective-permute-done.3.refs_0_.refs_2_
  21.3 0.5 collective-permute-done.4.refs_1_.refs_3_
  21.8 0.5 collective-permute-done.5.refs_2_.refs_4_
  22.2 0.4 far.1.refs_5_.refs_9_
  22.6 0.0 copy-start
  22.6 0.0 copy-start.1
  22.6 2.7 %collective-permute-start.7 = (bf16[208,512]{1,0:T(8,128)(2,1)S(1)}, bf16[208,512]{1,0:T(8,128)(2,1)S(1)}, u32[]{:S(2)}, u32[]{:S(2)}) collective-permute-start(bf16[208,512]{1,0:T(8,128)(2,1)S(1)} %far.1.refs_5_.refs_9_), channel_id=1, source_target_pairs={{0,8},{2,10},{4,12},{6,14},{8,0},{10,2},{12,4},{14,6},{1,9},{3,11}... | collective-permute-start | bytes 638984 | tf_op jit(solution)/shard_map/ppermute | solution.py:433
  25.3 4.2 %mean.6 = (bf16[144,128]{1,0:T(8,128)(2,1)S(1)}, bf16[144,128]{1,0:T(8,128)(2,1)S(1)}, bf16[144,128]{1,0:T(8,128)(2,1)S(1)}) custom-call(s32[8,1,1280]{2,1,0:T(1,128)S(1)} %get-tuple-element.43.refs_2_.refs_6_.refs_0_, f32[12288,1,128]{2,1,0:T(1,128)S(1)} %bitcast.8, bf16[160,128]{1,0:T(8,128)(2,1)S(1)} %collective-permute-done.3.refs_0_.refs_2_, ...), custom_call_target="tpu_custom_call" | custom-call | flops 6600000000 | tf_op jit(solution)/shard_map/mean/pallas_call | solution.py:468
  29.5 1.7 %collective-permute-start.8 = (bf16[144,128]{1,0:T(8,128)(2,1)S(1)}, bf16[144,128]{1,0:T(8,128)(2,1)S(1)}, u32[]{:S(2)}, u32[]{:S(2)}) collective-permute-start(bf16[144,128]{1,0:T(8,128)(2,1)S(1)} %get-tuple-element.57), channel_id=1, source_target_pairs={{0,6},{2,4},{4,2},{6,0},{8,14},{10,12},{12,10},{14,8},{1,7},{3,5},... | collective-permute-start | bytes 110600 | tf_op jit(solution)/shard_map/ppermute | solution.py:433
  31.3 0.9 %collective-permute-start.9 = (bf16[144,128]{1,0:T(8,128)(2,1)S(1)}, bf16[144,128]{1,0:T(8,128)(2,1)S(1)}, u32[]{:S(2)}, u32[]{:S(2)}) collective-permute-start(bf16[144,128]{1,0:T(8,128)(2,1)S(1)} %get-tuple-element.58), channel_id=1, source_target_pairs={{0,4},{2,6},{4,0},{6,2},{8,12},{10,14},{12,8},{14,10},{1,5},{3,7},... | collective-permute-start | bytes 110600 | tf_op jit(solution)/shard_map/ppermute | solution.py:433
  32.1 1.1 %collective-permute-start.10 = (bf16[144,128]{1,0:T(8,128)(2,1)S(1)}, bf16[144,128]{1,0:T(8,128)(2,1)S(1)}, u32[]{:S(2)}, u32[]{:S(2)}) collective-permute-start(bf16[144,128]{1,0:T(8,128)(2,1)S(1)} %get-tuple-element.59), channel_id=1, source_target_pairs={{0,2},{2,0},{4,6},{6,4},{8,10},{10,8},{12,14},{14,12},{1,3},{3,1},... | collective-permute-start | bytes 110600 | tf_op jit(solution)/shard_map/ppermute | solution.py:433
  33.2 0.0 copy-done
  33.2 0.0 copy-done.1
  33.2 2.3 %mean.7 = (bf16[144,128]{1,0:T(8,128)(2,1)S(1)}, bf16[256,768]{1,0:T(8,128)(2,1)S(1)}) custom-call(bf16[512,512]{1,0:T(8,128)(2,1)S(1)} %copy-done, bf16[512,512]{1,0:T(8,128)(2,1)S(1)} %copy-done.1, bf16[176,512]{1,0:T(8,128)(2,1)S(1)} %collective-permute-done.refs_1_.refs_0_.refs_2_, bf16[176,512]{1,0:T(8,128)(2,1)S(1)} %collective-permute-done.1.refs_2_.refs_1_.refs_3_, ...), custom_call_target="tpu_custom_call" | custom-call | tf_op jit(solution)/shard_map/mean/pallas_call | solution.py:468
  35.5 0.3 collective-permute-done.8.refs_0_
  35.8 0.0 collective-permute-done.9.refs_1_
  35.8 0.4 collective-permute-done.10.refs_2_
  36.2 0.4 near.1.refs_1_
  36.5 0.0 collective-permute-done.7.refs_2_.refs_0_
  36.6 0.2 hidden.1.refs_1_
  36.7 0.1 collective-permute-start.11
  36.8 0.9 %far_times.1 = (bf16[256,768]{1,0:T(8,128)(2,1)S(1)}, bf16[2,192,512]{2,1,0:T(8,128)(2,1)S(1)}, bf16[192,512]{1,0:T(8,128)(2,1)}) custom-call(bf16[208,512]{1,0:T(8,128)(2,1)S(1)} %collective-permute-done.7.refs_2_.refs_0_, bf16[192,512]{1,0:T(8,128)(2,1)S(1)} %hidden.1.refs_1_, bf16[512,512]{1,0:T(8,128)(2,1)S(1)} %copy-done, bf16[512,512]{1,0:T(8,128)(2,1)S(1)} %copy-done.1), custom_call_target="tpu_custom_call" | custom-call | flops 1100000000 | tf_op jit(solution)/shard_map/far_times/pallas_call | solution.py:468
  37.7 0.6 %collective-permute-done.11.refs_2_ = bf16[192,512]{1,0:T(8,128)(2,1)S(1)} collective-permute-done((bf16[192,512]{1,0:T(8,128)(2,1)S(1)}, bf16[192,512]{1,0:T(8,128)(2,1)S(1)}, u32[]{:S(2)}, u32[]{:S(2)}) %collective-permute-start.11) | collective-permute-done | bytes 196640 | tf_op jit(solution)/shard_map/ppermute | solution.py:433
  38.2 0.6 %far_share.1 = (bf16[64,512]{1,0:T(8,128)(2,1)S(1)}, bf16[64,512]{1,0:T(8,128)(2,1)S(1)}, bf16[64,512]{1,0:T(8,128)(2,1)S(1)}, bf16[64,512]{1,0:T(8,128)(2,1)S(1)}, bf16[768,512]{1,0:T(8,128)(2,1)S(1)}) custom-call(bf16[256,768]{1,0:T(8,128)(2,1)S(1)} %get-tuple-element.64.refs_0_, bf16[2,192,512]{2,1,0:T(8,128)(2,1)S(1)} %get-tuple-element.65.refs_1_, ...), custom_call_target="tpu_custom_call" | custom-call | flops 1100000000 | tf_op jit(solution)/shard_map/far_share/pallas_call | solution.py:468
  38.8 0.0 copy-start.3
  38.8 2.5 %collective-permute-start.14 = (bf16[64,512]{1,0:T(8,128)(2,1)S(1)}, bf16[64,512]{1,0:T(8,128)(2,1)S(1)}, u32[]{:S(2)}, u32[]{:S(2)}) collective-permute-start(bf16[64,512]{1,0:T(8,128)(2,1)S(1)} %get-tuple-element.69), channel_id=1, source_target_pairs={{0,6},{2,4},{4,2},{6,0},{8,14},{10,12},{12,10},{14,8},{1,7},{3,5},... | collective-permute-start | bytes 196616 | tf_op jit(solution)/shard_map/ppermute | solution.py:433
  41.3 0.0 collective-permute-start.15
  41.4 1.0 %collective-permute-start.16 = (bf16[64,512]{1,0:T(8,128)(2,1)S(1)}, bf16[64,512]{1,0:T(8,128)(2,1)S(1)}, u32[]{:S(2)}, u32[]{:S(2)}) collective-permute-start(bf16[64,512]{1,0:T(8,128)(2,1)S(1)} %get-tuple-element.71), channel_id=1, source_target_pairs={{0,2},{2,0},{4,6},{6,4},{8,10},{10,8},{12,14},{14,12},{1,3},{3,1},... | collective-permute-start | bytes 196616 | tf_op jit(solution)/shard_map/ppermute | solution.py:433
  42.4 0.5 %near_share.2 = (bf16[64,512]{1,0:T(8,128)(2,1)S(1)}, bf16[64,512]{1,0:T(8,128)(2,1)S(1)}, bf16[64,512]{1,0:T(8,128)(2,1)S(1)}) custom-call(bf16[256,768]{1,0:T(8,128)(2,1)S(1)} %get-tuple-element.63.refs_0_, bf16[768,512]{1,0:T(8,128)(2,1)S(1)} %get-tuple-element.66.refs_1_), custom_call_target="tpu_custom_call" | custom-call | flops 1100000000 | tf_op jit(solution)/shard_map/near_share/pallas_call | solution.py:468
  42.9 2.5 %collective-permute-start.12 = (bf16[64,512]{1,0:T(8,128)(2,1)S(1)}, bf16[64,512]{1,0:T(8,128)(2,1)S(1)}, u32[]{:S(2)}, u32[]{:S(2)}) collective-permute-start(bf16[64,512]{1,0:T(8,128)(2,1)S(1)} %get-tuple-element.67), channel_id=1, source_target_pairs={{0,6},{2,4},{4,2},{6,0},{8,14},{10,12},{12,10},{14,8},{1,7},{3,5},... | collective-permute-start | bytes 196616 | tf_op jit(solution)/shard_map/ppermute | solution.py:433
  45.4 0.0 collective-permute-start.13
  45.4 0.0 collective-permute-done.14.refs_0_
  45.4 0.3 collective-permute-done.15.refs_1_
  45.7 0.0 collective-permute-done.16.refs_2_
  45.7 1.4 %collective-permute-start.18 = (bf16[72,512]{1,0:T(8,128)(2,1)S(1)}, bf16[72,512]{1,0:T(8,128)(2,1)S(1)}, u32[]{:S(2)}, u32[]{:S(2)}) collective-permute-start(bf16[72,512]{1,0:T(8,128)(2,1)S(1)} %side_sum.1.refs_2_), channel_id=1, source_target_pairs={{0,8},{2,10},{4,12},{6,14},{8,0},{10,2},{12,4},{14,6},{1,9},{3,11}... | collective-permute-start | bytes 221192 | tf_op jit(solution)/shard_map/ppermute | solution.py:433
  47.1 0.2 near_share.3
  47.4 1.3 %collective-permute-start.17 = (bf16[64,512]{1,0:T(8,128)(2,1)S(1)}, bf16[64,512]{1,0:T(8,128)(2,1)S(1)}, u32[]{:S(2)}, u32[]{:S(2)}) collective-permute-start(bf16[64,512]{1,0:T(8,128)(2,1)S(1)} %near_share.3), channel_id=1, source_target_pairs={{0,2},{2,0},{4,6},{6,4},{8,10},{10,8},{12,14},{14,12},{1,3},{3,1},... | collective-permute-start | bytes 196616 | tf_op jit(solution)/shard_map/ppermute | solution.py:433
  48.7 0.0 collective-permute-done.12.refs_1_
  48.7 1.5 %collective-permute-done.13.refs_2_ = bf16[64,512]{1,0:T(8,128)(2,1)S(1)} collective-permute-done((bf16[64,512]{1,0:T(8,128)(2,1)S(1)}, bf16[64,512]{1,0:T(8,128)(2,1)S(1)}, u32[]{:S(2)}, u32[]{:S(2)}) %collective-permute-start.13) | collective-permute-done | bytes 65568 | tf_op jit(solution)/shard_map/ppermute | solution.py:433
  50.2 1.5 %collective-permute-done.17.refs_3_ = bf16[64,512]{1,0:T(8,128)(2,1)S(1)} collective-permute-done((bf16[64,512]{1,0:T(8,128)(2,1)S(1)}, bf16[64,512]{1,0:T(8,128)(2,1)S(1)}, u32[]{:S(2)}, u32[]{:S(2)}) %collective-permute-start.17) | collective-permute-done | bytes 65568 | tf_op jit(solution)/shard_map/ppermute | solution.py:433
  51.7 0.0 collective-permute-done.18.refs_5_
  51.7 0.0 copy-done.3
  51.7 0.7 %seeds.1 = bf16[64,512]{1,0:T(8,128)(2,1)} custom-call(f32[1,512]{1,0:T(1,128)S(1)} %bitcast.11, bf16[64,512]{1,0:T(8,128)(2,1)S(1)} %collective-permute-done.12.refs_1_, bf16[64,512]{1,0:T(8,128)(2,1)S(1)} %collective-permute-done.13.refs_2_, bf16[64,512]{1,0:T(8,128)(2,1)S(1)} %collective-permute-done.17.refs_3_, ...), custom_call_target="tpu_custom_call" | custom-call | flops 1100000000 | tf_op jit(solution)/shard_map/seeds/pallas_call | solution.py:468
  (2 shorter events, 0.1 us)
Async XLA Ops:
  2.3 12.4 %collective-permute-start = (bf16[176,512]{1,0:T(8,128)(2,1)S(1)}, bf16[176,512]{1,0:T(8,128)(2,1)S(1)}, u32[]{:S(2)}, u32[]{:S(2)}) collective-permute-start(bf16[176,512]{1,0:T(8,128)(2,1)S(1)} %get-tuple-element.38), channel_id=1, source_target_pairs={{0,6},{2,4},{4,2},{6,0},{8,14},{10,12},{12,10},{14,8},{1,7},{3,5},... | collective-permute-start | bytes 540680 | tf_op jit(solution)/shard_map/ppermute | solution.py:433
  6.4 8.6 %collective-permute-start.1 = (bf16[176,512]{1,0:T(8,128)(2,1)S(1)}, bf16[176,512]{1,0:T(8,128)(2,1)S(1)}, u32[]{:S(2)}, u32[]{:S(2)}) collective-permute-start(bf16[176,512]{1,0:T(8,128)(2,1)S(1)} %get-tuple-element.39), channel_id=1, source_target_pairs={{0,4},{2,6},{4,0},{6,2},{8,12},{10,14},{12,8},{14,10},{1,5},{3,7},... | collective-permute-start | bytes 540680 | tf_op jit(solution)/shard_map/ppermute | solution.py:433
  6.8 8.2 %collective-permute-start.2 = (bf16[176,512]{1,0:T(8,128)(2,1)S(1)}, bf16[176,512]{1,0:T(8,128)(2,1)S(1)}, u32[]{:S(2)}, u32[]{:S(2)}) collective-permute-start(bf16[176,512]{1,0:T(8,128)(2,1)S(1)} %get-tuple-element.40), channel_id=1, source_target_pairs={{0,2},{2,0},{4,6},{6,4},{8,10},{10,8},{12,14},{14,12},{1,3},{3,1},... | collective-permute-start | bytes 540680 | tf_op jit(solution)/shard_map/ppermute | solution.py:433
  7.0 11.7 %copy-start.2 = (f32[512]{0:T(512)S(1)}, f32[512]{0:T(512)}, u32[]{:S(2)}) copy-start(f32[512]{0:T(512)} %param.18) | copy-start | bytes 6148
  15.0 3.6 %collective-permute-start.6 = (bf16[4,96,512]{2,1,0:T(8,128)(2,1)S(1)}, bf16[4,96,512]{2,1,0:T(8,128)(2,1)S(1)}, u32[]{:S(2)}, u32[]{:S(2)}) collective-permute-start(bf16[4,96,512]{2,1,0:T(8,128)(2,1)S(1)} %get-tuple-element.50), channel_id=1, source_target_pairs={{0,1},{1,0},{2,3},{3,2},{4,5},{5,4},{6,7},{7,6},{8,9},{9,8},{10,11... | collective-permute-start | bytes 1179656 | tf_op jit(solution)/shard_map/ppermute | solution.py:433
  15.1 6.2 %collective-permute-start.3 = (bf16[160,128]{1,0:T(8,128)(2,1)S(1)}, bf16[160,128]{1,0:T(8,128)(2,1)S(1)}, u32[]{:S(2)}, u32[]{:S(2)}) collective-permute-start(bf16[160,128]{1,0:T(8,128)(2,1)S(1)} %get-tuple-element.47), channel_id=1, source_target_pairs={{0,6},{2,4},{4,2},{6,0},{8,14},{10,12},{12,10},{14,8},{1,7},{3,5},... | collective-permute-start | bytes 122888 | tf_op jit(solution)/shard_map/ppermute | solution.py:433
  17.8 4.0 %collective-permute-start.4 = (bf16[160,128]{1,0:T(8,128)(2,1)S(1)}, bf16[160,128]{1,0:T(8,128)(2,1)S(1)}, u32[]{:S(2)}, u32[]{:S(2)}) collective-permute-start(bf16[160,128]{1,0:T(8,128)(2,1)S(1)} %get-tuple-element.48), channel_id=1, source_target_pairs={{0,4},{2,6},{4,0},{6,2},{8,12},{10,14},{12,8},{14,10},{1,5},{3,7},... | collective-permute-start | bytes 122888 | tf_op jit(solution)/shard_map/ppermute | solution.py:433
  18.2 4.0 %collective-permute-start.5 = (bf16[160,128]{1,0:T(8,128)(2,1)S(1)}, bf16[160,128]{1,0:T(8,128)(2,1)S(1)}, u32[]{:S(2)}, u32[]{:S(2)}) collective-permute-start(bf16[160,128]{1,0:T(8,128)(2,1)S(1)} %get-tuple-element.49), channel_id=1, source_target_pairs={{0,2},{2,0},{4,6},{6,4},{8,10},{10,8},{12,14},{14,12},{1,3},{3,1},... | collective-permute-start | bytes 122888 | tf_op jit(solution)/shard_map/ppermute | solution.py:433
  22.6 10.6 %copy-start = (bf16[512,512]{1,0:T(8,128)(2,1)S(1)}, bf16[512,512]{1,0:T(8,128)(2,1)}, u32[]{:S(2)}) copy-start(bf16[512,512]{1,0:T(8,128)(2,1)} %refs_3_.5) | copy-start | bytes 1572868
  22.6 10.6 %copy-start.1 = (bf16[512,512]{1,0:T(8,128)(2,1)S(1)}, bf16[512,512]{1,0:T(8,128)(2,1)}, u32[]{:S(2)}) copy-start(bf16[512,512]{1,0:T(8,128)(2,1)} %refs_4_.3) | copy-start | bytes 1572868
  22.6 13.9 %collective-permute-start.7 = (bf16[208,512]{1,0:T(8,128)(2,1)S(1)}, bf16[208,512]{1,0:T(8,128)(2,1)S(1)}, u32[]{:S(2)}, u32[]{:S(2)}) collective-permute-start(bf16[208,512]{1,0:T(8,128)(2,1)S(1)} %far.1.refs_5_.refs_9_), channel_id=1, source_target_pairs={{0,8},{2,10},{4,12},{6,14},{8,0},{10,2},{12,4},{14,6},{1,9},{3,11}... | collective-permute-start | bytes 638984 | tf_op jit(solution)/shard_map/ppermute | solution.py:433
  29.5 6.3 %collective-permute-start.8 = (bf16[144,128]{1,0:T(8,128)(2,1)S(1)}, bf16[144,128]{1,0:T(8,128)(2,1)S(1)}, u32[]{:S(2)}, u32[]{:S(2)}) collective-permute-start(bf16[144,128]{1,0:T(8,128)(2,1)S(1)} %get-tuple-element.57), channel_id=1, source_target_pairs={{0,6},{2,4},{4,2},{6,0},{8,14},{10,12},{12,10},{14,8},{1,7},{3,5},... | collective-permute-start | bytes 110600 | tf_op jit(solution)/shard_map/ppermute | solution.py:433
  31.3 4.5 %collective-permute-start.9 = (bf16[144,128]{1,0:T(8,128)(2,1)S(1)}, bf16[144,128]{1,0:T(8,128)(2,1)S(1)}, u32[]{:S(2)}, u32[]{:S(2)}) collective-permute-start(bf16[144,128]{1,0:T(8,128)(2,1)S(1)} %get-tuple-element.58), channel_id=1, source_target_pairs={{0,4},{2,6},{4,0},{6,2},{8,12},{10,14},{12,8},{14,10},{1,5},{3,7},... | collective-permute-start | bytes 110600 | tf_op jit(solution)/shard_map/ppermute | solution.py:433
  32.1 4.1 %collective-permute-start.10 = (bf16[144,128]{1,0:T(8,128)(2,1)S(1)}, bf16[144,128]{1,0:T(8,128)(2,1)S(1)}, u32[]{:S(2)}, u32[]{:S(2)}) collective-permute-start(bf16[144,128]{1,0:T(8,128)(2,1)S(1)} %get-tuple-element.59), channel_id=1, source_target_pairs={{0,2},{2,0},{4,6},{6,4},{8,10},{10,8},{12,14},{14,12},{1,3},{3,1},... | collective-permute-start | bytes 110600 | tf_op jit(solution)/shard_map/ppermute | solution.py:433
  36.7 1.5 %collective-permute-start.11 = (bf16[192,512]{1,0:T(8,128)(2,1)S(1)}, bf16[192,512]{1,0:T(8,128)(2,1)S(1)}, u32[]{:S(2)}, u32[]{:S(2)}) collective-permute-start(bf16[192,512]{1,0:T(8,128)(2,1)S(1)} %hidden.1.refs_1_), channel_id=1, source_target_pairs={{0,1},{1,0},{2,3},{3,2},{4,5},{5,4},{6,7},{7,6},{8,9},{9,8},{10,11... | collective-permute-start | bytes 589832 | tf_op jit(solution)/shard_map/ppermute | solution.py:433
  38.8 12.9 %copy-start.3 = (f32[512]{0:T(512)S(1)}, f32[512]{0:T(512)}, u32[]{:S(2)}) copy-start(f32[512]{0:T(512)} %param.21) | copy-start | bytes 6148
  38.8 6.6 %collective-permute-start.14 = (bf16[64,512]{1,0:T(8,128)(2,1)S(1)}, bf16[64,512]{1,0:T(8,128)(2,1)S(1)}, u32[]{:S(2)}, u32[]{:S(2)}) collective-permute-start(bf16[64,512]{1,0:T(8,128)(2,1)S(1)} %get-tuple-element.69), channel_id=1, source_target_pairs={{0,6},{2,4},{4,2},{6,0},{8,14},{10,12},{12,10},{14,8},{1,7},{3,5},... | collective-permute-start | bytes 196616 | tf_op jit(solution)/shard_map/ppermute | solution.py:433
  41.3 4.4 %collective-permute-start.15 = (bf16[64,512]{1,0:T(8,128)(2,1)S(1)}, bf16[64,512]{1,0:T(8,128)(2,1)S(1)}, u32[]{:S(2)}, u32[]{:S(2)}) collective-permute-start(bf16[64,512]{1,0:T(8,128)(2,1)S(1)} %get-tuple-element.70), channel_id=1, source_target_pairs={{0,4},{2,6},{4,0},{6,2},{8,12},{10,14},{12,8},{14,10},{1,5},{3,7},... | collective-permute-start | bytes 196616 | tf_op jit(solution)/shard_map/ppermute | solution.py:433
  41.4 4.3 %collective-permute-start.16 = (bf16[64,512]{1,0:T(8,128)(2,1)S(1)}, bf16[64,512]{1,0:T(8,128)(2,1)S(1)}, u32[]{:S(2)}, u32[]{:S(2)}) collective-permute-start(bf16[64,512]{1,0:T(8,128)(2,1)S(1)} %get-tuple-element.71), channel_id=1, source_target_pairs={{0,2},{2,0},{4,6},{6,4},{8,10},{10,8},{12,14},{14,12},{1,3},{3,1},... | collective-permute-start | bytes 196616 | tf_op jit(solution)/shard_map/ppermute | solution.py:433
  42.9 5.8 %collective-permute-start.12 = (bf16[64,512]{1,0:T(8,128)(2,1)S(1)}, bf16[64,512]{1,0:T(8,128)(2,1)S(1)}, u32[]{:S(2)}, u32[]{:S(2)}) collective-permute-start(bf16[64,512]{1,0:T(8,128)(2,1)S(1)} %get-tuple-element.67), channel_id=1, source_target_pairs={{0,6},{2,4},{4,2},{6,0},{8,14},{10,12},{12,10},{14,8},{1,7},{3,5},... | collective-permute-start | bytes 196616 | tf_op jit(solution)/shard_map/ppermute | solution.py:433
  45.4 4.8 %collective-permute-start.13 = (bf16[64,512]{1,0:T(8,128)(2,1)S(1)}, bf16[64,512]{1,0:T(8,128)(2,1)S(1)}, u32[]{:S(2)}, u32[]{:S(2)}) collective-permute-start(bf16[64,512]{1,0:T(8,128)(2,1)S(1)} %get-tuple-element.68), channel_id=1, source_target_pairs={{0,4},{2,6},{4,0},{6,2},{8,12},{10,14},{12,8},{14,10},{1,5},{3,7},... | collective-permute-start | bytes 196616 | tf_op jit(solution)/shard_map/ppermute | solution.py:433
  45.7 6.0 %collective-permute-start.18 = (bf16[72,512]{1,0:T(8,128)(2,1)S(1)}, bf16[72,512]{1,0:T(8,128)(2,1)S(1)}, u32[]{:S(2)}, u32[]{:S(2)}) collective-permute-start(bf16[72,512]{1,0:T(8,128)(2,1)S(1)} %side_sum.1.refs_2_), channel_id=1, source_target_pairs={{0,8},{2,10},{4,12},{6,14},{8,0},{10,2},{12,4},{14,6},{1,9},{3,11}... | collective-permute-start | bytes 221192 | tf_op jit(solution)/shard_map/ppermute | solution.py:433
  47.4 4.3 %collective-permute-start.17 = (bf16[64,512]{1,0:T(8,128)(2,1)S(1)}, bf16[64,512]{1,0:T(8,128)(2,1)S(1)}, u32[]{:S(2)}, u32[]{:S(2)}) collective-permute-start(bf16[64,512]{1,0:T(8,128)(2,1)S(1)} %near_share.3), channel_id=1, source_target_pairs={{0,2},{2,0},{4,6},{6,4},{8,10},{10,8},{12,14},{14,12},{1,3},{3,1},... | collective-permute-start | bytes 196616 | tf_op jit(solution)/shard_map/ppermute | solution.py:433

commit v20 on v18

--- a/solution.py
+++ b/solution.py
@@ -409,17 +409,21 @@
     store_shares(near_ref, values_ref, out_refs)
 
 
+def copy_kernel(in_ref, out_ref):
+    out_ref[...] = in_ref[...]
+
+
 def side_sum_kernel(*refs):
     total = refs[0][...].astype(jnp.float32)
     for ref in refs[1:-1]:
         total = total + ref[...].astype(jnp.float32)
-    refs[-1][...] = total.astype(jnp.bfloat16)
+    refs[-1][: total.shape[0], :] = total.astype(jnp.bfloat16)
 
 
 def last_kernel(bias_ref, *refs):
     total = bias_ref[...]
     for ref in refs[:-1]:
-        total = total + ref[...].astype(jnp.float32)
+        total = total + ref[: refs[-1].shape[0], :].astype(jnp.float32)
     refs[-1][...] = jnp.maximum(total, 0.0).astype(jnp.bfloat16)
 
 
@@ -628,7 +632,7 @@
         limit=32 * MIB,
     )
     far_shares = send(far_shares)
-    near_shares = call(
+    *near_shares, near_late, near_last = call(
         near_share_kernel,
         "near_share",
         [((seed_count, width), bf16)] * half,
@@ -636,16 +640,25 @@
         (near_times, values),
         limit=32 * MIB,
     )
-    near_shares = send(near_shares)
+    near_shares = [swap(share, "feat", s) for share, s in zip(near_shares, steps)]
     (far_sum,) = call(
-        side_sum_kernel, "side_sum", [((seed_count, width), bf16)], [vmem] * half, far_shares
+        side_sum_kernel, "side_sum", [((seed_count + 8, width), bf16)], [vmem] * half, far_shares
+    )
+    (near_late,) = call(
+        copy_kernel, "late", [((seed_count, width), bf16)], [vmem], (near_late,), after=(far_sum,)
     )
     (seed_out,) = call(
         last_kernel,
         "seeds",
         [((seed_count, width), bf16)],
         [vmem] * (half + 2),
-        (bias_two[None], *near_shares, swap(far_sum, "feat", half)),
+        (
+            bias_two[None],
+            *near_shares,
+            swap(near_late, "feat", 1),
+            near_last,
+            swap(far_sum, "feat", half),
+        ),
     )
     return (result[None, None], seed_out)
 

time: 53.3 us -> 53.8 us (level); the launches traced: 52.9 us -> 54.1 us
  waiting for transfers between devices: 6.62 us -> 8.19 us
    ppermute x19, waiting for transfers between devices: 6.62 us -> 8.19 us  [swap(): return lax.ppermute(value, axis, [(i, i ^ step) for i in range(size)])]
    pallas_call x14 -> x15, Pallas kernels: 21.7 us -> 21.6 us  [call(): pl.pallas_call(wrapped, out_shape=tuple((jax.ShapeDtypeStruct(shape, dtyp...]
  transfers between devices with their start and end apart: 19 -> 19, of which waited for: 8 -> 10; matrix products, arithmetic and copies ran while one was open for 0% -> 0% of each run, Pallas kernels for 34% -> 33%
where the time goes in v20:
time: 53.8 us; the launch traced here: 54.1 us
  starting transfers between devices  22.8 us (42%)
  Pallas kernels  21.6 us (40%)
  waiting for transfers between devices  8.19 us (15%)
  between operations  1.47 us (3%)
    ppermute x19, starting transfers between devices, swap(): return lax.ppermute(value, axis, [(i, i ^ step) for i in range(size)])  22.8 us
    pallas_call x15, Pallas kernels, call(): pl.pallas_call(wrapped, out_shape=tuple((jax.ShapeDtypeStruct(shape, dtyp...  21.6 us
    ppermute x19, waiting for transfers between devices, swap(): return lax.ppermute(value, axis, [(i, i ^ step) for i in range(size)])  8.19 us
  transfers between devices with their start and end apart: 19, of which 10 were waited for; matrix products, arithmetic and copies ran while one was open for 0% of the time, Pallas kernels for 33%

profile of v20, /device:TPU:0, one launch (start us, length us, event | category | flops | bytes accessed | tf_op | source)
XLA Modules:
  0.0 54.1 jit_solution(13393664936195771549)
XLA Ops:
  0.6 1.7 %pack.1 = (bf16[176,512]{1,0:T(8,128)(2,1)S(1)}, bf16[176,512]{1,0:T(8,128)(2,1)S(1)}, bf16[176,512]{1,0:T(8,128)(2,1)S(1)}, bf16[176,512]{1,0:T(8,128)(2,1)S(1)...) custom-call(bf16[96,12288]{1,0:T(8,128)(2,1)} %refs_1_.2, s32[1,64]{1,0:T(1,128)} %bitcast.14, ...), custom_call_target="tpu_custom_call" | custom-call | flops 1100000000 | tf_op jit(solution)/shard_map/pack/pallas_call | solution.py:467
  2.3 4.0 %collective-permute-start = (bf16[176,512]{1,0:T(8,128)(2,1)S(1)}, bf16[176,512]{1,0:T(8,128)(2,1)S(1)}, u32[]{:S(2)}, u32[]{:S(2)}) collective-permute-start(bf16[176,512]{1,0:T(8,128)(2,1)S(1)} %get-tuple-element.39), channel_id=1, source_target_pairs={{0,6},{2,4},{4,2},{6,0},{8,14},{10,12},{12,10},{14,8},{1,7},{3,5},... | collective-permute-start | bytes 540680 | tf_op jit(solution)/shard_map/ppermute | solution.py:432
  6.4 0.5 collective-permute-start.1
  6.8 0.2 collective-permute-start.2
  7.0 0.0 copy-start.2
  7.0 7.1 %mean.4 = (bf16[144,128]{1,0:T(8,128)(2,1)S(1)}, bf16[144,128]{1,0:T(8,128)(2,1)S(1)}, bf16[144,128]{1,0:T(8,128)(2,1)S(1)}, f32[12288,128]{1,0:T(8,128)S(1)}) custom-call(bf16[96,3072]{1,0:T(8,128)(2,1)S(1)} %get-tuple-element.43.refs_0_, bf16[96,12288]{1,0:T(8,128)(2,1)} %refs_1_.2, s32[8,1,1280]{2,1,0:T(1,128)S(1)} %get-tuple-element.44.refs_2_.refs_6_.refs_0_), custom_call_target="tpu_custom_call" | custom-call | flops 6600000000 | tf_op jit(solution)/shard_map/mean/pallas_call | solution.py:467
  14.7 0.0 collective-permute-done.refs_1_.refs_0_.refs_2_
  14.7 0.2 collective-permute-done.1.refs_2_.refs_1_.refs_3_
  15.0 0.0 collective-permute-done.2.refs_3_.refs_2_.refs_4_
  15.0 0.1 collective-permute-start.6
  15.1 2.7 %collective-permute-start.3 = (bf16[160,128]{1,0:T(8,128)(2,1)S(1)}, bf16[160,128]{1,0:T(8,128)(2,1)S(1)}, u32[]{:S(2)}, u32[]{:S(2)}) collective-permute-start(bf16[160,128]{1,0:T(8,128)(2,1)S(1)} %get-tuple-element.48), channel_id=1, source_target_pairs={{0,6},{2,4},{4,2},{6,0},{8,14},{10,12},{12,10},{14,8},{1,7},{3,5},... | collective-permute-start | bytes 122888 | tf_op jit(solution)/shard_map/ppermute | solution.py:432
  17.8 0.5 collective-permute-start.4
  18.2 0.4 collective-permute-start.5
  18.7 0.0 collective-permute-done.6.refs_4_
  18.7 0.0 copy-done.2
  18.7 2.6 %mean.5 = (bf16[144,128]{1,0:T(8,128)(2,1)S(1)}, bf16[4,96,512]{2,1,0:T(8,128)(2,1)S(1)}, f32[192,512]{1,0:T(8,128)S(1)}, f32[192,512]{1,0:T(8,128)S(1)}, bf16[16,512]{1,0:T(8,128)(2,1)S(1)}) custom-call(bf16[176,512]{1,0:T(8,128)(2,1)S(1)} %collective-permute-done.refs_1_.refs_0_.refs_2_, ...), custom_call_target="tpu_custom_call" | custom-call | tf_op jit(solution)/shard_map/mean/pallas_call | solution.py:467
  21.3 0.0 collective-permute-done.3.refs_0_.refs_2_
  21.3 0.5 collective-permute-done.4.refs_1_.refs_3_
  21.8 0.5 collective-permute-done.5.refs_2_.refs_4_
  22.2 0.4 far.1.refs_5_.refs_9_
  22.6 0.0 copy-start
  22.6 0.0 copy-start.1
  22.6 2.7 %collective-permute-start.7 = (bf16[208,512]{1,0:T(8,128)(2,1)S(1)}, bf16[208,512]{1,0:T(8,128)(2,1)S(1)}, u32[]{:S(2)}, u32[]{:S(2)}) collective-permute-start(bf16[208,512]{1,0:T(8,128)(2,1)S(1)} %far.1.refs_5_.refs_9_), channel_id=1, source_target_pairs={{0,8},{2,10},{4,12},{6,14},{8,0},{10,2},{12,4},{14,6},{1,9},{3,11}... | collective-permute-start | bytes 638984 | tf_op jit(solution)/shard_map/ppermute | solution.py:432
  25.3 5.4 %mean.6 = (bf16[144,128]{1,0:T(8,128)(2,1)S(1)}, bf16[144,128]{1,0:T(8,128)(2,1)S(1)}, bf16[144,128]{1,0:T(8,128)(2,1)S(1)}) custom-call(s32[8,1,1280]{2,1,0:T(1,128)S(1)} %get-tuple-element.44.refs_2_.refs_6_.refs_0_, f32[12288,1,128]{2,1,0:T(1,128)S(1)} %bitcast.8, bf16[160,128]{1,0:T(8,128)(2,1)S(1)} %collective-permute-done.3.refs_0_.refs_2_, ...), custom_call_target="tpu_custom_call" | custom-call | flops 6600000000 | tf_op jit(solution)/shard_map/mean/pallas_call | solution.py:467
  30.7 0.5 collective-permute-start.8
  31.3 1.0 %collective-permute-start.9 = (bf16[144,128]{1,0:T(8,128)(2,1)S(1)}, bf16[144,128]{1,0:T(8,128)(2,1)S(1)}, u32[]{:S(2)}, u32[]{:S(2)}) collective-permute-start(bf16[144,128]{1,0:T(8,128)(2,1)S(1)} %get-tuple-element.59), channel_id=1, source_target_pairs={{0,4},{2,6},{4,0},{6,2},{8,12},{10,14},{12,8},{14,10},{1,5},{3,7},... | collective-permute-start | bytes 110600 | tf_op jit(solution)/shard_map/ppermute | solution.py:432
  32.2 2.0 %collective-permute-start.10 = (bf16[144,128]{1,0:T(8,128)(2,1)S(1)}, bf16[144,128]{1,0:T(8,128)(2,1)S(1)}, u32[]{:S(2)}, u32[]{:S(2)}) collective-permute-start(bf16[144,128]{1,0:T(8,128)(2,1)S(1)} %get-tuple-element.60), channel_id=1, source_target_pairs={{0,2},{2,0},{4,6},{6,4},{8,10},{10,8},{12,14},{14,12},{1,3},{3,1},... | collective-permute-start | bytes 110600 | tf_op jit(solution)/shard_map/ppermute | solution.py:432
  34.3 0.0 copy-done
  34.3 0.0 copy-done.1
  34.3 1.3 %mean.7 = (bf16[144,128]{1,0:T(8,128)(2,1)S(1)}, bf16[256,768]{1,0:T(8,128)(2,1)S(1)}) custom-call(bf16[512,512]{1,0:T(8,128)(2,1)S(1)} %copy-done, bf16[512,512]{1,0:T(8,128)(2,1)S(1)} %copy-done.1, bf16[176,512]{1,0:T(8,128)(2,1)S(1)} %collective-permute-done.refs_1_.refs_0_.refs_2_, bf16[176,512]{1,0:T(8,128)(2,1)S(1)} %collective-permute-done.1.refs_2_.refs_1_.refs_3_, ...), custom_call_target="tpu_custom_call" | custom-call | tf_op jit(solution)/shard_map/mean/pallas_call | solution.py:467
  35.6 0.2 collective-permute-done.8.refs_0_
  35.8 0.0 collective-permute-done.9.refs_1_
  35.8 0.4 collective-permute-done.10.refs_2_
  36.2 0.4 near.1.refs_1_
  36.6 0.0 collective-permute-done.7.refs_2_.refs_0_
  36.6 0.2 hidden.1.refs_1_
  36.8 0.1 collective-permute-start.11
  36.9 0.9 %far_times.1 = (bf16[256,768]{1,0:T(8,128)(2,1)S(1)}, bf16[2,192,512]{2,1,0:T(8,128)(2,1)S(1)}, bf16[192,512]{1,0:T(8,128)(2,1)}) custom-call(bf16[208,512]{1,0:T(8,128)(2,1)S(1)} %collective-permute-done.7.refs_2_.refs_0_, bf16[192,512]{1,0:T(8,128)(2,1)S(1)} %hidden.1.refs_1_, bf16[512,512]{1,0:T(8,128)(2,1)S(1)} %copy-done, bf16[512,512]{1,0:T(8,128)(2,1)S(1)} %copy-done.1), custom_call_target="tpu_custom_call" | custom-call | flops 1100000000 | tf_op jit(solution)/shard_map/far_times/pallas_call | solution.py:467
  37.7 0.6 %collective-permute-done.11.refs_2_ = bf16[192,512]{1,0:T(8,128)(2,1)S(1)} collective-permute-done((bf16[192,512]{1,0:T(8,128)(2,1)S(1)}, bf16[192,512]{1,0:T(8,128)(2,1)S(1)}, u32[]{:S(2)}, u32[]{:S(2)}) %collective-permute-start.11) | collective-permute-done | bytes 196640 | tf_op jit(solution)/shard_map/ppermute | solution.py:432
  38.3 0.6 %far_share.1 = (bf16[64,512]{1,0:T(8,128)(2,1)S(1)}, bf16[64,512]{1,0:T(8,128)(2,1)S(1)}, bf16[64,512]{1,0:T(8,128)(2,1)S(1)}, bf16[64,512]{1,0:T(8,128)(2,1)S(1)}, bf16[768,512]{1,0:T(8,128)(2,1)S(1)}) custom-call(bf16[256,768]{1,0:T(8,128)(2,1)S(1)} %get-tuple-element.65.refs_0_, bf16[2,192,512]{2,1,0:T(8,128)(2,1)S(1)} %get-tuple-element.66.refs_1_, ...), custom_call_target="tpu_custom_call" | custom-call | flops 1100000000 | tf_op jit(solution)/shard_map/far_share/pallas_call | solution.py:467
  38.9 0.0 copy-start.3
  38.9 1.9 %collective-permute-start.14 = (bf16[64,512]{1,0:T(8,128)(2,1)S(1)}, bf16[64,512]{1,0:T(8,128)(2,1)S(1)}, u32[]{:S(2)}, u32[]{:S(2)}) collective-permute-start(bf16[64,512]{1,0:T(8,128)(2,1)S(1)} %get-tuple-element.71), channel_id=1, source_target_pairs={{0,6},{2,4},{4,2},{6,0},{8,14},{10,12},{12,10},{14,8},{1,7},{3,5},... | collective-permute-start | bytes 196616 | tf_op jit(solution)/shard_map/ppermute | solution.py:432
  40.8 1.7 %collective-permute-start.15 = (bf16[64,512]{1,0:T(8,128)(2,1)S(1)}, bf16[64,512]{1,0:T(8,128)(2,1)S(1)}, u32[]{:S(2)}, u32[]{:S(2)}) collective-permute-start(bf16[64,512]{1,0:T(8,128)(2,1)S(1)} %get-tuple-element.72), channel_id=1, source_target_pairs={{0,4},{2,6},{4,0},{6,2},{8,12},{10,14},{12,8},{14,10},{1,5},{3,7},... | collective-permute-start | bytes 196616 | tf_op jit(solution)/shard_map/ppermute | solution.py:432
  42.5 0.0 collective-permute-start.16
  42.5 0.4 near_share.1
  42.8 1.9 %collective-permute-start.12 = (bf16[64,512]{1,0:T(8,128)(2,1)S(1)}, bf16[64,512]{1,0:T(8,128)(2,1)S(1)}, u32[]{:S(2)}, u32[]{:S(2)}) collective-permute-start(bf16[64,512]{1,0:T(8,128)(2,1)S(1)} %get-tuple-element.68), channel_id=1, source_target_pairs={{0,6},{2,4},{4,2},{6,0},{8,14},{10,12},{12,10},{14,8},{1,7},{3,5},... | collective-permute-start | bytes 196616 | tf_op jit(solution)/shard_map/ppermute | solution.py:432
  44.7 1.7 %collective-permute-start.13 = (bf16[64,512]{1,0:T(8,128)(2,1)S(1)}, bf16[64,512]{1,0:T(8,128)(2,1)S(1)}, u32[]{:S(2)}, u32[]{:S(2)}) collective-permute-start(bf16[64,512]{1,0:T(8,128)(2,1)S(1)} %get-tuple-element.69), channel_id=1, source_target_pairs={{0,4},{2,6},{4,0},{6,2},{8,12},{10,14},{12,8},{14,10},{1,5},{3,7},... | collective-permute-start | bytes 196616 | tf_op jit(solution)/shard_map/ppermute | solution.py:432
  46.4 0.0 collective-permute-done.14.refs_0_
  46.4 0.0 collective-permute-done.15.refs_1_
  46.4 1.0 %collective-permute-done.16.refs_2_ = bf16[64,512]{1,0:T(8,128)(2,1)S(1)} collective-permute-done((bf16[64,512]{1,0:T(8,128)(2,1)S(1)}, bf16[64,512]{1,0:T(8,128)(2,1)S(1)}, u32[]{:S(2)}, u32[]{:S(2)}) %collective-permute-start.16) | collective-permute-done | bytes 65568 | tf_op jit(solution)/shard_map/ppermute | solution.py:432
  47.4 0.1 collective-permute-start.18
  47.5 1.0 %collective-permute-start.17 = (bf16[64,512]{1,0:T(8,128)(2,1)S(1)}, bf16[64,512]{1,0:T(8,128)(2,1)S(1)}, u32[]{:S(2)}, u32[]{:S(2)}) collective-permute-start(bf16[64,512]{1,0:T(8,128)(2,1)S(1)} %late.1), channel_id=1, source_target_pairs={{0,2},{2,0},{4,6},{6,4},{8,10},{10,8},{12,14},{14,12},{1,3},{3,1},... | collective-permute-start | bytes 196616 | tf_op jit(solution)/shard_map/ppermute | solution.py:432
  48.5 0.0 collective-permute-done.12.refs_1_
  48.5 1.0 %collective-permute-done.13.refs_2_ = bf16[64,512]{1,0:T(8,128)(2,1)S(1)} collective-permute-done((bf16[64,512]{1,0:T(8,128)(2,1)S(1)}, bf16[64,512]{1,0:T(8,128)(2,1)S(1)}, u32[]{:S(2)}, u32[]{:S(2)}) %collective-permute-start.13) | collective-permute-done | bytes 65568 | tf_op jit(solution)/shard_map/ppermute | solution.py:432
  49.6 2.3 %collective-permute-done.17.refs_3_ = bf16[64,512]{1,0:T(8,128)(2,1)S(1)} collective-permute-done((bf16[64,512]{1,0:T(8,128)(2,1)S(1)}, bf16[64,512]{1,0:T(8,128)(2,1)S(1)}, u32[]{:S(2)}, u32[]{:S(2)}) %collective-permute-start.17) | collective-permute-done | bytes 65568 | tf_op jit(solution)/shard_map/ppermute | solution.py:432
  51.8 1.5 %collective-permute-done.18.refs_5_ = bf16[72,512]{1,0:T(8,128)(2,1)S(1)} collective-permute-done((bf16[72,512]{1,0:T(8,128)(2,1)S(1)}, bf16[72,512]{1,0:T(8,128)(2,1)S(1)}, u32[]{:S(2)}, u32[]{:S(2)}) %collective-permute-start.18) | collective-permute-done | bytes 73760 | tf_op jit(solution)/shard_map/ppermute | solution.py:432
  53.4 0.0 copy-done.3
  53.4 0.7 %seeds.1 = bf16[64,512]{1,0:T(8,128)(2,1)} custom-call(f32[1,512]{1,0:T(1,128)S(1)} %bitcast.11, bf16[64,512]{1,0:T(8,128)(2,1)S(1)} %collective-permute-done.12.refs_1_, bf16[64,512]{1,0:T(8,128)(2,1)S(1)} %collective-permute-done.13.refs_2_, bf16[64,512]{1,0:T(8,128)(2,1)S(1)} %collective-permute-done.17.refs_3_, ...), custom_call_target="tpu_custom_call" | custom-call | flops 1100000000 | tf_op jit(solution)/shard_map/seeds/pallas_call | solution.py:467
  (3 shorter events, 0.1 us)
Async XLA Ops:
  2.3 12.4 %collective-permute-start = (bf16[176,512]{1,0:T(8,128)(2,1)S(1)}, bf16[176,512]{1,0:T(8,128)(2,1)S(1)}, u32[]{:S(2)}, u32[]{:S(2)}) collective-permute-start(bf16[176,512]{1,0:T(8,128)(2,1)S(1)} %get-tuple-element.39), channel_id=1, source_target_pairs={{0,6},{2,4},{4,2},{6,0},{8,14},{10,12},{12,10},{14,8},{1,7},{3,5},... | collective-permute-start | bytes 540680 | tf_op jit(solution)/shard_map/ppermute | solution.py:432
  6.4 8.6 %collective-permute-start.1 = (bf16[176,512]{1,0:T(8,128)(2,1)S(1)}, bf16[176,512]{1,0:T(8,128)(2,1)S(1)}, u32[]{:S(2)}, u32[]{:S(2)}) collective-permute-start(bf16[176,512]{1,0:T(8,128)(2,1)S(1)} %get-tuple-element.40), channel_id=1, source_target_pairs={{0,4},{2,6},{4,0},{6,2},{8,12},{10,14},{12,8},{14,10},{1,5},{3,7},... | collective-permute-start | bytes 540680 | tf_op jit(solution)/shard_map/ppermute | solution.py:432
  6.8 8.2 %collective-permute-start.2 = (bf16[176,512]{1,0:T(8,128)(2,1)S(1)}, bf16[176,512]{1,0:T(8,128)(2,1)S(1)}, u32[]{:S(2)}, u32[]{:S(2)}) collective-permute-start(bf16[176,512]{1,0:T(8,128)(2,1)S(1)} %get-tuple-element.41), channel_id=1, source_target_pairs={{0,2},{2,0},{4,6},{6,4},{8,10},{10,8},{12,14},{14,12},{1,3},{3,1},... | collective-permute-start | bytes 540680 | tf_op jit(solution)/shard_map/ppermute | solution.py:432
  7.0 11.7 %copy-start.2 = (f32[512]{0:T(512)S(1)}, f32[512]{0:T(512)}, u32[]{:S(2)}) copy-start(f32[512]{0:T(512)} %param.18) | copy-start | bytes 6148
  15.0 3.6 %collective-permute-start.6 = (bf16[4,96,512]{2,1,0:T(8,128)(2,1)S(1)}, bf16[4,96,512]{2,1,0:T(8,128)(2,1)S(1)}, u32[]{:S(2)}, u32[]{:S(2)}) collective-permute-start(bf16[4,96,512]{2,1,0:T(8,128)(2,1)S(1)} %get-tuple-element.51), channel_id=1, source_target_pairs={{0,1},{1,0},{2,3},{3,2},{4,5},{5,4},{6,7},{7,6},{8,9},{9,8},{10,11... | collective-permute-start | bytes 1179656 | tf_op jit(solution)/shard_map/ppermute | solution.py:432
  15.1 6.2 %collective-permute-start.3 = (bf16[160,128]{1,0:T(8,128)(2,1)S(1)}, bf16[160,128]{1,0:T(8,128)(2,1)S(1)}, u32[]{:S(2)}, u32[]{:S(2)}) collective-permute-start(bf16[160,128]{1,0:T(8,128)(2,1)S(1)} %get-tuple-element.48), channel_id=1, source_target_pairs={{0,6},{2,4},{4,2},{6,0},{8,14},{10,12},{12,10},{14,8},{1,7},{3,5},... | collective-permute-start | bytes 122888 | tf_op jit(solution)/shard_map/ppermute | solution.py:432
  17.8 4.0 %collective-permute-start.4 = (bf16[160,128]{1,0:T(8,128)(2,1)S(1)}, bf16[160,128]{1,0:T(8,128)(2,1)S(1)}, u32[]{:S(2)}, u32[]{:S(2)}) collective-permute-start(bf16[160,128]{1,0:T(8,128)(2,1)S(1)} %get-tuple-element.49), channel_id=1, source_target_pairs={{0,4},{2,6},{4,0},{6,2},{8,12},{10,14},{12,8},{14,10},{1,5},{3,7},... | collective-permute-start | bytes 122888 | tf_op jit(solution)/shard_map/ppermute | solution.py:432
  18.2 4.0 %collective-permute-start.5 = (bf16[160,128]{1,0:T(8,128)(2,1)S(1)}, bf16[160,128]{1,0:T(8,128)(2,1)S(1)}, u32[]{:S(2)}, u32[]{:S(2)}) collective-permute-start(bf16[160,128]{1,0:T(8,128)(2,1)S(1)} %get-tuple-element.50), channel_id=1, source_target_pairs={{0,2},{2,0},{4,6},{6,4},{8,10},{10,8},{12,14},{14,12},{1,3},{3,1},... | collective-permute-start | bytes 122888 | tf_op jit(solution)/shard_map/ppermute | solution.py:432
  22.6 11.7 %copy-start = (bf16[512,512]{1,0:T(8,128)(2,1)S(1)}, bf16[512,512]{1,0:T(8,128)(2,1)}, u32[]{:S(2)}) copy-start(bf16[512,512]{1,0:T(8,128)(2,1)} %refs_3_.5) | copy-start | bytes 1572868
  22.6 11.7 %copy-start.1 = (bf16[512,512]{1,0:T(8,128)(2,1)S(1)}, bf16[512,512]{1,0:T(8,128)(2,1)}, u32[]{:S(2)}) copy-start(bf16[512,512]{1,0:T(8,128)(2,1)} %refs_4_.3) | copy-start | bytes 1572868
  22.6 14.0 %collective-permute-start.7 = (bf16[208,512]{1,0:T(8,128)(2,1)S(1)}, bf16[208,512]{1,0:T(8,128)(2,1)S(1)}, u32[]{:S(2)}, u32[]{:S(2)}) collective-permute-start(bf16[208,512]{1,0:T(8,128)(2,1)S(1)} %far.1.refs_5_.refs_9_), channel_id=1, source_target_pairs={{0,8},{2,10},{4,12},{6,14},{8,0},{10,2},{12,4},{14,6},{1,9},{3,11}... | collective-permute-start | bytes 638984 | tf_op jit(solution)/shard_map/ppermute | solution.py:432
  30.7 5.1 %collective-permute-start.8 = (bf16[144,128]{1,0:T(8,128)(2,1)S(1)}, bf16[144,128]{1,0:T(8,128)(2,1)S(1)}, u32[]{:S(2)}, u32[]{:S(2)}) collective-permute-start(bf16[144,128]{1,0:T(8,128)(2,1)S(1)} %get-tuple-element.58), channel_id=1, source_target_pairs={{0,6},{2,4},{4,2},{6,0},{8,14},{10,12},{12,10},{14,8},{1,7},{3,5},... | collective-permute-start | bytes 110600 | tf_op jit(solution)/shard_map/ppermute | solution.py:432
  31.3 4.6 %collective-permute-start.9 = (bf16[144,128]{1,0:T(8,128)(2,1)S(1)}, bf16[144,128]{1,0:T(8,128)(2,1)S(1)}, u32[]{:S(2)}, u32[]{:S(2)}) collective-permute-start(bf16[144,128]{1,0:T(8,128)(2,1)S(1)} %get-tuple-element.59), channel_id=1, source_target_pairs={{0,4},{2,6},{4,0},{6,2},{8,12},{10,14},{12,8},{14,10},{1,5},{3,7},... | collective-permute-start | bytes 110600 | tf_op jit(solution)/shard_map/ppermute | solution.py:432
  32.2 4.0 %collective-permute-start.10 = (bf16[144,128]{1,0:T(8,128)(2,1)S(1)}, bf16[144,128]{1,0:T(8,128)(2,1)S(1)}, u32[]{:S(2)}, u32[]{:S(2)}) collective-permute-start(bf16[144,128]{1,0:T(8,128)(2,1)S(1)} %get-tuple-element.60), channel_id=1, source_target_pairs={{0,2},{2,0},{4,6},{6,4},{8,10},{10,8},{12,14},{14,12},{1,3},{3,1},... | collective-permute-start | bytes 110600 | tf_op jit(solution)/shard_map/ppermute | solution.py:432
  36.8 1.5 %collective-permute-start.11 = (bf16[192,512]{1,0:T(8,128)(2,1)S(1)}, bf16[192,512]{1,0:T(8,128)(2,1)S(1)}, u32[]{:S(2)}, u32[]{:S(2)}) collective-permute-start(bf16[192,512]{1,0:T(8,128)(2,1)S(1)} %hidden.1.refs_1_), channel_id=1, source_target_pairs={{0,1},{1,0},{2,3},{3,2},{4,5},{5,4},{6,7},{7,6},{8,9},{9,8},{10,11... | collective-permute-start | bytes 589832 | tf_op jit(solution)/shard_map/ppermute | solution.py:432
  38.9 14.5 %copy-start.3 = (f32[512]{0:T(512)S(1)}, f32[512]{0:T(512)}, u32[]{:S(2)}) copy-start(f32[512]{0:T(512)} %param.21) | copy-start | bytes 6148
  38.9 7.5 %collective-permute-start.14 = (bf16[64,512]{1,0:T(8,128)(2,1)S(1)}, bf16[64,512]{1,0:T(8,128)(2,1)S(1)}, u32[]{:S(2)}, u32[]{:S(2)}) collective-permute-start(bf16[64,512]{1,0:T(8,128)(2,1)S(1)} %get-tuple-element.71), channel_id=1, source_target_pairs={{0,6},{2,4},{4,2},{6,0},{8,14},{10,12},{12,10},{14,8},{1,7},{3,5},... | collective-permute-start | bytes 196616 | tf_op jit(solution)/shard_map/ppermute | solution.py:432
  40.8 5.6 %collective-permute-start.15 = (bf16[64,512]{1,0:T(8,128)(2,1)S(1)}, bf16[64,512]{1,0:T(8,128)(2,1)S(1)}, u32[]{:S(2)}, u32[]{:S(2)}) collective-permute-start(bf16[64,512]{1,0:T(8,128)(2,1)S(1)} %get-tuple-element.72), channel_id=1, source_target_pairs={{0,4},{2,6},{4,0},{6,2},{8,12},{10,14},{12,8},{14,10},{1,5},{3,7},... | collective-permute-start | bytes 196616 | tf_op jit(solution)/shard_map/ppermute | solution.py:432
  42.5 4.9 %collective-permute-start.16 = (bf16[64,512]{1,0:T(8,128)(2,1)S(1)}, bf16[64,512]{1,0:T(8,128)(2,1)S(1)}, u32[]{:S(2)}, u32[]{:S(2)}) collective-permute-start(bf16[64,512]{1,0:T(8,128)(2,1)S(1)} %get-tuple-element.73), channel_id=1, source_target_pairs={{0,2},{2,0},{4,6},{6,4},{8,10},{10,8},{12,14},{14,12},{1,3},{3,1},... | collective-permute-start | bytes 196616 | tf_op jit(solution)/shard_map/ppermute | solution.py:432
  42.8 5.7 %collective-permute-start.12 = (bf16[64,512]{1,0:T(8,128)(2,1)S(1)}, bf16[64,512]{1,0:T(8,128)(2,1)S(1)}, u32[]{:S(2)}, u32[]{:S(2)}) collective-permute-start(bf16[64,512]{1,0:T(8,128)(2,1)S(1)} %get-tuple-element.68), channel_id=1, source_target_pairs={{0,6},{2,4},{4,2},{6,0},{8,14},{10,12},{12,10},{14,8},{1,7},{3,5},... | collective-permute-start | bytes 196616 | tf_op jit(solution)/shard_map/ppermute | solution.py:432
  44.7 4.8 %collective-permute-start.13 = (bf16[64,512]{1,0:T(8,128)(2,1)S(1)}, bf16[64,512]{1,0:T(8,128)(2,1)S(1)}, u32[]{:S(2)}, u32[]{:S(2)}) collective-permute-start(bf16[64,512]{1,0:T(8,128)(2,1)S(1)} %get-tuple-element.69), channel_id=1, source_target_pairs={{0,4},{2,6},{4,0},{6,2},{8,12},{10,14},{12,8},{14,10},{1,5},{3,7},... | collective-permute-start | bytes 196616 | tf_op jit(solution)/shard_map/ppermute | solution.py:432
  47.4 6.0 %collective-permute-start.18 = (bf16[72,512]{1,0:T(8,128)(2,1)S(1)}, bf16[72,512]{1,0:T(8,128)(2,1)S(1)}, u32[]{:S(2)}, u32[]{:S(2)}) collective-permute-start(bf16[72,512]{1,0:T(8,128)(2,1)S(1)} %side_sum.1.refs_1_), channel_id=1, source_target_pairs={{0,8},{2,10},{4,12},{6,14},{8,0},{10,2},{12,4},{14,6},{1,9},{3,11}... | collective-permute-start | bytes 221192 | tf_op jit(solution)/shard_map/ppermute | solution.py:432
  47.5 4.3 %collective-permute-start.17 = (bf16[64,512]{1,0:T(8,128)(2,1)S(1)}, bf16[64,512]{1,0:T(8,128)(2,1)S(1)}, u32[]{:S(2)}, u32[]{:S(2)}) collective-permute-start(bf16[64,512]{1,0:T(8,128)(2,1)S(1)} %late.1), channel_id=1, source_target_pairs={{0,2},{2,0},{4,6},{6,4},{8,10},{10,8},{12,14},{14,12},{1,3},{3,1},... | collective-permute-start | bytes 196616 | tf_op jit(solution)/shard_map/ppermute | solution.py:432

commit v21 on v19

--- a/solution.py
+++ b/solution.py
@@ -58,6 +58,23 @@
 
 def live_rows(ref):
     return jnp.max(ref[-TAG_ROWS:, :].astype(jnp.float32)).astype(jnp.int32)
+
+
+def row_code(row):
+    high = lax.shift_right_logical(row, 7)
+    code = (128 + (row & 127)).astype(jnp.float32)
+    for bit in range(7):
+        code = code * jnp.where((high >> bit) & 1 == 1, float(2 ** (2**bit)), 1.0)
+    return code
+
+
+def pair_codes(ref_low, ref_high, seed_count, fslice, n_idx, lanes):
+    low = lax.broadcasted_iota(jnp.int32, (n_idx, 2 * seed_count), 1) < seed_count
+    return jnp.where(
+        low,
+        read_digits(ref_low, fslice, n_idx, lanes),
+        read_digits(ref_high, fslice, n_idx, lanes),
+    )
 
 
 def pack_kernel(
@@ -103,8 +120,8 @@
     feat_pos = lax.axis_index("feat")
     first_core = lax.axis_index("rep") == 0
     idx = jnp.concatenate([seed_ref[...], nbr_ref[...]], axis=0)
-    high = lax.shift_right_logical(idx, 7)
-    digits = jnp.concatenate([high, idx - high * 128], axis=1).astype(jnp.float32)
+    code = row_code(idx)
+    digits = jnp.concatenate([code, code], axis=1)
     weight = jnp.where(first_core, w_self_ref[...], w_nbr_ref[...])
     copies[0].wait()
     for s, parcel_ref in zip(steps, parcel_refs):
@@ -275,14 +292,21 @@
         w_ref[s] = jnp.where(first_core, other, mine)
         weights.append(jnp.where(first_core, mine, other))
         feats.append(read_feats(parcel_refs[s], fslice, n_idx, 2 * pcap))
-        rows = pl.ds(s // 4 * n_idx, n_idx)
-        digits = read_digits(parcel_refs[s], fslice, n_idx, 2 * pcap)
-        idx_ref[rows, s % 4 * LANES : (s % 4 + 1) * LANES] = digits.astype(jnp.bfloat16)
     both = jnp.dot(
         jnp.concatenate(feats, axis=0).T.astype(jnp.bfloat16),
         jnp.concatenate(weights, axis=0),
         preferred_element_type=jnp.float32,
     )
+    part = n_idx // 2
+    blocks = []
+    for s in range(0, half, 2):
+        codes = pair_codes(
+            parcel_refs[s], parcel_refs[s + 1], LANES // 2, fslice, n_idx, 2 * pcap
+        )
+        blocks += [codes[:part], codes[part:]]
+    for i in range(0, len(blocks), 4):
+        rows = slice(i // 4 * part, (i // 4 + 1) * part)
+        idx_ref[rows, :] = jnp.concatenate(blocks[i : i + 4], axis=1).astype(jnp.bfloat16)
     pre_ref[...] = both[:pcap] + bias_ref[...]
     far_ref[...] = both[pcap:]
 
@@ -304,21 +328,16 @@
     cross_ref[pcap:, :] = idx_ref[...]
 
 
-def store_times(pcap, blocks, out_ref):
-    n_idx, pair = blocks[0].shape
+def store_times(pcap, names, out_ref):
+    n_idx, pair = names[0].shape
     seed_count = pair // 2
     core_rows = lax.axis_index("feat") * (2 * pcap)
     rep_pos = lax.axis_index("rep")
     row = lax.broadcasted_iota(jnp.int32, (2 * pcap, pair), 0)
-    slot = jnp.where(
-        row < pcap, row + core_rows + rep_pos * pcap, row + core_rows - rep_pos * pcap
-    ).astype(jnp.float32)
-    low = lax.broadcasted_iota(jnp.int32, (n_idx, pair), 1) < seed_count
-    for s in range(0, len(blocks), 2):
-        first, second = blocks[s].astype(jnp.float32), blocks[s + 1].astype(jnp.float32)
-        high_part = jnp.where(low, first, pltpu.roll(second, seed_count, 1))
-        low_part = jnp.where(low, pltpu.roll(first, seed_count, 1), second)
-        name = high_part * 128.0 + low_part
+    slot = row_code(
+        jnp.where(row < pcap, row + core_rows + rep_pos * pcap, row + core_rows - rep_pos * pcap)
+    )
+    for s, name in zip(range(0, 2 * len(names), 2), names):
         own = jnp.where(slot == name[:1], 1.0, 0.0)
         near = jnp.zeros((2 * pcap, pair), jnp.float32)
         for k in range(1, n_idx):
@@ -329,8 +348,11 @@
 
 
 def near_times_kernel(half, fslice, pcap, n_idx, _, __, *refs):
-    blocks = [read_digits(ref, fslice, n_idx, 2 * pcap) for ref in refs[:half]]
-    store_times(pcap, blocks, refs[half])
+    names = [
+        pair_codes(refs[s], refs[s + 1], LANES // 2, fslice, n_idx, 2 * pcap)
+        for s in range(0, half, 2)
+    ]
+    store_times(pcap, names, refs[half])
 
 
 def far_times_kernel(
@@ -349,13 +371,15 @@
     copy = pltpu.make_async_copy(hidden_ref, result_ref, sem)
     copy.start()
     pcap = hidden_ref.shape[0]
+    part = n_idx // 2
     blocks = [
         cross_ref[
-            pl.ds(pcap + s // 4 * n_idx, n_idx), s % 4 * LANES : (s % 4 + 1) * LANES
-        ]
-        for s in range(half)
+            pcap + i // 4 * part : pcap + (i // 4 + 1) * part, i % 4 * LANES : (i % 4 + 1) * LANES
+        ].astype(jnp.float32)
+        for i in range(half)
     ]
-    store_times(pcap, blocks, out_ref)
+    names = [jnp.concatenate(blocks[i : i + 2], axis=0) for i in range(0, half, 2)]
+    store_times(pcap, names, out_ref)
     store_values(hidden_ref[...], ws_ref, wn_ref, fanout_two, value_ref)
     copy.wait()
 
@@ -562,7 +586,7 @@
     )
     far_arrived = send(tagged)
     other_halves = swap(halves, "rep", 1)
-    idx_rows = -(-half // 4) * n_idx
+    idx_rows = half // 4 * (n_idx // 2)
     far_own, w_nbr, pre, far_pre, idx_tags = means(
         [half],
         table=table,

time: 52.9 us -> 52.8 us (level)
  starting transfers between devices: 23.5 us -> 22.4 us
  waiting for transfers between devices: 5.73 us -> 6.63 us
    ppermute x19, starting transfers between devices: 23.5 us -> 22.4 us  [swap(): return lax.ppermute(value, axis, [(i, i ^ step) for i in range(size)])]
    ppermute x19, waiting for transfers between devices: 5.73 us -> 6.63 us  [swap(): return lax.ppermute(value, axis, [(i, i ^ step) for i in range(size)])]
  transfers between devices with their start and end apart: 19 -> 19, of which waited for: 9 -> 10; matrix products, arithmetic and copies ran while one was open for 0% -> 0% of each run, Pallas kernels for 35% -> 35%
where the time goes in v21:
time: 52.8 us; the launch traced here: 52.5 us
  starting transfers between devices  22.4 us (42%)
  Pallas kernels  22.1 us (42%)
  waiting for transfers between devices  6.63 us (13%)
  between operations  1.46 us (3%)
    ppermute x19, starting transfers between devices, swap(): return lax.ppermute(value, axis, [(i, i ^ step) for i in range(size)])  22.4 us
    pallas_call x15, Pallas kernels, call(): pl.pallas_call(wrapped, out_shape=tuple((jax.ShapeDtypeStruct(shape, dtyp...  22.1 us
    ppermute x19, waiting for transfers between devices, swap(): return lax.ppermute(value, axis, [(i, i ^ step) for i in range(size)])  6.63 us
  transfers between devices with their start and end apart: 19, of which 10 were waited for; matrix products, arithmetic and copies ran while one was open for 0% of the time, Pallas kernels for 35%

profile of v21, /device:TPU:0, one launch (start us, length us, event | category | flops | bytes accessed | tf_op | source)
XLA Modules:
  0.0 52.5 jit_solution(545363989020231259)
XLA Ops:
  0.6 1.7 %pack.1 = (bf16[176,512]{1,0:T(8,128)(2,1)S(1)}, bf16[176,512]{1,0:T(8,128)(2,1)S(1)}, bf16[176,512]{1,0:T(8,128)(2,1)S(1)}, bf16[176,512]{1,0:T(8,128)(2,1)S(1)...) custom-call(bf16[96,12288]{1,0:T(8,128)(2,1)} %refs_1_.2, s32[1,64]{1,0:T(1,128)} %bitcast.14, ...), custom_call_target="tpu_custom_call" | custom-call | flops 1100000000 | tf_op jit(solution)/shard_map/pack/pallas_call | solution.py:492
  2.3 4.0 %collective-permute-start = (bf16[176,512]{1,0:T(8,128)(2,1)S(1)}, bf16[176,512]{1,0:T(8,128)(2,1)S(1)}, u32[]{:S(2)}, u32[]{:S(2)}) collective-permute-start(bf16[176,512]{1,0:T(8,128)(2,1)S(1)} %get-tuple-element.38), channel_id=1, source_target_pairs={{0,6},{2,4},{4,2},{6,0},{8,14},{10,12},{12,10},{14,8},{1,7},{3,5},... | collective-permute-start | bytes 540680 | tf_op jit(solution)/shard_map/ppermute | solution.py:457
  6.4 0.5 collective-permute-start.1
  6.8 0.2 collective-permute-start.2
  7.0 0.0 copy-start.2
  7.0 7.1 %mean.4 = (bf16[144,128]{1,0:T(8,128)(2,1)S(1)}, bf16[144,128]{1,0:T(8,128)(2,1)S(1)}, bf16[144,128]{1,0:T(8,128)(2,1)S(1)}, f32[12288,128]{1,0:T(8,128)S(1)}) custom-call(bf16[96,3072]{1,0:T(8,128)(2,1)S(1)} %get-tuple-element.42.refs_0_, bf16[96,12288]{1,0:T(8,128)(2,1)} %refs_1_.2, s32[8,1,1280]{2,1,0:T(1,128)S(1)} %get-tuple-element.43.refs_2_.refs_6_.refs_0_), custom_call_target="tpu_custom_call" | custom-call | flops 6600000000 | tf_op jit(solution)/shard_map/mean/pallas_call | solution.py:492
  14.7 0.0 collective-permute-done.refs_1_.refs_0_.refs_2_
  14.8 0.2 collective-permute-done.1.refs_2_.refs_1_.refs_3_
  15.0 0.0 collective-permute-done.2.refs_3_.refs_2_.refs_4_
  15.0 0.1 collective-permute-start.6
  15.1 2.7 %collective-permute-start.3 = (bf16[160,128]{1,0:T(8,128)(2,1)S(1)}, bf16[160,128]{1,0:T(8,128)(2,1)S(1)}, u32[]{:S(2)}, u32[]{:S(2)}) collective-permute-start(bf16[160,128]{1,0:T(8,128)(2,1)S(1)} %get-tuple-element.47), channel_id=1, source_target_pairs={{0,6},{2,4},{4,2},{6,0},{8,14},{10,12},{12,10},{14,8},{1,7},{3,5},... | collective-permute-start | bytes 122888 | tf_op jit(solution)/shard_map/ppermute | solution.py:457
  17.8 0.5 collective-permute-start.4
  18.3 0.4 collective-permute-start.5
  18.7 0.0 collective-permute-done.6.refs_4_
  18.7 0.0 copy-done.2
  18.7 2.6 %mean.5 = (bf16[144,128]{1,0:T(8,128)(2,1)S(1)}, bf16[4,96,512]{2,1,0:T(8,128)(2,1)S(1)}, f32[192,512]{1,0:T(8,128)S(1)}, f32[192,512]{1,0:T(8,128)S(1)}, bf16[8,512]{1,0:T(8,128)(2,1)S(1)}) custom-call(bf16[176,512]{1,0:T(8,128)(2,1)S(1)} %collective-permute-done.refs_1_.refs_0_.refs_2_, ...), custom_call_target="tpu_custom_call" | custom-call | tf_op jit(solution)/shard_map/mean/pallas_call | solution.py:492
  21.3 0.0 collective-permute-done.3.refs_0_.refs_2_
  21.3 0.5 collective-permute-done.4.refs_1_.refs_3_
  21.8 0.5 collective-permute-done.5.refs_2_.refs_4_
  22.3 0.4 far.1.refs_5_.refs_9_
  22.7 0.0 copy-start
  22.7 0.0 copy-start.1
  22.7 2.6 %collective-permute-start.7 = (bf16[200,512]{1,0:T(8,128)(2,1)S(1)}, bf16[200,512]{1,0:T(8,128)(2,1)S(1)}, u32[]{:S(2)}, u32[]{:S(2)}) collective-permute-start(bf16[200,512]{1,0:T(8,128)(2,1)S(1)} %far.1.refs_5_.refs_9_), channel_id=1, source_target_pairs={{0,8},{2,10},{4,12},{6,14},{8,0},{10,2},{12,4},{14,6},{1,9},{3,11}... | collective-permute-start | bytes 614408 | tf_op jit(solution)/shard_map/ppermute | solution.py:457
  25.3 4.5 %mean.6 = (bf16[144,128]{1,0:T(8,128)(2,1)S(1)}, bf16[144,128]{1,0:T(8,128)(2,1)S(1)}, bf16[144,128]{1,0:T(8,128)(2,1)S(1)}) custom-call(s32[8,1,1280]{2,1,0:T(1,128)S(1)} %get-tuple-element.43.refs_2_.refs_6_.refs_0_, f32[12288,1,128]{2,1,0:T(1,128)S(1)} %bitcast.8, bf16[160,128]{1,0:T(8,128)(2,1)S(1)} %collective-permute-done.3.refs_0_.refs_2_, ...), custom_call_target="tpu_custom_call" | custom-call | flops 6600000000 | tf_op jit(solution)/shard_map/mean/pallas_call | solution.py:492
  29.8 0.9 %collective-permute-start.8 = (bf16[144,128]{1,0:T(8,128)(2,1)S(1)}, bf16[144,128]{1,0:T(8,128)(2,1)S(1)}, u32[]{:S(2)}, u32[]{:S(2)}) collective-permute-start(bf16[144,128]{1,0:T(8,128)(2,1)S(1)} %get-tuple-element.57), channel_id=1, source_target_pairs={{0,6},{2,4},{4,2},{6,0},{8,14},{10,12},{12,10},{14,8},{1,7},{3,5},... | collective-permute-start | bytes 110600 | tf_op jit(solution)/shard_map/ppermute | solution.py:457
  30.7 1.1 %collective-permute-start.9 = (bf16[144,128]{1,0:T(8,128)(2,1)S(1)}, bf16[144,128]{1,0:T(8,128)(2,1)S(1)}, u32[]{:S(2)}, u32[]{:S(2)}) collective-permute-start(bf16[144,128]{1,0:T(8,128)(2,1)S(1)} %get-tuple-element.58), channel_id=1, source_target_pairs={{0,4},{2,6},{4,0},{6,2},{8,12},{10,14},{12,8},{14,10},{1,5},{3,7},... | collective-permute-start | bytes 110600 | tf_op jit(solution)/shard_map/ppermute | solution.py:457
  31.9 1.5 %collective-permute-start.10 = (bf16[144,128]{1,0:T(8,128)(2,1)S(1)}, bf16[144,128]{1,0:T(8,128)(2,1)S(1)}, u32[]{:S(2)}, u32[]{:S(2)}) collective-permute-start(bf16[144,128]{1,0:T(8,128)(2,1)S(1)} %get-tuple-element.59), channel_id=1, source_target_pairs={{0,2},{2,0},{4,6},{6,4},{8,10},{10,8},{12,14},{14,12},{1,3},{3,1},... | collective-permute-start | bytes 110600 | tf_op jit(solution)/shard_map/ppermute | solution.py:457
  33.4 0.0 copy-done
  33.4 0.0 copy-done.1
  33.4 2.1 %mean.7 = (bf16[144,128]{1,0:T(8,128)(2,1)S(1)}, bf16[256,768]{1,0:T(8,128)(2,1)S(1)}) custom-call(bf16[512,512]{1,0:T(8,128)(2,1)S(1)} %copy-done, bf16[512,512]{1,0:T(8,128)(2,1)S(1)} %copy-done.1, bf16[176,512]{1,0:T(8,128)(2,1)S(1)} %collective-permute-done.refs_1_.refs_0_.refs_2_, bf16[176,512]{1,0:T(8,128)(2,1)S(1)} %collective-permute-done.1.refs_2_.refs_1_.refs_3_, ...), custom_call_target="tpu_custom_call" | custom-call | tf_op jit(solution)/shard_map/mean/pallas_call | solution.py:492
  35.5 0.1 collective-permute-done.8.refs_0_
  35.5 0.0 collective-permute-done.9.refs_1_
  35.5 0.4 collective-permute-done.10.refs_2_
  35.9 0.4 near.1.refs_1_
  36.3 0.0 collective-permute-done.7.refs_2_.refs_0_
  36.3 0.2 hidden.1.refs_1_
  36.5 0.1 collective-permute-start.11
  36.6 1.1 %far_times.1 = (bf16[256,768]{1,0:T(8,128)(2,1)S(1)}, bf16[2,192,512]{2,1,0:T(8,128)(2,1)S(1)}, bf16[192,512]{1,0:T(8,128)(2,1)}) custom-call(bf16[200,512]{1,0:T(8,128)(2,1)S(1)} %collective-permute-done.7.refs_2_.refs_0_, bf16[192,512]{1,0:T(8,128)(2,1)S(1)} %hidden.1.refs_1_, bf16[512,512]{1,0:T(8,128)(2,1)S(1)} %copy-done, bf16[512,512]{1,0:T(8,128)(2,1)S(1)} %copy-done.1), custom_call_target="tpu_custom_call" | custom-call | flops 1100000000 | tf_op jit(solution)/shard_map/far_times/pallas_call | solution.py:492
  37.7 0.3 collective-permute-done.11.refs_2_
  38.0 0.6 %far_share.1 = (bf16[64,512]{1,0:T(8,128)(2,1)S(1)}, bf16[64,512]{1,0:T(8,128)(2,1)S(1)}, bf16[64,512]{1,0:T(8,128)(2,1)S(1)}, bf16[64,512]{1,0:T(8,128)(2,1)S(1)}, bf16[768,512]{1,0:T(8,128)(2,1)S(1)}) custom-call(bf16[256,768]{1,0:T(8,128)(2,1)S(1)} %get-tuple-element.64.refs_0_, bf16[2,192,512]{2,1,0:T(8,128)(2,1)S(1)} %get-tuple-element.65.refs_1_, ...), custom_call_target="tpu_custom_call" | custom-call | flops 1100000000 | tf_op jit(solution)/shard_map/far_share/pallas_call | solution.py:492
  38.6 0.0 copy-start.3
  38.6 2.5 %collective-permute-start.14 = (bf16[64,512]{1,0:T(8,128)(2,1)S(1)}, bf16[64,512]{1,0:T(8,128)(2,1)S(1)}, u32[]{:S(2)}, u32[]{:S(2)}) collective-permute-start(bf16[64,512]{1,0:T(8,128)(2,1)S(1)} %get-tuple-element.69), channel_id=1, source_target_pairs={{0,6},{2,4},{4,2},{6,0},{8,14},{10,12},{12,10},{14,8},{1,7},{3,5},... | collective-permute-start | bytes 196616 | tf_op jit(solution)/shard_map/ppermute | solution.py:457
  41.1 0.5 collective-permute-start.15
  41.5 0.6 %collective-permute-start.16 = (bf16[64,512]{1,0:T(8,128)(2,1)S(1)}, bf16[64,512]{1,0:T(8,128)(2,1)S(1)}, u32[]{:S(2)}, u32[]{:S(2)}) collective-permute-start(bf16[64,512]{1,0:T(8,128)(2,1)S(1)} %get-tuple-element.71), channel_id=1, source_target_pairs={{0,2},{2,0},{4,6},{6,4},{8,10},{10,8},{12,14},{14,12},{1,3},{3,1},... | collective-permute-start | bytes 196616 | tf_op jit(solution)/shard_map/ppermute | solution.py:457
  42.1 0.5 %near_share.2 = (bf16[64,512]{1,0:T(8,128)(2,1)S(1)}, bf16[64,512]{1,0:T(8,128)(2,1)S(1)}, bf16[64,512]{1,0:T(8,128)(2,1)S(1)}) custom-call(bf16[256,768]{1,0:T(8,128)(2,1)S(1)} %get-tuple-element.63.refs_0_, bf16[768,512]{1,0:T(8,128)(2,1)S(1)} %get-tuple-element.66.refs_1_), custom_call_target="tpu_custom_call" | custom-call | flops 1100000000 | tf_op jit(solution)/shard_map/near_share/pallas_call | solution.py:492
  42.7 2.5 %collective-permute-start.12 = (bf16[64,512]{1,0:T(8,128)(2,1)S(1)}, bf16[64,512]{1,0:T(8,128)(2,1)S(1)}, u32[]{:S(2)}, u32[]{:S(2)}) collective-permute-start(bf16[64,512]{1,0:T(8,128)(2,1)S(1)} %get-tuple-element.67), channel_id=1, source_target_pairs={{0,6},{2,4},{4,2},{6,0},{8,14},{10,12},{12,10},{14,8},{1,7},{3,5},... | collective-permute-start | bytes 196616 | tf_op jit(solution)/shard_map/ppermute | solution.py:457
  45.1 0.5 collective-permute-start.13
  45.6 0.0 collective-permute-done.14.refs_0_
  45.6 0.0 collective-permute-done.15.refs_1_
  45.6 0.9 %collective-permute-done.16.refs_2_ = bf16[64,512]{1,0:T(8,128)(2,1)S(1)} collective-permute-done((bf16[64,512]{1,0:T(8,128)(2,1)S(1)}, bf16[64,512]{1,0:T(8,128)(2,1)S(1)}, u32[]{:S(2)}, u32[]{:S(2)}) %collective-permute-start.16) | collective-permute-done | bytes 65568 | tf_op jit(solution)/shard_map/ppermute | solution.py:457
  46.5 0.2 collective-permute-start.18
  46.7 0.2 near_share.3
  46.9 1.1 %collective-permute-start.17 = (bf16[64,512]{1,0:T(8,128)(2,1)S(1)}, bf16[64,512]{1,0:T(8,128)(2,1)S(1)}, u32[]{:S(2)}, u32[]{:S(2)}) collective-permute-start(bf16[64,512]{1,0:T(8,128)(2,1)S(1)} %near_share.3), channel_id=1, source_target_pairs={{0,2},{2,0},{4,6},{6,4},{8,10},{10,8},{12,14},{14,12},{1,3},{3,1},... | collective-permute-start | bytes 196616 | tf_op jit(solution)/shard_map/ppermute | solution.py:457
  48.1 0.0 collective-permute-done.12.refs_1_
  48.1 1.9 %collective-permute-done.13.refs_2_ = bf16[64,512]{1,0:T(8,128)(2,1)S(1)} collective-permute-done((bf16[64,512]{1,0:T(8,128)(2,1)S(1)}, bf16[64,512]{1,0:T(8,128)(2,1)S(1)}, u32[]{:S(2)}, u32[]{:S(2)}) %collective-permute-start.13) | collective-permute-done | bytes 65568 | tf_op jit(solution)/shard_map/ppermute | solution.py:457
  50.0 1.3 %collective-permute-done.17.refs_3_ = bf16[64,512]{1,0:T(8,128)(2,1)S(1)} collective-permute-done((bf16[64,512]{1,0:T(8,128)(2,1)S(1)}, bf16[64,512]{1,0:T(8,128)(2,1)S(1)}, u32[]{:S(2)}, u32[]{:S(2)}) %collective-permute-start.17) | collective-permute-done | bytes 65568 | tf_op jit(solution)/shard_map/ppermute | solution.py:457
  51.3 0.6 %collective-permute-done.18.refs_5_ = bf16[72,512]{1,0:T(8,128)(2,1)S(1)} collective-permute-done((bf16[72,512]{1,0:T(8,128)(2,1)S(1)}, bf16[72,512]{1,0:T(8,128)(2,1)S(1)}, u32[]{:S(2)}, u32[]{:S(2)}) %collective-permute-start.18) | collective-permute-done | bytes 73760 | tf_op jit(solution)/shard_map/ppermute | solution.py:457
  51.8 0.0 copy-done.3
  51.8 0.7 %seeds.1 = bf16[64,512]{1,0:T(8,128)(2,1)} custom-call(f32[1,512]{1,0:T(1,128)S(1)} %bitcast.11, bf16[64,512]{1,0:T(8,128)(2,1)S(1)} %collective-permute-done.12.refs_1_, bf16[64,512]{1,0:T(8,128)(2,1)S(1)} %collective-permute-done.13.refs_2_, bf16[64,512]{1,0:T(8,128)(2,1)S(1)} %collective-permute-done.17.refs_3_, ...), custom_call_target="tpu_custom_call" | custom-call | flops 1100000000 | tf_op jit(solution)/shard_map/seeds/pallas_call | solution.py:492
  (2 shorter events, 0.1 us)
Async XLA Ops:
  2.3 12.4 %collective-permute-start = (bf16[176,512]{1,0:T(8,128)(2,1)S(1)}, bf16[176,512]{1,0:T(8,128)(2,1)S(1)}, u32[]{:S(2)}, u32[]{:S(2)}) collective-permute-start(bf16[176,512]{1,0:T(8,128)(2,1)S(1)} %get-tuple-element.38), channel_id=1, source_target_pairs={{0,6},{2,4},{4,2},{6,0},{8,14},{10,12},{12,10},{14,8},{1,7},{3,5},... | collective-permute-start | bytes 540680 | tf_op jit(solution)/shard_map/ppermute | solution.py:457
  6.4 8.6 %collective-permute-start.1 = (bf16[176,512]{1,0:T(8,128)(2,1)S(1)}, bf16[176,512]{1,0:T(8,128)(2,1)S(1)}, u32[]{:S(2)}, u32[]{:S(2)}) collective-permute-start(bf16[176,512]{1,0:T(8,128)(2,1)S(1)} %get-tuple-element.39), channel_id=1, source_target_pairs={{0,4},{2,6},{4,0},{6,2},{8,12},{10,14},{12,8},{14,10},{1,5},{3,7},... | collective-permute-start | bytes 540680 | tf_op jit(solution)/shard_map/ppermute | solution.py:457
  6.8 8.2 %collective-permute-start.2 = (bf16[176,512]{1,0:T(8,128)(2,1)S(1)}, bf16[176,512]{1,0:T(8,128)(2,1)S(1)}, u32[]{:S(2)}, u32[]{:S(2)}) collective-permute-start(bf16[176,512]{1,0:T(8,128)(2,1)S(1)} %get-tuple-element.40), channel_id=1, source_target_pairs={{0,2},{2,0},{4,6},{6,4},{8,10},{10,8},{12,14},{14,12},{1,3},{3,1},... | collective-permute-start | bytes 540680 | tf_op jit(solution)/shard_map/ppermute | solution.py:457
  7.0 11.7 %copy-start.2 = (f32[512]{0:T(512)S(1)}, f32[512]{0:T(512)}, u32[]{:S(2)}) copy-start(f32[512]{0:T(512)} %param.18) | copy-start | bytes 6148
  15.0 3.6 %collective-permute-start.6 = (bf16[4,96,512]{2,1,0:T(8,128)(2,1)S(1)}, bf16[4,96,512]{2,1,0:T(8,128)(2,1)S(1)}, u32[]{:S(2)}, u32[]{:S(2)}) collective-permute-start(bf16[4,96,512]{2,1,0:T(8,128)(2,1)S(1)} %get-tuple-element.50), channel_id=1, source_target_pairs={{0,1},{1,0},{2,3},{3,2},{4,5},{5,4},{6,7},{7,6},{8,9},{9,8},{10,11... | collective-permute-start | bytes 1179656 | tf_op jit(solution)/shard_map/ppermute | solution.py:457
  15.1 6.2 %collective-permute-start.3 = (bf16[160,128]{1,0:T(8,128)(2,1)S(1)}, bf16[160,128]{1,0:T(8,128)(2,1)S(1)}, u32[]{:S(2)}, u32[]{:S(2)}) collective-permute-start(bf16[160,128]{1,0:T(8,128)(2,1)S(1)} %get-tuple-element.47), channel_id=1, source_target_pairs={{0,6},{2,4},{4,2},{6,0},{8,14},{10,12},{12,10},{14,8},{1,7},{3,5},... | collective-permute-start | bytes 122888 | tf_op jit(solution)/shard_map/ppermute | solution.py:457
  17.8 4.0 %collective-permute-start.4 = (bf16[160,128]{1,0:T(8,128)(2,1)S(1)}, bf16[160,128]{1,0:T(8,128)(2,1)S(1)}, u32[]{:S(2)}, u32[]{:S(2)}) collective-permute-start(bf16[160,128]{1,0:T(8,128)(2,1)S(1)} %get-tuple-element.48), channel_id=1, source_target_pairs={{0,4},{2,6},{4,0},{6,2},{8,12},{10,14},{12,8},{14,10},{1,5},{3,7},... | collective-permute-start | bytes 122888 | tf_op jit(solution)/shard_map/ppermute | solution.py:457
  18.3 4.0 %collective-permute-start.5 = (bf16[160,128]{1,0:T(8,128)(2,1)S(1)}, bf16[160,128]{1,0:T(8,128)(2,1)S(1)}, u32[]{:S(2)}, u32[]{:S(2)}) collective-permute-start(bf16[160,128]{1,0:T(8,128)(2,1)S(1)} %get-tuple-element.49), channel_id=1, source_target_pairs={{0,2},{2,0},{4,6},{6,4},{8,10},{10,8},{12,14},{14,12},{1,3},{3,1},... | collective-permute-start | bytes 122888 | tf_op jit(solution)/shard_map/ppermute | solution.py:457
  22.7 10.7 %copy-start = (bf16[512,512]{1,0:T(8,128)(2,1)S(1)}, bf16[512,512]{1,0:T(8,128)(2,1)}, u32[]{:S(2)}) copy-start(bf16[512,512]{1,0:T(8,128)(2,1)} %refs_3_.5) | copy-start | bytes 1572868
  22.7 10.7 %copy-start.1 = (bf16[512,512]{1,0:T(8,128)(2,1)S(1)}, bf16[512,512]{1,0:T(8,128)(2,1)}, u32[]{:S(2)}) copy-start(bf16[512,512]{1,0:T(8,128)(2,1)} %refs_4_.3) | copy-start | bytes 1572868
  22.7 13.6 %collective-permute-start.7 = (bf16[200,512]{1,0:T(8,128)(2,1)S(1)}, bf16[200,512]{1,0:T(8,128)(2,1)S(1)}, u32[]{:S(2)}, u32[]{:S(2)}) collective-permute-start(bf16[200,512]{1,0:T(8,128)(2,1)S(1)} %far.1.refs_5_.refs_9_), channel_id=1, source_target_pairs={{0,8},{2,10},{4,12},{6,14},{8,0},{10,2},{12,4},{14,6},{1,9},{3,11}... | collective-permute-start | bytes 614408 | tf_op jit(solution)/shard_map/ppermute | solution.py:457
  29.8 5.7 %collective-permute-start.8 = (bf16[144,128]{1,0:T(8,128)(2,1)S(1)}, bf16[144,128]{1,0:T(8,128)(2,1)S(1)}, u32[]{:S(2)}, u32[]{:S(2)}) collective-permute-start(bf16[144,128]{1,0:T(8,128)(2,1)S(1)} %get-tuple-element.57), channel_id=1, source_target_pairs={{0,6},{2,4},{4,2},{6,0},{8,14},{10,12},{12,10},{14,8},{1,7},{3,5},... | collective-permute-start | bytes 110600 | tf_op jit(solution)/shard_map/ppermute | solution.py:457
  30.7 4.8 %collective-permute-start.9 = (bf16[144,128]{1,0:T(8,128)(2,1)S(1)}, bf16[144,128]{1,0:T(8,128)(2,1)S(1)}, u32[]{:S(2)}, u32[]{:S(2)}) collective-permute-start(bf16[144,128]{1,0:T(8,128)(2,1)S(1)} %get-tuple-element.58), channel_id=1, source_target_pairs={{0,4},{2,6},{4,0},{6,2},{8,12},{10,14},{12,8},{14,10},{1,5},{3,7},... | collective-permute-start | bytes 110600 | tf_op jit(solution)/shard_map/ppermute | solution.py:457
  31.9 4.0 %collective-permute-start.10 = (bf16[144,128]{1,0:T(8,128)(2,1)S(1)}, bf16[144,128]{1,0:T(8,128)(2,1)S(1)}, u32[]{:S(2)}, u32[]{:S(2)}) collective-permute-start(bf16[144,128]{1,0:T(8,128)(2,1)S(1)} %get-tuple-element.59), channel_id=1, source_target_pairs={{0,2},{2,0},{4,6},{6,4},{8,10},{10,8},{12,14},{14,12},{1,3},{3,1},... | collective-permute-start | bytes 110600 | tf_op jit(solution)/shard_map/ppermute | solution.py:457
  36.5 1.5 %collective-permute-start.11 = (bf16[192,512]{1,0:T(8,128)(2,1)S(1)}, bf16[192,512]{1,0:T(8,128)(2,1)S(1)}, u32[]{:S(2)}, u32[]{:S(2)}) collective-permute-start(bf16[192,512]{1,0:T(8,128)(2,1)S(1)} %hidden.1.refs_1_), channel_id=1, source_target_pairs={{0,1},{1,0},{2,3},{3,2},{4,5},{5,4},{6,7},{7,6},{8,9},{9,8},{10,11... | collective-permute-start | bytes 589832 | tf_op jit(solution)/shard_map/ppermute | solution.py:457
  38.6 13.3 %copy-start.3 = (f32[512]{0:T(512)S(1)}, f32[512]{0:T(512)}, u32[]{:S(2)}) copy-start(f32[512]{0:T(512)} %param.21) | copy-start | bytes 6148
  38.6 7.0 %collective-permute-start.14 = (bf16[64,512]{1,0:T(8,128)(2,1)S(1)}, bf16[64,512]{1,0:T(8,128)(2,1)S(1)}, u32[]{:S(2)}, u32[]{:S(2)}) collective-permute-start(bf16[64,512]{1,0:T(8,128)(2,1)S(1)} %get-tuple-element.69), channel_id=1, source_target_pairs={{0,6},{2,4},{4,2},{6,0},{8,14},{10,12},{12,10},{14,8},{1,7},{3,5},... | collective-permute-start | bytes 196616 | tf_op jit(solution)/shard_map/ppermute | solution.py:457
  41.1 4.5 %collective-permute-start.15 = (bf16[64,512]{1,0:T(8,128)(2,1)S(1)}, bf16[64,512]{1,0:T(8,128)(2,1)S(1)}, u32[]{:S(2)}, u32[]{:S(2)}) collective-permute-start(bf16[64,512]{1,0:T(8,128)(2,1)S(1)} %get-tuple-element.70), channel_id=1, source_target_pairs={{0,4},{2,6},{4,0},{6,2},{8,12},{10,14},{12,8},{14,10},{1,5},{3,7},... | collective-permute-start | bytes 196616 | tf_op jit(solution)/shard_map/ppermute | solution.py:457
  41.5 5.0 %collective-permute-start.16 = (bf16[64,512]{1,0:T(8,128)(2,1)S(1)}, bf16[64,512]{1,0:T(8,128)(2,1)S(1)}, u32[]{:S(2)}, u32[]{:S(2)}) collective-permute-start(bf16[64,512]{1,0:T(8,128)(2,1)S(1)} %get-tuple-element.71), channel_id=1, source_target_pairs={{0,2},{2,0},{4,6},{6,4},{8,10},{10,8},{12,14},{14,12},{1,3},{3,1},... | collective-permute-start | bytes 196616 | tf_op jit(solution)/shard_map/ppermute | solution.py:457
  42.7 5.4 %collective-permute-start.12 = (bf16[64,512]{1,0:T(8,128)(2,1)S(1)}, bf16[64,512]{1,0:T(8,128)(2,1)S(1)}, u32[]{:S(2)}, u32[]{:S(2)}) collective-permute-start(bf16[64,512]{1,0:T(8,128)(2,1)S(1)} %get-tuple-element.67), channel_id=1, source_target_pairs={{0,6},{2,4},{4,2},{6,0},{8,14},{10,12},{12,10},{14,8},{1,7},{3,5},... | collective-permute-start | bytes 196616 | tf_op jit(solution)/shard_map/ppermute | solution.py:457
  45.1 4.8 %collective-permute-start.13 = (bf16[64,512]{1,0:T(8,128)(2,1)S(1)}, bf16[64,512]{1,0:T(8,128)(2,1)S(1)}, u32[]{:S(2)}, u32[]{:S(2)}) collective-permute-start(bf16[64,512]{1,0:T(8,128)(2,1)S(1)} %get-tuple-element.68), channel_id=1, source_target_pairs={{0,4},{2,6},{4,0},{6,2},{8,12},{10,14},{12,8},{14,10},{1,5},{3,7},... | collective-permute-start | bytes 196616 | tf_op jit(solution)/shard_map/ppermute | solution.py:457
  46.5 5.3 %collective-permute-start.18 = (bf16[72,512]{1,0:T(8,128)(2,1)S(1)}, bf16[72,512]{1,0:T(8,128)(2,1)S(1)}, u32[]{:S(2)}, u32[]{:S(2)}) collective-permute-start(bf16[72,512]{1,0:T(8,128)(2,1)S(1)} %side_sum.1.refs_2_), channel_id=1, source_target_pairs={{0,8},{2,10},{4,12},{6,14},{8,0},{10,2},{12,4},{14,6},{1,9},{3,11}... | collective-permute-start | bytes 221192 | tf_op jit(solution)/shard_map/ppermute | solution.py:457
  46.9 4.3 %collective-permute-start.17 = (bf16[64,512]{1,0:T(8,128)(2,1)S(1)}, bf16[64,512]{1,0:T(8,128)(2,1)S(1)}, u32[]{:S(2)}, u32[]{:S(2)}) collective-permute-start(bf16[64,512]{1,0:T(8,128)(2,1)S(1)} %near_share.3), channel_id=1, source_target_pairs={{0,2},{2,0},{4,6},{6,4},{8,10},{10,8},{12,14},{14,12},{1,3},{3,1},... | collective-permute-start | bytes 196616 | tf_op jit(solution)/shard_map/ppermute | solution.py:457

commit v22 on v21

--- a/solution.py
+++ b/solution.py
@@ -280,23 +280,28 @@
         ref[-TAG_ROWS:, :] = live
 
 
-def own_kernel(half, n_idx, *refs):
-    parcel_refs = refs[:half]
-    other_ref, bias_ref, w_ref, pre_ref, far_ref, idx_ref = refs[half:]
-    fslice = w_ref.shape[1]
-    pcap, width = pre_ref.shape
+def own_product(parcel_refs, other_ref, n_idx, pcap, lanes):
     first_core = lax.axis_index("rep") == 0
+    fslice = other_ref.shape[1]
     feats, weights = [], []
-    for s in range(half):
-        mine, other = parcel_refs[s][:fslice, :], other_ref[s]
-        w_ref[s] = jnp.where(first_core, other, mine)
-        weights.append(jnp.where(first_core, mine, other))
-        feats.append(read_feats(parcel_refs[s], fslice, n_idx, 2 * pcap))
-    both = jnp.dot(
+    for s, ref in enumerate(parcel_refs):
+        weights.append(jnp.where(first_core, ref[:fslice, :], other_ref[s]))
+        feats.append(read_feats(ref, fslice, n_idx, 2 * pcap)[:, lanes])
+    return jnp.dot(
         jnp.concatenate(feats, axis=0).T.astype(jnp.bfloat16),
         jnp.concatenate(weights, axis=0),
         preferred_element_type=jnp.float32,
     )
+
+
+def own_kernel(half, n_idx, *refs):
+    parcel_refs = refs[:half]
+    other_ref, w_ref, far_ref, idx_ref = refs[half:]
+    fslice = w_ref.shape[1]
+    pcap = far_ref.shape[0]
+    first_core = lax.axis_index("rep") == 0
+    for s in range(half):
+        w_ref[s] = jnp.where(first_core, other_ref[s], parcel_refs[s][:fslice, :])
     part = n_idx // 2
     blocks = []
     for s in range(0, half, 2):
@@ -307,8 +312,7 @@
     for i in range(0, len(blocks), 4):
         rows = slice(i // 4 * part, (i // 4 + 1) * part)
         idx_ref[rows, :] = jnp.concatenate(blocks[i : i + 4], axis=1).astype(jnp.bfloat16)
-    pre_ref[...] = both[:pcap] + bias_ref[...]
-    far_ref[...] = both[pcap:]
+    far_ref[...] = own_product(parcel_refs, other_ref, n_idx, pcap, slice(pcap, 2 * pcap))
 
 
 def add_means(half, pre, mean_refs, w_ref, turn=0):
@@ -347,12 +351,14 @@
         out_ref[place, 2 * pcap :] = near.T.astype(jnp.bfloat16)
 
 
-def near_times_kernel(half, fslice, pcap, n_idx, _, __, *refs):
+def near_times_kernel(half, fslice, pcap, n_idx, _, __, other_ref, bias_ref, *refs):
     names = [
         pair_codes(refs[s], refs[s + 1], LANES // 2, fslice, n_idx, 2 * pcap)
         for s in range(0, half, 2)
     ]
     store_times(pcap, names, refs[half])
+    own = own_product(refs[:half], other_ref, n_idx, pcap, slice(0, pcap))
+    refs[half + 1][...] = own + bias_ref[...]
 
 
 def far_times_kernel(
@@ -587,14 +593,13 @@
     far_arrived = send(tagged)
     other_halves = swap(halves, "rep", 1)
     idx_rows = half // 4 * (n_idx // 2)
-    far_own, w_nbr, pre, far_pre, idx_tags = means(
+    far_own, w_nbr, far_pre, idx_tags = means(
         [half],
         table=table,
         before=functools.partial(own_kernel, half, n_idx),
-        ins=(*arrived, other_halves, bias_one[None]),
+        ins=(*arrived, other_halves),
         outs=[
             ((half, fslice, width), bf16),
-            ((pcap, width), jnp.float32),
             ((pcap, width), jnp.float32),
             ((idx_rows, width), bf16),
         ],
@@ -610,14 +615,14 @@
     turned = steps[:-1]
     near_means = means(turned, far_arrived, (cross,), table=table)
     near_arrived = send(near_means, turned)
-    near_own, near_times = means(
+    near_own, near_times, pre = means(
         [0],
         [live],
         table=table,
         after=(cross,),
         before=functools.partial(near_times_kernel, half, fslice, pcap, n_idx),
-        ins=(w2_self, w2_nbr, *arrived),
-        outs=[((half * seed_count, 4 * pcap), bf16)],
+        ins=(w2_self, w2_nbr, other_halves, bias_one[None], *arrived),
+        outs=[((half * seed_count, 4 * pcap), bf16), ((pcap, width), jnp.float32)],
     )
     (near_pre,) = call(
         functools.partial(near_kernel, half),

time: 52.8 us -> 52.8 us (level)
  waiting for transfers between devices: 6.63 us -> 5.71 us
  Pallas kernels: 22.1 us -> 22.9 us
    ppermute x19, waiting for transfers between devices: 6.63 us -> 5.71 us  [swap(): return lax.ppermute(value, axis, [(i, i ^ step) for i in range(size)])]
    pallas_call x15, Pallas kernels: 22.1 us -> 22.9 us  [call(): pl.pallas_call(wrapped, out_shape=tuple((jax.ShapeDtypeStruct(shape, dtyp...]
  transfers between devices with their start and end apart: 19 -> 19, of which waited for: 10 -> 11; matrix products, arithmetic and copies ran while one was open for 0% -> 0% of each run, Pallas kernels for 35% -> 37%
where the time goes in v22:
time: 52.8 us; the launch traced here: 52.6 us
  Pallas kernels  22.9 us (43%)
  starting transfers between devices  22.5 us (43%)
  waiting for transfers between devices  5.71 us (11%)
  between operations  1.48 us (3%)
    pallas_call x15, Pallas kernels, call(): pl.pallas_call(wrapped, out_shape=tuple((jax.ShapeDtypeStruct(shape, dtyp...  22.9 us
    ppermute x19, starting transfers between devices, swap(): return lax.ppermute(value, axis, [(i, i ^ step) for i in range(size)])  22.5 us
    ppermute x19, waiting for transfers between devices, swap(): return lax.ppermute(value, axis, [(i, i ^ step) for i in range(size)])  5.71 us
  transfers between devices with their start and end apart: 19, of which 11 were waited for; matrix products, arithmetic and copies ran while one was open for 0% of the time, Pallas kernels for 37%

profile of v22, /device:TPU:0, one launch (start us, length us, event | category | flops | bytes accessed | tf_op | source)
XLA Modules:
  0.0 52.6 jit_solution(6814597477367257225)
XLA Ops:
  0.6 1.7 %pack.1 = (bf16[176,512]{1,0:T(8,128)(2,1)S(1)}, bf16[176,512]{1,0:T(8,128)(2,1)S(1)}, bf16[176,512]{1,0:T(8,128)(2,1)S(1)}, bf16[176,512]{1,0:T(8,128)(2,1)S(1)...) custom-call(bf16[96,12288]{1,0:T(8,128)(2,1)} %refs_1_.2, s32[1,64]{1,0:T(1,128)} %bitcast.14, ...), custom_call_target="tpu_custom_call" | custom-call | flops 1100000000 | tf_op jit(solution)/shard_map/pack/pallas_call | solution.py:498
  2.3 4.0 %collective-permute-start = (bf16[176,512]{1,0:T(8,128)(2,1)S(1)}, bf16[176,512]{1,0:T(8,128)(2,1)S(1)}, u32[]{:S(2)}, u32[]{:S(2)}) collective-permute-start(bf16[176,512]{1,0:T(8,128)(2,1)S(1)} %get-tuple-element.38), channel_id=1, source_target_pairs={{0,6},{2,4},{4,2},{6,0},{8,14},{10,12},{12,10},{14,8},{1,7},{3,5},... | collective-permute-start | bytes 540680 | tf_op jit(solution)/shard_map/ppermute | solution.py:463
  6.4 0.5 collective-permute-start.1
  6.8 0.2 collective-permute-start.2
  7.0 7.0 %mean.4 = (bf16[144,128]{1,0:T(8,128)(2,1)S(1)}, bf16[144,128]{1,0:T(8,128)(2,1)S(1)}, bf16[144,128]{1,0:T(8,128)(2,1)S(1)}, f32[12288,128]{1,0:T(8,128)S(1)}) custom-call(bf16[96,3072]{1,0:T(8,128)(2,1)S(1)} %get-tuple-element.42.refs_0_, bf16[96,12288]{1,0:T(8,128)(2,1)} %refs_1_.2, s32[8,1,1280]{2,1,0:T(1,128)S(1)} %get-tuple-element.43.refs_2_.refs_5_.refs_0_.refs_8_), custom_call_target="tpu_custom_call" | custom-call | flops 6600000000 | tf_op jit(solution)/shard_map/mean/pallas_call | solution.py:498
  14.7 0.0 collective-permute-done.refs_1_.refs_0_.refs_4_
  14.7 0.3 collective-permute-done.1.refs_2_.refs_1_.refs_5_
  15.0 0.0 collective-permute-done.2.refs_3_.refs_2_.refs_6_
  15.0 0.1 collective-permute-start.6
  15.1 2.7 %collective-permute-start.3 = (bf16[160,128]{1,0:T(8,128)(2,1)S(1)}, bf16[160,128]{1,0:T(8,128)(2,1)S(1)}, u32[]{:S(2)}, u32[]{:S(2)}) collective-permute-start(bf16[160,128]{1,0:T(8,128)(2,1)S(1)} %get-tuple-element.47), channel_id=1, source_target_pairs={{0,6},{2,4},{4,2},{6,0},{8,14},{10,12},{12,10},{14,8},{1,7},{3,5},... | collective-permute-start | bytes 122888 | tf_op jit(solution)/shard_map/ppermute | solution.py:463
  17.8 0.5 collective-permute-start.4
  18.2 0.4 collective-permute-start.5
  18.7 0.0 collective-permute-done.6.refs_4_.refs_2_
  18.7 2.5 %mean.5 = (bf16[144,128]{1,0:T(8,128)(2,1)S(1)}, bf16[4,96,512]{2,1,0:T(8,128)(2,1)S(1)}, f32[192,512]{1,0:T(8,128)S(1)}, bf16[8,512]{1,0:T(8,128)(2,1)S(1)}) custom-call(bf16[176,512]{1,0:T(8,128)(2,1)S(1)} %collective-permute-done.refs_1_.refs_0_.refs_4_, bf16[176,512]{1,0:T(8,128)(2,1)S(1)} %collective-permute-done.1.refs_2_.refs_1_.refs_5_, ...), custom_call_target="tpu_custom_call" | custom-call | tf_op jit(solution)/shard_map/mean/pallas_call | solution.py:498
  21.2 0.0 collective-permute-done.3.refs_0_.refs_2_
  21.2 0.6 %collective-permute-done.4.refs_1_.refs_3_ = bf16[160,128]{1,0:T(8,128)(2,1)S(1)} collective-permute-done((bf16[160,128]{1,0:T(8,128)(2,1)S(1)}, bf16[160,128]{1,0:T(8,128)(2,1)S(1)}, u32[]{:S(2)}, u32[]{:S(2)}) %collective-permute-start.4) | collective-permute-done | bytes 40992 | tf_op jit(solution)/shard_map/ppermute | solution.py:463
  21.8 0.5 collective-permute-done.5.refs_2_.refs_4_
  22.2 0.4 far.1.refs_5_.refs_11_
  22.6 0.0 copy-start
  22.6 0.0 copy-start.1
  22.6 0.0 copy-start.2
  22.7 2.7 %collective-permute-start.7 = (bf16[200,512]{1,0:T(8,128)(2,1)S(1)}, bf16[200,512]{1,0:T(8,128)(2,1)S(1)}, u32[]{:S(2)}, u32[]{:S(2)}) collective-permute-start(bf16[200,512]{1,0:T(8,128)(2,1)S(1)} %far.1.refs_5_.refs_11_), channel_id=1, source_target_pairs={{0,8},{2,10},{4,12},{6,14},{8,0},{10,2},{12,4},{14,6},{1,9},{3,11}... | collective-permute-start | bytes 614408 | tf_op jit(solution)/shard_map/ppermute | solution.py:463
  25.3 4.7 %mean.6 = (bf16[144,128]{1,0:T(8,128)(2,1)S(1)}, bf16[144,128]{1,0:T(8,128)(2,1)S(1)}, bf16[144,128]{1,0:T(8,128)(2,1)S(1)}) custom-call(s32[8,1,1280]{2,1,0:T(1,128)S(1)} %get-tuple-element.43.refs_2_.refs_5_.refs_0_.refs_8_, f32[12288,1,128]{2,1,0:T(1,128)S(1)} %bitcast.8, bf16[160,128]{1,0:T(8,128)(2,1)S(1)} %collective-permute-done.3.refs_0_.refs_2_, ...), custom_call_target="tpu_custom_call" | custom-call | flops 6600000000 | tf_op jit(solution)/shard_map/mean/pallas_call | solution.py:498
  30.1 1.5 %collective-permute-start.8 = (bf16[144,128]{1,0:T(8,128)(2,1)S(1)}, bf16[144,128]{1,0:T(8,128)(2,1)S(1)}, u32[]{:S(2)}, u32[]{:S(2)}) collective-permute-start(bf16[144,128]{1,0:T(8,128)(2,1)S(1)} %get-tuple-element.57), channel_id=1, source_target_pairs={{0,6},{2,4},{4,2},{6,0},{8,14},{10,12},{12,10},{14,8},{1,7},{3,5},... | collective-permute-start | bytes 110600 | tf_op jit(solution)/shard_map/ppermute | solution.py:463
  31.6 1.1 %collective-permute-start.9 = (bf16[144,128]{1,0:T(8,128)(2,1)S(1)}, bf16[144,128]{1,0:T(8,128)(2,1)S(1)}, u32[]{:S(2)}, u32[]{:S(2)}) collective-permute-start(bf16[144,128]{1,0:T(8,128)(2,1)S(1)} %get-tuple-element.58), channel_id=1, source_target_pairs={{0,4},{2,6},{4,0},{6,2},{8,12},{10,14},{12,8},{14,10},{1,5},{3,7},... | collective-permute-start | bytes 110600 | tf_op jit(solution)/shard_map/ppermute | solution.py:463
  32.7 0.9 %collective-permute-start.10 = (bf16[144,128]{1,0:T(8,128)(2,1)S(1)}, bf16[144,128]{1,0:T(8,128)(2,1)S(1)}, u32[]{:S(2)}, u32[]{:S(2)}) collective-permute-start(bf16[144,128]{1,0:T(8,128)(2,1)S(1)} %get-tuple-element.59), channel_id=1, source_target_pairs={{0,2},{2,0},{4,6},{6,4},{8,10},{10,8},{12,14},{14,12},{1,3},{3,1},... | collective-permute-start | bytes 110600 | tf_op jit(solution)/shard_map/ppermute | solution.py:463
  33.6 0.0 copy-done
  33.6 0.0 copy-done.1
  33.6 0.0 copy-done.2
  33.6 2.8 %mean.7 = (bf16[144,128]{1,0:T(8,128)(2,1)S(1)}, bf16[256,768]{1,0:T(8,128)(2,1)S(1)}, f32[192,512]{1,0:T(8,128)S(1)}) custom-call(bf16[512,512]{1,0:T(8,128)(2,1)S(1)} %copy-done, bf16[512,512]{1,0:T(8,128)(2,1)S(1)} %copy-done.1, bf16[4,96,512]{2,1,0:T(8,128)(2,1)S(1)} %collective-permute-done.6.refs_4_.refs_2_, f32[1,512]{1,0:T(1,128)S(1)} %bitcast.10, ...), custom_call_target="tpu_custom_call" | custom-call | tf_op jit(solution)/shard_map/mean/pallas_call | solution.py:498
  36.4 0.0 collective-permute-done.8.refs_0_
  36.4 0.0 collective-permute-done.9.refs_1_
  36.4 0.3 collective-permute-done.10.refs_2_
  36.7 0.4 near.1.refs_1_
  37.1 0.0 collective-permute-done.7.refs_2_.refs_0_
  37.1 0.2 hidden.1.refs_1_
  37.3 0.1 collective-permute-start.11
  37.3 1.1 %far_times.1 = (bf16[256,768]{1,0:T(8,128)(2,1)S(1)}, bf16[2,192,512]{2,1,0:T(8,128)(2,1)S(1)}, bf16[192,512]{1,0:T(8,128)(2,1)}) custom-call(bf16[200,512]{1,0:T(8,128)(2,1)S(1)} %collective-permute-done.7.refs_2_.refs_0_, bf16[192,512]{1,0:T(8,128)(2,1)S(1)} %hidden.1.refs_1_, bf16[512,512]{1,0:T(8,128)(2,1)S(1)} %copy-done, bf16[512,512]{1,0:T(8,128)(2,1)S(1)} %copy-done.1), custom_call_target="tpu_custom_call" | custom-call | flops 1100000000 | tf_op jit(solution)/shard_map/far_times/pallas_call | solution.py:498
  38.5 0.3 collective-permute-done.11.refs_2_
  38.8 0.6 %far_share.1 = (bf16[64,512]{1,0:T(8,128)(2,1)S(1)}, bf16[64,512]{1,0:T(8,128)(2,1)S(1)}, bf16[64,512]{1,0:T(8,128)(2,1)S(1)}, bf16[64,512]{1,0:T(8,128)(2,1)S(1)}, bf16[768,512]{1,0:T(8,128)(2,1)S(1)}) custom-call(bf16[256,768]{1,0:T(8,128)(2,1)S(1)} %get-tuple-element.64.refs_0_, bf16[2,192,512]{2,1,0:T(8,128)(2,1)S(1)} %get-tuple-element.65.refs_1_, ...), custom_call_target="tpu_custom_call" | custom-call | flops 1100000000 | tf_op jit(solution)/shard_map/far_share/pallas_call | solution.py:498
  39.4 0.0 copy-start.3
  39.4 2.4 %collective-permute-start.14 = (bf16[64,512]{1,0:T(8,128)(2,1)S(1)}, bf16[64,512]{1,0:T(8,128)(2,1)S(1)}, u32[]{:S(2)}, u32[]{:S(2)}) collective-permute-start(bf16[64,512]{1,0:T(8,128)(2,1)S(1)} %get-tuple-element.69), channel_id=1, source_target_pairs={{0,6},{2,4},{4,2},{6,0},{8,14},{10,12},{12,10},{14,8},{1,7},{3,5},... | collective-permute-start | bytes 196616 | tf_op jit(solution)/shard_map/ppermute | solution.py:463
  41.7 0.1 collective-permute-start.15
  41.8 1.1 %collective-permute-start.16 = (bf16[64,512]{1,0:T(8,128)(2,1)S(1)}, bf16[64,512]{1,0:T(8,128)(2,1)S(1)}, u32[]{:S(2)}, u32[]{:S(2)}) collective-permute-start(bf16[64,512]{1,0:T(8,128)(2,1)S(1)} %get-tuple-element.71), channel_id=1, source_target_pairs={{0,2},{2,0},{4,6},{6,4},{8,10},{10,8},{12,14},{14,12},{1,3},{3,1},... | collective-permute-start | bytes 196616 | tf_op jit(solution)/shard_map/ppermute | solution.py:463
  42.9 0.5 %near_share.2 = (bf16[64,512]{1,0:T(8,128)(2,1)S(1)}, bf16[64,512]{1,0:T(8,128)(2,1)S(1)}, bf16[64,512]{1,0:T(8,128)(2,1)S(1)}) custom-call(bf16[256,768]{1,0:T(8,128)(2,1)S(1)} %get-tuple-element.63.refs_0_, bf16[768,512]{1,0:T(8,128)(2,1)S(1)} %get-tuple-element.66.refs_1_), custom_call_target="tpu_custom_call" | custom-call | flops 1100000000 | tf_op jit(solution)/shard_map/near_share/pallas_call | solution.py:498
  43.5 2.4 %collective-permute-start.12 = (bf16[64,512]{1,0:T(8,128)(2,1)S(1)}, bf16[64,512]{1,0:T(8,128)(2,1)S(1)}, u32[]{:S(2)}, u32[]{:S(2)}) collective-permute-start(bf16[64,512]{1,0:T(8,128)(2,1)S(1)} %get-tuple-element.67), channel_id=1, source_target_pairs={{0,6},{2,4},{4,2},{6,0},{8,14},{10,12},{12,10},{14,8},{1,7},{3,5},... | collective-permute-start | bytes 196616 | tf_op jit(solution)/shard_map/ppermute | solution.py:463
  45.8 0.1 collective-permute-start.13
  45.9 0.0 collective-permute-done.14.refs_0_
  45.9 0.1 collective-permute-done.15.refs_1_
  46.0 0.1 collective-permute-done.16.refs_2_
  46.1 0.9 %collective-permute-start.18 = (bf16[72,512]{1,0:T(8,128)(2,1)S(1)}, bf16[72,512]{1,0:T(8,128)(2,1)S(1)}, u32[]{:S(2)}, u32[]{:S(2)}) collective-permute-start(bf16[72,512]{1,0:T(8,128)(2,1)S(1)} %side_sum.1.refs_2_), channel_id=1, source_target_pairs={{0,8},{2,10},{4,12},{6,14},{8,0},{10,2},{12,4},{14,6},{1,9},{3,11}... | collective-permute-start | bytes 221192 | tf_op jit(solution)/shard_map/ppermute | solution.py:463
  47.0 0.2 near_share.3
  47.2 1.0 %collective-permute-start.17 = (bf16[64,512]{1,0:T(8,128)(2,1)S(1)}, bf16[64,512]{1,0:T(8,128)(2,1)S(1)}, u32[]{:S(2)}, u32[]{:S(2)}) collective-permute-start(bf16[64,512]{1,0:T(8,128)(2,1)S(1)} %near_share.3), channel_id=1, source_target_pairs={{0,2},{2,0},{4,6},{6,4},{8,10},{10,8},{12,14},{14,12},{1,3},{3,1},... | collective-permute-start | bytes 196616 | tf_op jit(solution)/shard_map/ppermute | solution.py:463
  48.3 0.5 %collective-permute-done.12.refs_1_ = bf16[64,512]{1,0:T(8,128)(2,1)S(1)} collective-permute-done((bf16[64,512]{1,0:T(8,128)(2,1)S(1)}, bf16[64,512]{1,0:T(8,128)(2,1)S(1)}, u32[]{:S(2)}, u32[]{:S(2)}) %collective-permute-start.12) | collective-permute-done | bytes 65568 | tf_op jit(solution)/shard_map/ppermute | solution.py:463
  48.8 1.8 %collective-permute-done.13.refs_2_ = bf16[64,512]{1,0:T(8,128)(2,1)S(1)} collective-permute-done((bf16[64,512]{1,0:T(8,128)(2,1)S(1)}, bf16[64,512]{1,0:T(8,128)(2,1)S(1)}, u32[]{:S(2)}, u32[]{:S(2)}) %collective-permute-start.13) | collective-permute-done | bytes 65568 | tf_op jit(solution)/shard_map/ppermute | solution.py:463
  50.6 1.0 %collective-permute-done.17.refs_3_ = bf16[64,512]{1,0:T(8,128)(2,1)S(1)} collective-permute-done((bf16[64,512]{1,0:T(8,128)(2,1)S(1)}, bf16[64,512]{1,0:T(8,128)(2,1)S(1)}, u32[]{:S(2)}, u32[]{:S(2)}) %collective-permute-start.17) | collective-permute-done | bytes 65568 | tf_op jit(solution)/shard_map/ppermute | solution.py:463
  51.6 0.3 collective-permute-done.18.refs_5_
  51.9 0.0 copy-done.3
  51.9 0.7 %seeds.1 = bf16[64,512]{1,0:T(8,128)(2,1)} custom-call(f32[1,512]{1,0:T(1,128)S(1)} %bitcast.11, bf16[64,512]{1,0:T(8,128)(2,1)S(1)} %collective-permute-done.12.refs_1_, bf16[64,512]{1,0:T(8,128)(2,1)S(1)} %collective-permute-done.13.refs_2_, bf16[64,512]{1,0:T(8,128)(2,1)S(1)} %collective-permute-done.17.refs_3_, ...), custom_call_target="tpu_custom_call" | custom-call | flops 1100000000 | tf_op jit(solution)/shard_map/seeds/pallas_call | solution.py:498
  (2 shorter events, 0.1 us)
Async XLA Ops:
  2.3 12.4 %collective-permute-start = (bf16[176,512]{1,0:T(8,128)(2,1)S(1)}, bf16[176,512]{1,0:T(8,128)(2,1)S(1)}, u32[]{:S(2)}, u32[]{:S(2)}) collective-permute-start(bf16[176,512]{1,0:T(8,128)(2,1)S(1)} %get-tuple-element.38), channel_id=1, source_target_pairs={{0,6},{2,4},{4,2},{6,0},{8,14},{10,12},{12,10},{14,8},{1,7},{3,5},... | collective-permute-start | bytes 540680 | tf_op jit(solution)/shard_map/ppermute | solution.py:463
  6.4 8.6 %collective-permute-start.1 = (bf16[176,512]{1,0:T(8,128)(2,1)S(1)}, bf16[176,512]{1,0:T(8,128)(2,1)S(1)}, u32[]{:S(2)}, u32[]{:S(2)}) collective-permute-start(bf16[176,512]{1,0:T(8,128)(2,1)S(1)} %get-tuple-element.39), channel_id=1, source_target_pairs={{0,4},{2,6},{4,0},{6,2},{8,12},{10,14},{12,8},{14,10},{1,5},{3,7},... | collective-permute-start | bytes 540680 | tf_op jit(solution)/shard_map/ppermute | solution.py:463
  6.8 8.2 %collective-permute-start.2 = (bf16[176,512]{1,0:T(8,128)(2,1)S(1)}, bf16[176,512]{1,0:T(8,128)(2,1)S(1)}, u32[]{:S(2)}, u32[]{:S(2)}) collective-permute-start(bf16[176,512]{1,0:T(8,128)(2,1)S(1)} %get-tuple-element.40), channel_id=1, source_target_pairs={{0,2},{2,0},{4,6},{6,4},{8,10},{10,8},{12,14},{14,12},{1,3},{3,1},... | collective-permute-start | bytes 540680 | tf_op jit(solution)/shard_map/ppermute | solution.py:463
  15.0 3.6 %collective-permute-start.6 = (bf16[4,96,512]{2,1,0:T(8,128)(2,1)S(1)}, bf16[4,96,512]{2,1,0:T(8,128)(2,1)S(1)}, u32[]{:S(2)}, u32[]{:S(2)}) collective-permute-start(bf16[4,96,512]{2,1,0:T(8,128)(2,1)S(1)} %get-tuple-element.50), channel_id=1, source_target_pairs={{0,1},{1,0},{2,3},{3,2},{4,5},{5,4},{6,7},{7,6},{8,9},{9,8},{10,11... | collective-permute-start | bytes 1179656 | tf_op jit(solution)/shard_map/ppermute | solution.py:463
  15.1 6.1 %collective-permute-start.3 = (bf16[160,128]{1,0:T(8,128)(2,1)S(1)}, bf16[160,128]{1,0:T(8,128)(2,1)S(1)}, u32[]{:S(2)}, u32[]{:S(2)}) collective-permute-start(bf16[160,128]{1,0:T(8,128)(2,1)S(1)} %get-tuple-element.47), channel_id=1, source_target_pairs={{0,6},{2,4},{4,2},{6,0},{8,14},{10,12},{12,10},{14,8},{1,7},{3,5},... | collective-permute-start | bytes 122888 | tf_op jit(solution)/shard_map/ppermute | solution.py:463
  17.8 4.0 %collective-permute-start.4 = (bf16[160,128]{1,0:T(8,128)(2,1)S(1)}, bf16[160,128]{1,0:T(8,128)(2,1)S(1)}, u32[]{:S(2)}, u32[]{:S(2)}) collective-permute-start(bf16[160,128]{1,0:T(8,128)(2,1)S(1)} %get-tuple-element.48), channel_id=1, source_target_pairs={{0,4},{2,6},{4,0},{6,2},{8,12},{10,14},{12,8},{14,10},{1,5},{3,7},... | collective-permute-start | bytes 122888 | tf_op jit(solution)/shard_map/ppermute | solution.py:463
  18.2 4.0 %collective-permute-start.5 = (bf16[160,128]{1,0:T(8,128)(2,1)S(1)}, bf16[160,128]{1,0:T(8,128)(2,1)S(1)}, u32[]{:S(2)}, u32[]{:S(2)}) collective-permute-start(bf16[160,128]{1,0:T(8,128)(2,1)S(1)} %get-tuple-element.49), channel_id=1, source_target_pairs={{0,2},{2,0},{4,6},{6,4},{8,10},{10,8},{12,14},{14,12},{1,3},{3,1},... | collective-permute-start | bytes 122888 | tf_op jit(solution)/shard_map/ppermute | solution.py:463
  22.6 11.0 %copy-start = (bf16[512,512]{1,0:T(8,128)(2,1)S(1)}, bf16[512,512]{1,0:T(8,128)(2,1)}, u32[]{:S(2)}) copy-start(bf16[512,512]{1,0:T(8,128)(2,1)} %refs_3_.5) | copy-start | bytes 1572868
  22.6 11.0 %copy-start.1 = (bf16[512,512]{1,0:T(8,128)(2,1)S(1)}, bf16[512,512]{1,0:T(8,128)(2,1)}, u32[]{:S(2)}) copy-start(bf16[512,512]{1,0:T(8,128)(2,1)} %refs_4_.3) | copy-start | bytes 1572868
  22.6 11.0 %copy-start.2 = (f32[512]{0:T(512)S(1)}, f32[512]{0:T(512)}, u32[]{:S(2)}) copy-start(f32[512]{0:T(512)} %param.18) | copy-start | bytes 6148
  22.7 14.4 %collective-permute-start.7 = (bf16[200,512]{1,0:T(8,128)(2,1)S(1)}, bf16[200,512]{1,0:T(8,128)(2,1)S(1)}, u32[]{:S(2)}, u32[]{:S(2)}) collective-permute-start(bf16[200,512]{1,0:T(8,128)(2,1)S(1)} %far.1.refs_5_.refs_11_), channel_id=1, source_target_pairs={{0,8},{2,10},{4,12},{6,14},{8,0},{10,2},{12,4},{14,6},{1,9},{3,11}... | collective-permute-start | bytes 614408 | tf_op jit(solution)/shard_map/ppermute | solution.py:463
  30.1 6.3 %collective-permute-start.8 = (bf16[144,128]{1,0:T(8,128)(2,1)S(1)}, bf16[144,128]{1,0:T(8,128)(2,1)S(1)}, u32[]{:S(2)}, u32[]{:S(2)}) collective-permute-start(bf16[144,128]{1,0:T(8,128)(2,1)S(1)} %get-tuple-element.57), channel_id=1, source_target_pairs={{0,6},{2,4},{4,2},{6,0},{8,14},{10,12},{12,10},{14,8},{1,7},{3,5},... | collective-permute-start | bytes 110600 | tf_op jit(solution)/shard_map/ppermute | solution.py:463
  31.6 4.8 %collective-permute-start.9 = (bf16[144,128]{1,0:T(8,128)(2,1)S(1)}, bf16[144,128]{1,0:T(8,128)(2,1)S(1)}, u32[]{:S(2)}, u32[]{:S(2)}) collective-permute-start(bf16[144,128]{1,0:T(8,128)(2,1)S(1)} %get-tuple-element.58), channel_id=1, source_target_pairs={{0,4},{2,6},{4,0},{6,2},{8,12},{10,14},{12,8},{14,10},{1,5},{3,7},... | collective-permute-start | bytes 110600 | tf_op jit(solution)/shard_map/ppermute | solution.py:463
  32.7 4.0 %collective-permute-start.10 = (bf16[144,128]{1,0:T(8,128)(2,1)S(1)}, bf16[144,128]{1,0:T(8,128)(2,1)S(1)}, u32[]{:S(2)}, u32[]{:S(2)}) collective-permute-start(bf16[144,128]{1,0:T(8,128)(2,1)S(1)} %get-tuple-element.59), channel_id=1, source_target_pairs={{0,2},{2,0},{4,6},{6,4},{8,10},{10,8},{12,14},{14,12},{1,3},{3,1},... | collective-permute-start | bytes 110600 | tf_op jit(solution)/shard_map/ppermute | solution.py:463
  37.3 1.5 %collective-permute-start.11 = (bf16[192,512]{1,0:T(8,128)(2,1)S(1)}, bf16[192,512]{1,0:T(8,128)(2,1)S(1)}, u32[]{:S(2)}, u32[]{:S(2)}) collective-permute-start(bf16[192,512]{1,0:T(8,128)(2,1)S(1)} %hidden.1.refs_1_), channel_id=1, source_target_pairs={{0,1},{1,0},{2,3},{3,2},{4,5},{5,4},{6,7},{7,6},{8,9},{9,8},{10,11... | collective-permute-start | bytes 589832 | tf_op jit(solution)/shard_map/ppermute | solution.py:463
  39.4 12.6 %copy-start.3 = (f32[512]{0:T(512)S(1)}, f32[512]{0:T(512)}, u32[]{:S(2)}) copy-start(f32[512]{0:T(512)} %param.21) | copy-start | bytes 6148
  39.4 6.5 %collective-permute-start.14 = (bf16[64,512]{1,0:T(8,128)(2,1)S(1)}, bf16[64,512]{1,0:T(8,128)(2,1)S(1)}, u32[]{:S(2)}, u32[]{:S(2)}) collective-permute-start(bf16[64,512]{1,0:T(8,128)(2,1)S(1)} %get-tuple-element.69), channel_id=1, source_target_pairs={{0,6},{2,4},{4,2},{6,0},{8,14},{10,12},{12,10},{14,8},{1,7},{3,5},... | collective-permute-start | bytes 196616 | tf_op jit(solution)/shard_map/ppermute | solution.py:463
  41.7 4.3 %collective-permute-start.15 = (bf16[64,512]{1,0:T(8,128)(2,1)S(1)}, bf16[64,512]{1,0:T(8,128)(2,1)S(1)}, u32[]{:S(2)}, u32[]{:S(2)}) collective-permute-start(bf16[64,512]{1,0:T(8,128)(2,1)S(1)} %get-tuple-element.70), channel_id=1, source_target_pairs={{0,4},{2,6},{4,0},{6,2},{8,12},{10,14},{12,8},{14,10},{1,5},{3,7},... | collective-permute-start | bytes 196616 | tf_op jit(solution)/shard_map/ppermute | solution.py:463
  41.8 4.3 %collective-permute-start.16 = (bf16[64,512]{1,0:T(8,128)(2,1)S(1)}, bf16[64,512]{1,0:T(8,128)(2,1)S(1)}, u32[]{:S(2)}, u32[]{:S(2)}) collective-permute-start(bf16[64,512]{1,0:T(8,128)(2,1)S(1)} %get-tuple-element.71), channel_id=1, source_target_pairs={{0,2},{2,0},{4,6},{6,4},{8,10},{10,8},{12,14},{14,12},{1,3},{3,1},... | collective-permute-start | bytes 196616 | tf_op jit(solution)/shard_map/ppermute | solution.py:463
  43.5 5.3 %collective-permute-start.12 = (bf16[64,512]{1,0:T(8,128)(2,1)S(1)}, bf16[64,512]{1,0:T(8,128)(2,1)S(1)}, u32[]{:S(2)}, u32[]{:S(2)}) collective-permute-start(bf16[64,512]{1,0:T(8,128)(2,1)S(1)} %get-tuple-element.67), channel_id=1, source_target_pairs={{0,6},{2,4},{4,2},{6,0},{8,14},{10,12},{12,10},{14,8},{1,7},{3,5},... | collective-permute-start | bytes 196616 | tf_op jit(solution)/shard_map/ppermute | solution.py:463
  45.8 4.8 %collective-permute-start.13 = (bf16[64,512]{1,0:T(8,128)(2,1)S(1)}, bf16[64,512]{1,0:T(8,128)(2,1)S(1)}, u32[]{:S(2)}, u32[]{:S(2)}) collective-permute-start(bf16[64,512]{1,0:T(8,128)(2,1)S(1)} %get-tuple-element.68), channel_id=1, source_target_pairs={{0,4},{2,6},{4,0},{6,2},{8,12},{10,14},{12,8},{14,10},{1,5},{3,7},... | collective-permute-start | bytes 196616 | tf_op jit(solution)/shard_map/ppermute | solution.py:463
  46.1 5.8 %collective-permute-start.18 = (bf16[72,512]{1,0:T(8,128)(2,1)S(1)}, bf16[72,512]{1,0:T(8,128)(2,1)S(1)}, u32[]{:S(2)}, u32[]{:S(2)}) collective-permute-start(bf16[72,512]{1,0:T(8,128)(2,1)S(1)} %side_sum.1.refs_2_), channel_id=1, source_target_pairs={{0,8},{2,10},{4,12},{6,14},{8,0},{10,2},{12,4},{14,6},{1,9},{3,11}... | collective-permute-start | bytes 221192 | tf_op jit(solution)/shard_map/ppermute | solution.py:463
  47.2 4.3 %collective-permute-start.17 = (bf16[64,512]{1,0:T(8,128)(2,1)S(1)}, bf16[64,512]{1,0:T(8,128)(2,1)S(1)}, u32[]{:S(2)}, u32[]{:S(2)}) collective-permute-start(bf16[64,512]{1,0:T(8,128)(2,1)S(1)} %near_share.3), channel_id=1, source_target_pairs={{0,2},{2,0},{4,6},{6,4},{8,10},{10,8},{12,14},{14,12},{1,3},{3,1},... | collective-permute-start | bytes 196616 | tf_op jit(solution)/shard_map/ppermute | solution.py:463
